TPU v7x, 32 devices: a whole 2x2x4 slice. The times are simulated.
32 devices in a mesh: parts: 2 (over x), expert: 16 (over z, y, core).
Axes of the slice: x: 2, y: 2, z: 4, core: 2. Of those that a mesh axis runs over, the one named last changes fastest.
Arguments:
- routes: int32 [4096, 8], P(('parts', 'expert')), parts along dimension 0, may hold values from 0 to 15, all different within a row; in each aligned block of 128 rows (0 to 127, 128 to 255, ...) at most 80 rows name the same one
- probs: float32 [4096, 8], P(('parts', 'expert')), parts along dimension 0, may hold values from 0.05 to 1
- tokens: bfloat16 [4096, 2048], P(('parts', 'expert')), parts along dimension 0, may hold values from -6 to 6
- gate_weight: bfloat16 [16, 2048, 768], P('expert'), may hold values from -0.125 to 0.125
- up_weight: bfloat16 [16, 2048, 768], P('expert'), may hold values from -0.125 to 0.125
- down_weight: bfloat16 [16, 768, 2048], P('expert'), may hold values from -0.21875 to 0.21875
Outputs:
- gram: float32 [32, 768, 768], P(('parts', 'expert')), parts along dimension 0
- mixed: bfloat16 [4096, 2048], P(('parts', 'expert')), parts along dimension 0
There are 2 independent parts, one for each index of `parts`. A program takes and returns all parts, laid end to end along the dimension named above; an argument that names none is the same for every part. Nothing has to cross between parts.
Inputs may be any that keep to these rules, and one draw needn't show every extreme that they name: `routes`: among the rows of one device no expert is named more than 80 times, a bound that some block reaches; every expert is named by some row.
All inputs are finite; a program needn't handle non-finite values.
Results may differ from a plain program's by a relative error of at most 0.006.
Values may be sent and summed in bfloat16 or wider, within the bound.
No kernel may reach another device: no remote copies, remote signals or barrier semaphores. Data moves between devices by JAX's collectives and lax.ppermute only.
A program may use at most 128 MiB of HBM per device.

v0:
```python
import jax
import jax.numpy as jnp
from jax import lax
from jax.sharding import PartitionSpec as P


def prefix(part, axis, combine, identity):
    place = lax.axis_index(axis)
    gathered = lax.all_gather(part, axis)
    state = jnp.zeros_like(part) + jnp.asarray(identity, part.dtype)

    def one(turn, state):
        return combine(state, lax.dynamic_index_in_dim(gathered, turn, 0, False))

    return lax.fori_loop(0, place, one, state)


def for_sending(array):
    return jax.tree.map(lambda a: a.astype(jnp.bfloat16) if a.dtype == jnp.float32 else a, array)


def add_counts(earlier, later):
    return earlier + later


def gram_of(rows):
    return lax.dot_general(rows, rows, (((0,), (0,)), ((), ())), preferred_element_type=jnp.float32)


def expert_pass(rows, w_gate, w_up, w_down):
    gate = jnp.dot(rows, w_gate, preferred_element_type=jnp.float32)
    up = jnp.dot(rows, w_up, preferred_element_type=jnp.float32)
    act = (jax.nn.silu(gate) * up).astype(jnp.bfloat16)
    gram_sum = gram_of(act)
    made = jnp.dot(act, w_down, preferred_element_type=jnp.float32).astype(jnp.bfloat16)
    return (gram_sum, made)


def shards(routes, probs, tokens, gate_weight, up_weight, down_weight):
    tok_rows, top = routes.shape
    features = tokens.shape[1]
    ranks_total = lax.axis_size("expert")
    experts = ranks_total * down_weight.shape[0]
    slots = 5 * tok_rows * top // (4 * experts)
    capacity = tok_rows * top // 2
    pairs = tok_rows * top
    flat_routes = routes.reshape(pairs)
    onehot = (flat_routes[:, None] == jnp.arange(experts, dtype=jnp.int32)[None, :]).astype(
        jnp.int32
    )
    local_rank = jnp.sum((jnp.cumsum(onehot, axis=0) - onehot) * onehot, axis=1)
    sent_count = jnp.sum(onehot, axis=0)
    table = (
        jnp.zeros((experts, slots), jnp.int32)
        .at[flat_routes, local_rank]
        .set(jnp.arange(pairs, dtype=jnp.int32))
    )
    position = jnp.arange(slots, dtype=jnp.int32)
    earlier = prefix(sent_count, "expert", add_counts, jnp.zeros_like(sent_count))
    sent_count = jnp.clip(capacity - earlier, 0, sent_count)
    live = position[None, :] < sent_count[:, None]
    outgoing = jnp.where(live[:, :, None], tokens[table // top], jnp.zeros((), tokens.dtype))
    arrived, arrived_count = (
        lax.all_to_all(outgoing, "expert", split_axis=0, concat_axis=0, tiled=True),
        lax.all_to_all(
            for_sending(sent_count[:, None]), "expert", split_axis=0, concat_axis=0, tiled=True
        ),
    )
    source_count = arrived_count[:, 0]
    total = jnp.sum(source_count)
    w_gate = gate_weight[0]
    w_up = up_weight[0]
    w_down = down_weight[0]
    valid = position[None, :] < source_count[:, None]
    rows = jnp.where(valid[:, :, None], arrived, jnp.zeros((), arrived.dtype)).reshape(
        ranks_total * slots, features
    )
    gram_sum, produced = expert_pass(rows, w_gate, w_up, w_down)
    produced = produced.reshape(ranks_total, slots, w_down.shape[1])
    gram = gram_sum * (2.0 / total.astype(jnp.float32))
    returned = lax.all_to_all(produced, "expert", split_axis=0, concat_axis=0, tiled=True)
    picked = returned.reshape(experts * slots, returned.shape[2])[flat_routes * slots + local_rank]
    mixed = jnp.sum(
        picked.reshape(tok_rows, top, returned.shape[2]).astype(jnp.float32) * probs[:, :, None],
        axis=1,
    )
    return (gram[None], mixed.astype(jnp.bfloat16))


def solution(mesh):
    placed = (
        P(("parts", "expert"), None),
        P(("parts", "expert"), None),
        P(("parts", "expert"), None),
        P("expert", None, None),
        P("expert", None, None),
        P("expert", None, None),
    )
    return jax.shard_map(
        shards,
        mesh=mesh,
        in_specs=placed,
        out_specs=(P(("parts", "expert"), None, None), P(("parts", "expert"), None)),
        check_vma=False,
    )
```

profile of v0, /device:TPU:15, one launch (start us, length us, event | category | flops | bytes accessed | tf_op | source)
XLA Modules:
  0.0 328.5 jit_solution(10247902401398407033)
XLA Ops:
  0.6 0.0 copy-start
  0.6 0.9 copy.24
  1.6 0.1 eq.29
  1.7 0.1 eq.25
  1.8 4.5 %reduce-window.6 = s32[16,8,128]{2,1,0:T(8,128)S(1)} reduce-window(s32[16,8,128]{2,1,0:T(8,128)S(1)} %fusion.8, s32[]{:T(128)} %constant.19.clone.1), window={size=1x1x128 pad=0_0x0_0x127_0}, to_apply=%region_3.4 | reduce-window | flops 2080768 | bytes 131076 | tf_op jit(solution)/shard_map/reduce-window
  6.3 0.1 slice.12
  6.4 0.1 copy.28
  6.6 0.1 copy.29
  6.6 0.1 broadcast_add_fusion
  6.7 0.1 convert_reduce_fusion
  6.9 1.2 dynamic-slice
  8.8 0.2 dynamic-update-slice
  9.0 7.9 %all-reduce = s32[256]{0:T(256)S(1)} all-reduce(s32[256]{0:T(256)S(1)} %dynamic-update-slice), channel_id=2, replica_groups=mesh['parts'=2,'expert'=16] {'expert'}, use_global_device_ids=true, to_apply=%add | all-reduce | flops 256 | bytes 2048
  16.9 0.1 reshape.184
  17.0 0.3 while.10
  17.3 0.7 copy.25
  18.0 8.1 %all-to-all-start = ((s32[16,1,1]{2,1,0:T(1,128)}), s32[16,1,1]{2,1,0:T(1,128)S(1)}, u32[]{:S(2)}, u32[]{:S(2)}) async-start(s32[16,1,1]{2,1,0:T(1,128)} %copy.25), calls=%async_computation | async-start | bytes 16384 | tf_op jit(solution)/shard_map/all_to_all | solution.py:65
  26.1 0.1 reshape.152
  26.2 0.1 iota_compare_fusion.2
  26.3 0.7 multiply_reduce_fusion
  27.0 0.7 and_reduce_fusion
  27.8 4.3 %scatter_custom_fusion = s32[1280]{0:T(1024)S(1)} fusion(s32[1024]{0:T(1024)S(1)} %broadcast_select_fusion.2, s32[1024]{0:T(1024)S(1)} %iota.22, s32[]{:T(128)} %constant.19.clone.1), kind=kCustom, calls=%fused_computation.42 | custom fusion | bytes 5124
  32.1 0.1 reshape.160
  32.2 0.1 reshape.164
  32.3 11.9 %gather_fusion = bf16[1280,2048]{1,0:T(8,128)(2,1)} fusion(bf16[128,2048]{1,0:T(8,128)(2,1)} %param.10, s32[2048]{0:T(1024)S(1)} %pad_clamp_fusion), kind=kCustom, calls=%fused_computation | custom fusion | bytes 10490880 | tf_op jit(solution)/shard_map/gather | solution.py:62
  44.2 5.2 %broadcast_select_fusion = bf16[16,80,2048]{2,1,0:T(8,128)(2,1)} fusion(bf16[16,80,2048]{2,1,0:T(8,128)(2,1)} %bitcast.41, pred[16,80]{1,0:T(8,128)(4,1)S(1)} %iota_compare_fusion.2), kind=kLoop, calls=%fused_computation.7 | loop fusion | flops 2621440 | bytes 10487040 | tf_op jit(solution)/shard_map/jit(_where)/select_n | solution.py:62
  49.4 0.0 all-to-all-done
  49.5 6.1 %all-to-all-start.1 = ((bf16[16,80,2048]{2,1,0:T(8,128)(2,1)}), bf16[16,80,2048]{2,1,0:T(8,128)(2,1)}, u32[]{:S(2)}, u32[]{:S(2)}) async-start(bf16[16,80,2048]{2,1,0:T(8,128)(2,1)} %broadcast_select_fusion), calls=%async_computation.1 | async-start | bytes 10485760 | tf_op jit(solution)/shard_map/all_to_all | solution.py:64
  55.5 0.9 fusion.13
  56.4 0.1 iota_compare_fusion.3
  56.5 113.9 %all-to-all-done.1 = bf16[16,80,2048]{2,1,0:T(8,128)(2,1)} async-done(((bf16[16,80,2048]{2,1,0:T(8,128)(2,1)}), bf16[16,80,2048]{2,1,0:T(8,128)(2,1)}, u32[]{:S(2)}, u32[]{:S(2)}) %all-to-all-start.1) | async-done | bytes 5242912 | tf_op jit(solution)/shard_map/all_to_all | solution.py:64
  170.5 0.0 copy-start.3
  170.5 3.1 broadcast_select_fusion.1
  173.5 0.4 copy-done.3
  173.9 0.0 copy-start.4
  173.9 4.3 %fusion.4 = f32[1280,768]{1,0:T(8,128)S(1)} fusion(bf16[1280,2048]{1,0:T(8,128)(2,1)S(1)} %bitcast.43, bf16[1,2048,768]{2,1,0:T(8,128)(2,1)S(1)} %copy-done.3), kind=kOutput, calls=%fused_computation.13 | convolution fusion | flops 4026531840 | bytes 12320768 | tf_op jit(solution)/shard_map/dot_general | solution.py:31
  178.2 0.0 copy-done.4
  178.2 4.8 %fusion.1 = bf16[1280,768]{1,0:T(8,128)(2,1)S(1)} fusion(bf16[1280,2048]{1,0:T(8,128)(2,1)S(1)} %bitcast.44, f32[1280,768]{1,0:T(8,128)S(1)} %fusion.4, bf16[1,2048,768]{2,1,0:T(8,128)(2,1)S(1)} %copy-done.4), kind=kOutput, calls=%fused_computation.10 | convolution fusion | flops 4032430080 | bytes 14286848 | tf_op jit(solution)/shard_map/dot_general | solution.py:32
  183.0 0.0 copy-done
  183.0 0.0 copy-start.1
  183.1 6.1 %convolution_convert_fusion = bf16[1280,2048]{1,0:T(8,128)(2,1)} fusion(bf16[1280,768]{1,0:T(8,128)(2,1)S(1)} %fusion.1, bf16[1,768,2048]{2,1,0:T(8,128)(2,1)S(1)} %copy-done), kind=kOutput, calls=%fused_computation.6 | convolution fusion | flops 4029153280 | bytes 10354688 | tf_op jit(solution)/shard_map/dot_general | solution.py:35
  189.1 0.0 copy-done.1
  189.1 0.0 copy-start.2
  189.1 5.0 %all-to-all-start.2 = ((bf16[16,80,2048]{2,1,0:T(8,128)(2,1)}), bf16[16,80,2048]{2,1,0:T(8,128)(2,1)}, u32[]{:S(2)}, u32[]{:S(2)}) async-start(bf16[16,80,2048]{2,1,0:T(8,128)(2,1)} %bitcast.42), calls=%async_computation.2 | async-start | bytes 10485760 | tf_op jit(solution)/shard_map/all_to_all | solution.py:81
  194.2 0.0 copy-done.2
  194.2 0.1 copy.30
  195.0 5.3 %multiply_bitcast_fusion = f32[1,768,768]{2,1,0:T(8,128)} fusion(bf16[1280,768]{1,0:T(8,128)(2,1)} %copy-done.1, f32[]{:T(128)S(6)} %div.24), kind=kOutput, calls=%fused_computation.15 | convolution fusion | flops 1510539264 | bytes 4325380 | tf_op jit(solution)/shard_map/dot_general | solution.py:27
  200.2 108.8 %all-to-all-done.2 = bf16[16,80,2048]{2,1,0:T(8,128)(2,1)} async-done(((bf16[16,80,2048]{2,1,0:T(8,128)(2,1)}), bf16[16,80,2048]{2,1,0:T(8,128)(2,1)}, u32[]{:S(2)}, u32[]{:S(2)}) %all-to-all-start.2) | async-done | bytes 5242912 | tf_op jit(solution)/shard_map/all_to_all | solution.py:81
  309.1 12.0 %gather_fusion.1 = bf16[1024,2048]{1,0:T(8,128)(2,1)} fusion(bf16[1280,2048]{1,0:T(8,128)(2,1)} %bitcast.13, s32[1024]{0:T(1024)S(1)} %broadcast_clamp_fusion), kind=kCustom, calls=%fused_computation.1 | custom fusion | bytes 8392704 | tf_op jit(solution)/shard_map/gather | solution.py:82
  321.1 7.3 %fusion = bf16[128,2048]{1,0:T(8,128)(2,1)} fusion(bf16[1024,2048]{1,0:T(8,128)(2,1)} %gather_fusion.1, f32[128,8]{1,0:T(8,128)S(1)} %copy.30), kind=kLoop, calls=%fused_computation.5 | loop fusion | flops 6029312 | bytes 4722688 | tf_op jit(solution)/shard_map/reduce_sum | solution.py:83
  (19 shorter events, 0.2 us)
Async XLA Ops:
  0.6 182.4 %copy-start = (bf16[1,768,2048]{2,1,0:T(8,128)(2,1)S(1)}, bf16[1,768,2048]{2,1,0:T(8,128)(2,1)}, u32[]{:S(2)}) copy-start(bf16[1,768,2048]{2,1,0:T(8,128)(2,1)} %param.13) | copy-start | bytes 9437188
  18.0 31.5 %all-to-all-start = ((s32[16,1,1]{2,1,0:T(1,128)}), s32[16,1,1]{2,1,0:T(1,128)S(1)}, u32[]{:S(2)}, u32[]{:S(2)}) async-start(s32[16,1,1]{2,1,0:T(1,128)} %copy.25), calls=%async_computation | async-start | bytes 16384 | tf_op jit(solution)/shard_map/all_to_all | solution.py:65
  49.5 121.0 %all-to-all-start.1 = ((bf16[16,80,2048]{2,1,0:T(8,128)(2,1)}), bf16[16,80,2048]{2,1,0:T(8,128)(2,1)}, u32[]{:S(2)}, u32[]{:S(2)}) async-start(bf16[16,80,2048]{2,1,0:T(8,128)(2,1)} %broadcast_select_fusion), calls=%async_computation.1 | async-start | bytes 10485760 | tf_op jit(solution)/shard_map/all_to_all | solution.py:64
  170.5 3.4 %copy-start.3 = (bf16[1,2048,768]{2,1,0:T(8,128)(2,1)S(1)}, bf16[1,2048,768]{2,1,0:T(8,128)(2,1)}, u32[]{:S(2)}) copy-start(bf16[1,2048,768]{2,1,0:T(8,128)(2,1)} %param.11) | copy-start | bytes 9437188
  173.9 4.3 %copy-start.4 = (bf16[1,2048,768]{2,1,0:T(8,128)(2,1)S(1)}, bf16[1,2048,768]{2,1,0:T(8,128)(2,1)}, u32[]{:S(2)}) copy-start(bf16[1,2048,768]{2,1,0:T(8,128)(2,1)} %param.12) | copy-start | bytes 9437188
  183.0 6.1 %copy-start.1 = (bf16[1280,768]{1,0:T(8,128)(2,1)}, bf16[1280,768]{1,0:T(8,128)(2,1)S(1)}, u32[]{:S(2)}) copy-start(bf16[1280,768]{1,0:T(8,128)(2,1)S(1)} %fusion.1) | copy-start | bytes 5898244
  189.1 5.0 %copy-start.2 = (f32[128,8]{0,1:T(8,128)S(1)}, f32[128,8]{0,1:T(8,128)}, u32[]{:S(2)}) copy-start(f32[128,8]{0,1:T(8,128)} %param.9) | copy-start | bytes 12292
  189.1 120.0 %all-to-all-start.2 = ((bf16[16,80,2048]{2,1,0:T(8,128)(2,1)}), bf16[16,80,2048]{2,1,0:T(8,128)(2,1)}, u32[]{:S(2)}, u32[]{:S(2)}) async-start(bf16[16,80,2048]{2,1,0:T(8,128)(2,1)} %bitcast.42), calls=%async_computation.2 | async-start | bytes 10485760 | tf_op jit(solution)/shard_map/all_to_all | solution.py:81
where the time goes:
time: 329 us; the launch traced here: 328 us
  waiting for transfers between devices  223 us (68%)
  local copies, waits for them, and re-layouts  32.7 us (10%)
  other arithmetic  23.1 us (7%)
  matrix products  20.4 us (6%)
  starting transfers between devices  19.2 us (6%)
  blocking collectives  7.89 us (2%)
    all_to_all x1, waiting for transfers between devices, shards(): lax.all_to_all(outgoing, 'expert', split_axis=0, concat_axis=0, tiled=True)  114 us
    all_to_all x1, waiting for transfers between devices, shards(): lax.all_to_all(produced, 'expert', split_axis=0, concat_axis=0, tiled=True)  109 us
    gather x1, local copies, waits for them, and re-layouts, shards(): returned.reshape(experts * slots, returned.shape[2])  12 us
    gather x1, local copies, waits for them, and re-layouts, shards(): tokens[table // top]  11.9 us
    all_to_all x1, starting transfers between devices, shards(): lax.all_to_all(for_sending(sent_count[:, None]), 'expert', split_axis=0,...  8.11 us
    unnamed x1, blocking collectives  7.89 us
    reduce_sum x1, other arithmetic, shards(): jnp.sum(picked.reshape(tok_rows, top, returned.shape[2]).astype(jnp.float...  7.32 us
    unnamed x16, local copies, waits for them, and re-layouts  7.24 us
  transfers between devices with their start and end apart: 3, of which 2 were waited for; matrix products, arithmetic and copies ran while one was open for 9% of the time, Pallas kernels for 0%

commit v1 on v0

v1 whole, which is shorter than its diff:
```python
import jax
import jax.numpy as jnp
from jax import lax
from jax.sharding import PartitionSpec as P


def gram_of(rows):
    return lax.dot_general(rows, rows, (((0,), (0,)), ((), ())), preferred_element_type=jnp.float32)


def expert_pass(rows, w_gate, w_up, w_down):
    gate = jnp.dot(rows, w_gate, preferred_element_type=jnp.float32)
    up = jnp.dot(rows, w_up, preferred_element_type=jnp.float32)
    act = (jax.nn.silu(gate) * up).astype(jnp.bfloat16)
    gram_sum = gram_of(act)
    made = jnp.dot(act, w_down, preferred_element_type=jnp.float32).astype(jnp.bfloat16)
    return (gram_sum, made)


def small_gather(part, axis):
    size = lax.axis_size(axis)
    copies = jnp.broadcast_to(part[None], (size,) + part.shape)
    return lax.all_to_all(copies, axis, split_axis=0, concat_axis=0, tiled=True)


def shards(routes, probs, tokens, gate_weight, up_weight, down_weight):
    tok_rows, top = routes.shape
    ranks_total = lax.axis_size("expert")
    capacity = tok_rows * top // 2
    expert = lax.axis_index("expert")
    every_token = lax.all_gather(tokens, "expert", tiled=True)
    every_route = small_gather(routes, "expert")
    every_prob = small_gather(probs, "expert")
    names = every_route == expert
    named = jnp.any(names, axis=2).astype(jnp.int32)
    weight = jnp.sum(jnp.where(names, every_prob, 0.0), axis=2).reshape(ranks_total * tok_rows)
    within = jnp.cumsum(named, axis=1) - named
    per_device = jnp.sum(named, axis=1)
    before = jnp.cumsum(per_device) - per_device
    rank = within + before[:, None]
    kept = (named == 1) & (rank < capacity)
    count = jnp.minimum(jnp.sum(per_device), capacity)
    slot = jnp.where(kept, rank, -1).reshape(ranks_total * tok_rows)
    place = jnp.arange(capacity, dtype=jnp.int32)
    select = (place[:, None] == slot[None, :]).astype(jnp.bfloat16)
    rows = jnp.dot(select, every_token, preferred_element_type=jnp.float32).astype(jnp.bfloat16)
    gram_sum, made = expert_pass(rows, gate_weight[0], up_weight[0], down_weight[0])
    gram = gram_sum * (2.0 / count.astype(jnp.float32))
    spread = lax.dot_general(
        select, made, (((0,), (0,)), ((), ())), preferred_element_type=jnp.float32
    )
    partial = (spread * weight[:, None]).astype(jnp.bfloat16)
    mixed = lax.psum_scatter(partial, "expert", scatter_dimension=0, tiled=True)
    return (gram[None], mixed.astype(jnp.bfloat16))


def solution(mesh):
    placed = (
        P(("parts", "expert"), None),
        P(("parts", "expert"), None),
        P(("parts", "expert"), None),
        P("expert", None, None),
        P("expert", None, None),
        P("expert", None, None),
    )
    return jax.shard_map(
        shards,
        mesh=mesh,
        in_specs=placed,
        out_specs=(P(("parts", "expert"), None, None), P(("parts", "expert"), None)),
        check_vma=False,
    )
```

time: 329 us -> 222 us (0.67)
  the two profiles are of different devices: /device:TPU:15 before, /device:TPU:0 now
where the time goes in v1:
time: 222 us; the launch traced here: 221 us
  waiting for transfers between devices  159 us (72%)
  matrix products  26 us (12%)
  between operations  14.8 us (7%)
  blocking collectives  14.1 us (6%)
  starting transfers between devices  3.58 us (2%)
  local copies, waits for them, and re-layouts  2.4 us (1%)
    reduce_scatter x1, waiting for transfers between devices, shards(): mixed = lax.psum_scatter(partial, 'expert', scatter_dimension=0, tiled=True)  98.6 us
    all_gather x1, waiting for transfers between devices, shards(): every_token = lax.all_gather(tokens, 'expert', tiled=True)  51.9 us
    all_to_all x1, blocking collectives, small_gather(): return lax.all_to_all(copies, axis, split_axis=0, concat_axis=0, tiled=True)  14.1 us
    dot_general x1, matrix products, shards(): lax.dot_general(select, made, (((0,), (0,)), ((), ())), preferred_element...  9.52 us
    dot_general x1, matrix products, shards(): jnp.dot(select, every_token, preferred_element_type=jnp.float32)  8.22 us
    all_to_all x1, waiting for transfers between devices, small_gather(): return lax.all_to_all(copies, axis, split_axis=0, concat_axis=0, tiled=True)  8.17 us
  transfers between devices with their start and end apart: 3, of which 3 were waited for; matrix products, arithmetic and copies ran while one was open for 3% of the time, Pallas kernels for 0%

profile of v1, /device:TPU:0, one launch (start us, length us, event | category | flops | bytes accessed | tf_op | source)
XLA Modules:
  0.0 221.5 jit_solution(7681868332779929569)
XLA Ops:
  7.2 0.0 copy-start
  7.2 0.0 all-gather.2.cloned.1.call-start
  7.2 0.7 all-gather.2.cloned.1.call-update
  7.9 0.9 broadcast_in_dim.14
  8.8 14.1 %all_to_all.10 = s32[16,128,8]{1,2,0:T(8,128)S(1)} all-to-all(s32[16,128,8]{1,2,0:T(8,128)S(1)} %broadcast_in_dim.14), channel_id=1, replica_groups=mesh['parts'=2,'expert'=16] {'expert'}, dimensions={0} | all-to-all | bytes 131072 | tf_op jit(solution)/shard_map/all_to_all | solution.py:23
  22.9 1.3 broadcast_in_dim.28
  24.2 3.5 %all-to-all-start.1 = ((f32[16,128,8]{1,2,0:T(8,128)}), f32[16,128,8]{1,2,0:T(8,128)S(1)}, u32[]{:S(2)}, u32[]{:S(2)}) async-start(f32[16,128,8]{1,2,0:T(8,128)} %broadcast_in_dim.28), calls=%async_computation.1 | async-start | bytes 131072 | tf_op jit(solution)/shard_map/all_to_all | solution.py:23
  27.7 0.0 reduce-scatter.2.cloned.1.call-start
  27.8 8.2 %all-to-all-done.1 = f32[16,128,8]{1,2,0:T(8,128)S(1)} async-done(((f32[16,128,8]{1,2,0:T(8,128)}), f32[16,128,8]{1,2,0:T(8,128)S(1)}, u32[]{:S(2)}, u32[]{:S(2)}) %all-to-all-start.1) | async-done | bytes 65568 | tf_op jit(solution)/shard_map/all_to_all | solution.py:23
  36.0 0.6 convert_reduce_fusion
  36.6 0.1 copy.14
  36.8 0.1 reduce.1
  36.9 0.3 reduce_window_sum.18
  37.2 0.1 fusion.19
  37.3 51.9 %all-gather.2.cloned.1.call-done = bf16[2048,2048]{1,0:T(8,128)(2,1)} async-done(((bf16[128,2048]{1,0:T(8,128)(2,1)}), bf16[2048,2048]{1,0:T(8,128)(2,1)}) %all-gather.2.cloned.1.call-update) | async-done | bytes 8388624 | tf_op jit(solution)/shard_map/all_gather | solution.py:31
  89.1 0.0 copy-start.1
  89.1 8.2 %fusion.10 = bf16[512,2048]{1,0:T(8,128)(2,1)S(1)} fusion(bf16[2048,2048]{1,0:T(8,128)(2,1)} %all-gather.2.cloned.1.call-done, s32[2048]{0:T(1024)S(1)} %fusion.19), kind=kOutput, calls=%fused_computation.10 | convolution fusion | flops 4297064448 | bytes 10493952 | tf_op jit(solution)/shard_map/dot_general | solution.py:46
  97.4 0.0 copy-done.1
  97.4 0.0 copy-start.2
  97.4 1.8 fusion.5
  99.2 0.1 copy-done.2
  99.3 2.9 %multiply_convert_fusion.1 = bf16[512,768]{1,0:T(8,128)(2,1)} fusion(f32[512,768]{1,0:T(8,128)S(1)} %fusion.5, bf16[512,2048]{1,0:T(8,128)(2,1)S(1)} %fusion.10, bf16[1,2048,768]{2,1,0:T(8,128)(2,1)S(1)} %copy-done.2), kind=kOutput, calls=%fused_computation.14 | convolution fusion | flops 1612972032 | bytes 7602176 | tf_op jit(solution)/shard_map/dot_general | solution.py:13
  102.1 0.0 copy-done
  102.1 9.5 %multiply_convert_fusion = bf16[2048,2048]{1,0:T(8,128)(2,1)} fusion(f32[2048]{0:T(1024)S(1)} %bitcast.42, s32[2048]{0:T(1024)S(1)} %fusion.19, bf16[512,768]{1,0:T(8,128)(2,1)} %multiply_convert_fusion.1, bf16[1,768,2048]{2,1,0:T(8,128)(2,1)S(1)} %copy-done), kind=kOutput, calls=%fused_computation | convolution fusion | flops 5916065792 | bytes 12337152 | tf_op jit(solution)/shard_map/dot_general | solution.py:49
  111.7 0.0 reduce-scatter.2.cloned.1.call-update
  112.4 3.6 %multiply_bitcast_fusion = f32[1,768,768]{2,1,0:T(8,128)} fusion(bf16[512,768]{1,0:T(8,128)(2,1)} %multiply_convert_fusion.1, f32[]{:T(128)S(6)} %div.8), kind=kOutput, calls=%fused_computation.11 | convolution fusion | flops 604569600 | bytes 3145732 | tf_op jit(solution)/shard_map/dot_general | solution.py:8
  116.0 98.6 %reduce-scatter.2.cloned.1.call-done = bf16[128,2048]{1,0:T(8,128)(2,1)} async-done(((bf16[2048,2048]{1,0:T(8,128)(2,1)}), bf16[128,2048]{1,0:T(8,128)(2,1)}) %reduce-scatter.2.cloned.1.call-update) | async-done | bytes 524304 | tf_op jit(solution)/shard_map/reduce_scatter | solution.py:53
  (5 shorter events, 0.1 us)
Async XLA Ops:
  7.2 95.0 %copy-start = (bf16[1,768,2048]{2,1,0:T(8,128)(2,1)S(1)}, bf16[1,768,2048]{2,1,0:T(8,128)(2,1)}, u32[]{:S(2)}) copy-start(bf16[1,768,2048]{2,1,0:T(8,128)(2,1)} %param.11) | copy-start | bytes 9437188
  7.2 82.0 %all-gather.2.cloned.1.call-start = ((), (), s32[]{:S(2)}) async-start(), calls=%async_computation.3 | async-start | bytes 8912896 | tf_op jit(solution)/shard_map/all_gather | solution.py:31
  24.2 11.7 %all-to-all-start.1 = ((f32[16,128,8]{1,2,0:T(8,128)}), f32[16,128,8]{1,2,0:T(8,128)S(1)}, u32[]{:S(2)}, u32[]{:S(2)}) async-start(f32[16,128,8]{1,2,0:T(8,128)} %broadcast_in_dim.28), calls=%async_computation.1 | async-start | bytes 131072 | tf_op jit(solution)/shard_map/all_to_all | solution.py:23
  27.7 186.9 %reduce-scatter.2.cloned.1.call-start = ((), (), s32[]{:S(2)}) async-start(), calls=%async_computation.4 | async-start | bytes 8912896 | tf_op jit(solution)/shard_map/reduce_scatter | solution.py:53
  89.1 8.2 %copy-start.1 = (bf16[1,2048,768]{2,1,0:T(8,128)(2,1)S(1)}, bf16[1,2048,768]{2,1,0:T(8,128)(2,1)}, u32[]{:S(2)}) copy-start(bf16[1,2048,768]{2,1,0:T(8,128)(2,1)} %param.9) | copy-start | bytes 9437188
  97.4 1.9 copy-start.2
Sparse Core Ops, SparseCore 0:
  10.2 78.9 all-gather.1
  111.8 102.8 reduce-scatter.1

commit v2 on v1

v2 whole, which is shorter than its diff:
```python
import functools

import jax
import jax.numpy as jnp
from jax import lax
from jax.experimental import pallas as pl
from jax.experimental.pallas import tpu as pltpu
from jax.sharding import PartitionSpec as P


def gram_of(rows):
    return lax.dot_general(rows, rows, (((0,), (0,)), ((), ())), preferred_element_type=jnp.float32)


def expert_pass(rows, w_gate, w_up, w_down):
    gate = jnp.dot(rows, w_gate, preferred_element_type=jnp.float32)
    up = jnp.dot(rows, w_up, preferred_element_type=jnp.float32)
    act = (jax.nn.silu(gate) * up).astype(jnp.bfloat16)
    gram_sum = gram_of(act)
    made = jnp.dot(act, w_down, preferred_element_type=jnp.float32).astype(jnp.bfloat16)
    return (gram_sum, made)


def weights_for_me(routes, probs, experts):
    names = routes.T[None, :, :] == jnp.arange(experts, dtype=jnp.int32)[:, None, None]
    weight = jnp.sum(jnp.where(names, probs.T[None, :, :], 0.0), axis=1)
    mine = jnp.where(jnp.any(names, axis=1), weight, -1.0)
    return lax.all_to_all(mine, "expert", split_axis=0, concat_axis=0, tiled=True)


def summed(*parts):
    total = parts[0].astype(jnp.float32)
    for part in parts[1:]:
        total = total + part.astype(jnp.float32)
    return total.astype(jnp.bfloat16)


def plane_kernel(
    capacity, order, weight, x0, x1, x2, x3, w_gate, w_up, w_down,
    keep, give, act,
    x, rows, made, ranks, gates, ups, downs, x_sem, gate_sem, up_sem, down_sem,
):
    blocks, tok = weight.shape
    features = x.shape[1]
    hidden = act.shape[1]
    slots = act.shape[0]
    wide = 256
    copies = [
        pltpu.make_async_copy(block, x.at[pl.ds(i * tok, tok), :], x_sem.at[i])
        for i, block in enumerate((x0, x1, x2, x3))
    ]
    for copy in copies:
        copy.start()
    gate_copies, up_copies = [], []
    for i in range(hidden // wide):
        span = pl.ds(i * wide, wide)
        gate_copies.append(pltpu.make_async_copy(w_gate.at[:, span], gates.at[i], gate_sem.at[i]))
        up_copies.append(pltpu.make_async_copy(w_up.at[:, span], ups.at[i], up_sem.at[i]))
        gate_copies[i].start()
        up_copies[i].start()
    down_copy = pltpu.make_async_copy(w_down, downs, down_sem)
    down_copy.start()

    named = (weight[...] >= 0.0).astype(jnp.float32)
    lane = lax.broadcasted_iota(jnp.int32, (tok, tok), 0)
    below = (lane < lax.broadcasted_iota(jnp.int32, (tok, tok), 1)).astype(jnp.float32)
    within = jnp.dot(named, below, preferred_element_type=jnp.float32)
    totals = jnp.broadcast_to(jnp.sum(named, axis=1, keepdims=True), (blocks, tok))
    row = lax.broadcasted_iota(jnp.int32, (blocks, blocks), 0)
    earlier = (lax.broadcasted_iota(jnp.int32, (blocks, blocks), 1) < row).astype(jnp.float32)
    before = jnp.dot(earlier, totals, preferred_element_type=jnp.float32)
    rank = within + before
    kept = (named > 0.0) & (rank < capacity)
    first = order[0] // 4 * 4
    block_row = lax.broadcasted_iota(jnp.int32, (blocks, tok), 0)
    start = jnp.sum(jnp.where(block_row == first, before, 0.0), axis=0, keepdims=True)
    ranks[...] = jnp.where(kept, rank - start, -1.0)

    places = [ranks[pl.ds(order[i], 1), :] for i in range(4)]
    shares = [weight[pl.ds(order[i], 1), :] for i in range(4)]
    place = jnp.concatenate(places, axis=1)
    share = jnp.concatenate(shares, axis=1)
    slot = lax.broadcasted_iota(jnp.int32, (slots, 4 * tok), 0).astype(jnp.float32)
    hits = slot == place
    scale = jnp.sum(jnp.where(hits, share, 0.0), axis=1, keepdims=True)
    select = hits.astype(jnp.float32).astype(jnp.bfloat16)
    for copy in copies:
        copy.wait()
    for i in range(features // 512):
        span = pl.ds(i * 512, 512)
        rows[:, span] = jnp.dot(
            select, x[:, span], preferred_element_type=jnp.float32
        ).astype(jnp.bfloat16)
    for i in range(hidden // wide):
        gate_copies[i].wait()
        up_copies[i].wait()
        gate = jnp.dot(rows[...], gates[i], preferred_element_type=jnp.float32)
        up = jnp.dot(rows[...], ups[i], preferred_element_type=jnp.float32)
        act[:, pl.ds(i * wide, wide)] = (gate / (1.0 + jnp.exp(-gate)) * up).astype(jnp.bfloat16)
    down_copy.wait()
    back = select.T
    for i in range(features // 512):
        span = pl.ds(i * 512, 512)
        result = jnp.dot(act[...], downs[:, span], preferred_element_type=jnp.float32)
        made[...] = (result * scale).astype(jnp.bfloat16)
        spread = jnp.dot(back, made[...], preferred_element_type=jnp.float32).astype(jnp.bfloat16)
        keep[:, span] = spread[: 2 * tok]
        give[:, span] = spread[2 * tok :]


def plane_pass(order, weight, xs, w_gate, w_up, w_down, slots, capacity):
    tok, features = xs[0].shape
    hidden = w_gate.shape[1]
    half = jax.ShapeDtypeStruct((2 * tok, features), jnp.bfloat16)
    rows = 4 * slots
    flops = 2 * rows * (3 * features * hidden + 8 * tok * features)
    moved = 2 * (3 * features * hidden + 8 * tok * features)
    return pl.pallas_call(
        functools.partial(plane_kernel, capacity),
        out_shape=(half, half, jax.ShapeDtypeStruct((rows, hidden), jnp.bfloat16)),
        in_specs=[pl.BlockSpec(memory_space=pltpu.SMEM), pl.BlockSpec(memory_space=pltpu.VMEM)]
        + [pl.BlockSpec(memory_space=pl.ANY)] * 7,
        out_specs=[pl.BlockSpec(memory_space=pltpu.VMEM)] * 3,
        scratch_shapes=[
            pltpu.VMEM((4 * tok, features), jnp.bfloat16),
            pltpu.VMEM((rows, features), jnp.bfloat16),
            pltpu.VMEM((rows, 512), jnp.bfloat16),
            pltpu.VMEM(weight.shape, jnp.float32),
            pltpu.VMEM((hidden // 256, features, 256), jnp.bfloat16),
            pltpu.VMEM((hidden // 256, features, 256), jnp.bfloat16),
            pltpu.VMEM((hidden, features), jnp.bfloat16),
            pltpu.SemaphoreType.DMA((4,)),
            pltpu.SemaphoreType.DMA((hidden // 256,)),
            pltpu.SemaphoreType.DMA((hidden // 256,)),
            pltpu.SemaphoreType.DMA,
        ],
        compiler_params=pltpu.CompilerParams(vmem_limit_bytes=32 * 1024 * 1024),
        cost_estimate=pl.CostEstimate(
            flops=flops, bytes_accessed=moved, transcendentals=rows * hidden
        ),
    )(order, weight, *xs, w_gate, w_up, w_down)


def pairs_of(size, planes, step):
    found = []
    for device in range(size):
        z, y, core = device // 4, device // 2 % 2, device % 2
        if z in planes:
            z, y, core = step(z, y, core)
            found.append((device, (z * 2 + y) * 2 + core))
    return found


def staged(routes, probs, tokens, w_gate, w_up, w_down):
    tok, top = routes.shape
    size = lax.axis_size("expert")
    slots = 5 * tok * top // (4 * size)
    capacity = tok * top // 2
    me = lax.axis_index("expert")
    z, y, core = me // 4, me // 2 % 2, me % 2
    middle = (z == 1) | (z == 2)
    every = (0, 1, 2, 3)

    def moved(array, planes, step):
        return lax.ppermute(array, "expert", pairs_of(size, planes, step))

    def pair(z, y, core):
        return z ^ 1, y, core

    def across(z, y, core):
        return 3 - z, y, core

    def column(z, y, core):
        return z, 1 - y, core

    def sibling(z, y, core):
        return z, y, 1 - core

    weight = weights_for_me(routes, probs, size)

    held_1 = moved(tokens, every, pair)
    crossed = moved(tokens, (1, 2), across)
    outward = moved(crossed, (1, 2), pair)
    far_mid = moved(held_1, (1, 2), across)
    far_end = moved(far_mid, (1, 2), pair)
    held = [
        tokens,
        held_1,
        jnp.where(middle, crossed, outward),
        jnp.where(middle, far_mid, far_end),
    ]
    planes = [z, z ^ 1, jnp.where(middle, 3 - z, (3 - z) ^ 1), jnp.where(middle, (3 - z) ^ 1, 3 - z)]
    keeps, gives, acts = [], [], []
    for mine, plane in zip(held, planes):
        other = moved(mine, every, column)
        xs = (mine, other, moved(mine, every, sibling), moved(other, every, sibling))
        base = plane * 4
        order = jnp.stack(
            [
                base + y * 2 + core,
                base + (1 - y) * 2 + core,
                base + y * 2 + 1 - core,
                base + (1 - y) * 2 + 1 - core,
            ]
        ).astype(jnp.int32)
        keep, give, act = plane_pass(order, weight, xs, w_gate, w_up, w_down, slots, capacity)
        keeps.append(keep)
        gives.append(give)
        acts.append(act)

    reduced = [None] * 4
    for k in (3, 2, 1, 0):
        came = moved(gives[k], every, sibling)
        send = summed(keeps[k][tok:], came[tok:])
        crossed = moved(send, every, column)
        reduced[k] = (keeps[k][:tok], came[:tok], crossed)
    far_in = moved(summed(*reduced[3]), (0, 3), pair)
    far_across = moved(summed(*reduced[3], far_in), (1, 2), across)
    near_in = moved(summed(*reduced[2]), (0, 3), pair)
    near_across = moved(summed(*reduced[2], near_in), (1, 2), across)
    last = moved(summed(*reduced[1], far_across), every, pair)
    mixed = summed(*reduced[0], last, near_across)

    count = jnp.minimum(jnp.sum((weight >= 0.0).astype(jnp.float32)), float(capacity))
    gram = gram_of(jnp.concatenate(acts, axis=0)) * (2.0 / count)
    return gram[None], mixed


def gathered(routes, probs, tokens, w_gate, w_up, w_down):
    tok_rows, top = routes.shape
    size = lax.axis_size("expert")
    capacity = tok_rows * top // 2
    every_token = lax.all_gather(tokens, "expert", tiled=True)
    weight = weights_for_me(routes, probs, size)
    named = (weight >= 0.0).astype(jnp.int32)
    within = jnp.cumsum(named, axis=1) - named
    per_device = jnp.sum(named, axis=1)
    before = jnp.cumsum(per_device) - per_device
    rank = within + before[:, None]
    kept = (named == 1) & (rank < capacity)
    count = jnp.minimum(jnp.sum(per_device), capacity)
    slot = jnp.where(kept, rank, -1).reshape(size * tok_rows)
    place = jnp.arange(capacity, dtype=jnp.int32)
    select = (place[:, None] == slot[None, :]).astype(jnp.bfloat16)
    rows = jnp.dot(select, every_token, preferred_element_type=jnp.float32).astype(jnp.bfloat16)
    gram_sum, made = expert_pass(rows, w_gate, w_up, w_down)
    gram = gram_sum * (2.0 / count.astype(jnp.float32))
    spread = lax.dot_general(
        select, made, (((0,), (0,)), ((), ())), preferred_element_type=jnp.float32
    )
    partial = (spread * weight.reshape(size * tok_rows, 1)).astype(jnp.bfloat16)
    mixed = lax.psum_scatter(partial, "expert", scatter_dimension=0, tiled=True)
    return gram[None], mixed.astype(jnp.bfloat16)


def shards(routes, probs, tokens, gate_weight, up_weight, down_weight):
    body = staged if lax.axis_size("expert") == 16 else gathered
    return body(routes, probs, tokens, gate_weight[0], up_weight[0], down_weight[0])


def solution(mesh):
    placed = (
        P(("parts", "expert"), None),
        P(("parts", "expert"), None),
        P(("parts", "expert"), None),
        P("expert", None, None),
        P("expert", None, None),
        P("expert", None, None),
    )
    return jax.shard_map(
        shards,
        mesh=mesh,
        in_specs=placed,
        out_specs=(P(("parts", "expert"), None, None), P(("parts", "expert"), None)),
        check_vma=False,
    )
```

time: 222 us -> 192 us (0.86)
  waiting for transfers between devices: 159 us -> 84.6 us
  starting transfers between devices: 3.58 us -> 38.5 us
  Pallas kernels: 0 us -> 32.6 us
  matrix products: 26 us -> 3.22 us
  local copies, waits for them, and re-layouts: 2.4 us -> 18.4 us
  blocking collectives: 14.1 us -> 0 us
  between operations: 14.8 us -> 1.73 us
  other arithmetic: 1.22 us -> 11.9 us
    reduce_scatter x1 -> x0, waiting for transfers between devices: 98.6 us -> none  [shards(): mixed = lax.psum_scatter(partial, 'expert', scatter_dimension=0, tiled=True)]
    ppermute x0 -> x30, waiting for transfers between devices: none -> 84.6 us  [moved(): return lax.ppermute(array, 'expert', pairs_of(size, planes, step))]
    all_gather x1 -> x0, waiting for transfers between devices: 51.9 us -> none  [shards(): every_token = lax.all_gather(tokens, 'expert', tiled=True)]
    ppermute x0 -> x30, starting transfers between devices: none -> 33.6 us  [moved(): return lax.ppermute(array, 'expert', pairs_of(size, planes, step))]
    pallas_call x0 -> x4, Pallas kernels: none -> 32.6 us  [plane_pass(): pl.pallas_call(functools.partial(plane_kernel, capacity), out_shape=(half...]
    dot_general x4 -> x0, matrix products: 22.4 us -> none  [the longest x1 9.52 us: shards(): lax.dot_general(select, made, (((0,), (0,)), ((), ())), preferred_element...]
    unnamed x6 -> x50, local copies, waits for them, and re-layouts: 0.11 us -> 18.4 us
    all_to_all x1 -> x0, blocking collectives: 14.1 us -> none  [small_gather(): return lax.all_to_all(copies, axis, split_axis=0, concat_axis=0, tiled=True)]
  transfers between devices with their start and end apart: 3 -> 31, of which waited for: 3 -> 10; matrix products, arithmetic and copies ran while one was open for 3% -> 7% of each run, Pallas kernels for 0% -> 17%
where the time goes in v2:
time: 192 us; the launch traced here: 191 us
  waiting for transfers between devices  84.6 us (44%)
  starting transfers between devices  38.5 us (20%)
  Pallas kernels  32.6 us (17%)
  local copies, waits for them, and re-layouts  18.4 us (10%)
  other arithmetic  11.9 us (6%)
  matrix products  3.22 us (2%)
    ppermute x30, waiting for transfers between devices, moved(): return lax.ppermute(array, 'expert', pairs_of(size, planes, step))  84.6 us
    ppermute x30, starting transfers between devices, moved(): return lax.ppermute(array, 'expert', pairs_of(size, planes, step))  33.6 us
    pallas_call x4, Pallas kernels, plane_pass(): pl.pallas_call(functools.partial(plane_kernel, capacity), out_shape=(half...  32.6 us
    unnamed x50, local copies, waits for them, and re-layouts  18.4 us
    convert_element_type x10, other arithmetic, summed(): return total.astype(jnp.bfloat16)  10.2 us
    all_to_all x1, starting transfers between devices, weights_for_me(): lax.all_to_all(mine, 'expert', split_axis=0, concat_axis=0, tiled=True)  4.92 us
  transfers between devices with their start and end apart: 31, of which 10 were waited for; matrix products, arithmetic and copies ran while one was open for 7% of the time, Pallas kernels for 17%

profile of v2, /device:TPU:0, one launch (start us, length us, event | category | flops | bytes accessed | tf_op | source)
XLA Modules:
  0.0 191.0 jit_solution(18044807652058725495)
XLA Ops:
  0.6 3.1 %collective-permute-start.3 = (bf16[128,2048]{1,0:T(8,128)(2,1)}, bf16[128,2048]{1,0:T(8,128)(2,1)}, u32[]{:S(2)}, u32[]{:S(2)}) collective-permute-start(bf16[128,2048]{1,0:T(8,128)(2,1)} %x0.1), channel_id=1, source_target_pairs={{0,4},{1,5},{2,6},{3,7},{4,0},{5,1},{6,2},{7,3},{8,12},{9,13},{10,... | collective-permute-start | bytes 1572872 | tf_op jit(solution)/shard_map/ppermute | solution.py:165
  3.7 12.2 %collective-permute-done.3.x0 = bf16[128,2048]{1,0:T(8,128)(2,1)} collective-permute-done((bf16[128,2048]{1,0:T(8,128)(2,1)}, bf16[128,2048]{1,0:T(8,128)(2,1)}, u32[]{:S(2)}, u32[]{:S(2)}) %collective-permute-start.3) | collective-permute-done | bytes 524320 | tf_op jit(solution)/shard_map/ppermute | solution.py:165
  16.0 0.7 collective-permute-start.12
  16.7 0.7 collective-permute-start.7
  17.4 1.3 collective-permute-start.13
  18.7 1.3 collective-permute-start.8
  20.0 24.0 %collective-permute-done.13 = bf16[128,2048]{1,0:T(8,128)(2,1)S(1)} collective-permute-done((bf16[128,2048]{1,0:T(8,128)(2,1)S(1)}, bf16[128,2048]{1,0:T(8,128)(2,1)S(1)}, u32[]{:S(2)}, u32[]{:S(2)}) %collective-permute-start.13) | collective-permute-done | bytes 524320 | tf_op jit(solution)/shard_map/ppermute | solution.py:165
  44.1 1.6 collective-permute-start.14
  45.7 0.5 collective-permute-start
  46.2 9.1 %collective-permute-done.8 = bf16[128,2048]{1,0:T(8,128)(2,1)S(1)} collective-permute-done((bf16[128,2048]{1,0:T(8,128)(2,1)S(1)}, bf16[128,2048]{1,0:T(8,128)(2,1)S(1)}, u32[]{:S(2)}, u32[]{:S(2)}) %collective-permute-start.8) | collective-permute-done | bytes 524320 | tf_op jit(solution)/shard_map/ppermute | solution.py:165
  55.3 1.6 collective-permute-start.9
  56.9 2.1 %collective-permute-done.14.x1 = bf16[128,2048]{1,0:T(8,128)(2,1)S(1)} collective-permute-done((bf16[128,2048]{1,0:T(8,128)(2,1)S(1)}, bf16[128,2048]{1,0:T(8,128)(2,1)S(1)}, u32[]{:S(2)}, u32[]{:S(2)}) %collective-permute-start.14) | collective-permute-done | bytes 524320 | tf_op jit(solution)/shard_map/ppermute | solution.py:165
  59.0 0.8 copy-done.7
  59.9 0.6 broadcast_select_fusion.2
  60.5 4.9 %all-to-all-start = ((f32[16,1,128]{2,1,0:T(1,128)}), f32[16,1,128]{2,1,0:T(1,128)S(1)}, u32[]{:S(2)}, u32[]{:S(2)}) async-start(f32[16,1,128]{2,1,0:T(1,128)} %bitcast.7), calls=%async_computation | async-start | bytes 16384 | tf_op jit(solution)/shard_map/all_to_all | solution.py:28
  65.4 1.9 collective-permute-start.4
  67.4 14.2 %collective-permute-done.9.x1 = bf16[128,2048]{1,0:T(8,128)(2,1)} collective-permute-done((bf16[128,2048]{1,0:T(8,128)(2,1)S(1)}, bf16[128,2048]{1,0:T(8,128)(2,1)}, u32[]{:S(2)}, u32[]{:S(2)}) %collective-permute-start.9) | collective-permute-done | bytes 524320 | tf_op jit(solution)/shard_map/ppermute | solution.py:165
  81.6 0.8 copy-done.9
  82.4 0.5 collective-permute-start.11
  82.9 0.8 copy-done.11
  83.7 1.9 copy-done
  85.6 1.9 copy-done.2
  87.5 1.9 copy-done.4
  89.3 1.0 copy-done.8
  90.4 1.0 copy-done.10
  91.4 1.0 copy-done.12
  92.5 8.0 %shard_map.80 = (bf16[256,2048]{1,0:T(8,128)(2,1)S(1)}, bf16[256,2048]{1,0:T(8,128)(2,1)S(1)}, bf16[320,768]{1,0:T(8,128)(2,1)S(1)}) custom-call(s32[4]{0:T(128)S(1)} %pad_add_fusion.3.order, f32[16,128]{1,0:T(8,128)S(1)} %bitcast.27, bf16[128,2048]{1,0:T(8,128)(2,1)S(1)} %broadcast_select_fusion.x0, bf16[128,2048]{1,0:T(8,128)(2,1)S(1)} %copy-done.8, ...), custom_call_target="tpu_custom_call" | custom-call | flops 4362076160 | bytes 13631488 | tf_op jit(solution)/shard_map/pallas_call | solution.py:118
  100.5 0.8 copy-done.13
  101.4 0.5 collective-permute-start.5
  102.2 0.4 collective-permute-start.1
  102.7 1.9 copy-done.1
  104.6 1.9 copy-done.3
  106.5 1.9 copy-done.5
  108.3 8.3 %shard_map.79 = (bf16[256,2048]{1,0:T(8,128)(2,1)S(1)}, bf16[256,2048]{1,0:T(8,128)(2,1)S(1)}, bf16[320,768]{1,0:T(8,128)(2,1)S(1)}) custom-call(s32[4]{0:T(128)S(1)} %pad_add_fusion.2.order, f32[16,128]{1,0:T(8,128)S(1)} %bitcast.28, bf16[128,2048]{1,0:T(8,128)(2,1)S(1)} %broadcast_select_fusion.1.x0, bf16[128,2048]{1,0:T(8,128)(2,1)} %collective-permute-done.9.x1, ...), custom_call_target="tpu_custom_call" | custom-call | flops 4362076160 | bytes 13631488 | tf_op jit(solution)/shard_map/pallas_call | solution.py:118
  116.6 0.8 copy-done.15
  117.4 0.4 collective-permute-start.26
  117.8 8.4 %shard_map.78 = (bf16[256,2048]{1,0:T(8,128)(2,1)S(1)}, bf16[256,2048]{1,0:T(8,128)(2,1)S(1)}, bf16[320,768]{1,0:T(8,128)(2,1)S(1)}) custom-call(s32[4]{0:T(128)S(1)} %pad_add_fusion.1.order, f32[16,128]{1,0:T(8,128)S(1)} %bitcast.29, bf16[128,2048]{1,0:T(8,128)(2,1)} %collective-permute-done.3.x0, bf16[128,2048]{1,0:T(8,128)(2,1)} %collective-permute-done.4.x1, ...), custom_call_target="tpu_custom_call" | custom-call | flops 4362076160 | bytes 13631488 | tf_op jit(solution)/shard_map/pallas_call | solution.py:118
  126.2 0.2 collective-permute-start.19
  126.4 1.2 add_convert_fusion.5
  127.6 1.6 collective-permute-start.22
  129.2 8.0 %shard_map.77 = (bf16[256,2048]{1,0:T(8,128)(2,1)S(1)}, bf16[256,2048]{1,0:T(8,128)(2,1)S(1)}, bf16[320,768]{1,0:T(8,128)(2,1)S(1)}) custom-call(s32[4]{0:T(128)S(1)} %pad_add_fusion.order, f32[16,128]{1,0:T(8,128)S(1)} %bitcast.30, bf16[128,2048]{1,0:T(8,128)(2,1)S(1)} %copy-done.6, bf16[128,2048]{1,0:T(8,128)(2,1)} %collective-permute-done.x1, ...), custom_call_target="tpu_custom_call" | custom-call | flops 4362076160 | bytes 13631488 | tf_op jit(solution)/shard_map/pallas_call | solution.py:118
  137.2 0.2 collective-permute-start.17
  137.5 0.6 collective-permute-start.27
  138.1 4.3 %collective-permute-done.22 = bf16[128,2048]{1,0:T(8,128)(2,1)S(1)} collective-permute-done((bf16[128,2048]{1,0:T(8,128)(2,1)S(1)}, bf16[128,2048]{1,0:T(8,128)(2,1)S(1)}, u32[]{:S(2)}, u32[]{:S(2)}) %collective-permute-start.22) | collective-permute-done | bytes 524320 | tf_op jit(solution)/shard_map/ppermute | solution.py:165
  142.4 1.3 fusion.10
  143.7 3.2 %collective-permute-start.23 = (bf16[128,2048]{1,0:T(8,128)(2,1)S(1)}, bf16[128,2048]{1,0:T(8,128)(2,1)S(1)}, u32[]{:S(2)}, u32[]{:S(2)}) collective-permute-start(bf16[128,2048]{1,0:T(8,128)(2,1)S(1)} %fusion.10), channel_id=1, source_target_pairs={{0,4},{1,5},{2,6},{3,7},{12,8},{13,9},{14,10},{15,11},{16,20},{17,... | collective-permute-start | bytes 1572872 | tf_op jit(solution)/shard_map/ppermute | solution.py:165
  147.0 1.6 collective-permute-start.20
  148.6 5.0 %collective-permute-done.27 = bf16[128,2048]{1,0:T(8,128)(2,1)S(1)} collective-permute-done((bf16[128,2048]{1,0:T(8,128)(2,1)S(1)}, bf16[128,2048]{1,0:T(8,128)(2,1)S(1)}, u32[]{:S(2)}, u32[]{:S(2)}) %collective-permute-start.27) | collective-permute-done | bytes 524320 | tf_op jit(solution)/shard_map/ppermute | solution.py:165
  153.6 0.2 fusion.11
  153.9 3.2 %collective-permute-start.28 = (bf16[128,2048]{1,0:T(8,128)(2,1)S(1)}, bf16[128,2048]{1,0:T(8,128)(2,1)S(1)}, u32[]{:S(2)}, u32[]{:S(2)}) collective-permute-start(bf16[128,2048]{1,0:T(8,128)(2,1)S(1)} %fusion.11), channel_id=1, source_target_pairs={{0,4},{1,5},{2,6},{3,7},{12,8},{13,9},{14,10},{15,11},{16,20},{17,... | collective-permute-start | bytes 1572872 | tf_op jit(solution)/shard_map/ppermute | solution.py:165
  157.1 1.2 collective-permute-done.23
  158.3 1.4 add_convert_fusion.4
  159.7 0.7 collective-permute-start.24
  160.5 0.9 add_convert_fusion.7
  161.4 1.5 collective-permute-start.18
  162.9 5.7 %collective-permute-done.28 = bf16[128,2048]{1,0:T(8,128)(2,1)S(1)} collective-permute-done((bf16[128,2048]{1,0:T(8,128)(2,1)S(1)}, bf16[128,2048]{1,0:T(8,128)(2,1)S(1)}, u32[]{:S(2)}, u32[]{:S(2)}) %collective-permute-start.28) | collective-permute-done | bytes 524320 | tf_op jit(solution)/shard_map/ppermute | solution.py:165
  168.6 1.1 add_convert_fusion.1
  169.7 1.5 collective-permute-start.29
  171.2 1.1 add_convert_fusion.3
  172.3 4.7 %collective-permute-start.25 = (bf16[128,2048]{1,0:T(8,128)(2,1)}, bf16[128,2048]{1,0:T(8,128)(2,1)}, u32[]{:S(2)}, u32[]{:S(2)}) collective-permute-start(bf16[128,2048]{1,0:T(8,128)(2,1)} %add_convert_fusion.3), channel_id=1, source_target_pairs={{0,4},{1,5},{2,6},{3,7},{4,0},{5,1},{6,2},{7,3},{8,12},{9,13},{10,... | collective-permute-start | bytes 1572872 | tf_op jit(solution)/shard_map/ppermute | solution.py:165
  177.1 0.6 convert_reduce_fusion
  178.4 3.2 %multiply_bitcast_fusion = f32[1,768,768]{2,1,0:T(8,128)} fusion(f32[]{:T(128)S(6)} %div.24, bf16[320,768]{1,0:T(8,128)(2,1)S(1)} %copy-done.14, bf16[320,768]{1,0:T(8,128)(2,1)S(1)} %copy-done.16, bf16[320,768]{1,0:T(8,128)(2,1)S(1)} %copy-done.18, bf16[320,768]{1,0:T(8,128)(2,1)S(1)} %copy-done.20), kind=kOutput, calls=%fused_computation | convolution fusion | flops 1518403584 | bytes 4325380 | tf_op jit(solution)/shard_map/dot_general | solution.py:12
  181.6 6.8 %collective-permute-done.25 = bf16[128,2048]{1,0:T(8,128)(2,1)} collective-permute-done((bf16[128,2048]{1,0:T(8,128)(2,1)}, bf16[128,2048]{1,0:T(8,128)(2,1)}, u32[]{:S(2)}, u32[]{:S(2)}) %collective-permute-start.25) | collective-permute-done | bytes 524320 | tf_op jit(solution)/shard_map/ppermute | solution.py:165
  188.4 2.6 %add_convert_fusion = bf16[128,2048]{1,0:T(8,128)(2,1)} fusion(bf16[128,2048]{1,0:T(8,128)(2,1)} %collective-permute-done.29, bf16[128,2048]{1,0:T(8,128)(2,1)} %collective-permute-done.25, bf16[128,2048]{1,0:T(8,128)(2,1)} %collective-permute-done.18, bf16[256,2048]{1,0:T(8,128)(2,1)S(1)} %copy-done.22, bf16[256,2048]{1,0:T(8,128)(2,1)S(1)} %get-tuple-element.18), kind=kLoop, calls=%fused_computation.9 | loop fusion | flops 2621440 | bytes 3145728 | tf_op jit(solution)/shard_map/convert_element_type | solution.py:35
  (73 shorter events, 1.1 us)
Async XLA Ops:
  0.6 59.2 %copy-start.23 = (s32[128,8]{0,1:T(8,128)S(1)}, s32[128,8]{0,1:T(8,128)}, u32[]{:S(2)}) copy-start(s32[128,8]{0,1:T(8,128)} %param.6) | copy-start | bytes 12292
  0.6 59.2 %copy-start.24 = (f32[128,8]{0,1:T(8,128)S(1)}, f32[128,8]{0,1:T(8,128)}, u32[]{:S(2)}) copy-start(f32[128,8]{0,1:T(8,128)} %param.7) | copy-start | bytes 12292
  0.6 15.3 %collective-permute-start.3 = (bf16[128,2048]{1,0:T(8,128)(2,1)}, bf16[128,2048]{1,0:T(8,128)(2,1)}, u32[]{:S(2)}, u32[]{:S(2)}) collective-permute-start(bf16[128,2048]{1,0:T(8,128)(2,1)} %x0.1), channel_id=1, source_target_pairs={{0,4},{1,5},{2,6},{3,7},{4,0},{5,1},{6,2},{7,3},{8,12},{9,13},{10,... | collective-permute-start | bytes 1572872 | tf_op jit(solution)/shard_map/ppermute | solution.py:165
  16.0 1.4 collective-permute-start.12
  16.7 2.0 %collective-permute-start.7 = (bf16[128,2048]{1,0:T(8,128)(2,1)}, bf16[128,2048]{1,0:T(8,128)(2,1)S(1)}, u32[]{:S(2)}, u32[]{:S(2)}) collective-permute-start(bf16[128,2048]{1,0:T(8,128)(2,1)} %x0.1), channel_id=1, source_target_pairs={{4,8},{5,9},{6,10},{7,11},{8,4},{9,5},{10,6},{11,7},{20,24},{21,25... | collective-permute-start | bytes 1572872 | tf_op jit(solution)/shard_map/ppermute | solution.py:165
  17.4 26.6 %collective-permute-start.13 = (bf16[128,2048]{1,0:T(8,128)(2,1)S(1)}, bf16[128,2048]{1,0:T(8,128)(2,1)S(1)}, u32[]{:S(2)}, u32[]{:S(2)}) collective-permute-start(bf16[128,2048]{1,0:T(8,128)(2,1)S(1)} %collective-permute-done.12), channel_id=1, source_target_pairs={{4,0},{5,1},{6,2},{7,3},{8,12},{9,13},{10,14},{11,15},{20,16},{21,... | collective-permute-start | bytes 1572872 | tf_op jit(solution)/shard_map/ppermute | solution.py:165
  18.7 36.5 %collective-permute-start.8 = (bf16[128,2048]{1,0:T(8,128)(2,1)S(1)}, bf16[128,2048]{1,0:T(8,128)(2,1)S(1)}, u32[]{:S(2)}, u32[]{:S(2)}) collective-permute-start(bf16[128,2048]{1,0:T(8,128)(2,1)S(1)} %collective-permute-done.7), channel_id=1, source_target_pairs={{4,0},{5,1},{6,2},{7,3},{8,12},{9,13},{10,14},{11,15},{20,16},{21,... | collective-permute-start | bytes 1572872 | tf_op jit(solution)/shard_map/ppermute | solution.py:165
  44.1 14.9 %collective-permute-start.14 = (bf16[128,2048]{1,0:T(8,128)(2,1)S(1)}, bf16[128,2048]{1,0:T(8,128)(2,1)S(1)}, u32[]{:S(2)}, u32[]{:S(2)}) collective-permute-start(bf16[128,2048]{1,0:T(8,128)(2,1)S(1)} %broadcast_select_fusion.x0), channel_id=1, source_target_pairs={{0,2},{1,3},{2,0},{3,1},{4,6},{5,7},{6,4},{7,5},{8,10},{9,11},{10,... | collective-permute-start | bytes 1572872 | tf_op jit(solution)/shard_map/ppermute | solution.py:165
  45.7 55.7 %collective-permute-start = (bf16[128,2048]{1,0:T(8,128)(2,1)}, bf16[128,2048]{1,0:T(8,128)(2,1)}, u32[]{:S(2)}, u32[]{:S(2)}) collective-permute-start(bf16[128,2048]{1,0:T(8,128)(2,1)} %x0.1), channel_id=1, source_target_pairs={{0,2},{1,3},{2,0},{3,1},{4,6},{5,7},{6,4},{7,5},{8,10},{9,11},{10,... | collective-permute-start | bytes 1572872 | tf_op jit(solution)/shard_map/ppermute | solution.py:165
  55.3 26.3 %collective-permute-start.9 = (bf16[128,2048]{1,0:T(8,128)(2,1)S(1)}, bf16[128,2048]{1,0:T(8,128)(2,1)}, u32[]{:S(2)}, u32[]{:S(2)}) collective-permute-start(bf16[128,2048]{1,0:T(8,128)(2,1)S(1)} %broadcast_select_fusion.1.x0), channel_id=1, source_target_pairs={{0,2},{1,3},{2,0},{3,1},{4,6},{5,7},{6,4},{7,5},{8,10},{9,11},{10,... | collective-permute-start | bytes 1572872 | tf_op jit(solution)/shard_map/ppermute | solution.py:165
  56.9 24.7 %collective-permute-start.15 = (bf16[128,2048]{1,0:T(8,128)(2,1)S(1)}, bf16[128,2048]{1,0:T(8,128)(2,1)S(1)}, u32[]{:S(2)}, u32[]{:S(2)}) collective-permute-start(bf16[128,2048]{1,0:T(8,128)(2,1)S(1)} %broadcast_select_fusion.x0), channel_id=1, source_target_pairs={{0,1},{1,0},{2,3},{3,2},{4,5},{5,4},{6,7},{7,6},{8,9},{9,8},{10,11... | collective-permute-start | bytes 1572872 | tf_op jit(solution)/shard_map/ppermute | solution.py:165
  59.0 23.9 %collective-permute-start.16 = (bf16[128,2048]{1,0:T(8,128)(2,1)S(1)}, bf16[128,2048]{1,0:T(8,128)(2,1)S(1)}, u32[]{:S(2)}, u32[]{:S(2)}) collective-permute-start(bf16[128,2048]{1,0:T(8,128)(2,1)S(1)} %collective-permute-done.14.x1), channel_id=1, source_target_pairs={{0,1},{1,0},{2,3},{3,2},{4,5},{5,4},{6,7},{7,6},{8,9},{9,8},{10,11... | collective-permute-start | bytes 1572872 | tf_op jit(solution)/shard_map/ppermute | solution.py:165
  59.0 0.8 copy-start.7
  60.5 22.4 %all-to-all-start = ((f32[16,1,128]{2,1,0:T(1,128)}), f32[16,1,128]{2,1,0:T(1,128)S(1)}, u32[]{:S(2)}, u32[]{:S(2)}) async-start(f32[16,1,128]{2,1,0:T(1,128)} %bitcast.7), calls=%async_computation | async-start | bytes 16384 | tf_op jit(solution)/shard_map/all_to_all | solution.py:28
  65.4 36.5 %collective-permute-start.4 = (bf16[128,2048]{1,0:T(8,128)(2,1)}, bf16[128,2048]{1,0:T(8,128)(2,1)}, u32[]{:S(2)}, u32[]{:S(2)}) collective-permute-start(bf16[128,2048]{1,0:T(8,128)(2,1)} %collective-permute-done.3.x0), channel_id=1, source_target_pairs={{0,2},{1,3},{2,0},{3,1},{4,6},{5,7},{6,4},{7,5},{8,10},{9,11},{10,... | collective-permute-start | bytes 1572872 | tf_op jit(solution)/shard_map/ppermute | solution.py:165
  81.6 20.6 %collective-permute-start.10 = (bf16[128,2048]{1,0:T(8,128)(2,1)S(1)}, bf16[128,2048]{1,0:T(8,128)(2,1)}, u32[]{:S(2)}, u32[]{:S(2)}) collective-permute-start(bf16[128,2048]{1,0:T(8,128)(2,1)S(1)} %broadcast_select_fusion.1.x0), channel_id=1, source_target_pairs={{0,1},{1,0},{2,3},{3,2},{4,5},{5,4},{6,7},{7,6},{8,9},{9,8},{10,11... | collective-permute-start | bytes 1572872 | tf_op jit(solution)/shard_map/ppermute | solution.py:165
  81.6 0.8 copy-start.9
  82.4 20.2 %collective-permute-start.11 = (bf16[128,2048]{1,0:T(8,128)(2,1)}, bf16[128,2048]{1,0:T(8,128)(2,1)}, u32[]{:S(2)}, u32[]{:S(2)}) collective-permute-start(bf16[128,2048]{1,0:T(8,128)(2,1)} %collective-permute-done.9.x1), channel_id=1, source_target_pairs={{0,1},{1,0},{2,3},{3,2},{4,5},{5,4},{6,7},{7,6},{8,9},{9,8},{10,11... | collective-permute-start | bytes 1572872 | tf_op jit(solution)/shard_map/ppermute | solution.py:165
  82.9 0.8 copy-start.11
  83.7 1.9 copy-start
  85.6 1.9 copy-start.2
  87.5 1.9 copy-start.4
  89.3 1.0 copy-start.8
  90.4 1.0 copy-start.10
  91.4 1.0 copy-start.12
  100.5 0.8 copy-start.13
  101.3 25.1 %collective-permute-start.21 = (bf16[256,2048]{1,0:T(8,128)(2,1)S(1)}, bf16[256,2048]{1,0:T(8,128)(2,1)}, u32[]{:S(2)}, u32[]{:S(2)}) collective-permute-start(bf16[256,2048]{1,0:T(8,128)(2,1)S(1)} %get-tuple-element.23), channel_id=1, source_target_pairs={{0,1},{1,0},{2,3},{3,2},{4,5},{5,4},{6,7},{7,6},{8,9},{9,8},{10,11... | collective-permute-start | bytes 3145736 | tf_op jit(solution)/shard_map/ppermute | solution.py:165
  101.4 16.0 %collective-permute-start.5 = (bf16[128,2048]{1,0:T(8,128)(2,1)}, bf16[128,2048]{1,0:T(8,128)(2,1)}, u32[]{:S(2)}, u32[]{:S(2)}) collective-permute-start(bf16[128,2048]{1,0:T(8,128)(2,1)} %collective-permute-done.3.x0), channel_id=1, source_target_pairs={{0,1},{1,0},{2,3},{3,2},{4,5},{5,4},{6,7},{7,6},{8,9},{9,8},{10,11... | collective-permute-start | bytes 1572872 | tf_op jit(solution)/shard_map/ppermute | solution.py:165
  101.9 15.9 %collective-permute-start.6 = (bf16[128,2048]{1,0:T(8,128)(2,1)}, bf16[128,2048]{1,0:T(8,128)(2,1)}, u32[]{:S(2)}, u32[]{:S(2)}) collective-permute-start(bf16[128,2048]{1,0:T(8,128)(2,1)} %collective-permute-done.4.x1), channel_id=1, source_target_pairs={{0,1},{1,0},{2,3},{3,2},{4,5},{5,4},{6,7},{7,6},{8,9},{9,8},{10,11... | collective-permute-start | bytes 1572872 | tf_op jit(solution)/shard_map/ppermute | solution.py:165
  102.2 27.0 %collective-permute-start.1 = (bf16[128,2048]{1,0:T(8,128)(2,1)}, bf16[128,2048]{1,0:T(8,128)(2,1)S(1)}, u32[]{:S(2)}, u32[]{:S(2)}) collective-permute-start(bf16[128,2048]{1,0:T(8,128)(2,1)} %x0.1), channel_id=1, source_target_pairs={{0,1},{1,0},{2,3},{3,2},{4,5},{5,4},{6,7},{7,6},{8,9},{9,8},{10,11... | collective-permute-start | bytes 1572872 | tf_op jit(solution)/shard_map/ppermute | solution.py:165
  102.6 26.6 %collective-permute-start.2 = (bf16[128,2048]{1,0:T(8,128)(2,1)}, bf16[128,2048]{1,0:T(8,128)(2,1)S(1)}, u32[]{:S(2)}, u32[]{:S(2)}) collective-permute-start(bf16[128,2048]{1,0:T(8,128)(2,1)} %collective-permute-done.x1), channel_id=1, source_target_pairs={{0,1},{1,0},{2,3},{3,2},{4,5},{5,4},{6,7},{7,6},{8,9},{9,8},{10,11... | collective-permute-start | bytes 1572872 | tf_op jit(solution)/shard_map/ppermute | solution.py:165
  102.7 1.9 copy-start.1
  104.6 1.9 copy-start.3
  106.5 1.9 copy-start.5
  116.6 0.8 copy-start.15
  117.4 11.8 %copy-start.6 = (bf16[128,2048]{1,0:T(8,128)(2,1)S(1)}, bf16[128,2048]{1,0:T(8,128)(2,1)}, u32[]{:S(2)}) copy-start(bf16[128,2048]{1,0:T(8,128)(2,1)} %x0.1) | copy-start | bytes 1572868
  117.4 20.0 %collective-permute-start.26 = (bf16[256,2048]{1,0:T(8,128)(2,1)S(1)}, bf16[256,2048]{1,0:T(8,128)(2,1)S(1)}, u32[]{:S(2)}, u32[]{:S(2)}) collective-permute-start(bf16[256,2048]{1,0:T(8,128)(2,1)S(1)} %get-tuple-element.25), channel_id=1, source_target_pairs={{0,1},{1,0},{2,3},{3,2},{4,5},{5,4},{6,7},{7,6},{8,9},{9,8},{10,11... | collective-permute-start | bytes 3145736 | tf_op jit(solution)/shard_map/ppermute | solution.py:165
  126.2 3.0 %copy-start.17 = (bf16[320,768]{1,0:T(8,128)(2,1)}, bf16[320,768]{1,0:T(8,128)(2,1)S(1)}, u32[]{:S(2)}) copy-start(bf16[320,768]{1,0:T(8,128)(2,1)S(1)} %get-tuple-element.15) | copy-start | bytes 1474564
  126.2 20.7 %collective-permute-start.19 = (bf16[256,2048]{1,0:T(8,128)(2,1)S(1)}, bf16[256,2048]{1,0:T(8,128)(2,1)S(1)}, u32[]{:S(2)}, u32[]{:S(2)}) collective-permute-start(bf16[256,2048]{1,0:T(8,128)(2,1)S(1)} %get-tuple-element.21), channel_id=1, source_target_pairs={{0,1},{1,0},{2,3},{3,2},{4,5},{5,4},{6,7},{7,6},{8,9},{9,8},{10,11... | collective-permute-start | bytes 3145736 | tf_op jit(solution)/shard_map/ppermute | solution.py:165
  127.6 14.8 %collective-permute-start.22 = (bf16[128,2048]{1,0:T(8,128)(2,1)S(1)}, bf16[128,2048]{1,0:T(8,128)(2,1)S(1)}, u32[]{:S(2)}, u32[]{:S(2)}) collective-permute-start(bf16[128,2048]{1,0:T(8,128)(2,1)S(1)} %add_convert_fusion.5), channel_id=1, source_target_pairs={{0,2},{1,3},{2,0},{3,1},{4,6},{5,7},{6,4},{7,5},{8,10},{9,11},{10,... | collective-permute-start | bytes 1572872 | tf_op jit(solution)/shard_map/ppermute | solution.py:165
  137.2 16.7 %copy-start.19 = (bf16[320,768]{1,0:T(8,128)(2,1)}, bf16[320,768]{1,0:T(8,128)(2,1)S(1)}, u32[]{:S(2)}) copy-start(bf16[320,768]{1,0:T(8,128)(2,1)S(1)} %get-tuple-element.14) | copy-start | bytes 1474564
  137.2 23.2 %collective-permute-start.17 = (bf16[256,2048]{1,0:T(8,128)(2,1)S(1)}, bf16[256,2048]{1,0:T(8,128)(2,1)S(1)}, u32[]{:S(2)}, u32[]{:S(2)}) collective-permute-start(bf16[256,2048]{1,0:T(8,128)(2,1)S(1)} %get-tuple-element.19), channel_id=1, source_target_pairs={{0,1},{1,0},{2,3},{3,2},{4,5},{5,4},{6,7},{7,6},{8,9},{9,8},{10,11... | collective-permute-start | bytes 3145736 | tf_op jit(solution)/shard_map/ppermute | solution.py:165
  137.5 16.1 %collective-permute-start.27 = (bf16[128,2048]{1,0:T(8,128)(2,1)S(1)}, bf16[128,2048]{1,0:T(8,128)(2,1)S(1)}, u32[]{:S(2)}, u32[]{:S(2)}) collective-permute-start(bf16[128,2048]{1,0:T(8,128)(2,1)S(1)} %add_convert_fusion.2), channel_id=1, source_target_pairs={{0,2},{1,3},{2,0},{3,1},{4,6},{5,7},{6,4},{7,5},{8,10},{9,11},{10,... | collective-permute-start | bytes 1572872 | tf_op jit(solution)/shard_map/ppermute | solution.py:165
  143.7 14.6 %collective-permute-start.23 = (bf16[128,2048]{1,0:T(8,128)(2,1)S(1)}, bf16[128,2048]{1,0:T(8,128)(2,1)S(1)}, u32[]{:S(2)}, u32[]{:S(2)}) collective-permute-start(bf16[128,2048]{1,0:T(8,128)(2,1)S(1)} %fusion.10), channel_id=1, source_target_pairs={{0,4},{1,5},{2,6},{3,7},{12,8},{13,9},{14,10},{15,11},{16,20},{17,... | collective-permute-start | bytes 1572872 | tf_op jit(solution)/shard_map/ppermute | solution.py:165
  147.0 24.2 %collective-permute-start.20 = (bf16[128,2048]{1,0:T(8,128)(2,1)S(1)}, bf16[128,2048]{1,0:T(8,128)(2,1)S(1)}, u32[]{:S(2)}, u32[]{:S(2)}) collective-permute-start(bf16[128,2048]{1,0:T(8,128)(2,1)S(1)} %add_convert_fusion.6), channel_id=1, source_target_pairs={{0,2},{1,3},{2,0},{3,1},{4,6},{5,7},{6,4},{7,5},{8,10},{9,11},{10,... | collective-permute-start | bytes 1572872 | tf_op jit(solution)/shard_map/ppermute | solution.py:165
  153.9 14.7 %collective-permute-start.28 = (bf16[128,2048]{1,0:T(8,128)(2,1)S(1)}, bf16[128,2048]{1,0:T(8,128)(2,1)S(1)}, u32[]{:S(2)}, u32[]{:S(2)}) collective-permute-start(bf16[128,2048]{1,0:T(8,128)(2,1)S(1)} %fusion.11), channel_id=1, source_target_pairs={{0,4},{1,5},{2,6},{3,7},{12,8},{13,9},{14,10},{15,11},{16,20},{17,... | collective-permute-start | bytes 1572872 | tf_op jit(solution)/shard_map/ppermute | solution.py:165
  159.7 11.5 %collective-permute-start.24 = (bf16[128,2048]{1,0:T(8,128)(2,1)S(1)}, bf16[128,2048]{1,0:T(8,128)(2,1)S(1)}, u32[]{:S(2)}, u32[]{:S(2)}) collective-permute-start(bf16[128,2048]{1,0:T(8,128)(2,1)S(1)} %add_convert_fusion.4), channel_id=1, source_target_pairs={{4,8},{5,9},{6,10},{7,11},{8,4},{9,5},{10,6},{11,7},{20,24},{21,25... | collective-permute-start | bytes 1572872 | tf_op jit(solution)/shard_map/ppermute | solution.py:165
  160.4 11.9 %copy-start.21 = (bf16[256,2048]{1,0:T(8,128)(2,1)}, bf16[256,2048]{1,0:T(8,128)(2,1)S(1)}, u32[]{:S(2)}) copy-start(bf16[256,2048]{1,0:T(8,128)(2,1)S(1)} %collective-permute-done.17) | copy-start | bytes 3145732
  160.4 17.9 %copy-start.14 = (bf16[320,768]{1,0:T(8,128)(2,1)S(1)}, bf16[320,768]{1,0:T(8,128)(2,1)}, u32[]{:S(2)}) copy-start(bf16[320,768]{1,0:T(8,128)(2,1)} %copy-done.13) | copy-start | bytes 1474564
  160.4 17.9 %copy-start.16 = (bf16[320,768]{1,0:T(8,128)(2,1)S(1)}, bf16[320,768]{1,0:T(8,128)(2,1)}, u32[]{:S(2)}) copy-start(bf16[320,768]{1,0:T(8,128)(2,1)} %copy-done.15) | copy-start | bytes 1474564
  160.5 17.9 %copy-start.18 = (bf16[320,768]{1,0:T(8,128)(2,1)S(1)}, bf16[320,768]{1,0:T(8,128)(2,1)}, u32[]{:S(2)}) copy-start(bf16[320,768]{1,0:T(8,128)(2,1)} %copy-done.17) | copy-start | bytes 1474564
  160.5 17.9 %copy-start.20 = (bf16[320,768]{1,0:T(8,128)(2,1)S(1)}, bf16[320,768]{1,0:T(8,128)(2,1)}, u32[]{:S(2)}) copy-start(bf16[320,768]{1,0:T(8,128)(2,1)} %copy-done.19) | copy-start | bytes 1474564
  161.4 20.2 %collective-permute-start.18 = (bf16[128,2048]{1,0:T(8,128)(2,1)}, bf16[128,2048]{1,0:T(8,128)(2,1)}, u32[]{:S(2)}, u32[]{:S(2)}) collective-permute-start(bf16[128,2048]{1,0:T(8,128)(2,1)} %add_convert_fusion.7), channel_id=1, source_target_pairs={{0,2},{1,3},{2,0},{3,1},{4,6},{5,7},{6,4},{7,5},{8,10},{9,11},{10,... | collective-permute-start | bytes 1572872 | tf_op jit(solution)/shard_map/ppermute | solution.py:165
  169.7 11.9 %collective-permute-start.29 = (bf16[128,2048]{1,0:T(8,128)(2,1)}, bf16[128,2048]{1,0:T(8,128)(2,1)}, u32[]{:S(2)}, u32[]{:S(2)}) collective-permute-start(bf16[128,2048]{1,0:T(8,128)(2,1)} %add_convert_fusion.1), channel_id=1, source_target_pairs={{4,8},{5,9},{6,10},{7,11},{8,4},{9,5},{10,6},{11,7},{20,24},{21,25... | collective-permute-start | bytes 1572872 | tf_op jit(solution)/shard_map/ppermute | solution.py:165
  172.3 16.1 %collective-permute-start.25 = (bf16[128,2048]{1,0:T(8,128)(2,1)}, bf16[128,2048]{1,0:T(8,128)(2,1)}, u32[]{:S(2)}, u32[]{:S(2)}) collective-permute-start(bf16[128,2048]{1,0:T(8,128)(2,1)} %add_convert_fusion.3), channel_id=1, source_target_pairs={{0,4},{1,5},{2,6},{3,7},{4,0},{5,1},{6,2},{7,3},{8,12},{9,13},{10,... | collective-permute-start | bytes 1572872 | tf_op jit(solution)/shard_map/ppermute | solution.py:165
  178.4 10.0 %copy-start.22 = (bf16[256,2048]{1,0:T(8,128)(2,1)S(1)}, bf16[256,2048]{1,0:T(8,128)(2,1)}, u32[]{:S(2)}) copy-start(bf16[256,2048]{1,0:T(8,128)(2,1)} %copy-done.21) | copy-start | bytes 3145732

commit v3 on v2

--- a/solution.py
+++ b/solution.py
@@ -119,7 +119,8 @@
         functools.partial(plane_kernel, capacity),
         out_shape=(half, half, jax.ShapeDtypeStruct((rows, hidden), jnp.bfloat16)),
         in_specs=[pl.BlockSpec(memory_space=pltpu.SMEM), pl.BlockSpec(memory_space=pltpu.VMEM)]
-        + [pl.BlockSpec(memory_space=pl.ANY)] * 7,
+        + [pl.BlockSpec(memory_space=pl.ANY)] * 4
+        + [pl.BlockSpec(memory_space=pltpu.HBM)] * 3,
         out_specs=[pl.BlockSpec(memory_space=pltpu.VMEM)] * 3,
         scratch_shapes=[
             pltpu.VMEM((4 * tok, features), jnp.bfloat16),
@@ -176,26 +177,12 @@
     def sibling(z, y, core):
         return z, y, 1 - core
 
-    weight = weights_for_me(routes, probs, size)
-
-    held_1 = moved(tokens, every, pair)
-    crossed = moved(tokens, (1, 2), across)
-    outward = moved(crossed, (1, 2), pair)
-    far_mid = moved(held_1, (1, 2), across)
-    far_end = moved(far_mid, (1, 2), pair)
-    held = [
-        tokens,
-        held_1,
-        jnp.where(middle, crossed, outward),
-        jnp.where(middle, far_mid, far_end),
-    ]
-    planes = [z, z ^ 1, jnp.where(middle, 3 - z, (3 - z) ^ 1), jnp.where(middle, (3 - z) ^ 1, 3 - z)]
-    keeps, gives, acts = [], [], []
-    for mine, plane in zip(held, planes):
-        other = moved(mine, every, column)
-        xs = (mine, other, moved(mine, every, sibling), moved(other, every, sibling))
+    def together(*arrays):
+        return lax.optimization_barrier(arrays)
+
+    def sources(plane):
         base = plane * 4
-        order = jnp.stack(
+        return jnp.stack(
             [
                 base + y * 2 + core,
                 base + (1 - y) * 2 + core,
@@ -203,26 +190,82 @@
                 base + (1 - y) * 2 + 1 - core,
             ]
         ).astype(jnp.int32)
-        keep, give, act = plane_pass(order, weight, xs, w_gate, w_up, w_down, slots, capacity)
-        keeps.append(keep)
-        gives.append(give)
-        acts.append(act)
-
-    reduced = [None] * 4
-    for k in (3, 2, 1, 0):
-        came = moved(gives[k], every, sibling)
-        send = summed(keeps[k][tok:], came[tok:])
-        crossed = moved(send, every, column)
-        reduced[k] = (keeps[k][:tok], came[:tok], crossed)
-    far_in = moved(summed(*reduced[3]), (0, 3), pair)
-    far_across = moved(summed(*reduced[3], far_in), (1, 2), across)
-    near_in = moved(summed(*reduced[2]), (0, 3), pair)
-    near_across = moved(summed(*reduced[2], near_in), (1, 2), across)
-    last = moved(summed(*reduced[1], far_across), every, pair)
-    mixed = summed(*reduced[0], last, near_across)
-
+
+    def expert(plane, *xs):
+        return plane_pass(sources(plane), weight, xs, w_gate, w_up, w_down, slots, capacity)
+
+    weight = weights_for_me(routes, probs, size)
+    a0, a1, crossed, b0, c0, weight = together(
+        tokens,
+        moved(tokens, every, pair),
+        moved(tokens, (1, 2), across),
+        moved(tokens, every, column),
+        moved(tokens, every, sibling),
+        weight,
+    )
+    outward = moved(crossed, (1, 2), pair)
+    far_mid = moved(a1, (1, 2), across)
+    crossed, outward, far_mid, b1, d0, c1 = together(
+        crossed,
+        outward,
+        far_mid,
+        moved(a1, every, column),
+        moved(b0, every, sibling),
+        moved(a1, every, sibling),
+    )
+    a2 = jnp.where(middle, crossed, outward)
+    far_end = moved(far_mid, (1, 2), pair)
+    keep0, give0, act0 = expert(z, a0, b0, c0, d0)
+    far_mid, far_end, b2, d1, c2, keep0, give0, act0 = together(
+        far_mid,
+        far_end,
+        moved(a2, every, column),
+        moved(b1, every, sibling),
+        moved(a2, every, sibling),
+        keep0,
+        give0,
+        act0,
+    )
+    a3 = jnp.where(middle, far_mid, far_end)
+    keep1, give1, act1 = expert(z ^ 1, a1, b1, c1, d1)
+    b3, d2, c3, got0, keep1, give1, act1 = together(
+        moved(a3, every, column),
+        moved(b2, every, sibling),
+        moved(a3, every, sibling),
+        moved(give0, every, sibling),
+        keep1,
+        give1,
+        act1,
+    )
+    near = jnp.where(middle, 3 - z, (3 - z) ^ 1)
+    keep2, give2, act2 = expert(near, a2, b2, c2, d2)
+    d3, got1, keep2, give2, act2 = together(
+        moved(b3, every, sibling), moved(give1, every, sibling), keep2, give2, act2
+    )
+    keep3, give3, act3 = expert(near ^ 1, a3, b3, c3, d3)
+
+    def sent(keep, got):
+        return moved(summed(keep[tok:], got[tok:]), every, column)
+
+    keep3, give3, act3, got2 = together(keep3, give3, act3, moved(give2, every, sibling))
+    got3 = moved(give3, every, sibling)
+    came3, got3 = together(sent(keep3, got3), got3)
+    sum3 = summed(keep3[:tok], got3[:tok], came3)
+    sum3, far_in, came2 = together(sum3, moved(sum3, (0, 3), pair), sent(keep2, got2))
+    sum2 = summed(keep2[:tok], got2[:tok], came2)
+    sum2, far_across, near_in, came1 = together(
+        sum2,
+        moved(summed(sum3, far_in), (1, 2), across),
+        moved(sum2, (0, 3), pair),
+        sent(keep1, got1),
+    )
+    near_across = moved(summed(sum2, near_in), (1, 2), across)
+    last = moved(summed(keep1[:tok], got1[:tok], came1, far_across), every, pair)
+    mixed = summed(keep0[:tok], got0[:tok], sent(keep0, got0), last, near_across)
+
+    acts = jnp.concatenate([act0, act1, act2, act3], axis=0)
     count = jnp.minimum(jnp.sum((weight >= 0.0).astype(jnp.float32)), float(capacity))
-    gram = gram_of(jnp.concatenate(acts, axis=0)) * (2.0 / count)
+    gram = gram_of(acts) * (2.0 / count)
     return gram[None], mixed
 
 

time: 192 us -> 193 us (level)
  waiting for transfers between devices: 84.6 us -> 43.4 us
  local copies, waits for them, and re-layouts: 18.4 us -> 38.5 us
  blocking collectives: 0 us -> 13.7 us
  other arithmetic: 11.9 us -> 16.3 us
  Pallas kernels: 32.6 us -> 35.3 us
    ppermute x30, waiting for transfers between devices: 84.6 us -> 43.4 us  [moved(): return lax.ppermute(array, 'expert', pairs_of(size, planes, step))]
    unnamed x50 -> x70, local copies, waits for them, and re-layouts: 18.4 us -> 38.5 us
    all_to_all x0 -> x1, blocking collectives: none -> 13.7 us  [weights_for_me(): lax.all_to_all(mine, 'expert', split_axis=0, concat_axis=0, tiled=True)]
    all_to_all x1 -> x0, starting transfers between devices: 4.92 us -> none  [weights_for_me(): lax.all_to_all(mine, 'expert', split_axis=0, concat_axis=0, tiled=True)]
    ppermute x30, starting transfers between devices: 33.6 us -> 38.1 us  [moved(): return lax.ppermute(array, 'expert', pairs_of(size, planes, step))]
    pallas_call x4, Pallas kernels: 32.6 us -> 35.3 us  [plane_pass(): pl.pallas_call(functools.partial(plane_kernel, capacity), out_shape=(half...]
    select_n x2, other arithmetic: 0.12 us -> 2.21 us  [the longest x1 1.11 us: staged(): a2 = jnp.where(middle, crossed, outward)]
  transfers between devices with their start and end apart: 31 -> 30, of which waited for: 10 -> 8; matrix products, arithmetic and copies ran while one was open for 7% -> 10% of each run, Pallas kernels for 17% -> 18%
where the time goes in v3:
time: 193 us; the launch traced here: 192 us
  waiting for transfers between devices  43.4 us (22%)
  local copies, waits for them, and re-layouts  38.5 us (20%)
  starting transfers between devices  38.1 us (20%)
  Pallas kernels  35.3 us (18%)
  other arithmetic  16.3 us (8%)
  blocking collectives  13.7 us (7%)
  matrix products  4.67 us (2%)
    ppermute x30, waiting for transfers between devices, moved(): return lax.ppermute(array, 'expert', pairs_of(size, planes, step))  43.4 us
    unnamed x70, local copies, waits for them, and re-layouts  38.5 us
    ppermute x30, starting transfers between devices, moved(): return lax.ppermute(array, 'expert', pairs_of(size, planes, step))  38.1 us
    pallas_call x4, Pallas kernels, plane_pass(): pl.pallas_call(functools.partial(plane_kernel, capacity), out_shape=(half...  35.3 us
    all_to_all x1, blocking collectives, weights_for_me(): lax.all_to_all(mine, 'expert', split_axis=0, concat_axis=0, tiled=True)  13.7 us
    convert_element_type x10, other arithmetic, summed(): return total.astype(jnp.bfloat16)  11.7 us
    dot_general x1, matrix products, gram_of(): lax.dot_general(rows, rows, (((0,), (0,)), ((), ())), preferred_element_t...  4.67 us
  transfers between devices with their start and end apart: 30, of which 8 were waited for; matrix products, arithmetic and copies ran while one was open for 10% of the time, Pallas kernels for 18%

profile of v3, /device:TPU:0, one launch (start us, length us, event | category | flops | bytes accessed | tf_op | source)
XLA Modules:
  0.0 191.5 jit_solution(1658149884637171800)
XLA Ops:
  0.6 3.1 %collective-permute-start = (bf16[128,2048]{1,0:T(8,128)(2,1)}, bf16[128,2048]{1,0:T(8,128)(2,1)S(1)}, u32[]{:S(2)}, u32[]{:S(2)}) collective-permute-start(bf16[128,2048]{1,0:T(8,128)(2,1)} %x0), channel_id=1, source_target_pairs={{0,4},{1,5},{2,6},{3,7},{4,0},{5,1},{6,2},{7,3},{8,12},{9,13},{10,... | collective-permute-start | bytes 1572872 | tf_op jit(solution)/shard_map/ppermute | solution.py:166
  4.4 1.6 collective-permute-start.2
  7.5 13.7 %all_to_all.9 = f32[16,1,128]{2,1,0:T(1,128)S(1)} all-to-all(f32[16,1,128]{2,1,0:T(1,128)S(1)} %bitcast.44), channel_id=1, replica_groups=mesh['parts'=2,'expert'=16] {'expert'}, dimensions={0} | all-to-all | bytes 16384 | tf_op jit(solution)/shard_map/all_to_all | solution.py:28
  21.2 0.8 copy-done.25
  21.9 1.3 collective-permute-start.4
  23.2 1.5 collective-permute-start.5
  25.3 0.8 copy-done.23
  26.6 11.0 %collective-permute-done.4 = bf16[128,2048]{1,0:T(8,128)(2,1)} collective-permute-done((bf16[128,2048]{1,0:T(8,128)(2,1)S(1)}, bf16[128,2048]{1,0:T(8,128)(2,1)}, u32[]{:S(2)}, u32[]{:S(2)}) %collective-permute-start.4) | collective-permute-done | bytes 524320 | tf_op jit(solution)/shard_map/ppermute | solution.py:166
  37.6 0.8 collective-permute-done.6.x1
  38.4 0.8 copy-done.27
  39.2 0.8 copy-done.19
  40.0 1.3 collective-permute-start.9
  41.3 1.1 broadcast_select_fusion.1.x0
  43.7 1.9 copy-done.4
  45.6 1.9 copy-done.8
  47.5 1.9 copy-done.12
  49.3 1.0 copy-done.16
  50.4 1.0 copy-done.24
  51.4 1.0 copy-done.26
  52.5 1.0 copy-done.28
  53.5 9.0 %shard_map.77 = (bf16[256,2048]{1,0:T(8,128)(2,1)S(1)}, bf16[256,2048]{1,0:T(8,128)(2,1)}, bf16[320,768]{1,0:T(8,128)(2,1)S(1)}) custom-call(s32[4]{0:T(128)S(1)} %pad_add_fusion.order, f32[16,128]{1,0:T(8,128)S(1)} %bitcast.27, bf16[128,2048]{1,0:T(8,128)(2,1)S(1)} %copy-done.16, bf16[128,2048]{1,0:T(8,128)(2,1)S(1)} %copy-done.24, ...), custom_call_target="tpu_custom_call" | custom-call | flops 4362076160 | bytes 13631488 | tf_op jit(solution)/shard_map/pallas_call | solution.py:118
  62.5 0.8 copy-done.29
  63.3 0.8 copy-done.21
  64.2 1.1 broadcast_select_fusion.x0
  65.3 1.5 collective-permute-start.13
  67.4 1.9 copy-done.5
  69.3 1.9 copy-done.9
  71.2 1.9 copy-done.13
  73.1 1.0 copy-done.18
  74.1 1.0 copy-done.20
  75.1 9.0 %shard_map.78 = (bf16[256,2048]{1,0:T(8,128)(2,1)S(1)}, bf16[256,2048]{1,0:T(8,128)(2,1)}, bf16[320,768]{1,0:T(8,128)(2,1)S(1)}) custom-call(s32[4]{0:T(128)S(1)} %pad_add_fusion.1.order, f32[16,128]{1,0:T(8,128)S(1)} %bitcast.28, bf16[128,2048]{1,0:T(8,128)(2,1)S(1)} %collective-permute-done.x0, bf16[128,2048]{1,0:T(8,128)(2,1)S(1)} %copy-done.18, ...), custom_call_target="tpu_custom_call" | custom-call | flops 4362076160 | bytes 13631488 | tf_op jit(solution)/shard_map/pallas_call | solution.py:118
  84.1 0.8 copy-done.31
  85.6 1.0 copy-done.1
  86.7 1.9 copy-done.6
  88.6 1.9 copy-done.10
  90.5 1.9 copy-done.14
  92.4 1.0 copy-done.22
  93.4 9.1 %shard_map.79 = (bf16[256,2048]{1,0:T(8,128)(2,1)S(1)}, bf16[256,2048]{1,0:T(8,128)(2,1)}, bf16[320,768]{1,0:T(8,128)(2,1)S(1)}) custom-call(s32[4]{0:T(128)S(1)} %pad_add_fusion.2.order, f32[16,128]{1,0:T(8,128)S(1)} %bitcast.29, bf16[128,2048]{1,0:T(8,128)(2,1)S(1)} %copy-done.1, bf16[128,2048]{1,0:T(8,128)(2,1)} %collective-permute-done.10.x1, ...), custom_call_target="tpu_custom_call" | custom-call | flops 4362076160 | bytes 13631488 | tf_op jit(solution)/shard_map/pallas_call | solution.py:118
  102.5 0.8 copy-done.33
  103.6 1.0 copy-done.3
  104.7 1.9 copy-done.7
  106.5 1.9 copy-done.11
  108.4 1.9 copy-done.15
  110.3 8.2 %shard_map.80 = (bf16[256,2048]{1,0:T(8,128)(2,1)S(1)}, bf16[256,2048]{1,0:T(8,128)(2,1)S(1)}, bf16[320,768]{1,0:T(8,128)(2,1)S(1)}) custom-call(s32[4]{0:T(128)S(1)} %pad_add_fusion.3.order, f32[16,128]{1,0:T(8,128)S(1)} %bitcast.30, bf16[128,2048]{1,0:T(8,128)(2,1)S(1)} %copy-done.3, bf16[128,2048]{1,0:T(8,128)(2,1)} %collective-permute-done.13.x1, ...), custom_call_target="tpu_custom_call" | custom-call | flops 4362076160 | bytes 13631488 | tf_op jit(solution)/shard_map/pallas_call | solution.py:118
  119.0 2.4 %collective-permute-done.21 = bf16[256,2048]{1,0:T(8,128)(2,1)S(1)} collective-permute-done((bf16[256,2048]{1,0:T(8,128)(2,1)S(1)}, bf16[256,2048]{1,0:T(8,128)(2,1)S(1)}, u32[]{:S(2)}, u32[]{:S(2)}) %collective-permute-start.21) | collective-permute-done | bytes 1048608 | tf_op jit(solution)/shard_map/ppermute | solution.py:166
  122.1 1.2 add_convert_fusion.6
  123.2 1.5 collective-permute-start.24
  124.8 11.5 %collective-permute-done.22 = bf16[128,2048]{1,0:T(8,128)(2,1)S(1)} collective-permute-done((bf16[128,2048]{1,0:T(8,128)(2,1)S(1)}, bf16[128,2048]{1,0:T(8,128)(2,1)S(1)}, u32[]{:S(2)}, u32[]{:S(2)}) %collective-permute-start.22) | collective-permute-done | bytes 524320 | tf_op jit(solution)/shard_map/ppermute | solution.py:166
  136.5 6.8 %collective-permute-start.23 = (bf16[128,2048]{1,0:T(8,128)(2,1)S(1)}, bf16[128,2048]{1,0:T(8,128)(2,1)S(1)}, u32[]{:S(2)}, u32[]{:S(2)}) collective-permute-start(bf16[128,2048]{1,0:T(8,128)(2,1)S(1)} %add_convert_fusion.7), channel_id=1, source_target_pairs={{0,4},{1,5},{2,6},{3,7},{12,8},{13,9},{14,10},{15,11},{16,20},{17,... | collective-permute-start | bytes 1572872 | tf_op jit(solution)/shard_map/ppermute | solution.py:166
  143.3 1.2 add_convert_fusion.3
  145.1 2.4 %collective-permute-done.24 = bf16[128,2048]{1,0:T(8,128)(2,1)S(1)} collective-permute-done((bf16[128,2048]{1,0:T(8,128)(2,1)S(1)}, bf16[128,2048]{1,0:T(8,128)(2,1)S(1)}, u32[]{:S(2)}, u32[]{:S(2)}) %collective-permute-start.24) | collective-permute-done | bytes 524320 | tf_op jit(solution)/shard_map/ppermute | solution.py:166
  147.5 6.0 %collective-permute-done.23 = bf16[128,2048]{1,0:T(8,128)(2,1)S(1)} collective-permute-done((bf16[128,2048]{1,0:T(8,128)(2,1)S(1)}, bf16[128,2048]{1,0:T(8,128)(2,1)S(1)}, u32[]{:S(2)}, u32[]{:S(2)}) %collective-permute-start.23) | collective-permute-done | bytes 524320 | tf_op jit(solution)/shard_map/ppermute | solution.py:166
  153.5 1.3 add_convert_fusion.5
  154.9 0.8 collective-permute-start.25
  155.7 5.9 %collective-permute-start.26 = (bf16[128,2048]{1,0:T(8,128)(2,1)S(1)}, bf16[128,2048]{1,0:T(8,128)(2,1)S(1)}, u32[]{:S(2)}, u32[]{:S(2)}) collective-permute-start(bf16[128,2048]{1,0:T(8,128)(2,1)S(1)} %add_convert_fusion.5), channel_id=1, source_target_pairs={{0,4},{1,5},{2,6},{3,7},{12,8},{13,9},{14,10},{15,11},{16,20},{17,... | collective-permute-start | bytes 1572872 | tf_op jit(solution)/shard_map/ppermute | solution.py:166
  161.7 2.0 %add_convert_fusion.9 = bf16[128,2048]{1,0:T(8,128)(2,1)} fusion(bf16[256,2048]{1,0:T(8,128)(2,1)} %collective-permute-done.16, bf16[256,2048]{1,0:T(8,128)(2,1)S(1)} %get-tuple-element.99), kind=kLoop, calls=%fused_computation.18 | loop fusion | flops 1048576 | bytes 1572864 | tf_op jit(solution)/shard_map/convert_element_type | solution.py:35
  164.2 6.4 %collective-permute-done.26 = bf16[128,2048]{1,0:T(8,128)(2,1)S(1)} collective-permute-done((bf16[128,2048]{1,0:T(8,128)(2,1)S(1)}, bf16[128,2048]{1,0:T(8,128)(2,1)S(1)}, u32[]{:S(2)}, u32[]{:S(2)}) %collective-permute-start.26) | collective-permute-done | bytes 524320 | tf_op jit(solution)/shard_map/ppermute | solution.py:166
  170.6 0.9 add_convert_fusion.1
  171.6 1.5 collective-permute-start.29
  173.0 2.2 %add_convert_fusion.2 = bf16[128,2048]{1,0:T(8,128)(2,1)} fusion(bf16[128,2048]{1,0:T(8,128)(2,1)S(1)} %collective-permute-done.25, bf16[128,2048]{1,0:T(8,128)(2,1)S(1)} %collective-permute-done.27, bf16[256,2048]{1,0:T(8,128)(2,1)} %collective-permute-done.18, bf16[256,2048]{1,0:T(8,128)(2,1)S(1)} %get-tuple-element.101), kind=kLoop, calls=%fused_computation.11 | loop fusion | flops 2097152 | bytes 2621440 | tf_op jit(solution)/shard_map/convert_element_type | solution.py:35
  175.2 4.9 %collective-permute-start.28 = (bf16[128,2048]{1,0:T(8,128)(2,1)}, bf16[128,2048]{1,0:T(8,128)(2,1)S(1)}, u32[]{:S(2)}, u32[]{:S(2)}) collective-permute-start(bf16[128,2048]{1,0:T(8,128)(2,1)} %add_convert_fusion.2), channel_id=1, source_target_pairs={{0,4},{1,5},{2,6},{3,7},{4,0},{5,1},{6,2},{7,3},{8,12},{9,13},{10,... | collective-permute-start | bytes 1572872 | tf_op jit(solution)/shard_map/ppermute | solution.py:166
  181.4 4.7 %multiply_bitcast_fusion = f32[1,768,768]{2,1,0:T(8,128)} fusion(f32[]{:T(128)S(6)} %div.24, bf16[320,768]{1,0:T(8,128)(2,1)} %copy-done.34, bf16[320,768]{1,0:T(8,128)(2,1)} %copy-done.33, bf16[320,768]{1,0:T(8,128)(2,1)S(1)} %copy-done.32, bf16[320,768]{1,0:T(8,128)(2,1)S(1)} %copy-done.30), kind=kOutput, calls=%fused_computation | convolution fusion | flops 1518403584 | bytes 4325380 | tf_op jit(solution)/shard_map/dot_general | solution.py:12
  186.1 2.9 %collective-permute-done.28 = bf16[128,2048]{1,0:T(8,128)(2,1)S(1)} collective-permute-done((bf16[128,2048]{1,0:T(8,128)(2,1)}, bf16[128,2048]{1,0:T(8,128)(2,1)S(1)}, u32[]{:S(2)}, u32[]{:S(2)}) %collective-permute-start.28) | collective-permute-done | bytes 524320 | tf_op jit(solution)/shard_map/ppermute | solution.py:166
  188.9 2.6 %add_convert_fusion = bf16[128,2048]{1,0:T(8,128)(2,1)} fusion(bf16[128,2048]{1,0:T(8,128)(2,1)} %collective-permute-done.29, bf16[128,2048]{1,0:T(8,128)(2,1)S(1)} %collective-permute-done.28, bf16[128,2048]{1,0:T(8,128)(2,1)} %collective-permute-done.20, bf16[256,2048]{1,0:T(8,128)(2,1)} %collective-permute-done.16, bf16[256,2048]{1,0:T(8,128)(2,1)S(1)} %get-tuple-element.99), kind=kLoop, calls=%fused_computation.9 | loop fusion | flops 2621440 | bytes 3145728 | tf_op jit(solution)/shard_map/convert_element_type | solution.py:35
  (92 shorter events, 9.4 us)
Async XLA Ops:
  0.6 20.5 %collective-permute-start = (bf16[128,2048]{1,0:T(8,128)(2,1)}, bf16[128,2048]{1,0:T(8,128)(2,1)S(1)}, u32[]{:S(2)}, u32[]{:S(2)}) collective-permute-start(bf16[128,2048]{1,0:T(8,128)(2,1)} %x0), channel_id=1, source_target_pairs={{0,4},{1,5},{2,6},{3,7},{4,0},{5,1},{6,2},{7,3},{8,12},{9,13},{10,... | collective-permute-start | bytes 1572872 | tf_op jit(solution)/shard_map/ppermute | solution.py:166
  3.7 17.4 %collective-permute-start.1 = (bf16[128,2048]{1,0:T(8,128)(2,1)}, bf16[128,2048]{1,0:T(8,128)(2,1)S(1)}, u32[]{:S(2)}, u32[]{:S(2)}) collective-permute-start(bf16[128,2048]{1,0:T(8,128)(2,1)} %x0), channel_id=1, source_target_pairs={{4,8},{5,9},{6,10},{7,11},{8,4},{9,5},{10,6},{11,7},{20,24},{21,25... | collective-permute-start | bytes 1572872 | tf_op jit(solution)/shard_map/ppermute | solution.py:166
  4.4 16.7 %collective-permute-start.2 = (bf16[128,2048]{1,0:T(8,128)(2,1)}, bf16[128,2048]{1,0:T(8,128)(2,1)S(1)}, u32[]{:S(2)}, u32[]{:S(2)}) collective-permute-start(bf16[128,2048]{1,0:T(8,128)(2,1)} %x0), channel_id=1, source_target_pairs={{0,2},{1,3},{2,0},{3,1},{4,6},{5,7},{6,4},{7,5},{8,10},{9,11},{10,... | collective-permute-start | bytes 1572872 | tf_op jit(solution)/shard_map/ppermute | solution.py:166
  6.0 15.1 %collective-permute-start.3 = (bf16[128,2048]{1,0:T(8,128)(2,1)}, bf16[128,2048]{1,0:T(8,128)(2,1)S(1)}, u32[]{:S(2)}, u32[]{:S(2)}) collective-permute-start(bf16[128,2048]{1,0:T(8,128)(2,1)} %x0), channel_id=1, source_target_pairs={{0,1},{1,0},{2,3},{3,2},{4,5},{5,4},{6,7},{7,6},{8,9},{9,8},{10,11... | collective-permute-start | bytes 1572872 | tf_op jit(solution)/shard_map/ppermute | solution.py:166
  21.1 0.8 copy-start.25
  21.9 15.7 %collective-permute-start.4 = (bf16[128,2048]{1,0:T(8,128)(2,1)S(1)}, bf16[128,2048]{1,0:T(8,128)(2,1)}, u32[]{:S(2)}, u32[]{:S(2)}) collective-permute-start(bf16[128,2048]{1,0:T(8,128)(2,1)S(1)} %collective-permute-done.1), channel_id=1, source_target_pairs={{4,0},{5,1},{6,2},{7,3},{8,12},{9,13},{10,14},{11,15},{20,16},{21,... | collective-permute-start | bytes 1572872 | tf_op jit(solution)/shard_map/ppermute | solution.py:166
  23.2 14.4 %collective-permute-start.5 = (bf16[128,2048]{1,0:T(8,128)(2,1)S(1)}, bf16[128,2048]{1,0:T(8,128)(2,1)}, u32[]{:S(2)}, u32[]{:S(2)}) collective-permute-start(bf16[128,2048]{1,0:T(8,128)(2,1)S(1)} %collective-permute-done.x0), channel_id=1, source_target_pairs={{4,8},{5,9},{6,10},{7,11},{8,4},{9,5},{10,6},{11,7},{20,24},{21,25... | collective-permute-start | bytes 1572872 | tf_op jit(solution)/shard_map/ppermute | solution.py:166
  24.7 13.7 %collective-permute-start.6 = (bf16[128,2048]{1,0:T(8,128)(2,1)S(1)}, bf16[128,2048]{1,0:T(8,128)(2,1)S(1)}, u32[]{:S(2)}, u32[]{:S(2)}) collective-permute-start(bf16[128,2048]{1,0:T(8,128)(2,1)S(1)} %collective-permute-done.x0), channel_id=1, source_target_pairs={{0,2},{1,3},{2,0},{3,1},{4,6},{5,7},{6,4},{7,5},{8,10},{9,11},{10,... | collective-permute-start | bytes 1572872 | tf_op jit(solution)/shard_map/ppermute | solution.py:166
  25.3 13.1 %collective-permute-start.7 = (bf16[128,2048]{1,0:T(8,128)(2,1)S(1)}, bf16[128,2048]{1,0:T(8,128)(2,1)S(1)}, u32[]{:S(2)}, u32[]{:S(2)}) collective-permute-start(bf16[128,2048]{1,0:T(8,128)(2,1)S(1)} %collective-permute-done.2.x1), channel_id=1, source_target_pairs={{0,1},{1,0},{2,3},{3,2},{4,5},{5,4},{6,7},{7,6},{8,9},{9,8},{10,11... | collective-permute-start | bytes 1572872 | tf_op jit(solution)/shard_map/ppermute | solution.py:166
  26.1 13.2 %collective-permute-start.8 = (bf16[128,2048]{1,0:T(8,128)(2,1)S(1)}, bf16[128,2048]{1,0:T(8,128)(2,1)S(1)}, u32[]{:S(2)}, u32[]{:S(2)}) collective-permute-start(bf16[128,2048]{1,0:T(8,128)(2,1)S(1)} %collective-permute-done.x0), channel_id=1, source_target_pairs={{0,1},{1,0},{2,3},{3,2},{4,5},{5,4},{6,7},{7,6},{8,9},{9,8},{10,11... | collective-permute-start | bytes 1572872 | tf_op jit(solution)/shard_map/ppermute | solution.py:166
  38.4 24.1 %copy-start.17 = (bf16[128,2048]{1,0:T(8,128)(2,1)}, bf16[128,2048]{1,0:T(8,128)(2,1)S(1)}, u32[]{:S(2)}) copy-start(bf16[128,2048]{1,0:T(8,128)(2,1)S(1)} %collective-permute-done.6.x1) | copy-start | bytes 1572868
  38.4 0.9 copy-start.27
  39.2 0.8 copy-start.19
  40.0 23.3 %collective-permute-start.9 = (bf16[128,2048]{1,0:T(8,128)(2,1)}, bf16[128,2048]{1,0:T(8,128)(2,1)}, u32[]{:S(2)}, u32[]{:S(2)}) collective-permute-start(bf16[128,2048]{1,0:T(8,128)(2,1)} %collective-permute-done.5), channel_id=1, source_target_pairs={{4,0},{5,1},{6,2},{7,3},{8,12},{9,13},{10,14},{11,15},{20,16},{21,... | collective-permute-start | bytes 1572872 | tf_op jit(solution)/shard_map/ppermute | solution.py:166
  42.4 20.1 %copy-start = (bf16[128,2048]{1,0:T(8,128)(2,1)}, bf16[128,2048]{1,0:T(8,128)(2,1)S(1)}, u32[]{:S(2)}) copy-start(bf16[128,2048]{1,0:T(8,128)(2,1)S(1)} %broadcast_select_fusion.1.x0) | copy-start | bytes 1572868
  42.5 20.9 %collective-permute-start.10 = (bf16[128,2048]{1,0:T(8,128)(2,1)S(1)}, bf16[128,2048]{1,0:T(8,128)(2,1)}, u32[]{:S(2)}, u32[]{:S(2)}) collective-permute-start(bf16[128,2048]{1,0:T(8,128)(2,1)S(1)} %broadcast_select_fusion.1.x0), channel_id=1, source_target_pairs={{0,2},{1,3},{2,0},{3,1},{4,6},{5,7},{6,4},{7,5},{8,10},{9,11},{10,... | collective-permute-start | bytes 1572872 | tf_op jit(solution)/shard_map/ppermute | solution.py:166
  43.1 20.2 %collective-permute-start.11 = (bf16[128,2048]{1,0:T(8,128)(2,1)S(1)}, bf16[128,2048]{1,0:T(8,128)(2,1)}, u32[]{:S(2)}, u32[]{:S(2)}) collective-permute-start(bf16[128,2048]{1,0:T(8,128)(2,1)S(1)} %collective-permute-done.6.x1), channel_id=1, source_target_pairs={{0,1},{1,0},{2,3},{3,2},{4,5},{5,4},{6,7},{7,6},{8,9},{9,8},{10,11... | collective-permute-start | bytes 1572872 | tf_op jit(solution)/shard_map/ppermute | solution.py:166
  43.1 20.2 %collective-permute-start.12 = (bf16[128,2048]{1,0:T(8,128)(2,1)S(1)}, bf16[128,2048]{1,0:T(8,128)(2,1)S(1)}, u32[]{:S(2)}, u32[]{:S(2)}) collective-permute-start(bf16[128,2048]{1,0:T(8,128)(2,1)S(1)} %broadcast_select_fusion.1.x0), channel_id=1, source_target_pairs={{0,1},{1,0},{2,3},{3,2},{4,5},{5,4},{6,7},{7,6},{8,9},{9,8},{10,11... | collective-permute-start | bytes 1572872 | tf_op jit(solution)/shard_map/ppermute | solution.py:166
  43.7 1.9 copy-start.4
  45.6 1.9 copy-start.8
  47.5 1.9 copy-start.12
  49.3 1.0 copy-start.16
  50.4 1.0 copy-start.24
  51.4 1.0 copy-start.26
  52.5 1.0 copy-start.28
  62.5 0.8 copy-start.29
  63.3 0.8 copy-start.21
  64.2 20.8 %collective-permute-start.16 = (bf16[256,2048]{1,0:T(8,128)(2,1)}, bf16[256,2048]{1,0:T(8,128)(2,1)}, u32[]{:S(2)}, u32[]{:S(2)}) collective-permute-start(bf16[256,2048]{1,0:T(8,128)(2,1)} %get-tuple-element.77), channel_id=1, source_target_pairs={{0,1},{1,0},{2,3},{3,2},{4,5},{5,4},{6,7},{7,6},{8,9},{9,8},{10,11... | collective-permute-start | bytes 3145736 | tf_op jit(solution)/shard_map/ppermute | solution.py:166
  65.3 18.9 %copy-start.2 = (bf16[128,2048]{1,0:T(8,128)(2,1)}, bf16[128,2048]{1,0:T(8,128)(2,1)S(1)}, u32[]{:S(2)}) copy-start(bf16[128,2048]{1,0:T(8,128)(2,1)S(1)} %broadcast_select_fusion.x0) | copy-start | bytes 1572868
  65.3 19.7 %collective-permute-start.13 = (bf16[128,2048]{1,0:T(8,128)(2,1)S(1)}, bf16[128,2048]{1,0:T(8,128)(2,1)}, u32[]{:S(2)}, u32[]{:S(2)}) collective-permute-start(bf16[128,2048]{1,0:T(8,128)(2,1)S(1)} %broadcast_select_fusion.x0), channel_id=1, source_target_pairs={{0,2},{1,3},{2,0},{3,1},{4,6},{5,7},{6,4},{7,5},{8,10},{9,11},{10,... | collective-permute-start | bytes 1572872 | tf_op jit(solution)/shard_map/ppermute | solution.py:166
  66.8 18.2 %collective-permute-start.14 = (bf16[128,2048]{1,0:T(8,128)(2,1)}, bf16[128,2048]{1,0:T(8,128)(2,1)}, u32[]{:S(2)}, u32[]{:S(2)}) collective-permute-start(bf16[128,2048]{1,0:T(8,128)(2,1)} %collective-permute-done.10.x1), channel_id=1, source_target_pairs={{0,1},{1,0},{2,3},{3,2},{4,5},{5,4},{6,7},{7,6},{8,9},{9,8},{10,11... | collective-permute-start | bytes 1572872 | tf_op jit(solution)/shard_map/ppermute | solution.py:166
  67.0 18.0 %collective-permute-start.15 = (bf16[128,2048]{1,0:T(8,128)(2,1)S(1)}, bf16[128,2048]{1,0:T(8,128)(2,1)}, u32[]{:S(2)}, u32[]{:S(2)}) collective-permute-start(bf16[128,2048]{1,0:T(8,128)(2,1)S(1)} %broadcast_select_fusion.x0), channel_id=1, source_target_pairs={{0,1},{1,0},{2,3},{3,2},{4,5},{5,4},{6,7},{7,6},{8,9},{9,8},{10,11... | collective-permute-start | bytes 1572872 | tf_op jit(solution)/shard_map/ppermute | solution.py:166
  67.4 1.9 copy-start.5
  69.3 1.9 copy-start.9
  71.2 1.9 copy-start.13
  73.1 1.0 copy-start.18
  74.1 1.0 copy-start.20
  84.1 0.8 copy-start.31
  85.0 18.3 %collective-permute-start.18 = (bf16[256,2048]{1,0:T(8,128)(2,1)}, bf16[256,2048]{1,0:T(8,128)(2,1)}, u32[]{:S(2)}, u32[]{:S(2)}) collective-permute-start(bf16[256,2048]{1,0:T(8,128)(2,1)} %get-tuple-element.85), channel_id=1, source_target_pairs={{0,1},{1,0},{2,3},{3,2},{4,5},{5,4},{6,7},{7,6},{8,9},{9,8},{10,11... | collective-permute-start | bytes 3145736 | tf_op jit(solution)/shard_map/ppermute | solution.py:166
  85.3 18.0 %collective-permute-start.17 = (bf16[128,2048]{1,0:T(8,128)(2,1)}, bf16[128,2048]{1,0:T(8,128)(2,1)}, u32[]{:S(2)}, u32[]{:S(2)}) collective-permute-start(bf16[128,2048]{1,0:T(8,128)(2,1)} %collective-permute-done.13.x1), channel_id=1, source_target_pairs={{0,1},{1,0},{2,3},{3,2},{4,5},{5,4},{6,7},{7,6},{8,9},{9,8},{10,11... | collective-permute-start | bytes 1572872 | tf_op jit(solution)/shard_map/ppermute | solution.py:166
  85.6 1.0 copy-start.1
  86.7 1.9 copy-start.6
  88.6 1.9 copy-start.10
  90.5 1.9 copy-start.14
  92.4 1.0 copy-start.22
  102.5 0.8 copy-start.33
  103.3 15.3 %collective-permute-start.19 = (bf16[256,2048]{1,0:T(8,128)(2,1)}, bf16[256,2048]{1,0:T(8,128)(2,1)}, u32[]{:S(2)}, u32[]{:S(2)}) collective-permute-start(bf16[256,2048]{1,0:T(8,128)(2,1)} %get-tuple-element.97), channel_id=1, source_target_pairs={{0,1},{1,0},{2,3},{3,2},{4,5},{5,4},{6,7},{7,6},{8,9},{9,8},{10,11... | collective-permute-start | bytes 3145736 | tf_op jit(solution)/shard_map/ppermute | solution.py:166
  103.6 1.0 copy-start.3
  104.7 1.9 copy-start.7
  106.5 1.9 copy-start.11
  108.4 1.9 copy-start.15
  118.6 56.6 %copy-start.34 = (bf16[320,768]{1,0:T(8,128)(2,1)}, bf16[320,768]{1,0:T(8,128)(2,1)S(1)}, u32[]{:S(2)}) copy-start(bf16[320,768]{1,0:T(8,128)(2,1)S(1)} %get-tuple-element.98) | copy-start | bytes 1474564
  118.6 2.7 %collective-permute-start.21 = (bf16[256,2048]{1,0:T(8,128)(2,1)S(1)}, bf16[256,2048]{1,0:T(8,128)(2,1)S(1)}, u32[]{:S(2)}, u32[]{:S(2)}) collective-permute-start(bf16[256,2048]{1,0:T(8,128)(2,1)S(1)} %get-tuple-element.106), channel_id=1, source_target_pairs={{0,1},{1,0},{2,3},{3,2},{4,5},{5,4},{6,7},{7,6},{8,9},{9,8},{10,11... | collective-permute-start | bytes 3145736 | tf_op jit(solution)/shard_map/ppermute | solution.py:166
  121.5 14.8 %collective-permute-start.22 = (bf16[128,2048]{1,0:T(8,128)(2,1)S(1)}, bf16[128,2048]{1,0:T(8,128)(2,1)S(1)}, u32[]{:S(2)}, u32[]{:S(2)}) collective-permute-start(bf16[128,2048]{1,0:T(8,128)(2,1)S(1)} %add_convert_fusion.8), channel_id=1, source_target_pairs={{0,2},{1,3},{2,0},{3,1},{4,6},{5,7},{6,4},{7,5},{8,10},{9,11},{10,... | collective-permute-start | bytes 1572872 | tf_op jit(solution)/shard_map/ppermute | solution.py:166
  123.2 24.3 %collective-permute-start.24 = (bf16[128,2048]{1,0:T(8,128)(2,1)S(1)}, bf16[128,2048]{1,0:T(8,128)(2,1)S(1)}, u32[]{:S(2)}, u32[]{:S(2)}) collective-permute-start(bf16[128,2048]{1,0:T(8,128)(2,1)S(1)} %add_convert_fusion.6), channel_id=1, source_target_pairs={{0,2},{1,3},{2,0},{3,1},{4,6},{5,7},{6,4},{7,5},{8,10},{9,11},{10,... | collective-permute-start | bytes 1572872 | tf_op jit(solution)/shard_map/ppermute | solution.py:166
  136.5 16.9 %collective-permute-start.23 = (bf16[128,2048]{1,0:T(8,128)(2,1)S(1)}, bf16[128,2048]{1,0:T(8,128)(2,1)S(1)}, u32[]{:S(2)}, u32[]{:S(2)}) collective-permute-start(bf16[128,2048]{1,0:T(8,128)(2,1)S(1)} %add_convert_fusion.7), channel_id=1, source_target_pairs={{0,4},{1,5},{2,6},{3,7},{12,8},{13,9},{14,10},{15,11},{16,20},{17,... | collective-permute-start | bytes 1572872 | tf_op jit(solution)/shard_map/ppermute | solution.py:166
  144.5 19.7 %collective-permute-start.27 = (bf16[128,2048]{1,0:T(8,128)(2,1)S(1)}, bf16[128,2048]{1,0:T(8,128)(2,1)S(1)}, u32[]{:S(2)}, u32[]{:S(2)}) collective-permute-start(bf16[128,2048]{1,0:T(8,128)(2,1)S(1)} %add_convert_fusion.3), channel_id=1, source_target_pairs={{0,2},{1,3},{2,0},{3,1},{4,6},{5,7},{6,4},{7,5},{8,10},{9,11},{10,... | collective-permute-start | bytes 1572872 | tf_op jit(solution)/shard_map/ppermute | solution.py:166
  154.9 26.5 %copy-start.30 = (bf16[320,768]{1,0:T(8,128)(2,1)S(1)}, bf16[320,768]{1,0:T(8,128)(2,1)}, u32[]{:S(2)}) copy-start(bf16[320,768]{1,0:T(8,128)(2,1)} %copy-done.29) | copy-start | bytes 1474564
  154.9 26.5 %copy-start.32 = (bf16[320,768]{1,0:T(8,128)(2,1)S(1)}, bf16[320,768]{1,0:T(8,128)(2,1)}, u32[]{:S(2)}) copy-start(bf16[320,768]{1,0:T(8,128)(2,1)} %copy-done.31) | copy-start | bytes 1474564
  154.9 9.3 %collective-permute-start.25 = (bf16[128,2048]{1,0:T(8,128)(2,1)S(1)}, bf16[128,2048]{1,0:T(8,128)(2,1)S(1)}, u32[]{:S(2)}, u32[]{:S(2)}) collective-permute-start(bf16[128,2048]{1,0:T(8,128)(2,1)S(1)} %add_convert_fusion.4), channel_id=1, source_target_pairs={{4,8},{5,9},{6,10},{7,11},{8,4},{9,5},{10,6},{11,7},{20,24},{21,25... | collective-permute-start | bytes 1572872 | tf_op jit(solution)/shard_map/ppermute | solution.py:166
  155.7 14.9 %collective-permute-start.26 = (bf16[128,2048]{1,0:T(8,128)(2,1)S(1)}, bf16[128,2048]{1,0:T(8,128)(2,1)S(1)}, u32[]{:S(2)}, u32[]{:S(2)}) collective-permute-start(bf16[128,2048]{1,0:T(8,128)(2,1)S(1)} %add_convert_fusion.5), channel_id=1, source_target_pairs={{0,4},{1,5},{2,6},{3,7},{12,8},{13,9},{14,10},{15,11},{16,20},{17,... | collective-permute-start | bytes 1572872 | tf_op jit(solution)/shard_map/ppermute | solution.py:166
  163.6 22.4 %collective-permute-start.20 = (bf16[128,2048]{1,0:T(8,128)(2,1)}, bf16[128,2048]{1,0:T(8,128)(2,1)}, u32[]{:S(2)}, u32[]{:S(2)}) collective-permute-start(bf16[128,2048]{1,0:T(8,128)(2,1)} %add_convert_fusion.9), channel_id=1, source_target_pairs={{0,2},{1,3},{2,0},{3,1},{4,6},{5,7},{6,4},{7,5},{8,10},{9,11},{10,... | collective-permute-start | bytes 1572872 | tf_op jit(solution)/shard_map/ppermute | solution.py:166
  171.6 14.5 %collective-permute-start.29 = (bf16[128,2048]{1,0:T(8,128)(2,1)}, bf16[128,2048]{1,0:T(8,128)(2,1)}, u32[]{:S(2)}, u32[]{:S(2)}) collective-permute-start(bf16[128,2048]{1,0:T(8,128)(2,1)} %add_convert_fusion.1), channel_id=1, source_target_pairs={{4,8},{5,9},{6,10},{7,11},{8,4},{9,5},{10,6},{11,7},{20,24},{21,25... | collective-permute-start | bytes 1572872 | tf_op jit(solution)/shard_map/ppermute | solution.py:166
  175.2 13.7 %collective-permute-start.28 = (bf16[128,2048]{1,0:T(8,128)(2,1)}, bf16[128,2048]{1,0:T(8,128)(2,1)S(1)}, u32[]{:S(2)}, u32[]{:S(2)}) collective-permute-start(bf16[128,2048]{1,0:T(8,128)(2,1)} %add_convert_fusion.2), channel_id=1, source_target_pairs={{0,4},{1,5},{2,6},{3,7},{4,0},{5,1},{6,2},{7,3},{8,12},{9,13},{10,... | collective-permute-start | bytes 1572872 | tf_op jit(solution)/shard_map/ppermute | solution.py:166
  (1 other events, 0.8 us)

commit v4 on v1

v4 whole, which is shorter than its diff:
```python
import jax
import jax.numpy as jnp
from jax import lax
from jax.sharding import PartitionSpec as P


def gram_of(rows):
    return lax.dot_general(rows, rows, (((0,), (0,)), ((), ())), preferred_element_type=jnp.float32)


def expert_pass(rows, w_gate, w_up, w_down):
    gate = jnp.dot(rows, w_gate, preferred_element_type=jnp.float32)
    up = jnp.dot(rows, w_up, preferred_element_type=jnp.float32)
    act = (jax.nn.silu(gate) * up).astype(jnp.bfloat16)
    gram_sum = gram_of(act)
    made = jnp.dot(act, w_down, preferred_element_type=jnp.float32).astype(jnp.bfloat16)
    return (gram_sum, made)


def weights_for_me(routes, probs, experts):
    names = routes.T[None, :, :] == jnp.arange(experts, dtype=jnp.int32)[:, None, None]
    weight = jnp.sum(jnp.where(names, probs.T[None, :, :], 0.0), axis=1)
    mine = jnp.where(jnp.any(names, axis=1), weight, -1.0)
    return lax.all_to_all(mine, "expert", split_axis=0, concat_axis=0, tiled=True)


def shards(routes, probs, tokens, gate_weight, up_weight, down_weight):
    tok_rows, top = routes.shape
    features = tokens.shape[1]
    size = lax.axis_size("expert")
    capacity = tok_rows * top // 2
    core = lax.axis_index("expert") % 2
    groups = [list(range(core, size, 2)) for core in range(2)]
    swap = [(i, i ^ 1) for i in range(size)]

    weight = weights_for_me(routes, probs, size)
    near = lax.all_gather(tokens, "expert", axis_index_groups=groups, tiled=True)
    far = lax.ppermute(near, "expert", swap)

    named = (weight >= 0.0).astype(jnp.int32)
    within = jnp.cumsum(named, axis=1) - named
    per_device = jnp.sum(named, axis=1)
    before = jnp.cumsum(per_device) - per_device
    rank = within + before[:, None]
    kept = (named == 1) & (rank < capacity)
    count = jnp.minimum(jnp.sum(per_device), capacity)
    slot = jnp.where(kept, rank, -1).reshape(size // 2, 2, tok_rows)
    place = jnp.arange(capacity, dtype=jnp.int32)

    def select_of(which):
        own = lax.dynamic_index_in_dim(slot, which, 1, False).reshape(size // 2 * tok_rows)
        return (place[:, None] == own[None, :]).astype(jnp.bfloat16)

    def spread_of(select, which):
        share = lax.dynamic_index_in_dim(
            weight.reshape(size // 2, 2, tok_rows), which, 1, False
        ).reshape(size // 2 * tok_rows, 1)
        spread = lax.dot_general(
            select, made, (((0,), (0,)), ((), ())), preferred_element_type=jnp.float32
        )
        return (spread * share).astype(jnp.bfloat16)

    near_select, far_select = select_of(core), select_of(1 - core)
    near_rows = jnp.dot(near_select, near, preferred_element_type=jnp.float32)
    rows = near_rows + jnp.dot(far_select, far, preferred_element_type=jnp.float32)
    rows = rows.astype(jnp.bfloat16)
    gram_sum, made = expert_pass(rows, gate_weight[0], up_weight[0], down_weight[0])
    gram = gram_sum * (2.0 / count.astype(jnp.float32))
    came = lax.ppermute(spread_of(far_select, 1 - core), "expert", swap)
    partial = spread_of(near_select, core).astype(jnp.float32) + came.astype(jnp.float32)
    mixed = lax.psum_scatter(
        partial.astype(jnp.bfloat16),
        "expert",
        scatter_dimension=0,
        axis_index_groups=groups,
        tiled=True,
    )
    return (gram[None], mixed)


def solution(mesh):
    placed = (
        P(("parts", "expert"), None),
        P(("parts", "expert"), None),
        P(("parts", "expert"), None),
        P("expert", None, None),
        P("expert", None, None),
        P("expert", None, None),
    )
    return jax.shard_map(
        shards,
        mesh=mesh,
        in_specs=placed,
        out_specs=(P(("parts", "expert"), None, None), P(("parts", "expert"), None)),
        check_vma=False,
    )
```

time: 222 us -> 222 us (level)
  blocking collectives: 14.1 us -> 0 us
  waiting for transfers between devices: 159 us -> 173 us
  other arithmetic: 1.22 us -> 3.78 us
    all_gather x1, waiting for transfers between devices: 51.9 us -> 78.4 us  [shards(): lax.all_gather(tokens, 'expert', axis_index_groups=groups, tiled=True)]
    reduce_scatter x1, waiting for transfers between devices: 98.6 us -> 81 us  [shards(): lax.psum_scatter(partial.astype(jnp.bfloat16), 'expert', scatter_dimensio...]
    all_to_all x1 -> x0, blocking collectives: 14.1 us -> none  [small_gather(): return lax.all_to_all(copies, axis, split_axis=0, concat_axis=0, tiled=True)]
    ppermute x0 -> x2, waiting for transfers between devices: none -> 7.15 us  [the longest x1 7.15 us: shards(): came = lax.ppermute(spread_of(far_select, 1 - core), 'expert', swap)]
    dot_general x2 -> x5, matrix products: 17.7 us -> 18.5 us  [the longest x2 7.37 us: spread_of(): lax.dot_general(select, made, (((0,), (0,)), ((), ())), preferred_element...]
  transfers between devices with their start and end apart: 3 -> 5, of which waited for: 3 -> 4; matrix products, arithmetic and copies ran while one was open for 3% -> 6% of each run, Pallas kernels for 0% -> 0%
where the time goes in v4:
time: 222 us
  waiting for transfers between devices  173 us (78%)
  matrix products  25.8 us (12%)
  between operations  14.9 us (7%)
  other arithmetic  3.78 us (2%)
  starting transfers between devices  3.62 us (2%)
    reduce_scatter x1, waiting for transfers between devices, shards(): lax.psum_scatter(partial.astype(jnp.bfloat16), 'expert', scatter_dimensio...  81 us
    all_gather x1, waiting for transfers between devices, shards(): lax.all_gather(tokens, 'expert', axis_index_groups=groups, tiled=True)  78.4 us
    dot_general x2, matrix products, spread_of(): lax.dot_general(select, made, (((0,), (0,)), ((), ())), preferred_element...  7.37 us
    ppermute x1, waiting for transfers between devices, shards(): came = lax.ppermute(spread_of(far_select, 1 - core), 'expert', swap)  7.15 us
    all_to_all x1, waiting for transfers between devices, weights_for_me(): lax.all_to_all(mine, 'expert', split_axis=0, concat_axis=0, tiled=True)  6.22 us
    dot_general x1, matrix products, shards(): jnp.dot(far_select, far, preferred_element_type=jnp.float32)  4.73 us
    dot_general x1, matrix products, shards(): near_rows = jnp.dot(near_select, near, preferred_element_type=jnp.float32)  4.52 us
  transfers between devices with their start and end apart: 5, of which 4 were waited for; matrix products, arithmetic and copies ran while one was open for 6% of the time, Pallas kernels for 0%

profile of v4, /device:TPU:0, one launch (start us, length us, event | category | flops | bytes accessed | tf_op | source)
XLA Modules:
  0.0 221.9 jit_solution(1774317052126117722)
XLA Ops:
  7.2 0.0 copy-start
  7.2 0.0 all-gather.2.cloned.1.call-start
  7.2 0.7 all-gather.2.cloned.1.call-update
  7.9 78.4 %all-gather.2.cloned.1.call-done = bf16[1024,2048]{1,0:T(8,128)(2,1)} async-done(((bf16[128,2048]{1,0:T(8,128)(2,1)}), bf16[1024,2048]{1,0:T(8,128)(2,1)}) %all-gather.2.cloned.1.call-update) | async-done | bytes 4194320 | tf_op jit(solution)/shard_map/all_gather | solution.py:37
  86.3 0.0 collective-permute-start
  86.3 0.7 fusion.16
  87.0 0.7 select_reduce_fusion
  87.7 0.6 broadcast_select_fusion
  88.3 3.5 %all-to-all-start = ((f32[16,1,128]{2,1,0:T(1,128)}), f32[16,1,128]{2,1,0:T(1,128)S(1)}, u32[]{:S(2)}, u32[]{:S(2)}) async-start(f32[16,1,128]{2,1,0:T(1,128)} %bitcast.3), calls=%async_computation | async-start | bytes 16384 | tf_op jit(solution)/shard_map/all_to_all | solution.py:24
  91.8 0.0 reduce-scatter.2.cloned.1.call-start
  91.9 6.2 %all-to-all-done = f32[16,1,128]{2,1,0:T(1,128)S(1)} async-done(((f32[16,1,128]{2,1,0:T(1,128)}), f32[16,1,128]{2,1,0:T(1,128)S(1)}, u32[]{:S(2)}, u32[]{:S(2)}) %all-to-all-start) | async-done | bytes 8224 | tf_op jit(solution)/shard_map/all_to_all | solution.py:24
  98.1 0.9 fusion.18
  99.0 0.1 reduce_sum.31
  99.1 0.1 copy.18
  99.2 0.1 reduce.3
  99.3 0.1 reshape.60
  99.4 0.1 copy.19
  99.5 0.6 reduce_window_sum.18
  100.1 0.1 and_select_fusion
  100.2 4.5 %fusion.9 = f32[512,2048]{1,0:T(8,128)S(1)} fusion(bf16[1024,2048]{1,0:T(8,128)(2,1)} %all-gather.2.cloned.1.call-done, s32[1024]{0:T(1024)S(1)} %get-tuple-element.7), kind=kOutput, calls=%fused_computation.14 | convolution fusion | flops 2148007936 | bytes 8392704 | tf_op jit(solution)/shard_map/dot_general | solution.py:64
  104.7 0.0 collective-permute-done
  104.7 0.0 copy-start.1
  104.7 4.7 %add_convert_fusion.1 = bf16[512,2048]{1,0:T(8,128)(2,1)S(1)} fusion(f32[512,2048]{1,0:T(8,128)S(1)} %fusion.9, bf16[1024,2048]{1,0:T(8,128)(2,1)} %collective-permute-done, s32[1024]{0:T(1024)S(1)} %get-tuple-element.6), kind=kOutput, calls=%fused_computation.3 | convolution fusion | flops 2150105088 | bytes 10489856 | tf_op jit(solution)/shard_map/dot_general | solution.py:65
  109.5 0.0 copy-done.1
  109.5 0.0 copy-start.2
  109.5 1.8 fusion.4
  111.3 0.1 copy-done.2
  111.4 1.9 multiply_convert_fusion.2
  113.3 0.0 copy-done
  113.3 0.0 copy-start.3
  113.3 1.8 fusion.6
  115.2 0.0 copy-done.3
  115.2 2.4 %multiply_convert_fusion = bf16[1024,2048]{1,0:T(8,128)(2,1)S(1)} fusion(bf16[512,2048]{1,0:T(8,128)(2,1)S(1)} %fusion.6, f32[1024]{0:T(1024)S(1)} %bitcast.44, s32[1024]{0:T(1024)S(1)} %get-tuple-element.6), kind=kOutput, calls=%fused_computation.1 | convolution fusion | flops 2152202240 | bytes 6299648 | tf_op jit(solution)/shard_map/dot_general | solution.py:58
  117.6 0.1 collective-permute-start.1
  117.7 7.1 %collective-permute-done.1 = bf16[1024,2048]{1,0:T(8,128)(2,1)S(1)} collective-permute-done((bf16[1024,2048]{1,0:T(8,128)(2,1)S(1)}, bf16[1024,2048]{1,0:T(8,128)(2,1)S(1)}, u32[]{:S(2)}, u32[]{:S(2)}) %collective-permute-start.1) | collective-permute-done | bytes 4194336 | tf_op jit(solution)/shard_map/ppermute | solution.py:69
  124.8 4.9 %add_convert_fusion = bf16[1024,2048]{1,0:T(8,128)(2,1)} fusion(bf16[1024,2048]{1,0:T(8,128)(2,1)S(1)} %collective-permute-done.1, f32[1024]{0:T(1024)S(1)} %bitcast.43, bf16[512,2048]{1,0:T(8,128)(2,1)S(1)} %fusion.6, s32[1024]{0:T(1024)S(1)} %get-tuple-element.7), kind=kOutput, calls=%fused_computation | convolution fusion | flops 2160590848 | bytes 10493952 | tf_op jit(solution)/shard_map/dot_general | solution.py:58
  129.8 0.0 reduce-scatter.2.cloned.1.call-update
  130.5 3.6 %multiply_bitcast_fusion = f32[1,768,768]{2,1,0:T(8,128)} fusion(bf16[512,768]{1,0:T(8,128)(2,1)} %copy-done.3, f32[]{:T(128)S(6)} %div.8), kind=kOutput, calls=%fused_computation.11 | convolution fusion | flops 604569600 | bytes 3145732 | tf_op jit(solution)/shard_map/dot_general | solution.py:8
  134.1 81.0 %reduce-scatter.2.cloned.1.call-done = bf16[128,2048]{1,0:T(8,128)(2,1)} async-done(((bf16[1024,2048]{1,0:T(8,128)(2,1)}), bf16[128,2048]{1,0:T(8,128)(2,1)}) %reduce-scatter.2.cloned.1.call-update) | async-done | bytes 524304 | tf_op jit(solution)/shard_map/reduce_scatter | solution.py:71
  (5 shorter events, 0.1 us)
Async XLA Ops:
  7.2 106.1 %copy-start = (bf16[1,768,2048]{2,1,0:T(8,128)(2,1)S(1)}, bf16[1,768,2048]{2,1,0:T(8,128)(2,1)}, u32[]{:S(2)}) copy-start(bf16[1,768,2048]{2,1,0:T(8,128)(2,1)} %param.11) | copy-start | bytes 9437188
  7.2 79.1 %all-gather.2.cloned.1.call-start = ((), (), s32[]{:S(2)}) async-start(), calls=%async_computation.2 | async-start | bytes 4718592 | tf_op jit(solution)/shard_map/all_gather | solution.py:37
  86.3 18.4 %collective-permute-start = (bf16[1024,2048]{1,0:T(8,128)(2,1)}, bf16[1024,2048]{1,0:T(8,128)(2,1)}, u32[]{:S(2)}, u32[]{:S(2)}) collective-permute-start(bf16[1024,2048]{1,0:T(8,128)(2,1)} %all-gather.2.cloned.1.call-done), channel_id=1, source_target_pairs={{0,1},{1,0},{2,3},{3,2},{4,5},{5,4},{6,7},{7,6},{8,9},{9,8},{10,11... | collective-permute-start | bytes 12582920 | tf_op jit(solution)/shard_map/ppermute | solution.py:38
  88.3 9.8 %all-to-all-start = ((f32[16,1,128]{2,1,0:T(1,128)}), f32[16,1,128]{2,1,0:T(1,128)S(1)}, u32[]{:S(2)}, u32[]{:S(2)}) async-start(f32[16,1,128]{2,1,0:T(1,128)} %bitcast.3), calls=%async_computation | async-start | bytes 16384 | tf_op jit(solution)/shard_map/all_to_all | solution.py:24
  91.8 123.3 %reduce-scatter.2.cloned.1.call-start = ((), (), s32[]{:S(2)}) async-start(), calls=%async_computation.3 | async-start | bytes 4718592 | tf_op jit(solution)/shard_map/reduce_scatter | solution.py:71
  104.7 4.8 %copy-start.1 = (bf16[1,2048,768]{2,1,0:T(8,128)(2,1)S(1)}, bf16[1,2048,768]{2,1,0:T(8,128)(2,1)}, u32[]{:S(2)}) copy-start(bf16[1,2048,768]{2,1,0:T(8,128)(2,1)} %param.9) | copy-start | bytes 9437188
  109.5 1.9 copy-start.2
  113.3 1.9 copy-start.3
  117.6 7.2 %collective-permute-start.1 = (bf16[1024,2048]{1,0:T(8,128)(2,1)S(1)}, bf16[1024,2048]{1,0:T(8,128)(2,1)S(1)}, u32[]{:S(2)}, u32[]{:S(2)}) collective-permute-start(bf16[1024,2048]{1,0:T(8,128)(2,1)S(1)} %multiply_convert_fusion), channel_id=1, source_target_pairs={{0,1},{1,0},{2,3},{3,2},{4,5},{5,4},{6,7},{7,6},{8,9},{9,8},{10,11... | collective-permute-start | bytes 12582920 | tf_op jit(solution)/shard_map/ppermute | solution.py:69
Sparse Core Ops, SparseCore 0:
  10.1 76.0 all-gather.1
  129.9 85.1 reduce-scatter.1

commit v5 on v2

v5 whole, which is shorter than its diff:
```python
import functools

import jax
import jax.numpy as jnp
from jax import lax
from jax.experimental import pallas as pl
from jax.experimental.pallas import tpu as pltpu
from jax.sharding import PartitionSpec as P


def gram_of(rows):
    return lax.dot_general(rows, rows, (((0,), (0,)), ((), ())), preferred_element_type=jnp.float32)


def expert_pass(rows, w_gate, w_up, w_down):
    gate = jnp.dot(rows, w_gate, preferred_element_type=jnp.float32)
    up = jnp.dot(rows, w_up, preferred_element_type=jnp.float32)
    act = (jax.nn.silu(gate) * up).astype(jnp.bfloat16)
    gram_sum = gram_of(act)
    made = jnp.dot(act, w_down, preferred_element_type=jnp.float32).astype(jnp.bfloat16)
    return (gram_sum, made)


def weights_for_me(routes, probs, experts):
    names = routes.T[None, :, :] == jnp.arange(experts, dtype=jnp.int32)[:, None, None]
    weight = jnp.sum(jnp.where(names, probs.T[None, :, :], 0.0), axis=1)
    mine = jnp.where(jnp.any(names, axis=1), weight, -1.0)
    return lax.all_to_all(mine, "expert", split_axis=0, concat_axis=0, tiled=True)


def summed(*parts):
    total = parts[0].astype(jnp.float32)
    for part in parts[1:]:
        total = total + part.astype(jnp.float32)
    return total.astype(jnp.bfloat16)


def plane_kernel(
    capacity, order, weight, x0, x1, x2, x3, w_gate, w_up, w_down, keep, give, act, rows, ranks
):
    blocks, tok = weight.shape
    features = x0.shape[1]
    slots, hidden = act.shape
    wide = 256
    named = (weight[...] >= 0.0).astype(jnp.float32)
    lane = lax.broadcasted_iota(jnp.int32, (tok, tok), 0)
    below = (lane < lax.broadcasted_iota(jnp.int32, (tok, tok), 1)).astype(jnp.float32)
    within = jnp.dot(named, below, preferred_element_type=jnp.float32)
    totals = jnp.broadcast_to(jnp.sum(named, axis=1, keepdims=True), (blocks, tok))
    row = lax.broadcasted_iota(jnp.int32, (blocks, blocks), 0)
    earlier = (lax.broadcasted_iota(jnp.int32, (blocks, blocks), 1) < row).astype(jnp.float32)
    before = jnp.dot(earlier, totals, preferred_element_type=jnp.float32)
    rank = within + before
    kept = (named > 0.0) & (rank < capacity)
    first = order[0] // 4 * 4
    block_row = lax.broadcasted_iota(jnp.int32, (blocks, tok), 0)
    start = jnp.sum(jnp.where(block_row == first, before, 0.0), axis=0, keepdims=True)
    ranks[...] = jnp.where(kept, rank - start, -1.0)

    places = [ranks[pl.ds(order[i], 1), :] for i in range(4)]
    shares = [weight[pl.ds(order[i], 1), :] for i in range(4)]
    place = jnp.concatenate(places, axis=1)
    share = jnp.concatenate(shares, axis=1)
    slot = lax.broadcasted_iota(jnp.int32, (slots, 4 * tok), 0).astype(jnp.float32)
    hits = slot == place
    scale = jnp.sum(jnp.where(hits, share, 0.0), axis=1, keepdims=True)
    select = hits.astype(jnp.float32).astype(jnp.bfloat16)
    for i in range(features // 512):
        span = pl.ds(i * 512, 512)
        x = jnp.concatenate([x0[:, span], x1[:, span], x2[:, span], x3[:, span]], axis=0)
        rows[:, span] = jnp.dot(select, x, preferred_element_type=jnp.float32).astype(jnp.bfloat16)
    for i in range(hidden // wide):
        span = pl.ds(i * wide, wide)
        gate = jnp.dot(rows[...], w_gate[:, span], preferred_element_type=jnp.float32)
        up = jnp.dot(rows[...], w_up[:, span], preferred_element_type=jnp.float32)
        act[:, span] = (gate / (1.0 + jnp.exp(-gate)) * up).astype(jnp.bfloat16)
    back = select.T
    for i in range(features // 512):
        span = pl.ds(i * 512, 512)
        result = jnp.dot(act[...], w_down[:, span], preferred_element_type=jnp.float32)
        made = (result * scale).astype(jnp.bfloat16)
        spread = jnp.dot(back, made, preferred_element_type=jnp.float32).astype(jnp.bfloat16)
        keep[:, span] = spread[: 2 * tok]
        give[:, span] = spread[2 * tok :]


def plane_pass(order, weight, xs, w_gate, w_up, w_down, slots, capacity):
    tok, features = xs[0].shape
    hidden = w_gate.shape[1]
    half = jax.ShapeDtypeStruct((2 * tok, features), jnp.bfloat16)
    rows = 4 * slots
    flops = 2 * rows * (3 * features * hidden + 8 * tok * features)
    moved = 2 * (3 * features * hidden + 8 * tok * features)
    return pl.pallas_call(
        functools.partial(plane_kernel, capacity),
        out_shape=(half, half, jax.ShapeDtypeStruct((rows, hidden), jnp.bfloat16)),
        in_specs=[pl.BlockSpec(memory_space=pltpu.SMEM)]
        + [pl.BlockSpec(memory_space=pltpu.VMEM)] * 8,
        out_specs=[pl.BlockSpec(memory_space=pltpu.VMEM)] * 3,
        scratch_shapes=[
            pltpu.VMEM((rows, features), jnp.bfloat16),
            pltpu.VMEM(weight.shape, jnp.float32),
        ],
        compiler_params=pltpu.CompilerParams(vmem_limit_bytes=32 * 1024 * 1024),
        cost_estimate=pl.CostEstimate(
            flops=flops, bytes_accessed=moved, transcendentals=rows * hidden
        ),
    )(order, weight, *xs, w_gate, w_up, w_down)


def staged(routes, probs, tokens, w_gate, w_up, w_down):
    tok, top = routes.shape
    size = lax.axis_size("expert")
    slots = 5 * tok * top // (4 * size)
    capacity = tok * top // 2
    half = tok // 2
    me = lax.axis_index("expert")
    z, y, core = me // 4, me // 2 % 2, me % 2

    def swapped(array, bit):
        return lax.ppermute(array, "expert", [(i, i ^ bit) for i in range(size)])

    sibling = functools.partial(swapped, bit=1)
    column = functools.partial(swapped, bit=2)
    pair = functools.partial(swapped, bit=4)
    far = functools.partial(swapped, bit=8)

    def together(*arrays):
        return lax.optimization_barrier(arrays)

    def expert(k, *xs):
        base = (z ^ k) * 4
        order = jnp.stack(
            [
                base + y * 2 + core,
                base + (1 - y) * 2 + core,
                base + y * 2 + 1 - core,
                base + (1 - y) * 2 + 1 - core,
            ]
        ).astype(jnp.int32)
        return plane_pass(order, weight, xs, w_gate, w_up, w_down, slots, capacity)

    weight = weights_for_me(routes, probs, size)
    a0 = tokens
    a1 = pair(a0)
    a2 = far(a0)
    b0 = column(a0)
    c0 = sibling(a0)
    a1, b0, c0, weight = together(a1, b0, c0, weight)
    b1 = column(a1)
    d0 = sibling(b0)
    c1 = sibling(a1)
    keep0, give0, act0 = expert(0, a0, b0, c0, d0)
    a2, b1, c1, keep0, give0, act0 = together(a2, b1, c1, keep0, give0, act0)
    a3 = pair(a2)
    b2 = column(a2)
    d1 = sibling(b1)
    c2 = sibling(a2)
    keep1, give1, act1 = expert(1, a1, b1, c1, d1)
    a3, b2, c2, keep1, give1, act1 = together(a3, b2, c2, keep1, give1, act1)
    b3_low = pair(b2[:half])
    b3_high = column(a3[half:])
    d2 = sibling(b2)
    c3 = sibling(a3)
    got1 = sibling(give1)
    keep2, give2, act2 = expert(2, a2, b2, c2, d2)
    b3_low, b3_high, c3, got1, keep2, give2, act2 = together(
        b3_low, b3_high, c3, got1, keep2, give2, act2
    )
    b3 = jnp.concatenate([b3_low, b3_high], axis=0)
    d3 = sibling(b3)
    came1 = column(summed(keep1[tok:], got1[tok:]))
    got2 = sibling(give2)
    keep3, give3, act3 = expert(3, a3, b3, c3, d3)

    keep3, give3, act3, got2, came1 = together(keep3, give3, act3, got2, came1)
    got3 = sibling(give3)
    got0 = sibling(give0)
    got3, got0 = together(got3, got0)
    low = pair(summed(keep3[tok : tok + half], got3[tok : tok + half]))
    high = column(summed(keep3[tok + half :], got3[tok + half :]))
    low, high = together(low, high)
    far3 = jnp.concatenate(
        [summed(keep3[:half], got3[:half]), summed(keep3[half:tok], got3[half:tok], high)], axis=0
    )
    side2 = jnp.concatenate(
        [
            summed(keep2[tok : tok + half], got2[tok : tok + half], low),
            summed(keep2[tok + half :], got2[tok + half :]),
        ],
        axis=0,
    )
    far3, side2 = together(pair(far3), column(side2))
    last2 = far(summed(keep2[:tok], got2[:tok], far3, side2))
    last1 = pair(summed(keep1[:tok], got1[:tok], came1))
    last0 = column(summed(keep0[tok:], got0[tok:]))
    mixed = summed(keep0[:tok], got0[:tok], last0, last1, last2)

    acts = jnp.concatenate([act0, act1, act2, act3], axis=0)
    count = jnp.minimum(jnp.sum((weight >= 0.0).astype(jnp.float32)), float(capacity))
    gram = gram_of(acts) * (2.0 / count)
    return gram[None], mixed


def gathered(routes, probs, tokens, w_gate, w_up, w_down):
    tok_rows, top = routes.shape
    size = lax.axis_size("expert")
    capacity = tok_rows * top // 2
    every_token = lax.all_gather(tokens, "expert", tiled=True)
    weight = weights_for_me(routes, probs, size)
    named = (weight >= 0.0).astype(jnp.int32)
    within = jnp.cumsum(named, axis=1) - named
    per_device = jnp.sum(named, axis=1)
    before = jnp.cumsum(per_device) - per_device
    rank = within + before[:, None]
    kept = (named == 1) & (rank < capacity)
    count = jnp.minimum(jnp.sum(per_device), capacity)
    slot = jnp.where(kept, rank, -1).reshape(size * tok_rows)
    place = jnp.arange(capacity, dtype=jnp.int32)
    select = (place[:, None] == slot[None, :]).astype(jnp.bfloat16)
    rows = jnp.dot(select, every_token, preferred_element_type=jnp.float32).astype(jnp.bfloat16)
    gram_sum, made = expert_pass(rows, w_gate, w_up, w_down)
    gram = gram_sum * (2.0 / count.astype(jnp.float32))
    spread = lax.dot_general(
        select, made, (((0,), (0,)), ((), ())), preferred_element_type=jnp.float32
    )
    partial = (spread * weight.reshape(size * tok_rows, 1)).astype(jnp.bfloat16)
    mixed = lax.psum_scatter(partial, "expert", scatter_dimension=0, tiled=True)
    return gram[None], mixed.astype(jnp.bfloat16)


def shards(routes, probs, tokens, gate_weight, up_weight, down_weight):
    body = staged if lax.axis_size("expert") == 16 else gathered
    return body(routes, probs, tokens, gate_weight[0], up_weight[0], down_weight[0])


def solution(mesh):
    placed = (
        P(("parts", "expert"), None),
        P(("parts", "expert"), None),
        P(("parts", "expert"), None),
        P("expert", None, None),
        P("expert", None, None),
        P("expert", None, None),
    )
    return jax.shard_map(
        shards,
        mesh=mesh,
        in_specs=placed,
        out_specs=(P(("parts", "expert"), None, None), P(("parts", "expert"), None)),
        check_vma=False,
    )
```

time: 192 us -> 167 us (0.87)
  waiting for transfers between devices: 84.6 us -> 39.7 us
  local copies, waits for them, and re-layouts: 18.4 us -> 44.8 us
  starting transfers between devices: 38.5 us -> 20.9 us
  blocking collectives: 0 us -> 12.4 us
  Pallas kernels: 32.6 us -> 28.6 us
  matrix products: 3.22 us -> 5.31 us
    ppermute x30 -> x28, waiting for transfers between devices: 84.6 us -> 39.7 us  [swapped(): return lax.ppermute(array, 'expert', [(i, i ^ bit) for i in range(size)])]
    unnamed x50 -> x81, local copies, waits for them, and re-layouts: 18.4 us -> 43.1 us
    ppermute x30 -> x28, starting transfers between devices: 33.6 us -> 20.9 us  [swapped(): return lax.ppermute(array, 'expert', [(i, i ^ bit) for i in range(size)])]
    all_to_all x0 -> x1, blocking collectives: none -> 12.4 us  [weights_for_me(): lax.all_to_all(mine, 'expert', split_axis=0, concat_axis=0, tiled=True)]
    all_to_all x1 -> x0, starting transfers between devices: 4.92 us -> none  [weights_for_me(): lax.all_to_all(mine, 'expert', split_axis=0, concat_axis=0, tiled=True)]
    pallas_call x4, Pallas kernels: 32.6 us -> 28.6 us  [plane_pass(): pl.pallas_call(functools.partial(plane_kernel, capacity), out_shape=(half...]
    dot_general x1, matrix products: 3.22 us -> 5.31 us  [gram_of(): lax.dot_general(rows, rows, (((0,), (0,)), ((), ())), preferred_element_t...]
    convert_element_type x10 -> x8, other arithmetic: 10.2 us -> 9.77 us  [summed(): return total.astype(jnp.bfloat16)]
  transfers between devices with their start and end apart: 31 -> 28, of which waited for: 10 -> 10; matrix products, arithmetic and copies ran while one was open for 7% -> 9% of each run, Pallas kernels for 17% -> 17%
where the time goes in v5:
time: 167 us; the launch traced here: 166 us
  local copies, waits for them, and re-layouts  44.8 us (27%)
  waiting for transfers between devices  39.7 us (24%)
  Pallas kernels  28.6 us (17%)
  starting transfers between devices  20.9 us (13%)
  blocking collectives  12.4 us (7%)
  other arithmetic  12.2 us (7%)
  matrix products  5.31 us (3%)
    unnamed x81, local copies, waits for them, and re-layouts  43.1 us
    ppermute x28, waiting for transfers between devices, swapped(): return lax.ppermute(array, 'expert', [(i, i ^ bit) for i in range(size)])  39.7 us
    pallas_call x4, Pallas kernels, plane_pass(): pl.pallas_call(functools.partial(plane_kernel, capacity), out_shape=(half...  28.6 us
    ppermute x28, starting transfers between devices, swapped(): return lax.ppermute(array, 'expert', [(i, i ^ bit) for i in range(size)])  20.9 us
    all_to_all x1, blocking collectives, weights_for_me(): lax.all_to_all(mine, 'expert', split_axis=0, concat_axis=0, tiled=True)  12.4 us
    convert_element_type x8, other arithmetic, summed(): return total.astype(jnp.bfloat16)  9.77 us
    dot_general x1, matrix products, gram_of(): lax.dot_general(rows, rows, (((0,), (0,)), ((), ())), preferred_element_t...  5.31 us
  transfers between devices with their start and end apart: 28, of which 10 were waited for; matrix products, arithmetic and copies ran while one was open for 9% of the time, Pallas kernels for 17%

profile of v5, /device:TPU:0, one launch (start us, length us, event | category | flops | bytes accessed | tf_op | source)
XLA Modules:
  0.0 165.5 jit_solution(12853232702013105577)
XLA Ops:
  0.6 3.1 %collective-permute-start.1 = (bf16[128,2048]{1,0:T(8,128)(2,1)}, bf16[128,2048]{1,0:T(8,128)(2,1)S(1)}, u32[]{:S(2)}, u32[]{:S(2)}) collective-permute-start(bf16[128,2048]{1,0:T(8,128)(2,1)} %x0.1), channel_id=1, source_target_pairs={{0,4},{1,5},{2,6},{3,7},{4,0},{5,1},{6,2},{7,3},{8,12},{9,13},{10,... | collective-permute-start | bytes 1572872 | tf_op jit(solution)/shard_map/ppermute | solution.py:121
  3.7 1.5 collective-permute-start.2
  6.7 12.4 %all_to_all.9 = f32[16,1,128]{2,1,0:T(1,128)S(1)} all-to-all(f32[16,1,128]{2,1,0:T(1,128)S(1)} %bitcast.44), channel_id=1, replica_groups=mesh['parts'=2,'expert'=16] {'expert'}, dimensions={0} | all-to-all | bytes 16384 | tf_op jit(solution)/shard_map/all_to_all | solution.py:28
  19.1 0.8 copy-done.26
  20.0 0.8 copy-done.24
  20.8 1.0 collective-permute-start
  21.7 1.5 collective-permute-start.4
  23.3 0.8 copy-done.28
  24.2 1.9 %copy-done.2 = bf16[1,2048,768]{2,1,0:T(8,128)(2,1)S(1)} copy-done((bf16[1,2048,768]{2,1,0:T(8,128)(2,1)S(1)}, bf16[1,2048,768]{2,1,0:T(8,128)(2,1)}, u32[]{:S(2)}) %copy-start.2) | copy-done | bytes 3145752
  26.0 1.9 %copy-done.6 = bf16[1,2048,768]{2,1,0:T(8,128)(2,1)S(1)} copy-done((bf16[1,2048,768]{2,1,0:T(8,128)(2,1)S(1)}, bf16[1,2048,768]{2,1,0:T(8,128)(2,1)}, u32[]{:S(2)}) %copy-start.6) | copy-done | bytes 3145752
  27.9 1.9 %copy-done.10 = bf16[1,768,2048]{2,1,0:T(8,128)(2,1)S(1)} copy-done((bf16[1,768,2048]{2,1,0:T(8,128)(2,1)S(1)}, bf16[1,768,2048]{2,1,0:T(8,128)(2,1)}, u32[]{:S(2)}) %copy-start.10) | copy-done | bytes 3145752
  29.8 1.0 copy-done.15
  30.9 1.0 copy-done.25
  31.9 1.0 copy-done.27
  32.9 1.0 copy-done.29
  34.0 6.3 %shard_map.77 = (bf16[256,2048]{1,0:T(8,128)(2,1)S(1)}, bf16[256,2048]{1,0:T(8,128)(2,1)S(1)}, bf16[320,768]{1,0:T(8,128)(2,1)S(1)}) custom-call(s32[4]{0:T(128)S(1)} %pad_add_fusion.order, f32[16,128]{1,0:T(8,128)S(1)} %bitcast.27, bf16[128,2048]{1,0:T(8,128)(2,1)S(1)} %copy-done.15, bf16[128,2048]{1,0:T(8,128)(2,1)S(1)} %copy-done.25, ...), custom_call_target="tpu_custom_call" | custom-call | flops 4362076160 | bytes 13631488 | tf_op jit(solution)/shard_map/pallas_call | solution.py:94
  40.3 1.0 copy-done.14
  41.3 6.1 %collective-permute-done.x0 = bf16[128,2048]{1,0:T(8,128)(2,1)S(1)} collective-permute-done((bf16[128,2048]{1,0:T(8,128)(2,1)}, bf16[128,2048]{1,0:T(8,128)(2,1)S(1)}, u32[]{:S(2)}, u32[]{:S(2)}) %collective-permute-start) | collective-permute-done | bytes 524320 | tf_op jit(solution)/shard_map/ppermute | solution.py:121
  47.4 0.8 copy-done.22
  48.3 0.8 copy-done.20
  50.2 0.8 copy-done.32
  51.0 1.9 %copy-done.3 = bf16[1,2048,768]{2,1,0:T(8,128)(2,1)S(1)} copy-done((bf16[1,2048,768]{2,1,0:T(8,128)(2,1)S(1)}, bf16[1,2048,768]{2,1,0:T(8,128)(2,1)}, u32[]{:S(2)}) %copy-start.3) | copy-done | bytes 3145752
  52.9 1.9 %copy-done.7 = bf16[1,2048,768]{2,1,0:T(8,128)(2,1)S(1)} copy-done((bf16[1,2048,768]{2,1,0:T(8,128)(2,1)S(1)}, bf16[1,2048,768]{2,1,0:T(8,128)(2,1)}, u32[]{:S(2)}) %copy-start.7) | copy-done | bytes 3145752
  54.7 1.9 %copy-done.11 = bf16[1,768,2048]{2,1,0:T(8,128)(2,1)S(1)} copy-done((bf16[1,768,2048]{2,1,0:T(8,128)(2,1)S(1)}, bf16[1,768,2048]{2,1,0:T(8,128)(2,1)}, u32[]{:S(2)}) %copy-start.11) | copy-done | bytes 3145752
  56.6 1.0 copy-done.19
  57.7 1.0 copy-done.21
  58.7 1.0 copy-done.23
  59.8 1.0 copy-done.33
  60.8 7.2 %shard_map.78 = (bf16[256,2048]{1,0:T(8,128)(2,1)S(1)}, bf16[256,2048]{1,0:T(8,128)(2,1)}, bf16[320,768]{1,0:T(8,128)(2,1)S(1)}) custom-call(s32[4]{0:T(128)S(1)} %pad_add_fusion.1.order, f32[16,128]{1,0:T(8,128)S(1)} %bitcast.28, bf16[128,2048]{1,0:T(8,128)(2,1)S(1)} %copy-done.19, bf16[128,2048]{1,0:T(8,128)(2,1)S(1)} %copy-done.21, ...), custom_call_target="tpu_custom_call" | custom-call | flops 4362076160 | bytes 13631488 | tf_op jit(solution)/shard_map/pallas_call | solution.py:94
  69.6 1.0 slice.73
  70.5 2.0 %collective-permute-start.11 = (bf16[64,2048]{1,0:T(8,128)(2,1)S(1)}, bf16[64,2048]{1,0:T(8,128)(2,1)S(1)}, u32[]{:S(2)}, u32[]{:S(2)}) collective-permute-start(bf16[64,2048]{1,0:T(8,128)(2,1)S(1)} %slice.72), channel_id=1, source_target_pairs={{0,4},{1,5},{2,6},{3,7},{4,0},{5,1},{6,2},{7,3},{8,12},{9,13},{10,... | collective-permute-start | bytes 786440 | tf_op jit(solution)/shard_map/ppermute | solution.py:121
  72.5 1.5 collective-permute-start.12
  74.1 0.8 copy-done.30
  74.9 1.0 copy-done.1
  75.9 1.9 %copy-done.4 = bf16[1,2048,768]{2,1,0:T(8,128)(2,1)S(1)} copy-done((bf16[1,2048,768]{2,1,0:T(8,128)(2,1)S(1)}, bf16[1,2048,768]{2,1,0:T(8,128)(2,1)}, u32[]{:S(2)}) %copy-start.4) | copy-done | bytes 3145752
  77.8 1.9 %copy-done.8 = bf16[1,2048,768]{2,1,0:T(8,128)(2,1)S(1)} copy-done((bf16[1,2048,768]{2,1,0:T(8,128)(2,1)S(1)}, bf16[1,2048,768]{2,1,0:T(8,128)(2,1)}, u32[]{:S(2)}) %copy-start.8) | copy-done | bytes 3145752
  79.7 1.9 %copy-done.12 = bf16[1,768,2048]{2,1,0:T(8,128)(2,1)S(1)} copy-done((bf16[1,768,2048]{2,1,0:T(8,128)(2,1)S(1)}, bf16[1,768,2048]{2,1,0:T(8,128)(2,1)}, u32[]{:S(2)}) %copy-start.12) | copy-done | bytes 3145752
  81.6 1.0 copy-done.17
  82.6 1.0 copy-done.31
  83.7 7.9 %shard_map.79 = (bf16[256,2048]{1,0:T(8,128)(2,1)S(1)}, bf16[256,2048]{1,0:T(8,128)(2,1)}, bf16[320,768]{1,0:T(8,128)(2,1)S(1)}) custom-call(s32[4]{0:T(128)S(1)} %pad_add_fusion.2.order, f32[16,128]{1,0:T(8,128)S(1)} %bitcast.29, bf16[128,2048]{1,0:T(8,128)(2,1)S(1)} %copy-done.17, bf16[128,2048]{1,0:T(8,128)(2,1)S(1)} %copy-done.1, ...), custom_call_target="tpu_custom_call" | custom-call | flops 4362076160 | bytes 13631488 | tf_op jit(solution)/shard_map/pallas_call | solution.py:94
  94.3 2.0 %add_convert_fusion.4 = bf16[128,2048]{1,0:T(8,128)(2,1)} fusion(bf16[256,2048]{1,0:T(8,128)(2,1)} %collective-permute-done.14, bf16[256,2048]{1,0:T(8,128)(2,1)S(1)} %get-tuple-element.78), kind=kLoop, calls=%fused_computation.13 | loop fusion | flops 1048576 | bytes 1572864 | tf_op jit(solution)/shard_map/convert_element_type | solution.py:35
  97.0 1.9 %copy-done.5 = bf16[1,2048,768]{2,1,0:T(8,128)(2,1)S(1)} copy-done((bf16[1,2048,768]{2,1,0:T(8,128)(2,1)S(1)}, bf16[1,2048,768]{2,1,0:T(8,128)(2,1)}, u32[]{:S(2)}) %copy-start.5) | copy-done | bytes 3145752
  98.8 1.9 %copy-done.9 = bf16[1,2048,768]{2,1,0:T(8,128)(2,1)S(1)} copy-done((bf16[1,2048,768]{2,1,0:T(8,128)(2,1)S(1)}, bf16[1,2048,768]{2,1,0:T(8,128)(2,1)}, u32[]{:S(2)}) %copy-start.9) | copy-done | bytes 3145752
  100.7 1.9 %copy-done.13 = bf16[1,768,2048]{2,1,0:T(8,128)(2,1)S(1)} copy-done((bf16[1,768,2048]{2,1,0:T(8,128)(2,1)S(1)}, bf16[1,768,2048]{2,1,0:T(8,128)(2,1)}, u32[]{:S(2)}) %copy-start.13) | copy-done | bytes 3145752
  102.6 7.2 %shard_map.80 = (bf16[256,2048]{1,0:T(8,128)(2,1)S(1)}, bf16[256,2048]{1,0:T(8,128)(2,1)S(1)}, bf16[320,768]{1,0:T(8,128)(2,1)S(1)}) custom-call(s32[4]{0:T(128)S(1)} %pad_add_fusion.3.order, f32[16,128]{1,0:T(8,128)S(1)} %bitcast.30, bf16[128,2048]{1,0:T(8,128)(2,1)} %collective-permute-done.7.x0, bf16[128,2048]{1,0:T(8,128)(2,1)} %constant_dynamic-update-slice_fusion.x1, ...), custom_call_target="tpu_custom_call" | custom-call | flops 4362076160 | bytes 13631488 | tf_op jit(solution)/shard_map/pallas_call | solution.py:94
  110.5 2.6 %collective-permute-done.19 = bf16[256,2048]{1,0:T(8,128)(2,1)S(1)} collective-permute-done((bf16[256,2048]{1,0:T(8,128)(2,1)S(1)}, bf16[256,2048]{1,0:T(8,128)(2,1)S(1)}, u32[]{:S(2)}, u32[]{:S(2)}) %collective-permute-start.19) | collective-permute-done | bytes 1048608 | tf_op jit(solution)/shard_map/ppermute | solution.py:121
  113.4 1.1 collective-permute-start.23
  114.6 1.1 collective-permute-start.24
  115.6 6.2 %collective-permute-done.23 = bf16[64,2048]{1,0:T(8,128)(2,1)S(1)} collective-permute-done((bf16[64,2048]{1,0:T(8,128)(2,1)S(1)}, bf16[64,2048]{1,0:T(8,128)(2,1)S(1)}, u32[]{:S(2)}, u32[]{:S(2)}) %collective-permute-start.23) | collective-permute-done | bytes 262176 | tf_op jit(solution)/shard_map/ppermute | solution.py:121
  121.8 1.0 collective-permute-done.24
  122.8 1.2 add_convert_fusion.6
  124.1 0.9 collective-permute-start.26
  125.2 1.3 collective-permute-start.25
  126.5 2.3 %add_convert_fusion.2 = bf16[128,2048]{1,0:T(8,128)(2,1)} fusion(bf16[128,2048]{1,0:T(8,128)(2,1)} %collective-permute-done.18, bf16[256,2048]{1,0:T(8,128)(2,1)} %collective-permute-done.14, bf16[256,2048]{1,0:T(8,128)(2,1)S(1)} %get-tuple-element.78), kind=kLoop, calls=%fused_computation.11 | loop fusion | flops 1572864 | bytes 2097152 | tf_op jit(solution)/shard_map/convert_element_type | solution.py:35
  128.7 0.8 collective-permute-start.22
  129.7 1.3 collective-permute-start.21
  130.9 8.1 %collective-permute-done.26 = bf16[128,2048]{1,0:T(8,128)(2,1)S(1)} collective-permute-done((bf16[128,2048]{1,0:T(8,128)(2,1)S(1)}, bf16[128,2048]{1,0:T(8,128)(2,1)S(1)}, u32[]{:S(2)}, u32[]{:S(2)}) %collective-permute-start.26) | collective-permute-done | bytes 524320 | tf_op jit(solution)/shard_map/ppermute | solution.py:121
  139.1 1.1 collective-permute-done.25
  140.1 1.3 add_convert_fusion.1
  141.5 1.4 collective-permute-start.27
  144.1 5.3 %multiply_bitcast_fusion = f32[1,768,768]{2,1,0:T(8,128)} fusion(f32[]{:T(128)S(6)} %div.24, bf16[320,768]{1,0:T(8,128)(2,1)} %copy-done.37, bf16[320,768]{1,0:T(8,128)(2,1)} %copy-done.36, bf16[320,768]{1,0:T(8,128)(2,1)} %copy-done.35, bf16[320,768]{1,0:T(8,128)(2,1)} %copy-done.34), kind=kOutput, calls=%fused_computation | convolution fusion | flops 1518403584 | bytes 4325380 | tf_op jit(solution)/shard_map/dot_general | solution.py:12
  149.4 9.3 %collective-permute-done.22 = bf16[128,2048]{1,0:T(8,128)(2,1)} collective-permute-done((bf16[128,2048]{1,0:T(8,128)(2,1)}, bf16[128,2048]{1,0:T(8,128)(2,1)}, u32[]{:S(2)}, u32[]{:S(2)}) %collective-permute-start.22) | collective-permute-done | bytes 524320 | tf_op jit(solution)/shard_map/ppermute | solution.py:121
  158.7 4.4 %collective-permute-done.27 = bf16[128,2048]{1,0:T(8,128)(2,1)S(1)} collective-permute-done((bf16[128,2048]{1,0:T(8,128)(2,1)S(1)}, bf16[128,2048]{1,0:T(8,128)(2,1)S(1)}, u32[]{:S(2)}, u32[]{:S(2)}) %collective-permute-start.27) | collective-permute-done | bytes 524320 | tf_op jit(solution)/shard_map/ppermute | solution.py:121
  163.1 2.5 %add_convert_fusion = bf16[128,2048]{1,0:T(8,128)(2,1)} fusion(bf16[128,2048]{1,0:T(8,128)(2,1)S(1)} %collective-permute-done.27, bf16[128,2048]{1,0:T(8,128)(2,1)} %collective-permute-done.22, bf16[128,2048]{1,0:T(8,128)(2,1)} %collective-permute-done.21, bf16[256,2048]{1,0:T(8,128)(2,1)S(1)} %copy-done.39, bf16[256,2048]{1,0:T(8,128)(2,1)S(1)} %get-tuple-element.81), kind=kLoop, calls=%fused_computation.9 | loop fusion | flops 2621440 | bytes 3145728 | tf_op jit(solution)/shard_map/convert_element_type | solution.py:35
  (100 shorter events, 9.4 us)
Async XLA Ops:
  0.6 18.5 %collective-permute-start.1 = (bf16[128,2048]{1,0:T(8,128)(2,1)}, bf16[128,2048]{1,0:T(8,128)(2,1)S(1)}, u32[]{:S(2)}, u32[]{:S(2)}) collective-permute-start(bf16[128,2048]{1,0:T(8,128)(2,1)} %x0.1), channel_id=1, source_target_pairs={{0,4},{1,5},{2,6},{3,7},{4,0},{5,1},{6,2},{7,3},{8,12},{9,13},{10,... | collective-permute-start | bytes 1572872 | tf_op jit(solution)/shard_map/ppermute | solution.py:121
  3.7 15.4 %collective-permute-start.2 = (bf16[128,2048]{1,0:T(8,128)(2,1)}, bf16[128,2048]{1,0:T(8,128)(2,1)S(1)}, u32[]{:S(2)}, u32[]{:S(2)}) collective-permute-start(bf16[128,2048]{1,0:T(8,128)(2,1)} %x0.1), channel_id=1, source_target_pairs={{0,2},{1,3},{2,0},{3,1},{4,6},{5,7},{6,4},{7,5},{8,10},{9,11},{10,... | collective-permute-start | bytes 1572872 | tf_op jit(solution)/shard_map/ppermute | solution.py:121
  5.2 13.9 %collective-permute-start.3 = (bf16[128,2048]{1,0:T(8,128)(2,1)}, bf16[128,2048]{1,0:T(8,128)(2,1)S(1)}, u32[]{:S(2)}, u32[]{:S(2)}) collective-permute-start(bf16[128,2048]{1,0:T(8,128)(2,1)} %x0.1), channel_id=1, source_target_pairs={{0,1},{1,0},{2,3},{3,2},{4,5},{5,4},{6,7},{7,6},{8,9},{9,8},{10,11... | collective-permute-start | bytes 1572872 | tf_op jit(solution)/shard_map/ppermute | solution.py:121
  19.1 21.2 %copy-start.18 = (bf16[128,2048]{1,0:T(8,128)(2,1)}, bf16[128,2048]{1,0:T(8,128)(2,1)S(1)}, u32[]{:S(2)}) copy-start(bf16[128,2048]{1,0:T(8,128)(2,1)S(1)} %collective-permute-done.1.x0) | copy-start | bytes 1572868
  19.1 0.9 copy-start.26
  20.0 3.4 %collective-permute-start.6 = (bf16[128,2048]{1,0:T(8,128)(2,1)S(1)}, bf16[128,2048]{1,0:T(8,128)(2,1)S(1)}, u32[]{:S(2)}, u32[]{:S(2)}) collective-permute-start(bf16[128,2048]{1,0:T(8,128)(2,1)S(1)} %collective-permute-done.2.x1), channel_id=1, source_target_pairs={{0,1},{1,0},{2,3},{3,2},{4,5},{5,4},{6,7},{7,6},{8,9},{9,8},{10,11... | collective-permute-start | bytes 1572872 | tf_op jit(solution)/shard_map/ppermute | solution.py:121
  20.8 26.6 %collective-permute-start = (bf16[128,2048]{1,0:T(8,128)(2,1)}, bf16[128,2048]{1,0:T(8,128)(2,1)S(1)}, u32[]{:S(2)}, u32[]{:S(2)}) collective-permute-start(bf16[128,2048]{1,0:T(8,128)(2,1)} %x0.1), channel_id=1, source_target_pairs={{0,8},{1,9},{2,10},{3,11},{4,12},{5,13},{6,14},{7,15},{8,0},{9,1},... | collective-permute-start | bytes 1572872 | tf_op jit(solution)/shard_map/ppermute | solution.py:121
  21.7 25.7 %collective-permute-start.4 = (bf16[128,2048]{1,0:T(8,128)(2,1)S(1)}, bf16[128,2048]{1,0:T(8,128)(2,1)S(1)}, u32[]{:S(2)}, u32[]{:S(2)}) collective-permute-start(bf16[128,2048]{1,0:T(8,128)(2,1)S(1)} %collective-permute-done.1.x0), channel_id=1, source_target_pairs={{0,2},{1,3},{2,0},{3,1},{4,6},{5,7},{6,4},{7,5},{8,10},{9,11},{10,... | collective-permute-start | bytes 1572872 | tf_op jit(solution)/shard_map/ppermute | solution.py:121
  23.3 24.1 %collective-permute-start.5 = (bf16[128,2048]{1,0:T(8,128)(2,1)S(1)}, bf16[128,2048]{1,0:T(8,128)(2,1)S(1)}, u32[]{:S(2)}, u32[]{:S(2)}) collective-permute-start(bf16[128,2048]{1,0:T(8,128)(2,1)S(1)} %collective-permute-done.1.x0), channel_id=1, source_target_pairs={{0,1},{1,0},{2,3},{3,2},{4,5},{5,4},{6,7},{7,6},{8,9},{9,8},{10,11... | collective-permute-start | bytes 1572872 | tf_op jit(solution)/shard_map/ppermute | solution.py:121
  23.3 0.8 copy-start.28
  24.2 1.9 %copy-start.2 = (bf16[1,2048,768]{2,1,0:T(8,128)(2,1)S(1)}, bf16[1,2048,768]{2,1,0:T(8,128)(2,1)}, u32[]{:S(2)}) copy-start(bf16[1,2048,768]{2,1,0:T(8,128)(2,1)} %param.9) | copy-start | bytes 9437188
  26.0 1.9 %copy-start.6 = (bf16[1,2048,768]{2,1,0:T(8,128)(2,1)S(1)}, bf16[1,2048,768]{2,1,0:T(8,128)(2,1)}, u32[]{:S(2)}) copy-start(bf16[1,2048,768]{2,1,0:T(8,128)(2,1)} %param.10) | copy-start | bytes 9437188
  27.9 1.9 %copy-start.10 = (bf16[1,768,2048]{2,1,0:T(8,128)(2,1)S(1)}, bf16[1,768,2048]{2,1,0:T(8,128)(2,1)}, u32[]{:S(2)}) copy-start(bf16[1,768,2048]{2,1,0:T(8,128)(2,1)} %param.11) | copy-start | bytes 9437188
  29.8 1.0 copy-start.15
  30.9 1.0 copy-start.25
  31.9 1.0 copy-start.27
  32.9 1.0 copy-start.29
  40.3 1.0 copy-start.14
  41.3 7.8 %copy-start.34 = (bf16[320,768]{1,0:T(8,128)(2,1)}, bf16[320,768]{1,0:T(8,128)(2,1)S(1)}, u32[]{:S(2)}) copy-start(bf16[320,768]{1,0:T(8,128)(2,1)S(1)} %get-tuple-element.55) | copy-start | bytes 1474564
  47.4 20.6 %copy-start.16 = (bf16[128,2048]{1,0:T(8,128)(2,1)}, bf16[128,2048]{1,0:T(8,128)(2,1)S(1)}, u32[]{:S(2)}) copy-start(bf16[128,2048]{1,0:T(8,128)(2,1)S(1)} %collective-permute-done.x0) | copy-start | bytes 1572868
  47.4 0.8 copy-start.22
  48.2 1.9 %collective-permute-start.10 = (bf16[128,2048]{1,0:T(8,128)(2,1)S(1)}, bf16[128,2048]{1,0:T(8,128)(2,1)S(1)}, u32[]{:S(2)}, u32[]{:S(2)}) collective-permute-start(bf16[128,2048]{1,0:T(8,128)(2,1)S(1)} %collective-permute-done.4.x1), channel_id=1, source_target_pairs={{0,1},{1,0},{2,3},{3,2},{4,5},{5,4},{6,7},{7,6},{8,9},{9,8},{10,11... | collective-permute-start | bytes 1572872 | tf_op jit(solution)/shard_map/ppermute | solution.py:121
  49.1 18.9 %collective-permute-start.7 = (bf16[128,2048]{1,0:T(8,128)(2,1)S(1)}, bf16[128,2048]{1,0:T(8,128)(2,1)}, u32[]{:S(2)}, u32[]{:S(2)}) collective-permute-start(bf16[128,2048]{1,0:T(8,128)(2,1)S(1)} %collective-permute-done.x0), channel_id=1, source_target_pairs={{0,4},{1,5},{2,6},{3,7},{4,0},{5,1},{6,2},{7,3},{8,12},{9,13},{10,... | collective-permute-start | bytes 1572872 | tf_op jit(solution)/shard_map/ppermute | solution.py:121
  49.1 18.9 %collective-permute-start.8 = (bf16[128,2048]{1,0:T(8,128)(2,1)S(1)}, bf16[128,2048]{1,0:T(8,128)(2,1)S(1)}, u32[]{:S(2)}, u32[]{:S(2)}) collective-permute-start(bf16[128,2048]{1,0:T(8,128)(2,1)S(1)} %collective-permute-done.x0), channel_id=1, source_target_pairs={{0,2},{1,3},{2,0},{3,1},{4,6},{5,7},{6,4},{7,5},{8,10},{9,11},{10,... | collective-permute-start | bytes 1572872 | tf_op jit(solution)/shard_map/ppermute | solution.py:121
  49.6 18.5 %collective-permute-start.9 = (bf16[128,2048]{1,0:T(8,128)(2,1)S(1)}, bf16[128,2048]{1,0:T(8,128)(2,1)}, u32[]{:S(2)}, u32[]{:S(2)}) collective-permute-start(bf16[128,2048]{1,0:T(8,128)(2,1)S(1)} %collective-permute-done.x0), channel_id=1, source_target_pairs={{0,1},{1,0},{2,3},{3,2},{4,5},{5,4},{6,7},{7,6},{8,9},{9,8},{10,11... | collective-permute-start | bytes 1572872 | tf_op jit(solution)/shard_map/ppermute | solution.py:121
  50.2 0.8 copy-start.32
  51.0 1.9 %copy-start.3 = (bf16[1,2048,768]{2,1,0:T(8,128)(2,1)S(1)}, bf16[1,2048,768]{2,1,0:T(8,128)(2,1)}, u32[]{:S(2)}) copy-start(bf16[1,2048,768]{2,1,0:T(8,128)(2,1)} %param.9) | copy-start | bytes 9437188
  52.9 1.9 %copy-start.7 = (bf16[1,2048,768]{2,1,0:T(8,128)(2,1)S(1)}, bf16[1,2048,768]{2,1,0:T(8,128)(2,1)}, u32[]{:S(2)}) copy-start(bf16[1,2048,768]{2,1,0:T(8,128)(2,1)} %param.10) | copy-start | bytes 9437188
  54.7 1.9 %copy-start.11 = (bf16[1,768,2048]{2,1,0:T(8,128)(2,1)S(1)}, bf16[1,768,2048]{2,1,0:T(8,128)(2,1)}, u32[]{:S(2)}) copy-start(bf16[1,768,2048]{2,1,0:T(8,128)(2,1)} %param.11) | copy-start | bytes 9437188
  56.6 1.0 copy-start.19
  57.7 1.0 copy-start.21
  58.7 1.0 copy-start.23
  59.8 1.0 copy-start.33
  68.0 6.0 %copy-start = (bf16[128,2048]{1,0:T(8,128)(2,1)}, bf16[128,2048]{1,0:T(8,128)(2,1)S(1)}, u32[]{:S(2)}) copy-start(bf16[128,2048]{1,0:T(8,128)(2,1)S(1)} %collective-permute-done.8.x1) | copy-start | bytes 1572868
  68.8 23.6 %collective-permute-start.14 = (bf16[256,2048]{1,0:T(8,128)(2,1)}, bf16[256,2048]{1,0:T(8,128)(2,1)}, u32[]{:S(2)}, u32[]{:S(2)}) collective-permute-start(bf16[256,2048]{1,0:T(8,128)(2,1)} %get-tuple-element.65), channel_id=1, source_target_pairs={{0,1},{1,0},{2,3},{3,2},{4,5},{5,4},{6,7},{7,6},{8,9},{9,8},{10,11... | collective-permute-start | bytes 3145736 | tf_op jit(solution)/shard_map/ppermute | solution.py:121
  68.9 5.1 %collective-permute-start.15 = (bf16[128,2048]{1,0:T(8,128)(2,1)S(1)}, bf16[128,2048]{1,0:T(8,128)(2,1)S(1)}, u32[]{:S(2)}, u32[]{:S(2)}) collective-permute-start(bf16[128,2048]{1,0:T(8,128)(2,1)S(1)} %collective-permute-done.8.x1), channel_id=1, source_target_pairs={{0,1},{1,0},{2,3},{3,2},{4,5},{5,4},{6,7},{7,6},{8,9},{9,8},{10,11... | collective-permute-start | bytes 1572872 | tf_op jit(solution)/shard_map/ppermute | solution.py:121
  69.3 23.1 %collective-permute-start.13 = (bf16[128,2048]{1,0:T(8,128)(2,1)}, bf16[128,2048]{1,0:T(8,128)(2,1)}, u32[]{:S(2)}, u32[]{:S(2)}) collective-permute-start(bf16[128,2048]{1,0:T(8,128)(2,1)} %collective-permute-done.7.x0), channel_id=1, source_target_pairs={{0,1},{1,0},{2,3},{3,2},{4,5},{5,4},{6,7},{7,6},{8,9},{9,8},{10,11... | collective-permute-start | bytes 1572872 | tf_op jit(solution)/shard_map/ppermute | solution.py:121
  70.5 21.8 %collective-permute-start.11 = (bf16[64,2048]{1,0:T(8,128)(2,1)S(1)}, bf16[64,2048]{1,0:T(8,128)(2,1)S(1)}, u32[]{:S(2)}, u32[]{:S(2)}) collective-permute-start(bf16[64,2048]{1,0:T(8,128)(2,1)S(1)} %slice.72), channel_id=1, source_target_pairs={{0,4},{1,5},{2,6},{3,7},{4,0},{5,1},{6,2},{7,3},{8,12},{9,13},{10,... | collective-permute-start | bytes 786440 | tf_op jit(solution)/shard_map/ppermute | solution.py:121
  72.5 19.8 %collective-permute-start.12 = (bf16[64,2048]{1,0:T(8,128)(2,1)S(1)}, bf16[64,2048]{1,0:T(8,128)(2,1)S(1)}, u32[]{:S(2)}, u32[]{:S(2)}) collective-permute-start(bf16[64,2048]{1,0:T(8,128)(2,1)S(1)} %slice.73), channel_id=1, source_target_pairs={{0,2},{1,3},{2,0},{3,1},{4,6},{5,7},{6,4},{7,5},{8,10},{9,11},{10,... | collective-permute-start | bytes 786440 | tf_op jit(solution)/shard_map/ppermute | solution.py:121
  74.1 0.8 copy-start.30
  74.9 1.0 copy-start.1
  75.9 1.9 %copy-start.4 = (bf16[1,2048,768]{2,1,0:T(8,128)(2,1)S(1)}, bf16[1,2048,768]{2,1,0:T(8,128)(2,1)}, u32[]{:S(2)}) copy-start(bf16[1,2048,768]{2,1,0:T(8,128)(2,1)} %param.9) | copy-start | bytes 9437188
  77.8 1.9 %copy-start.8 = (bf16[1,2048,768]{2,1,0:T(8,128)(2,1)S(1)}, bf16[1,2048,768]{2,1,0:T(8,128)(2,1)}, u32[]{:S(2)}) copy-start(bf16[1,2048,768]{2,1,0:T(8,128)(2,1)} %param.10) | copy-start | bytes 9437188
  79.7 1.9 %copy-start.12 = (bf16[1,768,2048]{2,1,0:T(8,128)(2,1)S(1)}, bf16[1,768,2048]{2,1,0:T(8,128)(2,1)}, u32[]{:S(2)}) copy-start(bf16[1,768,2048]{2,1,0:T(8,128)(2,1)} %param.11) | copy-start | bytes 9437188
  81.6 1.0 copy-start.17
  82.6 1.0 copy-start.31
  93.1 17.4 %collective-permute-start.17 = (bf16[256,2048]{1,0:T(8,128)(2,1)}, bf16[256,2048]{1,0:T(8,128)(2,1)}, u32[]{:S(2)}, u32[]{:S(2)}) collective-permute-start(bf16[256,2048]{1,0:T(8,128)(2,1)} %get-tuple-element.77), channel_id=1, source_target_pairs={{0,1},{1,0},{2,3},{3,2},{4,5},{5,4},{6,7},{7,6},{8,9},{9,8},{10,11... | collective-permute-start | bytes 3145736 | tf_op jit(solution)/shard_map/ppermute | solution.py:121
  93.8 3.1 %collective-permute-start.16 = (bf16[128,2048]{1,0:T(8,128)(2,1)}, bf16[128,2048]{1,0:T(8,128)(2,1)}, u32[]{:S(2)}, u32[]{:S(2)}) collective-permute-start(bf16[128,2048]{1,0:T(8,128)(2,1)} %constant_dynamic-update-slice_fusion.x1), channel_id=1, source_target_pairs={{0,1},{1,0},{2,3},{3,2},{4,5},{5,4},{6,7},{7,6},{8,9},{9,8},{10,11... | collective-permute-start | bytes 1572872 | tf_op jit(solution)/shard_map/ppermute | solution.py:121
  96.4 14.1 %collective-permute-start.18 = (bf16[128,2048]{1,0:T(8,128)(2,1)}, bf16[128,2048]{1,0:T(8,128)(2,1)}, u32[]{:S(2)}, u32[]{:S(2)}) collective-permute-start(bf16[128,2048]{1,0:T(8,128)(2,1)} %add_convert_fusion.4), channel_id=1, source_target_pairs={{0,2},{1,3},{2,0},{3,1},{4,6},{5,7},{6,4},{7,5},{8,10},{9,11},{10,... | collective-permute-start | bytes 1572872 | tf_op jit(solution)/shard_map/ppermute | solution.py:121
  96.9 13.6 %collective-permute-start.20 = (bf16[256,2048]{1,0:T(8,128)(2,1)}, bf16[256,2048]{1,0:T(8,128)(2,1)S(1)}, u32[]{:S(2)}, u32[]{:S(2)}) collective-permute-start(bf16[256,2048]{1,0:T(8,128)(2,1)} %copy-done.14), channel_id=1, source_target_pairs={{0,1},{1,0},{2,3},{3,2},{4,5},{5,4},{6,7},{7,6},{8,9},{9,8},{10,11... | collective-permute-start | bytes 3145736 | tf_op jit(solution)/shard_map/ppermute | solution.py:121
  96.9 1.9 %copy-start.5 = (bf16[1,2048,768]{2,1,0:T(8,128)(2,1)S(1)}, bf16[1,2048,768]{2,1,0:T(8,128)(2,1)}, u32[]{:S(2)}) copy-start(bf16[1,2048,768]{2,1,0:T(8,128)(2,1)} %param.9) | copy-start | bytes 9437188
  98.8 1.9 %copy-start.9 = (bf16[1,2048,768]{2,1,0:T(8,128)(2,1)S(1)}, bf16[1,2048,768]{2,1,0:T(8,128)(2,1)}, u32[]{:S(2)}) copy-start(bf16[1,2048,768]{2,1,0:T(8,128)(2,1)} %param.10) | copy-start | bytes 9437188
  100.7 1.9 %copy-start.13 = (bf16[1,768,2048]{2,1,0:T(8,128)(2,1)S(1)}, bf16[1,768,2048]{2,1,0:T(8,128)(2,1)}, u32[]{:S(2)}) copy-start(bf16[1,768,2048]{2,1,0:T(8,128)(2,1)} %param.11) | copy-start | bytes 9437188
  109.8 15.3 %copy-start.37 = (bf16[320,768]{1,0:T(8,128)(2,1)}, bf16[320,768]{1,0:T(8,128)(2,1)S(1)}, u32[]{:S(2)}) copy-start(bf16[320,768]{1,0:T(8,128)(2,1)S(1)} %get-tuple-element.80) | copy-start | bytes 1474564
  110.5 2.7 %collective-permute-start.19 = (bf16[256,2048]{1,0:T(8,128)(2,1)S(1)}, bf16[256,2048]{1,0:T(8,128)(2,1)S(1)}, u32[]{:S(2)}, u32[]{:S(2)}) collective-permute-start(bf16[256,2048]{1,0:T(8,128)(2,1)S(1)} %get-tuple-element.82), channel_id=1, source_target_pairs={{0,1},{1,0},{2,3},{3,2},{4,5},{5,4},{6,7},{7,6},{8,9},{9,8},{10,11... | collective-permute-start | bytes 3145736 | tf_op jit(solution)/shard_map/ppermute | solution.py:121
  110.5 19.0 %copy-start.38 = (bf16[256,2048]{1,0:T(8,128)(2,1)}, bf16[256,2048]{1,0:T(8,128)(2,1)S(1)}, u32[]{:S(2)}) copy-start(bf16[256,2048]{1,0:T(8,128)(2,1)S(1)} %collective-permute-done.20) | copy-start | bytes 3145732
  113.4 8.4 %collective-permute-start.23 = (bf16[64,2048]{1,0:T(8,128)(2,1)S(1)}, bf16[64,2048]{1,0:T(8,128)(2,1)S(1)}, u32[]{:S(2)}, u32[]{:S(2)}) collective-permute-start(bf16[64,2048]{1,0:T(8,128)(2,1)S(1)} %get-tuple-element.98), channel_id=1, source_target_pairs={{0,4},{1,5},{2,6},{3,7},{4,0},{5,1},{6,2},{7,3},{8,12},{9,13},{10,... | collective-permute-start | bytes 786440 | tf_op jit(solution)/shard_map/ppermute | solution.py:121
  114.6 8.3 %collective-permute-start.24 = (bf16[64,2048]{1,0:T(8,128)(2,1)S(1)}, bf16[64,2048]{1,0:T(8,128)(2,1)S(1)}, u32[]{:S(2)}, u32[]{:S(2)}) collective-permute-start(bf16[64,2048]{1,0:T(8,128)(2,1)S(1)} %get-tuple-element.97), channel_id=1, source_target_pairs={{0,2},{1,3},{2,0},{3,1},{4,6},{5,7},{6,4},{7,5},{8,10},{9,11},{10,... | collective-permute-start | bytes 786440 | tf_op jit(solution)/shard_map/ppermute | solution.py:121
  124.1 14.9 %collective-permute-start.26 = (bf16[128,2048]{1,0:T(8,128)(2,1)S(1)}, bf16[128,2048]{1,0:T(8,128)(2,1)S(1)}, u32[]{:S(2)}, u32[]{:S(2)}) collective-permute-start(bf16[128,2048]{1,0:T(8,128)(2,1)S(1)} %pad_maximum_fusion.1), channel_id=1, source_target_pairs={{0,2},{1,3},{2,0},{3,1},{4,6},{5,7},{6,4},{7,5},{8,10},{9,11},{10,... | collective-permute-start | bytes 1572872 | tf_op jit(solution)/shard_map/ppermute | solution.py:121
  125.2 14.9 %collective-permute-start.25 = (bf16[128,2048]{1,0:T(8,128)(2,1)S(1)}, bf16[128,2048]{1,0:T(8,128)(2,1)S(1)}, u32[]{:S(2)}, u32[]{:S(2)}) collective-permute-start(bf16[128,2048]{1,0:T(8,128)(2,1)S(1)} %pad_maximum_fusion), channel_id=1, source_target_pairs={{0,4},{1,5},{2,6},{3,7},{4,0},{5,1},{6,2},{7,3},{8,12},{9,13},{10,... | collective-permute-start | bytes 1572872 | tf_op jit(solution)/shard_map/ppermute | solution.py:121
  128.7 30.0 %collective-permute-start.22 = (bf16[128,2048]{1,0:T(8,128)(2,1)}, bf16[128,2048]{1,0:T(8,128)(2,1)}, u32[]{:S(2)}, u32[]{:S(2)}) collective-permute-start(bf16[128,2048]{1,0:T(8,128)(2,1)} %add_convert_fusion.2), channel_id=1, source_target_pairs={{0,4},{1,5},{2,6},{3,7},{4,0},{5,1},{6,2},{7,3},{8,12},{9,13},{10,... | collective-permute-start | bytes 1572872 | tf_op jit(solution)/shard_map/ppermute | solution.py:121
  129.7 29.0 %collective-permute-start.21 = (bf16[128,2048]{1,0:T(8,128)(2,1)S(1)}, bf16[128,2048]{1,0:T(8,128)(2,1)}, u32[]{:S(2)}, u32[]{:S(2)}) collective-permute-start(bf16[128,2048]{1,0:T(8,128)(2,1)S(1)} %add_convert_fusion.3), channel_id=1, source_target_pairs={{0,2},{1,3},{2,0},{3,1},{4,6},{5,7},{6,4},{7,5},{8,10},{9,11},{10,... | collective-permute-start | bytes 1572872 | tf_op jit(solution)/shard_map/ppermute | solution.py:121
  141.5 21.6 %collective-permute-start.27 = (bf16[128,2048]{1,0:T(8,128)(2,1)S(1)}, bf16[128,2048]{1,0:T(8,128)(2,1)S(1)}, u32[]{:S(2)}, u32[]{:S(2)}) collective-permute-start(bf16[128,2048]{1,0:T(8,128)(2,1)S(1)} %add_convert_fusion.1), channel_id=1, source_target_pairs={{0,8},{1,9},{2,10},{3,11},{4,12},{5,13},{6,14},{7,15},{8,0},{9,1},... | collective-permute-start | bytes 1572872 | tf_op jit(solution)/shard_map/ppermute | solution.py:121
  144.1 19.0 %copy-start.39 = (bf16[256,2048]{1,0:T(8,128)(2,1)S(1)}, bf16[256,2048]{1,0:T(8,128)(2,1)}, u32[]{:S(2)}) copy-start(bf16[256,2048]{1,0:T(8,128)(2,1)} %copy-done.38) | copy-start | bytes 3145732
  (4 other events, 3.1 us)

commit v6 on v5

--- a/solution.py
+++ b/solution.py
@@ -36,12 +36,37 @@
 
 
 def plane_kernel(
-    capacity, order, weight, x0, x1, x2, x3, w_gate, w_up, w_down, keep, give, act, rows, ranks
+    capacity, order, weight, x0, x1, x2, x3, w_gate, w_up, w_down, keep, give, act,
+    x, rows, ranks, gates, ups, downs, x_sem, gate_sem, up_sem, down_sem,
 ):
     blocks, tok = weight.shape
-    features = x0.shape[1]
     slots, hidden = act.shape
-    wide = 256
+    tiles, features, wide = gates.shape
+    cuts, _, cut = downs.shape
+    x_copies = [
+        pltpu.make_async_copy(block, x.at[pl.ds(i * tok, tok), :], x_sem.at[i])
+        for i, block in enumerate((x0, x1, x2, x3))
+    ]
+    gate_copies = [
+        pltpu.make_async_copy(w_gate.at[:, pl.ds(i * wide, wide)], gates.at[i], gate_sem.at[i])
+        for i in range(tiles)
+    ]
+    up_copies = [
+        pltpu.make_async_copy(w_up.at[:, pl.ds(i * wide, wide)], ups.at[i], up_sem.at[i])
+        for i in range(tiles)
+    ]
+    down_copies = [
+        pltpu.make_async_copy(w_down.at[:, pl.ds(i * cut, cut)], downs.at[i], down_sem.at[i])
+        for i in range(cuts)
+    ]
+    for copy in x_copies:
+        copy.start()
+    for gate_copy, up_copy in zip(gate_copies, up_copies):
+        gate_copy.start()
+        up_copy.start()
+    for copy in down_copies:
+        copy.start()
+
     named = (weight[...] >= 0.0).astype(jnp.float32)
     lane = lax.broadcasted_iota(jnp.int32, (tok, tok), 0)
     below = (lane < lax.broadcasted_iota(jnp.int32, (tok, tok), 1)).astype(jnp.float32)
@@ -65,19 +90,24 @@
     hits = slot == place
     scale = jnp.sum(jnp.where(hits, share, 0.0), axis=1, keepdims=True)
     select = hits.astype(jnp.float32).astype(jnp.bfloat16)
-    for i in range(features // 512):
-        span = pl.ds(i * 512, 512)
-        x = jnp.concatenate([x0[:, span], x1[:, span], x2[:, span], x3[:, span]], axis=0)
-        rows[:, span] = jnp.dot(select, x, preferred_element_type=jnp.float32).astype(jnp.bfloat16)
-    for i in range(hidden // wide):
-        span = pl.ds(i * wide, wide)
-        gate = jnp.dot(rows[...], w_gate[:, span], preferred_element_type=jnp.float32)
-        up = jnp.dot(rows[...], w_up[:, span], preferred_element_type=jnp.float32)
-        act[:, span] = (gate / (1.0 + jnp.exp(-gate)) * up).astype(jnp.bfloat16)
+    for copy in x_copies:
+        copy.wait()
+    for i in range(cuts):
+        span = pl.ds(i * cut, cut)
+        rows[:, span] = jnp.dot(
+            select, x[:, span], preferred_element_type=jnp.float32
+        ).astype(jnp.bfloat16)
+    for i in range(tiles):
+        gate_copies[i].wait()
+        gate = jnp.dot(rows[...], gates[i], preferred_element_type=jnp.float32)
+        up_copies[i].wait()
+        up = jnp.dot(rows[...], ups[i], preferred_element_type=jnp.float32)
+        act[:, pl.ds(i * wide, wide)] = (gate / (1.0 + jnp.exp(-gate)) * up).astype(jnp.bfloat16)
     back = select.T
-    for i in range(features // 512):
-        span = pl.ds(i * 512, 512)
-        result = jnp.dot(act[...], w_down[:, span], preferred_element_type=jnp.float32)
+    for i in range(cuts):
+        span = pl.ds(i * cut, cut)
+        down_copies[i].wait()
+        result = jnp.dot(act[...], downs[i], preferred_element_type=jnp.float32)
         made = (result * scale).astype(jnp.bfloat16)
         spread = jnp.dot(back, made, preferred_element_type=jnp.float32).astype(jnp.bfloat16)
         keep[:, span] = spread[: 2 * tok]
@@ -89,19 +119,29 @@
     hidden = w_gate.shape[1]
     half = jax.ShapeDtypeStruct((2 * tok, features), jnp.bfloat16)
     rows = 4 * slots
+    wide, cut = 256, 512
+    tiles, cuts = hidden // wide, features // cut
     flops = 2 * rows * (3 * features * hidden + 8 * tok * features)
     moved = 2 * (3 * features * hidden + 8 * tok * features)
     return pl.pallas_call(
         functools.partial(plane_kernel, capacity),
         out_shape=(half, half, jax.ShapeDtypeStruct((rows, hidden), jnp.bfloat16)),
-        in_specs=[pl.BlockSpec(memory_space=pltpu.SMEM)]
-        + [pl.BlockSpec(memory_space=pltpu.VMEM)] * 8,
+        in_specs=[pl.BlockSpec(memory_space=pltpu.SMEM), pl.BlockSpec(memory_space=pltpu.VMEM)]
+        + [pl.BlockSpec(memory_space=pl.ANY)] * 7,
         out_specs=[pl.BlockSpec(memory_space=pltpu.VMEM)] * 3,
         scratch_shapes=[
+            pltpu.VMEM((4 * tok, features), jnp.bfloat16),
             pltpu.VMEM((rows, features), jnp.bfloat16),
             pltpu.VMEM(weight.shape, jnp.float32),
+            pltpu.VMEM((tiles, features, wide), jnp.bfloat16),
+            pltpu.VMEM((tiles, features, wide), jnp.bfloat16),
+            pltpu.VMEM((cuts, hidden, cut), jnp.bfloat16),
+            pltpu.SemaphoreType.DMA((4,)),
+            pltpu.SemaphoreType.DMA((tiles,)),
+            pltpu.SemaphoreType.DMA((tiles,)),
+            pltpu.SemaphoreType.DMA((cuts,)),
         ],
-        compiler_params=pltpu.CompilerParams(vmem_limit_bytes=32 * 1024 * 1024),
+        compiler_params=pltpu.CompilerParams(vmem_limit_bytes=58 * 1024 * 1024),
         cost_estimate=pl.CostEstimate(
             flops=flops, bytes_accessed=moved, transcendentals=rows * hidden
         ),
@@ -142,16 +182,16 @@
 
     weight = weights_for_me(routes, probs, size)
     a0 = tokens
-    a1 = pair(a0)
-    a2 = far(a0)
-    b0 = column(a0)
-    c0 = sibling(a0)
-    a1, b0, c0, weight = together(a1, b0, c0, weight)
+    a1, low, b0, c0, weight = together(
+        pair(a0), far(a0[:half]), column(a0), sibling(a0), weight
+    )
     b1 = column(a1)
+    high = far(a0[half:])
     d0 = sibling(b0)
     c1 = sibling(a1)
     keep0, give0, act0 = expert(0, a0, b0, c0, d0)
-    a2, b1, c1, keep0, give0, act0 = together(a2, b1, c1, keep0, give0, act0)
+    high, b1, c1, keep0, give0, act0 = together(high, b1, c1, keep0, give0, act0)
+    a2 = jnp.concatenate([low, high], axis=0)
     a3 = pair(a2)
     b2 = column(a2)
     d1 = sibling(b1)

time: 167 us -> 152 us (0.910)
  local copies, waits for them, and re-layouts: 44.8 us -> 5.09 us
  Pallas kernels: 28.6 us -> 51.7 us
  waiting for transfers between devices: 39.7 us -> 32.9 us
  starting transfers between devices: 20.9 us -> 24 us
  other arithmetic: 12.2 us -> 14.3 us
  blocking collectives: 12.4 us -> 14.2 us
    unnamed x81 -> x34, local copies, waits for them, and re-layouts: 43.1 us -> 3.25 us
    pallas_call x4, Pallas kernels: 28.6 us -> 51.7 us  [plane_pass(): pl.pallas_call(functools.partial(plane_kernel, capacity), out_shape=(half...]
    ppermute x28 -> x29, waiting for transfers between devices: 39.7 us -> 32.9 us  [swapped(): return lax.ppermute(array, 'expert', [(i, i ^ bit) for i in range(size)])]
    ppermute x28 -> x29, starting transfers between devices: 20.9 us -> 24 us  [swapped(): return lax.ppermute(array, 'expert', [(i, i ^ bit) for i in range(size)])]
    another operation x4, other arithmetic: 0.31 us -> 2.46 us  [expert(): jnp.stack([base + y * 2 + core, base + (1 - y) * 2 + core, base + y * 2 +...]
    all_to_all x1, blocking collectives: 12.4 us -> 14.2 us  [weights_for_me(): lax.all_to_all(mine, 'expert', split_axis=0, concat_axis=0, tiled=True)]
  transfers between devices with their start and end apart: 28 -> 29, of which waited for: 10 -> 10; matrix products, arithmetic and copies ran while one was open for 9% -> 12% of each run, Pallas kernels for 17% -> 35%
where the time goes in v6:
time: 152 us; the launch traced here: 149 us
  Pallas kernels  51.7 us (34%)
  waiting for transfers between devices  32.9 us (22%)
  starting transfers between devices  24 us (16%)
  other arithmetic  14.3 us (9%)
  blocking collectives  14.2 us (9%)
  matrix products  5.24 us (3%)
  local copies, waits for them, and re-layouts  5.09 us (3%)
  between operations  1.72 us (1%)
    pallas_call x4, Pallas kernels, plane_pass(): pl.pallas_call(functools.partial(plane_kernel, capacity), out_shape=(half...  51.7 us
    ppermute x29, waiting for transfers between devices, swapped(): return lax.ppermute(array, 'expert', [(i, i ^ bit) for i in range(size)])  32.9 us
    ppermute x29, starting transfers between devices, swapped(): return lax.ppermute(array, 'expert', [(i, i ^ bit) for i in range(size)])  24 us
    all_to_all x1, blocking collectives, weights_for_me(): lax.all_to_all(mine, 'expert', split_axis=0, concat_axis=0, tiled=True)  14.2 us
    convert_element_type x8, other arithmetic, summed(): return total.astype(jnp.bfloat16)  9.69 us
    dot_general x1, matrix products, gram_of(): lax.dot_general(rows, rows, (((0,), (0,)), ((), ())), preferred_element_t...  5.24 us
    unnamed x34, local copies, waits for them, and re-layouts  3.25 us
  transfers between devices with their start and end apart: 29, of which 10 were waited for; matrix products, arithmetic and copies ran while one was open for 12% of the time, Pallas kernels for 35%

profile of v6, /device:TPU:0, one launch (start us, length us, event | category | flops | bytes accessed | tf_op | source)
XLA Modules:
  0.0 149.2 jit_solution(3453584913295334182)
XLA Ops:
  0.6 3.1 %collective-permute-start.1 = (bf16[128,2048]{1,0:T(8,128)(2,1)}, bf16[128,2048]{1,0:T(8,128)(2,1)S(1)}, u32[]{:S(2)}, u32[]{:S(2)}) collective-permute-start(bf16[128,2048]{1,0:T(8,128)(2,1)} %x0.1), channel_id=1, source_target_pairs={{0,4},{1,5},{2,6},{3,7},{4,0},{5,1},{6,2},{7,3},{8,12},{9,13},{10,... | collective-permute-start | bytes 1572872 | tf_op jit(solution)/shard_map/ppermute | solution.py:161
  3.7 1.5 %collective-permute-start.3 = (bf16[128,2048]{1,0:T(8,128)(2,1)}, bf16[128,2048]{1,0:T(8,128)(2,1)S(1)}, u32[]{:S(2)}, u32[]{:S(2)}) collective-permute-start(bf16[128,2048]{1,0:T(8,128)(2,1)} %x0.1), channel_id=1, source_target_pairs={{0,2},{1,3},{2,0},{3,1},{4,6},{5,7},{6,4},{7,5},{8,10},{9,11},{10,... | collective-permute-start | bytes 1572872 | tf_op jit(solution)/shard_map/ppermute | solution.py:161
  5.2 1.1 fusion.12
  6.3 2.7 %collective-permute-start.2 = (bf16[64,2048]{1,0:T(8,128)(2,1)S(1)}, bf16[64,2048]{1,0:T(8,128)(2,1)S(1)}, u32[]{:S(2)}, u32[]{:S(2)}) collective-permute-start(bf16[64,2048]{1,0:T(8,128)(2,1)S(1)} %get-tuple-element.102), channel_id=1, source_target_pairs={{0,8},{1,9},{2,10},{3,11},{4,12},{5,13},{6,14},{7,15},{8,0},{9,1},... | collective-permute-start | bytes 786440 | tf_op jit(solution)/shard_map/ppermute | solution.py:161
  9.0 0.7 select_reduce_fusion
  9.7 0.7 fusion.10
  10.4 14.2 %all_to_all.9 = f32[16,1,128]{2,1,0:T(1,128)} all-to-all(f32[16,1,128]{2,1,0:T(1,128)S(1)} %bitcast.32), channel_id=1, replica_groups=mesh['parts'=2,'expert'=16] {'expert'}, dimensions={0} | all-to-all | bytes 16384 | tf_op jit(solution)/shard_map/all_to_all | solution.py:28
  24.7 0.0 copy-start.11
  24.7 0.1 collective-permute-start.7
  24.8 0.6 collective-permute-start
  25.4 0.6 collective-permute-start.5
  26.0 0.6 pad_add_fusion.order
  26.6 0.1 collective-permute-done.7.x3
  26.7 0.8 copy-done.13
  27.5 12.9 %shard_map.77 = (bf16[256,2048]{1,0:T(8,128)(2,1)}, bf16[256,2048]{1,0:T(8,128)(2,1)}, bf16[320,768]{1,0:T(8,128)(2,1)}) custom-call(s32[4]{0:T(128)} %pad_add_fusion.order, f32[16,128]{1,0:T(8,128)} %bitcast.27, bf16[128,2048]{1,0:T(8,128)(2,1)} %x0.1, bf16[128,2048]{1,0:T(8,128)(2,1)} %copy-done.11, bf16[128,2048]{1,0:T(8,128)(2,1)} %copy-done.12, ...), custom_call_target="tpu_custom_call" | custom-call | flops 4362076160 | bytes 13631488 | tf_op jit(solution)/shard_map/pallas_call | solution.py:126
  40.4 0.8 copy-done.10
  41.2 0.4 collective-permute-start.11
  41.7 0.2 collective-permute-start.10
  41.9 1.6 %collective-permute-start.8 = (bf16[128,2048]{1,0:T(8,128)(2,1)S(1)}, bf16[128,2048]{1,0:T(8,128)(2,1)S(1)}, u32[]{:S(2)}, u32[]{:S(2)}) collective-permute-start(bf16[128,2048]{1,0:T(8,128)(2,1)S(1)} %constant_dynamic-update-slice_fusion.x0), channel_id=1, source_target_pairs={{0,4},{1,5},{2,6},{3,7},{4,0},{5,1},{6,2},{7,3},{8,12},{9,13},{10,... | collective-permute-start | bytes 1572872 | tf_op jit(solution)/shard_map/ppermute | solution.py:161
  43.5 1.4 collective-permute-start.9
  44.9 0.6 pad_add_fusion.1.order
  45.5 0.8 copy-done.15
  46.3 12.9 %shard_map.78 = (bf16[256,2048]{1,0:T(8,128)(2,1)}, bf16[256,2048]{1,0:T(8,128)(2,1)}, bf16[320,768]{1,0:T(8,128)(2,1)}) custom-call(s32[4]{0:T(128)} %pad_add_fusion.1.order, f32[16,128]{1,0:T(8,128)} %bitcast.28, bf16[128,2048]{1,0:T(8,128)(2,1)} %copy-done.9, bf16[128,2048]{1,0:T(8,128)(2,1)} %collective-permute-done.5.x1, bf16[128,2048]{1,0:T(8,128)(2,1)} %copy-done.10, ...), custom_call_target="tpu_custom_call" | custom-call | flops 4362076160 | bytes 13631488 | tf_op jit(solution)/shard_map/pallas_call | solution.py:126
  59.2 0.1 collective-permute-start.15
  59.3 0.5 collective-permute-start.16
  59.8 0.1 collective-permute-start.14
  59.9 0.7 pad_add_fusion.2.order
  60.6 0.5 collective-permute-start.12
  61.1 0.8 collective-permute-start.13
  61.9 0.9 collective-permute-done.16.x3
  62.8 13.0 %shard_map.79 = (bf16[256,2048]{1,0:T(8,128)(2,1)}, bf16[256,2048]{1,0:T(8,128)(2,1)}, bf16[320,768]{1,0:T(8,128)(2,1)}) custom-call(s32[4]{0:T(128)} %pad_add_fusion.2.order, f32[16,128]{1,0:T(8,128)} %bitcast.29, bf16[128,2048]{1,0:T(8,128)(2,1)} %copy-done.7, bf16[128,2048]{1,0:T(8,128)(2,1)} %copy-done.6, bf16[128,2048]{1,0:T(8,128)(2,1)} %copy-done.14, ...), custom_call_target="tpu_custom_call" | custom-call | flops 4362076160 | bytes 13631488 | tf_op jit(solution)/shard_map/pallas_call | solution.py:126
  75.9 0.8 constant_dynamic-update-slice_fusion.3
  76.7 0.1 collective-permute-start.18
  76.8 0.7 constant_dynamic-update-slice_fusion.2.x1
  77.6 0.4 collective-permute-start.17
  77.9 1.0 add_convert_fusion.4
  78.9 0.7 collective-permute-start.19
  79.6 0.6 pad_add_fusion.3.order
  80.2 0.3 collective-permute-done.17.x3
  80.5 13.0 %shard_map.80 = (bf16[256,2048]{1,0:T(8,128)(2,1)}, bf16[256,2048]{1,0:T(8,128)(2,1)}, bf16[320,768]{1,0:T(8,128)(2,1)}) custom-call(s32[4]{0:T(128)} %pad_add_fusion.3.order, f32[16,128]{1,0:T(8,128)} %bitcast.30, bf16[128,2048]{1,0:T(8,128)(2,1)} %copy-done.5, bf16[128,2048]{1,0:T(8,128)(2,1)} %constant_dynamic-update-slice_fusion.2.x1, ...), custom_call_target="tpu_custom_call" | custom-call | flops 4362076160 | bytes 13631488 | tf_op jit(solution)/shard_map/pallas_call | solution.py:126
  93.5 0.2 collective-permute-start.20
  93.7 2.7 %collective-permute-done.20 = bf16[256,2048]{1,0:T(8,128)(2,1)S(1)} collective-permute-done((bf16[256,2048]{1,0:T(8,128)(2,1)}, bf16[256,2048]{1,0:T(8,128)(2,1)S(1)}, u32[]{:S(2)}, u32[]{:S(2)}) %collective-permute-start.20) | collective-permute-done | bytes 1048608 | tf_op jit(solution)/shard_map/ppermute | solution.py:161
  96.4 1.4 add_convert_fusion.10
  97.8 1.1 collective-permute-start.24
  98.9 0.9 collective-permute-start.25
  99.8 6.4 %collective-permute-done.24 = bf16[64,2048]{1,0:T(8,128)(2,1)S(1)} collective-permute-done((bf16[64,2048]{1,0:T(8,128)(2,1)S(1)}, bf16[64,2048]{1,0:T(8,128)(2,1)S(1)}, u32[]{:S(2)}, u32[]{:S(2)}) %collective-permute-start.24) | collective-permute-done | bytes 262176 | tf_op jit(solution)/shard_map/ppermute | solution.py:161
  106.2 1.0 collective-permute-done.25
  107.2 0.2 add_convert_fusion.6
  107.4 0.7 collective-permute-start.27
  108.1 1.0 add_convert_fusion.7
  109.2 1.5 %collective-permute-start.26 = (bf16[128,2048]{1,0:T(8,128)(2,1)S(1)}, bf16[128,2048]{1,0:T(8,128)(2,1)S(1)}, u32[]{:S(2)}, u32[]{:S(2)}) collective-permute-start(bf16[128,2048]{1,0:T(8,128)(2,1)S(1)} %pad_maximum_fusion), channel_id=1, source_target_pairs={{0,4},{1,5},{2,6},{3,7},{4,0},{5,1},{6,2},{7,3},{8,12},{9,13},{10,... | collective-permute-start | bytes 1572872 | tf_op jit(solution)/shard_map/ppermute | solution.py:161
  110.8 2.1 %add_convert_fusion.2 = bf16[128,2048]{1,0:T(8,128)(2,1)} fusion(bf16[128,2048]{1,0:T(8,128)(2,1)} %collective-permute-done.19, bf16[256,2048]{1,0:T(8,128)(2,1)S(1)} %copy-done.4, bf16[256,2048]{1,0:T(8,128)(2,1)S(1)} %copy-done.2), kind=kLoop, calls=%fused_computation.11 | loop fusion | flops 1572864 | bytes 2097152 | tf_op jit(solution)/shard_map/convert_element_type | solution.py:35
  112.9 0.5 collective-permute-start.23
  113.4 1.2 add_convert_fusion.3
  114.6 1.4 collective-permute-start.22
  116.0 6.3 %collective-permute-done.27 = bf16[128,2048]{1,0:T(8,128)(2,1)S(1)} collective-permute-done((bf16[128,2048]{1,0:T(8,128)(2,1)S(1)}, bf16[128,2048]{1,0:T(8,128)(2,1)S(1)}, u32[]{:S(2)}, u32[]{:S(2)}) %collective-permute-start.27) | collective-permute-done | bytes 524320 | tf_op jit(solution)/shard_map/ppermute | solution.py:161
  122.3 1.8 %collective-permute-done.26 = bf16[128,2048]{1,0:T(8,128)(2,1)S(1)} collective-permute-done((bf16[128,2048]{1,0:T(8,128)(2,1)S(1)}, bf16[128,2048]{1,0:T(8,128)(2,1)S(1)}, u32[]{:S(2)}, u32[]{:S(2)}) %collective-permute-start.26) | collective-permute-done | bytes 524320 | tf_op jit(solution)/shard_map/ppermute | solution.py:161
  124.2 0.3 add_convert_fusion.1
  124.5 2.3 %collective-permute-start.28 = (bf16[128,2048]{1,0:T(8,128)(2,1)S(1)}, bf16[128,2048]{1,0:T(8,128)(2,1)S(1)}, u32[]{:S(2)}, u32[]{:S(2)}) collective-permute-start(bf16[128,2048]{1,0:T(8,128)(2,1)S(1)} %add_convert_fusion.1), channel_id=1, source_target_pairs={{0,8},{1,9},{2,10},{3,11},{4,12},{5,13},{6,14},{7,15},{8,0},{9,1},... | collective-permute-start | bytes 1572872 | tf_op jit(solution)/shard_map/ppermute | solution.py:161
  126.8 0.6 convert_reduce_fusion
  128.1 5.2 %multiply_bitcast_fusion = f32[1,768,768]{2,1,0:T(8,128)} fusion(f32[]{:T(128)S(6)} %div.24, bf16[320,768]{1,0:T(8,128)(2,1)} %get-tuple-element.82, bf16[320,768]{1,0:T(8,128)(2,1)} %get-tuple-element.72, bf16[320,768]{1,0:T(8,128)(2,1)} %get-tuple-element.64, bf16[320,768]{1,0:T(8,128)(2,1)} %get-tuple-element.56), kind=kOutput, calls=%fused_computation | convolution fusion | flops 1518403584 | bytes 4325380 | tf_op jit(solution)/shard_map/dot_general | solution.py:12
  133.4 11.1 %collective-permute-done.23 = bf16[128,2048]{1,0:T(8,128)(2,1)} collective-permute-done((bf16[128,2048]{1,0:T(8,128)(2,1)}, bf16[128,2048]{1,0:T(8,128)(2,1)}, u32[]{:S(2)}, u32[]{:S(2)}) %collective-permute-start.23) | collective-permute-done | bytes 524320 | tf_op jit(solution)/shard_map/ppermute | solution.py:161
  144.4 2.2 %collective-permute-done.28 = bf16[128,2048]{1,0:T(8,128)(2,1)S(1)} collective-permute-done((bf16[128,2048]{1,0:T(8,128)(2,1)S(1)}, bf16[128,2048]{1,0:T(8,128)(2,1)S(1)}, u32[]{:S(2)}, u32[]{:S(2)}) %collective-permute-start.28) | collective-permute-done | bytes 524320 | tf_op jit(solution)/shard_map/ppermute | solution.py:161
  146.6 2.6 %add_convert_fusion = bf16[128,2048]{1,0:T(8,128)(2,1)} fusion(bf16[128,2048]{1,0:T(8,128)(2,1)S(1)} %collective-permute-done.28, bf16[128,2048]{1,0:T(8,128)(2,1)} %collective-permute-done.23, bf16[128,2048]{1,0:T(8,128)(2,1)} %collective-permute-done.22, bf16[256,2048]{1,0:T(8,128)(2,1)} %collective-permute-done.21, bf16[256,2048]{1,0:T(8,128)(2,1)S(1)} %copy-done.1), kind=kLoop, calls=%fused_computation.9 | loop fusion | flops 2621440 | bytes 3145728 | tf_op jit(solution)/shard_map/convert_element_type | solution.py:35
  (57 shorter events, 0.3 us)
Async XLA Ops:
  0.6 24.0 %collective-permute-start.1 = (bf16[128,2048]{1,0:T(8,128)(2,1)}, bf16[128,2048]{1,0:T(8,128)(2,1)S(1)}, u32[]{:S(2)}, u32[]{:S(2)}) collective-permute-start(bf16[128,2048]{1,0:T(8,128)(2,1)} %x0.1), channel_id=1, source_target_pairs={{0,4},{1,5},{2,6},{3,7},{4,0},{5,1},{6,2},{7,3},{8,12},{9,13},{10,... | collective-permute-start | bytes 1572872 | tf_op jit(solution)/shard_map/ppermute | solution.py:161
  3.7 21.0 %collective-permute-start.3 = (bf16[128,2048]{1,0:T(8,128)(2,1)}, bf16[128,2048]{1,0:T(8,128)(2,1)S(1)}, u32[]{:S(2)}, u32[]{:S(2)}) collective-permute-start(bf16[128,2048]{1,0:T(8,128)(2,1)} %x0.1), channel_id=1, source_target_pairs={{0,2},{1,3},{2,0},{3,1},{4,6},{5,7},{6,4},{7,5},{8,10},{9,11},{10,... | collective-permute-start | bytes 1572872 | tf_op jit(solution)/shard_map/ppermute | solution.py:161
  5.2 19.5 %collective-permute-start.4 = (bf16[128,2048]{1,0:T(8,128)(2,1)}, bf16[128,2048]{1,0:T(8,128)(2,1)S(1)}, u32[]{:S(2)}, u32[]{:S(2)}) collective-permute-start(bf16[128,2048]{1,0:T(8,128)(2,1)} %x0.1), channel_id=1, source_target_pairs={{0,1},{1,0},{2,3},{3,2},{4,5},{5,4},{6,7},{7,6},{8,9},{9,8},{10,11... | collective-permute-start | bytes 1572872 | tf_op jit(solution)/shard_map/ppermute | solution.py:161
  6.3 18.4 %collective-permute-start.2 = (bf16[64,2048]{1,0:T(8,128)(2,1)S(1)}, bf16[64,2048]{1,0:T(8,128)(2,1)S(1)}, u32[]{:S(2)}, u32[]{:S(2)}) collective-permute-start(bf16[64,2048]{1,0:T(8,128)(2,1)S(1)} %get-tuple-element.102), channel_id=1, source_target_pairs={{0,8},{1,9},{2,10},{3,11},{4,12},{5,13},{6,14},{7,15},{8,0},{9,1},... | collective-permute-start | bytes 786440 | tf_op jit(solution)/shard_map/ppermute | solution.py:161
  24.7 15.7 %copy-start.9 = (bf16[128,2048]{1,0:T(8,128)(2,1)}, bf16[128,2048]{1,0:T(8,128)(2,1)S(1)}, u32[]{:S(2)}) copy-start(bf16[128,2048]{1,0:T(8,128)(2,1)S(1)} %collective-permute-done.1.x0) | copy-start | bytes 1572868
  24.7 2.0 %copy-start.11 = (bf16[128,2048]{1,0:T(8,128)(2,1)}, bf16[128,2048]{1,0:T(8,128)(2,1)S(1)}, u32[]{:S(2)}) copy-start(bf16[128,2048]{1,0:T(8,128)(2,1)S(1)} %collective-permute-done.3.x1) | copy-start | bytes 1572868
  24.7 2.0 %copy-start.12 = (bf16[128,2048]{1,0:T(8,128)(2,1)}, bf16[128,2048]{1,0:T(8,128)(2,1)S(1)}, u32[]{:S(2)}) copy-start(bf16[128,2048]{1,0:T(8,128)(2,1)S(1)} %collective-permute-done.4.x2) | copy-start | bytes 1572868
  24.7 2.0 %collective-permute-start.7 = (bf16[128,2048]{1,0:T(8,128)(2,1)S(1)}, bf16[128,2048]{1,0:T(8,128)(2,1)S(1)}, u32[]{:S(2)}, u32[]{:S(2)}) collective-permute-start(bf16[128,2048]{1,0:T(8,128)(2,1)S(1)} %collective-permute-done.3.x1), channel_id=1, source_target_pairs={{0,1},{1,0},{2,3},{3,2},{4,5},{5,4},{6,7},{7,6},{8,9},{9,8},{10,11... | collective-permute-start | bytes 1572872 | tf_op jit(solution)/shard_map/ppermute | solution.py:161
  24.8 15.6 %collective-permute-start = (bf16[64,2048]{1,0:T(8,128)(2,1)S(1)}, bf16[64,2048]{1,0:T(8,128)(2,1)S(1)}, u32[]{:S(2)}, u32[]{:S(2)}) collective-permute-start(bf16[64,2048]{1,0:T(8,128)(2,1)S(1)} %get-tuple-element.101), channel_id=1, source_target_pairs={{0,8},{1,9},{2,10},{3,11},{4,12},{5,13},{6,14},{7,15},{8,0},{9,1},... | collective-permute-start | bytes 786440 | tf_op jit(solution)/shard_map/ppermute | solution.py:161
  25.4 15.0 %collective-permute-start.5 = (bf16[128,2048]{1,0:T(8,128)(2,1)S(1)}, bf16[128,2048]{1,0:T(8,128)(2,1)}, u32[]{:S(2)}, u32[]{:S(2)}) collective-permute-start(bf16[128,2048]{1,0:T(8,128)(2,1)S(1)} %collective-permute-done.1.x0), channel_id=1, source_target_pairs={{0,2},{1,3},{2,0},{3,1},{4,6},{5,7},{6,4},{7,5},{8,10},{9,11},{10,... | collective-permute-start | bytes 1572872 | tf_op jit(solution)/shard_map/ppermute | solution.py:161
  26.0 14.4 %collective-permute-start.6 = (bf16[128,2048]{1,0:T(8,128)(2,1)S(1)}, bf16[128,2048]{1,0:T(8,128)(2,1)S(1)}, u32[]{:S(2)}, u32[]{:S(2)}) collective-permute-start(bf16[128,2048]{1,0:T(8,128)(2,1)S(1)} %collective-permute-done.1.x0), channel_id=1, source_target_pairs={{0,1},{1,0},{2,3},{3,2},{4,5},{5,4},{6,7},{7,6},{8,9},{9,8},{10,11... | collective-permute-start | bytes 1572872 | tf_op jit(solution)/shard_map/ppermute | solution.py:161
  26.7 0.8 copy-start.13
  40.4 0.8 copy-start.10
  41.2 4.2 %collective-permute-start.11 = (bf16[128,2048]{1,0:T(8,128)(2,1)}, bf16[128,2048]{1,0:T(8,128)(2,1)S(1)}, u32[]{:S(2)}, u32[]{:S(2)}) collective-permute-start(bf16[128,2048]{1,0:T(8,128)(2,1)} %collective-permute-done.5.x1), channel_id=1, source_target_pairs={{0,1},{1,0},{2,3},{3,2},{4,5},{5,4},{6,7},{7,6},{8,9},{9,8},{10,11... | collective-permute-start | bytes 1572872 | tf_op jit(solution)/shard_map/ppermute | solution.py:161
  41.7 17.5 %copy-start.7 = (bf16[128,2048]{1,0:T(8,128)(2,1)}, bf16[128,2048]{1,0:T(8,128)(2,1)S(1)}, u32[]{:S(2)}) copy-start(bf16[128,2048]{1,0:T(8,128)(2,1)S(1)} %constant_dynamic-update-slice_fusion.x0) | copy-start | bytes 1572868
  41.7 17.5 %collective-permute-start.10 = (bf16[128,2048]{1,0:T(8,128)(2,1)S(1)}, bf16[128,2048]{1,0:T(8,128)(2,1)S(1)}, u32[]{:S(2)}, u32[]{:S(2)}) collective-permute-start(bf16[128,2048]{1,0:T(8,128)(2,1)S(1)} %constant_dynamic-update-slice_fusion.x0), channel_id=1, source_target_pairs={{0,1},{1,0},{2,3},{3,2},{4,5},{5,4},{6,7},{7,6},{8,9},{9,8},{10,11... | collective-permute-start | bytes 1572872 | tf_op jit(solution)/shard_map/ppermute | solution.py:161
  41.9 17.3 %collective-permute-start.8 = (bf16[128,2048]{1,0:T(8,128)(2,1)S(1)}, bf16[128,2048]{1,0:T(8,128)(2,1)S(1)}, u32[]{:S(2)}, u32[]{:S(2)}) collective-permute-start(bf16[128,2048]{1,0:T(8,128)(2,1)S(1)} %constant_dynamic-update-slice_fusion.x0), channel_id=1, source_target_pairs={{0,4},{1,5},{2,6},{3,7},{4,0},{5,1},{6,2},{7,3},{8,12},{9,13},{10,... | collective-permute-start | bytes 1572872 | tf_op jit(solution)/shard_map/ppermute | solution.py:161
  43.5 15.7 %collective-permute-start.9 = (bf16[128,2048]{1,0:T(8,128)(2,1)S(1)}, bf16[128,2048]{1,0:T(8,128)(2,1)S(1)}, u32[]{:S(2)}, u32[]{:S(2)}) collective-permute-start(bf16[128,2048]{1,0:T(8,128)(2,1)S(1)} %constant_dynamic-update-slice_fusion.x0), channel_id=1, source_target_pairs={{0,2},{1,3},{2,0},{3,1},{4,6},{5,7},{6,4},{7,5},{8,10},{9,11},{10,... | collective-permute-start | bytes 1572872 | tf_op jit(solution)/shard_map/ppermute | solution.py:161
  45.5 0.8 copy-start.15
  59.2 1.4 copy-start.14
  59.2 16.7 %copy-start.5 = (bf16[128,2048]{1,0:T(8,128)(2,1)}, bf16[128,2048]{1,0:T(8,128)(2,1)S(1)}, u32[]{:S(2)}) copy-start(bf16[128,2048]{1,0:T(8,128)(2,1)S(1)} %collective-permute-done.8.x0) | copy-start | bytes 1572868
  59.2 3.6 %copy-start.6 = (bf16[128,2048]{1,0:T(8,128)(2,1)}, bf16[128,2048]{1,0:T(8,128)(2,1)S(1)}, u32[]{:S(2)}) copy-start(bf16[128,2048]{1,0:T(8,128)(2,1)S(1)} %collective-permute-done.9.x1) | copy-start | bytes 1572868
  59.2 16.7 %collective-permute-start.15 = (bf16[256,2048]{1,0:T(8,128)(2,1)}, bf16[256,2048]{1,0:T(8,128)(2,1)S(1)}, u32[]{:S(2)}, u32[]{:S(2)}) collective-permute-start(bf16[256,2048]{1,0:T(8,128)(2,1)} %get-tuple-element.67), channel_id=1, source_target_pairs={{0,1},{1,0},{2,3},{3,2},{4,5},{5,4},{6,7},{7,6},{8,9},{9,8},{10,11... | collective-permute-start | bytes 3145736 | tf_op jit(solution)/shard_map/ppermute | solution.py:161
  59.3 3.5 %collective-permute-start.16 = (bf16[128,2048]{1,0:T(8,128)(2,1)S(1)}, bf16[128,2048]{1,0:T(8,128)(2,1)}, u32[]{:S(2)}, u32[]{:S(2)}) collective-permute-start(bf16[128,2048]{1,0:T(8,128)(2,1)S(1)} %collective-permute-done.9.x1), channel_id=1, source_target_pairs={{0,1},{1,0},{2,3},{3,2},{4,5},{5,4},{6,7},{7,6},{8,9},{9,8},{10,11... | collective-permute-start | bytes 1572872 | tf_op jit(solution)/shard_map/ppermute | solution.py:161
  59.8 16.1 %collective-permute-start.14 = (bf16[128,2048]{1,0:T(8,128)(2,1)S(1)}, bf16[128,2048]{1,0:T(8,128)(2,1)}, u32[]{:S(2)}, u32[]{:S(2)}) collective-permute-start(bf16[128,2048]{1,0:T(8,128)(2,1)S(1)} %collective-permute-done.8.x0), channel_id=1, source_target_pairs={{0,1},{1,0},{2,3},{3,2},{4,5},{5,4},{6,7},{7,6},{8,9},{9,8},{10,11... | collective-permute-start | bytes 1572872 | tf_op jit(solution)/shard_map/ppermute | solution.py:161
  60.6 17.3 %copy-start.2 = (bf16[256,2048]{1,0:T(8,128)(2,1)S(1)}, bf16[256,2048]{1,0:T(8,128)(2,1)}, u32[]{:S(2)}) copy-start(bf16[256,2048]{1,0:T(8,128)(2,1)} %get-tuple-element.80) | copy-start | bytes 3145732
  60.6 15.3 %collective-permute-start.12 = (bf16[64,2048]{1,0:T(8,128)(2,1)S(1)}, bf16[64,2048]{1,0:T(8,128)(2,1)S(1)}, u32[]{:S(2)}, u32[]{:S(2)}) collective-permute-start(bf16[64,2048]{1,0:T(8,128)(2,1)S(1)} %slice.80), channel_id=1, source_target_pairs={{0,4},{1,5},{2,6},{3,7},{4,0},{5,1},{6,2},{7,3},{8,12},{9,13},{10,... | collective-permute-start | bytes 786440 | tf_op jit(solution)/shard_map/ppermute | solution.py:161
  61.1 14.8 %collective-permute-start.13 = (bf16[64,2048]{1,0:T(8,128)(2,1)S(1)}, bf16[64,2048]{1,0:T(8,128)(2,1)S(1)}, u32[]{:S(2)}, u32[]{:S(2)}) collective-permute-start(bf16[64,2048]{1,0:T(8,128)(2,1)S(1)} %slice.81), channel_id=1, source_target_pairs={{0,2},{1,3},{2,0},{3,1},{4,6},{5,7},{6,4},{7,5},{8,10},{9,11},{10,... | collective-permute-start | bytes 786440 | tf_op jit(solution)/shard_map/ppermute | solution.py:161
  75.9 17.5 %copy-start.3 = (bf16[256,2048]{1,0:T(8,128)(2,1)}, bf16[256,2048]{1,0:T(8,128)(2,1)S(1)}, u32[]{:S(2)}) copy-start(bf16[256,2048]{1,0:T(8,128)(2,1)S(1)} %collective-permute-done.15) | copy-start | bytes 3145732
  76.7 16.7 %collective-permute-start.18 = (bf16[256,2048]{1,0:T(8,128)(2,1)}, bf16[256,2048]{1,0:T(8,128)(2,1)S(1)}, u32[]{:S(2)}, u32[]{:S(2)}) collective-permute-start(bf16[256,2048]{1,0:T(8,128)(2,1)} %get-tuple-element.79), channel_id=1, source_target_pairs={{0,1},{1,0},{2,3},{3,2},{4,5},{5,4},{6,7},{7,6},{8,9},{9,8},{10,11... | collective-permute-start | bytes 3145736 | tf_op jit(solution)/shard_map/ppermute | solution.py:161
  77.6 2.9 %collective-permute-start.17 = (bf16[128,2048]{1,0:T(8,128)(2,1)}, bf16[128,2048]{1,0:T(8,128)(2,1)}, u32[]{:S(2)}, u32[]{:S(2)}) collective-permute-start(bf16[128,2048]{1,0:T(8,128)(2,1)} %constant_dynamic-update-slice_fusion.2.x1), channel_id=1, source_target_pairs={{0,1},{1,0},{2,3},{3,2},{4,5},{5,4},{6,7},{7,6},{8,9},{9,8},{10,11... | collective-permute-start | bytes 1572872 | tf_op jit(solution)/shard_map/ppermute | solution.py:161
  78.9 14.5 %collective-permute-start.19 = (bf16[128,2048]{1,0:T(8,128)(2,1)}, bf16[128,2048]{1,0:T(8,128)(2,1)}, u32[]{:S(2)}, u32[]{:S(2)}) collective-permute-start(bf16[128,2048]{1,0:T(8,128)(2,1)} %add_convert_fusion.4), channel_id=1, source_target_pairs={{0,2},{1,3},{2,0},{3,1},{4,6},{5,7},{6,4},{7,5},{8,10},{9,11},{10,... | collective-permute-start | bytes 1572872 | tf_op jit(solution)/shard_map/ppermute | solution.py:161
  80.2 27.0 %copy-start = (bf16[256,2048]{1,0:T(8,128)(2,1)S(1)}, bf16[256,2048]{1,0:T(8,128)(2,1)}, u32[]{:S(2)}) copy-start(bf16[256,2048]{1,0:T(8,128)(2,1)} %get-tuple-element.88) | copy-start | bytes 3145732
  80.2 13.5 %collective-permute-start.21 = (bf16[256,2048]{1,0:T(8,128)(2,1)}, bf16[256,2048]{1,0:T(8,128)(2,1)}, u32[]{:S(2)}, u32[]{:S(2)}) collective-permute-start(bf16[256,2048]{1,0:T(8,128)(2,1)} %get-tuple-element.85), channel_id=1, source_target_pairs={{0,1},{1,0},{2,3},{3,2},{4,5},{5,4},{6,7},{7,6},{8,9},{9,8},{10,11... | collective-permute-start | bytes 3145736 | tf_op jit(solution)/shard_map/ppermute | solution.py:161
  93.5 17.3 %copy-start.4 = (bf16[256,2048]{1,0:T(8,128)(2,1)S(1)}, bf16[256,2048]{1,0:T(8,128)(2,1)}, u32[]{:S(2)}) copy-start(bf16[256,2048]{1,0:T(8,128)(2,1)} %copy-done.3) | copy-start | bytes 3145732
  93.5 2.9 %collective-permute-start.20 = (bf16[256,2048]{1,0:T(8,128)(2,1)}, bf16[256,2048]{1,0:T(8,128)(2,1)S(1)}, u32[]{:S(2)}, u32[]{:S(2)}) collective-permute-start(bf16[256,2048]{1,0:T(8,128)(2,1)} %get-tuple-element.84), channel_id=1, source_target_pairs={{0,1},{1,0},{2,3},{3,2},{4,5},{5,4},{6,7},{7,6},{8,9},{9,8},{10,11... | collective-permute-start | bytes 3145736 | tf_op jit(solution)/shard_map/ppermute | solution.py:161
  97.8 8.4 %collective-permute-start.24 = (bf16[64,2048]{1,0:T(8,128)(2,1)S(1)}, bf16[64,2048]{1,0:T(8,128)(2,1)S(1)}, u32[]{:S(2)}, u32[]{:S(2)}) collective-permute-start(bf16[64,2048]{1,0:T(8,128)(2,1)S(1)} %get-tuple-element.100), channel_id=1, source_target_pairs={{0,4},{1,5},{2,6},{3,7},{4,0},{5,1},{6,2},{7,3},{8,12},{9,13},{10,... | collective-permute-start | bytes 786440 | tf_op jit(solution)/shard_map/ppermute | solution.py:161
  98.9 14.5 %copy-start.1 = (bf16[256,2048]{1,0:T(8,128)(2,1)S(1)}, bf16[256,2048]{1,0:T(8,128)(2,1)}, u32[]{:S(2)}) copy-start(bf16[256,2048]{1,0:T(8,128)(2,1)} %get-tuple-element.83) | copy-start | bytes 3145732
  98.9 8.3 %collective-permute-start.25 = (bf16[64,2048]{1,0:T(8,128)(2,1)S(1)}, bf16[64,2048]{1,0:T(8,128)(2,1)S(1)}, u32[]{:S(2)}, u32[]{:S(2)}) collective-permute-start(bf16[64,2048]{1,0:T(8,128)(2,1)S(1)} %get-tuple-element.99), channel_id=1, source_target_pairs={{0,2},{1,3},{2,0},{3,1},{4,6},{5,7},{6,4},{7,5},{8,10},{9,11},{10,... | collective-permute-start | bytes 786440 | tf_op jit(solution)/shard_map/ppermute | solution.py:161
  107.4 14.9 %collective-permute-start.27 = (bf16[128,2048]{1,0:T(8,128)(2,1)S(1)}, bf16[128,2048]{1,0:T(8,128)(2,1)S(1)}, u32[]{:S(2)}, u32[]{:S(2)}) collective-permute-start(bf16[128,2048]{1,0:T(8,128)(2,1)S(1)} %pad_maximum_fusion.1), channel_id=1, source_target_pairs={{0,2},{1,3},{2,0},{3,1},{4,6},{5,7},{6,4},{7,5},{8,10},{9,11},{10,... | collective-permute-start | bytes 1572872 | tf_op jit(solution)/shard_map/ppermute | solution.py:161
  109.2 17.6 %copy-start.8 = (f32[16,1,128]{2,1,0:T(1,128)S(1)}, f32[16,1,128]{2,1,0:T(1,128)}, u32[]{:S(2)}) copy-start(f32[16,1,128]{2,1,0:T(1,128)} %all_to_all.9) | copy-start | bytes 24580
  109.2 14.9 %collective-permute-start.26 = (bf16[128,2048]{1,0:T(8,128)(2,1)S(1)}, bf16[128,2048]{1,0:T(8,128)(2,1)S(1)}, u32[]{:S(2)}, u32[]{:S(2)}) collective-permute-start(bf16[128,2048]{1,0:T(8,128)(2,1)S(1)} %pad_maximum_fusion), channel_id=1, source_target_pairs={{0,4},{1,5},{2,6},{3,7},{4,0},{5,1},{6,2},{7,3},{8,12},{9,13},{10,... | collective-permute-start | bytes 1572872 | tf_op jit(solution)/shard_map/ppermute | solution.py:161
  112.9 31.6 %collective-permute-start.23 = (bf16[128,2048]{1,0:T(8,128)(2,1)}, bf16[128,2048]{1,0:T(8,128)(2,1)}, u32[]{:S(2)}, u32[]{:S(2)}) collective-permute-start(bf16[128,2048]{1,0:T(8,128)(2,1)} %add_convert_fusion.2), channel_id=1, source_target_pairs={{0,4},{1,5},{2,6},{3,7},{4,0},{5,1},{6,2},{7,3},{8,12},{9,13},{10,... | collective-permute-start | bytes 1572872 | tf_op jit(solution)/shard_map/ppermute | solution.py:161
  114.6 29.9 %collective-permute-start.22 = (bf16[128,2048]{1,0:T(8,128)(2,1)S(1)}, bf16[128,2048]{1,0:T(8,128)(2,1)}, u32[]{:S(2)}, u32[]{:S(2)}) collective-permute-start(bf16[128,2048]{1,0:T(8,128)(2,1)S(1)} %add_convert_fusion.3), channel_id=1, source_target_pairs={{0,2},{1,3},{2,0},{3,1},{4,6},{5,7},{6,4},{7,5},{8,10},{9,11},{10,... | collective-permute-start | bytes 1572872 | tf_op jit(solution)/shard_map/ppermute | solution.py:161
  124.5 22.1 %collective-permute-start.28 = (bf16[128,2048]{1,0:T(8,128)(2,1)S(1)}, bf16[128,2048]{1,0:T(8,128)(2,1)S(1)}, u32[]{:S(2)}, u32[]{:S(2)}) collective-permute-start(bf16[128,2048]{1,0:T(8,128)(2,1)S(1)} %add_convert_fusion.1), channel_id=1, source_target_pairs={{0,8},{1,9},{2,10},{3,11},{4,12},{5,13},{6,14},{7,15},{8,0},{9,1},... | collective-permute-start | bytes 1572872 | tf_op jit(solution)/shard_map/ppermute | solution.py:161

commit v7 on v6

--- a/solution.py
+++ b/solution.py
@@ -35,37 +35,31 @@
     return total.astype(jnp.bfloat16)
 
 
-def plane_kernel(
-    capacity, order, weight, x0, x1, x2, x3, w_gate, w_up, w_down, keep, give, act,
-    x, rows, ranks, gates, ups, downs, x_sem, gate_sem, up_sem, down_sem,
-):
+def plane_kernel(capacity, k, parts, spots, weight, *refs):
+    xs, refs = refs[:parts], refs[parts:]
+    w_gate, w_up, w_down, keep, give, act_out = refs[:6]
+    x, rows, act, out, ranks, gates, ups, downs, x_sem, gate_sem, up_sem, down_sem, out_sem = refs[6:]
     blocks, tok = weight.shape
     slots, hidden = act.shape
     tiles, features, wide = gates.shape
     cuts, _, cut = downs.shape
-    x_copies = [
-        pltpu.make_async_copy(block, x.at[pl.ds(i * tok, tok), :], x_sem.at[i])
-        for i, block in enumerate((x0, x1, x2, x3))
-    ]
-    gate_copies = [
-        pltpu.make_async_copy(w_gate.at[:, pl.ds(i * wide, wide)], gates.at[i], gate_sem.at[i])
-        for i in range(tiles)
-    ]
-    up_copies = [
-        pltpu.make_async_copy(w_up.at[:, pl.ds(i * wide, wide)], ups.at[i], up_sem.at[i])
-        for i in range(tiles)
-    ]
-    down_copies = [
-        pltpu.make_async_copy(w_down.at[:, pl.ds(i * cut, cut)], downs.at[i], down_sem.at[i])
-        for i in range(cuts)
-    ]
+    x_copies, at = [], 0
+    for i, block in enumerate(xs):
+        target = x.at[pl.ds(at, block.shape[0]), :]
+        x_copies.append(pltpu.make_async_copy(block, target, x_sem.at[i]))
+        at += block.shape[0]
+    loads = []
+    for i in range(tiles):
+        span = pl.ds(i * wide, wide)
+        loads.append(pltpu.make_async_copy(w_gate.at[:, span], gates.at[i], gate_sem.at[i]))
+        loads.append(pltpu.make_async_copy(w_up.at[:, span], ups.at[i], up_sem.at[i]))
+    for i in range(cuts):
+        span = pl.ds(i * cut, cut)
+        loads.append(pltpu.make_async_copy(w_down.at[:, span], downs.at[i], down_sem.at[i]))
     for copy in x_copies:
         copy.start()
-    for gate_copy, up_copy in zip(gate_copies, up_copies):
-        gate_copy.start()
-        up_copy.start()
-    for copy in down_copies:
-        copy.start()
+    loads[0].start()
+    loads[1].start()
 
     named = (weight[...] >= 0.0).astype(jnp.float32)
     lane = lax.broadcasted_iota(jnp.int32, (tok, tok), 0)
@@ -77,45 +71,56 @@
     before = jnp.dot(earlier, totals, preferred_element_type=jnp.float32)
     rank = within + before
     kept = (named > 0.0) & (rank < capacity)
+    order = [spots[4 * k + i] for i in range(4)]
     first = order[0] // 4 * 4
     block_row = lax.broadcasted_iota(jnp.int32, (blocks, tok), 0)
     start = jnp.sum(jnp.where(block_row == first, before, 0.0), axis=0, keepdims=True)
     ranks[...] = jnp.where(kept, rank - start, -1.0)
-
-    places = [ranks[pl.ds(order[i], 1), :] for i in range(4)]
-    shares = [weight[pl.ds(order[i], 1), :] for i in range(4)]
-    place = jnp.concatenate(places, axis=1)
-    share = jnp.concatenate(shares, axis=1)
+    place = jnp.concatenate([ranks[pl.ds(i, 1), :] for i in order], axis=1)
+    share = jnp.concatenate([weight[pl.ds(i, 1), :] for i in order], axis=1)
     slot = lax.broadcasted_iota(jnp.int32, (slots, 4 * tok), 0).astype(jnp.float32)
     hits = slot == place
     scale = jnp.sum(jnp.where(hits, share, 0.0), axis=1, keepdims=True)
     select = hits.astype(jnp.float32).astype(jnp.bfloat16)
     for copy in x_copies:
         copy.wait()
+    for load in loads[2 : 2 * tiles]:
+        load.start()
     for i in range(cuts):
         span = pl.ds(i * cut, cut)
         rows[:, span] = jnp.dot(
             select, x[:, span], preferred_element_type=jnp.float32
         ).astype(jnp.bfloat16)
+    for load in loads[2 * tiles :]:
+        load.start()
+    act_copy = pltpu.make_async_copy(act, act_out, out_sem.at[2 * cuts])
     for i in range(tiles):
-        gate_copies[i].wait()
+        loads[2 * i].wait()
         gate = jnp.dot(rows[...], gates[i], preferred_element_type=jnp.float32)
-        up_copies[i].wait()
+        loads[2 * i + 1].wait()
         up = jnp.dot(rows[...], ups[i], preferred_element_type=jnp.float32)
         act[:, pl.ds(i * wide, wide)] = (gate / (1.0 + jnp.exp(-gate)) * up).astype(jnp.bfloat16)
+    act_copy.start()
     back = select.T
+    out_copies = []
     for i in range(cuts):
         span = pl.ds(i * cut, cut)
-        down_copies[i].wait()
+        loads[2 * tiles + i].wait()
         result = jnp.dot(act[...], downs[i], preferred_element_type=jnp.float32)
         made = (result * scale).astype(jnp.bfloat16)
-        spread = jnp.dot(back, made, preferred_element_type=jnp.float32).astype(jnp.bfloat16)
-        keep[:, span] = spread[: 2 * tok]
-        give[:, span] = spread[2 * tok :]
-
-
-def plane_pass(order, weight, xs, w_gate, w_up, w_down, slots, capacity):
-    tok, features = xs[0].shape
+        out[i] = jnp.dot(back, made, preferred_element_type=jnp.float32).astype(jnp.bfloat16)
+        for half, target in enumerate((keep, give)):
+            source = out.at[i, pl.ds(half * 2 * tok, 2 * tok), :]
+            copy = pltpu.make_async_copy(source, target.at[:, span], out_sem.at[2 * i + half])
+            copy.start()
+            out_copies.append(copy)
+    act_copy.wait()
+    for copy in out_copies:
+        copy.wait()
+
+
+def plane_pass(k, spots, weight, xs, w_gate, w_up, w_down, slots, capacity):
+    tok, features = weight.shape[1], w_gate.shape[0]
     hidden = w_gate.shape[1]
     half = jax.ShapeDtypeStruct((2 * tok, features), jnp.bfloat16)
     rows = 4 * slots
@@ -124,28 +129,31 @@
     flops = 2 * rows * (3 * features * hidden + 8 * tok * features)
     moved = 2 * (3 * features * hidden + 8 * tok * features)
     return pl.pallas_call(
-        functools.partial(plane_kernel, capacity),
+        functools.partial(plane_kernel, capacity, k, len(xs)),
         out_shape=(half, half, jax.ShapeDtypeStruct((rows, hidden), jnp.bfloat16)),
         in_specs=[pl.BlockSpec(memory_space=pltpu.SMEM), pl.BlockSpec(memory_space=pltpu.VMEM)]
-        + [pl.BlockSpec(memory_space=pl.ANY)] * 7,
-        out_specs=[pl.BlockSpec(memory_space=pltpu.VMEM)] * 3,
+        + [pl.BlockSpec(memory_space=pl.ANY)] * (len(xs) + 3),
+        out_specs=[pl.BlockSpec(memory_space=pl.ANY)] * 3,
         scratch_shapes=[
             pltpu.VMEM((4 * tok, features), jnp.bfloat16),
             pltpu.VMEM((rows, features), jnp.bfloat16),
+            pltpu.VMEM((rows, hidden), jnp.bfloat16),
+            pltpu.VMEM((cuts, 4 * tok, cut), jnp.bfloat16),
             pltpu.VMEM(weight.shape, jnp.float32),
             pltpu.VMEM((tiles, features, wide), jnp.bfloat16),
             pltpu.VMEM((tiles, features, wide), jnp.bfloat16),
             pltpu.VMEM((cuts, hidden, cut), jnp.bfloat16),
-            pltpu.SemaphoreType.DMA((4,)),
+            pltpu.SemaphoreType.DMA((len(xs),)),
             pltpu.SemaphoreType.DMA((tiles,)),
             pltpu.SemaphoreType.DMA((tiles,)),
             pltpu.SemaphoreType.DMA((cuts,)),
+            pltpu.SemaphoreType.DMA((2 * cuts + 1,)),
         ],
         compiler_params=pltpu.CompilerParams(vmem_limit_bytes=58 * 1024 * 1024),
         cost_estimate=pl.CostEstimate(
             flops=flops, bytes_accessed=moved, transcendentals=rows * hidden
         ),
-    )(order, weight, *xs, w_gate, w_up, w_down)
+    )(spots, weight, *xs, w_gate, w_up, w_down)
 
 
 def staged(routes, probs, tokens, w_gate, w_up, w_down):
@@ -168,17 +176,17 @@
     def together(*arrays):
         return lax.optimization_barrier(arrays)
 
+    spots = jnp.stack(
+        [
+            (z ^ k) * 4 + (y ^ column_bit) * 2 + (core ^ core_bit)
+            for k in range(4)
+            for core_bit in range(2)
+            for column_bit in range(2)
+        ]
+    ).astype(jnp.int32)
+
     def expert(k, *xs):
-        base = (z ^ k) * 4
-        order = jnp.stack(
-            [
-                base + y * 2 + core,
-                base + (1 - y) * 2 + core,
-                base + y * 2 + 1 - core,
-                base + (1 - y) * 2 + 1 - core,
-            ]
-        ).astype(jnp.int32)
-        return plane_pass(order, weight, xs, w_gate, w_up, w_down, slots, capacity)
+        return plane_pass(k, spots, weight, xs, w_gate, w_up, w_down, slots, capacity)
 
     weight = weights_for_me(routes, probs, size)
     a0 = tokens
@@ -207,11 +215,11 @@
     b3_low, b3_high, c3, got1, keep2, give2, act2 = together(
         b3_low, b3_high, c3, got1, keep2, give2, act2
     )
-    b3 = jnp.concatenate([b3_low, b3_high], axis=0)
-    d3 = sibling(b3)
+    d3_low = sibling(b3_low)
+    d3_high = sibling(b3_high)
     came1 = column(summed(keep1[tok:], got1[tok:]))
     got2 = sibling(give2)
-    keep3, give3, act3 = expert(3, a3, b3, c3, d3)
+    keep3, give3, act3 = expert(3, a3, b3_low, b3_high, c3, d3_low, d3_high)
 
     keep3, give3, act3, got2, came1 = together(keep3, give3, act3, got2, came1)
     got3 = sibling(give3)
@@ -230,10 +238,12 @@
         ],
         axis=0,
     )
-    far3, side2 = together(pair(far3), column(side2))
+    near1 = summed(keep1[:tok], got1[:tok], came1)
+    side0 = summed(keep0[tok:], got0[tok:])
+    far3, side2, near1, side0 = together(pair(far3), column(side2), near1, side0)
     last2 = far(summed(keep2[:tok], got2[:tok], far3, side2))
-    last1 = pair(summed(keep1[:tok], got1[:tok], came1))
-    last0 = column(summed(keep0[tok:], got0[tok:]))
+    last1 = pair(near1)
+    last0 = column(side0)
     mixed = summed(keep0[:tok], got0[:tok], last0, last1, last2)
 
     acts = jnp.concatenate([act0, act1, act2, act3], axis=0)

time: 152 us -> 151 us (level); the launches traced: 149 us -> 150 us
  other arithmetic: 14.3 us -> 8.89 us
  waiting for transfers between devices: 32.9 us -> 37.1 us
  starting transfers between devices: 24 us -> 26.2 us
    ppermute x29 -> x30, waiting for transfers between devices: 32.9 us -> 37.1 us  [swapped(): return lax.ppermute(array, 'expert', [(i, i ^ bit) for i in range(size)])]
    convert_element_type x8, other arithmetic: 9.69 us -> 6.77 us  [summed(): return total.astype(jnp.bfloat16)]
    another operation x4 -> x0, other arithmetic: 2.46 us -> none  [expert(): jnp.stack([base + y * 2 + core, base + (1 - y) * 2 + core, base + y * 2 +...]
    ppermute x29 -> x30, starting transfers between devices: 24 us -> 26.2 us  [swapped(): return lax.ppermute(array, 'expert', [(i, i ^ bit) for i in range(size)])]
    unnamed x34 -> x43, local copies, waits for them, and re-layouts: 3.25 us -> 4.14 us
  transfers between devices with their start and end apart: 29 -> 30, of which waited for: 10 -> 11; matrix products, arithmetic and copies ran while one was open for 12% -> 7% of each run, Pallas kernels for 35% -> 34%
where the time goes in v7:
time: 151 us; the launch traced here: 150 us
  Pallas kernels  50.4 us (33%)
  waiting for transfers between devices  37.1 us (25%)
  starting transfers between devices  26.2 us (17%)
  blocking collectives  14.6 us (10%)
  other arithmetic  8.89 us (6%)
  local copies, waits for them, and re-layouts  5.95 us (4%)
  matrix products  5.31 us (4%)
  between operations  1.75 us (1%)
    pallas_call x4, Pallas kernels, plane_pass(): pl.pallas_call(functools.partial(plane_kernel, capacity, k, len(xs)), out...  50.4 us
    ppermute x30, waiting for transfers between devices, swapped(): return lax.ppermute(array, 'expert', [(i, i ^ bit) for i in range(size)])  37.1 us
    ppermute x30, starting transfers between devices, swapped(): return lax.ppermute(array, 'expert', [(i, i ^ bit) for i in range(size)])  26.2 us
    all_to_all x1, blocking collectives, weights_for_me(): lax.all_to_all(mine, 'expert', split_axis=0, concat_axis=0, tiled=True)  14.6 us
    convert_element_type x8, other arithmetic, summed(): return total.astype(jnp.bfloat16)  6.77 us
    dot_general x1, matrix products, gram_of(): lax.dot_general(rows, rows, (((0,), (0,)), ((), ())), preferred_element_t...  5.31 us
    unnamed x43, local copies, waits for them, and re-layouts  4.14 us
  transfers between devices with their start and end apart: 30, of which 11 were waited for; matrix products, arithmetic and copies ran while one was open for 7% of the time, Pallas kernels for 34%

profile of v7, /device:TPU:0, one launch (start us, length us, event | category | flops | bytes accessed | tf_op | source)
XLA Modules:
  0.0 150.2 jit_solution(8038089992989125330)
XLA Ops:
  0.6 3.0 %collective-permute-start.3 = (bf16[128,2048]{1,0:T(8,128)(2,1)}, bf16[128,2048]{1,0:T(8,128)(2,1)S(1)}, u32[]{:S(2)}, u32[]{:S(2)}) collective-permute-start(bf16[128,2048]{1,0:T(8,128)(2,1)} %refs_0_.1), channel_id=1, source_target_pairs={{0,2},{1,3},{2,0},{3,1},{4,6},{5,7},{6,4},{7,5},{8,10},{9,11},{10,... | collective-permute-start | bytes 1572872 | tf_op jit(solution)/shard_map/ppermute | solution.py:169
  3.7 1.6 %collective-permute-start.1 = (bf16[128,2048]{1,0:T(8,128)(2,1)}, bf16[128,2048]{1,0:T(8,128)(2,1)S(1)}, u32[]{:S(2)}, u32[]{:S(2)}) collective-permute-start(bf16[128,2048]{1,0:T(8,128)(2,1)} %refs_0_.1), channel_id=1, source_target_pairs={{0,4},{1,5},{2,6},{3,7},{4,0},{5,1},{6,2},{7,3},{8,12},{9,13},{10,... | collective-permute-start | bytes 1572872 | tf_op jit(solution)/shard_map/ppermute | solution.py:169
  5.2 1.1 fusion.12
  6.3 2.7 %collective-permute-start.2 = (bf16[64,2048]{1,0:T(8,128)(2,1)S(1)}, bf16[64,2048]{1,0:T(8,128)(2,1)S(1)}, u32[]{:S(2)}, u32[]{:S(2)}) collective-permute-start(bf16[64,2048]{1,0:T(8,128)(2,1)S(1)} %get-tuple-element.106), channel_id=1, source_target_pairs={{0,8},{1,9},{2,10},{3,11},{4,12},{5,13},{6,14},{7,15},{8,0},{9,1},... | collective-permute-start | bytes 786440 | tf_op jit(solution)/shard_map/ppermute | solution.py:169
  9.0 0.7 select_reduce_fusion
  9.7 0.7 fusion.10
  10.4 14.6 %all_to_all.9 = f32[16,1,128]{2,1,0:T(1,128)} all-to-all(f32[16,1,128]{2,1,0:T(1,128)S(1)} %bitcast.32), channel_id=1, replica_groups=mesh['parts'=2,'expert'=16] {'expert'}, dimensions={0} | all-to-all | bytes 16384 | tf_op jit(solution)/shard_map/all_to_all | solution.py:28
  25.1 0.1 collective-permute-start.7
  25.2 0.5 collective-permute-start.6
  25.7 1.5 collective-permute-start.5
  27.1 0.6 collective-permute-start
  27.7 0.7 stack.67.spots
  28.4 12.6 %shard_map.77 = (bf16[256,2048]{1,0:T(8,128)(2,1)}, bf16[256,2048]{1,0:T(8,128)(2,1)}, bf16[320,768]{1,0:T(8,128)(2,1)}) custom-call(s32[16]{0:T(128)} %stack.67.spots, f32[16,128]{1,0:T(8,128)} %bitcast.27, bf16[128,2048]{1,0:T(8,128)(2,1)} %refs_0_.1, bf16[128,2048]{1,0:T(8,128)(2,1)} %copy-done.10, bf16[128,2048]{1,0:T(8,128)(2,1)} %copy-done.13, ...), custom_call_target="tpu_custom_call" | custom-call | flops 4362076160 | bytes 13631488 | tf_op jit(solution)/shard_map/pallas_call | solution.py:131
  41.0 0.7 collective-permute-done
  41.7 0.1 collective-permute-start.11
  41.8 0.6 collective-permute-start.10
  42.4 0.6 collective-permute-start.9
  43.0 1.0 collective-permute-start.8
  44.0 0.8 copy-done.16
  44.8 12.5 %shard_map.78 = (bf16[256,2048]{1,0:T(8,128)(2,1)}, bf16[256,2048]{1,0:T(8,128)(2,1)}, bf16[320,768]{1,0:T(8,128)(2,1)}) custom-call(s32[16]{0:T(128)} %stack.67.spots, f32[16,128]{1,0:T(8,128)} %bitcast.28, bf16[128,2048]{1,0:T(8,128)(2,1)} %copy-done.9, bf16[128,2048]{1,0:T(8,128)(2,1)} %copy-done.12, bf16[128,2048]{1,0:T(8,128)(2,1)} %copy-done.11, ...), custom_call_target="tpu_custom_call" | custom-call | flops 4362076160 | bytes 13631488 | tf_op jit(solution)/shard_map/pallas_call | solution.py:131
  57.5 0.5 collective-permute-start.16
  58.0 0.1 collective-permute-start.14
  58.2 1.4 collective-permute-start.13
  59.6 1.1 collective-permute-start.12
  60.7 0.2 collective-permute-done.16.refs_3_
  60.9 0.8 copy-done.17
  61.7 12.7 %shard_map.79 = (bf16[256,2048]{1,0:T(8,128)(2,1)}, bf16[256,2048]{1,0:T(8,128)(2,1)}, bf16[320,768]{1,0:T(8,128)(2,1)}) custom-call(s32[16]{0:T(128)} %stack.67.spots, f32[16,128]{1,0:T(8,128)} %bitcast.29, bf16[128,2048]{1,0:T(8,128)(2,1)} %copy-done.7, bf16[128,2048]{1,0:T(8,128)(2,1)} %copy-done.6, bf16[128,2048]{1,0:T(8,128)(2,1)} %copy-done.15, ...), custom_call_target="tpu_custom_call" | custom-call | flops 4362076160 | bytes 13631488 | tf_op jit(solution)/shard_map/pallas_call | solution.py:131
  74.5 0.2 collective-permute-start.19
  74.7 0.4 collective-permute-start.17
  75.1 0.3 copy-done.14
  75.4 0.1 collective-permute-start.18
  75.5 0.1 add_convert_fusion.4
  75.7 1.5 collective-permute-start.20
  77.1 0.1 collective-permute-start.22
  77.2 1.0 collective-permute-done.17.refs_4_
  78.2 0.7 copy-done.19
  78.9 0.7 copy-done.20
  79.6 12.6 %shard_map.80 = (bf16[256,2048]{1,0:T(8,128)(2,1)}, bf16[256,2048]{1,0:T(8,128)(2,1)}, bf16[320,768]{1,0:T(8,128)(2,1)}) custom-call(s32[16]{0:T(128)} %stack.67.spots, f32[16,128]{1,0:T(8,128)} %bitcast.30, bf16[128,2048]{1,0:T(8,128)(2,1)} %copy-done.5, bf16[64,2048]{1,0:T(8,128)(2,1)} %collective-permute-done.12.refs_1_, bf16[64,2048]{1,0:T(8,128)(2,1)} %copy-done.18, ...), custom_call_target="tpu_custom_call" | custom-call | flops 4362076160 | bytes 13631488 | tf_op jit(solution)/shard_map/pallas_call | solution.py:131
  92.2 0.8 copy-done.3
  93.0 0.1 collective-permute-start.21
  93.1 2.7 %collective-permute-done.21 = bf16[256,2048]{1,0:T(8,128)(2,1)S(1)} collective-permute-done((bf16[256,2048]{1,0:T(8,128)(2,1)}, bf16[256,2048]{1,0:T(8,128)(2,1)S(1)}, u32[]{:S(2)}, u32[]{:S(2)}) %collective-permute-start.21) | collective-permute-done | bytes 1048608 | tf_op jit(solution)/shard_map/ppermute | solution.py:169
  95.9 1.4 add_convert_fusion.10
  97.2 1.4 collective-permute-start.24
  98.7 1.1 collective-permute-start.23
  99.8 5.9 %collective-permute-done.24 = bf16[64,2048]{1,0:T(8,128)(2,1)S(1)} collective-permute-done((bf16[64,2048]{1,0:T(8,128)(2,1)S(1)}, bf16[64,2048]{1,0:T(8,128)(2,1)S(1)}, u32[]{:S(2)}, u32[]{:S(2)}) %collective-permute-start.24) | collective-permute-done | bytes 262176 | tf_op jit(solution)/shard_map/ppermute | solution.py:169
  105.6 1.1 collective-permute-done.23
  106.7 1.0 add_convert_fusion.7
  107.8 0.2 add_convert_fusion.6
  108.0 0.7 collective-permute-start.26
  108.8 1.1 collective-permute-start.25
  109.9 1.0 add_convert_fusion.3
  110.9 0.1 add_convert_fusion.2
  111.0 9.9 %collective-permute-done.26 = bf16[128,2048]{1,0:T(8,128)(2,1)S(1)} collective-permute-done((bf16[128,2048]{1,0:T(8,128)(2,1)S(1)}, bf16[128,2048]{1,0:T(8,128)(2,1)S(1)}, u32[]{:S(2)}, u32[]{:S(2)}) %collective-permute-start.26) | collective-permute-done | bytes 524320 | tf_op jit(solution)/shard_map/ppermute | solution.py:169
  120.9 0.5 collective-permute-done.25
  121.4 1.4 collective-permute-start.27
  122.8 1.1 collective-permute-start.28
  123.9 0.3 add_convert_fusion.1
  124.2 1.8 %collective-permute-start.29 = (bf16[128,2048]{1,0:T(8,128)(2,1)S(1)}, bf16[128,2048]{1,0:T(8,128)(2,1)}, u32[]{:S(2)}, u32[]{:S(2)}) collective-permute-start(bf16[128,2048]{1,0:T(8,128)(2,1)S(1)} %add_convert_fusion.1), channel_id=1, source_target_pairs={{0,8},{1,9},{2,10},{3,11},{4,12},{5,13},{6,14},{7,15},{8,0},{9,1},... | collective-permute-start | bytes 1572872 | tf_op jit(solution)/shard_map/ppermute | solution.py:169
  126.0 0.6 convert_reduce_fusion
  127.3 5.3 %multiply_bitcast_fusion = f32[1,768,768]{2,1,0:T(8,128)} fusion(f32[]{:T(128)S(6)} %div.24, bf16[320,768]{1,0:T(8,128)(2,1)} %get-tuple-element.84, bf16[320,768]{1,0:T(8,128)(2,1)} %get-tuple-element.74, bf16[320,768]{1,0:T(8,128)(2,1)} %get-tuple-element.66, bf16[320,768]{1,0:T(8,128)(2,1)} %get-tuple-element.58), kind=kOutput, calls=%fused_computation | convolution fusion | flops 1518403584 | bytes 4325380 | tf_op jit(solution)/shard_map/dot_general | solution.py:12
  132.6 0.6 collective-permute-done.27
  133.1 11.5 %collective-permute-done.28 = bf16[128,2048]{1,0:T(8,128)(2,1)} collective-permute-done((bf16[128,2048]{1,0:T(8,128)(2,1)}, bf16[128,2048]{1,0:T(8,128)(2,1)}, u32[]{:S(2)}, u32[]{:S(2)}) %collective-permute-start.28) | collective-permute-done | bytes 524320 | tf_op jit(solution)/shard_map/ppermute | solution.py:169
  144.6 3.0 %collective-permute-done.29 = bf16[128,2048]{1,0:T(8,128)(2,1)} collective-permute-done((bf16[128,2048]{1,0:T(8,128)(2,1)S(1)}, bf16[128,2048]{1,0:T(8,128)(2,1)}, u32[]{:S(2)}, u32[]{:S(2)}) %collective-permute-start.29) | collective-permute-done | bytes 524320 | tf_op jit(solution)/shard_map/ppermute | solution.py:169
  147.6 2.6 %add_convert_fusion = bf16[128,2048]{1,0:T(8,128)(2,1)} fusion(bf16[128,2048]{1,0:T(8,128)(2,1)} %collective-permute-done.29, bf16[128,2048]{1,0:T(8,128)(2,1)} %collective-permute-done.28, bf16[128,2048]{1,0:T(8,128)(2,1)} %collective-permute-done.27, bf16[256,2048]{1,0:T(8,128)(2,1)S(1)} %collective-permute-done.22, bf16[256,2048]{1,0:T(8,128)(2,1)S(1)} %copy-done.1), kind=kLoop, calls=%fused_computation.9 | loop fusion | flops 2621440 | bytes 3145728 | tf_op jit(solution)/shard_map/convert_element_type | solution.py:35
  (64 shorter events, 0.4 us)
Async XLA Ops:
  0.6 24.4 %collective-permute-start.3 = (bf16[128,2048]{1,0:T(8,128)(2,1)}, bf16[128,2048]{1,0:T(8,128)(2,1)S(1)}, u32[]{:S(2)}, u32[]{:S(2)}) collective-permute-start(bf16[128,2048]{1,0:T(8,128)(2,1)} %refs_0_.1), channel_id=1, source_target_pairs={{0,2},{1,3},{2,0},{3,1},{4,6},{5,7},{6,4},{7,5},{8,10},{9,11},{10,... | collective-permute-start | bytes 1572872 | tf_op jit(solution)/shard_map/ppermute | solution.py:169
  3.7 21.4 %collective-permute-start.1 = (bf16[128,2048]{1,0:T(8,128)(2,1)}, bf16[128,2048]{1,0:T(8,128)(2,1)S(1)}, u32[]{:S(2)}, u32[]{:S(2)}) collective-permute-start(bf16[128,2048]{1,0:T(8,128)(2,1)} %refs_0_.1), channel_id=1, source_target_pairs={{0,4},{1,5},{2,6},{3,7},{4,0},{5,1},{6,2},{7,3},{8,12},{9,13},{10,... | collective-permute-start | bytes 1572872 | tf_op jit(solution)/shard_map/ppermute | solution.py:169
  5.2 19.8 %collective-permute-start.4 = (bf16[128,2048]{1,0:T(8,128)(2,1)}, bf16[128,2048]{1,0:T(8,128)(2,1)S(1)}, u32[]{:S(2)}, u32[]{:S(2)}) collective-permute-start(bf16[128,2048]{1,0:T(8,128)(2,1)} %refs_0_.1), channel_id=1, source_target_pairs={{0,1},{1,0},{2,3},{3,2},{4,5},{5,4},{6,7},{7,6},{8,9},{9,8},{10,11... | collective-permute-start | bytes 1572872 | tf_op jit(solution)/shard_map/ppermute | solution.py:169
  6.3 18.7 %collective-permute-start.2 = (bf16[64,2048]{1,0:T(8,128)(2,1)S(1)}, bf16[64,2048]{1,0:T(8,128)(2,1)S(1)}, u32[]{:S(2)}, u32[]{:S(2)}) collective-permute-start(bf16[64,2048]{1,0:T(8,128)(2,1)S(1)} %get-tuple-element.106), channel_id=1, source_target_pairs={{0,8},{1,9},{2,10},{3,11},{4,12},{5,13},{6,14},{7,15},{8,0},{9,1},... | collective-permute-start | bytes 786440 | tf_op jit(solution)/shard_map/ppermute | solution.py:169
  25.1 3.4 %copy-start.10 = (bf16[128,2048]{1,0:T(8,128)(2,1)}, bf16[128,2048]{1,0:T(8,128)(2,1)S(1)}, u32[]{:S(2)}) copy-start(bf16[128,2048]{1,0:T(8,128)(2,1)S(1)} %collective-permute-done.3.refs_1_) | copy-start | bytes 1572868
  25.1 15.9 %copy-start.9 = (bf16[128,2048]{1,0:T(8,128)(2,1)}, bf16[128,2048]{1,0:T(8,128)(2,1)S(1)}, u32[]{:S(2)}) copy-start(bf16[128,2048]{1,0:T(8,128)(2,1)S(1)} %collective-permute-done.1.refs_0_) | copy-start | bytes 1572868
  25.1 2.6 %copy-start.13 = (bf16[128,2048]{1,0:T(8,128)(2,1)}, bf16[128,2048]{1,0:T(8,128)(2,1)S(1)}, u32[]{:S(2)}) copy-start(bf16[128,2048]{1,0:T(8,128)(2,1)S(1)} %collective-permute-done.4.refs_2_) | copy-start | bytes 1572868
  25.1 3.3 %collective-permute-start.7 = (bf16[128,2048]{1,0:T(8,128)(2,1)S(1)}, bf16[128,2048]{1,0:T(8,128)(2,1)}, u32[]{:S(2)}, u32[]{:S(2)}) collective-permute-start(bf16[128,2048]{1,0:T(8,128)(2,1)S(1)} %collective-permute-done.3.refs_1_), channel_id=1, source_target_pairs={{0,1},{1,0},{2,3},{3,2},{4,5},{5,4},{6,7},{7,6},{8,9},{9,8},{10,11... | collective-permute-start | bytes 1572872 | tf_op jit(solution)/shard_map/ppermute | solution.py:169
  25.2 16.5 %collective-permute-start.6 = (bf16[128,2048]{1,0:T(8,128)(2,1)S(1)}, bf16[128,2048]{1,0:T(8,128)(2,1)S(1)}, u32[]{:S(2)}, u32[]{:S(2)}) collective-permute-start(bf16[128,2048]{1,0:T(8,128)(2,1)S(1)} %collective-permute-done.1.refs_0_), channel_id=1, source_target_pairs={{0,1},{1,0},{2,3},{3,2},{4,5},{5,4},{6,7},{7,6},{8,9},{9,8},{10,11... | collective-permute-start | bytes 1572872 | tf_op jit(solution)/shard_map/ppermute | solution.py:169
  25.7 16.0 %collective-permute-start.5 = (bf16[128,2048]{1,0:T(8,128)(2,1)S(1)}, bf16[128,2048]{1,0:T(8,128)(2,1)S(1)}, u32[]{:S(2)}, u32[]{:S(2)}) collective-permute-start(bf16[128,2048]{1,0:T(8,128)(2,1)S(1)} %collective-permute-done.1.refs_0_), channel_id=1, source_target_pairs={{0,2},{1,3},{2,0},{3,1},{4,6},{5,7},{6,4},{7,5},{8,10},{9,11},{10,... | collective-permute-start | bytes 1572872 | tf_op jit(solution)/shard_map/ppermute | solution.py:169
  27.1 14.5 %collective-permute-start = (bf16[64,2048]{1,0:T(8,128)(2,1)S(1)}, bf16[64,2048]{1,0:T(8,128)(2,1)S(1)}, u32[]{:S(2)}, u32[]{:S(2)}) collective-permute-start(bf16[64,2048]{1,0:T(8,128)(2,1)S(1)} %get-tuple-element.105), channel_id=1, source_target_pairs={{0,8},{1,9},{2,10},{3,11},{4,12},{5,13},{6,14},{7,15},{8,0},{9,1},... | collective-permute-start | bytes 786440 | tf_op jit(solution)/shard_map/ppermute | solution.py:169
  41.7 2.3 %copy-start.11 = (bf16[128,2048]{1,0:T(8,128)(2,1)}, bf16[128,2048]{1,0:T(8,128)(2,1)S(1)}, u32[]{:S(2)}) copy-start(bf16[128,2048]{1,0:T(8,128)(2,1)S(1)} %collective-permute-done.6.refs_2_) | copy-start | bytes 1572868
  41.7 2.3 %copy-start.12 = (bf16[128,2048]{1,0:T(8,128)(2,1)}, bf16[128,2048]{1,0:T(8,128)(2,1)S(1)}, u32[]{:S(2)}) copy-start(bf16[128,2048]{1,0:T(8,128)(2,1)S(1)} %collective-permute-done.5.refs_1_) | copy-start | bytes 1572868
  41.7 2.3 %collective-permute-start.11 = (bf16[128,2048]{1,0:T(8,128)(2,1)S(1)}, bf16[128,2048]{1,0:T(8,128)(2,1)S(1)}, u32[]{:S(2)}, u32[]{:S(2)}) collective-permute-start(bf16[128,2048]{1,0:T(8,128)(2,1)S(1)} %collective-permute-done.5.refs_1_), channel_id=1, source_target_pairs={{0,1},{1,0},{2,3},{3,2},{4,5},{5,4},{6,7},{7,6},{8,9},{9,8},{10,11... | collective-permute-start | bytes 1572872 | tf_op jit(solution)/shard_map/ppermute | solution.py:169
  41.8 15.5 %copy-start.7 = (bf16[128,2048]{1,0:T(8,128)(2,1)}, bf16[128,2048]{1,0:T(8,128)(2,1)S(1)}, u32[]{:S(2)}) copy-start(bf16[128,2048]{1,0:T(8,128)(2,1)S(1)} %constant_dynamic-update-slice_fusion.refs_0_) | copy-start | bytes 1572868
  41.8 15.5 %collective-permute-start.10 = (bf16[128,2048]{1,0:T(8,128)(2,1)S(1)}, bf16[128,2048]{1,0:T(8,128)(2,1)S(1)}, u32[]{:S(2)}, u32[]{:S(2)}) collective-permute-start(bf16[128,2048]{1,0:T(8,128)(2,1)S(1)} %constant_dynamic-update-slice_fusion.refs_0_), channel_id=1, source_target_pairs={{0,1},{1,0},{2,3},{3,2},{4,5},{5,4},{6,7},{7,6},{8,9},{9,8},{10,11... | collective-permute-start | bytes 1572872 | tf_op jit(solution)/shard_map/ppermute | solution.py:169
  42.4 15.0 %collective-permute-start.9 = (bf16[128,2048]{1,0:T(8,128)(2,1)S(1)}, bf16[128,2048]{1,0:T(8,128)(2,1)S(1)}, u32[]{:S(2)}, u32[]{:S(2)}) collective-permute-start(bf16[128,2048]{1,0:T(8,128)(2,1)S(1)} %constant_dynamic-update-slice_fusion.refs_0_), channel_id=1, source_target_pairs={{0,2},{1,3},{2,0},{3,1},{4,6},{5,7},{6,4},{7,5},{8,10},{9,11},{10,... | collective-permute-start | bytes 1572872 | tf_op jit(solution)/shard_map/ppermute | solution.py:169
  43.0 14.5 %collective-permute-start.8 = (bf16[128,2048]{1,0:T(8,128)(2,1)S(1)}, bf16[128,2048]{1,0:T(8,128)(2,1)S(1)}, u32[]{:S(2)}, u32[]{:S(2)}) collective-permute-start(bf16[128,2048]{1,0:T(8,128)(2,1)S(1)} %constant_dynamic-update-slice_fusion.refs_0_), channel_id=1, source_target_pairs={{0,4},{1,5},{2,6},{3,7},{4,0},{5,1},{6,2},{7,3},{8,12},{9,13},{10,... | collective-permute-start | bytes 1572872 | tf_op jit(solution)/shard_map/ppermute | solution.py:169
  44.0 0.8 copy-start.16
  57.4 3.5 %copy-start.15 = (bf16[128,2048]{1,0:T(8,128)(2,1)}, bf16[128,2048]{1,0:T(8,128)(2,1)S(1)}, u32[]{:S(2)}) copy-start(bf16[128,2048]{1,0:T(8,128)(2,1)S(1)} %collective-permute-done.10.refs_2_) | copy-start | bytes 1572868
  57.4 3.5 %copy-start.6 = (bf16[128,2048]{1,0:T(8,128)(2,1)}, bf16[128,2048]{1,0:T(8,128)(2,1)S(1)}, u32[]{:S(2)}) copy-start(bf16[128,2048]{1,0:T(8,128)(2,1)S(1)} %collective-permute-done.9.refs_1_) | copy-start | bytes 1572868
  57.4 17.0 %copy-start.5 = (bf16[128,2048]{1,0:T(8,128)(2,1)}, bf16[128,2048]{1,0:T(8,128)(2,1)S(1)}, u32[]{:S(2)}) copy-start(bf16[128,2048]{1,0:T(8,128)(2,1)S(1)} %collective-permute-done.8.refs_0_) | copy-start | bytes 1572868
  57.4 17.1 %collective-permute-start.15 = (bf16[256,2048]{1,0:T(8,128)(2,1)}, bf16[256,2048]{1,0:T(8,128)(2,1)S(1)}, u32[]{:S(2)}, u32[]{:S(2)}) collective-permute-start(bf16[256,2048]{1,0:T(8,128)(2,1)} %get-tuple-element.69), channel_id=1, source_target_pairs={{0,1},{1,0},{2,3},{3,2},{4,5},{5,4},{6,7},{7,6},{8,9},{9,8},{10,11... | collective-permute-start | bytes 3145736 | tf_op jit(solution)/shard_map/ppermute | solution.py:169
  57.5 3.4 %collective-permute-start.16 = (bf16[128,2048]{1,0:T(8,128)(2,1)S(1)}, bf16[128,2048]{1,0:T(8,128)(2,1)S(1)}, u32[]{:S(2)}, u32[]{:S(2)}) collective-permute-start(bf16[128,2048]{1,0:T(8,128)(2,1)S(1)} %collective-permute-done.9.refs_1_), channel_id=1, source_target_pairs={{0,1},{1,0},{2,3},{3,2},{4,5},{5,4},{6,7},{7,6},{8,9},{9,8},{10,11... | collective-permute-start | bytes 1572872 | tf_op jit(solution)/shard_map/ppermute | solution.py:169
  58.0 16.5 %collective-permute-start.14 = (bf16[128,2048]{1,0:T(8,128)(2,1)S(1)}, bf16[128,2048]{1,0:T(8,128)(2,1)S(1)}, u32[]{:S(2)}, u32[]{:S(2)}) collective-permute-start(bf16[128,2048]{1,0:T(8,128)(2,1)S(1)} %collective-permute-done.8.refs_0_), channel_id=1, source_target_pairs={{0,1},{1,0},{2,3},{3,2},{4,5},{5,4},{6,7},{7,6},{8,9},{9,8},{10,11... | collective-permute-start | bytes 1572872 | tf_op jit(solution)/shard_map/ppermute | solution.py:169
  58.1 17.4 %copy-start.2 = (bf16[256,2048]{1,0:T(8,128)(2,1)S(1)}, bf16[256,2048]{1,0:T(8,128)(2,1)}, u32[]{:S(2)}) copy-start(bf16[256,2048]{1,0:T(8,128)(2,1)} %get-tuple-element.82) | copy-start | bytes 3145732
  58.2 16.3 %collective-permute-start.13 = (bf16[64,2048]{1,0:T(8,128)(2,1)S(1)}, bf16[64,2048]{1,0:T(8,128)(2,1)S(1)}, u32[]{:S(2)}, u32[]{:S(2)}) collective-permute-start(bf16[64,2048]{1,0:T(8,128)(2,1)S(1)} %slice.81), channel_id=1, source_target_pairs={{0,2},{1,3},{2,0},{3,1},{4,6},{5,7},{6,4},{7,5},{8,10},{9,11},{10,... | collective-permute-start | bytes 786440 | tf_op jit(solution)/shard_map/ppermute | solution.py:169
  59.6 14.9 %collective-permute-start.12 = (bf16[64,2048]{1,0:T(8,128)(2,1)S(1)}, bf16[64,2048]{1,0:T(8,128)(2,1)}, u32[]{:S(2)}, u32[]{:S(2)}) collective-permute-start(bf16[64,2048]{1,0:T(8,128)(2,1)S(1)} %slice.80), channel_id=1, source_target_pairs={{0,4},{1,5},{2,6},{3,7},{4,0},{5,1},{6,2},{7,3},{8,12},{9,13},{10,... | collective-permute-start | bytes 786440 | tf_op jit(solution)/shard_map/ppermute | solution.py:169
  60.9 0.8 copy-start.17
  74.5 3.7 %copy-start.18 = (bf16[64,2048]{1,0:T(8,128)(2,1)}, bf16[64,2048]{1,0:T(8,128)(2,1)S(1)}, u32[]{:S(2)}) copy-start(bf16[64,2048]{1,0:T(8,128)(2,1)S(1)} %collective-permute-done.13.refs_2_) | copy-start | bytes 786436
  74.5 0.9 copy-start.14
  74.5 17.7 %collective-permute-start.19 = (bf16[256,2048]{1,0:T(8,128)(2,1)}, bf16[256,2048]{1,0:T(8,128)(2,1)S(1)}, u32[]{:S(2)}, u32[]{:S(2)}) collective-permute-start(bf16[256,2048]{1,0:T(8,128)(2,1)} %get-tuple-element.81), channel_id=1, source_target_pairs={{0,1},{1,0},{2,3},{3,2},{4,5},{5,4},{6,7},{7,6},{8,9},{9,8},{10,11... | collective-permute-start | bytes 3145736 | tf_op jit(solution)/shard_map/ppermute | solution.py:169
  74.7 3.5 %collective-permute-start.17 = (bf16[64,2048]{1,0:T(8,128)(2,1)}, bf16[64,2048]{1,0:T(8,128)(2,1)S(1)}, u32[]{:S(2)}, u32[]{:S(2)}) collective-permute-start(bf16[64,2048]{1,0:T(8,128)(2,1)} %collective-permute-done.12.refs_1_), channel_id=1, source_target_pairs={{0,1},{1,0},{2,3},{3,2},{4,5},{5,4},{6,7},{7,6},{8,9},{9,8},{10,11... | collective-permute-start | bytes 786440 | tf_op jit(solution)/shard_map/ppermute | solution.py:169
  75.4 2.8 %collective-permute-start.18 = (bf16[64,2048]{1,0:T(8,128)(2,1)S(1)}, bf16[64,2048]{1,0:T(8,128)(2,1)S(1)}, u32[]{:S(2)}, u32[]{:S(2)}) collective-permute-start(bf16[64,2048]{1,0:T(8,128)(2,1)S(1)} %collective-permute-done.13.refs_2_), channel_id=1, source_target_pairs={{0,1},{1,0},{2,3},{3,2},{4,5},{5,4},{6,7},{7,6},{8,9},{9,8},{10,11... | collective-permute-start | bytes 786440 | tf_op jit(solution)/shard_map/ppermute | solution.py:169
  75.7 16.5 %collective-permute-start.20 = (bf16[128,2048]{1,0:T(8,128)(2,1)S(1)}, bf16[128,2048]{1,0:T(8,128)(2,1)S(1)}, u32[]{:S(2)}, u32[]{:S(2)}) collective-permute-start(bf16[128,2048]{1,0:T(8,128)(2,1)S(1)} %add_convert_fusion.4), channel_id=1, source_target_pairs={{0,2},{1,3},{2,0},{3,1},{4,6},{5,7},{6,4},{7,5},{8,10},{9,11},{10,... | collective-permute-start | bytes 1572872 | tf_op jit(solution)/shard_map/ppermute | solution.py:169
  77.1 16.0 %collective-permute-start.22 = (bf16[256,2048]{1,0:T(8,128)(2,1)}, bf16[256,2048]{1,0:T(8,128)(2,1)S(1)}, u32[]{:S(2)}, u32[]{:S(2)}) collective-permute-start(bf16[256,2048]{1,0:T(8,128)(2,1)} %get-tuple-element.87), channel_id=1, source_target_pairs={{0,1},{1,0},{2,3},{3,2},{4,5},{5,4},{6,7},{7,6},{8,9},{9,8},{10,11... | collective-permute-start | bytes 3145736 | tf_op jit(solution)/shard_map/ppermute | solution.py:169
  78.2 0.7 copy-start.19
  78.9 0.7 copy-start.20
  92.2 15.6 %copy-start = (bf16[256,2048]{1,0:T(8,128)(2,1)S(1)}, bf16[256,2048]{1,0:T(8,128)(2,1)}, u32[]{:S(2)}) copy-start(bf16[256,2048]{1,0:T(8,128)(2,1)} %get-tuple-element.92) | copy-start | bytes 3145732
  92.2 0.8 copy-start.3
  93.0 16.9 %copy-start.4 = (bf16[128,2048]{1,0:T(8,128)(2,1)S(1)}, bf16[128,2048]{1,0:T(8,128)(2,1)}, u32[]{:S(2)}) copy-start(bf16[128,2048]{1,0:T(8,128)(2,1)} %copy-done.3) | copy-start | bytes 1572868
  93.0 2.9 %collective-permute-start.21 = (bf16[256,2048]{1,0:T(8,128)(2,1)}, bf16[256,2048]{1,0:T(8,128)(2,1)S(1)}, u32[]{:S(2)}, u32[]{:S(2)}) collective-permute-start(bf16[256,2048]{1,0:T(8,128)(2,1)} %get-tuple-element.86), channel_id=1, source_target_pairs={{0,1},{1,0},{2,3},{3,2},{4,5},{5,4},{6,7},{7,6},{8,9},{9,8},{10,11... | collective-permute-start | bytes 3145736 | tf_op jit(solution)/shard_map/ppermute | solution.py:169
  97.2 8.4 %collective-permute-start.24 = (bf16[64,2048]{1,0:T(8,128)(2,1)S(1)}, bf16[64,2048]{1,0:T(8,128)(2,1)S(1)}, u32[]{:S(2)}, u32[]{:S(2)}) collective-permute-start(bf16[64,2048]{1,0:T(8,128)(2,1)S(1)} %get-tuple-element.103), channel_id=1, source_target_pairs={{0,2},{1,3},{2,0},{3,1},{4,6},{5,7},{6,4},{7,5},{8,10},{9,11},{10,... | collective-permute-start | bytes 786440 | tf_op jit(solution)/shard_map/ppermute | solution.py:169
  98.7 8.1 %collective-permute-start.23 = (bf16[64,2048]{1,0:T(8,128)(2,1)S(1)}, bf16[64,2048]{1,0:T(8,128)(2,1)S(1)}, u32[]{:S(2)}, u32[]{:S(2)}) collective-permute-start(bf16[64,2048]{1,0:T(8,128)(2,1)S(1)} %get-tuple-element.104), channel_id=1, source_target_pairs={{0,4},{1,5},{2,6},{3,7},{4,0},{5,1},{6,2},{7,3},{8,12},{9,13},{10,... | collective-permute-start | bytes 786440 | tf_op jit(solution)/shard_map/ppermute | solution.py:169
  107.8 3.1 %copy-start.1 = (bf16[256,2048]{1,0:T(8,128)(2,1)S(1)}, bf16[256,2048]{1,0:T(8,128)(2,1)}, u32[]{:S(2)}) copy-start(bf16[256,2048]{1,0:T(8,128)(2,1)} %get-tuple-element.85) | copy-start | bytes 3145732
  108.0 12.9 %collective-permute-start.26 = (bf16[128,2048]{1,0:T(8,128)(2,1)S(1)}, bf16[128,2048]{1,0:T(8,128)(2,1)S(1)}, u32[]{:S(2)}, u32[]{:S(2)}) collective-permute-start(bf16[128,2048]{1,0:T(8,128)(2,1)S(1)} %pad_maximum_fusion.1), channel_id=1, source_target_pairs={{0,2},{1,3},{2,0},{3,1},{4,6},{5,7},{6,4},{7,5},{8,10},{9,11},{10,... | collective-permute-start | bytes 1572872 | tf_op jit(solution)/shard_map/ppermute | solution.py:169
  108.8 17.2 %copy-start.8 = (f32[16,1,128]{2,1,0:T(1,128)S(1)}, f32[16,1,128]{2,1,0:T(1,128)}, u32[]{:S(2)}) copy-start(f32[16,1,128]{2,1,0:T(1,128)} %all_to_all.9) | copy-start | bytes 24580
  108.8 12.6 %collective-permute-start.25 = (bf16[128,2048]{1,0:T(8,128)(2,1)S(1)}, bf16[128,2048]{1,0:T(8,128)(2,1)S(1)}, u32[]{:S(2)}, u32[]{:S(2)}) collective-permute-start(bf16[128,2048]{1,0:T(8,128)(2,1)S(1)} %pad_maximum_fusion), channel_id=1, source_target_pairs={{0,4},{1,5},{2,6},{3,7},{4,0},{5,1},{6,2},{7,3},{8,12},{9,13},{10,... | collective-permute-start | bytes 1572872 | tf_op jit(solution)/shard_map/ppermute | solution.py:169
  121.4 11.7 %collective-permute-start.27 = (bf16[128,2048]{1,0:T(8,128)(2,1)S(1)}, bf16[128,2048]{1,0:T(8,128)(2,1)}, u32[]{:S(2)}, u32[]{:S(2)}) collective-permute-start(bf16[128,2048]{1,0:T(8,128)(2,1)S(1)} %add_convert_fusion.2), channel_id=1, source_target_pairs={{0,2},{1,3},{2,0},{3,1},{4,6},{5,7},{6,4},{7,5},{8,10},{9,11},{10,... | collective-permute-start | bytes 1572872 | tf_op jit(solution)/shard_map/ppermute | solution.py:169
  122.8 21.8 %collective-permute-start.28 = (bf16[128,2048]{1,0:T(8,128)(2,1)}, bf16[128,2048]{1,0:T(8,128)(2,1)}, u32[]{:S(2)}, u32[]{:S(2)}) collective-permute-start(bf16[128,2048]{1,0:T(8,128)(2,1)} %add_convert_fusion.3), channel_id=1, source_target_pairs={{0,4},{1,5},{2,6},{3,7},{4,0},{5,1},{6,2},{7,3},{8,12},{9,13},{10,... | collective-permute-start | bytes 1572872 | tf_op jit(solution)/shard_map/ppermute | solution.py:169
  124.2 23.4 %collective-permute-start.29 = (bf16[128,2048]{1,0:T(8,128)(2,1)S(1)}, bf16[128,2048]{1,0:T(8,128)(2,1)}, u32[]{:S(2)}, u32[]{:S(2)}) collective-permute-start(bf16[128,2048]{1,0:T(8,128)(2,1)S(1)} %add_convert_fusion.1), channel_id=1, source_target_pairs={{0,8},{1,9},{2,10},{3,11},{4,12},{5,13},{6,14},{7,15},{8,0},{9,1},... | collective-permute-start | bytes 1572872 | tf_op jit(solution)/shard_map/ppermute | solution.py:169

commit v8 on v7

--- a/solution.py
+++ b/solution.py
@@ -38,28 +38,33 @@
 def plane_kernel(capacity, k, parts, spots, weight, *refs):
     xs, refs = refs[:parts], refs[parts:]
     w_gate, w_up, w_down, keep, give, act_out = refs[:6]
-    x, rows, act, out, ranks, gates, ups, downs, x_sem, gate_sem, up_sem, down_sem, out_sem = refs[6:]
+    x, rows, act, gated, made, out, ranks, gates, ups, downs = refs[6:16]
+    x_sem, gate_sem, up_sem, down_sem, out_sem = refs[16:]
     blocks, tok = weight.shape
     slots, hidden = act.shape
-    tiles, features, wide = gates.shape
-    cuts, _, cut = downs.shape
+    features = x.shape[1]
+    wide, cut = 256, 512
     x_copies, at = [], 0
     for i, block in enumerate(xs):
         target = x.at[pl.ds(at, block.shape[0]), :]
         x_copies.append(pltpu.make_async_copy(block, target, x_sem.at[i]))
         at += block.shape[0]
-    loads = []
-    for i in range(tiles):
-        span = pl.ds(i * wide, wide)
-        loads.append(pltpu.make_async_copy(w_gate.at[:, span], gates.at[i], gate_sem.at[i]))
-        loads.append(pltpu.make_async_copy(w_up.at[:, span], ups.at[i], up_sem.at[i]))
-    for i in range(cuts):
-        span = pl.ds(i * cut, cut)
-        loads.append(pltpu.make_async_copy(w_down.at[:, span], downs.at[i], down_sem.at[i]))
-    for copy in x_copies:
+
+    def loads(source, target, sems):
+        count = sems.shape[0]
+        some = source.shape[0] // count
+        return [
+            pltpu.make_async_copy(
+                source.at[pl.ds(i * some, some), :], target.at[pl.ds(i * some, some), :], sems.at[i]
+            )
+            for i in range(count)
+        ]
+
+    gate_copies = loads(w_gate, gates, gate_sem)
+    up_copies = loads(w_up, ups, up_sem)
+    down_copies = loads(w_down, downs, down_sem)
+    for copy in x_copies + gate_copies:
         copy.start()
-    loads[0].start()
-    loads[1].start()
 
     named = (weight[...] >= 0.0).astype(jnp.float32)
     lane = lax.broadcasted_iota(jnp.int32, (tok, tok), 0)
@@ -84,36 +89,48 @@
     select = hits.astype(jnp.float32).astype(jnp.bfloat16)
     for copy in x_copies:
         copy.wait()
-    for load in loads[2 : 2 * tiles]:
-        load.start()
-    for i in range(cuts):
+    for copy in up_copies:
+        copy.start()
+    for i in range(features // cut):
         span = pl.ds(i * cut, cut)
         rows[:, span] = jnp.dot(
             select, x[:, span], preferred_element_type=jnp.float32
         ).astype(jnp.bfloat16)
-    for load in loads[2 * tiles :]:
-        load.start()
-    act_copy = pltpu.make_async_copy(act, act_out, out_sem.at[2 * cuts])
-    for i in range(tiles):
-        loads[2 * i].wait()
-        gate = jnp.dot(rows[...], gates[i], preferred_element_type=jnp.float32)
-        loads[2 * i + 1].wait()
-        up = jnp.dot(rows[...], ups[i], preferred_element_type=jnp.float32)
-        act[:, pl.ds(i * wide, wide)] = (gate / (1.0 + jnp.exp(-gate)) * up).astype(jnp.bfloat16)
+    for copy in gate_copies:
+        copy.wait()
+    for copy in down_copies:
+        copy.start()
+    for i in range(hidden // wide):
+        span = pl.ds(i * wide, wide)
+        gate = jnp.dot(rows[...], gates[:, span], preferred_element_type=jnp.float32)
+        gated[:, span] = gate / (1.0 + jnp.exp(-gate))
+    for copy in up_copies:
+        copy.wait()
+    for i in range(hidden // wide):
+        span = pl.ds(i * wide, wide)
+        up = jnp.dot(rows[...], ups[:, span], preferred_element_type=jnp.float32)
+        act[:, span] = (gated[:, span] * up).astype(jnp.bfloat16)
+    act_copy = pltpu.make_async_copy(act, act_out, out_sem.at[2])
     act_copy.start()
+    for copy in down_copies:
+        copy.wait()
+    for i in range(features // cut):
+        span = pl.ds(i * cut, cut)
+        result = jnp.dot(act[...], downs[:, span], preferred_element_type=jnp.float32)
+        made[:, span] = (result * scale).astype(jnp.bfloat16)
     back = select.T
     out_copies = []
-    for i in range(cuts):
-        span = pl.ds(i * cut, cut)
-        loads[2 * tiles + i].wait()
-        result = jnp.dot(act[...], downs[i], preferred_element_type=jnp.float32)
-        made = (result * scale).astype(jnp.bfloat16)
-        out[i] = jnp.dot(back, made, preferred_element_type=jnp.float32).astype(jnp.bfloat16)
-        for half, target in enumerate((keep, give)):
-            source = out.at[i, pl.ds(half * 2 * tok, 2 * tok), :]
-            copy = pltpu.make_async_copy(source, target.at[:, span], out_sem.at[2 * i + half])
-            copy.start()
-            out_copies.append(copy)
+    for half, target in ((1, give), (0, keep)):
+        for i in range(features // cut):
+            span = pl.ds(i * cut, cut)
+            out[half, :, span] = jnp.dot(
+                back[half * 2 * tok : (half + 1) * 2 * tok],
+                made[:, span],
+                preferred_element_type=jnp.float32,
+            ).astype(jnp.bfloat16)
+        copy = pltpu.make_async_copy(out.at[half], target, out_sem.at[half])
+        copy.start()
+        out_copies.append(copy)
     act_copy.wait()
     for copy in out_copies:
         copy.wait()
@@ -124,8 +141,6 @@
     hidden = w_gate.shape[1]
     half = jax.ShapeDtypeStruct((2 * tok, features), jnp.bfloat16)
     rows = 4 * slots
-    wide, cut = 256, 512
-    tiles, cuts = hidden // wide, features // cut
     flops = 2 * rows * (3 * features * hidden + 8 * tok * features)
     moved = 2 * (3 * features * hidden + 8 * tok * features)
     return pl.pallas_call(
@@ -138,16 +153,18 @@
             pltpu.VMEM((4 * tok, features), jnp.bfloat16),
             pltpu.VMEM((rows, features), jnp.bfloat16),
             pltpu.VMEM((rows, hidden), jnp.bfloat16),
-            pltpu.VMEM((cuts, 4 * tok, cut), jnp.bfloat16),
+            pltpu.VMEM((rows, hidden), jnp.float32),
+            pltpu.VMEM((rows, features), jnp.bfloat16),
+            pltpu.VMEM((2, 2 * tok, features), jnp.bfloat16),
             pltpu.VMEM(weight.shape, jnp.float32),
-            pltpu.VMEM((tiles, features, wide), jnp.bfloat16),
-            pltpu.VMEM((tiles, features, wide), jnp.bfloat16),
-            pltpu.VMEM((cuts, hidden, cut), jnp.bfloat16),
+            pltpu.VMEM((features, hidden), jnp.bfloat16),
+            pltpu.VMEM((features, hidden), jnp.bfloat16),
+            pltpu.VMEM((hidden, features), jnp.bfloat16),
             pltpu.SemaphoreType.DMA((len(xs),)),
-            pltpu.SemaphoreType.DMA((tiles,)),
-            pltpu.SemaphoreType.DMA((tiles,)),
-            pltpu.SemaphoreType.DMA((cuts,)),
-            pltpu.SemaphoreType.DMA((2 * cuts + 1,)),
+            pltpu.SemaphoreType.DMA((4,)),
+            pltpu.SemaphoreType.DMA((4,)),
+            pltpu.SemaphoreType.DMA((4,)),
+            pltpu.SemaphoreType.DMA((3,)),
         ],
         compiler_params=pltpu.CompilerParams(vmem_limit_bytes=58 * 1024 * 1024),
         cost_estimate=pl.CostEstimate(

time: 151 us -> 145 us (0.960)
  Pallas kernels: 50.4 us -> 41.7 us
  waiting for transfers between devices: 37.1 us -> 43.2 us
  starting transfers between devices: 26.2 us -> 23.2 us
    pallas_call x4, Pallas kernels: 50.4 us -> 41.7 us  [plane_pass(): pl.pallas_call(functools.partial(plane_kernel, capacity, k, len(xs)), out...]
    ppermute x30, waiting for transfers between devices: 37.1 us -> 43.2 us  [swapped(): return lax.ppermute(array, 'expert', [(i, i ^ bit) for i in range(size)])]
    ppermute x30, starting transfers between devices: 26.2 us -> 23.2 us  [swapped(): return lax.ppermute(array, 'expert', [(i, i ^ bit) for i in range(size)])]
  transfers between devices with their start and end apart: 30 -> 30, of which waited for: 11 -> 14; matrix products, arithmetic and copies ran while one was open for 7% -> 7% of each run, Pallas kernels for 34% -> 29%
where the time goes in v8:
time: 145 us
  waiting for transfers between devices  43.2 us (30%)
  Pallas kernels  41.7 us (29%)
  starting transfers between devices  23.2 us (16%)
  blocking collectives  14.6 us (10%)
  other arithmetic  8.89 us (6%)
  local copies, waits for them, and re-layouts  5.95 us (4%)
  matrix products  5.31 us (4%)
  between operations  1.7 us (1%)
    ppermute x30, waiting for transfers between devices, swapped(): return lax.ppermute(array, 'expert', [(i, i ^ bit) for i in range(size)])  43.2 us
    pallas_call x4, Pallas kernels, plane_pass(): pl.pallas_call(functools.partial(plane_kernel, capacity, k, len(xs)), out...  41.7 us
    ppermute x30, starting transfers between devices, swapped(): return lax.ppermute(array, 'expert', [(i, i ^ bit) for i in range(size)])  23.2 us
    all_to_all x1, blocking collectives, weights_for_me(): lax.all_to_all(mine, 'expert', split_axis=0, concat_axis=0, tiled=True)  14.6 us
    convert_element_type x8, other arithmetic, summed(): return total.astype(jnp.bfloat16)  6.77 us
    dot_general x1, matrix products, gram_of(): lax.dot_general(rows, rows, (((0,), (0,)), ((), ())), preferred_element_t...  5.31 us
    unnamed x43, local copies, waits for them, and re-layouts  4.14 us
  transfers between devices with their start and end apart: 30, of which 14 were waited for; matrix products, arithmetic and copies ran while one was open for 7% of the time, Pallas kernels for 29%

profile of v8, /device:TPU:0, one launch (start us, length us, event | category | flops | bytes accessed | tf_op | source)
XLA Modules:
  0.0 144.6 jit_solution(15174607253048341108)
XLA Ops:
  0.6 3.0 %collective-permute-start.3 = (bf16[128,2048]{1,0:T(8,128)(2,1)}, bf16[128,2048]{1,0:T(8,128)(2,1)S(1)}, u32[]{:S(2)}, u32[]{:S(2)}) collective-permute-start(bf16[128,2048]{1,0:T(8,128)(2,1)} %refs_0_.1), channel_id=1, source_target_pairs={{0,2},{1,3},{2,0},{3,1},{4,6},{5,7},{6,4},{7,5},{8,10},{9,11},{10,... | collective-permute-start | bytes 1572872 | tf_op jit(solution)/shard_map/ppermute | solution.py:186
  3.7 1.6 %collective-permute-start.1 = (bf16[128,2048]{1,0:T(8,128)(2,1)}, bf16[128,2048]{1,0:T(8,128)(2,1)S(1)}, u32[]{:S(2)}, u32[]{:S(2)}) collective-permute-start(bf16[128,2048]{1,0:T(8,128)(2,1)} %refs_0_.1), channel_id=1, source_target_pairs={{0,4},{1,5},{2,6},{3,7},{4,0},{5,1},{6,2},{7,3},{8,12},{9,13},{10,... | collective-permute-start | bytes 1572872 | tf_op jit(solution)/shard_map/ppermute | solution.py:186
  5.2 1.1 fusion.12
  6.3 2.7 %collective-permute-start.2 = (bf16[64,2048]{1,0:T(8,128)(2,1)S(1)}, bf16[64,2048]{1,0:T(8,128)(2,1)S(1)}, u32[]{:S(2)}, u32[]{:S(2)}) collective-permute-start(bf16[64,2048]{1,0:T(8,128)(2,1)S(1)} %get-tuple-element.106), channel_id=1, source_target_pairs={{0,8},{1,9},{2,10},{3,11},{4,12},{5,13},{6,14},{7,15},{8,0},{9,1},... | collective-permute-start | bytes 786440 | tf_op jit(solution)/shard_map/ppermute | solution.py:186
  9.0 0.7 select_reduce_fusion
  9.7 0.7 fusion.10
  10.4 14.6 %all_to_all.9 = f32[16,1,128]{2,1,0:T(1,128)} all-to-all(f32[16,1,128]{2,1,0:T(1,128)S(1)} %bitcast.32), channel_id=1, replica_groups=mesh['parts'=2,'expert'=16] {'expert'}, dimensions={0} | all-to-all | bytes 16384 | tf_op jit(solution)/shard_map/all_to_all | solution.py:28
  25.1 0.1 collective-permute-start.7
  25.2 0.5 collective-permute-start.6
  25.7 1.5 %collective-permute-start.5 = (bf16[128,2048]{1,0:T(8,128)(2,1)S(1)}, bf16[128,2048]{1,0:T(8,128)(2,1)S(1)}, u32[]{:S(2)}, u32[]{:S(2)}) collective-permute-start(bf16[128,2048]{1,0:T(8,128)(2,1)S(1)} %collective-permute-done.1.refs_0_), channel_id=1, source_target_pairs={{0,2},{1,3},{2,0},{3,1},{4,6},{5,7},{6,4},{7,5},{8,10},{9,11},{10,... | collective-permute-start | bytes 1572872 | tf_op jit(solution)/shard_map/ppermute | solution.py:186
  27.1 0.6 collective-permute-start
  27.7 0.7 stack.67.spots
  28.4 10.4 %shard_map.77 = (bf16[256,2048]{1,0:T(8,128)(2,1)}, bf16[256,2048]{1,0:T(8,128)(2,1)}, bf16[320,768]{1,0:T(8,128)(2,1)}) custom-call(s32[16]{0:T(128)} %stack.67.spots, f32[16,128]{1,0:T(8,128)} %bitcast.27, bf16[128,2048]{1,0:T(8,128)(2,1)} %refs_0_.1, bf16[128,2048]{1,0:T(8,128)(2,1)} %copy-done.10, bf16[128,2048]{1,0:T(8,128)(2,1)} %copy-done.13, ...), custom_call_target="tpu_custom_call" | custom-call | flops 4362076160 | bytes 13631488 | tf_op jit(solution)/shard_map/pallas_call | solution.py:146
  38.8 2.8 %collective-permute-done = bf16[64,2048]{1,0:T(8,128)(2,1)S(1)} collective-permute-done((bf16[64,2048]{1,0:T(8,128)(2,1)S(1)}, bf16[64,2048]{1,0:T(8,128)(2,1)S(1)}, u32[]{:S(2)}, u32[]{:S(2)}) %collective-permute-start) | collective-permute-done | bytes 262176 | tf_op jit(solution)/shard_map/ppermute | solution.py:186
  41.7 0.1 collective-permute-start.11
  41.8 0.6 collective-permute-start.10
  42.4 0.6 collective-permute-start.9
  43.0 0.7 collective-permute-done.11.refs_3_
  43.7 0.8 copy-done.16
  44.5 10.3 %shard_map.78 = (bf16[256,2048]{1,0:T(8,128)(2,1)}, bf16[256,2048]{1,0:T(8,128)(2,1)}, bf16[320,768]{1,0:T(8,128)(2,1)}) custom-call(s32[16]{0:T(128)} %stack.67.spots, f32[16,128]{1,0:T(8,128)} %bitcast.28, bf16[128,2048]{1,0:T(8,128)(2,1)} %copy-done.9, bf16[128,2048]{1,0:T(8,128)(2,1)} %copy-done.12, bf16[128,2048]{1,0:T(8,128)(2,1)} %copy-done.11, ...), custom_call_target="tpu_custom_call" | custom-call | flops 4362076160 | bytes 13631488 | tf_op jit(solution)/shard_map/pallas_call | solution.py:146
  54.9 1.4 collective-permute-done.9.refs_1_
  56.3 0.3 collective-permute-done.8.refs_0_
  56.6 0.5 collective-permute-start.16
  57.2 1.5 %collective-permute-start.13 = (bf16[64,2048]{1,0:T(8,128)(2,1)S(1)}, bf16[64,2048]{1,0:T(8,128)(2,1)S(1)}, u32[]{:S(2)}, u32[]{:S(2)}) collective-permute-start(bf16[64,2048]{1,0:T(8,128)(2,1)S(1)} %slice.81), channel_id=1, source_target_pairs={{0,2},{1,3},{2,0},{3,1},{4,6},{5,7},{6,4},{7,5},{8,10},{9,11},{10,... | collective-permute-start | bytes 786440 | tf_op jit(solution)/shard_map/ppermute | solution.py:186
  58.7 0.3 collective-permute-start.12
  59.0 0.6 collective-permute-done.16.refs_3_
  59.6 0.8 copy-done.17
  60.4 10.5 %shard_map.79 = (bf16[256,2048]{1,0:T(8,128)(2,1)}, bf16[256,2048]{1,0:T(8,128)(2,1)}, bf16[320,768]{1,0:T(8,128)(2,1)}) custom-call(s32[16]{0:T(128)} %stack.67.spots, f32[16,128]{1,0:T(8,128)} %bitcast.29, bf16[128,2048]{1,0:T(8,128)(2,1)} %copy-done.7, bf16[128,2048]{1,0:T(8,128)(2,1)} %copy-done.6, bf16[128,2048]{1,0:T(8,128)(2,1)} %copy-done.15, ...), custom_call_target="tpu_custom_call" | custom-call | flops 4362076160 | bytes 13631488 | tf_op jit(solution)/shard_map/pallas_call | solution.py:146
  71.0 0.4 collective-permute-start.19
  71.4 0.1 collective-permute-start.17
  71.6 0.3 copy-done.14
  71.9 0.4 collective-permute-start.18
  72.3 0.1 add_convert_fusion.4
  72.4 1.5 %collective-permute-start.20 = (bf16[128,2048]{1,0:T(8,128)(2,1)S(1)}, bf16[128,2048]{1,0:T(8,128)(2,1)S(1)}, u32[]{:S(2)}, u32[]{:S(2)}) collective-permute-start(bf16[128,2048]{1,0:T(8,128)(2,1)S(1)} %add_convert_fusion.4), channel_id=1, source_target_pairs={{0,2},{1,3},{2,0},{3,1},{4,6},{5,7},{6,4},{7,5},{8,10},{9,11},{10,... | collective-permute-start | bytes 1572872 | tf_op jit(solution)/shard_map/ppermute | solution.py:186
  73.9 0.8 collective-permute-done.17.refs_4_
  74.7 0.7 copy-done.19
  75.4 0.7 copy-done.20
  76.1 10.5 %shard_map.80 = (bf16[256,2048]{1,0:T(8,128)(2,1)}, bf16[256,2048]{1,0:T(8,128)(2,1)}, bf16[320,768]{1,0:T(8,128)(2,1)}) custom-call(s32[16]{0:T(128)} %stack.67.spots, f32[16,128]{1,0:T(8,128)} %bitcast.30, bf16[128,2048]{1,0:T(8,128)(2,1)} %copy-done.5, bf16[64,2048]{1,0:T(8,128)(2,1)} %collective-permute-done.12.refs_1_, bf16[64,2048]{1,0:T(8,128)(2,1)} %copy-done.18, ...), custom_call_target="tpu_custom_call" | custom-call | flops 4362076160 | bytes 13631488 | tf_op jit(solution)/shard_map/pallas_call | solution.py:146
  86.7 0.8 copy-done.3
  87.4 0.4 collective-permute-start.21
  87.8 2.5 %collective-permute-done.21 = bf16[256,2048]{1,0:T(8,128)(2,1)S(1)} collective-permute-done((bf16[256,2048]{1,0:T(8,128)(2,1)}, bf16[256,2048]{1,0:T(8,128)(2,1)S(1)}, u32[]{:S(2)}, u32[]{:S(2)}) %collective-permute-start.21) | collective-permute-done | bytes 1048608 | tf_op jit(solution)/shard_map/ppermute | solution.py:186
  90.3 1.4 add_convert_fusion.10
  91.7 1.5 %collective-permute-start.24 = (bf16[64,2048]{1,0:T(8,128)(2,1)S(1)}, bf16[64,2048]{1,0:T(8,128)(2,1)S(1)}, u32[]{:S(2)}, u32[]{:S(2)}) collective-permute-start(bf16[64,2048]{1,0:T(8,128)(2,1)S(1)} %get-tuple-element.103), channel_id=1, source_target_pairs={{0,2},{1,3},{2,0},{3,1},{4,6},{5,7},{6,4},{7,5},{8,10},{9,11},{10,... | collective-permute-start | bytes 786440 | tf_op jit(solution)/shard_map/ppermute | solution.py:186
  93.2 0.3 collective-permute-start.23
  93.5 6.8 %collective-permute-done.24 = bf16[64,2048]{1,0:T(8,128)(2,1)S(1)} collective-permute-done((bf16[64,2048]{1,0:T(8,128)(2,1)S(1)}, bf16[64,2048]{1,0:T(8,128)(2,1)S(1)}, u32[]{:S(2)}, u32[]{:S(2)}) %collective-permute-start.24) | collective-permute-done | bytes 262176 | tf_op jit(solution)/shard_map/ppermute | solution.py:186
  100.3 1.2 collective-permute-done.23
  101.5 1.0 add_convert_fusion.7
  102.6 0.2 add_convert_fusion.6
  102.8 0.6 collective-permute-start.26
  103.5 0.9 collective-permute-start.25
  104.4 1.0 add_convert_fusion.3
  105.5 0.1 add_convert_fusion.2
  105.6 10.3 %collective-permute-done.26 = bf16[128,2048]{1,0:T(8,128)(2,1)S(1)} collective-permute-done((bf16[128,2048]{1,0:T(8,128)(2,1)S(1)}, bf16[128,2048]{1,0:T(8,128)(2,1)S(1)}, u32[]{:S(2)}, u32[]{:S(2)}) %collective-permute-start.26) | collective-permute-done | bytes 524320 | tf_op jit(solution)/shard_map/ppermute | solution.py:186
  115.9 0.4 collective-permute-done.25
  116.4 1.4 collective-permute-start.27
  117.8 0.3 collective-permute-start.28
  118.1 0.3 add_convert_fusion.1
  118.4 1.8 %collective-permute-start.29 = (bf16[128,2048]{1,0:T(8,128)(2,1)S(1)}, bf16[128,2048]{1,0:T(8,128)(2,1)}, u32[]{:S(2)}, u32[]{:S(2)}) collective-permute-start(bf16[128,2048]{1,0:T(8,128)(2,1)S(1)} %add_convert_fusion.1), channel_id=1, source_target_pairs={{0,8},{1,9},{2,10},{3,11},{4,12},{5,13},{6,14},{7,15},{8,0},{9,1},... | collective-permute-start | bytes 1572872 | tf_op jit(solution)/shard_map/ppermute | solution.py:186
  120.3 0.6 convert_reduce_fusion
  121.5 5.3 %multiply_bitcast_fusion = f32[1,768,768]{2,1,0:T(8,128)} fusion(f32[]{:T(128)S(6)} %div.24, bf16[320,768]{1,0:T(8,128)(2,1)} %get-tuple-element.84, bf16[320,768]{1,0:T(8,128)(2,1)} %get-tuple-element.74, bf16[320,768]{1,0:T(8,128)(2,1)} %get-tuple-element.66, bf16[320,768]{1,0:T(8,128)(2,1)} %get-tuple-element.58), kind=kOutput, calls=%fused_computation | convolution fusion | flops 1518403584 | bytes 4325380 | tf_op jit(solution)/shard_map/dot_general | solution.py:12
  126.9 1.5 %collective-permute-done.27 = bf16[128,2048]{1,0:T(8,128)(2,1)} collective-permute-done((bf16[128,2048]{1,0:T(8,128)(2,1)S(1)}, bf16[128,2048]{1,0:T(8,128)(2,1)}, u32[]{:S(2)}, u32[]{:S(2)}) %collective-permute-start.27) | collective-permute-done | bytes 524320 | tf_op jit(solution)/shard_map/ppermute | solution.py:186
  128.4 11.3 %collective-permute-done.28 = bf16[128,2048]{1,0:T(8,128)(2,1)} collective-permute-done((bf16[128,2048]{1,0:T(8,128)(2,1)}, bf16[128,2048]{1,0:T(8,128)(2,1)}, u32[]{:S(2)}, u32[]{:S(2)}) %collective-permute-start.28) | collective-permute-done | bytes 524320 | tf_op jit(solution)/shard_map/ppermute | solution.py:186
  139.6 2.4 %collective-permute-done.29 = bf16[128,2048]{1,0:T(8,128)(2,1)} collective-permute-done((bf16[128,2048]{1,0:T(8,128)(2,1)S(1)}, bf16[128,2048]{1,0:T(8,128)(2,1)}, u32[]{:S(2)}, u32[]{:S(2)}) %collective-permute-start.29) | collective-permute-done | bytes 524320 | tf_op jit(solution)/shard_map/ppermute | solution.py:186
  142.1 2.6 %add_convert_fusion = bf16[128,2048]{1,0:T(8,128)(2,1)} fusion(bf16[128,2048]{1,0:T(8,128)(2,1)} %collective-permute-done.29, bf16[128,2048]{1,0:T(8,128)(2,1)} %collective-permute-done.28, bf16[128,2048]{1,0:T(8,128)(2,1)} %collective-permute-done.27, bf16[256,2048]{1,0:T(8,128)(2,1)S(1)} %collective-permute-done.22, bf16[256,2048]{1,0:T(8,128)(2,1)S(1)} %copy-done.1), kind=kLoop, calls=%fused_computation.9 | loop fusion | flops 2621440 | bytes 3145728 | tf_op jit(solution)/shard_map/convert_element_type | solution.py:35
  (64 shorter events, 0.3 us)
Async XLA Ops:
  0.6 24.4 %collective-permute-start.3 = (bf16[128,2048]{1,0:T(8,128)(2,1)}, bf16[128,2048]{1,0:T(8,128)(2,1)S(1)}, u32[]{:S(2)}, u32[]{:S(2)}) collective-permute-start(bf16[128,2048]{1,0:T(8,128)(2,1)} %refs_0_.1), channel_id=1, source_target_pairs={{0,2},{1,3},{2,0},{3,1},{4,6},{5,7},{6,4},{7,5},{8,10},{9,11},{10,... | collective-permute-start | bytes 1572872 | tf_op jit(solution)/shard_map/ppermute | solution.py:186
  3.7 21.4 %collective-permute-start.1 = (bf16[128,2048]{1,0:T(8,128)(2,1)}, bf16[128,2048]{1,0:T(8,128)(2,1)S(1)}, u32[]{:S(2)}, u32[]{:S(2)}) collective-permute-start(bf16[128,2048]{1,0:T(8,128)(2,1)} %refs_0_.1), channel_id=1, source_target_pairs={{0,4},{1,5},{2,6},{3,7},{4,0},{5,1},{6,2},{7,3},{8,12},{9,13},{10,... | collective-permute-start | bytes 1572872 | tf_op jit(solution)/shard_map/ppermute | solution.py:186
  5.2 19.8 %collective-permute-start.4 = (bf16[128,2048]{1,0:T(8,128)(2,1)}, bf16[128,2048]{1,0:T(8,128)(2,1)S(1)}, u32[]{:S(2)}, u32[]{:S(2)}) collective-permute-start(bf16[128,2048]{1,0:T(8,128)(2,1)} %refs_0_.1), channel_id=1, source_target_pairs={{0,1},{1,0},{2,3},{3,2},{4,5},{5,4},{6,7},{7,6},{8,9},{9,8},{10,11... | collective-permute-start | bytes 1572872 | tf_op jit(solution)/shard_map/ppermute | solution.py:186
  6.3 18.7 %collective-permute-start.2 = (bf16[64,2048]{1,0:T(8,128)(2,1)S(1)}, bf16[64,2048]{1,0:T(8,128)(2,1)S(1)}, u32[]{:S(2)}, u32[]{:S(2)}) collective-permute-start(bf16[64,2048]{1,0:T(8,128)(2,1)S(1)} %get-tuple-element.106), channel_id=1, source_target_pairs={{0,8},{1,9},{2,10},{3,11},{4,12},{5,13},{6,14},{7,15},{8,0},{9,1},... | collective-permute-start | bytes 786440 | tf_op jit(solution)/shard_map/ppermute | solution.py:186
  25.1 3.4 %copy-start.10 = (bf16[128,2048]{1,0:T(8,128)(2,1)}, bf16[128,2048]{1,0:T(8,128)(2,1)S(1)}, u32[]{:S(2)}) copy-start(bf16[128,2048]{1,0:T(8,128)(2,1)S(1)} %collective-permute-done.3.refs_1_) | copy-start | bytes 1572868
  25.1 13.8 %copy-start.9 = (bf16[128,2048]{1,0:T(8,128)(2,1)}, bf16[128,2048]{1,0:T(8,128)(2,1)S(1)}, u32[]{:S(2)}) copy-start(bf16[128,2048]{1,0:T(8,128)(2,1)S(1)} %collective-permute-done.1.refs_0_) | copy-start | bytes 1572868
  25.1 2.6 %copy-start.13 = (bf16[128,2048]{1,0:T(8,128)(2,1)}, bf16[128,2048]{1,0:T(8,128)(2,1)S(1)}, u32[]{:S(2)}) copy-start(bf16[128,2048]{1,0:T(8,128)(2,1)S(1)} %collective-permute-done.4.refs_2_) | copy-start | bytes 1572868
  25.1 3.3 %collective-permute-start.7 = (bf16[128,2048]{1,0:T(8,128)(2,1)S(1)}, bf16[128,2048]{1,0:T(8,128)(2,1)}, u32[]{:S(2)}, u32[]{:S(2)}) collective-permute-start(bf16[128,2048]{1,0:T(8,128)(2,1)S(1)} %collective-permute-done.3.refs_1_), channel_id=1, source_target_pairs={{0,1},{1,0},{2,3},{3,2},{4,5},{5,4},{6,7},{7,6},{8,9},{9,8},{10,11... | collective-permute-start | bytes 1572872 | tf_op jit(solution)/shard_map/ppermute | solution.py:186
  25.2 16.5 %collective-permute-start.6 = (bf16[128,2048]{1,0:T(8,128)(2,1)S(1)}, bf16[128,2048]{1,0:T(8,128)(2,1)S(1)}, u32[]{:S(2)}, u32[]{:S(2)}) collective-permute-start(bf16[128,2048]{1,0:T(8,128)(2,1)S(1)} %collective-permute-done.1.refs_0_), channel_id=1, source_target_pairs={{0,1},{1,0},{2,3},{3,2},{4,5},{5,4},{6,7},{7,6},{8,9},{9,8},{10,11... | collective-permute-start | bytes 1572872 | tf_op jit(solution)/shard_map/ppermute | solution.py:186
  25.7 16.0 %collective-permute-start.5 = (bf16[128,2048]{1,0:T(8,128)(2,1)S(1)}, bf16[128,2048]{1,0:T(8,128)(2,1)S(1)}, u32[]{:S(2)}, u32[]{:S(2)}) collective-permute-start(bf16[128,2048]{1,0:T(8,128)(2,1)S(1)} %collective-permute-done.1.refs_0_), channel_id=1, source_target_pairs={{0,2},{1,3},{2,0},{3,1},{4,6},{5,7},{6,4},{7,5},{8,10},{9,11},{10,... | collective-permute-start | bytes 1572872 | tf_op jit(solution)/shard_map/ppermute | solution.py:186
  27.1 14.5 %collective-permute-start = (bf16[64,2048]{1,0:T(8,128)(2,1)S(1)}, bf16[64,2048]{1,0:T(8,128)(2,1)S(1)}, u32[]{:S(2)}, u32[]{:S(2)}) collective-permute-start(bf16[64,2048]{1,0:T(8,128)(2,1)S(1)} %get-tuple-element.105), channel_id=1, source_target_pairs={{0,8},{1,9},{2,10},{3,11},{4,12},{5,13},{6,14},{7,15},{8,0},{9,1},... | collective-permute-start | bytes 786440 | tf_op jit(solution)/shard_map/ppermute | solution.py:186
  41.7 2.0 %copy-start.11 = (bf16[128,2048]{1,0:T(8,128)(2,1)}, bf16[128,2048]{1,0:T(8,128)(2,1)S(1)}, u32[]{:S(2)}) copy-start(bf16[128,2048]{1,0:T(8,128)(2,1)S(1)} %collective-permute-done.6.refs_2_) | copy-start | bytes 1572868
  41.7 2.0 %copy-start.12 = (bf16[128,2048]{1,0:T(8,128)(2,1)}, bf16[128,2048]{1,0:T(8,128)(2,1)S(1)}, u32[]{:S(2)}) copy-start(bf16[128,2048]{1,0:T(8,128)(2,1)S(1)} %collective-permute-done.5.refs_1_) | copy-start | bytes 1572868
  41.7 2.0 %collective-permute-start.11 = (bf16[128,2048]{1,0:T(8,128)(2,1)S(1)}, bf16[128,2048]{1,0:T(8,128)(2,1)S(1)}, u32[]{:S(2)}, u32[]{:S(2)}) collective-permute-start(bf16[128,2048]{1,0:T(8,128)(2,1)S(1)} %collective-permute-done.5.refs_1_), channel_id=1, source_target_pairs={{0,1},{1,0},{2,3},{3,2},{4,5},{5,4},{6,7},{7,6},{8,9},{9,8},{10,11... | collective-permute-start | bytes 1572872 | tf_op jit(solution)/shard_map/ppermute | solution.py:186
  41.8 13.0 %copy-start.7 = (bf16[128,2048]{1,0:T(8,128)(2,1)}, bf16[128,2048]{1,0:T(8,128)(2,1)S(1)}, u32[]{:S(2)}) copy-start(bf16[128,2048]{1,0:T(8,128)(2,1)S(1)} %constant_dynamic-update-slice_fusion.refs_0_) | copy-start | bytes 1572868
  41.8 13.0 %collective-permute-start.10 = (bf16[128,2048]{1,0:T(8,128)(2,1)S(1)}, bf16[128,2048]{1,0:T(8,128)(2,1)S(1)}, u32[]{:S(2)}, u32[]{:S(2)}) collective-permute-start(bf16[128,2048]{1,0:T(8,128)(2,1)S(1)} %constant_dynamic-update-slice_fusion.refs_0_), channel_id=1, source_target_pairs={{0,1},{1,0},{2,3},{3,2},{4,5},{5,4},{6,7},{7,6},{8,9},{9,8},{10,11... | collective-permute-start | bytes 1572872 | tf_op jit(solution)/shard_map/ppermute | solution.py:186
  42.4 13.9 %collective-permute-start.9 = (bf16[128,2048]{1,0:T(8,128)(2,1)S(1)}, bf16[128,2048]{1,0:T(8,128)(2,1)S(1)}, u32[]{:S(2)}, u32[]{:S(2)}) collective-permute-start(bf16[128,2048]{1,0:T(8,128)(2,1)S(1)} %constant_dynamic-update-slice_fusion.refs_0_), channel_id=1, source_target_pairs={{0,2},{1,3},{2,0},{3,1},{4,6},{5,7},{6,4},{7,5},{8,10},{9,11},{10,... | collective-permute-start | bytes 1572872 | tf_op jit(solution)/shard_map/ppermute | solution.py:186
  43.0 13.6 %collective-permute-start.8 = (bf16[128,2048]{1,0:T(8,128)(2,1)S(1)}, bf16[128,2048]{1,0:T(8,128)(2,1)S(1)}, u32[]{:S(2)}, u32[]{:S(2)}) collective-permute-start(bf16[128,2048]{1,0:T(8,128)(2,1)S(1)} %constant_dynamic-update-slice_fusion.refs_0_), channel_id=1, source_target_pairs={{0,4},{1,5},{2,6},{3,7},{4,0},{5,1},{6,2},{7,3},{8,12},{9,13},{10,... | collective-permute-start | bytes 1572872 | tf_op jit(solution)/shard_map/ppermute | solution.py:186
  43.7 0.8 copy-start.16
  54.9 4.8 %copy-start.15 = (bf16[128,2048]{1,0:T(8,128)(2,1)}, bf16[128,2048]{1,0:T(8,128)(2,1)S(1)}, u32[]{:S(2)}) copy-start(bf16[128,2048]{1,0:T(8,128)(2,1)S(1)} %collective-permute-done.10.refs_2_) | copy-start | bytes 1572868
  56.3 3.3 %copy-start.6 = (bf16[128,2048]{1,0:T(8,128)(2,1)}, bf16[128,2048]{1,0:T(8,128)(2,1)S(1)}, u32[]{:S(2)}) copy-start(bf16[128,2048]{1,0:T(8,128)(2,1)S(1)} %collective-permute-done.9.refs_1_) | copy-start | bytes 1572868
  56.6 14.4 %copy-start.5 = (bf16[128,2048]{1,0:T(8,128)(2,1)}, bf16[128,2048]{1,0:T(8,128)(2,1)S(1)}, u32[]{:S(2)}) copy-start(bf16[128,2048]{1,0:T(8,128)(2,1)S(1)} %collective-permute-done.8.refs_0_) | copy-start | bytes 1572868
  56.6 14.4 %collective-permute-start.15 = (bf16[256,2048]{1,0:T(8,128)(2,1)}, bf16[256,2048]{1,0:T(8,128)(2,1)S(1)}, u32[]{:S(2)}, u32[]{:S(2)}) collective-permute-start(bf16[256,2048]{1,0:T(8,128)(2,1)} %get-tuple-element.69), channel_id=1, source_target_pairs={{0,1},{1,0},{2,3},{3,2},{4,5},{5,4},{6,7},{7,6},{8,9},{9,8},{10,11... | collective-permute-start | bytes 3145736 | tf_op jit(solution)/shard_map/ppermute | solution.py:186
  56.6 3.0 %collective-permute-start.16 = (bf16[128,2048]{1,0:T(8,128)(2,1)S(1)}, bf16[128,2048]{1,0:T(8,128)(2,1)S(1)}, u32[]{:S(2)}, u32[]{:S(2)}) collective-permute-start(bf16[128,2048]{1,0:T(8,128)(2,1)S(1)} %collective-permute-done.9.refs_1_), channel_id=1, source_target_pairs={{0,1},{1,0},{2,3},{3,2},{4,5},{5,4},{6,7},{7,6},{8,9},{9,8},{10,11... | collective-permute-start | bytes 1572872 | tf_op jit(solution)/shard_map/ppermute | solution.py:186
  57.1 13.9 %collective-permute-start.14 = (bf16[128,2048]{1,0:T(8,128)(2,1)S(1)}, bf16[128,2048]{1,0:T(8,128)(2,1)S(1)}, u32[]{:S(2)}, u32[]{:S(2)}) collective-permute-start(bf16[128,2048]{1,0:T(8,128)(2,1)S(1)} %collective-permute-done.8.refs_0_), channel_id=1, source_target_pairs={{0,1},{1,0},{2,3},{3,2},{4,5},{5,4},{6,7},{7,6},{8,9},{9,8},{10,11... | collective-permute-start | bytes 1572872 | tf_op jit(solution)/shard_map/ppermute | solution.py:186
  57.1 15.1 %copy-start.2 = (bf16[256,2048]{1,0:T(8,128)(2,1)S(1)}, bf16[256,2048]{1,0:T(8,128)(2,1)}, u32[]{:S(2)}) copy-start(bf16[256,2048]{1,0:T(8,128)(2,1)} %get-tuple-element.82) | copy-start | bytes 3145732
  57.2 13.8 %collective-permute-start.13 = (bf16[64,2048]{1,0:T(8,128)(2,1)S(1)}, bf16[64,2048]{1,0:T(8,128)(2,1)S(1)}, u32[]{:S(2)}, u32[]{:S(2)}) collective-permute-start(bf16[64,2048]{1,0:T(8,128)(2,1)S(1)} %slice.81), channel_id=1, source_target_pairs={{0,2},{1,3},{2,0},{3,1},{4,6},{5,7},{6,4},{7,5},{8,10},{9,11},{10,... | collective-permute-start | bytes 786440 | tf_op jit(solution)/shard_map/ppermute | solution.py:186
  58.7 12.3 %collective-permute-start.12 = (bf16[64,2048]{1,0:T(8,128)(2,1)S(1)}, bf16[64,2048]{1,0:T(8,128)(2,1)}, u32[]{:S(2)}, u32[]{:S(2)}) collective-permute-start(bf16[64,2048]{1,0:T(8,128)(2,1)S(1)} %slice.80), channel_id=1, source_target_pairs={{0,4},{1,5},{2,6},{3,7},{4,0},{5,1},{6,2},{7,3},{8,12},{9,13},{10,... | collective-permute-start | bytes 786440 | tf_op jit(solution)/shard_map/ppermute | solution.py:186
  59.6 0.8 copy-start.17
  71.0 3.7 %copy-start.18 = (bf16[64,2048]{1,0:T(8,128)(2,1)}, bf16[64,2048]{1,0:T(8,128)(2,1)S(1)}, u32[]{:S(2)}) copy-start(bf16[64,2048]{1,0:T(8,128)(2,1)S(1)} %collective-permute-done.13.refs_2_) | copy-start | bytes 786436
  71.0 0.9 copy-start.14
  71.0 15.7 %collective-permute-start.19 = (bf16[256,2048]{1,0:T(8,128)(2,1)}, bf16[256,2048]{1,0:T(8,128)(2,1)S(1)}, u32[]{:S(2)}, u32[]{:S(2)}) collective-permute-start(bf16[256,2048]{1,0:T(8,128)(2,1)} %get-tuple-element.81), channel_id=1, source_target_pairs={{0,1},{1,0},{2,3},{3,2},{4,5},{5,4},{6,7},{7,6},{8,9},{9,8},{10,11... | collective-permute-start | bytes 3145736 | tf_op jit(solution)/shard_map/ppermute | solution.py:186
  71.4 3.3 %collective-permute-start.17 = (bf16[64,2048]{1,0:T(8,128)(2,1)}, bf16[64,2048]{1,0:T(8,128)(2,1)S(1)}, u32[]{:S(2)}, u32[]{:S(2)}) collective-permute-start(bf16[64,2048]{1,0:T(8,128)(2,1)} %collective-permute-done.12.refs_1_), channel_id=1, source_target_pairs={{0,1},{1,0},{2,3},{3,2},{4,5},{5,4},{6,7},{7,6},{8,9},{9,8},{10,11... | collective-permute-start | bytes 786440 | tf_op jit(solution)/shard_map/ppermute | solution.py:186
  71.9 2.8 %collective-permute-start.18 = (bf16[64,2048]{1,0:T(8,128)(2,1)S(1)}, bf16[64,2048]{1,0:T(8,128)(2,1)S(1)}, u32[]{:S(2)}, u32[]{:S(2)}) collective-permute-start(bf16[64,2048]{1,0:T(8,128)(2,1)S(1)} %collective-permute-done.13.refs_2_), channel_id=1, source_target_pairs={{0,1},{1,0},{2,3},{3,2},{4,5},{5,4},{6,7},{7,6},{8,9},{9,8},{10,11... | collective-permute-start | bytes 786440 | tf_op jit(solution)/shard_map/ppermute | solution.py:186
  72.4 14.2 %collective-permute-start.20 = (bf16[128,2048]{1,0:T(8,128)(2,1)S(1)}, bf16[128,2048]{1,0:T(8,128)(2,1)S(1)}, u32[]{:S(2)}, u32[]{:S(2)}) collective-permute-start(bf16[128,2048]{1,0:T(8,128)(2,1)S(1)} %add_convert_fusion.4), channel_id=1, source_target_pairs={{0,2},{1,3},{2,0},{3,1},{4,6},{5,7},{6,4},{7,5},{8,10},{9,11},{10,... | collective-permute-start | bytes 1572872 | tf_op jit(solution)/shard_map/ppermute | solution.py:186
  73.9 13.9 %collective-permute-start.22 = (bf16[256,2048]{1,0:T(8,128)(2,1)}, bf16[256,2048]{1,0:T(8,128)(2,1)S(1)}, u32[]{:S(2)}, u32[]{:S(2)}) collective-permute-start(bf16[256,2048]{1,0:T(8,128)(2,1)} %get-tuple-element.87), channel_id=1, source_target_pairs={{0,1},{1,0},{2,3},{3,2},{4,5},{5,4},{6,7},{7,6},{8,9},{9,8},{10,11... | collective-permute-start | bytes 3145736 | tf_op jit(solution)/shard_map/ppermute | solution.py:186
  74.7 0.7 copy-start.19
  75.4 0.7 copy-start.20
  86.6 15.9 %copy-start = (bf16[256,2048]{1,0:T(8,128)(2,1)S(1)}, bf16[256,2048]{1,0:T(8,128)(2,1)}, u32[]{:S(2)}) copy-start(bf16[256,2048]{1,0:T(8,128)(2,1)} %get-tuple-element.92) | copy-start | bytes 3145732
  86.6 0.8 copy-start.3
  87.4 17.0 %copy-start.4 = (bf16[128,2048]{1,0:T(8,128)(2,1)S(1)}, bf16[128,2048]{1,0:T(8,128)(2,1)}, u32[]{:S(2)}) copy-start(bf16[128,2048]{1,0:T(8,128)(2,1)} %copy-done.3) | copy-start | bytes 1572868
  87.4 2.9 %collective-permute-start.21 = (bf16[256,2048]{1,0:T(8,128)(2,1)}, bf16[256,2048]{1,0:T(8,128)(2,1)S(1)}, u32[]{:S(2)}, u32[]{:S(2)}) collective-permute-start(bf16[256,2048]{1,0:T(8,128)(2,1)} %get-tuple-element.86), channel_id=1, source_target_pairs={{0,1},{1,0},{2,3},{3,2},{4,5},{5,4},{6,7},{7,6},{8,9},{9,8},{10,11... | collective-permute-start | bytes 3145736 | tf_op jit(solution)/shard_map/ppermute | solution.py:186
  91.7 8.6 %collective-permute-start.24 = (bf16[64,2048]{1,0:T(8,128)(2,1)S(1)}, bf16[64,2048]{1,0:T(8,128)(2,1)S(1)}, u32[]{:S(2)}, u32[]{:S(2)}) collective-permute-start(bf16[64,2048]{1,0:T(8,128)(2,1)S(1)} %get-tuple-element.103), channel_id=1, source_target_pairs={{0,2},{1,3},{2,0},{3,1},{4,6},{5,7},{6,4},{7,5},{8,10},{9,11},{10,... | collective-permute-start | bytes 786440 | tf_op jit(solution)/shard_map/ppermute | solution.py:186
  93.2 8.3 %collective-permute-start.23 = (bf16[64,2048]{1,0:T(8,128)(2,1)S(1)}, bf16[64,2048]{1,0:T(8,128)(2,1)S(1)}, u32[]{:S(2)}, u32[]{:S(2)}) collective-permute-start(bf16[64,2048]{1,0:T(8,128)(2,1)S(1)} %get-tuple-element.104), channel_id=1, source_target_pairs={{0,4},{1,5},{2,6},{3,7},{4,0},{5,1},{6,2},{7,3},{8,12},{9,13},{10,... | collective-permute-start | bytes 786440 | tf_op jit(solution)/shard_map/ppermute | solution.py:186
  102.6 2.9 %copy-start.1 = (bf16[256,2048]{1,0:T(8,128)(2,1)S(1)}, bf16[256,2048]{1,0:T(8,128)(2,1)}, u32[]{:S(2)}) copy-start(bf16[256,2048]{1,0:T(8,128)(2,1)} %get-tuple-element.85) | copy-start | bytes 3145732
  102.8 13.1 %collective-permute-start.26 = (bf16[128,2048]{1,0:T(8,128)(2,1)S(1)}, bf16[128,2048]{1,0:T(8,128)(2,1)S(1)}, u32[]{:S(2)}, u32[]{:S(2)}) collective-permute-start(bf16[128,2048]{1,0:T(8,128)(2,1)S(1)} %pad_maximum_fusion.1), channel_id=1, source_target_pairs={{0,2},{1,3},{2,0},{3,1},{4,6},{5,7},{6,4},{7,5},{8,10},{9,11},{10,... | collective-permute-start | bytes 1572872 | tf_op jit(solution)/shard_map/ppermute | solution.py:186
  103.5 16.8 %copy-start.8 = (f32[16,1,128]{2,1,0:T(1,128)S(1)}, f32[16,1,128]{2,1,0:T(1,128)}, u32[]{:S(2)}) copy-start(f32[16,1,128]{2,1,0:T(1,128)} %all_to_all.9) | copy-start | bytes 24580
  103.5 12.9 %collective-permute-start.25 = (bf16[128,2048]{1,0:T(8,128)(2,1)S(1)}, bf16[128,2048]{1,0:T(8,128)(2,1)S(1)}, u32[]{:S(2)}, u32[]{:S(2)}) collective-permute-start(bf16[128,2048]{1,0:T(8,128)(2,1)S(1)} %pad_maximum_fusion), channel_id=1, source_target_pairs={{0,4},{1,5},{2,6},{3,7},{4,0},{5,1},{6,2},{7,3},{8,12},{9,13},{10,... | collective-permute-start | bytes 1572872 | tf_op jit(solution)/shard_map/ppermute | solution.py:186
  116.4 12.0 %collective-permute-start.27 = (bf16[128,2048]{1,0:T(8,128)(2,1)S(1)}, bf16[128,2048]{1,0:T(8,128)(2,1)}, u32[]{:S(2)}, u32[]{:S(2)}) collective-permute-start(bf16[128,2048]{1,0:T(8,128)(2,1)S(1)} %add_convert_fusion.2), channel_id=1, source_target_pairs={{0,2},{1,3},{2,0},{3,1},{4,6},{5,7},{6,4},{7,5},{8,10},{9,11},{10,... | collective-permute-start | bytes 1572872 | tf_op jit(solution)/shard_map/ppermute | solution.py:186
  117.8 21.8 %collective-permute-start.28 = (bf16[128,2048]{1,0:T(8,128)(2,1)}, bf16[128,2048]{1,0:T(8,128)(2,1)}, u32[]{:S(2)}, u32[]{:S(2)}) collective-permute-start(bf16[128,2048]{1,0:T(8,128)(2,1)} %add_convert_fusion.3), channel_id=1, source_target_pairs={{0,4},{1,5},{2,6},{3,7},{4,0},{5,1},{6,2},{7,3},{8,12},{9,13},{10,... | collective-permute-start | bytes 1572872 | tf_op jit(solution)/shard_map/ppermute | solution.py:186
  118.4 23.6 %collective-permute-start.29 = (bf16[128,2048]{1,0:T(8,128)(2,1)S(1)}, bf16[128,2048]{1,0:T(8,128)(2,1)}, u32[]{:S(2)}, u32[]{:S(2)}) collective-permute-start(bf16[128,2048]{1,0:T(8,128)(2,1)S(1)} %add_convert_fusion.1), channel_id=1, source_target_pairs={{0,8},{1,9},{2,10},{3,11},{4,12},{5,13},{6,14},{7,15},{8,0},{9,1},... | collective-permute-start | bytes 1572872 | tf_op jit(solution)/shard_map/ppermute | solution.py:186

commit v9 on v5

--- a/solution.py
+++ b/solution.py
@@ -35,13 +35,13 @@
     return total.astype(jnp.bfloat16)
 
 
-def plane_kernel(
-    capacity, order, weight, x0, x1, x2, x3, w_gate, w_up, w_down, keep, give, act, rows, ranks
-):
+def plane_kernel(capacity, k, parts, spots, weight, *refs):
+    xs, refs = refs[:parts], refs[parts:]
+    w_gate, w_up, w_down, keep, give, act, rows, ranks = refs
     blocks, tok = weight.shape
-    features = x0.shape[1]
     slots, hidden = act.shape
-    wide = 256
+    features = rows.shape[1]
+    wide, cut = 256, 512
     named = (weight[...] >= 0.0).astype(jnp.float32)
     lane = lax.broadcasted_iota(jnp.int32, (tok, tok), 0)
     below = (lane < lax.broadcasted_iota(jnp.int32, (tok, tok), 1)).astype(jnp.float32)
@@ -52,22 +52,20 @@
     before = jnp.dot(earlier, totals, preferred_element_type=jnp.float32)
     rank = within + before
     kept = (named > 0.0) & (rank < capacity)
+    order = [spots[4 * k + i] for i in range(4)]
     first = order[0] // 4 * 4
     block_row = lax.broadcasted_iota(jnp.int32, (blocks, tok), 0)
     start = jnp.sum(jnp.where(block_row == first, before, 0.0), axis=0, keepdims=True)
     ranks[...] = jnp.where(kept, rank - start, -1.0)
-
-    places = [ranks[pl.ds(order[i], 1), :] for i in range(4)]
-    shares = [weight[pl.ds(order[i], 1), :] for i in range(4)]
-    place = jnp.concatenate(places, axis=1)
-    share = jnp.concatenate(shares, axis=1)
+    place = jnp.concatenate([ranks[pl.ds(i, 1), :] for i in order], axis=1)
+    share = jnp.concatenate([weight[pl.ds(i, 1), :] for i in order], axis=1)
     slot = lax.broadcasted_iota(jnp.int32, (slots, 4 * tok), 0).astype(jnp.float32)
     hits = slot == place
     scale = jnp.sum(jnp.where(hits, share, 0.0), axis=1, keepdims=True)
     select = hits.astype(jnp.float32).astype(jnp.bfloat16)
-    for i in range(features // 512):
-        span = pl.ds(i * 512, 512)
-        x = jnp.concatenate([x0[:, span], x1[:, span], x2[:, span], x3[:, span]], axis=0)
+    for i in range(features // cut):
+        span = pl.ds(i * cut, cut)
+        x = jnp.concatenate([block[:, span] for block in xs], axis=0)
         rows[:, span] = jnp.dot(select, x, preferred_element_type=jnp.float32).astype(jnp.bfloat16)
     for i in range(hidden // wide):
         span = pl.ds(i * wide, wide)
@@ -75,8 +73,8 @@
         up = jnp.dot(rows[...], w_up[:, span], preferred_element_type=jnp.float32)
         act[:, span] = (gate / (1.0 + jnp.exp(-gate)) * up).astype(jnp.bfloat16)
     back = select.T
-    for i in range(features // 512):
-        span = pl.ds(i * 512, 512)
+    for i in range(features // cut):
+        span = pl.ds(i * cut, cut)
         result = jnp.dot(act[...], w_down[:, span], preferred_element_type=jnp.float32)
         made = (result * scale).astype(jnp.bfloat16)
         spread = jnp.dot(back, made, preferred_element_type=jnp.float32).astype(jnp.bfloat16)
@@ -84,28 +82,28 @@
         give[:, span] = spread[2 * tok :]
 
 
-def plane_pass(order, weight, xs, w_gate, w_up, w_down, slots, capacity):
-    tok, features = xs[0].shape
+def plane_pass(k, spots, weight, xs, w_gate, w_up, w_down, slots, capacity):
+    tok, features = weight.shape[1], w_gate.shape[0]
     hidden = w_gate.shape[1]
     half = jax.ShapeDtypeStruct((2 * tok, features), jnp.bfloat16)
     rows = 4 * slots
     flops = 2 * rows * (3 * features * hidden + 8 * tok * features)
     moved = 2 * (3 * features * hidden + 8 * tok * features)
     return pl.pallas_call(
-        functools.partial(plane_kernel, capacity),
+        functools.partial(plane_kernel, capacity, k, len(xs)),
         out_shape=(half, half, jax.ShapeDtypeStruct((rows, hidden), jnp.bfloat16)),
         in_specs=[pl.BlockSpec(memory_space=pltpu.SMEM)]
-        + [pl.BlockSpec(memory_space=pltpu.VMEM)] * 8,
+        + [pl.BlockSpec(memory_space=pltpu.VMEM)] * (len(xs) + 4),
         out_specs=[pl.BlockSpec(memory_space=pltpu.VMEM)] * 3,
         scratch_shapes=[
             pltpu.VMEM((rows, features), jnp.bfloat16),
             pltpu.VMEM(weight.shape, jnp.float32),
         ],
-        compiler_params=pltpu.CompilerParams(vmem_limit_bytes=32 * 1024 * 1024),
+        compiler_params=pltpu.CompilerParams(vmem_limit_bytes=12 * 1024 * 1024),
         cost_estimate=pl.CostEstimate(
             flops=flops, bytes_accessed=moved, transcendentals=rows * hidden
         ),
-    )(order, weight, *xs, w_gate, w_up, w_down)
+    )(spots, weight, *xs, w_gate, w_up, w_down)
 
 
 def staged(routes, probs, tokens, w_gate, w_up, w_down):
@@ -128,30 +126,30 @@
     def together(*arrays):
         return lax.optimization_barrier(arrays)
 
+    spots = jnp.stack(
+        [
+            (z ^ k) * 4 + (y ^ column_bit) * 2 + (core ^ core_bit)
+            for k in range(4)
+            for core_bit in range(2)
+            for column_bit in range(2)
+        ]
+    ).astype(jnp.int32)
+
     def expert(k, *xs):
-        base = (z ^ k) * 4
-        order = jnp.stack(
-            [
-                base + y * 2 + core,
-                base + (1 - y) * 2 + core,
-                base + y * 2 + 1 - core,
-                base + (1 - y) * 2 + 1 - core,
-            ]
-        ).astype(jnp.int32)
-        return plane_pass(order, weight, xs, w_gate, w_up, w_down, slots, capacity)
+        return plane_pass(k, spots, weight, xs, w_gate, w_up, w_down, slots, capacity)
 
     weight = weights_for_me(routes, probs, size)
     a0 = tokens
-    a1 = pair(a0)
-    a2 = far(a0)
-    b0 = column(a0)
-    c0 = sibling(a0)
-    a1, b0, c0, weight = together(a1, b0, c0, weight)
+    a1, low, b0, c0, weight = together(
+        pair(a0), far(a0[:half]), column(a0), sibling(a0), weight
+    )
     b1 = column(a1)
+    high = far(a0[half:])
     d0 = sibling(b0)
     c1 = sibling(a1)
     keep0, give0, act0 = expert(0, a0, b0, c0, d0)
-    a2, b1, c1, keep0, give0, act0 = together(a2, b1, c1, keep0, give0, act0)
+    high, b1, c1, keep0, give0, act0 = together(high, b1, c1, keep0, give0, act0)
+    a2 = jnp.concatenate([low, high], axis=0)
     a3 = pair(a2)
     b2 = column(a2)
     d1 = sibling(b1)
@@ -167,11 +165,11 @@
     b3_low, b3_high, c3, got1, keep2, give2, act2 = together(
         b3_low, b3_high, c3, got1, keep2, give2, act2
     )
-    b3 = jnp.concatenate([b3_low, b3_high], axis=0)
-    d3 = sibling(b3)
+    d3_low = sibling(b3_low)
+    d3_high = sibling(b3_high)
     came1 = column(summed(keep1[tok:], got1[tok:]))
     got2 = sibling(give2)
-    keep3, give3, act3 = expert(3, a3, b3, c3, d3)
+    keep3, give3, act3 = expert(3, a3, b3_low, b3_high, c3, d3_low, d3_high)
 
     keep3, give3, act3, got2, came1 = together(keep3, give3, act3, got2, came1)
     got3 = sibling(give3)
@@ -190,10 +188,12 @@
         ],
         axis=0,
     )
-    far3, side2 = together(pair(far3), column(side2))
+    near1 = summed(keep1[:tok], got1[:tok], came1)
+    side0 = summed(keep0[tok:], got0[tok:])
+    far3, side2, near1, side0 = together(pair(far3), column(side2), near1, side0)
     last2 = far(summed(keep2[:tok], got2[:tok], far3, side2))
-    last1 = pair(summed(keep1[:tok], got1[:tok], came1))
-    last0 = column(summed(keep0[tok:], got0[tok:]))
+    last1 = pair(near1)
+    last0 = column(side0)
     mixed = summed(keep0[:tok], got0[:tok], last0, last1, last2)
 
     acts = jnp.concatenate([act0, act1, act2, act3], axis=0)

time: 167 us -> 142 us (0.85)
  local copies, waits for them, and re-layouts: 44.8 us -> 13.3 us
  waiting for transfers between devices: 39.7 us -> 49.2 us
  starting transfers between devices: 20.9 us -> 26.9 us
  other arithmetic: 12.2 us -> 8.41 us
  Pallas kernels: 28.6 us -> 25.1 us
  matrix products: 5.31 us -> 3.18 us
    unnamed x81 -> x31, local copies, waits for them, and re-layouts: 43.1 us -> 10.4 us
    ppermute x28 -> x30, waiting for transfers between devices: 39.7 us -> 49.2 us  [swapped(): return lax.ppermute(array, 'expert', [(i, i ^ bit) for i in range(size)])]
    ppermute x28 -> x30, starting transfers between devices: 20.9 us -> 26.9 us  [swapped(): return lax.ppermute(array, 'expert', [(i, i ^ bit) for i in range(size)])]
    pallas_call x4, Pallas kernels: 28.6 us -> 25.1 us  [plane_pass(): pl.pallas_call(functools.partial(plane_kernel, capacity, k, len(xs)), out...]
    convert_element_type x8, other arithmetic: 9.77 us -> 6.31 us  [summed(): return total.astype(jnp.bfloat16)]
    dot_general x1, matrix products: 5.31 us -> 3.18 us  [gram_of(): lax.dot_general(rows, rows, (((0,), (0,)), ((), ())), preferred_element_t...]
    slice x0 -> x1, local copies, waits for them, and re-layouts: none -> 1.78 us  [staged(): high = far(a0[half:])]
  transfers between devices with their start and end apart: 28 -> 30, of which waited for: 10 -> 14; matrix products, arithmetic and copies ran while one was open for 9% -> 8% of each run, Pallas kernels for 17% -> 18%
where the time goes in v9:
time: 142 us
  waiting for transfers between devices  49.2 us (35%)
  starting transfers between devices  26.9 us (19%)
  Pallas kernels  25.1 us (18%)
  blocking collectives  13.9 us (10%)
  local copies, waits for them, and re-layouts  13.3 us (9%)
  other arithmetic  8.41 us (6%)
  matrix products  3.18 us (2%)
  between operations  1.53 us (1%)
    ppermute x30, waiting for transfers between devices, swapped(): return lax.ppermute(array, 'expert', [(i, i ^ bit) for i in range(size)])  49.2 us
    ppermute x30, starting transfers between devices, swapped(): return lax.ppermute(array, 'expert', [(i, i ^ bit) for i in range(size)])  26.9 us
    pallas_call x4, Pallas kernels, plane_pass(): pl.pallas_call(functools.partial(plane_kernel, capacity, k, len(xs)), out...  25.1 us
    all_to_all x1, blocking collectives, weights_for_me(): lax.all_to_all(mine, 'expert', split_axis=0, concat_axis=0, tiled=True)  13.9 us
    unnamed x31, local copies, waits for them, and re-layouts  10.4 us
    convert_element_type x8, other arithmetic, summed(): return total.astype(jnp.bfloat16)  6.31 us
    dot_general x1, matrix products, gram_of(): lax.dot_general(rows, rows, (((0,), (0,)), ((), ())), preferred_element_t...  3.18 us
  transfers between devices with their start and end apart: 30, of which 14 were waited for; matrix products, arithmetic and copies ran while one was open for 8% of the time, Pallas kernels for 18%

profile of v9, /device:TPU:0, one launch (start us, length us, event | category | flops | bytes accessed | tf_op | source)
XLA Modules:
  0.0 141.6 jit_solution(3414989916416981781)
XLA Ops:
  0.6 3.0 %collective-permute-start.3 = (bf16[128,2048]{1,0:T(8,128)(2,1)}, bf16[128,2048]{1,0:T(8,128)(2,1)S(1)}, u32[]{:S(2)}, u32[]{:S(2)}) collective-permute-start(bf16[128,2048]{1,0:T(8,128)(2,1)} %refs_0_.1), channel_id=1, source_target_pairs={{0,2},{1,3},{2,0},{3,1},{4,6},{5,7},{6,4},{7,5},{8,10},{9,11},{10,... | collective-permute-start | bytes 1572872 | tf_op jit(solution)/shard_map/ppermute | solution.py:119
  3.7 1.6 %collective-permute-start.1 = (bf16[128,2048]{1,0:T(8,128)(2,1)}, bf16[128,2048]{1,0:T(8,128)(2,1)S(1)}, u32[]{:S(2)}, u32[]{:S(2)}) collective-permute-start(bf16[128,2048]{1,0:T(8,128)(2,1)} %refs_0_.1), channel_id=1, source_target_pairs={{0,4},{1,5},{2,6},{3,7},{4,0},{5,1},{6,2},{7,3},{8,12},{9,13},{10,... | collective-permute-start | bytes 1572872 | tf_op jit(solution)/shard_map/ppermute | solution.py:119
  5.2 1.8 %fusion.12 = (bf16[64,2048]{1,0:T(8,128)(2,1)}, bf16[64,2048]{1,0:T(8,128)(2,1)S(1)}) fusion(bf16[128,2048]{1,0:T(8,128)(2,1)} %refs_0_.1), kind=kLoop, calls=%fused_computation.30 | loop fusion | bytes 1048576 | tf_op jit(solution)/shard_map/slice | solution.py:147
  7.0 2.6 %collective-permute-start.2 = (bf16[64,2048]{1,0:T(8,128)(2,1)S(1)}, bf16[64,2048]{1,0:T(8,128)(2,1)S(1)}, u32[]{:S(2)}, u32[]{:S(2)}) collective-permute-start(bf16[64,2048]{1,0:T(8,128)(2,1)S(1)} %get-tuple-element.106), channel_id=1, source_target_pairs={{0,8},{1,9},{2,10},{3,11},{4,12},{5,13},{6,14},{7,15},{8,0},{9,1},... | collective-permute-start | bytes 786440 | tf_op jit(solution)/shard_map/ppermute | solution.py:119
  9.6 0.7 select_reduce_fusion
  10.3 0.7 fusion.10
  11.1 13.9 %all_to_all.9 = f32[16,1,128]{2,1,0:T(1,128)S(1)} all-to-all(f32[16,1,128]{2,1,0:T(1,128)S(1)} %bitcast.44), channel_id=1, replica_groups=mesh['parts'=2,'expert'=16] {'expert'}, dimensions={0} | all-to-all | bytes 16384 | tf_op jit(solution)/shard_map/all_to_all | solution.py:28
  25.0 0.8 copy-done.5
  25.8 0.5 collective-permute-start.6
  26.3 1.5 %collective-permute-start.5 = (bf16[128,2048]{1,0:T(8,128)(2,1)S(1)}, bf16[128,2048]{1,0:T(8,128)(2,1)S(1)}, u32[]{:S(2)}, u32[]{:S(2)}) collective-permute-start(bf16[128,2048]{1,0:T(8,128)(2,1)S(1)} %collective-permute-done.1.refs_0_), channel_id=1, source_target_pairs={{0,2},{1,3},{2,0},{3,1},{4,6},{5,7},{6,4},{7,5},{8,10},{9,11},{10,... | collective-permute-start | bytes 1572872 | tf_op jit(solution)/shard_map/ppermute | solution.py:119
  27.7 0.6 collective-permute-start
  28.3 0.1 stack.67.spots
  28.4 0.8 copy-done.7
  29.2 1.0 copy-done
  30.3 1.9 %copy-done.1 = bf16[1,2048,768]{2,1,0:T(8,128)(2,1)S(1)} copy-done((bf16[1,2048,768]{2,1,0:T(8,128)(2,1)S(1)}, bf16[1,2048,768]{2,1,0:T(8,128)(2,1)}, u32[]{:S(2)}) %copy-start.1) | copy-done | bytes 3145752
  32.2 1.9 %copy-done.3 = bf16[1,2048,768]{2,1,0:T(8,128)(2,1)S(1)} copy-done((bf16[1,2048,768]{2,1,0:T(8,128)(2,1)S(1)}, bf16[1,2048,768]{2,1,0:T(8,128)(2,1)}, u32[]{:S(2)}) %copy-start.3) | copy-done | bytes 3145752
  34.1 1.9 %copy-done.4 = bf16[1,768,2048]{2,1,0:T(8,128)(2,1)S(1)} copy-done((bf16[1,768,2048]{2,1,0:T(8,128)(2,1)S(1)}, bf16[1,768,2048]{2,1,0:T(8,128)(2,1)}, u32[]{:S(2)}) %copy-start.4) | copy-done | bytes 3145752
  35.9 1.0 copy-done.6
  37.0 1.0 copy-done.8
  38.0 6.2 %shard_map.77 = (bf16[256,2048]{1,0:T(8,128)(2,1)S(1)}, bf16[256,2048]{1,0:T(8,128)(2,1)S(1)}, bf16[320,768]{1,0:T(8,128)(2,1)S(1)}) custom-call(s32[16]{0:T(128)S(1)} %stack.67.spots, f32[16,128]{1,0:T(8,128)S(1)} %bitcast.27, bf16[128,2048]{1,0:T(8,128)(2,1)S(1)} %copy-done, bf16[128,2048]{1,0:T(8,128)(2,1)S(1)} %collective-permute-done.3.refs_1_, ...), custom_call_target="tpu_custom_call" | custom-call | flops 4362076160 | bytes 13631488 | tf_op jit(solution)/shard_map/pallas_call | solution.py:92
  44.4 1.0 constant_dynamic-update-slice_fusion.refs_0_
  45.4 0.5 collective-permute-start.10
  45.9 0.7 collective-permute-start.9
  46.6 1.5 %collective-permute-start.8 = (bf16[128,2048]{1,0:T(8,128)(2,1)S(1)}, bf16[128,2048]{1,0:T(8,128)(2,1)S(1)}, u32[]{:S(2)}, u32[]{:S(2)}) collective-permute-start(bf16[128,2048]{1,0:T(8,128)(2,1)S(1)} %constant_dynamic-update-slice_fusion.refs_0_), channel_id=1, source_target_pairs={{0,4},{1,5},{2,6},{3,7},{4,0},{5,1},{6,2},{7,3},{8,12},{9,13},{10,... | collective-permute-start | bytes 1572872 | tf_op jit(solution)/shard_map/ppermute | solution.py:119
  48.2 6.2 %shard_map.78 = (bf16[256,2048]{1,0:T(8,128)(2,1)S(1)}, bf16[256,2048]{1,0:T(8,128)(2,1)S(1)}, bf16[320,768]{1,0:T(8,128)(2,1)S(1)}) custom-call(s32[16]{0:T(128)S(1)} %stack.67.spots, f32[16,128]{1,0:T(8,128)S(1)} %bitcast.28, bf16[128,2048]{1,0:T(8,128)(2,1)S(1)} %collective-permute-done.1.refs_0_, bf16[128,2048]{1,0:T(8,128)(2,1)S(1)} %collective-permute-done.5.refs_1_, ...), custom_call_target="tpu_custom_call" | custom-call | flops 4362076160 | bytes 13631488 | tf_op jit(solution)/shard_map/pallas_call | solution.py:92
  54.5 5.4 %collective-permute-done.9.refs_1_ = bf16[128,2048]{1,0:T(8,128)(2,1)S(1)} collective-permute-done((bf16[128,2048]{1,0:T(8,128)(2,1)S(1)}, bf16[128,2048]{1,0:T(8,128)(2,1)S(1)}, u32[]{:S(2)}, u32[]{:S(2)}) %collective-permute-start.9) | collective-permute-done | bytes 524320 | tf_op jit(solution)/shard_map/ppermute | solution.py:119
  59.8 0.5 collective-permute-done.8.refs_0_
  60.3 0.5 collective-permute-start.16
  60.9 1.3 collective-permute-start.13
  62.2 1.6 %collective-permute-start.12 = (bf16[64,2048]{1,0:T(8,128)(2,1)S(1)}, bf16[64,2048]{1,0:T(8,128)(2,1)S(1)}, u32[]{:S(2)}, u32[]{:S(2)}) collective-permute-start(bf16[64,2048]{1,0:T(8,128)(2,1)S(1)} %slice.80), channel_id=1, source_target_pairs={{0,4},{1,5},{2,6},{3,7},{4,0},{5,1},{6,2},{7,3},{8,12},{9,13},{10,... | collective-permute-start | bytes 786440 | tf_op jit(solution)/shard_map/ppermute | solution.py:119
  63.8 6.4 %shard_map.79 = (bf16[256,2048]{1,0:T(8,128)(2,1)S(1)}, bf16[256,2048]{1,0:T(8,128)(2,1)S(1)}, bf16[320,768]{1,0:T(8,128)(2,1)S(1)}) custom-call(s32[16]{0:T(128)S(1)} %stack.67.spots, f32[16,128]{1,0:T(8,128)S(1)} %bitcast.29, bf16[128,2048]{1,0:T(8,128)(2,1)S(1)} %constant_dynamic-update-slice_fusion.refs_0_, ...), custom_call_target="tpu_custom_call" | custom-call | flops 4362076160 | bytes 13631488 | tf_op jit(solution)/shard_map/pallas_call | solution.py:92
  70.3 0.4 collective-permute-done.12.refs_1_
  70.7 0.5 collective-permute-start.17
  71.3 0.1 add_convert_fusion.4
  71.4 1.0 collective-permute-start.20
  72.4 0.1 collective-permute-start.22
  72.5 1.2 collective-permute-done.17.refs_4_
  73.7 0.4 collective-permute-done.18.refs_5_
  74.1 6.3 %shard_map.80 = (bf16[256,2048]{1,0:T(8,128)(2,1)S(1)}, bf16[256,2048]{1,0:T(8,128)(2,1)S(1)}, bf16[320,768]{1,0:T(8,128)(2,1)S(1)}) custom-call(s32[16]{0:T(128)S(1)} %stack.67.spots, f32[16,128]{1,0:T(8,128)S(1)} %bitcast.30, bf16[128,2048]{1,0:T(8,128)(2,1)S(1)} %collective-permute-done.8.refs_0_, bf16[64,2048]{1,0:T(8,128)(2,1)S(1)} %collective-permute-done.12.refs_1_, ...), custom_call_target="tpu_custom_call" | custom-call | flops 4362076160 | bytes 13631488 | tf_op jit(solution)/shard_map/pallas_call | solution.py:92
  80.4 5.4 %collective-permute-done.20 = bf16[128,2048]{1,0:T(8,128)(2,1)S(1)} collective-permute-done((bf16[128,2048]{1,0:T(8,128)(2,1)S(1)}, bf16[128,2048]{1,0:T(8,128)(2,1)S(1)}, u32[]{:S(2)}, u32[]{:S(2)}) %collective-permute-start.20) | collective-permute-done | bytes 524320 | tf_op jit(solution)/shard_map/ppermute | solution.py:119
  85.7 2.6 %collective-permute-done.21 = bf16[256,2048]{1,0:T(8,128)(2,1)S(1)} collective-permute-done((bf16[256,2048]{1,0:T(8,128)(2,1)S(1)}, bf16[256,2048]{1,0:T(8,128)(2,1)S(1)}, u32[]{:S(2)}, u32[]{:S(2)}) %collective-permute-start.21) | collective-permute-done | bytes 1048608 | tf_op jit(solution)/shard_map/ppermute | solution.py:119
  88.4 0.3 add_convert_fusion.10
  88.7 0.9 collective-permute-start.24
  89.6 1.6 %collective-permute-start.23 = (bf16[64,2048]{1,0:T(8,128)(2,1)S(1)}, bf16[64,2048]{1,0:T(8,128)(2,1)S(1)}, u32[]{:S(2)}, u32[]{:S(2)}) collective-permute-start(bf16[64,2048]{1,0:T(8,128)(2,1)S(1)} %get-tuple-element.104), channel_id=1, source_target_pairs={{0,4},{1,5},{2,6},{3,7},{4,0},{5,1},{6,2},{7,3},{8,12},{9,13},{10,... | collective-permute-start | bytes 786440 | tf_op jit(solution)/shard_map/ppermute | solution.py:119
  91.2 5.9 %collective-permute-done.24 = bf16[64,2048]{1,0:T(8,128)(2,1)S(1)} collective-permute-done((bf16[64,2048]{1,0:T(8,128)(2,1)S(1)}, bf16[64,2048]{1,0:T(8,128)(2,1)S(1)}, u32[]{:S(2)}, u32[]{:S(2)}) %collective-permute-start.24) | collective-permute-done | bytes 262176 | tf_op jit(solution)/shard_map/ppermute | solution.py:119
  97.1 0.6 collective-permute-done.23
  97.6 0.1 add_convert_fusion.7
  97.7 0.2 add_convert_fusion.6
  98.0 1.2 collective-permute-start.26
  99.3 1.7 %collective-permute-start.25 = (bf16[128,2048]{1,0:T(8,128)(2,1)S(1)}, bf16[128,2048]{1,0:T(8,128)(2,1)S(1)}, u32[]{:S(2)}, u32[]{:S(2)}) collective-permute-start(bf16[128,2048]{1,0:T(8,128)(2,1)S(1)} %pad_maximum_fusion), channel_id=1, source_target_pairs={{0,4},{1,5},{2,6},{3,7},{4,0},{5,1},{6,2},{7,3},{8,12},{9,13},{10,... | collective-permute-start | bytes 1572872 | tf_op jit(solution)/shard_map/ppermute | solution.py:119
  100.9 1.0 add_convert_fusion.3
  102.0 0.9 add_convert_fusion.2
  102.9 8.0 %collective-permute-done.26 = bf16[128,2048]{1,0:T(8,128)(2,1)S(1)} collective-permute-done((bf16[128,2048]{1,0:T(8,128)(2,1)S(1)}, bf16[128,2048]{1,0:T(8,128)(2,1)S(1)}, u32[]{:S(2)}, u32[]{:S(2)}) %collective-permute-start.26) | collective-permute-done | bytes 524320 | tf_op jit(solution)/shard_map/ppermute | solution.py:119
  110.9 1.0 collective-permute-done.25
  111.9 0.9 collective-permute-start.27
  112.7 1.6 %collective-permute-start.28 = (bf16[128,2048]{1,0:T(8,128)(2,1)}, bf16[128,2048]{1,0:T(8,128)(2,1)}, u32[]{:S(2)}, u32[]{:S(2)}) collective-permute-start(bf16[128,2048]{1,0:T(8,128)(2,1)} %add_convert_fusion.3), channel_id=1, source_target_pairs={{0,4},{1,5},{2,6},{3,7},{4,0},{5,1},{6,2},{7,3},{8,12},{9,13},{10,... | collective-permute-start | bytes 1572872 | tf_op jit(solution)/shard_map/ppermute | solution.py:119
  114.3 1.1 add_convert_fusion.1
  115.5 1.3 collective-permute-start.29
  116.8 0.6 convert_reduce_fusion
  118.0 3.2 %multiply_bitcast_fusion = f32[1,768,768]{2,1,0:T(8,128)} fusion(f32[]{:T(128)S(6)} %div.24, bf16[320,768]{1,0:T(8,128)(2,1)S(1)} %get-tuple-element.84, bf16[320,768]{1,0:T(8,128)(2,1)S(1)} %get-tuple-element.74, bf16[320,768]{1,0:T(8,128)(2,1)S(1)} %copy-done.12, bf16[320,768]{1,0:T(8,128)(2,1)S(1)} %copy-done.10), kind=kOutput, calls=%fused_computation | convolution fusion | flops 1518403584 | bytes 4325380 | tf_op jit(solution)/shard_map/dot_general | solution.py:12
  121.1 2.7 %collective-permute-done.27 = bf16[128,2048]{1,0:T(8,128)(2,1)} collective-permute-done((bf16[128,2048]{1,0:T(8,128)(2,1)}, bf16[128,2048]{1,0:T(8,128)(2,1)}, u32[]{:S(2)}, u32[]{:S(2)}) %collective-permute-start.27) | collective-permute-done | bytes 524320 | tf_op jit(solution)/shard_map/ppermute | solution.py:119
  123.8 10.3 %collective-permute-done.28 = bf16[128,2048]{1,0:T(8,128)(2,1)} collective-permute-done((bf16[128,2048]{1,0:T(8,128)(2,1)}, bf16[128,2048]{1,0:T(8,128)(2,1)}, u32[]{:S(2)}, u32[]{:S(2)}) %collective-permute-start.28) | collective-permute-done | bytes 524320 | tf_op jit(solution)/shard_map/ppermute | solution.py:119
  134.1 4.9 %collective-permute-done.29 = bf16[128,2048]{1,0:T(8,128)(2,1)} collective-permute-done((bf16[128,2048]{1,0:T(8,128)(2,1)}, bf16[128,2048]{1,0:T(8,128)(2,1)}, u32[]{:S(2)}, u32[]{:S(2)}) %collective-permute-start.29) | collective-permute-done | bytes 524320 | tf_op jit(solution)/shard_map/ppermute | solution.py:119
  139.0 2.6 %add_convert_fusion = bf16[128,2048]{1,0:T(8,128)(2,1)} fusion(bf16[128,2048]{1,0:T(8,128)(2,1)} %collective-permute-done.29, bf16[128,2048]{1,0:T(8,128)(2,1)} %collective-permute-done.28, bf16[128,2048]{1,0:T(8,128)(2,1)} %collective-permute-done.27, bf16[256,2048]{1,0:T(8,128)(2,1)S(1)} %copy-done.14, bf16[256,2048]{1,0:T(8,128)(2,1)S(1)} %get-tuple-element.85), kind=kLoop, calls=%fused_computation.9 | loop fusion | flops 2621440 | bytes 3145728 | tf_op jit(solution)/shard_map/convert_element_type | solution.py:35
  (52 shorter events, 0.4 us)
Async XLA Ops:
  0.6 24.3 %collective-permute-start.3 = (bf16[128,2048]{1,0:T(8,128)(2,1)}, bf16[128,2048]{1,0:T(8,128)(2,1)S(1)}, u32[]{:S(2)}, u32[]{:S(2)}) collective-permute-start(bf16[128,2048]{1,0:T(8,128)(2,1)} %refs_0_.1), channel_id=1, source_target_pairs={{0,2},{1,3},{2,0},{3,1},{4,6},{5,7},{6,4},{7,5},{8,10},{9,11},{10,... | collective-permute-start | bytes 1572872 | tf_op jit(solution)/shard_map/ppermute | solution.py:119
  3.7 21.3 %collective-permute-start.1 = (bf16[128,2048]{1,0:T(8,128)(2,1)}, bf16[128,2048]{1,0:T(8,128)(2,1)S(1)}, u32[]{:S(2)}, u32[]{:S(2)}) collective-permute-start(bf16[128,2048]{1,0:T(8,128)(2,1)} %refs_0_.1), channel_id=1, source_target_pairs={{0,4},{1,5},{2,6},{3,7},{4,0},{5,1},{6,2},{7,3},{8,12},{9,13},{10,... | collective-permute-start | bytes 1572872 | tf_op jit(solution)/shard_map/ppermute | solution.py:119
  5.2 19.7 %collective-permute-start.4 = (bf16[128,2048]{1,0:T(8,128)(2,1)}, bf16[128,2048]{1,0:T(8,128)(2,1)S(1)}, u32[]{:S(2)}, u32[]{:S(2)}) collective-permute-start(bf16[128,2048]{1,0:T(8,128)(2,1)} %refs_0_.1), channel_id=1, source_target_pairs={{0,1},{1,0},{2,3},{3,2},{4,5},{5,4},{6,7},{7,6},{8,9},{9,8},{10,11... | collective-permute-start | bytes 1572872 | tf_op jit(solution)/shard_map/ppermute | solution.py:119
  7.0 17.9 %collective-permute-start.2 = (bf16[64,2048]{1,0:T(8,128)(2,1)S(1)}, bf16[64,2048]{1,0:T(8,128)(2,1)S(1)}, u32[]{:S(2)}, u32[]{:S(2)}) collective-permute-start(bf16[64,2048]{1,0:T(8,128)(2,1)S(1)} %get-tuple-element.106), channel_id=1, source_target_pairs={{0,8},{1,9},{2,10},{3,11},{4,12},{5,13},{6,14},{7,15},{8,0},{9,1},... | collective-permute-start | bytes 786440 | tf_op jit(solution)/shard_map/ppermute | solution.py:119
  25.0 0.8 copy-start.5
  25.8 2.7 %collective-permute-start.7 = (bf16[128,2048]{1,0:T(8,128)(2,1)S(1)}, bf16[128,2048]{1,0:T(8,128)(2,1)S(1)}, u32[]{:S(2)}, u32[]{:S(2)}) collective-permute-start(bf16[128,2048]{1,0:T(8,128)(2,1)S(1)} %collective-permute-done.3.refs_1_), channel_id=1, source_target_pairs={{0,1},{1,0},{2,3},{3,2},{4,5},{5,4},{6,7},{7,6},{8,9},{9,8},{10,11... | collective-permute-start | bytes 1572872 | tf_op jit(solution)/shard_map/ppermute | solution.py:119
  25.8 18.5 %collective-permute-start.6 = (bf16[128,2048]{1,0:T(8,128)(2,1)S(1)}, bf16[128,2048]{1,0:T(8,128)(2,1)S(1)}, u32[]{:S(2)}, u32[]{:S(2)}) collective-permute-start(bf16[128,2048]{1,0:T(8,128)(2,1)S(1)} %collective-permute-done.1.refs_0_), channel_id=1, source_target_pairs={{0,1},{1,0},{2,3},{3,2},{4,5},{5,4},{6,7},{7,6},{8,9},{9,8},{10,11... | collective-permute-start | bytes 1572872 | tf_op jit(solution)/shard_map/ppermute | solution.py:119
  26.3 18.0 %collective-permute-start.5 = (bf16[128,2048]{1,0:T(8,128)(2,1)S(1)}, bf16[128,2048]{1,0:T(8,128)(2,1)S(1)}, u32[]{:S(2)}, u32[]{:S(2)}) collective-permute-start(bf16[128,2048]{1,0:T(8,128)(2,1)S(1)} %collective-permute-done.1.refs_0_), channel_id=1, source_target_pairs={{0,2},{1,3},{2,0},{3,1},{4,6},{5,7},{6,4},{7,5},{8,10},{9,11},{10,... | collective-permute-start | bytes 1572872 | tf_op jit(solution)/shard_map/ppermute | solution.py:119
  27.7 16.5 %collective-permute-start = (bf16[64,2048]{1,0:T(8,128)(2,1)}, bf16[64,2048]{1,0:T(8,128)(2,1)}, u32[]{:S(2)}, u32[]{:S(2)}) collective-permute-start(bf16[64,2048]{1,0:T(8,128)(2,1)} %get-tuple-element.105), channel_id=1, source_target_pairs={{0,8},{1,9},{2,10},{3,11},{4,12},{5,13},{6,14},{7,15},{8,0},{9,1},... | collective-permute-start | bytes 786440 | tf_op jit(solution)/shard_map/ppermute | solution.py:119
  28.4 0.8 copy-start.7
  29.2 1.0 copy-start
  30.3 1.9 %copy-start.1 = (bf16[1,2048,768]{2,1,0:T(8,128)(2,1)S(1)}, bf16[1,2048,768]{2,1,0:T(8,128)(2,1)}, u32[]{:S(2)}) copy-start(bf16[1,2048,768]{2,1,0:T(8,128)(2,1)} %param.9) | copy-start | bytes 9437188
  32.2 1.9 %copy-start.3 = (bf16[1,2048,768]{2,1,0:T(8,128)(2,1)S(1)}, bf16[1,2048,768]{2,1,0:T(8,128)(2,1)}, u32[]{:S(2)}) copy-start(bf16[1,2048,768]{2,1,0:T(8,128)(2,1)} %param.10) | copy-start | bytes 9437188
  34.0 1.9 %copy-start.4 = (bf16[1,768,2048]{2,1,0:T(8,128)(2,1)S(1)}, bf16[1,768,2048]{2,1,0:T(8,128)(2,1)}, u32[]{:S(2)}) copy-start(bf16[1,768,2048]{2,1,0:T(8,128)(2,1)} %param.11) | copy-start | bytes 9437188
  35.9 1.0 copy-start.6
  37.0 1.0 copy-start.8
  44.3 10.2 %copy-start.9 = (bf16[320,768]{1,0:T(8,128)(2,1)}, bf16[320,768]{1,0:T(8,128)(2,1)S(1)}, u32[]{:S(2)}) copy-start(bf16[320,768]{1,0:T(8,128)(2,1)S(1)} %get-tuple-element.58) | copy-start | bytes 1474564
  44.3 3.9 %collective-permute-start.11 = (bf16[128,2048]{1,0:T(8,128)(2,1)S(1)}, bf16[128,2048]{1,0:T(8,128)(2,1)S(1)}, u32[]{:S(2)}, u32[]{:S(2)}) collective-permute-start(bf16[128,2048]{1,0:T(8,128)(2,1)S(1)} %collective-permute-done.5.refs_1_), channel_id=1, source_target_pairs={{0,1},{1,0},{2,3},{3,2},{4,5},{5,4},{6,7},{7,6},{8,9},{9,8},{10,11... | collective-permute-start | bytes 1572872 | tf_op jit(solution)/shard_map/ppermute | solution.py:119
  45.4 9.0 %collective-permute-start.10 = (bf16[128,2048]{1,0:T(8,128)(2,1)S(1)}, bf16[128,2048]{1,0:T(8,128)(2,1)S(1)}, u32[]{:S(2)}, u32[]{:S(2)}) collective-permute-start(bf16[128,2048]{1,0:T(8,128)(2,1)S(1)} %constant_dynamic-update-slice_fusion.refs_0_), channel_id=1, source_target_pairs={{0,1},{1,0},{2,3},{3,2},{4,5},{5,4},{6,7},{7,6},{8,9},{9,8},{10,11... | collective-permute-start | bytes 1572872 | tf_op jit(solution)/shard_map/ppermute | solution.py:119
  45.9 13.9 %collective-permute-start.9 = (bf16[128,2048]{1,0:T(8,128)(2,1)S(1)}, bf16[128,2048]{1,0:T(8,128)(2,1)S(1)}, u32[]{:S(2)}, u32[]{:S(2)}) collective-permute-start(bf16[128,2048]{1,0:T(8,128)(2,1)S(1)} %constant_dynamic-update-slice_fusion.refs_0_), channel_id=1, source_target_pairs={{0,2},{1,3},{2,0},{3,1},{4,6},{5,7},{6,4},{7,5},{8,10},{9,11},{10,... | collective-permute-start | bytes 1572872 | tf_op jit(solution)/shard_map/ppermute | solution.py:119
  46.6 13.7 %collective-permute-start.8 = (bf16[128,2048]{1,0:T(8,128)(2,1)S(1)}, bf16[128,2048]{1,0:T(8,128)(2,1)S(1)}, u32[]{:S(2)}, u32[]{:S(2)}) collective-permute-start(bf16[128,2048]{1,0:T(8,128)(2,1)S(1)} %constant_dynamic-update-slice_fusion.refs_0_), channel_id=1, source_target_pairs={{0,4},{1,5},{2,6},{3,7},{4,0},{5,1},{6,2},{7,3},{8,12},{9,13},{10,... | collective-permute-start | bytes 1572872 | tf_op jit(solution)/shard_map/ppermute | solution.py:119
  54.4 9.4 %copy-start.11 = (bf16[320,768]{1,0:T(8,128)(2,1)}, bf16[320,768]{1,0:T(8,128)(2,1)S(1)}, u32[]{:S(2)}) copy-start(bf16[320,768]{1,0:T(8,128)(2,1)S(1)} %get-tuple-element.66) | copy-start | bytes 1474564
  60.3 10.3 %collective-permute-start.15 = (bf16[256,2048]{1,0:T(8,128)(2,1)S(1)}, bf16[256,2048]{1,0:T(8,128)(2,1)S(1)}, u32[]{:S(2)}, u32[]{:S(2)}) collective-permute-start(bf16[256,2048]{1,0:T(8,128)(2,1)S(1)} %get-tuple-element.69), channel_id=1, source_target_pairs={{0,1},{1,0},{2,3},{3,2},{4,5},{5,4},{6,7},{7,6},{8,9},{9,8},{10,11... | collective-permute-start | bytes 3145736 | tf_op jit(solution)/shard_map/ppermute | solution.py:119
  60.3 3.5 %collective-permute-start.16 = (bf16[128,2048]{1,0:T(8,128)(2,1)S(1)}, bf16[128,2048]{1,0:T(8,128)(2,1)S(1)}, u32[]{:S(2)}, u32[]{:S(2)}) collective-permute-start(bf16[128,2048]{1,0:T(8,128)(2,1)S(1)} %collective-permute-done.9.refs_1_), channel_id=1, source_target_pairs={{0,1},{1,0},{2,3},{3,2},{4,5},{5,4},{6,7},{7,6},{8,9},{9,8},{10,11... | collective-permute-start | bytes 1572872 | tf_op jit(solution)/shard_map/ppermute | solution.py:119
  60.8 9.8 %collective-permute-start.14 = (bf16[128,2048]{1,0:T(8,128)(2,1)S(1)}, bf16[128,2048]{1,0:T(8,128)(2,1)S(1)}, u32[]{:S(2)}, u32[]{:S(2)}) collective-permute-start(bf16[128,2048]{1,0:T(8,128)(2,1)S(1)} %collective-permute-done.8.refs_0_), channel_id=1, source_target_pairs={{0,1},{1,0},{2,3},{3,2},{4,5},{5,4},{6,7},{7,6},{8,9},{9,8},{10,11... | collective-permute-start | bytes 1572872 | tf_op jit(solution)/shard_map/ppermute | solution.py:119
  60.9 13.2 %copy-start.2 = (bf16[1,2048,768]{2,1,0:T(8,128)(2,1)S(1)}, bf16[1,2048,768]{2,1,0:T(8,128)(2,1)}, u32[]{:S(2)}) copy-start(bf16[1,2048,768]{2,1,0:T(8,128)(2,1)} %param.9) | copy-start | bytes 9437188
  60.9 9.3 %collective-permute-start.13 = (bf16[64,2048]{1,0:T(8,128)(2,1)S(1)}, bf16[64,2048]{1,0:T(8,128)(2,1)S(1)}, u32[]{:S(2)}, u32[]{:S(2)}) collective-permute-start(bf16[64,2048]{1,0:T(8,128)(2,1)S(1)} %slice.81), channel_id=1, source_target_pairs={{0,2},{1,3},{2,0},{3,1},{4,6},{5,7},{6,4},{7,5},{8,10},{9,11},{10,... | collective-permute-start | bytes 786440 | tf_op jit(solution)/shard_map/ppermute | solution.py:119
  62.2 8.4 %collective-permute-start.12 = (bf16[64,2048]{1,0:T(8,128)(2,1)S(1)}, bf16[64,2048]{1,0:T(8,128)(2,1)S(1)}, u32[]{:S(2)}, u32[]{:S(2)}) collective-permute-start(bf16[64,2048]{1,0:T(8,128)(2,1)S(1)} %slice.80), channel_id=1, source_target_pairs={{0,4},{1,5},{2,6},{3,7},{4,0},{5,1},{6,2},{7,3},{8,12},{9,13},{10,... | collective-permute-start | bytes 786440 | tf_op jit(solution)/shard_map/ppermute | solution.py:119
  70.7 15.1 %collective-permute-start.19 = (bf16[256,2048]{1,0:T(8,128)(2,1)S(1)}, bf16[256,2048]{1,0:T(8,128)(2,1)S(1)}, u32[]{:S(2)}, u32[]{:S(2)}) collective-permute-start(bf16[256,2048]{1,0:T(8,128)(2,1)S(1)} %get-tuple-element.81), channel_id=1, source_target_pairs={{0,1},{1,0},{2,3},{3,2},{4,5},{5,4},{6,7},{7,6},{8,9},{9,8},{10,11... | collective-permute-start | bytes 3145736 | tf_op jit(solution)/shard_map/ppermute | solution.py:119
  70.7 3.0 %collective-permute-start.17 = (bf16[64,2048]{1,0:T(8,128)(2,1)S(1)}, bf16[64,2048]{1,0:T(8,128)(2,1)S(1)}, u32[]{:S(2)}, u32[]{:S(2)}) collective-permute-start(bf16[64,2048]{1,0:T(8,128)(2,1)S(1)} %collective-permute-done.12.refs_1_), channel_id=1, source_target_pairs={{0,1},{1,0},{2,3},{3,2},{4,5},{5,4},{6,7},{7,6},{8,9},{9,8},{10,11... | collective-permute-start | bytes 786440 | tf_op jit(solution)/shard_map/ppermute | solution.py:119
  71.2 2.9 %collective-permute-start.18 = (bf16[64,2048]{1,0:T(8,128)(2,1)S(1)}, bf16[64,2048]{1,0:T(8,128)(2,1)S(1)}, u32[]{:S(2)}, u32[]{:S(2)}) collective-permute-start(bf16[64,2048]{1,0:T(8,128)(2,1)S(1)} %collective-permute-done.13.refs_2_), channel_id=1, source_target_pairs={{0,1},{1,0},{2,3},{3,2},{4,5},{5,4},{6,7},{7,6},{8,9},{9,8},{10,11... | collective-permute-start | bytes 786440 | tf_op jit(solution)/shard_map/ppermute | solution.py:119
  71.4 14.3 %collective-permute-start.20 = (bf16[128,2048]{1,0:T(8,128)(2,1)S(1)}, bf16[128,2048]{1,0:T(8,128)(2,1)S(1)}, u32[]{:S(2)}, u32[]{:S(2)}) collective-permute-start(bf16[128,2048]{1,0:T(8,128)(2,1)S(1)} %add_convert_fusion.4), channel_id=1, source_target_pairs={{0,2},{1,3},{2,0},{3,1},{4,6},{5,7},{6,4},{7,5},{8,10},{9,11},{10,... | collective-permute-start | bytes 1572872 | tf_op jit(solution)/shard_map/ppermute | solution.py:119
  72.4 13.3 %collective-permute-start.22 = (bf16[256,2048]{1,0:T(8,128)(2,1)S(1)}, bf16[256,2048]{1,0:T(8,128)(2,1)S(1)}, u32[]{:S(2)}, u32[]{:S(2)}) collective-permute-start(bf16[256,2048]{1,0:T(8,128)(2,1)S(1)} %get-tuple-element.87), channel_id=1, source_target_pairs={{0,1},{1,0},{2,3},{3,2},{4,5},{5,4},{6,7},{7,6},{8,9},{9,8},{10,11... | collective-permute-start | bytes 3145736 | tf_op jit(solution)/shard_map/ppermute | solution.py:119
  85.7 2.7 %collective-permute-start.21 = (bf16[256,2048]{1,0:T(8,128)(2,1)S(1)}, bf16[256,2048]{1,0:T(8,128)(2,1)S(1)}, u32[]{:S(2)}, u32[]{:S(2)}) collective-permute-start(bf16[256,2048]{1,0:T(8,128)(2,1)S(1)} %get-tuple-element.86), channel_id=1, source_target_pairs={{0,1},{1,0},{2,3},{3,2},{4,5},{5,4},{6,7},{7,6},{8,9},{9,8},{10,11... | collective-permute-start | bytes 3145736 | tf_op jit(solution)/shard_map/ppermute | solution.py:119
  85.7 16.2 %copy-start.13 = (bf16[256,2048]{1,0:T(8,128)(2,1)}, bf16[256,2048]{1,0:T(8,128)(2,1)S(1)}, u32[]{:S(2)}) copy-start(bf16[256,2048]{1,0:T(8,128)(2,1)S(1)} %collective-permute-done.22) | copy-start | bytes 3145732
  88.7 8.4 %collective-permute-start.24 = (bf16[64,2048]{1,0:T(8,128)(2,1)S(1)}, bf16[64,2048]{1,0:T(8,128)(2,1)S(1)}, u32[]{:S(2)}, u32[]{:S(2)}) collective-permute-start(bf16[64,2048]{1,0:T(8,128)(2,1)S(1)} %get-tuple-element.103), channel_id=1, source_target_pairs={{0,2},{1,3},{2,0},{3,1},{4,6},{5,7},{6,4},{7,5},{8,10},{9,11},{10,... | collective-permute-start | bytes 786440 | tf_op jit(solution)/shard_map/ppermute | solution.py:119
  89.6 8.1 %collective-permute-start.23 = (bf16[64,2048]{1,0:T(8,128)(2,1)S(1)}, bf16[64,2048]{1,0:T(8,128)(2,1)S(1)}, u32[]{:S(2)}, u32[]{:S(2)}) collective-permute-start(bf16[64,2048]{1,0:T(8,128)(2,1)S(1)} %get-tuple-element.104), channel_id=1, source_target_pairs={{0,4},{1,5},{2,6},{3,7},{4,0},{5,1},{6,2},{7,3},{8,12},{9,13},{10,... | collective-permute-start | bytes 786440 | tf_op jit(solution)/shard_map/ppermute | solution.py:119
  98.0 12.9 %collective-permute-start.26 = (bf16[128,2048]{1,0:T(8,128)(2,1)S(1)}, bf16[128,2048]{1,0:T(8,128)(2,1)S(1)}, u32[]{:S(2)}, u32[]{:S(2)}) collective-permute-start(bf16[128,2048]{1,0:T(8,128)(2,1)S(1)} %pad_maximum_fusion.1), channel_id=1, source_target_pairs={{0,2},{1,3},{2,0},{3,1},{4,6},{5,7},{6,4},{7,5},{8,10},{9,11},{10,... | collective-permute-start | bytes 1572872 | tf_op jit(solution)/shard_map/ppermute | solution.py:119
  99.2 18.7 %copy-start.10 = (bf16[320,768]{1,0:T(8,128)(2,1)S(1)}, bf16[320,768]{1,0:T(8,128)(2,1)}, u32[]{:S(2)}) copy-start(bf16[320,768]{1,0:T(8,128)(2,1)} %copy-done.9) | copy-start | bytes 1474564
  99.3 18.7 %copy-start.12 = (bf16[320,768]{1,0:T(8,128)(2,1)S(1)}, bf16[320,768]{1,0:T(8,128)(2,1)}, u32[]{:S(2)}) copy-start(bf16[320,768]{1,0:T(8,128)(2,1)} %copy-done.11) | copy-start | bytes 1474564
  99.3 12.6 %collective-permute-start.25 = (bf16[128,2048]{1,0:T(8,128)(2,1)S(1)}, bf16[128,2048]{1,0:T(8,128)(2,1)S(1)}, u32[]{:S(2)}, u32[]{:S(2)}) collective-permute-start(bf16[128,2048]{1,0:T(8,128)(2,1)S(1)} %pad_maximum_fusion), channel_id=1, source_target_pairs={{0,4},{1,5},{2,6},{3,7},{4,0},{5,1},{6,2},{7,3},{8,12},{9,13},{10,... | collective-permute-start | bytes 1572872 | tf_op jit(solution)/shard_map/ppermute | solution.py:119
  111.9 11.9 %collective-permute-start.27 = (bf16[128,2048]{1,0:T(8,128)(2,1)}, bf16[128,2048]{1,0:T(8,128)(2,1)}, u32[]{:S(2)}, u32[]{:S(2)}) collective-permute-start(bf16[128,2048]{1,0:T(8,128)(2,1)} %add_convert_fusion.2), channel_id=1, source_target_pairs={{0,2},{1,3},{2,0},{3,1},{4,6},{5,7},{6,4},{7,5},{8,10},{9,11},{10,... | collective-permute-start | bytes 1572872 | tf_op jit(solution)/shard_map/ppermute | solution.py:119
  112.7 21.4 %collective-permute-start.28 = (bf16[128,2048]{1,0:T(8,128)(2,1)}, bf16[128,2048]{1,0:T(8,128)(2,1)}, u32[]{:S(2)}, u32[]{:S(2)}) collective-permute-start(bf16[128,2048]{1,0:T(8,128)(2,1)} %add_convert_fusion.3), channel_id=1, source_target_pairs={{0,4},{1,5},{2,6},{3,7},{4,0},{5,1},{6,2},{7,3},{8,12},{9,13},{10,... | collective-permute-start | bytes 1572872 | tf_op jit(solution)/shard_map/ppermute | solution.py:119
  115.5 23.5 %collective-permute-start.29 = (bf16[128,2048]{1,0:T(8,128)(2,1)}, bf16[128,2048]{1,0:T(8,128)(2,1)}, u32[]{:S(2)}, u32[]{:S(2)}) collective-permute-start(bf16[128,2048]{1,0:T(8,128)(2,1)} %add_convert_fusion.1), channel_id=1, source_target_pairs={{0,8},{1,9},{2,10},{3,11},{4,12},{5,13},{6,14},{7,15},{8,0},{9,1},... | collective-permute-start | bytes 1572872 | tf_op jit(solution)/shard_map/ppermute | solution.py:119
  117.9 21.1 %copy-start.14 = (bf16[256,2048]{1,0:T(8,128)(2,1)S(1)}, bf16[256,2048]{1,0:T(8,128)(2,1)}, u32[]{:S(2)}) copy-start(bf16[256,2048]{1,0:T(8,128)(2,1)} %copy-done.13) | copy-start | bytes 3145732

commit v10 on v9

--- a/solution.py
+++ b/solution.py
@@ -140,41 +140,36 @@
 
     weight = weights_for_me(routes, probs, size)
     a0 = tokens
-    a1, low, b0, c0, weight = together(
-        pair(a0), far(a0[:half]), column(a0), sibling(a0), weight
-    )
+    a1, a2, b0, c0, weight = together(pair(a0), far(a0), column(a0), sibling(a0), weight)
+    a3 = pair(a2)
     b1 = column(a1)
-    high = far(a0[half:])
     d0 = sibling(b0)
     c1 = sibling(a1)
     keep0, give0, act0 = expert(0, a0, b0, c0, d0)
-    high, b1, c1, keep0, give0, act0 = together(high, b1, c1, keep0, give0, act0)
-    a2 = jnp.concatenate([low, high], axis=0)
-    a3 = pair(a2)
+    a3, b1, c1, keep0, give0, act0 = together(a3, b1, c1, keep0, give0, act0)
     b2 = column(a2)
+    b3_low = far(b1[:half])
     d1 = sibling(b1)
     c2 = sibling(a2)
+    got0 = sibling(give0)
     keep1, give1, act1 = expert(1, a1, b1, c1, d1)
-    a3, b2, c2, keep1, give1, act1 = together(a3, b2, c2, keep1, give1, act1)
-    b3_low = pair(b2[:half])
+    b2, b3_low, c2, got0, keep1, give1, act1 = together(b2, b3_low, c2, got0, keep1, give1, act1)
     b3_high = column(a3[half:])
     d2 = sibling(b2)
     c3 = sibling(a3)
+    d3_low = sibling(b3_low)
     got1 = sibling(give1)
     keep2, give2, act2 = expert(2, a2, b2, c2, d2)
-    b3_low, b3_high, c3, got1, keep2, give2, act2 = together(
-        b3_low, b3_high, c3, got1, keep2, give2, act2
-    )
-    d3_low = sibling(b3_low)
+    b3_high, c3, d3_low, got1, keep2, give2, act2 = together(
+        b3_high, c3, d3_low, got1, keep2, give2, act2
+    )
     d3_high = sibling(b3_high)
+    got2 = sibling(give2)
     came1 = column(summed(keep1[tok:], got1[tok:]))
-    got2 = sibling(give2)
     keep3, give3, act3 = expert(3, a3, b3_low, b3_high, c3, d3_low, d3_high)
-
-    keep3, give3, act3, got2, came1 = together(keep3, give3, act3, got2, came1)
-    got3 = sibling(give3)
-    got0 = sibling(give0)
-    got3, got0 = together(got3, got0)
+    keep3, give3, act3, got2 = together(keep3, give3, act3, got2)
+
+    got3, came1 = together(sibling(give3), came1)
     low = pair(summed(keep3[tok : tok + half], got3[tok : tok + half]))
     high = column(summed(keep3[tok + half :], got3[tok + half :]))
     low, high = together(low, high)
@@ -191,10 +186,10 @@
     near1 = summed(keep1[:tok], got1[:tok], came1)
     side0 = summed(keep0[tok:], got0[tok:])
     far3, side2, near1, side0 = together(pair(far3), column(side2), near1, side0)
-    last2 = far(summed(keep2[:tok], got2[:tok], far3, side2))
-    last1 = pair(near1)
-    last0 = column(side0)
-    mixed = summed(keep0[:tok], got0[:tok], last0, last1, last2)
+    far2, near1, side0 = together(
+        summed(keep2[:tok], got2[:tok], far3, side2), near1, side0
+    )
+    mixed = summed(keep0[:tok], got0[:tok], far(far2), pair(near1), column(side0))
 
     acts = jnp.concatenate([act0, act1, act2, act3], axis=0)
     count = jnp.minimum(jnp.sum((weight >= 0.0).astype(jnp.float32)), float(capacity))

time: 142 us -> 153 us (1.077)
  waiting for transfers between devices: 49.2 us -> 57 us
  blocking collectives: 13.9 us -> 21.3 us
  starting transfers between devices: 26.9 us -> 22.6 us
    ppermute x30 -> x29, waiting for transfers between devices: 49.2 us -> 57 us  [swapped(): return lax.ppermute(array, 'expert', [(i, i ^ bit) for i in range(size)])]
    all_to_all x1, blocking collectives: 13.9 us -> 21.3 us  [weights_for_me(): lax.all_to_all(mine, 'expert', split_axis=0, concat_axis=0, tiled=True)]
    ppermute x30 -> x29, starting transfers between devices: 26.9 us -> 22.6 us  [swapped(): return lax.ppermute(array, 'expert', [(i, i ^ bit) for i in range(size)])]
    unnamed x31 -> x34, local copies, waits for them, and re-layouts: 10.4 us -> 12.3 us
    slice x2 -> x1, local copies, waits for them, and re-layouts: 1.79 us -> 0.02 us  [staged(): b3_low = far(b1[:half])]
  transfers between devices with their start and end apart: 30 -> 29, of which waited for: 14 -> 12; matrix products, arithmetic and copies ran while one was open for 8% -> 5% of each run, Pallas kernels for 18% -> 17%
where the time goes in v10:
time: 153 us; the launch traced here: 152 us
  waiting for transfers between devices  57 us (37%)
  Pallas kernels  25.6 us (17%)
  starting transfers between devices  22.6 us (15%)
  blocking collectives  21.3 us (14%)
  local copies, waits for them, and re-layouts  12.4 us (8%)
  other arithmetic  8.48 us (6%)
  matrix products  3.17 us (2%)
    ppermute x29, waiting for transfers between devices, swapped(): return lax.ppermute(array, 'expert', [(i, i ^ bit) for i in range(size)])  57 us
    pallas_call x4, Pallas kernels, plane_pass(): pl.pallas_call(functools.partial(plane_kernel, capacity, k, len(xs)), out...  25.6 us
    ppermute x29, starting transfers between devices, swapped(): return lax.ppermute(array, 'expert', [(i, i ^ bit) for i in range(size)])  22.6 us
    all_to_all x1, blocking collectives, weights_for_me(): lax.all_to_all(mine, 'expert', split_axis=0, concat_axis=0, tiled=True)  21.3 us
    unnamed x34, local copies, waits for them, and re-layouts  12.3 us
    convert_element_type x8, other arithmetic, summed(): return total.astype(jnp.bfloat16)  6.39 us
    dot_general x1, matrix products, gram_of(): lax.dot_general(rows, rows, (((0,), (0,)), ((), ())), preferred_element_t...  3.17 us
  transfers between devices with their start and end apart: 29, of which 12 were waited for; matrix products, arithmetic and copies ran while one was open for 5% of the time, Pallas kernels for 17%

profile of v10, /device:TPU:0, one launch (start us, length us, event | category | flops | bytes accessed | tf_op | source)
XLA Modules:
  0.0 152.1 jit_solution(9540012920631667925)
XLA Ops:
  0.6 3.1 %collective-permute-start = (bf16[128,2048]{1,0:T(8,128)(2,1)}, bf16[128,2048]{1,0:T(8,128)(2,1)S(1)}, u32[]{:S(2)}, u32[]{:S(2)}) collective-permute-start(bf16[128,2048]{1,0:T(8,128)(2,1)} %refs_0_.1), channel_id=1, source_target_pairs={{0,4},{1,5},{2,6},{3,7},{4,0},{5,1},{6,2},{7,3},{8,12},{9,13},{10,... | collective-permute-start | bytes 1572872 | tf_op jit(solution)/shard_map/ppermute | solution.py:119
  3.7 2.6 %collective-permute-start.1 = (bf16[128,2048]{1,0:T(8,128)(2,1)}, bf16[128,2048]{1,0:T(8,128)(2,1)S(1)}, u32[]{:S(2)}, u32[]{:S(2)}) collective-permute-start(bf16[128,2048]{1,0:T(8,128)(2,1)} %refs_0_.1), channel_id=1, source_target_pairs={{0,8},{1,9},{2,10},{3,11},{4,12},{5,13},{6,14},{7,15},{8,0},{9,1},... | collective-permute-start | bytes 1572872 | tf_op jit(solution)/shard_map/ppermute | solution.py:119
  6.3 1.5 collective-permute-start.2
  7.8 0.7 fusion.10
  8.5 0.7 select_reduce_fusion
  9.3 21.3 %all_to_all.9 = f32[16,1,128]{2,1,0:T(1,128)S(1)} all-to-all(f32[16,1,128]{2,1,0:T(1,128)S(1)} %bitcast.44), channel_id=1, replica_groups=mesh['parts'=2,'expert'=16] {'expert'}, dimensions={0} | all-to-all | bytes 16384 | tf_op jit(solution)/shard_map/all_to_all | solution.py:28
  30.6 0.8 copy-done.7
  31.4 0.8 copy-done.5
  32.2 0.6 collective-permute-start.4
  32.8 0.6 collective-permute-start.5
  33.3 0.1 stack.67.spots
  33.5 0.8 copy-done.9
  34.3 1.9 %copy-done = bf16[1,2048,768]{2,1,0:T(8,128)(2,1)S(1)} copy-done((bf16[1,2048,768]{2,1,0:T(8,128)(2,1)S(1)}, bf16[1,2048,768]{2,1,0:T(8,128)(2,1)}, u32[]{:S(2)}) %copy-start) | copy-done | bytes 3145752
  36.2 1.9 %copy-done.2 = bf16[1,2048,768]{2,1,0:T(8,128)(2,1)S(1)} copy-done((bf16[1,2048,768]{2,1,0:T(8,128)(2,1)S(1)}, bf16[1,2048,768]{2,1,0:T(8,128)(2,1)}, u32[]{:S(2)}) %copy-start.2) | copy-done | bytes 3145752
  38.0 1.9 %copy-done.3 = bf16[1,768,2048]{2,1,0:T(8,128)(2,1)S(1)} copy-done((bf16[1,768,2048]{2,1,0:T(8,128)(2,1)S(1)}, bf16[1,768,2048]{2,1,0:T(8,128)(2,1)}, u32[]{:S(2)}) %copy-start.3) | copy-done | bytes 3145752
  39.9 1.0 copy-done.4
  41.0 1.0 copy-done.6
  42.0 1.0 copy-done.8
  43.1 1.0 copy-done.10
  44.1 6.2 %shard_map.77 = (bf16[256,2048]{1,0:T(8,128)(2,1)S(1)}, bf16[256,2048]{1,0:T(8,128)(2,1)S(1)}, bf16[320,768]{1,0:T(8,128)(2,1)S(1)}) custom-call(s32[16]{0:T(128)S(1)} %stack.67.spots, f32[16,128]{1,0:T(8,128)S(1)} %bitcast.27, bf16[128,2048]{1,0:T(8,128)(2,1)S(1)} %copy-done.4, bf16[128,2048]{1,0:T(8,128)(2,1)S(1)} %copy-done.6, ...), custom_call_target="tpu_custom_call" | custom-call | flops 4362076160 | bytes 13631488 | tf_op jit(solution)/shard_map/pallas_call | solution.py:92
  50.4 0.6 collective-permute-start.11
  50.9 0.1 collective-permute-start.12
  51.0 1.4 collective-permute-start.8
  52.5 0.2 collective-permute-start.10
  52.7 2.5 %collective-permute-start.9 = (bf16[64,2048]{1,0:T(8,128)(2,1)S(1)}, bf16[64,2048]{1,0:T(8,128)(2,1)S(1)}, u32[]{:S(2)}, u32[]{:S(2)}) collective-permute-start(bf16[64,2048]{1,0:T(8,128)(2,1)S(1)} %slice.72), channel_id=1, source_target_pairs={{0,8},{1,9},{2,10},{3,11},{4,12},{5,13},{6,14},{7,15},{8,0},{9,1},... | collective-permute-start | bytes 786440 | tf_op jit(solution)/shard_map/ppermute | solution.py:119
  55.2 6.7 %shard_map.78 = (bf16[256,2048]{1,0:T(8,128)(2,1)S(1)}, bf16[256,2048]{1,0:T(8,128)(2,1)S(1)}, bf16[320,768]{1,0:T(8,128)(2,1)S(1)}) custom-call(s32[16]{0:T(128)S(1)} %stack.67.spots, f32[16,128]{1,0:T(8,128)S(1)} %bitcast.28, bf16[128,2048]{1,0:T(8,128)(2,1)S(1)} %collective-permute-done.refs_0_, bf16[128,2048]{1,0:T(8,128)(2,1)S(1)} %collective-permute-done.5.refs_1_, ...), custom_call_target="tpu_custom_call" | custom-call | flops 4362076160 | bytes 13631488 | tf_op jit(solution)/shard_map/pallas_call | solution.py:92
  61.9 3.4 %collective-permute-done.8.refs_1_ = bf16[128,2048]{1,0:T(8,128)(2,1)S(1)} collective-permute-done((bf16[128,2048]{1,0:T(8,128)(2,1)S(1)}, bf16[128,2048]{1,0:T(8,128)(2,1)S(1)}, u32[]{:S(2)}, u32[]{:S(2)}) %collective-permute-start.8) | collective-permute-done | bytes 524320 | tf_op jit(solution)/shard_map/ppermute | solution.py:119
  65.3 2.5 %collective-permute-done.9.refs_1_ = bf16[64,2048]{1,0:T(8,128)(2,1)S(1)} collective-permute-done((bf16[64,2048]{1,0:T(8,128)(2,1)S(1)}, bf16[64,2048]{1,0:T(8,128)(2,1)S(1)}, u32[]{:S(2)}, u32[]{:S(2)}) %collective-permute-start.9) | collective-permute-done | bytes 262176 | tf_op jit(solution)/shard_map/ppermute | solution.py:119
  67.8 0.5 collective-permute-start.17
  68.4 0.6 collective-permute-start.13
  69.1 0.2 collective-permute-start.15
  69.2 2.0 %collective-permute-done.17.refs_3_ = bf16[128,2048]{1,0:T(8,128)(2,1)S(1)} collective-permute-done((bf16[128,2048]{1,0:T(8,128)(2,1)S(1)}, bf16[128,2048]{1,0:T(8,128)(2,1)S(1)}, u32[]{:S(2)}, u32[]{:S(2)}) %collective-permute-start.17) | collective-permute-done | bytes 524320 | tf_op jit(solution)/shard_map/ppermute | solution.py:119
  71.2 6.4 %shard_map.79 = (bf16[256,2048]{1,0:T(8,128)(2,1)S(1)}, bf16[256,2048]{1,0:T(8,128)(2,1)S(1)}, bf16[320,768]{1,0:T(8,128)(2,1)S(1)}) custom-call(s32[16]{0:T(128)S(1)} %stack.67.spots, f32[16,128]{1,0:T(8,128)S(1)} %bitcast.29, bf16[128,2048]{1,0:T(8,128)(2,1)S(1)} %collective-permute-done.1.refs_0_, bf16[128,2048]{1,0:T(8,128)(2,1)S(1)} %collective-permute-done.8.refs_1_, ...), custom_call_target="tpu_custom_call" | custom-call | flops 4362076160 | bytes 13631488 | tf_op jit(solution)/shard_map/pallas_call | solution.py:92
  77.7 0.2 collective-permute-start.19
  77.9 0.4 collective-permute-start.18
  78.2 2.5 %collective-permute-done.18.refs_5_ = bf16[64,2048]{1,0:T(8,128)(2,1)S(1)} collective-permute-done((bf16[64,2048]{1,0:T(8,128)(2,1)S(1)}, bf16[64,2048]{1,0:T(8,128)(2,1)S(1)}, u32[]{:S(2)}, u32[]{:S(2)}) %collective-permute-start.18) | collective-permute-done | bytes 262176 | tf_op jit(solution)/shard_map/ppermute | solution.py:119
  80.8 6.2 %shard_map.80 = (bf16[256,2048]{1,0:T(8,128)(2,1)S(1)}, bf16[256,2048]{1,0:T(8,128)(2,1)S(1)}, bf16[320,768]{1,0:T(8,128)(2,1)S(1)}) custom-call(s32[16]{0:T(128)S(1)} %stack.67.spots, f32[16,128]{1,0:T(8,128)S(1)} %bitcast.30, bf16[128,2048]{1,0:T(8,128)(2,1)S(1)} %collective-permute-done.4.refs_0_, bf16[64,2048]{1,0:T(8,128)(2,1)S(1)} %collective-permute-done.9.refs_1_, ...), custom_call_target="tpu_custom_call" | custom-call | flops 4362076160 | bytes 13631488 | tf_op jit(solution)/shard_map/pallas_call | solution.py:92
  87.0 0.2 collective-permute-start.20
  87.2 0.2 add_convert_fusion.4
  87.4 0.7 collective-permute-start.21
  88.0 13.6 %collective-permute-done.21 = bf16[128,2048]{1,0:T(8,128)(2,1)S(1)} collective-permute-done((bf16[128,2048]{1,0:T(8,128)(2,1)S(1)}, bf16[128,2048]{1,0:T(8,128)(2,1)S(1)}, u32[]{:S(2)}, u32[]{:S(2)}) %collective-permute-start.21) | collective-permute-done | bytes 524320 | tf_op jit(solution)/shard_map/ppermute | solution.py:119
  101.7 0.3 add_convert_fusion.10
  101.9 0.1 collective-permute-start.22
  102.0 0.6 collective-permute-start.23
  102.7 7.1 %collective-permute-done.22 = bf16[64,2048]{1,0:T(8,128)(2,1)S(1)} collective-permute-done((bf16[64,2048]{1,0:T(8,128)(2,1)S(1)}, bf16[64,2048]{1,0:T(8,128)(2,1)S(1)}, u32[]{:S(2)}, u32[]{:S(2)}) %collective-permute-start.22) | collective-permute-done | bytes 262176 | tf_op jit(solution)/shard_map/ppermute | solution.py:119
  109.8 0.1 collective-permute-done.23
  109.8 0.1 add_convert_fusion.7
  110.0 1.7 %collective-permute-start.24 = (bf16[128,2048]{1,0:T(8,128)(2,1)S(1)}, bf16[128,2048]{1,0:T(8,128)(2,1)S(1)}, u32[]{:S(2)}, u32[]{:S(2)}) collective-permute-start(bf16[128,2048]{1,0:T(8,128)(2,1)S(1)} %pad_maximum_fusion), channel_id=1, source_target_pairs={{0,4},{1,5},{2,6},{3,7},{4,0},{5,1},{6,2},{7,3},{8,12},{9,13},{10,... | collective-permute-start | bytes 1572872 | tf_op jit(solution)/shard_map/ppermute | solution.py:119
  111.7 0.2 add_convert_fusion.6
  112.0 0.6 collective-permute-start.25
  112.6 0.9 add_convert_fusion.2
  113.5 1.1 add_convert_fusion.3
  114.6 7.9 %collective-permute-done.24 = bf16[128,2048]{1,0:T(8,128)(2,1)S(1)} collective-permute-done((bf16[128,2048]{1,0:T(8,128)(2,1)S(1)}, bf16[128,2048]{1,0:T(8,128)(2,1)S(1)}, u32[]{:S(2)}, u32[]{:S(2)}) %collective-permute-start.24) | collective-permute-done | bytes 524320 | tf_op jit(solution)/shard_map/ppermute | solution.py:119
  122.5 1.4 collective-permute-done.25
  123.9 1.1 add_convert_fusion.1
  125.1 0.6 collective-permute-start.28
  125.7 0.6 collective-permute-start.27
  126.3 2.3 %collective-permute-start.26 = (bf16[128,2048]{1,0:T(8,128)(2,1)}, bf16[128,2048]{1,0:T(8,128)(2,1)}, u32[]{:S(2)}, u32[]{:S(2)}) collective-permute-start(bf16[128,2048]{1,0:T(8,128)(2,1)} %add_convert_fusion.1), channel_id=1, source_target_pairs={{0,8},{1,9},{2,10},{3,11},{4,12},{5,13},{6,14},{7,15},{8,0},{9,1},... | collective-permute-start | bytes 1572872 | tf_op jit(solution)/shard_map/ppermute | solution.py:119
  128.6 0.6 convert_reduce_fusion
  129.8 3.2 %multiply_bitcast_fusion = f32[1,768,768]{2,1,0:T(8,128)} fusion(f32[]{:T(128)S(6)} %div.24, bf16[320,768]{1,0:T(8,128)(2,1)S(1)} %get-tuple-element.86, bf16[320,768]{1,0:T(8,128)(2,1)S(1)} %get-tuple-element.78, bf16[320,768]{1,0:T(8,128)(2,1)S(1)} %copy-done.14, bf16[320,768]{1,0:T(8,128)(2,1)S(1)} %copy-done.12), kind=kOutput, calls=%fused_computation | convolution fusion | flops 1518403584 | bytes 4325380 | tf_op jit(solution)/shard_map/dot_general | solution.py:12
  133.0 3.4 %collective-permute-done.28 = bf16[128,2048]{1,0:T(8,128)(2,1)} collective-permute-done((bf16[128,2048]{1,0:T(8,128)(2,1)}, bf16[128,2048]{1,0:T(8,128)(2,1)}, u32[]{:S(2)}, u32[]{:S(2)}) %collective-permute-start.28) | collective-permute-done | bytes 524320 | tf_op jit(solution)/shard_map/ppermute | solution.py:119
  136.4 11.4 %collective-permute-done.27 = bf16[128,2048]{1,0:T(8,128)(2,1)} collective-permute-done((bf16[128,2048]{1,0:T(8,128)(2,1)}, bf16[128,2048]{1,0:T(8,128)(2,1)}, u32[]{:S(2)}, u32[]{:S(2)}) %collective-permute-start.27) | collective-permute-done | bytes 524320 | tf_op jit(solution)/shard_map/ppermute | solution.py:119
  147.7 1.8 %collective-permute-done.26 = bf16[128,2048]{1,0:T(8,128)(2,1)} collective-permute-done((bf16[128,2048]{1,0:T(8,128)(2,1)}, bf16[128,2048]{1,0:T(8,128)(2,1)}, u32[]{:S(2)}, u32[]{:S(2)}) %collective-permute-start.26) | collective-permute-done | bytes 524320 | tf_op jit(solution)/shard_map/ppermute | solution.py:119
  149.5 2.6 %add_convert_fusion = bf16[128,2048]{1,0:T(8,128)(2,1)} fusion(bf16[128,2048]{1,0:T(8,128)(2,1)} %collective-permute-done.28, bf16[128,2048]{1,0:T(8,128)(2,1)} %collective-permute-done.27, bf16[128,2048]{1,0:T(8,128)(2,1)} %collective-permute-done.26, bf16[256,2048]{1,0:T(8,128)(2,1)S(1)} %copy-done.16, bf16[256,2048]{1,0:T(8,128)(2,1)S(1)} %get-tuple-element.87), kind=kLoop, calls=%fused_computation.9 | loop fusion | flops 2621440 | bytes 3145728 | tf_op jit(solution)/shard_map/convert_element_type | solution.py:35
  (51 shorter events, 0.3 us)
Async XLA Ops:
  0.6 29.9 %collective-permute-start = (bf16[128,2048]{1,0:T(8,128)(2,1)}, bf16[128,2048]{1,0:T(8,128)(2,1)S(1)}, u32[]{:S(2)}, u32[]{:S(2)}) collective-permute-start(bf16[128,2048]{1,0:T(8,128)(2,1)} %refs_0_.1), channel_id=1, source_target_pairs={{0,4},{1,5},{2,6},{3,7},{4,0},{5,1},{6,2},{7,3},{8,12},{9,13},{10,... | collective-permute-start | bytes 1572872 | tf_op jit(solution)/shard_map/ppermute | solution.py:119
  3.7 26.9 %collective-permute-start.1 = (bf16[128,2048]{1,0:T(8,128)(2,1)}, bf16[128,2048]{1,0:T(8,128)(2,1)S(1)}, u32[]{:S(2)}, u32[]{:S(2)}) collective-permute-start(bf16[128,2048]{1,0:T(8,128)(2,1)} %refs_0_.1), channel_id=1, source_target_pairs={{0,8},{1,9},{2,10},{3,11},{4,12},{5,13},{6,14},{7,15},{8,0},{9,1},... | collective-permute-start | bytes 1572872 | tf_op jit(solution)/shard_map/ppermute | solution.py:119
  6.3 24.3 %collective-permute-start.2 = (bf16[128,2048]{1,0:T(8,128)(2,1)}, bf16[128,2048]{1,0:T(8,128)(2,1)S(1)}, u32[]{:S(2)}, u32[]{:S(2)}) collective-permute-start(bf16[128,2048]{1,0:T(8,128)(2,1)} %refs_0_.1), channel_id=1, source_target_pairs={{0,2},{1,3},{2,0},{3,1},{4,6},{5,7},{6,4},{7,5},{8,10},{9,11},{10,... | collective-permute-start | bytes 1572872 | tf_op jit(solution)/shard_map/ppermute | solution.py:119
  7.8 22.8 %collective-permute-start.3 = (bf16[128,2048]{1,0:T(8,128)(2,1)}, bf16[128,2048]{1,0:T(8,128)(2,1)S(1)}, u32[]{:S(2)}, u32[]{:S(2)}) collective-permute-start(bf16[128,2048]{1,0:T(8,128)(2,1)} %refs_0_.1), channel_id=1, source_target_pairs={{0,1},{1,0},{2,3},{3,2},{4,5},{5,4},{6,7},{7,6},{8,9},{9,8},{10,11... | collective-permute-start | bytes 1572872 | tf_op jit(solution)/shard_map/ppermute | solution.py:119
  30.6 0.8 copy-start.7
  31.4 2.0 %collective-permute-start.7 = (bf16[128,2048]{1,0:T(8,128)(2,1)S(1)}, bf16[128,2048]{1,0:T(8,128)(2,1)S(1)}, u32[]{:S(2)}, u32[]{:S(2)}) collective-permute-start(bf16[128,2048]{1,0:T(8,128)(2,1)S(1)} %collective-permute-done.2.refs_1_), channel_id=1, source_target_pairs={{0,1},{1,0},{2,3},{3,2},{4,5},{5,4},{6,7},{7,6},{8,9},{9,8},{10,11... | collective-permute-start | bytes 1572872 | tf_op jit(solution)/shard_map/ppermute | solution.py:119
  31.4 0.8 copy-start.5
  32.2 18.1 %collective-permute-start.4 = (bf16[128,2048]{1,0:T(8,128)(2,1)S(1)}, bf16[128,2048]{1,0:T(8,128)(2,1)S(1)}, u32[]{:S(2)}, u32[]{:S(2)}) collective-permute-start(bf16[128,2048]{1,0:T(8,128)(2,1)S(1)} %collective-permute-done.1.refs_0_), channel_id=1, source_target_pairs={{0,4},{1,5},{2,6},{3,7},{4,0},{5,1},{6,2},{7,3},{8,12},{9,13},{10,... | collective-permute-start | bytes 1572872 | tf_op jit(solution)/shard_map/ppermute | solution.py:119
  32.8 17.6 %collective-permute-start.5 = (bf16[128,2048]{1,0:T(8,128)(2,1)S(1)}, bf16[128,2048]{1,0:T(8,128)(2,1)S(1)}, u32[]{:S(2)}, u32[]{:S(2)}) collective-permute-start(bf16[128,2048]{1,0:T(8,128)(2,1)S(1)} %collective-permute-done.refs_0_), channel_id=1, source_target_pairs={{0,2},{1,3},{2,0},{3,1},{4,6},{5,7},{6,4},{7,5},{8,10},{9,11},{10,... | collective-permute-start | bytes 1572872 | tf_op jit(solution)/shard_map/ppermute | solution.py:119
  33.3 17.0 %collective-permute-start.6 = (bf16[128,2048]{1,0:T(8,128)(2,1)S(1)}, bf16[128,2048]{1,0:T(8,128)(2,1)}, u32[]{:S(2)}, u32[]{:S(2)}) collective-permute-start(bf16[128,2048]{1,0:T(8,128)(2,1)S(1)} %collective-permute-done.refs_0_), channel_id=1, source_target_pairs={{0,1},{1,0},{2,3},{3,2},{4,5},{5,4},{6,7},{7,6},{8,9},{9,8},{10,11... | collective-permute-start | bytes 1572872 | tf_op jit(solution)/shard_map/ppermute | solution.py:119
  33.4 0.8 copy-start.9
  34.3 1.9 %copy-start = (bf16[1,2048,768]{2,1,0:T(8,128)(2,1)S(1)}, bf16[1,2048,768]{2,1,0:T(8,128)(2,1)}, u32[]{:S(2)}) copy-start(bf16[1,2048,768]{2,1,0:T(8,128)(2,1)} %param.9) | copy-start | bytes 9437188
  36.2 1.9 %copy-start.2 = (bf16[1,2048,768]{2,1,0:T(8,128)(2,1)S(1)}, bf16[1,2048,768]{2,1,0:T(8,128)(2,1)}, u32[]{:S(2)}) copy-start(bf16[1,2048,768]{2,1,0:T(8,128)(2,1)} %param.10) | copy-start | bytes 9437188
  38.0 1.9 %copy-start.3 = (bf16[1,768,2048]{2,1,0:T(8,128)(2,1)S(1)}, bf16[1,768,2048]{2,1,0:T(8,128)(2,1)}, u32[]{:S(2)}) copy-start(bf16[1,768,2048]{2,1,0:T(8,128)(2,1)} %param.11) | copy-start | bytes 9437188
  39.9 1.0 copy-start.4
  41.0 1.0 copy-start.6
  42.0 1.0 copy-start.8
  43.1 1.0 copy-start.10
  50.3 4.9 %copy-start.11 = (bf16[320,768]{1,0:T(8,128)(2,1)}, bf16[320,768]{1,0:T(8,128)(2,1)S(1)}, u32[]{:S(2)}) copy-start(bf16[320,768]{1,0:T(8,128)(2,1)S(1)} %get-tuple-element.62) | copy-start | bytes 1474564
  50.4 17.4 %collective-permute-start.11 = (bf16[256,2048]{1,0:T(8,128)(2,1)S(1)}, bf16[256,2048]{1,0:T(8,128)(2,1)S(1)}, u32[]{:S(2)}, u32[]{:S(2)}) collective-permute-start(bf16[256,2048]{1,0:T(8,128)(2,1)S(1)} %get-tuple-element.64), channel_id=1, source_target_pairs={{0,1},{1,0},{2,3},{3,2},{4,5},{5,4},{6,7},{7,6},{8,9},{9,8},{10,11... | collective-permute-start | bytes 3145736 | tf_op jit(solution)/shard_map/ppermute | solution.py:119
  50.9 4.2 %collective-permute-start.12 = (bf16[128,2048]{1,0:T(8,128)(2,1)S(1)}, bf16[128,2048]{1,0:T(8,128)(2,1)S(1)}, u32[]{:S(2)}, u32[]{:S(2)}) collective-permute-start(bf16[128,2048]{1,0:T(8,128)(2,1)S(1)} %collective-permute-done.5.refs_1_), channel_id=1, source_target_pairs={{0,1},{1,0},{2,3},{3,2},{4,5},{5,4},{6,7},{7,6},{8,9},{9,8},{10,11... | collective-permute-start | bytes 1572872 | tf_op jit(solution)/shard_map/ppermute | solution.py:119
  51.0 14.3 %collective-permute-start.8 = (bf16[128,2048]{1,0:T(8,128)(2,1)S(1)}, bf16[128,2048]{1,0:T(8,128)(2,1)S(1)}, u32[]{:S(2)}, u32[]{:S(2)}) collective-permute-start(bf16[128,2048]{1,0:T(8,128)(2,1)S(1)} %collective-permute-done.1.refs_0_), channel_id=1, source_target_pairs={{0,2},{1,3},{2,0},{3,1},{4,6},{5,7},{6,4},{7,5},{8,10},{9,11},{10,... | collective-permute-start | bytes 1572872 | tf_op jit(solution)/shard_map/ppermute | solution.py:119
  52.5 12.8 %collective-permute-start.10 = (bf16[128,2048]{1,0:T(8,128)(2,1)S(1)}, bf16[128,2048]{1,0:T(8,128)(2,1)S(1)}, u32[]{:S(2)}, u32[]{:S(2)}) collective-permute-start(bf16[128,2048]{1,0:T(8,128)(2,1)S(1)} %collective-permute-done.1.refs_0_), channel_id=1, source_target_pairs={{0,1},{1,0},{2,3},{3,2},{4,5},{5,4},{6,7},{7,6},{8,9},{9,8},{10,11... | collective-permute-start | bytes 1572872 | tf_op jit(solution)/shard_map/ppermute | solution.py:119
  52.7 15.1 %collective-permute-start.9 = (bf16[64,2048]{1,0:T(8,128)(2,1)S(1)}, bf16[64,2048]{1,0:T(8,128)(2,1)S(1)}, u32[]{:S(2)}, u32[]{:S(2)}) collective-permute-start(bf16[64,2048]{1,0:T(8,128)(2,1)S(1)} %slice.72), channel_id=1, source_target_pairs={{0,8},{1,9},{2,10},{3,11},{4,12},{5,13},{6,14},{7,15},{8,0},{9,1},... | collective-permute-start | bytes 786440 | tf_op jit(solution)/shard_map/ppermute | solution.py:119
  61.9 7.3 %copy-start.13 = (bf16[320,768]{1,0:T(8,128)(2,1)}, bf16[320,768]{1,0:T(8,128)(2,1)S(1)}, u32[]{:S(2)}) copy-start(bf16[320,768]{1,0:T(8,128)(2,1)S(1)} %get-tuple-element.69) | copy-start | bytes 1474564
  67.8 44.8 %copy-start.15 = (bf16[256,2048]{1,0:T(8,128)(2,1)}, bf16[256,2048]{1,0:T(8,128)(2,1)S(1)}, u32[]{:S(2)}) copy-start(bf16[256,2048]{1,0:T(8,128)(2,1)S(1)} %collective-permute-done.11) | copy-start | bytes 3145732
  67.8 9.9 %collective-permute-start.16 = (bf16[256,2048]{1,0:T(8,128)(2,1)S(1)}, bf16[256,2048]{1,0:T(8,128)(2,1)S(1)}, u32[]{:S(2)}, u32[]{:S(2)}) collective-permute-start(bf16[256,2048]{1,0:T(8,128)(2,1)S(1)} %get-tuple-element.72), channel_id=1, source_target_pairs={{0,1},{1,0},{2,3},{3,2},{4,5},{5,4},{6,7},{7,6},{8,9},{9,8},{10,11... | collective-permute-start | bytes 3145736 | tf_op jit(solution)/shard_map/ppermute | solution.py:119
  67.8 3.4 %collective-permute-start.17 = (bf16[128,2048]{1,0:T(8,128)(2,1)S(1)}, bf16[128,2048]{1,0:T(8,128)(2,1)S(1)}, u32[]{:S(2)}, u32[]{:S(2)}) collective-permute-start(bf16[128,2048]{1,0:T(8,128)(2,1)S(1)} %collective-permute-done.8.refs_1_), channel_id=1, source_target_pairs={{0,1},{1,0},{2,3},{3,2},{4,5},{5,4},{6,7},{7,6},{8,9},{9,8},{10,11... | collective-permute-start | bytes 1572872 | tf_op jit(solution)/shard_map/ppermute | solution.py:119
  68.3 9.3 %collective-permute-start.14 = (bf16[128,2048]{1,0:T(8,128)(2,1)S(1)}, bf16[128,2048]{1,0:T(8,128)(2,1)S(1)}, u32[]{:S(2)}, u32[]{:S(2)}) collective-permute-start(bf16[128,2048]{1,0:T(8,128)(2,1)S(1)} %collective-permute-done.4.refs_0_), channel_id=1, source_target_pairs={{0,1},{1,0},{2,3},{3,2},{4,5},{5,4},{6,7},{7,6},{8,9},{9,8},{10,11... | collective-permute-start | bytes 1572872 | tf_op jit(solution)/shard_map/ppermute | solution.py:119
  68.4 12.4 %copy-start.1 = (bf16[1,2048,768]{2,1,0:T(8,128)(2,1)S(1)}, bf16[1,2048,768]{2,1,0:T(8,128)(2,1)}, u32[]{:S(2)}) copy-start(bf16[1,2048,768]{2,1,0:T(8,128)(2,1)} %param.9) | copy-start | bytes 9437188
  68.4 9.2 %collective-permute-start.13 = (bf16[64,2048]{1,0:T(8,128)(2,1)S(1)}, bf16[64,2048]{1,0:T(8,128)(2,1)S(1)}, u32[]{:S(2)}, u32[]{:S(2)}) collective-permute-start(bf16[64,2048]{1,0:T(8,128)(2,1)S(1)} %slice.73), channel_id=1, source_target_pairs={{0,2},{1,3},{2,0},{3,1},{4,6},{5,7},{6,4},{7,5},{8,10},{9,11},{10,... | collective-permute-start | bytes 786440 | tf_op jit(solution)/shard_map/ppermute | solution.py:119
  69.1 8.6 %collective-permute-start.15 = (bf16[64,2048]{1,0:T(8,128)(2,1)S(1)}, bf16[64,2048]{1,0:T(8,128)(2,1)S(1)}, u32[]{:S(2)}, u32[]{:S(2)}) collective-permute-start(bf16[64,2048]{1,0:T(8,128)(2,1)S(1)} %collective-permute-done.9.refs_1_), channel_id=1, source_target_pairs={{0,1},{1,0},{2,3},{3,2},{4,5},{5,4},{6,7},{7,6},{8,9},{9,8},{10,11... | collective-permute-start | bytes 786440 | tf_op jit(solution)/shard_map/ppermute | solution.py:119
  77.7 9.4 %collective-permute-start.19 = (bf16[256,2048]{1,0:T(8,128)(2,1)S(1)}, bf16[256,2048]{1,0:T(8,128)(2,1)S(1)}, u32[]{:S(2)}, u32[]{:S(2)}) collective-permute-start(bf16[256,2048]{1,0:T(8,128)(2,1)S(1)} %get-tuple-element.85), channel_id=1, source_target_pairs={{0,1},{1,0},{2,3},{3,2},{4,5},{5,4},{6,7},{7,6},{8,9},{9,8},{10,11... | collective-permute-start | bytes 3145736 | tf_op jit(solution)/shard_map/ppermute | solution.py:119
  77.9 2.9 %collective-permute-start.18 = (bf16[64,2048]{1,0:T(8,128)(2,1)S(1)}, bf16[64,2048]{1,0:T(8,128)(2,1)S(1)}, u32[]{:S(2)}, u32[]{:S(2)}) collective-permute-start(bf16[64,2048]{1,0:T(8,128)(2,1)S(1)} %collective-permute-done.13.refs_2_), channel_id=1, source_target_pairs={{0,1},{1,0},{2,3},{3,2},{4,5},{5,4},{6,7},{7,6},{8,9},{9,8},{10,11... | collective-permute-start | bytes 786440 | tf_op jit(solution)/shard_map/ppermute | solution.py:119
  87.0 14.6 %collective-permute-start.20 = (bf16[256,2048]{1,0:T(8,128)(2,1)S(1)}, bf16[256,2048]{1,0:T(8,128)(2,1)S(1)}, u32[]{:S(2)}, u32[]{:S(2)}) collective-permute-start(bf16[256,2048]{1,0:T(8,128)(2,1)S(1)} %get-tuple-element.92), channel_id=1, source_target_pairs={{0,1},{1,0},{2,3},{3,2},{4,5},{5,4},{6,7},{7,6},{8,9},{9,8},{10,11... | collective-permute-start | bytes 3145736 | tf_op jit(solution)/shard_map/ppermute | solution.py:119
  87.4 14.3 %collective-permute-start.21 = (bf16[128,2048]{1,0:T(8,128)(2,1)S(1)}, bf16[128,2048]{1,0:T(8,128)(2,1)S(1)}, u32[]{:S(2)}, u32[]{:S(2)}) collective-permute-start(bf16[128,2048]{1,0:T(8,128)(2,1)S(1)} %add_convert_fusion.4), channel_id=1, source_target_pairs={{0,2},{1,3},{2,0},{3,1},{4,6},{5,7},{6,4},{7,5},{8,10},{9,11},{10,... | collective-permute-start | bytes 1572872 | tf_op jit(solution)/shard_map/ppermute | solution.py:119
  101.9 7.8 %collective-permute-start.22 = (bf16[64,2048]{1,0:T(8,128)(2,1)S(1)}, bf16[64,2048]{1,0:T(8,128)(2,1)S(1)}, u32[]{:S(2)}, u32[]{:S(2)}) collective-permute-start(bf16[64,2048]{1,0:T(8,128)(2,1)S(1)} %get-tuple-element.110), channel_id=1, source_target_pairs={{0,4},{1,5},{2,6},{3,7},{4,0},{5,1},{6,2},{7,3},{8,12},{9,13},{10,... | collective-permute-start | bytes 786440 | tf_op jit(solution)/shard_map/ppermute | solution.py:119
  102.0 7.8 %collective-permute-start.23 = (bf16[64,2048]{1,0:T(8,128)(2,1)S(1)}, bf16[64,2048]{1,0:T(8,128)(2,1)S(1)}, u32[]{:S(2)}, u32[]{:S(2)}) collective-permute-start(bf16[64,2048]{1,0:T(8,128)(2,1)S(1)} %get-tuple-element.109), channel_id=1, source_target_pairs={{0,2},{1,3},{2,0},{3,1},{4,6},{5,7},{6,4},{7,5},{8,10},{9,11},{10,... | collective-permute-start | bytes 786440 | tf_op jit(solution)/shard_map/ppermute | solution.py:119
  110.0 12.5 %collective-permute-start.24 = (bf16[128,2048]{1,0:T(8,128)(2,1)S(1)}, bf16[128,2048]{1,0:T(8,128)(2,1)S(1)}, u32[]{:S(2)}, u32[]{:S(2)}) collective-permute-start(bf16[128,2048]{1,0:T(8,128)(2,1)S(1)} %pad_maximum_fusion), channel_id=1, source_target_pairs={{0,4},{1,5},{2,6},{3,7},{4,0},{5,1},{6,2},{7,3},{8,12},{9,13},{10,... | collective-permute-start | bytes 1572872 | tf_op jit(solution)/shard_map/ppermute | solution.py:119
  112.0 17.9 %copy-start.12 = (bf16[320,768]{1,0:T(8,128)(2,1)S(1)}, bf16[320,768]{1,0:T(8,128)(2,1)}, u32[]{:S(2)}) copy-start(bf16[320,768]{1,0:T(8,128)(2,1)} %copy-done.11) | copy-start | bytes 1474564
  112.0 17.9 %copy-start.14 = (bf16[320,768]{1,0:T(8,128)(2,1)S(1)}, bf16[320,768]{1,0:T(8,128)(2,1)}, u32[]{:S(2)}) copy-start(bf16[320,768]{1,0:T(8,128)(2,1)} %copy-done.13) | copy-start | bytes 1474564
  112.0 12.0 %collective-permute-start.25 = (bf16[128,2048]{1,0:T(8,128)(2,1)S(1)}, bf16[128,2048]{1,0:T(8,128)(2,1)S(1)}, u32[]{:S(2)}, u32[]{:S(2)}) collective-permute-start(bf16[128,2048]{1,0:T(8,128)(2,1)S(1)} %pad_maximum_fusion.1), channel_id=1, source_target_pairs={{0,2},{1,3},{2,0},{3,1},{4,6},{5,7},{6,4},{7,5},{8,10},{9,11},{10,... | collective-permute-start | bytes 1572872 | tf_op jit(solution)/shard_map/ppermute | solution.py:119
  125.1 11.3 %collective-permute-start.28 = (bf16[128,2048]{1,0:T(8,128)(2,1)}, bf16[128,2048]{1,0:T(8,128)(2,1)}, u32[]{:S(2)}, u32[]{:S(2)}) collective-permute-start(bf16[128,2048]{1,0:T(8,128)(2,1)} %add_convert_fusion.2), channel_id=1, source_target_pairs={{0,2},{1,3},{2,0},{3,1},{4,6},{5,7},{6,4},{7,5},{8,10},{9,11},{10,... | collective-permute-start | bytes 1572872 | tf_op jit(solution)/shard_map/ppermute | solution.py:119
  125.7 22.1 %collective-permute-start.27 = (bf16[128,2048]{1,0:T(8,128)(2,1)}, bf16[128,2048]{1,0:T(8,128)(2,1)}, u32[]{:S(2)}, u32[]{:S(2)}) collective-permute-start(bf16[128,2048]{1,0:T(8,128)(2,1)} %add_convert_fusion.3), channel_id=1, source_target_pairs={{0,4},{1,5},{2,6},{3,7},{4,0},{5,1},{6,2},{7,3},{8,12},{9,13},{10,... | collective-permute-start | bytes 1572872 | tf_op jit(solution)/shard_map/ppermute | solution.py:119
  126.3 23.2 %collective-permute-start.26 = (bf16[128,2048]{1,0:T(8,128)(2,1)}, bf16[128,2048]{1,0:T(8,128)(2,1)}, u32[]{:S(2)}, u32[]{:S(2)}) collective-permute-start(bf16[128,2048]{1,0:T(8,128)(2,1)} %add_convert_fusion.1), channel_id=1, source_target_pairs={{0,8},{1,9},{2,10},{3,11},{4,12},{5,13},{6,14},{7,15},{8,0},{9,1},... | collective-permute-start | bytes 1572872 | tf_op jit(solution)/shard_map/ppermute | solution.py:119
  129.8 19.7 %copy-start.16 = (bf16[256,2048]{1,0:T(8,128)(2,1)S(1)}, bf16[256,2048]{1,0:T(8,128)(2,1)}, u32[]{:S(2)}) copy-start(bf16[256,2048]{1,0:T(8,128)(2,1)} %copy-done.15) | copy-start | bytes 3145732

commit v11 on v10

--- a/solution.py
+++ b/solution.py
@@ -140,36 +140,33 @@
 
     weight = weights_for_me(routes, probs, size)
     a0 = tokens
-    a1, a2, b0, c0, weight = together(pair(a0), far(a0), column(a0), sibling(a0), weight)
-    a3 = pair(a2)
+    a1, b0, c0, weight = together(pair(a0), column(a0), sibling(a0), weight)
+    a2 = far(a0)
     b1 = column(a1)
     d0 = sibling(b0)
     c1 = sibling(a1)
     keep0, give0, act0 = expert(0, a0, b0, c0, d0)
-    a3, b1, c1, keep0, give0, act0 = together(a3, b1, c1, keep0, give0, act0)
+    a2, b1, c1, keep0, give0, act0 = together(a2, b1, c1, keep0, give0, act0)
+    a3 = pair(a2)
     b2 = column(a2)
-    b3_low = far(b1[:half])
     d1 = sibling(b1)
     c2 = sibling(a2)
     got0 = sibling(give0)
     keep1, give1, act1 = expert(1, a1, b1, c1, d1)
-    b2, b3_low, c2, got0, keep1, give1, act1 = together(b2, b3_low, c2, got0, keep1, give1, act1)
-    b3_high = column(a3[half:])
+    got1 = sibling(give1)
+    a3, b2, c2, got0, got1, keep1, act1 = together(a3, b2, c2, got0, got1, keep1, act1)
+    b3 = pair(b2)
+    came1 = column(summed(keep1[tok:], got1[tok:]))
     d2 = sibling(b2)
     c3 = sibling(a3)
-    d3_low = sibling(b3_low)
-    got1 = sibling(give1)
     keep2, give2, act2 = expert(2, a2, b2, c2, d2)
-    b3_high, c3, d3_low, got1, keep2, give2, act2 = together(
-        b3_high, c3, d3_low, got1, keep2, give2, act2
-    )
-    d3_high = sibling(b3_high)
+    b3, came1, c3, keep2, give2, act2 = together(b3, came1, c3, keep2, give2, act2)
+    d3 = sibling(b3)
     got2 = sibling(give2)
-    came1 = column(summed(keep1[tok:], got1[tok:]))
-    keep3, give3, act3 = expert(3, a3, b3_low, b3_high, c3, d3_low, d3_high)
+    keep3, give3, act3 = expert(3, a3, b3, c3, d3)
     keep3, give3, act3, got2 = together(keep3, give3, act3, got2)
 
-    got3, came1 = together(sibling(give3), came1)
+    got3 = sibling(give3)
     low = pair(summed(keep3[tok : tok + half], got3[tok : tok + half]))
     high = column(summed(keep3[tok + half :], got3[tok + half :]))
     low, high = together(low, high)

time: 153 us -> 149 us (0.974)
  waiting for transfers between devices: 57 us -> 69 us
  blocking collectives: 21.3 us -> 12.4 us
  starting transfers between devices: 22.6 us -> 18.8 us
  local copies, waits for them, and re-layouts: 12.4 us -> 9.42 us
    ppermute x29 -> x27, waiting for transfers between devices: 57 us -> 69 us  [swapped(): return lax.ppermute(array, 'expert', [(i, i ^ bit) for i in range(size)])]
    all_to_all x1, blocking collectives: 21.3 us -> 12.4 us  [weights_for_me(): lax.all_to_all(mine, 'expert', split_axis=0, concat_axis=0, tiled=True)]
    ppermute x29 -> x27, starting transfers between devices: 22.6 us -> 18.8 us  [swapped(): return lax.ppermute(array, 'expert', [(i, i ^ bit) for i in range(size)])]
    unnamed x34 -> x22, local copies, waits for them, and re-layouts: 12.3 us -> 9.33 us
  transfers between devices with their start and end apart: 29 -> 27, of which waited for: 12 -> 11; matrix products, arithmetic and copies ran while one was open for 5% -> 5% of each run, Pallas kernels for 17% -> 17%
where the time goes in v11:
time: 149 us; the launch traced here: 148 us
  waiting for transfers between devices  69 us (46%)
  Pallas kernels  25.8 us (17%)
  starting transfers between devices  18.8 us (13%)
  blocking collectives  12.4 us (8%)
  local copies, waits for them, and re-layouts  9.42 us (6%)
  other arithmetic  8.41 us (6%)
  matrix products  3.18 us (2%)
    ppermute x27, waiting for transfers between devices, swapped(): return lax.ppermute(array, 'expert', [(i, i ^ bit) for i in range(size)])  69 us
    pallas_call x4, Pallas kernels, plane_pass(): pl.pallas_call(functools.partial(plane_kernel, capacity, k, len(xs)), out...  25.8 us
    ppermute x27, starting transfers between devices, swapped(): return lax.ppermute(array, 'expert', [(i, i ^ bit) for i in range(size)])  18.8 us
    all_to_all x1, blocking collectives, weights_for_me(): lax.all_to_all(mine, 'expert', split_axis=0, concat_axis=0, tiled=True)  12.4 us
    unnamed x22, local copies, waits for them, and re-layouts  9.33 us
    convert_element_type x8, other arithmetic, summed(): return total.astype(jnp.bfloat16)  6.29 us
    dot_general x1, matrix products, gram_of(): lax.dot_general(rows, rows, (((0,), (0,)), ((), ())), preferred_element_t...  3.18 us
  transfers between devices with their start and end apart: 27, of which 11 were waited for; matrix products, arithmetic and copies ran while one was open for 5% of the time, Pallas kernels for 17%

profile of v11, /device:TPU:0, one launch (start us, length us, event | category | flops | bytes accessed | tf_op | source)
XLA Modules:
  0.0 148.5 jit_solution(7549177712399599628)
XLA Ops:
  0.6 3.1 %collective-permute-start.1 = (bf16[128,2048]{1,0:T(8,128)(2,1)}, bf16[128,2048]{1,0:T(8,128)(2,1)S(1)}, u32[]{:S(2)}, u32[]{:S(2)}) collective-permute-start(bf16[128,2048]{1,0:T(8,128)(2,1)} %refs_0_.1), channel_id=1, source_target_pairs={{0,4},{1,5},{2,6},{3,7},{4,0},{5,1},{6,2},{7,3},{8,12},{9,13},{10,... | collective-permute-start | bytes 1572872 | tf_op jit(solution)/shard_map/ppermute | solution.py:119
  3.7 1.5 %collective-permute-start.2 = (bf16[128,2048]{1,0:T(8,128)(2,1)}, bf16[128,2048]{1,0:T(8,128)(2,1)S(1)}, u32[]{:S(2)}, u32[]{:S(2)}) collective-permute-start(bf16[128,2048]{1,0:T(8,128)(2,1)} %refs_0_.1), channel_id=1, source_target_pairs={{0,2},{1,3},{2,0},{3,1},{4,6},{5,7},{6,4},{7,5},{8,10},{9,11},{10,... | collective-permute-start | bytes 1572872 | tf_op jit(solution)/shard_map/ppermute | solution.py:119
  5.2 0.7 fusion.10
  6.0 0.7 select_reduce_fusion
  6.7 12.4 %all_to_all.9 = f32[16,1,128]{2,1,0:T(1,128)S(1)} all-to-all(f32[16,1,128]{2,1,0:T(1,128)S(1)} %bitcast.44), channel_id=1, replica_groups=mesh['parts'=2,'expert'=16] {'expert'}, dimensions={0} | all-to-all | bytes 16384 | tf_op jit(solution)/shard_map/all_to_all | solution.py:28
  19.1 0.0 collective-permute-done.1.refs_0_
  19.1 0.0 collective-permute-done.2.refs_1_
  19.1 0.1 collective-permute-start.6
  19.2 1.0 collective-permute-start
  20.2 1.5 %collective-permute-start.4 = (bf16[128,2048]{1,0:T(8,128)(2,1)S(1)}, bf16[128,2048]{1,0:T(8,128)(2,1)}, u32[]{:S(2)}, u32[]{:S(2)}) collective-permute-start(bf16[128,2048]{1,0:T(8,128)(2,1)S(1)} %collective-permute-done.1.refs_0_), channel_id=1, source_target_pairs={{0,2},{1,3},{2,0},{3,1},{4,6},{5,7},{6,4},{7,5},{8,10},{9,11},{10,... | collective-permute-start | bytes 1572872 | tf_op jit(solution)/shard_map/ppermute | solution.py:119
  21.7 0.1 stack.67.spots
  21.8 0.0 copy-start.5
  21.8 0.8 copy-done.5
  22.6 1.9 %copy-done = bf16[1,2048,768]{2,1,0:T(8,128)(2,1)S(1)} copy-done((bf16[1,2048,768]{2,1,0:T(8,128)(2,1)S(1)}, bf16[1,2048,768]{2,1,0:T(8,128)(2,1)}, u32[]{:S(2)}) %copy-start) | copy-done | bytes 3145752
  24.5 1.9 %copy-done.2 = bf16[1,2048,768]{2,1,0:T(8,128)(2,1)S(1)} copy-done((bf16[1,2048,768]{2,1,0:T(8,128)(2,1)S(1)}, bf16[1,2048,768]{2,1,0:T(8,128)(2,1)}, u32[]{:S(2)}) %copy-start.2) | copy-done | bytes 3145752
  26.4 1.9 %copy-done.3 = bf16[1,768,2048]{2,1,0:T(8,128)(2,1)S(1)} copy-done((bf16[1,768,2048]{2,1,0:T(8,128)(2,1)S(1)}, bf16[1,768,2048]{2,1,0:T(8,128)(2,1)}, u32[]{:S(2)}) %copy-start.3) | copy-done | bytes 3145752
  28.3 1.0 copy-done.4
  29.3 1.0 copy-done.6
  30.4 6.2 %shard_map.77 = (bf16[256,2048]{1,0:T(8,128)(2,1)S(1)}, bf16[256,2048]{1,0:T(8,128)(2,1)S(1)}, bf16[320,768]{1,0:T(8,128)(2,1)S(1)}) custom-call(s32[16]{0:T(128)S(1)} %stack.67.spots, f32[16,128]{1,0:T(8,128)S(1)} %bitcast.27, bf16[128,2048]{1,0:T(8,128)(2,1)S(1)} %copy-done.4, bf16[128,2048]{1,0:T(8,128)(2,1)S(1)} %collective-permute-done.2.refs_1_, ...), custom_call_target="tpu_custom_call" | custom-call | flops 4362076160 | bytes 13631488 | tf_op jit(solution)/shard_map/pallas_call | solution.py:92
  36.6 0.0 copy-start.7
  36.6 0.8 copy-done.7
  37.4 8.4 %collective-permute-done.refs_0_ = bf16[128,2048]{1,0:T(8,128)(2,1)S(1)} collective-permute-done((bf16[128,2048]{1,0:T(8,128)(2,1)}, bf16[128,2048]{1,0:T(8,128)(2,1)S(1)}, u32[]{:S(2)}, u32[]{:S(2)}) %collective-permute-start) | collective-permute-done | bytes 524320 | tf_op jit(solution)/shard_map/ppermute | solution.py:119
  45.8 0.0 collective-permute-done.4.refs_1_
  45.8 0.1 collective-permute-start.11
  46.0 0.4 collective-permute-start.10
  46.4 1.6 %collective-permute-done.11.refs_3_ = bf16[128,2048]{1,0:T(8,128)(2,1)S(1)} collective-permute-done((bf16[128,2048]{1,0:T(8,128)(2,1)}, bf16[128,2048]{1,0:T(8,128)(2,1)S(1)}, u32[]{:S(2)}, u32[]{:S(2)}) %collective-permute-start.11) | collective-permute-done | bytes 524320 | tf_op jit(solution)/shard_map/ppermute | solution.py:119
  48.0 6.9 %shard_map.78 = (bf16[256,2048]{1,0:T(8,128)(2,1)S(1)}, bf16[256,2048]{1,0:T(8,128)(2,1)S(1)}, bf16[320,768]{1,0:T(8,128)(2,1)S(1)}) custom-call(s32[16]{0:T(128)S(1)} %stack.67.spots, f32[16,128]{1,0:T(8,128)S(1)} %bitcast.28, bf16[128,2048]{1,0:T(8,128)(2,1)S(1)} %collective-permute-done.1.refs_0_, bf16[128,2048]{1,0:T(8,128)(2,1)} %collective-permute-done.4.refs_1_, ...), custom_call_target="tpu_custom_call" | custom-call | flops 4362076160 | bytes 13631488 | tf_op jit(solution)/shard_map/pallas_call | solution.py:92
  54.9 0.2 collective-permute-start.12
  55.1 0.6 collective-permute-start.8
  55.7 0.1 collective-permute-start.9
  55.8 13.5 %collective-permute-done.7.refs_0_ = bf16[128,2048]{1,0:T(8,128)(2,1)S(1)} collective-permute-done((bf16[128,2048]{1,0:T(8,128)(2,1)S(1)}, bf16[128,2048]{1,0:T(8,128)(2,1)S(1)}, u32[]{:S(2)}, u32[]{:S(2)}) %collective-permute-start.7) | collective-permute-done | bytes 524320 | tf_op jit(solution)/shard_map/ppermute | solution.py:119
  69.4 0.1 collective-permute-start.16
  69.4 1.8 %collective-permute-start.13 = (bf16[128,2048]{1,0:T(8,128)(2,1)S(1)}, bf16[128,2048]{1,0:T(8,128)(2,1)S(1)}, u32[]{:S(2)}, u32[]{:S(2)}) collective-permute-start(bf16[128,2048]{1,0:T(8,128)(2,1)S(1)} %collective-permute-done.8.refs_1_), channel_id=1, source_target_pairs={{0,4},{1,5},{2,6},{3,7},{4,0},{5,1},{6,2},{7,3},{8,12},{9,13},{10,... | collective-permute-start | bytes 1572872 | tf_op jit(solution)/shard_map/ppermute | solution.py:119
  71.2 0.1 add_convert_fusion.4
  71.4 0.6 collective-permute-start.14
  72.0 6.4 %shard_map.79 = (bf16[256,2048]{1,0:T(8,128)(2,1)S(1)}, bf16[256,2048]{1,0:T(8,128)(2,1)S(1)}, bf16[320,768]{1,0:T(8,128)(2,1)S(1)}) custom-call(s32[16]{0:T(128)S(1)} %stack.67.spots, f32[16,128]{1,0:T(8,128)S(1)} %bitcast.29, bf16[128,2048]{1,0:T(8,128)(2,1)S(1)} %collective-permute-done.refs_0_, bf16[128,2048]{1,0:T(8,128)(2,1)S(1)} %collective-permute-done.8.refs_1_, ...), custom_call_target="tpu_custom_call" | custom-call | flops 4362076160 | bytes 13631488 | tf_op jit(solution)/shard_map/pallas_call | solution.py:92
  78.5 7.0 %collective-permute-done.14 = bf16[128,2048]{1,0:T(8,128)(2,1)S(1)} collective-permute-done((bf16[128,2048]{1,0:T(8,128)(2,1)S(1)}, bf16[128,2048]{1,0:T(8,128)(2,1)S(1)}, u32[]{:S(2)}, u32[]{:S(2)}) %collective-permute-start.14) | collective-permute-done | bytes 524320 | tf_op jit(solution)/shard_map/ppermute | solution.py:119
  85.4 0.5 collective-permute-start.17
  86.0 2.9 %collective-permute-done.17.refs_3_ = bf16[128,2048]{1,0:T(8,128)(2,1)S(1)} collective-permute-done((bf16[128,2048]{1,0:T(8,128)(2,1)S(1)}, bf16[128,2048]{1,0:T(8,128)(2,1)S(1)}, u32[]{:S(2)}, u32[]{:S(2)}) %collective-permute-start.17) | collective-permute-done | bytes 524320 | tf_op jit(solution)/shard_map/ppermute | solution.py:119
  88.9 6.2 %shard_map.80 = (bf16[256,2048]{1,0:T(8,128)(2,1)S(1)}, bf16[256,2048]{1,0:T(8,128)(2,1)S(1)}, bf16[320,768]{1,0:T(8,128)(2,1)S(1)}) custom-call(s32[16]{0:T(128)S(1)} %stack.67.spots, f32[16,128]{1,0:T(8,128)S(1)} %bitcast.30, bf16[128,2048]{1,0:T(8,128)(2,1)S(1)} %collective-permute-done.7.refs_0_, bf16[128,2048]{1,0:T(8,128)(2,1)S(1)} %collective-permute-done.13.refs_1_, ...), custom_call_target="tpu_custom_call" | custom-call | flops 4362076160 | bytes 13631488 | tf_op jit(solution)/shard_map/pallas_call | solution.py:92
  95.1 0.2 collective-permute-start.19
  95.3 2.5 %collective-permute-done.19 = bf16[256,2048]{1,0:T(8,128)(2,1)S(1)} collective-permute-done((bf16[256,2048]{1,0:T(8,128)(2,1)S(1)}, bf16[256,2048]{1,0:T(8,128)(2,1)S(1)}, u32[]{:S(2)}, u32[]{:S(2)}) %collective-permute-start.19) | collective-permute-done | bytes 1048608 | tf_op jit(solution)/shard_map/ppermute | solution.py:119
  97.8 0.2 add_convert_fusion.10
  98.1 0.4 collective-permute-start.20
  98.4 0.6 collective-permute-start.21
  99.0 7.5 %collective-permute-done.20 = bf16[64,2048]{1,0:T(8,128)(2,1)S(1)} collective-permute-done((bf16[64,2048]{1,0:T(8,128)(2,1)S(1)}, bf16[64,2048]{1,0:T(8,128)(2,1)S(1)}, u32[]{:S(2)}, u32[]{:S(2)}) %collective-permute-start.20) | collective-permute-done | bytes 262176 | tf_op jit(solution)/shard_map/ppermute | solution.py:119
  106.5 0.1 collective-permute-done.21
  106.6 0.2 add_convert_fusion.6
  106.8 0.6 collective-permute-start.23
  107.4 0.1 add_convert_fusion.7
  107.6 0.0 copy-start.8
  107.6 1.7 %collective-permute-start.22 = (bf16[128,2048]{1,0:T(8,128)(2,1)S(1)}, bf16[128,2048]{1,0:T(8,128)(2,1)S(1)}, u32[]{:S(2)}, u32[]{:S(2)}) collective-permute-start(bf16[128,2048]{1,0:T(8,128)(2,1)S(1)} %pad_maximum_fusion), channel_id=1, source_target_pairs={{0,4},{1,5},{2,6},{3,7},{4,0},{5,1},{6,2},{7,3},{8,12},{9,13},{10,... | collective-permute-start | bytes 1572872 | tf_op jit(solution)/shard_map/ppermute | solution.py:119
  109.3 0.9 add_convert_fusion.2
  110.2 1.0 add_convert_fusion.3
  111.3 8.7 %collective-permute-done.23 = bf16[128,2048]{1,0:T(8,128)(2,1)S(1)} collective-permute-done((bf16[128,2048]{1,0:T(8,128)(2,1)S(1)}, bf16[128,2048]{1,0:T(8,128)(2,1)S(1)}, u32[]{:S(2)}, u32[]{:S(2)}) %collective-permute-start.23) | collective-permute-done | bytes 524320 | tf_op jit(solution)/shard_map/ppermute | solution.py:119
  119.9 0.5 collective-permute-done.22
  120.4 1.1 add_convert_fusion.1
  121.6 1.8 %collective-permute-start.24 = (bf16[128,2048]{1,0:T(8,128)(2,1)}, bf16[128,2048]{1,0:T(8,128)(2,1)}, u32[]{:S(2)}, u32[]{:S(2)}) collective-permute-start(bf16[128,2048]{1,0:T(8,128)(2,1)} %add_convert_fusion.1), channel_id=1, source_target_pairs={{0,8},{1,9},{2,10},{3,11},{4,12},{5,13},{6,14},{7,15},{8,0},{9,1},... | collective-permute-start | bytes 1572872 | tf_op jit(solution)/shard_map/ppermute | solution.py:119
  123.4 0.6 collective-permute-start.25
  124.0 1.2 collective-permute-start.26
  125.2 0.6 convert_reduce_fusion
  126.4 3.2 %multiply_bitcast_fusion = f32[1,768,768]{2,1,0:T(8,128)} fusion(f32[]{:T(128)S(6)} %div.24, bf16[320,768]{1,0:T(8,128)(2,1)S(1)} %get-tuple-element.81, bf16[320,768]{1,0:T(8,128)(2,1)S(1)} %get-tuple-element.74, bf16[320,768]{1,0:T(8,128)(2,1)S(1)} %get-tuple-element.65, bf16[320,768]{1,0:T(8,128)(2,1)S(1)} %copy-done.8), kind=kOutput, calls=%fused_computation | convolution fusion | flops 1518403584 | bytes 4325380 | tf_op jit(solution)/shard_map/dot_general | solution.py:12
  129.6 16.2 %collective-permute-done.24 = bf16[128,2048]{1,0:T(8,128)(2,1)} collective-permute-done((bf16[128,2048]{1,0:T(8,128)(2,1)}, bf16[128,2048]{1,0:T(8,128)(2,1)}, u32[]{:S(2)}, u32[]{:S(2)}) %collective-permute-start.24) | collective-permute-done | bytes 524320 | tf_op jit(solution)/shard_map/ppermute | solution.py:119
  145.9 2.6 %add_convert_fusion = bf16[128,2048]{1,0:T(8,128)(2,1)} fusion(bf16[128,2048]{1,0:T(8,128)(2,1)} %collective-permute-done.26, bf16[128,2048]{1,0:T(8,128)(2,1)} %collective-permute-done.25, bf16[128,2048]{1,0:T(8,128)(2,1)} %collective-permute-done.24, bf16[256,2048]{1,0:T(8,128)(2,1)S(1)} %copy-done.10, bf16[256,2048]{1,0:T(8,128)(2,1)S(1)} %get-tuple-element.82), kind=kLoop, calls=%fused_computation.9 | loop fusion | flops 2621440 | bytes 3145728 | tf_op jit(solution)/shard_map/convert_element_type | solution.py:35
  (33 shorter events, 0.2 us)
Async XLA Ops:
  0.6 18.5 %collective-permute-start.1 = (bf16[128,2048]{1,0:T(8,128)(2,1)}, bf16[128,2048]{1,0:T(8,128)(2,1)S(1)}, u32[]{:S(2)}, u32[]{:S(2)}) collective-permute-start(bf16[128,2048]{1,0:T(8,128)(2,1)} %refs_0_.1), channel_id=1, source_target_pairs={{0,4},{1,5},{2,6},{3,7},{4,0},{5,1},{6,2},{7,3},{8,12},{9,13},{10,... | collective-permute-start | bytes 1572872 | tf_op jit(solution)/shard_map/ppermute | solution.py:119
  3.7 15.4 %collective-permute-start.2 = (bf16[128,2048]{1,0:T(8,128)(2,1)}, bf16[128,2048]{1,0:T(8,128)(2,1)S(1)}, u32[]{:S(2)}, u32[]{:S(2)}) collective-permute-start(bf16[128,2048]{1,0:T(8,128)(2,1)} %refs_0_.1), channel_id=1, source_target_pairs={{0,2},{1,3},{2,0},{3,1},{4,6},{5,7},{6,4},{7,5},{8,10},{9,11},{10,... | collective-permute-start | bytes 1572872 | tf_op jit(solution)/shard_map/ppermute | solution.py:119
  5.2 13.9 %collective-permute-start.3 = (bf16[128,2048]{1,0:T(8,128)(2,1)}, bf16[128,2048]{1,0:T(8,128)(2,1)S(1)}, u32[]{:S(2)}, u32[]{:S(2)}) collective-permute-start(bf16[128,2048]{1,0:T(8,128)(2,1)} %refs_0_.1), channel_id=1, source_target_pairs={{0,1},{1,0},{2,3},{3,2},{4,5},{5,4},{6,7},{7,6},{8,9},{9,8},{10,11... | collective-permute-start | bytes 1572872 | tf_op jit(solution)/shard_map/ppermute | solution.py:119
  19.1 2.7 %collective-permute-start.6 = (bf16[128,2048]{1,0:T(8,128)(2,1)S(1)}, bf16[128,2048]{1,0:T(8,128)(2,1)S(1)}, u32[]{:S(2)}, u32[]{:S(2)}) collective-permute-start(bf16[128,2048]{1,0:T(8,128)(2,1)S(1)} %collective-permute-done.2.refs_1_), channel_id=1, source_target_pairs={{0,1},{1,0},{2,3},{3,2},{4,5},{5,4},{6,7},{7,6},{8,9},{9,8},{10,11... | collective-permute-start | bytes 1572872 | tf_op jit(solution)/shard_map/ppermute | solution.py:119
  19.2 26.6 %collective-permute-start = (bf16[128,2048]{1,0:T(8,128)(2,1)}, bf16[128,2048]{1,0:T(8,128)(2,1)S(1)}, u32[]{:S(2)}, u32[]{:S(2)}) collective-permute-start(bf16[128,2048]{1,0:T(8,128)(2,1)} %refs_0_.1), channel_id=1, source_target_pairs={{0,8},{1,9},{2,10},{3,11},{4,12},{5,13},{6,14},{7,15},{8,0},{9,1},... | collective-permute-start | bytes 1572872 | tf_op jit(solution)/shard_map/ppermute | solution.py:119
  20.2 25.6 %collective-permute-start.4 = (bf16[128,2048]{1,0:T(8,128)(2,1)S(1)}, bf16[128,2048]{1,0:T(8,128)(2,1)}, u32[]{:S(2)}, u32[]{:S(2)}) collective-permute-start(bf16[128,2048]{1,0:T(8,128)(2,1)S(1)} %collective-permute-done.1.refs_0_), channel_id=1, source_target_pairs={{0,2},{1,3},{2,0},{3,1},{4,6},{5,7},{6,4},{7,5},{8,10},{9,11},{10,... | collective-permute-start | bytes 1572872 | tf_op jit(solution)/shard_map/ppermute | solution.py:119
  21.7 24.1 %collective-permute-start.5 = (bf16[128,2048]{1,0:T(8,128)(2,1)S(1)}, bf16[128,2048]{1,0:T(8,128)(2,1)}, u32[]{:S(2)}, u32[]{:S(2)}) collective-permute-start(bf16[128,2048]{1,0:T(8,128)(2,1)S(1)} %collective-permute-done.1.refs_0_), channel_id=1, source_target_pairs={{0,1},{1,0},{2,3},{3,2},{4,5},{5,4},{6,7},{7,6},{8,9},{9,8},{10,11... | collective-permute-start | bytes 1572872 | tf_op jit(solution)/shard_map/ppermute | solution.py:119
  21.8 0.8 copy-start.5
  22.6 1.9 %copy-start = (bf16[1,2048,768]{2,1,0:T(8,128)(2,1)S(1)}, bf16[1,2048,768]{2,1,0:T(8,128)(2,1)}, u32[]{:S(2)}) copy-start(bf16[1,2048,768]{2,1,0:T(8,128)(2,1)} %param.9) | copy-start | bytes 9437188
  24.5 1.9 %copy-start.2 = (bf16[1,2048,768]{2,1,0:T(8,128)(2,1)S(1)}, bf16[1,2048,768]{2,1,0:T(8,128)(2,1)}, u32[]{:S(2)}) copy-start(bf16[1,2048,768]{2,1,0:T(8,128)(2,1)} %param.10) | copy-start | bytes 9437188
  26.4 1.9 %copy-start.3 = (bf16[1,768,2048]{2,1,0:T(8,128)(2,1)S(1)}, bf16[1,768,2048]{2,1,0:T(8,128)(2,1)}, u32[]{:S(2)}) copy-start(bf16[1,768,2048]{2,1,0:T(8,128)(2,1)} %param.11) | copy-start | bytes 9437188
  28.3 1.0 copy-start.4
  29.3 1.0 copy-start.6
  36.6 0.8 copy-start.7
  45.8 26.2 %copy-start.1 = (bf16[1,2048,768]{2,1,0:T(8,128)(2,1)S(1)}, bf16[1,2048,768]{2,1,0:T(8,128)(2,1)}, u32[]{:S(2)}) copy-start(bf16[1,2048,768]{2,1,0:T(8,128)(2,1)} %param.9) | copy-start | bytes 9437188
  45.8 2.2 %collective-permute-start.11 = (bf16[128,2048]{1,0:T(8,128)(2,1)}, bf16[128,2048]{1,0:T(8,128)(2,1)S(1)}, u32[]{:S(2)}, u32[]{:S(2)}) collective-permute-start(bf16[128,2048]{1,0:T(8,128)(2,1)} %collective-permute-done.4.refs_1_), channel_id=1, source_target_pairs={{0,1},{1,0},{2,3},{3,2},{4,5},{5,4},{6,7},{7,6},{8,9},{9,8},{10,11... | collective-permute-start | bytes 1572872 | tf_op jit(solution)/shard_map/ppermute | solution.py:119
  46.0 23.4 %collective-permute-start.10 = (bf16[256,2048]{1,0:T(8,128)(2,1)S(1)}, bf16[256,2048]{1,0:T(8,128)(2,1)S(1)}, u32[]{:S(2)}, u32[]{:S(2)}) collective-permute-start(bf16[256,2048]{1,0:T(8,128)(2,1)S(1)} %get-tuple-element.59), channel_id=1, source_target_pairs={{0,1},{1,0},{2,3},{3,2},{4,5},{5,4},{6,7},{7,6},{8,9},{9,8},{10,11... | collective-permute-start | bytes 3145736 | tf_op jit(solution)/shard_map/ppermute | solution.py:119
  54.9 14.4 %collective-permute-start.12 = (bf16[256,2048]{1,0:T(8,128)(2,1)S(1)}, bf16[256,2048]{1,0:T(8,128)(2,1)S(1)}, u32[]{:S(2)}, u32[]{:S(2)}) collective-permute-start(bf16[256,2048]{1,0:T(8,128)(2,1)S(1)} %get-tuple-element.62), channel_id=1, source_target_pairs={{0,1},{1,0},{2,3},{3,2},{4,5},{5,4},{6,7},{7,6},{8,9},{9,8},{10,11... | collective-permute-start | bytes 3145736 | tf_op jit(solution)/shard_map/ppermute | solution.py:119
  55.1 14.2 %collective-permute-start.7 = (bf16[128,2048]{1,0:T(8,128)(2,1)S(1)}, bf16[128,2048]{1,0:T(8,128)(2,1)S(1)}, u32[]{:S(2)}, u32[]{:S(2)}) collective-permute-start(bf16[128,2048]{1,0:T(8,128)(2,1)S(1)} %collective-permute-done.refs_0_), channel_id=1, source_target_pairs={{0,4},{1,5},{2,6},{3,7},{4,0},{5,1},{6,2},{7,3},{8,12},{9,13},{10,... | collective-permute-start | bytes 1572872 | tf_op jit(solution)/shard_map/ppermute | solution.py:119
  55.1 14.2 %collective-permute-start.8 = (bf16[128,2048]{1,0:T(8,128)(2,1)S(1)}, bf16[128,2048]{1,0:T(8,128)(2,1)S(1)}, u32[]{:S(2)}, u32[]{:S(2)}) collective-permute-start(bf16[128,2048]{1,0:T(8,128)(2,1)S(1)} %collective-permute-done.refs_0_), channel_id=1, source_target_pairs={{0,2},{1,3},{2,0},{3,1},{4,6},{5,7},{6,4},{7,5},{8,10},{9,11},{10,... | collective-permute-start | bytes 1572872 | tf_op jit(solution)/shard_map/ppermute | solution.py:119
  55.7 13.6 %collective-permute-start.9 = (bf16[128,2048]{1,0:T(8,128)(2,1)S(1)}, bf16[128,2048]{1,0:T(8,128)(2,1)S(1)}, u32[]{:S(2)}, u32[]{:S(2)}) collective-permute-start(bf16[128,2048]{1,0:T(8,128)(2,1)S(1)} %collective-permute-done.refs_0_), channel_id=1, source_target_pairs={{0,1},{1,0},{2,3},{3,2},{4,5},{5,4},{6,7},{7,6},{8,9},{9,8},{10,11... | collective-permute-start | bytes 1572872 | tf_op jit(solution)/shard_map/ppermute | solution.py:119
  69.3 40.0 %copy-start.9 = (bf16[256,2048]{1,0:T(8,128)(2,1)}, bf16[256,2048]{1,0:T(8,128)(2,1)S(1)}, u32[]{:S(2)}) copy-start(bf16[256,2048]{1,0:T(8,128)(2,1)S(1)} %collective-permute-done.10) | copy-start | bytes 3145732
  69.4 2.6 %collective-permute-start.16 = (bf16[128,2048]{1,0:T(8,128)(2,1)S(1)}, bf16[128,2048]{1,0:T(8,128)(2,1)S(1)}, u32[]{:S(2)}, u32[]{:S(2)}) collective-permute-start(bf16[128,2048]{1,0:T(8,128)(2,1)S(1)} %collective-permute-done.8.refs_1_), channel_id=1, source_target_pairs={{0,1},{1,0},{2,3},{3,2},{4,5},{5,4},{6,7},{7,6},{8,9},{9,8},{10,11... | collective-permute-start | bytes 1572872 | tf_op jit(solution)/shard_map/ppermute | solution.py:119
  69.4 16.0 %collective-permute-start.13 = (bf16[128,2048]{1,0:T(8,128)(2,1)S(1)}, bf16[128,2048]{1,0:T(8,128)(2,1)S(1)}, u32[]{:S(2)}, u32[]{:S(2)}) collective-permute-start(bf16[128,2048]{1,0:T(8,128)(2,1)S(1)} %collective-permute-done.8.refs_1_), channel_id=1, source_target_pairs={{0,4},{1,5},{2,6},{3,7},{4,0},{5,1},{6,2},{7,3},{8,12},{9,13},{10,... | collective-permute-start | bytes 1572872 | tf_op jit(solution)/shard_map/ppermute | solution.py:119
  71.4 14.1 %collective-permute-start.14 = (bf16[128,2048]{1,0:T(8,128)(2,1)S(1)}, bf16[128,2048]{1,0:T(8,128)(2,1)S(1)}, u32[]{:S(2)}, u32[]{:S(2)}) collective-permute-start(bf16[128,2048]{1,0:T(8,128)(2,1)S(1)} %add_convert_fusion.4), channel_id=1, source_target_pairs={{0,2},{1,3},{2,0},{3,1},{4,6},{5,7},{6,4},{7,5},{8,10},{9,11},{10,... | collective-permute-start | bytes 1572872 | tf_op jit(solution)/shard_map/ppermute | solution.py:119
  72.0 13.4 %collective-permute-start.15 = (bf16[128,2048]{1,0:T(8,128)(2,1)S(1)}, bf16[128,2048]{1,0:T(8,128)(2,1)S(1)}, u32[]{:S(2)}, u32[]{:S(2)}) collective-permute-start(bf16[128,2048]{1,0:T(8,128)(2,1)S(1)} %collective-permute-done.7.refs_0_), channel_id=1, source_target_pairs={{0,1},{1,0},{2,3},{3,2},{4,5},{5,4},{6,7},{7,6},{8,9},{9,8},{10,11... | collective-permute-start | bytes 1572872 | tf_op jit(solution)/shard_map/ppermute | solution.py:119
  85.4 9.7 %collective-permute-start.18 = (bf16[256,2048]{1,0:T(8,128)(2,1)S(1)}, bf16[256,2048]{1,0:T(8,128)(2,1)S(1)}, u32[]{:S(2)}, u32[]{:S(2)}) collective-permute-start(bf16[256,2048]{1,0:T(8,128)(2,1)S(1)} %get-tuple-element.80), channel_id=1, source_target_pairs={{0,1},{1,0},{2,3},{3,2},{4,5},{5,4},{6,7},{7,6},{8,9},{9,8},{10,11... | collective-permute-start | bytes 3145736 | tf_op jit(solution)/shard_map/ppermute | solution.py:119
  85.4 3.4 %collective-permute-start.17 = (bf16[128,2048]{1,0:T(8,128)(2,1)S(1)}, bf16[128,2048]{1,0:T(8,128)(2,1)S(1)}, u32[]{:S(2)}, u32[]{:S(2)}) collective-permute-start(bf16[128,2048]{1,0:T(8,128)(2,1)S(1)} %collective-permute-done.13.refs_1_), channel_id=1, source_target_pairs={{0,1},{1,0},{2,3},{3,2},{4,5},{5,4},{6,7},{7,6},{8,9},{9,8},{10,11... | collective-permute-start | bytes 1572872 | tf_op jit(solution)/shard_map/ppermute | solution.py:119
  95.1 2.7 %collective-permute-start.19 = (bf16[256,2048]{1,0:T(8,128)(2,1)S(1)}, bf16[256,2048]{1,0:T(8,128)(2,1)S(1)}, u32[]{:S(2)}, u32[]{:S(2)}) collective-permute-start(bf16[256,2048]{1,0:T(8,128)(2,1)S(1)} %get-tuple-element.87), channel_id=1, source_target_pairs={{0,1},{1,0},{2,3},{3,2},{4,5},{5,4},{6,7},{7,6},{8,9},{9,8},{10,11... | collective-permute-start | bytes 3145736 | tf_op jit(solution)/shard_map/ppermute | solution.py:119
  98.1 8.4 %collective-permute-start.20 = (bf16[64,2048]{1,0:T(8,128)(2,1)S(1)}, bf16[64,2048]{1,0:T(8,128)(2,1)S(1)}, u32[]{:S(2)}, u32[]{:S(2)}) collective-permute-start(bf16[64,2048]{1,0:T(8,128)(2,1)S(1)} %get-tuple-element.102), channel_id=1, source_target_pairs={{0,4},{1,5},{2,6},{3,7},{4,0},{5,1},{6,2},{7,3},{8,12},{9,13},{10,... | collective-permute-start | bytes 786440 | tf_op jit(solution)/shard_map/ppermute | solution.py:119
  98.4 8.1 %collective-permute-start.21 = (bf16[64,2048]{1,0:T(8,128)(2,1)S(1)}, bf16[64,2048]{1,0:T(8,128)(2,1)S(1)}, u32[]{:S(2)}, u32[]{:S(2)}) collective-permute-start(bf16[64,2048]{1,0:T(8,128)(2,1)S(1)} %get-tuple-element.101), channel_id=1, source_target_pairs={{0,2},{1,3},{2,0},{3,1},{4,6},{5,7},{6,4},{7,5},{8,10},{9,11},{10,... | collective-permute-start | bytes 786440 | tf_op jit(solution)/shard_map/ppermute | solution.py:119
  106.8 13.1 %collective-permute-start.23 = (bf16[128,2048]{1,0:T(8,128)(2,1)S(1)}, bf16[128,2048]{1,0:T(8,128)(2,1)S(1)}, u32[]{:S(2)}, u32[]{:S(2)}) collective-permute-start(bf16[128,2048]{1,0:T(8,128)(2,1)S(1)} %pad_maximum_fusion.1), channel_id=1, source_target_pairs={{0,2},{1,3},{2,0},{3,1},{4,6},{5,7},{6,4},{7,5},{8,10},{9,11},{10,... | collective-permute-start | bytes 1572872 | tf_op jit(solution)/shard_map/ppermute | solution.py:119
  107.6 18.8 %copy-start.8 = (bf16[320,768]{1,0:T(8,128)(2,1)S(1)}, bf16[320,768]{1,0:T(8,128)(2,1)}, u32[]{:S(2)}) copy-start(bf16[320,768]{1,0:T(8,128)(2,1)} %copy-done.7) | copy-start | bytes 1474564
  107.6 12.8 %collective-permute-start.22 = (bf16[128,2048]{1,0:T(8,128)(2,1)S(1)}, bf16[128,2048]{1,0:T(8,128)(2,1)S(1)}, u32[]{:S(2)}, u32[]{:S(2)}) collective-permute-start(bf16[128,2048]{1,0:T(8,128)(2,1)S(1)} %pad_maximum_fusion), channel_id=1, source_target_pairs={{0,4},{1,5},{2,6},{3,7},{4,0},{5,1},{6,2},{7,3},{8,12},{9,13},{10,... | collective-permute-start | bytes 1572872 | tf_op jit(solution)/shard_map/ppermute | solution.py:119
  121.6 24.3 %collective-permute-start.24 = (bf16[128,2048]{1,0:T(8,128)(2,1)}, bf16[128,2048]{1,0:T(8,128)(2,1)}, u32[]{:S(2)}, u32[]{:S(2)}) collective-permute-start(bf16[128,2048]{1,0:T(8,128)(2,1)} %add_convert_fusion.1), channel_id=1, source_target_pairs={{0,8},{1,9},{2,10},{3,11},{4,12},{5,13},{6,14},{7,15},{8,0},{9,1},... | collective-permute-start | bytes 1572872 | tf_op jit(solution)/shard_map/ppermute | solution.py:119
  123.4 22.5 %collective-permute-start.25 = (bf16[128,2048]{1,0:T(8,128)(2,1)}, bf16[128,2048]{1,0:T(8,128)(2,1)}, u32[]{:S(2)}, u32[]{:S(2)}) collective-permute-start(bf16[128,2048]{1,0:T(8,128)(2,1)} %add_convert_fusion.3), channel_id=1, source_target_pairs={{0,4},{1,5},{2,6},{3,7},{4,0},{5,1},{6,2},{7,3},{8,12},{9,13},{10,... | collective-permute-start | bytes 1572872 | tf_op jit(solution)/shard_map/ppermute | solution.py:119
  124.0 21.9 %collective-permute-start.26 = (bf16[128,2048]{1,0:T(8,128)(2,1)}, bf16[128,2048]{1,0:T(8,128)(2,1)}, u32[]{:S(2)}, u32[]{:S(2)}) collective-permute-start(bf16[128,2048]{1,0:T(8,128)(2,1)} %add_convert_fusion.2), channel_id=1, source_target_pairs={{0,2},{1,3},{2,0},{3,1},{4,6},{5,7},{6,4},{7,5},{8,10},{9,11},{10,... | collective-permute-start | bytes 1572872 | tf_op jit(solution)/shard_map/ppermute | solution.py:119
  126.4 19.4 %copy-start.10 = (bf16[256,2048]{1,0:T(8,128)(2,1)S(1)}, bf16[256,2048]{1,0:T(8,128)(2,1)}, u32[]{:S(2)}) copy-start(bf16[256,2048]{1,0:T(8,128)(2,1)} %copy-done.9) | copy-start | bytes 3145732

commit v12 on v11

--- a/solution.py
+++ b/solution.py
@@ -25,6 +25,26 @@
     names = routes.T[None, :, :] == jnp.arange(experts, dtype=jnp.int32)[:, None, None]
     weight = jnp.sum(jnp.where(names, probs.T[None, :, :], 0.0), axis=1)
     mine = jnp.where(jnp.any(names, axis=1), weight, -1.0)
+    return lax.all_to_all(mine, "expert", split_axis=0, concat_axis=0, tiled=True)
+
+
+def table_kernel(routes, probs, w_gate, w_up, w_down, mine):
+    names, shares = routes[...], probs[...]
+    for e in range(mine.shape[0]):
+        hit = (names == e).astype(jnp.float32)
+        named = jnp.sum(hit, axis=0, keepdims=True)
+        share = jnp.sum(hit * shares, axis=0, keepdims=True)
+        mine[pl.ds(e, 1), :] = jnp.where(named > 0.0, share, -1.0)
+
+
+def table_pass(routes, probs, experts, w_gate, w_up, w_down):
+    mine = pl.pallas_call(
+        table_kernel,
+        out_shape=jax.ShapeDtypeStruct((experts, routes.shape[0]), jnp.float32),
+        in_specs=[pl.BlockSpec(memory_space=pltpu.VMEM)] * 5,
+        out_specs=pl.BlockSpec(memory_space=pltpu.VMEM),
+        compiler_params=pltpu.CompilerParams(vmem_limit_bytes=4 * 1024 * 1024),
+    )(routes.T, probs.T, w_gate, w_up, w_down)
     return lax.all_to_all(mine, "expert", split_axis=0, concat_axis=0, tiled=True)
 
 
@@ -138,24 +158,26 @@
     def expert(k, *xs):
         return plane_pass(k, spots, weight, xs, w_gate, w_up, w_down, slots, capacity)
 
-    weight = weights_for_me(routes, probs, size)
+    weight = table_pass(routes, probs, size, w_gate, w_up, w_down)
     a0 = tokens
-    a1, b0, c0, weight = together(pair(a0), column(a0), sibling(a0), weight)
-    a2 = far(a0)
+    a1, low, b0, c0, weight = together(
+        pair(a0), far(a0[:half]), column(a0), sibling(a0), weight
+    )
+    high = far(a0[half:])
     b1 = column(a1)
     d0 = sibling(b0)
     c1 = sibling(a1)
     keep0, give0, act0 = expert(0, a0, b0, c0, d0)
-    a2, b1, c1, keep0, give0, act0 = together(a2, b1, c1, keep0, give0, act0)
+    high, b1, c1, keep0, give0, act0 = together(high, b1, c1, keep0, give0, act0)
+    a2 = jnp.concatenate([low, high], axis=0)
     a3 = pair(a2)
     b2 = column(a2)
     d1 = sibling(b1)
     c2 = sibling(a2)
-    got0 = sibling(give0)
     keep1, give1, act1 = expert(1, a1, b1, c1, d1)
+    a3, b2, c2, keep1, give1, act1 = together(a3, b2, c2, keep1, give1, act1)
+    b3 = pair(b2)
     got1 = sibling(give1)
-    a3, b2, c2, got0, got1, keep1, act1 = together(a3, b2, c2, got0, got1, keep1, act1)
-    b3 = pair(b2)
     came1 = column(summed(keep1[tok:], got1[tok:]))
     d2 = sibling(b2)
     c3 = sibling(a3)
@@ -165,6 +187,7 @@
     got2 = sibling(give2)
     keep3, give3, act3 = expert(3, a3, b3, c3, d3)
     keep3, give3, act3, got2 = together(keep3, give3, act3, got2)
+    got0 = sibling(give0)
 
     got3 = sibling(give3)
     low = pair(summed(keep3[tok : tok + half], got3[tok : tok + half]))

time: 149 us -> 141 us (0.946)
  waiting for transfers between devices: 69 us -> 52 us
  local copies, waits for them, and re-layouts: 9.42 us -> 18.3 us
  starting transfers between devices: 18.8 us -> 22.2 us
  blocking collectives: 12.4 us -> 9.24 us
    ppermute x27 -> x28, waiting for transfers between devices: 69 us -> 52 us  [swapped(): return lax.ppermute(array, 'expert', [(i, i ^ bit) for i in range(size)])]
    unnamed x22 -> x45, local copies, waits for them, and re-layouts: 9.33 us -> 15.3 us
    ppermute x27 -> x28, starting transfers between devices: 18.8 us -> 22.2 us  [swapped(): return lax.ppermute(array, 'expert', [(i, i ^ bit) for i in range(size)])]
    all_to_all x1, blocking collectives: 12.4 us -> 9.24 us  [table_pass(): lax.all_to_all(mine, 'expert', split_axis=0, concat_axis=0, tiled=True)]
    slice x0 -> x1, local copies, waits for them, and re-layouts: none -> 1.77 us  [staged(): high = far(a0[half:])]
  transfers between devices with their start and end apart: 27 -> 28, of which waited for: 11 -> 14; matrix products, arithmetic and copies ran while one was open for 5% -> 7% of each run, Pallas kernels for 17% -> 19%
where the time goes in v12:
time: 141 us; the launch traced here: 140 us
  waiting for transfers between devices  52 us (37%)
  Pallas kernels  26.7 us (19%)
  starting transfers between devices  22.2 us (16%)
  local copies, waits for them, and re-layouts  18.3 us (13%)
  blocking collectives  9.24 us (7%)
  other arithmetic  7.01 us (5%)
  matrix products  3.16 us (2%)
  between operations  1.59 us (1%)
    ppermute x28, waiting for transfers between devices, swapped(): return lax.ppermute(array, 'expert', [(i, i ^ bit) for i in range(size)])  52 us
    pallas_call x4, Pallas kernels, plane_pass(): pl.pallas_call(functools.partial(plane_kernel, capacity, k, len(xs)), out...  26.6 us
    ppermute x28, starting transfers between devices, swapped(): return lax.ppermute(array, 'expert', [(i, i ^ bit) for i in range(size)])  22.2 us
    unnamed x45, local copies, waits for them, and re-layouts  15.3 us
    all_to_all x1, blocking collectives, table_pass(): lax.all_to_all(mine, 'expert', split_axis=0, concat_axis=0, tiled=True)  9.24 us
    convert_element_type x8, other arithmetic, summed(): return total.astype(jnp.bfloat16)  6.3 us
    dot_general x1, matrix products, gram_of(): lax.dot_general(rows, rows, (((0,), (0,)), ((), ())), preferred_element_t...  3.16 us
  transfers between devices with their start and end apart: 28, of which 14 were waited for; matrix products, arithmetic and copies ran while one was open for 7% of the time, Pallas kernels for 19%

profile of v12, /device:TPU:0, one launch (start us, length us, event | category | flops | bytes accessed | tf_op | source)
XLA Modules:
  0.0 140.1 jit_solution(80638053550941171)
XLA Ops:
  0.6 3.1 %collective-permute-start.1 = (bf16[128,2048]{1,0:T(8,128)(2,1)}, bf16[128,2048]{1,0:T(8,128)(2,1)}, u32[]{:S(2)}, u32[]{:S(2)}) collective-permute-start(bf16[128,2048]{1,0:T(8,128)(2,1)} %refs_0_.1), channel_id=1, source_target_pairs={{0,4},{1,5},{2,6},{3,7},{4,0},{5,1},{6,2},{7,3},{8,12},{9,13},{10,... | collective-permute-start | bytes 1572872 | tf_op jit(solution)/shard_map/ppermute | solution.py:139
  3.7 1.5 %collective-permute-start.3 = (bf16[128,2048]{1,0:T(8,128)(2,1)}, bf16[128,2048]{1,0:T(8,128)(2,1)}, u32[]{:S(2)}, u32[]{:S(2)}) collective-permute-start(bf16[128,2048]{1,0:T(8,128)(2,1)} %refs_0_.1), channel_id=1, source_target_pairs={{0,2},{1,3},{2,0},{3,1},{4,6},{5,7},{6,4},{7,5},{8,10},{9,11},{10,... | collective-permute-start | bytes 1572872 | tf_op jit(solution)/shard_map/ppermute | solution.py:139
  5.2 1.8 %fusion.11 = (bf16[64,2048]{1,0:T(8,128)(2,1)}, bf16[64,2048]{1,0:T(8,128)(2,1)S(1)}) fusion(bf16[128,2048]{1,0:T(8,128)(2,1)} %refs_0_.1), kind=kLoop, calls=%fused_computation.26 | loop fusion | bytes 1048576 | tf_op jit(solution)/shard_map/slice | solution.py:166
  7.0 2.6 %collective-permute-start.2 = (bf16[64,2048]{1,0:T(8,128)(2,1)S(1)}, bf16[64,2048]{1,0:T(8,128)(2,1)S(1)}, u32[]{:S(2)}, u32[]{:S(2)}) collective-permute-start(bf16[64,2048]{1,0:T(8,128)(2,1)S(1)} %get-tuple-element.104), channel_id=1, source_target_pairs={{0,8},{1,9},{2,10},{3,11},{4,12},{5,13},{6,14},{7,15},{8,0},{9,1},... | collective-permute-start | bytes 786440 | tf_op jit(solution)/shard_map/ppermute | solution.py:139
  9.6 1.9 %copy-done = bf16[1,2048,768]{2,1,0:T(8,128)(2,1)S(1)} copy-done((bf16[1,2048,768]{2,1,0:T(8,128)(2,1)S(1)}, bf16[1,2048,768]{2,1,0:T(8,128)(2,1)}, u32[]{:S(2)}) %copy-start) | copy-done | bytes 3145752
  11.5 1.9 %copy-done.2 = bf16[1,2048,768]{2,1,0:T(8,128)(2,1)S(1)} copy-done((bf16[1,2048,768]{2,1,0:T(8,128)(2,1)S(1)}, bf16[1,2048,768]{2,1,0:T(8,128)(2,1)}, u32[]{:S(2)}) %copy-start.2) | copy-done | bytes 3145752
  13.4 1.9 %copy-done.5 = bf16[1,768,2048]{2,1,0:T(8,128)(2,1)S(1)} copy-done((bf16[1,768,2048]{2,1,0:T(8,128)(2,1)S(1)}, bf16[1,768,2048]{2,1,0:T(8,128)(2,1)}, u32[]{:S(2)}) %copy-start.5) | copy-done | bytes 3145752
  15.3 0.7 copy-done.10
  16.0 0.7 copy-done.11
  16.7 9.2 %all_to_all.12 = f32[16,1,128]{2,1,0:T(1,128)S(1)} all-to-all(f32[16,1,128]{2,1,0:T(1,128)S(1)} %bitcast.42), channel_id=1, replica_groups=mesh['parts'=2,'expert'=16] {'expert'}, dimensions={0} | all-to-all | bytes 16384 | tf_op jit(solution)/shard_map/all_to_all | solution.py:48
  26.0 0.8 copy-done.12
  26.8 0.5 collective-permute-start.5
  27.3 0.2 collective-permute-start.6
  27.5 0.6 collective-permute-start
  28.2 0.8 collective-permute-done.7.refs_3_
  29.0 1.9 %copy-done.3 = bf16[1,2048,768]{2,1,0:T(8,128)(2,1)S(1)} copy-done((bf16[1,2048,768]{2,1,0:T(8,128)(2,1)S(1)}, bf16[1,2048,768]{2,1,0:T(8,128)(2,1)}, u32[]{:S(2)}) %copy-start.3) | copy-done | bytes 3145752
  30.9 1.9 %copy-done.6 = bf16[1,768,2048]{2,1,0:T(8,128)(2,1)S(1)} copy-done((bf16[1,768,2048]{2,1,0:T(8,128)(2,1)S(1)}, bf16[1,768,2048]{2,1,0:T(8,128)(2,1)}, u32[]{:S(2)}) %copy-start.6) | copy-done | bytes 3145752
  32.8 1.0 copy-done.9
  33.8 1.0 copy-done.13
  34.9 6.9 %shard_map.78 = (bf16[256,2048]{1,0:T(8,128)(2,1)S(1)}, bf16[256,2048]{1,0:T(8,128)(2,1)S(1)}, bf16[320,768]{1,0:T(8,128)(2,1)S(1)}) custom-call(s32[16]{0:T(128)S(1)} %stack.67.spots, f32[16,128]{1,0:T(8,128)S(1)} %bitcast.43, bf16[128,2048]{1,0:T(8,128)(2,1)S(1)} %copy-done.9, bf16[128,2048]{1,0:T(8,128)(2,1)} %collective-permute-done.3.refs_1_, ...), custom_call_target="tpu_custom_call" | custom-call | flops 4362076160 | bytes 13631488 | tf_op jit(solution)/shard_map/pallas_call | solution.py:112
  41.8 0.8 copy-done.14
  42.6 0.2 collective-permute-done
  42.9 1.1 constant_dynamic-update-slice_fusion.refs_0_
  43.9 0.5 collective-permute-start.10
  44.4 0.3 collective-permute-start.8
  44.8 1.1 collective-permute-start.9
  45.9 7.1 %shard_map.79 = (bf16[256,2048]{1,0:T(8,128)(2,1)S(1)}, bf16[256,2048]{1,0:T(8,128)(2,1)S(1)}, bf16[320,768]{1,0:T(8,128)(2,1)S(1)}) custom-call(s32[16]{0:T(128)S(1)} %stack.67.spots, f32[16,128]{1,0:T(8,128)S(1)} %bitcast.44, bf16[128,2048]{1,0:T(8,128)(2,1)} %collective-permute-done.1.refs_0_, bf16[128,2048]{1,0:T(8,128)(2,1)} %collective-permute-done.5.refs_1_, ...), custom_call_target="tpu_custom_call" | custom-call | flops 4362076160 | bytes 13631488 | tf_op jit(solution)/shard_map/pallas_call | solution.py:112
  53.0 5.4 %collective-permute-done.8.refs_0_ = bf16[128,2048]{1,0:T(8,128)(2,1)S(1)} collective-permute-done((bf16[128,2048]{1,0:T(8,128)(2,1)S(1)}, bf16[128,2048]{1,0:T(8,128)(2,1)S(1)}, u32[]{:S(2)}, u32[]{:S(2)}) %collective-permute-start.8) | collective-permute-done | bytes 524320 | tf_op jit(solution)/shard_map/ppermute | solution.py:139
  58.3 0.2 collective-permute-done.9.refs_1_
  58.6 0.5 collective-permute-start.16
  59.1 1.5 %collective-permute-start.12 = (bf16[128,2048]{1,0:T(8,128)(2,1)S(1)}, bf16[128,2048]{1,0:T(8,128)(2,1)S(1)}, u32[]{:S(2)}, u32[]{:S(2)}) collective-permute-start(bf16[128,2048]{1,0:T(8,128)(2,1)S(1)} %collective-permute-done.9.refs_1_), channel_id=1, source_target_pairs={{0,4},{1,5},{2,6},{3,7},{4,0},{5,1},{6,2},{7,3},{8,12},{9,13},{10,... | collective-permute-start | bytes 1572872 | tf_op jit(solution)/shard_map/ppermute | solution.py:139
  60.6 0.6 collective-permute-done.13
  61.2 0.1 add_convert_fusion.4
  61.4 1.4 collective-permute-start.14
  62.7 6.4 %shard_map.80 = (bf16[256,2048]{1,0:T(8,128)(2,1)S(1)}, bf16[256,2048]{1,0:T(8,128)(2,1)S(1)}, bf16[320,768]{1,0:T(8,128)(2,1)S(1)}) custom-call(s32[16]{0:T(128)S(1)} %stack.67.spots, f32[16,128]{1,0:T(8,128)S(1)} %bitcast.45, bf16[128,2048]{1,0:T(8,128)(2,1)S(1)} %constant_dynamic-update-slice_fusion.refs_0_, ...), custom_call_target="tpu_custom_call" | custom-call | flops 4362076160 | bytes 13631488 | tf_op jit(solution)/shard_map/pallas_call | solution.py:112
  69.2 0.8 copy-done.18
  70.0 2.9 %collective-permute-done.12.refs_1_ = bf16[128,2048]{1,0:T(8,128)(2,1)S(1)} collective-permute-done((bf16[128,2048]{1,0:T(8,128)(2,1)S(1)}, bf16[128,2048]{1,0:T(8,128)(2,1)S(1)}, u32[]{:S(2)}, u32[]{:S(2)}) %collective-permute-start.12) | collective-permute-done | bytes 524320 | tf_op jit(solution)/shard_map/ppermute | solution.py:139
  72.9 2.5 %collective-permute-done.14 = bf16[128,2048]{1,0:T(8,128)(2,1)S(1)} collective-permute-done((bf16[128,2048]{1,0:T(8,128)(2,1)S(1)}, bf16[128,2048]{1,0:T(8,128)(2,1)S(1)}, u32[]{:S(2)}, u32[]{:S(2)}) %collective-permute-start.14) | collective-permute-done | bytes 524320 | tf_op jit(solution)/shard_map/ppermute | solution.py:139
  75.4 0.5 collective-permute-start.17
  75.9 2.9 %collective-permute-done.17.refs_3_ = bf16[128,2048]{1,0:T(8,128)(2,1)S(1)} collective-permute-done((bf16[128,2048]{1,0:T(8,128)(2,1)S(1)}, bf16[128,2048]{1,0:T(8,128)(2,1)S(1)}, u32[]{:S(2)}, u32[]{:S(2)}) %collective-permute-start.17) | collective-permute-done | bytes 524320 | tf_op jit(solution)/shard_map/ppermute | solution.py:139
  78.8 6.3 %shard_map.81 = (bf16[256,2048]{1,0:T(8,128)(2,1)S(1)}, bf16[256,2048]{1,0:T(8,128)(2,1)S(1)}, bf16[320,768]{1,0:T(8,128)(2,1)S(1)}) custom-call(s32[16]{0:T(128)S(1)} %stack.67.spots, f32[16,128]{1,0:T(8,128)S(1)} %bitcast.46, bf16[128,2048]{1,0:T(8,128)(2,1)S(1)} %collective-permute-done.8.refs_0_, bf16[128,2048]{1,0:T(8,128)(2,1)S(1)} %collective-permute-done.12.refs_1_, ...), custom_call_target="tpu_custom_call" | custom-call | flops 4362076160 | bytes 13631488 | tf_op jit(solution)/shard_map/pallas_call | solution.py:112
  85.1 0.2 collective-permute-start.20
  85.3 2.5 %collective-permute-done.20 = bf16[256,2048]{1,0:T(8,128)(2,1)S(1)} collective-permute-done((bf16[256,2048]{1,0:T(8,128)(2,1)S(1)}, bf16[256,2048]{1,0:T(8,128)(2,1)S(1)}, u32[]{:S(2)}, u32[]{:S(2)}) %collective-permute-start.20) | collective-permute-done | bytes 1048608 | tf_op jit(solution)/shard_map/ppermute | solution.py:139
  87.8 0.2 add_convert_fusion.10
  88.1 1.6 %collective-permute-start.21 = (bf16[64,2048]{1,0:T(8,128)(2,1)S(1)}, bf16[64,2048]{1,0:T(8,128)(2,1)S(1)}, u32[]{:S(2)}, u32[]{:S(2)}) collective-permute-start(bf16[64,2048]{1,0:T(8,128)(2,1)S(1)} %get-tuple-element.102), channel_id=1, source_target_pairs={{0,4},{1,5},{2,6},{3,7},{4,0},{5,1},{6,2},{7,3},{8,12},{9,13},{10,... | collective-permute-start | bytes 786440 | tf_op jit(solution)/shard_map/ppermute | solution.py:139
  89.6 1.4 %collective-permute-start.22 = (bf16[64,2048]{1,0:T(8,128)(2,1)S(1)}, bf16[64,2048]{1,0:T(8,128)(2,1)S(1)}, u32[]{:S(2)}, u32[]{:S(2)}) collective-permute-start(bf16[64,2048]{1,0:T(8,128)(2,1)S(1)} %get-tuple-element.101), channel_id=1, source_target_pairs={{0,2},{1,3},{2,0},{3,1},{4,6},{5,7},{6,4},{7,5},{8,10},{9,11},{10,... | collective-permute-start | bytes 786440 | tf_op jit(solution)/shard_map/ppermute | solution.py:139
  91.1 5.4 %collective-permute-done.21 = bf16[64,2048]{1,0:T(8,128)(2,1)S(1)} collective-permute-done((bf16[64,2048]{1,0:T(8,128)(2,1)S(1)}, bf16[64,2048]{1,0:T(8,128)(2,1)S(1)}, u32[]{:S(2)}, u32[]{:S(2)}) %collective-permute-start.21) | collective-permute-done | bytes 262176 | tf_op jit(solution)/shard_map/ppermute | solution.py:139
  96.5 1.2 collective-permute-done.22
  97.7 0.2 add_convert_fusion.6
  98.0 1.5 %collective-permute-start.24 = (bf16[128,2048]{1,0:T(8,128)(2,1)S(1)}, bf16[128,2048]{1,0:T(8,128)(2,1)S(1)}, u32[]{:S(2)}, u32[]{:S(2)}) collective-permute-start(bf16[128,2048]{1,0:T(8,128)(2,1)S(1)} %pad_maximum_fusion.1), channel_id=1, source_target_pairs={{0,2},{1,3},{2,0},{3,1},{4,6},{5,7},{6,4},{7,5},{8,10},{9,11},{10,... | collective-permute-start | bytes 1572872 | tf_op jit(solution)/shard_map/ppermute | solution.py:139
  99.5 0.1 add_convert_fusion.7
  99.7 0.4 collective-permute-start.23
  100.1 0.9 add_convert_fusion.2
  101.0 1.0 add_convert_fusion.3
  102.0 8.8 %collective-permute-done.24 = bf16[128,2048]{1,0:T(8,128)(2,1)S(1)} collective-permute-done((bf16[128,2048]{1,0:T(8,128)(2,1)S(1)}, bf16[128,2048]{1,0:T(8,128)(2,1)S(1)}, u32[]{:S(2)}, u32[]{:S(2)}) %collective-permute-start.24) | collective-permute-done | bytes 524320 | tf_op jit(solution)/shard_map/ppermute | solution.py:139
  110.8 1.4 %collective-permute-done.23 = bf16[128,2048]{1,0:T(8,128)(2,1)S(1)} collective-permute-done((bf16[128,2048]{1,0:T(8,128)(2,1)S(1)}, bf16[128,2048]{1,0:T(8,128)(2,1)S(1)}, u32[]{:S(2)}, u32[]{:S(2)}) %collective-permute-start.23) | collective-permute-done | bytes 524320 | tf_op jit(solution)/shard_map/ppermute | solution.py:139
  112.3 1.1 add_convert_fusion.1
  113.4 1.5 %collective-permute-start.25 = (bf16[128,2048]{1,0:T(8,128)(2,1)}, bf16[128,2048]{1,0:T(8,128)(2,1)}, u32[]{:S(2)}, u32[]{:S(2)}) collective-permute-start(bf16[128,2048]{1,0:T(8,128)(2,1)} %add_convert_fusion.1), channel_id=1, source_target_pairs={{0,8},{1,9},{2,10},{3,11},{4,12},{5,13},{6,14},{7,15},{8,0},{9,1},... | collective-permute-start | bytes 1572872 | tf_op jit(solution)/shard_map/ppermute | solution.py:139
  114.9 0.6 collective-permute-start.26
  115.5 0.5 collective-permute-start.27
  116.1 0.6 convert_reduce_fusion
  117.4 3.2 %multiply_bitcast_fusion = f32[1,768,768]{2,1,0:T(8,128)} fusion(f32[]{:T(128)S(6)} %div.24, bf16[320,768]{1,0:T(8,128)(2,1)S(1)} %copy-done.21, bf16[320,768]{1,0:T(8,128)(2,1)S(1)} %copy-done.19, bf16[320,768]{1,0:T(8,128)(2,1)S(1)} %copy-done.17, bf16[320,768]{1,0:T(8,128)(2,1)S(1)} %copy-done.15), kind=kOutput, calls=%fused_computation | convolution fusion | flops 1518403584 | bytes 4325380 | tf_op jit(solution)/shard_map/dot_general | solution.py:12
  120.6 16.9 %collective-permute-done.25 = bf16[128,2048]{1,0:T(8,128)(2,1)} collective-permute-done((bf16[128,2048]{1,0:T(8,128)(2,1)}, bf16[128,2048]{1,0:T(8,128)(2,1)}, u32[]{:S(2)}, u32[]{:S(2)}) %collective-permute-start.25) | collective-permute-done | bytes 524320 | tf_op jit(solution)/shard_map/ppermute | solution.py:139
  137.5 2.6 %add_convert_fusion = bf16[128,2048]{1,0:T(8,128)(2,1)} fusion(bf16[128,2048]{1,0:T(8,128)(2,1)} %collective-permute-done.27, bf16[128,2048]{1,0:T(8,128)(2,1)} %collective-permute-done.26, bf16[128,2048]{1,0:T(8,128)(2,1)} %collective-permute-done.25, bf16[256,2048]{1,0:T(8,128)(2,1)S(1)} %collective-permute-done.19, bf16[256,2048]{1,0:T(8,128)(2,1)S(1)} %copy-done.8), kind=kLoop, calls=%fused_computation.9 | loop fusion | flops 2621440 | bytes 3145728 | tf_op jit(solution)/shard_map/convert_element_type | solution.py:55
  (58 shorter events, 0.4 us)
Async XLA Ops:
  0.6 25.3 %collective-permute-start.1 = (bf16[128,2048]{1,0:T(8,128)(2,1)}, bf16[128,2048]{1,0:T(8,128)(2,1)}, u32[]{:S(2)}, u32[]{:S(2)}) collective-permute-start(bf16[128,2048]{1,0:T(8,128)(2,1)} %refs_0_.1), channel_id=1, source_target_pairs={{0,4},{1,5},{2,6},{3,7},{4,0},{5,1},{6,2},{7,3},{8,12},{9,13},{10,... | collective-permute-start | bytes 1572872 | tf_op jit(solution)/shard_map/ppermute | solution.py:139
  3.7 22.2 %collective-permute-start.3 = (bf16[128,2048]{1,0:T(8,128)(2,1)}, bf16[128,2048]{1,0:T(8,128)(2,1)}, u32[]{:S(2)}, u32[]{:S(2)}) collective-permute-start(bf16[128,2048]{1,0:T(8,128)(2,1)} %refs_0_.1), channel_id=1, source_target_pairs={{0,2},{1,3},{2,0},{3,1},{4,6},{5,7},{6,4},{7,5},{8,10},{9,11},{10,... | collective-permute-start | bytes 1572872 | tf_op jit(solution)/shard_map/ppermute | solution.py:139
  5.2 20.7 %collective-permute-start.4 = (bf16[128,2048]{1,0:T(8,128)(2,1)}, bf16[128,2048]{1,0:T(8,128)(2,1)S(1)}, u32[]{:S(2)}, u32[]{:S(2)}) collective-permute-start(bf16[128,2048]{1,0:T(8,128)(2,1)} %refs_0_.1), channel_id=1, source_target_pairs={{0,1},{1,0},{2,3},{3,2},{4,5},{5,4},{6,7},{7,6},{8,9},{9,8},{10,11... | collective-permute-start | bytes 1572872 | tf_op jit(solution)/shard_map/ppermute | solution.py:139
  7.0 18.9 %collective-permute-start.2 = (bf16[64,2048]{1,0:T(8,128)(2,1)S(1)}, bf16[64,2048]{1,0:T(8,128)(2,1)S(1)}, u32[]{:S(2)}, u32[]{:S(2)}) collective-permute-start(bf16[64,2048]{1,0:T(8,128)(2,1)S(1)} %get-tuple-element.104), channel_id=1, source_target_pairs={{0,8},{1,9},{2,10},{3,11},{4,12},{5,13},{6,14},{7,15},{8,0},{9,1},... | collective-permute-start | bytes 786440 | tf_op jit(solution)/shard_map/ppermute | solution.py:139
  9.6 1.9 %copy-start = (bf16[1,2048,768]{2,1,0:T(8,128)(2,1)S(1)}, bf16[1,2048,768]{2,1,0:T(8,128)(2,1)}, u32[]{:S(2)}) copy-start(bf16[1,2048,768]{2,1,0:T(8,128)(2,1)} %param.9) | copy-start | bytes 9437188
  11.5 1.9 %copy-start.2 = (bf16[1,2048,768]{2,1,0:T(8,128)(2,1)S(1)}, bf16[1,2048,768]{2,1,0:T(8,128)(2,1)}, u32[]{:S(2)}) copy-start(bf16[1,2048,768]{2,1,0:T(8,128)(2,1)} %param.10) | copy-start | bytes 9437188
  13.4 1.9 %copy-start.5 = (bf16[1,768,2048]{2,1,0:T(8,128)(2,1)S(1)}, bf16[1,768,2048]{2,1,0:T(8,128)(2,1)}, u32[]{:S(2)}) copy-start(bf16[1,768,2048]{2,1,0:T(8,128)(2,1)} %param.11) | copy-start | bytes 9437188
  15.3 0.7 copy-start.10
  16.0 0.7 copy-start.11
  16.6 12.4 %copy-start.1 = (bf16[1,2048,768]{2,1,0:T(8,128)(2,1)S(1)}, bf16[1,2048,768]{2,1,0:T(8,128)(2,1)}, u32[]{:S(2)}) copy-start(bf16[1,2048,768]{2,1,0:T(8,128)(2,1)} %param.9) | copy-start | bytes 9437188
  26.0 0.8 copy-start.12
  26.8 2.3 %collective-permute-start.7 = (bf16[128,2048]{1,0:T(8,128)(2,1)}, bf16[128,2048]{1,0:T(8,128)(2,1)}, u32[]{:S(2)}, u32[]{:S(2)}) collective-permute-start(bf16[128,2048]{1,0:T(8,128)(2,1)} %collective-permute-done.3.refs_1_), channel_id=1, source_target_pairs={{0,1},{1,0},{2,3},{3,2},{4,5},{5,4},{6,7},{7,6},{8,9},{9,8},{10,11... | collective-permute-start | bytes 1572872 | tf_op jit(solution)/shard_map/ppermute | solution.py:139
  26.8 16.1 %collective-permute-start.5 = (bf16[128,2048]{1,0:T(8,128)(2,1)}, bf16[128,2048]{1,0:T(8,128)(2,1)}, u32[]{:S(2)}, u32[]{:S(2)}) collective-permute-start(bf16[128,2048]{1,0:T(8,128)(2,1)} %collective-permute-done.1.refs_0_), channel_id=1, source_target_pairs={{0,2},{1,3},{2,0},{3,1},{4,6},{5,7},{6,4},{7,5},{8,10},{9,11},{10,... | collective-permute-start | bytes 1572872 | tf_op jit(solution)/shard_map/ppermute | solution.py:139
  27.3 15.6 %collective-permute-start.6 = (bf16[128,2048]{1,0:T(8,128)(2,1)}, bf16[128,2048]{1,0:T(8,128)(2,1)}, u32[]{:S(2)}, u32[]{:S(2)}) collective-permute-start(bf16[128,2048]{1,0:T(8,128)(2,1)} %collective-permute-done.1.refs_0_), channel_id=1, source_target_pairs={{0,1},{1,0},{2,3},{3,2},{4,5},{5,4},{6,7},{7,6},{8,9},{9,8},{10,11... | collective-permute-start | bytes 1572872 | tf_op jit(solution)/shard_map/ppermute | solution.py:139
  27.5 15.3 %collective-permute-start = (bf16[64,2048]{1,0:T(8,128)(2,1)}, bf16[64,2048]{1,0:T(8,128)(2,1)}, u32[]{:S(2)}, u32[]{:S(2)}) collective-permute-start(bf16[64,2048]{1,0:T(8,128)(2,1)} %get-tuple-element.103), channel_id=1, source_target_pairs={{0,8},{1,9},{2,10},{3,11},{4,12},{5,13},{6,14},{7,15},{8,0},{9,1},... | collective-permute-start | bytes 786440 | tf_op jit(solution)/shard_map/ppermute | solution.py:139
  29.0 1.9 %copy-start.3 = (bf16[1,2048,768]{2,1,0:T(8,128)(2,1)S(1)}, bf16[1,2048,768]{2,1,0:T(8,128)(2,1)}, u32[]{:S(2)}) copy-start(bf16[1,2048,768]{2,1,0:T(8,128)(2,1)} %param.10) | copy-start | bytes 9437188
  30.9 1.9 %copy-start.6 = (bf16[1,768,2048]{2,1,0:T(8,128)(2,1)S(1)}, bf16[1,768,2048]{2,1,0:T(8,128)(2,1)}, u32[]{:S(2)}) copy-start(bf16[1,768,2048]{2,1,0:T(8,128)(2,1)} %param.11) | copy-start | bytes 9437188
  32.8 1.0 copy-start.9
  33.8 1.0 copy-start.13
  41.8 0.8 copy-start.14
  42.6 57.5 %copy-start.7 = (bf16[256,2048]{1,0:T(8,128)(2,1)}, bf16[256,2048]{1,0:T(8,128)(2,1)S(1)}, u32[]{:S(2)}) copy-start(bf16[256,2048]{1,0:T(8,128)(2,1)S(1)} %get-tuple-element.82) | copy-start | bytes 3145732
  42.8 3.1 %collective-permute-start.11 = (bf16[128,2048]{1,0:T(8,128)(2,1)}, bf16[128,2048]{1,0:T(8,128)(2,1)S(1)}, u32[]{:S(2)}, u32[]{:S(2)}) collective-permute-start(bf16[128,2048]{1,0:T(8,128)(2,1)} %collective-permute-done.5.refs_1_), channel_id=1, source_target_pairs={{0,1},{1,0},{2,3},{3,2},{4,5},{5,4},{6,7},{7,6},{8,9},{9,8},{10,11... | collective-permute-start | bytes 1572872 | tf_op jit(solution)/shard_map/ppermute | solution.py:139
  43.9 18.8 %copy-start.4 = (bf16[1,2048,768]{2,1,0:T(8,128)(2,1)S(1)}, bf16[1,2048,768]{2,1,0:T(8,128)(2,1)}, u32[]{:S(2)}) copy-start(bf16[1,2048,768]{2,1,0:T(8,128)(2,1)} %param.10) | copy-start | bytes 9437188
  43.9 9.0 %collective-permute-start.10 = (bf16[128,2048]{1,0:T(8,128)(2,1)S(1)}, bf16[128,2048]{1,0:T(8,128)(2,1)S(1)}, u32[]{:S(2)}, u32[]{:S(2)}) collective-permute-start(bf16[128,2048]{1,0:T(8,128)(2,1)S(1)} %constant_dynamic-update-slice_fusion.refs_0_), channel_id=1, source_target_pairs={{0,1},{1,0},{2,3},{3,2},{4,5},{5,4},{6,7},{7,6},{8,9},{9,8},{10,11... | collective-permute-start | bytes 1572872 | tf_op jit(solution)/shard_map/ppermute | solution.py:139
  44.4 13.9 %collective-permute-start.8 = (bf16[128,2048]{1,0:T(8,128)(2,1)S(1)}, bf16[128,2048]{1,0:T(8,128)(2,1)S(1)}, u32[]{:S(2)}, u32[]{:S(2)}) collective-permute-start(bf16[128,2048]{1,0:T(8,128)(2,1)S(1)} %constant_dynamic-update-slice_fusion.refs_0_), channel_id=1, source_target_pairs={{0,4},{1,5},{2,6},{3,7},{4,0},{5,1},{6,2},{7,3},{8,12},{9,13},{10,... | collective-permute-start | bytes 1572872 | tf_op jit(solution)/shard_map/ppermute | solution.py:139
  44.8 13.8 %collective-permute-start.9 = (bf16[128,2048]{1,0:T(8,128)(2,1)S(1)}, bf16[128,2048]{1,0:T(8,128)(2,1)S(1)}, u32[]{:S(2)}, u32[]{:S(2)}) collective-permute-start(bf16[128,2048]{1,0:T(8,128)(2,1)S(1)} %constant_dynamic-update-slice_fusion.refs_0_), channel_id=1, source_target_pairs={{0,2},{1,3},{2,0},{3,1},{4,6},{5,7},{6,4},{7,5},{8,10},{9,11},{10,... | collective-permute-start | bytes 1572872 | tf_op jit(solution)/shard_map/ppermute | solution.py:139
  52.9 9.8 %copy-start.16 = (bf16[320,768]{1,0:T(8,128)(2,1)}, bf16[320,768]{1,0:T(8,128)(2,1)S(1)}, u32[]{:S(2)}) copy-start(bf16[320,768]{1,0:T(8,128)(2,1)S(1)} %get-tuple-element.65) | copy-start | bytes 1474564
  58.6 2.7 %collective-permute-start.13 = (bf16[256,2048]{1,0:T(8,128)(2,1)S(1)}, bf16[256,2048]{1,0:T(8,128)(2,1)S(1)}, u32[]{:S(2)}, u32[]{:S(2)}) collective-permute-start(bf16[256,2048]{1,0:T(8,128)(2,1)S(1)} %get-tuple-element.68), channel_id=1, source_target_pairs={{0,1},{1,0},{2,3},{3,2},{4,5},{5,4},{6,7},{7,6},{8,9},{9,8},{10,11... | collective-permute-start | bytes 3145736 | tf_op jit(solution)/shard_map/ppermute | solution.py:139
  58.6 4.2 %collective-permute-start.16 = (bf16[128,2048]{1,0:T(8,128)(2,1)S(1)}, bf16[128,2048]{1,0:T(8,128)(2,1)S(1)}, u32[]{:S(2)}, u32[]{:S(2)}) collective-permute-start(bf16[128,2048]{1,0:T(8,128)(2,1)S(1)} %collective-permute-done.9.refs_1_), channel_id=1, source_target_pairs={{0,1},{1,0},{2,3},{3,2},{4,5},{5,4},{6,7},{7,6},{8,9},{9,8},{10,11... | collective-permute-start | bytes 1572872 | tf_op jit(solution)/shard_map/ppermute | solution.py:139
  59.1 13.8 %collective-permute-start.12 = (bf16[128,2048]{1,0:T(8,128)(2,1)S(1)}, bf16[128,2048]{1,0:T(8,128)(2,1)S(1)}, u32[]{:S(2)}, u32[]{:S(2)}) collective-permute-start(bf16[128,2048]{1,0:T(8,128)(2,1)S(1)} %collective-permute-done.9.refs_1_), channel_id=1, source_target_pairs={{0,4},{1,5},{2,6},{3,7},{4,0},{5,1},{6,2},{7,3},{8,12},{9,13},{10,... | collective-permute-start | bytes 1572872 | tf_op jit(solution)/shard_map/ppermute | solution.py:139
  60.6 12.3 %collective-permute-start.15 = (bf16[128,2048]{1,0:T(8,128)(2,1)S(1)}, bf16[128,2048]{1,0:T(8,128)(2,1)S(1)}, u32[]{:S(2)}, u32[]{:S(2)}) collective-permute-start(bf16[128,2048]{1,0:T(8,128)(2,1)S(1)} %collective-permute-done.8.refs_0_), channel_id=1, source_target_pairs={{0,1},{1,0},{2,3},{3,2},{4,5},{5,4},{6,7},{7,6},{8,9},{9,8},{10,11... | collective-permute-start | bytes 1572872 | tf_op jit(solution)/shard_map/ppermute | solution.py:139
  61.4 14.0 %collective-permute-start.14 = (bf16[128,2048]{1,0:T(8,128)(2,1)S(1)}, bf16[128,2048]{1,0:T(8,128)(2,1)S(1)}, u32[]{:S(2)}, u32[]{:S(2)}) collective-permute-start(bf16[128,2048]{1,0:T(8,128)(2,1)S(1)} %add_convert_fusion.4), channel_id=1, source_target_pairs={{0,2},{1,3},{2,0},{3,1},{4,6},{5,7},{6,4},{7,5},{8,10},{9,11},{10,... | collective-permute-start | bytes 1572872 | tf_op jit(solution)/shard_map/ppermute | solution.py:139
  69.2 0.8 copy-start.18
  75.4 9.7 %collective-permute-start.18 = (bf16[256,2048]{1,0:T(8,128)(2,1)S(1)}, bf16[256,2048]{1,0:T(8,128)(2,1)S(1)}, u32[]{:S(2)}, u32[]{:S(2)}) collective-permute-start(bf16[256,2048]{1,0:T(8,128)(2,1)S(1)} %get-tuple-element.80), channel_id=1, source_target_pairs={{0,1},{1,0},{2,3},{3,2},{4,5},{5,4},{6,7},{7,6},{8,9},{9,8},{10,11... | collective-permute-start | bytes 3145736 | tf_op jit(solution)/shard_map/ppermute | solution.py:139
  75.4 3.4 %collective-permute-start.17 = (bf16[128,2048]{1,0:T(8,128)(2,1)S(1)}, bf16[128,2048]{1,0:T(8,128)(2,1)S(1)}, u32[]{:S(2)}, u32[]{:S(2)}) collective-permute-start(bf16[128,2048]{1,0:T(8,128)(2,1)S(1)} %collective-permute-done.12.refs_1_), channel_id=1, source_target_pairs={{0,1},{1,0},{2,3},{3,2},{4,5},{5,4},{6,7},{7,6},{8,9},{9,8},{10,11... | collective-permute-start | bytes 1572872 | tf_op jit(solution)/shard_map/ppermute | solution.py:139
  85.1 14.5 %copy-start.20 = (bf16[320,768]{1,0:T(8,128)(2,1)}, bf16[320,768]{1,0:T(8,128)(2,1)S(1)}, u32[]{:S(2)}) copy-start(bf16[320,768]{1,0:T(8,128)(2,1)S(1)} %get-tuple-element.81) | copy-start | bytes 1474564
  85.1 2.7 %collective-permute-start.20 = (bf16[256,2048]{1,0:T(8,128)(2,1)S(1)}, bf16[256,2048]{1,0:T(8,128)(2,1)S(1)}, u32[]{:S(2)}, u32[]{:S(2)}) collective-permute-start(bf16[256,2048]{1,0:T(8,128)(2,1)S(1)} %get-tuple-element.87), channel_id=1, source_target_pairs={{0,1},{1,0},{2,3},{3,2},{4,5},{5,4},{6,7},{7,6},{8,9},{9,8},{10,11... | collective-permute-start | bytes 3145736 | tf_op jit(solution)/shard_map/ppermute | solution.py:139
  88.1 8.4 %collective-permute-start.21 = (bf16[64,2048]{1,0:T(8,128)(2,1)S(1)}, bf16[64,2048]{1,0:T(8,128)(2,1)S(1)}, u32[]{:S(2)}, u32[]{:S(2)}) collective-permute-start(bf16[64,2048]{1,0:T(8,128)(2,1)S(1)} %get-tuple-element.102), channel_id=1, source_target_pairs={{0,4},{1,5},{2,6},{3,7},{4,0},{5,1},{6,2},{7,3},{8,12},{9,13},{10,... | collective-permute-start | bytes 786440 | tf_op jit(solution)/shard_map/ppermute | solution.py:139
  89.6 8.1 %collective-permute-start.22 = (bf16[64,2048]{1,0:T(8,128)(2,1)S(1)}, bf16[64,2048]{1,0:T(8,128)(2,1)S(1)}, u32[]{:S(2)}, u32[]{:S(2)}) collective-permute-start(bf16[64,2048]{1,0:T(8,128)(2,1)S(1)} %get-tuple-element.101), channel_id=1, source_target_pairs={{0,2},{1,3},{2,0},{3,1},{4,6},{5,7},{6,4},{7,5},{8,10},{9,11},{10,... | collective-permute-start | bytes 786440 | tf_op jit(solution)/shard_map/ppermute | solution.py:139
  91.1 9.0 %collective-permute-start.19 = (bf16[256,2048]{1,0:T(8,128)(2,1)S(1)}, bf16[256,2048]{1,0:T(8,128)(2,1)S(1)}, u32[]{:S(2)}, u32[]{:S(2)}) collective-permute-start(bf16[256,2048]{1,0:T(8,128)(2,1)S(1)} %get-tuple-element.83), channel_id=1, source_target_pairs={{0,1},{1,0},{2,3},{3,2},{4,5},{5,4},{6,7},{7,6},{8,9},{9,8},{10,11... | collective-permute-start | bytes 3145736 | tf_op jit(solution)/shard_map/ppermute | solution.py:139
  98.0 12.9 %collective-permute-start.24 = (bf16[128,2048]{1,0:T(8,128)(2,1)S(1)}, bf16[128,2048]{1,0:T(8,128)(2,1)S(1)}, u32[]{:S(2)}, u32[]{:S(2)}) collective-permute-start(bf16[128,2048]{1,0:T(8,128)(2,1)S(1)} %pad_maximum_fusion.1), channel_id=1, source_target_pairs={{0,2},{1,3},{2,0},{3,1},{4,6},{5,7},{6,4},{7,5},{8,10},{9,11},{10,... | collective-permute-start | bytes 1572872 | tf_op jit(solution)/shard_map/ppermute | solution.py:139
  99.6 17.7 %copy-start.15 = (bf16[320,768]{1,0:T(8,128)(2,1)S(1)}, bf16[320,768]{1,0:T(8,128)(2,1)}, u32[]{:S(2)}) copy-start(bf16[320,768]{1,0:T(8,128)(2,1)} %copy-done.14) | copy-start | bytes 1474564
  99.6 17.7 %copy-start.17 = (bf16[320,768]{1,0:T(8,128)(2,1)S(1)}, bf16[320,768]{1,0:T(8,128)(2,1)}, u32[]{:S(2)}) copy-start(bf16[320,768]{1,0:T(8,128)(2,1)} %copy-done.16) | copy-start | bytes 1474564
  99.6 17.7 %copy-start.19 = (bf16[320,768]{1,0:T(8,128)(2,1)S(1)}, bf16[320,768]{1,0:T(8,128)(2,1)}, u32[]{:S(2)}) copy-start(bf16[320,768]{1,0:T(8,128)(2,1)} %copy-done.18) | copy-start | bytes 1474564
  99.7 17.7 %copy-start.21 = (bf16[320,768]{1,0:T(8,128)(2,1)S(1)}, bf16[320,768]{1,0:T(8,128)(2,1)}, u32[]{:S(2)}) copy-start(bf16[320,768]{1,0:T(8,128)(2,1)} %copy-done.20) | copy-start | bytes 1474564
  99.7 12.6 %collective-permute-start.23 = (bf16[128,2048]{1,0:T(8,128)(2,1)S(1)}, bf16[128,2048]{1,0:T(8,128)(2,1)S(1)}, u32[]{:S(2)}, u32[]{:S(2)}) collective-permute-start(bf16[128,2048]{1,0:T(8,128)(2,1)S(1)} %pad_maximum_fusion), channel_id=1, source_target_pairs={{0,4},{1,5},{2,6},{3,7},{4,0},{5,1},{6,2},{7,3},{8,12},{9,13},{10,... | collective-permute-start | bytes 1572872 | tf_op jit(solution)/shard_map/ppermute | solution.py:139
  113.4 24.1 %collective-permute-start.25 = (bf16[128,2048]{1,0:T(8,128)(2,1)}, bf16[128,2048]{1,0:T(8,128)(2,1)}, u32[]{:S(2)}, u32[]{:S(2)}) collective-permute-start(bf16[128,2048]{1,0:T(8,128)(2,1)} %add_convert_fusion.1), channel_id=1, source_target_pairs={{0,8},{1,9},{2,10},{3,11},{4,12},{5,13},{6,14},{7,15},{8,0},{9,1},... | collective-permute-start | bytes 1572872 | tf_op jit(solution)/shard_map/ppermute | solution.py:139
  114.9 22.5 %collective-permute-start.26 = (bf16[128,2048]{1,0:T(8,128)(2,1)}, bf16[128,2048]{1,0:T(8,128)(2,1)}, u32[]{:S(2)}, u32[]{:S(2)}) collective-permute-start(bf16[128,2048]{1,0:T(8,128)(2,1)} %add_convert_fusion.3), channel_id=1, source_target_pairs={{0,4},{1,5},{2,6},{3,7},{4,0},{5,1},{6,2},{7,3},{8,12},{9,13},{10,... | collective-permute-start | bytes 1572872 | tf_op jit(solution)/shard_map/ppermute | solution.py:139
  115.5 21.9 %collective-permute-start.27 = (bf16[128,2048]{1,0:T(8,128)(2,1)}, bf16[128,2048]{1,0:T(8,128)(2,1)}, u32[]{:S(2)}, u32[]{:S(2)}) collective-permute-start(bf16[128,2048]{1,0:T(8,128)(2,1)} %add_convert_fusion.2), channel_id=1, source_target_pairs={{0,2},{1,3},{2,0},{3,1},{4,6},{5,7},{6,4},{7,5},{8,10},{9,11},{10,... | collective-permute-start | bytes 1572872 | tf_op jit(solution)/shard_map/ppermute | solution.py:139
  117.4 20.1 %copy-start.8 = (bf16[256,2048]{1,0:T(8,128)(2,1)S(1)}, bf16[256,2048]{1,0:T(8,128)(2,1)}, u32[]{:S(2)}) copy-start(bf16[256,2048]{1,0:T(8,128)(2,1)} %copy-done.7) | copy-start | bytes 3145732

commit v13 on v12

--- a/solution.py
+++ b/solution.py
@@ -55,13 +55,8 @@
     return total.astype(jnp.bfloat16)
 
 
-def plane_kernel(capacity, k, parts, spots, weight, *refs):
-    xs, refs = refs[:parts], refs[parts:]
-    w_gate, w_up, w_down, keep, give, act, rows, ranks = refs
+def fill_tables(capacity, spots, weight, ranks, tables):
     blocks, tok = weight.shape
-    slots, hidden = act.shape
-    features = rows.shape[1]
-    wide, cut = 256, 512
     named = (weight[...] >= 0.0).astype(jnp.float32)
     lane = lax.broadcasted_iota(jnp.int32, (tok, tok), 0)
     below = (lane < lax.broadcasted_iota(jnp.int32, (tok, tok), 1)).astype(jnp.float32)
@@ -72,14 +67,26 @@
     before = jnp.dot(earlier, totals, preferred_element_type=jnp.float32)
     rank = within + before
     kept = (named > 0.0) & (rank < capacity)
-    order = [spots[4 * k + i] for i in range(4)]
-    first = order[0] // 4 * 4
-    block_row = lax.broadcasted_iota(jnp.int32, (blocks, tok), 0)
-    start = jnp.sum(jnp.where(block_row == first, before, 0.0), axis=0, keepdims=True)
+    first = lax.broadcasted_iota(jnp.int32, (blocks, blocks), 0) // 4 * 4
+    column = lax.broadcasted_iota(jnp.int32, (blocks, blocks), 1)
+    start = jnp.dot((column < first).astype(jnp.float32), totals, preferred_element_type=jnp.float32)
     ranks[...] = jnp.where(kept, rank - start, -1.0)
-    place = jnp.concatenate([ranks[pl.ds(i, 1), :] for i in order], axis=1)
-    share = jnp.concatenate([weight[pl.ds(i, 1), :] for i in order], axis=1)
-    slot = lax.broadcasted_iota(jnp.int32, (slots, 4 * tok), 0).astype(jnp.float32)
+    for k in range(blocks // 4):
+        for i in range(4):
+            span = pl.ds(i * tok, tok)
+            tables[pl.ds(k, 1), span] = ranks[pl.ds(spots[4 * k + i], 1), :]
+            tables[pl.ds(blocks // 4 + k, 1), span] = weight[pl.ds(spots[4 * k + i], 1), :]
+
+
+def plane_kernel(k, tables, *refs):
+    *xs, w_gate, w_up, w_down, keep, give, act, rows = refs
+    slots, hidden = act.shape
+    features = rows.shape[1]
+    half, width = keep.shape[0], tables.shape[1]
+    wide, cut = 256, 512
+    place = tables[pl.ds(k, 1), :]
+    share = tables[pl.ds(tables.shape[0] // 2 + k, 1), :]
+    slot = lax.broadcasted_iota(jnp.int32, (slots, width), 0).astype(jnp.float32)
     hits = slot == place
     scale = jnp.sum(jnp.where(hits, share, 0.0), axis=1, keepdims=True)
     select = hits.astype(jnp.float32).astype(jnp.bfloat16)
@@ -98,32 +105,65 @@
         result = jnp.dot(act[...], w_down[:, span], preferred_element_type=jnp.float32)
         made = (result * scale).astype(jnp.bfloat16)
         spread = jnp.dot(back, made, preferred_element_type=jnp.float32).astype(jnp.bfloat16)
-        keep[:, span] = spread[: 2 * tok]
-        give[:, span] = spread[2 * tok :]
-
-
-def plane_pass(k, spots, weight, xs, w_gate, w_up, w_down, slots, capacity):
-    tok, features = weight.shape[1], w_gate.shape[0]
+        keep[:, span] = spread[:half]
+        give[:, span] = spread[half:]
+
+
+def first_kernel(capacity, spots, weight, *refs):
+    *plane, tables, rows, ranks = refs
+    fill_tables(capacity, spots, weight, ranks, tables)
+    plane_kernel(0, tables, *plane, rows)
+
+
+def plane_pass(k, tables, xs, w_gate, w_up, w_down, slots, first=None):
+    tok, features = xs[0].shape
     hidden = w_gate.shape[1]
+    rows = 4 * slots
     half = jax.ShapeDtypeStruct((2 * tok, features), jnp.bfloat16)
-    rows = 4 * slots
+    outs = (half, half, jax.ShapeDtypeStruct((rows, hidden), jnp.bfloat16))
+    scratch = [pltpu.VMEM((rows, features), jnp.bfloat16)]
+    vmem = pl.BlockSpec(memory_space=pltpu.VMEM)
+    if first is None:
+        body, inputs, specs = functools.partial(plane_kernel, k), (tables,), [vmem]
+    else:
+        capacity, spots, weight = first
+        body = functools.partial(first_kernel, capacity)
+        inputs, specs = (spots, weight), [pl.BlockSpec(memory_space=pltpu.SMEM), vmem]
+        outs += (jax.ShapeDtypeStruct((weight.shape[0] // 2, 4 * tok), jnp.float32),)
+        scratch.append(pltpu.VMEM(weight.shape, jnp.float32))
     flops = 2 * rows * (3 * features * hidden + 8 * tok * features)
     moved = 2 * (3 * features * hidden + 8 * tok * features)
     return pl.pallas_call(
-        functools.partial(plane_kernel, capacity, k, len(xs)),
-        out_shape=(half, half, jax.ShapeDtypeStruct((rows, hidden), jnp.bfloat16)),
-        in_specs=[pl.BlockSpec(memory_space=pltpu.SMEM)]
-        + [pl.BlockSpec(memory_space=pltpu.VMEM)] * (len(xs) + 4),
-        out_specs=[pl.BlockSpec(memory_space=pltpu.VMEM)] * 3,
-        scratch_shapes=[
-            pltpu.VMEM((rows, features), jnp.bfloat16),
-            pltpu.VMEM(weight.shape, jnp.float32),
-        ],
+        body,
+        out_shape=outs,
+        in_specs=specs + [vmem] * (len(xs) + 3),
+        out_specs=[vmem] * len(outs),
+        scratch_shapes=scratch,
         compiler_params=pltpu.CompilerParams(vmem_limit_bytes=12 * 1024 * 1024),
         cost_estimate=pl.CostEstimate(
             flops=flops, bytes_accessed=moved, transcendentals=rows * hidden
         ),
-    )(spots, weight, *xs, w_gate, w_up, w_down)
+    )(*inputs, *xs, w_gate, w_up, w_down)
+
+
+def mix_kernel(keep, got, side, near_low, far_low, near_high, far_high, mixed):
+    most, tok = near_low.shape[0], mixed.shape[0]
+    for start, stop, near, far in ((0, most, near_low, far_low), (most, tok, near_high, far_high)):
+        total = keep[start:stop, :].astype(jnp.float32) + got[start:stop, :].astype(jnp.float32)
+        total = total + side[start:stop, :].astype(jnp.float32) + near[...].astype(jnp.float32)
+        mixed[start:stop, :] = (total + far[...].astype(jnp.float32)).astype(mixed.dtype)
+
+
+def mix_pass(*parts):
+    side = parts[2]
+    vmem = pl.BlockSpec(memory_space=pltpu.VMEM)
+    return pl.pallas_call(
+        mix_kernel,
+        out_shape=jax.ShapeDtypeStruct(side.shape, side.dtype),
+        in_specs=[vmem] * len(parts),
+        out_specs=vmem,
+        compiler_params=pltpu.CompilerParams(vmem_limit_bytes=12 * 1024 * 1024),
+    )(*parts)
 
 
 def staged(routes, probs, tokens, w_gate, w_up, w_down):
@@ -155,8 +195,8 @@
         ]
     ).astype(jnp.int32)
 
-    def expert(k, *xs):
-        return plane_pass(k, spots, weight, xs, w_gate, w_up, w_down, slots, capacity)
+    def expert(k, tables, *xs, first=None):
+        return plane_pass(k, tables, xs, w_gate, w_up, w_down, slots, first)
 
     weight = table_pass(routes, probs, size, w_gate, w_up, w_down)
     a0 = tokens
@@ -167,49 +207,61 @@
     b1 = column(a1)
     d0 = sibling(b0)
     c1 = sibling(a1)
-    keep0, give0, act0 = expert(0, a0, b0, c0, d0)
-    high, b1, c1, keep0, give0, act0 = together(high, b1, c1, keep0, give0, act0)
+    keep0, give0, act0, tables = expert(
+        0, None, a0, b0, c0, d0, first=(capacity, spots, weight)
+    )
+    high, b1, c1, keep0, give0, act0, tables = together(
+        high, b1, c1, keep0, give0, act0, tables
+    )
     a2 = jnp.concatenate([low, high], axis=0)
     a3 = pair(a2)
     b2 = column(a2)
     d1 = sibling(b1)
     c2 = sibling(a2)
-    keep1, give1, act1 = expert(1, a1, b1, c1, d1)
+    keep1, give1, act1 = expert(1, tables, a1, b1, c1, d1)
     a3, b2, c2, keep1, give1, act1 = together(a3, b2, c2, keep1, give1, act1)
     b3 = pair(b2)
     got1 = sibling(give1)
     came1 = column(summed(keep1[tok:], got1[tok:]))
     d2 = sibling(b2)
     c3 = sibling(a3)
-    keep2, give2, act2 = expert(2, a2, b2, c2, d2)
+    keep2, give2, act2 = expert(2, tables, a2, b2, c2, d2)
     b3, came1, c3, keep2, give2, act2 = together(b3, came1, c3, keep2, give2, act2)
+    near1 = summed(keep1[:tok], got1[:tok], came1)
+    most = 5 * tok // 8
     d3 = sibling(b3)
     got2 = sibling(give2)
-    keep3, give3, act3 = expert(3, a3, b3, c3, d3)
-    keep3, give3, act3, got2 = together(keep3, give3, act3, got2)
+    near1_low = pair(near1[:most])
+    keep3, give3, act3 = expert(3, tables, a3, b3, c3, d3)
+    keep3, give3, act3, got2, near1, near1_low = together(
+        keep3, give3, act3, got2, near1, near1_low
+    )
     got0 = sibling(give0)
 
+    def own(keep, got, start, stop, *more):
+        return summed(keep[start:stop], got[start:stop], *more)
+
     got3 = sibling(give3)
-    low = pair(summed(keep3[tok : tok + half], got3[tok : tok + half]))
-    high = column(summed(keep3[tok + half :], got3[tok + half :]))
-    low, high = together(low, high)
-    far3 = jnp.concatenate(
-        [summed(keep3[:half], got3[:half]), summed(keep3[half:tok], got3[half:tok], high)], axis=0
-    )
-    side2 = jnp.concatenate(
-        [
-            summed(keep2[tok : tok + half], got2[tok : tok + half], low),
-            summed(keep2[tok + half :], got2[tok + half :]),
-        ],
-        axis=0,
-    )
-    near1 = summed(keep1[:tok], got1[:tok], came1)
-    side0 = summed(keep0[tok:], got0[tok:])
-    far3, side2, near1, side0 = together(pair(far3), column(side2), near1, side0)
-    far2, near1, side0 = together(
-        summed(keep2[:tok], got2[:tok], far3, side2), near1, side0
-    )
-    mixed = summed(keep0[:tok], got0[:tok], far(far2), pair(near1), column(side0))
+    low = pair(own(keep3, got3, tok, tok + most))
+    high = column(own(keep3, got3, tok + most, 2 * tok))
+    side_high = column(own(keep2, got2, tok + most, 2 * tok))
+    sum3 = own(keep3, got3, 0, most)
+    low, high, side_high, got0, sum3 = together(low, high, side_high, got0, sum3)
+    far3_high = far(own(keep3, got3, most, tok, high))
+    far2_high = far(own(keep2, got2, most, tok, side_high))
+    pair3_low = pair(sum3)
+    side_low = column(own(keep2, got2, tok, tok + most, low))
+    side0 = own(keep0, got0, tok, 2 * tok)
+    far3_high, far2_high, pair3_low, side_low, side0 = together(
+        far3_high, far2_high, pair3_low, side_low, side0
+    )
+    sum2 = own(keep2, got2, 0, most, pair3_low, side_low)
+    sum1 = summed(near1[most:], far3_high)
+    sum2, sum1, side0 = together(sum2, sum1, side0)
+    far2_low = far(sum2)
+    near1_high = pair(sum1)
+    last0 = column(side0)
+    mixed = mix_pass(keep0, got0, last0, near1_low, far2_low, near1_high, far2_high)
 
     acts = jnp.concatenate([act0, act1, act2, act3], axis=0)
     count = jnp.minimum(jnp.sum((weight >= 0.0).astype(jnp.float32)), float(capacity))

time: 141 us -> 141 us (level)
  starting transfers between devices: 22.2 us -> 30.8 us
  waiting for transfers between devices: 52 us -> 45.7 us
  other arithmetic: 7.01 us -> 3.33 us
  matrix products: 3.16 us -> 4.98 us
    ppermute x28 -> x32, starting transfers between devices: 22.2 us -> 30.8 us  [swapped(): return lax.ppermute(array, 'expert', [(i, i ^ bit) for i in range(size)])]
    ppermute x28 -> x32, waiting for transfers between devices: 52 us -> 45.7 us  [swapped(): return lax.ppermute(array, 'expert', [(i, i ^ bit) for i in range(size)])]
    convert_element_type x8 -> x11, other arithmetic: 6.3 us -> 2.76 us  [summed(): return total.astype(jnp.bfloat16)]
    dot_general x1, matrix products: 3.16 us -> 4.98 us  [gram_of(): lax.dot_general(rows, rows, (((0,), (0,)), ((), ())), preferred_element_t...]
    pallas_call x4 -> x5, Pallas kernels: 26.6 us -> 26.2 us  [the longest x4 25.1 us: plane_pass(): pl.pallas_call(body, out_shape=outs, in_specs=specs + [vmem] * (len(xs) +...]
    unnamed x45 -> x41, local copies, waits for them, and re-layouts: 15.3 us -> 15.3 us
  transfers between devices with their start and end apart: 28 -> 32, of which waited for: 14 -> 17; matrix products, arithmetic and copies ran while one was open for 7% -> 7% of each run, Pallas kernels for 19% -> 18%
where the time goes in v13:
time: 141 us; the launch traced here: 140 us
  waiting for transfers between devices  45.7 us (32%)
  starting transfers between devices  30.8 us (22%)
  Pallas kernels  26.2 us (19%)
  local copies, waits for them, and re-layouts  18.2 us (13%)
  blocking collectives  9.24 us (7%)
  matrix products  4.98 us (4%)
  other arithmetic  3.33 us (2%)
  between operations  1.45 us (1%)
    ppermute x32, waiting for transfers between devices, swapped(): return lax.ppermute(array, 'expert', [(i, i ^ bit) for i in range(size)])  45.7 us
    ppermute x32, starting transfers between devices, swapped(): return lax.ppermute(array, 'expert', [(i, i ^ bit) for i in range(size)])  30.8 us
    pallas_call x4, Pallas kernels, plane_pass(): pl.pallas_call(body, out_shape=outs, in_specs=specs + [vmem] * (len(xs) +...  25.1 us
    unnamed x41, local copies, waits for them, and re-layouts  15.3 us
    all_to_all x1, blocking collectives, table_pass(): lax.all_to_all(mine, 'expert', split_axis=0, concat_axis=0, tiled=True)  9.24 us
    dot_general x1, matrix products, gram_of(): lax.dot_general(rows, rows, (((0,), (0,)), ((), ())), preferred_element_t...  4.98 us
  transfers between devices with their start and end apart: 32, of which 17 were waited for; matrix products, arithmetic and copies ran while one was open for 7% of the time, Pallas kernels for 18%

profile of v13, /device:TPU:0, one launch (start us, length us, event | category | flops | bytes accessed | tf_op | source)
XLA Modules:
  0.0 139.9 jit_solution(9309536363580585181)
XLA Ops:
  0.6 3.1 %collective-permute-start.1 = (bf16[128,2048]{1,0:T(8,128)(2,1)}, bf16[128,2048]{1,0:T(8,128)(2,1)}, u32[]{:S(2)}, u32[]{:S(2)}) collective-permute-start(bf16[128,2048]{1,0:T(8,128)(2,1)} %refs_0_.1), channel_id=1, source_target_pairs={{0,4},{1,5},{2,6},{3,7},{4,0},{5,1},{6,2},{7,3},{8,12},{9,13},{10,... | collective-permute-start | bytes 1572872 | tf_op jit(solution)/shard_map/ppermute | solution.py:179
  3.7 1.5 %collective-permute-start.3 = (bf16[128,2048]{1,0:T(8,128)(2,1)}, bf16[128,2048]{1,0:T(8,128)(2,1)}, u32[]{:S(2)}, u32[]{:S(2)}) collective-permute-start(bf16[128,2048]{1,0:T(8,128)(2,1)} %refs_0_.1), channel_id=1, source_target_pairs={{0,2},{1,3},{2,0},{3,1},{4,6},{5,7},{6,4},{7,5},{8,10},{9,11},{10,... | collective-permute-start | bytes 1572872 | tf_op jit(solution)/shard_map/ppermute | solution.py:179
  5.2 1.8 %fusion.11 = (bf16[64,2048]{1,0:T(8,128)(2,1)}, bf16[64,2048]{1,0:T(8,128)(2,1)S(1)}) fusion(bf16[128,2048]{1,0:T(8,128)(2,1)} %refs_0_.1), kind=kLoop, calls=%fused_computation.25 | loop fusion | bytes 1048576 | tf_op jit(solution)/shard_map/slice | solution.py:206
  7.0 2.6 %collective-permute-start.2 = (bf16[64,2048]{1,0:T(8,128)(2,1)S(1)}, bf16[64,2048]{1,0:T(8,128)(2,1)S(1)}, u32[]{:S(2)}, u32[]{:S(2)}) collective-permute-start(bf16[64,2048]{1,0:T(8,128)(2,1)S(1)} %get-tuple-element.117), channel_id=1, source_target_pairs={{0,8},{1,9},{2,10},{3,11},{4,12},{5,13},{6,14},{7,15},{8,0},{9,1},... | collective-permute-start | bytes 786440 | tf_op jit(solution)/shard_map/ppermute | solution.py:179
  9.6 1.9 %copy-done = bf16[1,2048,768]{2,1,0:T(8,128)(2,1)S(1)} copy-done((bf16[1,2048,768]{2,1,0:T(8,128)(2,1)S(1)}, bf16[1,2048,768]{2,1,0:T(8,128)(2,1)}, u32[]{:S(2)}) %copy-start) | copy-done | bytes 3145752
  11.5 1.9 %copy-done.2 = bf16[1,2048,768]{2,1,0:T(8,128)(2,1)S(1)} copy-done((bf16[1,2048,768]{2,1,0:T(8,128)(2,1)S(1)}, bf16[1,2048,768]{2,1,0:T(8,128)(2,1)}, u32[]{:S(2)}) %copy-start.2) | copy-done | bytes 3145752
  13.4 1.9 %copy-done.5 = bf16[1,768,2048]{2,1,0:T(8,128)(2,1)S(1)} copy-done((bf16[1,768,2048]{2,1,0:T(8,128)(2,1)S(1)}, bf16[1,768,2048]{2,1,0:T(8,128)(2,1)}, u32[]{:S(2)}) %copy-start.5) | copy-done | bytes 3145752
  15.3 0.7 copy-done.11
  16.0 0.7 copy-done.12
  16.7 9.2 %all_to_all.12 = f32[16,1,128]{2,1,0:T(1,128)S(1)} all-to-all(f32[16,1,128]{2,1,0:T(1,128)S(1)} %bitcast.42), channel_id=1, replica_groups=mesh['parts'=2,'expert'=16] {'expert'}, dimensions={0} | all-to-all | bytes 16384 | tf_op jit(solution)/shard_map/all_to_all | solution.py:48
  26.0 0.8 copy-done.13
  26.8 0.5 collective-permute-start.5
  27.5 0.6 collective-permute-start
  28.2 0.8 collective-permute-done.7.refs_3_
  29.0 1.9 %copy-done.3 = bf16[1,2048,768]{2,1,0:T(8,128)(2,1)S(1)} copy-done((bf16[1,2048,768]{2,1,0:T(8,128)(2,1)S(1)}, bf16[1,2048,768]{2,1,0:T(8,128)(2,1)}, u32[]{:S(2)}) %copy-start.3) | copy-done | bytes 3145752
  30.9 1.9 %copy-done.6 = bf16[1,768,2048]{2,1,0:T(8,128)(2,1)S(1)} copy-done((bf16[1,768,2048]{2,1,0:T(8,128)(2,1)S(1)}, bf16[1,768,2048]{2,1,0:T(8,128)(2,1)}, u32[]{:S(2)}) %copy-start.6) | copy-done | bytes 3145752
  32.8 1.0 copy-done.10
  33.8 1.0 copy-done.14
  34.9 7.0 %shard_map.78 = (bf16[256,2048]{1,0:T(8,128)(2,1)S(1)}, bf16[256,2048]{1,0:T(8,128)(2,1)S(1)}, bf16[320,768]{1,0:T(8,128)(2,1)S(1)}, f32[8,512]{1,0:T(8,128)S(1)}) custom-call(s32[16]{0:T(128)S(1)} %stack.67.spots, f32[16,128]{1,0:T(8,128)S(1)} %bitcast.43, bf16[128,2048]{1,0:T(8,128)(2,1)S(1)} %copy-done.10, ...), custom_call_target="tpu_custom_call" | custom-call | flops 4362076160 | bytes 13631488 | tf_op jit(solution)/shard_map/pallas_call | solution.py:136
  41.9 0.8 copy-done.19
  42.9 1.1 constant_dynamic-update-slice_fusion.refs_0_
  44.0 0.4 collective-permute-start.10
  44.4 0.4 collective-permute-start.8
  44.8 1.1 collective-permute-start.9
  45.9 6.9 %shard_map.79 = (bf16[256,2048]{1,0:T(8,128)(2,1)S(1)}, bf16[256,2048]{1,0:T(8,128)(2,1)S(1)}, bf16[320,768]{1,0:T(8,128)(2,1)S(1)}) custom-call(f32[8,512]{1,0:T(8,128)S(1)} %get-tuple-element.69.tables, bf16[128,2048]{1,0:T(8,128)(2,1)} %collective-permute-done.1.refs_0_, bf16[128,2048]{1,0:T(8,128)(2,1)} %collective-permute-done.5.refs_1_, ...), custom_call_target="tpu_custom_call" | custom-call | flops 4362076160 | bytes 13631488 | tf_op jit(solution)/shard_map/pallas_call | solution.py:136
  52.8 5.6 %collective-permute-done.8.refs_0_ = bf16[128,2048]{1,0:T(8,128)(2,1)S(1)} collective-permute-done((bf16[128,2048]{1,0:T(8,128)(2,1)S(1)}, bf16[128,2048]{1,0:T(8,128)(2,1)S(1)}, u32[]{:S(2)}, u32[]{:S(2)}) %collective-permute-start.8) | collective-permute-done | bytes 524320 | tf_op jit(solution)/shard_map/ppermute | solution.py:179
  58.4 0.2 collective-permute-done.9.refs_1_
  58.6 0.5 collective-permute-start.16
  59.1 1.5 %collective-permute-start.12 = (bf16[128,2048]{1,0:T(8,128)(2,1)S(1)}, bf16[128,2048]{1,0:T(8,128)(2,1)S(1)}, u32[]{:S(2)}, u32[]{:S(2)}) collective-permute-start(bf16[128,2048]{1,0:T(8,128)(2,1)S(1)} %collective-permute-done.9.refs_1_), channel_id=1, source_target_pairs={{0,4},{1,5},{2,6},{3,7},{4,0},{5,1},{6,2},{7,3},{8,12},{9,13},{10,... | collective-permute-start | bytes 1572872 | tf_op jit(solution)/shard_map/ppermute | solution.py:179
  60.7 0.6 collective-permute-done.13
  61.4 1.3 collective-permute-start.14
  62.7 5.7 %shard_map.80 = (bf16[256,2048]{1,0:T(8,128)(2,1)S(1)}, bf16[256,2048]{1,0:T(8,128)(2,1)S(1)}, bf16[320,768]{1,0:T(8,128)(2,1)S(1)}) custom-call(f32[8,512]{1,0:T(8,128)S(1)} %get-tuple-element.69.tables, bf16[128,2048]{1,0:T(8,128)(2,1)S(1)} %constant_dynamic-update-slice_fusion.refs_0_, bf16[128,2048]{1,0:T(8,128)(2,1)S(1)} %collective-permute-done.9.refs_1_, ...), custom_call_target="tpu_custom_call" | custom-call | flops 4362076160 | bytes 13631488 | tf_op jit(solution)/shard_map/pallas_call | solution.py:136
  68.4 0.8 copy-done.17
  69.2 3.7 %collective-permute-done.12.refs_1_ = bf16[128,2048]{1,0:T(8,128)(2,1)S(1)} collective-permute-done((bf16[128,2048]{1,0:T(8,128)(2,1)S(1)}, bf16[128,2048]{1,0:T(8,128)(2,1)S(1)}, u32[]{:S(2)}, u32[]{:S(2)}) %collective-permute-start.12) | collective-permute-done | bytes 524320 | tf_op jit(solution)/shard_map/ppermute | solution.py:179
  73.0 2.5 %collective-permute-done.14 = bf16[128,2048]{1,0:T(8,128)(2,1)S(1)} collective-permute-done((bf16[128,2048]{1,0:T(8,128)(2,1)S(1)}, bf16[128,2048]{1,0:T(8,128)(2,1)S(1)}, u32[]{:S(2)}, u32[]{:S(2)}) %collective-permute-start.14) | collective-permute-done | bytes 524320 | tf_op jit(solution)/shard_map/ppermute | solution.py:179
  75.5 0.5 collective-permute-start.17
  76.0 0.2 add_convert_fusion.1
  76.2 1.6 %collective-permute-start.19 = (bf16[80,2048]{1,0:T(8,128)(2,1)S(1)}, bf16[80,2048]{1,0:T(8,128)(2,1)S(1)}, u32[]{:S(2)}, u32[]{:S(2)}) collective-permute-start(bf16[80,2048]{1,0:T(8,128)(2,1)S(1)} %slice.106), channel_id=1, source_target_pairs={{0,4},{1,5},{2,6},{3,7},{4,0},{5,1},{6,2},{7,3},{8,12},{9,13},{10,... | collective-permute-start | bytes 983048 | tf_op jit(solution)/shard_map/ppermute | solution.py:179
  77.8 1.0 collective-permute-done.17.refs_3_
  78.9 5.5 %shard_map.81 = (bf16[256,2048]{1,0:T(8,128)(2,1)S(1)}, bf16[256,2048]{1,0:T(8,128)(2,1)S(1)}, bf16[320,768]{1,0:T(8,128)(2,1)S(1)}) custom-call(f32[8,512]{1,0:T(8,128)S(1)} %get-tuple-element.69.tables, bf16[128,2048]{1,0:T(8,128)(2,1)S(1)} %collective-permute-done.8.refs_0_, bf16[128,2048]{1,0:T(8,128)(2,1)S(1)} %collective-permute-done.12.refs_1_, ...), custom_call_target="tpu_custom_call" | custom-call | flops 4362076160 | bytes 13631488 | tf_op jit(solution)/shard_map/pallas_call | solution.py:136
  84.4 1.5 %collective-permute-done.19.near_low = bf16[80,2048]{1,0:T(8,128)(2,1)S(1)} collective-permute-done((bf16[80,2048]{1,0:T(8,128)(2,1)S(1)}, bf16[80,2048]{1,0:T(8,128)(2,1)S(1)}, u32[]{:S(2)}, u32[]{:S(2)}) %collective-permute-start.19) | collective-permute-done | bytes 327712 | tf_op jit(solution)/shard_map/ppermute | solution.py:179
  85.9 0.5 collective-permute-start.24
  86.5 1.3 collective-permute-start.23
  87.8 0.8 collective-permute-done.20
  88.8 1.6 %collective-permute-start.21 = (bf16[80,2048]{1,0:T(8,128)(2,1)S(1)}, bf16[80,2048]{1,0:T(8,128)(2,1)S(1)}, u32[]{:S(2)}, u32[]{:S(2)}) collective-permute-start(bf16[80,2048]{1,0:T(8,128)(2,1)S(1)} %get-tuple-element.115), channel_id=1, source_target_pairs={{0,4},{1,5},{2,6},{3,7},{4,0},{5,1},{6,2},{7,3},{8,12},{9,13},{10,... | collective-permute-start | bytes 983048 | tf_op jit(solution)/shard_map/ppermute | solution.py:179
  90.4 1.5 %collective-permute-start.22 = (bf16[48,2048]{1,0:T(8,128)(2,1)S(1)}, bf16[48,2048]{1,0:T(8,128)(2,1)S(1)}, u32[]{:S(2)}, u32[]{:S(2)}) collective-permute-start(bf16[48,2048]{1,0:T(8,128)(2,1)S(1)} %add_convert_fusion.11), channel_id=1, source_target_pairs={{0,2},{1,3},{2,0},{3,1},{4,6},{5,7},{6,4},{7,5},{8,10},{9,11},{10,... | collective-permute-start | bytes 589832 | tf_op jit(solution)/shard_map/ppermute | solution.py:179
  91.9 1.8 %collective-permute-done.23 = bf16[48,2048]{1,0:T(8,128)(2,1)S(1)} collective-permute-done((bf16[48,2048]{1,0:T(8,128)(2,1)S(1)}, bf16[48,2048]{1,0:T(8,128)(2,1)S(1)}, u32[]{:S(2)}, u32[]{:S(2)}) %collective-permute-start.23) | collective-permute-done | bytes 196640 | tf_op jit(solution)/shard_map/ppermute | solution.py:179
  93.7 3.9 %collective-permute-done.22 = bf16[48,2048]{1,0:T(8,128)(2,1)S(1)} collective-permute-done((bf16[48,2048]{1,0:T(8,128)(2,1)S(1)}, bf16[48,2048]{1,0:T(8,128)(2,1)S(1)}, u32[]{:S(2)}, u32[]{:S(2)}) %collective-permute-start.22) | collective-permute-done | bytes 196640 | tf_op jit(solution)/shard_map/ppermute | solution.py:179
  97.6 1.0 collective-permute-done.21
  98.8 1.3 collective-permute-start.28
  100.1 1.8 %collective-permute-start.26 = (bf16[48,2048]{1,0:T(8,128)(2,1)S(1)}, bf16[48,2048]{1,0:T(8,128)(2,1)S(1)}, u32[]{:S(2)}, u32[]{:S(2)}) collective-permute-start(bf16[48,2048]{1,0:T(8,128)(2,1)S(1)} %add_convert_fusion.8), channel_id=1, source_target_pairs={{0,8},{1,9},{2,10},{3,11},{4,12},{5,13},{6,14},{7,15},{8,0},{9,1},... | collective-permute-start | bytes 589832 | tf_op jit(solution)/shard_map/ppermute | solution.py:179
  102.0 1.2 collective-permute-start.25
  103.3 1.7 %collective-permute-start.27 = (bf16[80,2048]{1,0:T(8,128)(2,1)S(1)}, bf16[80,2048]{1,0:T(8,128)(2,1)S(1)}, u32[]{:S(2)}, u32[]{:S(2)}) collective-permute-start(bf16[80,2048]{1,0:T(8,128)(2,1)S(1)} %get-tuple-element.102), channel_id=1, source_target_pairs={{0,4},{1,5},{2,6},{3,7},{4,0},{5,1},{6,2},{7,3},{8,12},{9,13},{10,... | collective-permute-start | bytes 983048 | tf_op jit(solution)/shard_map/ppermute | solution.py:179
  104.9 0.9 add_convert_fusion
  105.9 10.8 %collective-permute-done.26.far_high = bf16[48,2048]{1,0:T(8,128)(2,1)S(1)} collective-permute-done((bf16[48,2048]{1,0:T(8,128)(2,1)S(1)}, bf16[48,2048]{1,0:T(8,128)(2,1)S(1)}, u32[]{:S(2)}, u32[]{:S(2)}) %collective-permute-start.26) | collective-permute-done | bytes 196640 | tf_op jit(solution)/shard_map/ppermute | solution.py:179
  116.6 2.9 %collective-permute-done.25 = bf16[48,2048]{1,0:T(8,128)(2,1)S(1)} collective-permute-done((bf16[48,2048]{1,0:T(8,128)(2,1)S(1)}, bf16[48,2048]{1,0:T(8,128)(2,1)S(1)}, u32[]{:S(2)}, u32[]{:S(2)}) %collective-permute-start.25) | collective-permute-done | bytes 196640 | tf_op jit(solution)/shard_map/ppermute | solution.py:179
  119.6 0.7 add_convert_fusion.7
  120.5 0.8 collective-permute-start.29
  121.3 0.6 convert_reduce_fusion
  122.7 2.9 %collective-permute-start.31 = (bf16[48,2048]{1,0:T(8,128)(2,1)}, bf16[48,2048]{1,0:T(8,128)(2,1)S(1)}, u32[]{:S(2)}, u32[]{:S(2)}) collective-permute-start(bf16[48,2048]{1,0:T(8,128)(2,1)} %add_convert_fusion.7), channel_id=1, source_target_pairs={{0,4},{1,5},{2,6},{3,7},{4,0},{5,1},{6,2},{7,3},{8,12},{9,13},{10,... | collective-permute-start | bytes 589832 | tf_op jit(solution)/shard_map/ppermute | solution.py:179
  125.6 5.0 %multiply_bitcast_fusion = f32[1,768,768]{2,1,0:T(8,128)} fusion(f32[]{:T(128)S(6)} %div.24, bf16[320,768]{1,0:T(8,128)(2,1)} %copy-done.18, bf16[320,768]{1,0:T(8,128)(2,1)} %copy-done.17, bf16[320,768]{1,0:T(8,128)(2,1)S(1)} %copy-done.16, bf16[320,768]{1,0:T(8,128)(2,1)} %copy-done.19), kind=kOutput, calls=%fused_computation | convolution fusion | flops 1518403584 | bytes 4325380 | tf_op jit(solution)/shard_map/dot_general | solution.py:12
  130.6 2.4 %collective-permute-done.31.near_high = bf16[48,2048]{1,0:T(8,128)(2,1)S(1)} collective-permute-done((bf16[48,2048]{1,0:T(8,128)(2,1)}, bf16[48,2048]{1,0:T(8,128)(2,1)S(1)}, u32[]{:S(2)}, u32[]{:S(2)}) %collective-permute-start.31) | collective-permute-done | bytes 196640 | tf_op jit(solution)/shard_map/ppermute | solution.py:179
  133.1 5.8 %collective-permute-done.30.far_low = bf16[80,2048]{1,0:T(8,128)(2,1)S(1)} collective-permute-done((bf16[80,2048]{1,0:T(8,128)(2,1)S(1)}, bf16[80,2048]{1,0:T(8,128)(2,1)S(1)}, u32[]{:S(2)}, u32[]{:S(2)}) %collective-permute-start.30) | collective-permute-done | bytes 327712 | tf_op jit(solution)/shard_map/ppermute | solution.py:179
  138.8 1.1 shard_map.82
  (65 shorter events, 1.8 us)
Async XLA Ops:
  0.6 25.3 %collective-permute-start.1 = (bf16[128,2048]{1,0:T(8,128)(2,1)}, bf16[128,2048]{1,0:T(8,128)(2,1)}, u32[]{:S(2)}, u32[]{:S(2)}) collective-permute-start(bf16[128,2048]{1,0:T(8,128)(2,1)} %refs_0_.1), channel_id=1, source_target_pairs={{0,4},{1,5},{2,6},{3,7},{4,0},{5,1},{6,2},{7,3},{8,12},{9,13},{10,... | collective-permute-start | bytes 1572872 | tf_op jit(solution)/shard_map/ppermute | solution.py:179
  3.7 22.2 %collective-permute-start.3 = (bf16[128,2048]{1,0:T(8,128)(2,1)}, bf16[128,2048]{1,0:T(8,128)(2,1)}, u32[]{:S(2)}, u32[]{:S(2)}) collective-permute-start(bf16[128,2048]{1,0:T(8,128)(2,1)} %refs_0_.1), channel_id=1, source_target_pairs={{0,2},{1,3},{2,0},{3,1},{4,6},{5,7},{6,4},{7,5},{8,10},{9,11},{10,... | collective-permute-start | bytes 1572872 | tf_op jit(solution)/shard_map/ppermute | solution.py:179
  5.2 20.7 %collective-permute-start.4 = (bf16[128,2048]{1,0:T(8,128)(2,1)}, bf16[128,2048]{1,0:T(8,128)(2,1)S(1)}, u32[]{:S(2)}, u32[]{:S(2)}) collective-permute-start(bf16[128,2048]{1,0:T(8,128)(2,1)} %refs_0_.1), channel_id=1, source_target_pairs={{0,1},{1,0},{2,3},{3,2},{4,5},{5,4},{6,7},{7,6},{8,9},{9,8},{10,11... | collective-permute-start | bytes 1572872 | tf_op jit(solution)/shard_map/ppermute | solution.py:179
  7.0 18.9 %collective-permute-start.2 = (bf16[64,2048]{1,0:T(8,128)(2,1)S(1)}, bf16[64,2048]{1,0:T(8,128)(2,1)S(1)}, u32[]{:S(2)}, u32[]{:S(2)}) collective-permute-start(bf16[64,2048]{1,0:T(8,128)(2,1)S(1)} %get-tuple-element.117), channel_id=1, source_target_pairs={{0,8},{1,9},{2,10},{3,11},{4,12},{5,13},{6,14},{7,15},{8,0},{9,1},... | collective-permute-start | bytes 786440 | tf_op jit(solution)/shard_map/ppermute | solution.py:179
  9.6 1.9 %copy-start = (bf16[1,2048,768]{2,1,0:T(8,128)(2,1)S(1)}, bf16[1,2048,768]{2,1,0:T(8,128)(2,1)}, u32[]{:S(2)}) copy-start(bf16[1,2048,768]{2,1,0:T(8,128)(2,1)} %param.9) | copy-start | bytes 9437188
  11.5 1.9 %copy-start.2 = (bf16[1,2048,768]{2,1,0:T(8,128)(2,1)S(1)}, bf16[1,2048,768]{2,1,0:T(8,128)(2,1)}, u32[]{:S(2)}) copy-start(bf16[1,2048,768]{2,1,0:T(8,128)(2,1)} %param.10) | copy-start | bytes 9437188
  13.4 1.9 %copy-start.5 = (bf16[1,768,2048]{2,1,0:T(8,128)(2,1)S(1)}, bf16[1,768,2048]{2,1,0:T(8,128)(2,1)}, u32[]{:S(2)}) copy-start(bf16[1,768,2048]{2,1,0:T(8,128)(2,1)} %param.11) | copy-start | bytes 9437188
  15.3 0.7 copy-start.11
  16.0 0.7 copy-start.12
  16.6 12.4 %copy-start.1 = (bf16[1,2048,768]{2,1,0:T(8,128)(2,1)S(1)}, bf16[1,2048,768]{2,1,0:T(8,128)(2,1)}, u32[]{:S(2)}) copy-start(bf16[1,2048,768]{2,1,0:T(8,128)(2,1)} %param.9) | copy-start | bytes 9437188
  26.0 0.8 copy-start.13
  26.8 2.3 %collective-permute-start.7 = (bf16[128,2048]{1,0:T(8,128)(2,1)}, bf16[128,2048]{1,0:T(8,128)(2,1)}, u32[]{:S(2)}, u32[]{:S(2)}) collective-permute-start(bf16[128,2048]{1,0:T(8,128)(2,1)} %collective-permute-done.3.refs_1_), channel_id=1, source_target_pairs={{0,1},{1,0},{2,3},{3,2},{4,5},{5,4},{6,7},{7,6},{8,9},{9,8},{10,11... | collective-permute-start | bytes 1572872 | tf_op jit(solution)/shard_map/ppermute | solution.py:179
  26.8 16.1 %collective-permute-start.5 = (bf16[128,2048]{1,0:T(8,128)(2,1)}, bf16[128,2048]{1,0:T(8,128)(2,1)}, u32[]{:S(2)}, u32[]{:S(2)}) collective-permute-start(bf16[128,2048]{1,0:T(8,128)(2,1)} %collective-permute-done.1.refs_0_), channel_id=1, source_target_pairs={{0,2},{1,3},{2,0},{3,1},{4,6},{5,7},{6,4},{7,5},{8,10},{9,11},{10,... | collective-permute-start | bytes 1572872 | tf_op jit(solution)/shard_map/ppermute | solution.py:179
  27.3 15.6 %collective-permute-start.6 = (bf16[128,2048]{1,0:T(8,128)(2,1)}, bf16[128,2048]{1,0:T(8,128)(2,1)}, u32[]{:S(2)}, u32[]{:S(2)}) collective-permute-start(bf16[128,2048]{1,0:T(8,128)(2,1)} %collective-permute-done.1.refs_0_), channel_id=1, source_target_pairs={{0,1},{1,0},{2,3},{3,2},{4,5},{5,4},{6,7},{7,6},{8,9},{9,8},{10,11... | collective-permute-start | bytes 1572872 | tf_op jit(solution)/shard_map/ppermute | solution.py:179
  27.5 15.3 %collective-permute-start = (bf16[64,2048]{1,0:T(8,128)(2,1)}, bf16[64,2048]{1,0:T(8,128)(2,1)}, u32[]{:S(2)}, u32[]{:S(2)}) collective-permute-start(bf16[64,2048]{1,0:T(8,128)(2,1)} %get-tuple-element.116), channel_id=1, source_target_pairs={{0,8},{1,9},{2,10},{3,11},{4,12},{5,13},{6,14},{7,15},{8,0},{9,1},... | collective-permute-start | bytes 786440 | tf_op jit(solution)/shard_map/ppermute | solution.py:179
  29.0 1.9 %copy-start.3 = (bf16[1,2048,768]{2,1,0:T(8,128)(2,1)S(1)}, bf16[1,2048,768]{2,1,0:T(8,128)(2,1)}, u32[]{:S(2)}) copy-start(bf16[1,2048,768]{2,1,0:T(8,128)(2,1)} %param.10) | copy-start | bytes 9437188
  30.9 1.9 %copy-start.6 = (bf16[1,768,2048]{2,1,0:T(8,128)(2,1)S(1)}, bf16[1,768,2048]{2,1,0:T(8,128)(2,1)}, u32[]{:S(2)}) copy-start(bf16[1,768,2048]{2,1,0:T(8,128)(2,1)} %param.11) | copy-start | bytes 9437188
  32.8 1.0 copy-start.10
  33.8 1.0 copy-start.14
  41.9 0.8 copy-start.19
  42.6 62.3 %copy-start.8 = (bf16[256,2048]{1,0:T(8,128)(2,1)}, bf16[256,2048]{1,0:T(8,128)(2,1)S(1)}, u32[]{:S(2)}) copy-start(bf16[256,2048]{1,0:T(8,128)(2,1)S(1)} %get-tuple-element.93.keep) | copy-start | bytes 3145732
  42.8 3.1 %collective-permute-start.11 = (bf16[128,2048]{1,0:T(8,128)(2,1)}, bf16[128,2048]{1,0:T(8,128)(2,1)S(1)}, u32[]{:S(2)}, u32[]{:S(2)}) collective-permute-start(bf16[128,2048]{1,0:T(8,128)(2,1)} %collective-permute-done.5.refs_1_), channel_id=1, source_target_pairs={{0,1},{1,0},{2,3},{3,2},{4,5},{5,4},{6,7},{7,6},{8,9},{9,8},{10,11... | collective-permute-start | bytes 1572872 | tf_op jit(solution)/shard_map/ppermute | solution.py:179
  44.0 18.8 %copy-start.4 = (bf16[1,2048,768]{2,1,0:T(8,128)(2,1)S(1)}, bf16[1,2048,768]{2,1,0:T(8,128)(2,1)}, u32[]{:S(2)}) copy-start(bf16[1,2048,768]{2,1,0:T(8,128)(2,1)} %param.10) | copy-start | bytes 9437188
  44.0 8.8 %collective-permute-start.10 = (bf16[128,2048]{1,0:T(8,128)(2,1)S(1)}, bf16[128,2048]{1,0:T(8,128)(2,1)S(1)}, u32[]{:S(2)}, u32[]{:S(2)}) collective-permute-start(bf16[128,2048]{1,0:T(8,128)(2,1)S(1)} %constant_dynamic-update-slice_fusion.refs_0_), channel_id=1, source_target_pairs={{0,1},{1,0},{2,3},{3,2},{4,5},{5,4},{6,7},{7,6},{8,9},{9,8},{10,11... | collective-permute-start | bytes 1572872 | tf_op jit(solution)/shard_map/ppermute | solution.py:179
  44.4 14.0 %collective-permute-start.8 = (bf16[128,2048]{1,0:T(8,128)(2,1)S(1)}, bf16[128,2048]{1,0:T(8,128)(2,1)S(1)}, u32[]{:S(2)}, u32[]{:S(2)}) collective-permute-start(bf16[128,2048]{1,0:T(8,128)(2,1)S(1)} %constant_dynamic-update-slice_fusion.refs_0_), channel_id=1, source_target_pairs={{0,4},{1,5},{2,6},{3,7},{4,0},{5,1},{6,2},{7,3},{8,12},{9,13},{10,... | collective-permute-start | bytes 1572872 | tf_op jit(solution)/shard_map/ppermute | solution.py:179
  44.8 13.8 %collective-permute-start.9 = (bf16[128,2048]{1,0:T(8,128)(2,1)S(1)}, bf16[128,2048]{1,0:T(8,128)(2,1)S(1)}, u32[]{:S(2)}, u32[]{:S(2)}) collective-permute-start(bf16[128,2048]{1,0:T(8,128)(2,1)S(1)} %constant_dynamic-update-slice_fusion.refs_0_), channel_id=1, source_target_pairs={{0,2},{1,3},{2,0},{3,1},{4,6},{5,7},{6,4},{7,5},{8,10},{9,11},{10,... | collective-permute-start | bytes 1572872 | tf_op jit(solution)/shard_map/ppermute | solution.py:179
  52.8 10.0 %copy-start.15 = (bf16[320,768]{1,0:T(8,128)(2,1)}, bf16[320,768]{1,0:T(8,128)(2,1)S(1)}, u32[]{:S(2)}) copy-start(bf16[320,768]{1,0:T(8,128)(2,1)S(1)} %get-tuple-element.75) | copy-start | bytes 1474564
  58.6 2.7 %collective-permute-start.13 = (bf16[256,2048]{1,0:T(8,128)(2,1)S(1)}, bf16[256,2048]{1,0:T(8,128)(2,1)S(1)}, u32[]{:S(2)}, u32[]{:S(2)}) collective-permute-start(bf16[256,2048]{1,0:T(8,128)(2,1)S(1)} %get-tuple-element.78), channel_id=1, source_target_pairs={{0,1},{1,0},{2,3},{3,2},{4,5},{5,4},{6,7},{7,6},{8,9},{9,8},{10,11... | collective-permute-start | bytes 3145736 | tf_op jit(solution)/shard_map/ppermute | solution.py:179
  58.6 4.1 %collective-permute-start.16 = (bf16[128,2048]{1,0:T(8,128)(2,1)S(1)}, bf16[128,2048]{1,0:T(8,128)(2,1)S(1)}, u32[]{:S(2)}, u32[]{:S(2)}) collective-permute-start(bf16[128,2048]{1,0:T(8,128)(2,1)S(1)} %collective-permute-done.9.refs_1_), channel_id=1, source_target_pairs={{0,1},{1,0},{2,3},{3,2},{4,5},{5,4},{6,7},{7,6},{8,9},{9,8},{10,11... | collective-permute-start | bytes 1572872 | tf_op jit(solution)/shard_map/ppermute | solution.py:179
  59.1 13.8 %collective-permute-start.12 = (bf16[128,2048]{1,0:T(8,128)(2,1)S(1)}, bf16[128,2048]{1,0:T(8,128)(2,1)S(1)}, u32[]{:S(2)}, u32[]{:S(2)}) collective-permute-start(bf16[128,2048]{1,0:T(8,128)(2,1)S(1)} %collective-permute-done.9.refs_1_), channel_id=1, source_target_pairs={{0,4},{1,5},{2,6},{3,7},{4,0},{5,1},{6,2},{7,3},{8,12},{9,13},{10,... | collective-permute-start | bytes 1572872 | tf_op jit(solution)/shard_map/ppermute | solution.py:179
  60.6 12.3 %collective-permute-start.15 = (bf16[128,2048]{1,0:T(8,128)(2,1)S(1)}, bf16[128,2048]{1,0:T(8,128)(2,1)S(1)}, u32[]{:S(2)}, u32[]{:S(2)}) collective-permute-start(bf16[128,2048]{1,0:T(8,128)(2,1)S(1)} %collective-permute-done.8.refs_0_), channel_id=1, source_target_pairs={{0,1},{1,0},{2,3},{3,2},{4,5},{5,4},{6,7},{7,6},{8,9},{9,8},{10,11... | collective-permute-start | bytes 1572872 | tf_op jit(solution)/shard_map/ppermute | solution.py:179
  61.4 17.5 %copy-start.7 = (bf16[1,768,2048]{2,1,0:T(8,128)(2,1)S(1)}, bf16[1,768,2048]{2,1,0:T(8,128)(2,1)}, u32[]{:S(2)}) copy-start(bf16[1,768,2048]{2,1,0:T(8,128)(2,1)} %param.11) | copy-start | bytes 9437188
  61.4 14.0 %collective-permute-start.14 = (bf16[128,2048]{1,0:T(8,128)(2,1)S(1)}, bf16[128,2048]{1,0:T(8,128)(2,1)S(1)}, u32[]{:S(2)}, u32[]{:S(2)}) collective-permute-start(bf16[128,2048]{1,0:T(8,128)(2,1)S(1)} %add_convert_fusion.2), channel_id=1, source_target_pairs={{0,2},{1,3},{2,0},{3,1},{4,6},{5,7},{6,4},{7,5},{8,10},{9,11},{10,... | collective-permute-start | bytes 1572872 | tf_op jit(solution)/shard_map/ppermute | solution.py:179
  68.4 0.8 copy-start.17
  75.5 10.5 %collective-permute-start.18 = (bf16[256,2048]{1,0:T(8,128)(2,1)S(1)}, bf16[256,2048]{1,0:T(8,128)(2,1)S(1)}, u32[]{:S(2)}, u32[]{:S(2)}) collective-permute-start(bf16[256,2048]{1,0:T(8,128)(2,1)S(1)} %get-tuple-element.90), channel_id=1, source_target_pairs={{0,1},{1,0},{2,3},{3,2},{4,5},{5,4},{6,7},{7,6},{8,9},{9,8},{10,11... | collective-permute-start | bytes 3145736 | tf_op jit(solution)/shard_map/ppermute | solution.py:179
  75.5 3.4 %collective-permute-start.17 = (bf16[128,2048]{1,0:T(8,128)(2,1)S(1)}, bf16[128,2048]{1,0:T(8,128)(2,1)S(1)}, u32[]{:S(2)}, u32[]{:S(2)}) collective-permute-start(bf16[128,2048]{1,0:T(8,128)(2,1)S(1)} %collective-permute-done.12.refs_1_), channel_id=1, source_target_pairs={{0,1},{1,0},{2,3},{3,2},{4,5},{5,4},{6,7},{7,6},{8,9},{9,8},{10,11... | collective-permute-start | bytes 1572872 | tf_op jit(solution)/shard_map/ppermute | solution.py:179
  76.2 9.7 %collective-permute-start.19 = (bf16[80,2048]{1,0:T(8,128)(2,1)S(1)}, bf16[80,2048]{1,0:T(8,128)(2,1)S(1)}, u32[]{:S(2)}, u32[]{:S(2)}) collective-permute-start(bf16[80,2048]{1,0:T(8,128)(2,1)S(1)} %slice.106), channel_id=1, source_target_pairs={{0,4},{1,5},{2,6},{3,7},{4,0},{5,1},{6,2},{7,3},{8,12},{9,13},{10,... | collective-permute-start | bytes 983048 | tf_op jit(solution)/shard_map/ppermute | solution.py:179
  84.4 21.5 %copy-start.18 = (bf16[320,768]{1,0:T(8,128)(2,1)}, bf16[320,768]{1,0:T(8,128)(2,1)S(1)}, u32[]{:S(2)}) copy-start(bf16[320,768]{1,0:T(8,128)(2,1)S(1)} %get-tuple-element.92) | copy-start | bytes 1474564
  85.9 2.7 %collective-permute-start.20 = (bf16[256,2048]{1,0:T(8,128)(2,1)S(1)}, bf16[256,2048]{1,0:T(8,128)(2,1)S(1)}, u32[]{:S(2)}, u32[]{:S(2)}) collective-permute-start(bf16[256,2048]{1,0:T(8,128)(2,1)S(1)} %get-tuple-element.95), channel_id=1, source_target_pairs={{0,1},{1,0},{2,3},{3,2},{4,5},{5,4},{6,7},{7,6},{8,9},{9,8},{10,11... | collective-permute-start | bytes 3145736 | tf_op jit(solution)/shard_map/ppermute | solution.py:179
  85.9 6.0 %collective-permute-start.24 = (bf16[256,2048]{1,0:T(8,128)(2,1)S(1)}, bf16[256,2048]{1,0:T(8,128)(2,1)S(1)}, u32[]{:S(2)}, u32[]{:S(2)}) collective-permute-start(bf16[256,2048]{1,0:T(8,128)(2,1)S(1)} %get-tuple-element.98), channel_id=1, source_target_pairs={{0,1},{1,0},{2,3},{3,2},{4,5},{5,4},{6,7},{7,6},{8,9},{9,8},{10,11... | collective-permute-start | bytes 3145736 | tf_op jit(solution)/shard_map/ppermute | solution.py:179
  86.5 7.2 %collective-permute-start.23 = (bf16[48,2048]{1,0:T(8,128)(2,1)S(1)}, bf16[48,2048]{1,0:T(8,128)(2,1)S(1)}, u32[]{:S(2)}, u32[]{:S(2)}) collective-permute-start(bf16[48,2048]{1,0:T(8,128)(2,1)S(1)} %add_convert_fusion.10), channel_id=1, source_target_pairs={{0,2},{1,3},{2,0},{3,1},{4,6},{5,7},{6,4},{7,5},{8,10},{9,11},{10,... | collective-permute-start | bytes 589832 | tf_op jit(solution)/shard_map/ppermute | solution.py:179
  88.8 9.8 %collective-permute-start.21 = (bf16[80,2048]{1,0:T(8,128)(2,1)S(1)}, bf16[80,2048]{1,0:T(8,128)(2,1)S(1)}, u32[]{:S(2)}, u32[]{:S(2)}) collective-permute-start(bf16[80,2048]{1,0:T(8,128)(2,1)S(1)} %get-tuple-element.115), channel_id=1, source_target_pairs={{0,4},{1,5},{2,6},{3,7},{4,0},{5,1},{6,2},{7,3},{8,12},{9,13},{10,... | collective-permute-start | bytes 983048 | tf_op jit(solution)/shard_map/ppermute | solution.py:179
  90.4 7.2 %collective-permute-start.22 = (bf16[48,2048]{1,0:T(8,128)(2,1)S(1)}, bf16[48,2048]{1,0:T(8,128)(2,1)S(1)}, u32[]{:S(2)}, u32[]{:S(2)}) collective-permute-start(bf16[48,2048]{1,0:T(8,128)(2,1)S(1)} %add_convert_fusion.11), channel_id=1, source_target_pairs={{0,2},{1,3},{2,0},{3,1},{4,6},{5,7},{6,4},{7,5},{8,10},{9,11},{10,... | collective-permute-start | bytes 589832 | tf_op jit(solution)/shard_map/ppermute | solution.py:179
  98.6 27.0 %copy-start.16 = (bf16[320,768]{1,0:T(8,128)(2,1)S(1)}, bf16[320,768]{1,0:T(8,128)(2,1)}, u32[]{:S(2)}) copy-start(bf16[320,768]{1,0:T(8,128)(2,1)} %copy-done.15) | copy-start | bytes 1474564
  98.8 20.8 %collective-permute-start.28 = (bf16[80,2048]{1,0:T(8,128)(2,1)S(1)}, bf16[80,2048]{1,0:T(8,128)(2,1)S(1)}, u32[]{:S(2)}, u32[]{:S(2)}) collective-permute-start(bf16[80,2048]{1,0:T(8,128)(2,1)S(1)} %add_convert_fusion.4), channel_id=1, source_target_pairs={{0,2},{1,3},{2,0},{3,1},{4,6},{5,7},{6,4},{7,5},{8,10},{9,11},{10,... | collective-permute-start | bytes 983048 | tf_op jit(solution)/shard_map/ppermute | solution.py:179
  100.1 16.5 %collective-permute-start.26 = (bf16[48,2048]{1,0:T(8,128)(2,1)S(1)}, bf16[48,2048]{1,0:T(8,128)(2,1)S(1)}, u32[]{:S(2)}, u32[]{:S(2)}) collective-permute-start(bf16[48,2048]{1,0:T(8,128)(2,1)S(1)} %add_convert_fusion.8), channel_id=1, source_target_pairs={{0,8},{1,9},{2,10},{3,11},{4,12},{5,13},{6,14},{7,15},{8,0},{9,1},... | collective-permute-start | bytes 589832 | tf_op jit(solution)/shard_map/ppermute | solution.py:179
  102.0 17.5 %collective-permute-start.25 = (bf16[48,2048]{1,0:T(8,128)(2,1)S(1)}, bf16[48,2048]{1,0:T(8,128)(2,1)S(1)}, u32[]{:S(2)}, u32[]{:S(2)}) collective-permute-start(bf16[48,2048]{1,0:T(8,128)(2,1)S(1)} %add_convert_fusion.9), channel_id=1, source_target_pairs={{0,8},{1,9},{2,10},{3,11},{4,12},{5,13},{6,14},{7,15},{8,0},{9,1},... | collective-permute-start | bytes 589832 | tf_op jit(solution)/shard_map/ppermute | solution.py:179
  103.3 16.3 %collective-permute-start.27 = (bf16[80,2048]{1,0:T(8,128)(2,1)S(1)}, bf16[80,2048]{1,0:T(8,128)(2,1)S(1)}, u32[]{:S(2)}, u32[]{:S(2)}) collective-permute-start(bf16[80,2048]{1,0:T(8,128)(2,1)S(1)} %get-tuple-element.102), channel_id=1, source_target_pairs={{0,4},{1,5},{2,6},{3,7},{4,0},{5,1},{6,2},{7,3},{8,12},{9,13},{10,... | collective-permute-start | bytes 983048 | tf_op jit(solution)/shard_map/ppermute | solution.py:179
  120.5 18.3 %collective-permute-start.29 = (bf16[128,2048]{1,0:T(8,128)(2,1)}, bf16[128,2048]{1,0:T(8,128)(2,1)S(1)}, u32[]{:S(2)}, u32[]{:S(2)}) collective-permute-start(bf16[128,2048]{1,0:T(8,128)(2,1)} %add_convert_fusion), channel_id=1, source_target_pairs={{0,2},{1,3},{2,0},{3,1},{4,6},{5,7},{6,4},{7,5},{8,10},{9,11},{10,... | collective-permute-start | bytes 1572872 | tf_op jit(solution)/shard_map/ppermute | solution.py:179
  122.5 16.3 %copy-start.9 = (bf16[256,2048]{1,0:T(8,128)(2,1)S(1)}, bf16[256,2048]{1,0:T(8,128)(2,1)}, u32[]{:S(2)}) copy-start(bf16[256,2048]{1,0:T(8,128)(2,1)} %copy-done.8) | copy-start | bytes 3145732
  122.5 16.3 %collective-permute-start.30 = (bf16[80,2048]{1,0:T(8,128)(2,1)S(1)}, bf16[80,2048]{1,0:T(8,128)(2,1)S(1)}, u32[]{:S(2)}, u32[]{:S(2)}) collective-permute-start(bf16[80,2048]{1,0:T(8,128)(2,1)S(1)} %add_convert_fusion.3), channel_id=1, source_target_pairs={{0,8},{1,9},{2,10},{3,11},{4,12},{5,13},{6,14},{7,15},{8,0},{9,1},... | collective-permute-start | bytes 983048 | tf_op jit(solution)/shard_map/ppermute | solution.py:179
  122.7 10.3 %collective-permute-start.31 = (bf16[48,2048]{1,0:T(8,128)(2,1)}, bf16[48,2048]{1,0:T(8,128)(2,1)S(1)}, u32[]{:S(2)}, u32[]{:S(2)}) collective-permute-start(bf16[48,2048]{1,0:T(8,128)(2,1)} %add_convert_fusion.7), channel_id=1, source_target_pairs={{0,4},{1,5},{2,6},{3,7},{4,0},{5,1},{6,2},{7,3},{8,12},{9,13},{10,... | collective-permute-start | bytes 589832 | tf_op jit(solution)/shard_map/ppermute | solution.py:179

commit v14 on v13

--- a/solution.py
+++ b/solution.py
@@ -78,8 +78,9 @@
             tables[pl.ds(blocks // 4 + k, 1), span] = weight[pl.ds(spots[4 * k + i], 1), :]
 
 
-def plane_kernel(k, tables, *refs):
-    *xs, w_gate, w_up, w_down, keep, give, act, rows = refs
+def plane_kernel(k, gives, tables, *refs):
+    *xs, w_gate, w_up, w_down, keep = refs[: -gives - 2]
+    *gives, act, rows = refs[-gives - 2 :]
     slots, hidden = act.shape
     features = rows.shape[1]
     half, width = keep.shape[0], tables.shape[1]
@@ -106,25 +107,31 @@
         made = (result * scale).astype(jnp.bfloat16)
         spread = jnp.dot(back, made, preferred_element_type=jnp.float32).astype(jnp.bfloat16)
         keep[:, span] = spread[:half]
-        give[:, span] = spread[half:]
+        start = half
+        for give in gives:
+            give[:, span] = spread[start : start + give.shape[0]]
+            start += give.shape[0]
 
 
 def first_kernel(capacity, spots, weight, *refs):
     *plane, tables, rows, ranks = refs
     fill_tables(capacity, spots, weight, ranks, tables)
-    plane_kernel(0, tables, *plane, rows)
-
-
-def plane_pass(k, tables, xs, w_gate, w_up, w_down, slots, first=None):
+    plane_kernel(0, 1, tables, *plane, rows)
+
+
+def plane_pass(k, tables, xs, w_gate, w_up, w_down, slots, first=None, pieces=None):
     tok, features = xs[0].shape
     hidden = w_gate.shape[1]
     rows = 4 * slots
-    half = jax.ShapeDtypeStruct((2 * tok, features), jnp.bfloat16)
-    outs = (half, half, jax.ShapeDtypeStruct((rows, hidden), jnp.bfloat16))
+    pieces = pieces or (2 * tok,)
+    outs = tuple(
+        jax.ShapeDtypeStruct((some, features), jnp.bfloat16) for some in (2 * tok, *pieces)
+    )
+    outs += (jax.ShapeDtypeStruct((rows, hidden), jnp.bfloat16),)
     scratch = [pltpu.VMEM((rows, features), jnp.bfloat16)]
     vmem = pl.BlockSpec(memory_space=pltpu.VMEM)
     if first is None:
-        body, inputs, specs = functools.partial(plane_kernel, k), (tables,), [vmem]
+        body, inputs, specs = functools.partial(plane_kernel, k, len(pieces)), (tables,), [vmem]
     else:
         capacity, spots, weight = first
         body = functools.partial(first_kernel, capacity)
@@ -146,12 +153,36 @@
     )(*inputs, *xs, w_gate, w_up, w_down)
 
 
-def mix_kernel(keep, got, side, near_low, far_low, near_high, far_high, mixed):
-    most, tok = near_low.shape[0], mixed.shape[0]
-    for start, stop, near, far in ((0, most, near_low, far_low), (most, tok, near_high, far_high)):
+def high_kernel(keep3, got3, high3, keep2, got2, high2, both):
+    tok, least = keep3.shape[0] // 2, high3.shape[0]
+    for i, parts in enumerate(((keep3, got3, high3), (keep2, got2, high2))):
+        keep, got = (part[tok - least : tok, :].astype(jnp.float32) for part in parts[:2])
+        total = keep + got + parts[2][...].astype(jnp.float32)
+        both[i * least : (i + 1) * least, :] = total.astype(both.dtype)
+
+
+def high_pass(*parts):
+    least, features = parts[2].shape
+    vmem = pl.BlockSpec(memory_space=pltpu.VMEM)
+    return pl.pallas_call(
+        high_kernel,
+        out_shape=jax.ShapeDtypeStruct((2 * least, features), parts[2].dtype),
+        in_specs=[vmem] * len(parts),
+        out_specs=vmem,
+        compiler_params=pltpu.CompilerParams(vmem_limit_bytes=12 * 1024 * 1024),
+    )(*parts)
+
+
+def mix_kernel(keep, got, side, near_low, near_mid, near_high, far_low, far_high, mixed):
+    least, most, tok = near_low.shape[0], far_low.shape[0], mixed.shape[0]
+    for start, stop, near, far in (
+        (0, least, near_low, far_low[:least, :]),
+        (least, most, near_mid, far_low[least:, :]),
+        (most, tok, near_high, far_high[tok - most :, :]),
+    ):
         total = keep[start:stop, :].astype(jnp.float32) + got[start:stop, :].astype(jnp.float32)
         total = total + side[start:stop, :].astype(jnp.float32) + near[...].astype(jnp.float32)
-        mixed[start:stop, :] = (total + far[...].astype(jnp.float32)).astype(mixed.dtype)
+        mixed[start:stop, :] = (total + far.astype(jnp.float32)).astype(mixed.dtype)
 
 
 def mix_pass(*parts):
@@ -195,8 +226,8 @@
         ]
     ).astype(jnp.int32)
 
-    def expert(k, tables, *xs, first=None):
-        return plane_pass(k, tables, xs, w_gate, w_up, w_down, slots, first)
+    def expert(k, tables, *xs, first=None, pieces=None):
+        return plane_pass(k, tables, xs, w_gate, w_up, w_down, slots, first, pieces)
 
     weight = table_pass(routes, probs, size, w_gate, w_up, w_down)
     a0 = tokens
@@ -218,20 +249,24 @@
     b2 = column(a2)
     d1 = sibling(b1)
     c2 = sibling(a2)
-    keep1, give1, act1 = expert(1, tables, a1, b1, c1, d1)
-    a3, b2, c2, keep1, give1, act1 = together(a3, b2, c2, keep1, give1, act1)
+    keep1, give1, *give1_side, act1 = expert(1, tables, a1, b1, c1, d1, pieces=(tok, tok))
+    got1_side = [sibling(piece) for piece in give1_side]
+    a3, b2, c2, keep1, give1, act1, *got1_side = together(
+        a3, b2, c2, keep1, give1, act1, *got1_side
+    )
     b3 = pair(b2)
+    came1 = column(summed(keep1[tok:], jnp.concatenate(got1_side, axis=0)))
     got1 = sibling(give1)
-    came1 = column(summed(keep1[tok:], got1[tok:]))
     d2 = sibling(b2)
     c3 = sibling(a3)
     keep2, give2, act2 = expert(2, tables, a2, b2, c2, d2)
-    b3, came1, c3, keep2, give2, act2 = together(b3, came1, c3, keep2, give2, act2)
-    near1 = summed(keep1[:tok], got1[:tok], came1)
+    b3, came1, c3, got1, keep2, give2, act2 = together(b3, came1, c3, got1, keep2, give2, act2)
+    d3 = sibling(b3)
+    near1 = summed(keep1[:tok], got1, came1)
     most = 5 * tok // 8
-    d3 = sibling(b3)
+    least = tok - most
     got2 = sibling(give2)
-    near1_low = pair(near1[:most])
+    near1_low = pair(near1[:least])
     keep3, give3, act3 = expert(3, tables, a3, b3, c3, d3)
     keep3, give3, act3, got2, near1, near1_low = together(
         keep3, give3, act3, got2, near1, near1_low
@@ -245,27 +280,28 @@
     low = pair(own(keep3, got3, tok, tok + most))
     high = column(own(keep3, got3, tok + most, 2 * tok))
     side_high = column(own(keep2, got2, tok + most, 2 * tok))
+    near1_mid = pair(near1[least:most])
     sum3 = own(keep3, got3, 0, most)
-    low, high, side_high, got0, sum3 = together(low, high, side_high, got0, sum3)
-    far3_high = far(own(keep3, got3, most, tok, high))
-    far2_high = far(own(keep2, got2, most, tok, side_high))
+    side0 = own(keep0, got0, tok, 2 * tok)
+    low, high, side_high, near1_mid, sum3, side0 = together(
+        low, high, side_high, near1_mid, sum3, side0
+    )
+    far_high = far(high_pass(keep3, got3, high, keep2, got2, side_high))
     pair3_low = pair(sum3)
     side_low = column(own(keep2, got2, tok, tok + most, low))
-    side0 = own(keep0, got0, tok, 2 * tok)
-    far3_high, far2_high, pair3_low, side_low, side0 = together(
-        far3_high, far2_high, pair3_low, side_low, side0
-    )
-    sum2 = own(keep2, got2, 0, most, pair3_low, side_low)
-    sum1 = summed(near1[most:], far3_high)
-    sum2, sum1, side0 = together(sum2, sum1, side0)
-    far2_low = far(sum2)
-    near1_high = pair(sum1)
     last0 = column(side0)
-    mixed = mix_pass(keep0, got0, last0, near1_low, far2_low, near1_high, far2_high)
-
     acts = jnp.concatenate([act0, act1, act2, act3], axis=0)
     count = jnp.minimum(jnp.sum((weight >= 0.0).astype(jnp.float32)), float(capacity))
     gram = gram_of(acts) * (2.0 / count)
+    far_high, pair3_low, side_low, last0, gram = together(
+        far_high, pair3_low, side_low, last0, gram
+    )
+    far2_low = far(own(keep2, got2, 0, most, pair3_low, side_low))
+    near1_high = pair(summed(near1[most:], far_high[:least]))
+    mixed = mix_pass(
+        keep0, got0, last0, near1_low, near1_mid, near1_high, far2_low, far_high
+    )
+
     return gram[None], mixed
 
 

time: 141 us -> 142 us (level)
  starting transfers between devices: 30.8 us -> 27.9 us
  Pallas kernels: 26.2 us -> 28.8 us
  local copies, waits for them, and re-layouts: 18.2 us -> 20.2 us
  matrix products: 4.98 us -> 3.16 us
    ppermute x32 -> x33, starting transfers between devices: 30.8 us -> 27.9 us  [swapped(): return lax.ppermute(array, 'expert', [(i, i ^ bit) for i in range(size)])]
    dot_general x1, matrix products: 4.98 us -> 3.16 us  [gram_of(): lax.dot_general(rows, rows, (((0,), (0,)), ((), ())), preferred_element_t...]
    pallas_call x0 -> x1, Pallas kernels: none -> 1.51 us  [high_pass(): pl.pallas_call(high_kernel, out_shape=jax.ShapeDtypeStruct((2 * least, fe...]
    convert_element_type x11 -> x9, other arithmetic: 2.76 us -> 4.04 us  [summed(): return total.astype(jnp.bfloat16)]
    unnamed x41 -> x57, local copies, waits for them, and re-layouts: 15.3 us -> 16.3 us
    ppermute x32 -> x33, waiting for transfers between devices: 45.7 us -> 45.6 us  [swapped(): return lax.ppermute(array, 'expert', [(i, i ^ bit) for i in range(size)])]
  transfers between devices with their start and end apart: 32 -> 33, of which waited for: 17 -> 11; matrix products, arithmetic and copies ran while one was open for 7% -> 8% of each run, Pallas kernels for 18% -> 19%
where the time goes in v14:
time: 142 us; the launch traced here: 141 us
  waiting for transfers between devices  45.6 us (32%)
  Pallas kernels  28.8 us (20%)
  starting transfers between devices  27.9 us (20%)
  local copies, waits for them, and re-layouts  20.2 us (14%)
  blocking collectives  9.24 us (7%)
  other arithmetic  4.64 us (3%)
  matrix products  3.16 us (2%)
  between operations  1.53 us (1%)
    ppermute x33, waiting for transfers between devices, swapped(): return lax.ppermute(array, 'expert', [(i, i ^ bit) for i in range(size)])  45.6 us
    ppermute x33, starting transfers between devices, swapped(): return lax.ppermute(array, 'expert', [(i, i ^ bit) for i in range(size)])  27.9 us
    pallas_call x4, Pallas kernels, plane_pass(): pl.pallas_call(body, out_shape=outs, in_specs=specs + [vmem] * (len(xs) +...  26.2 us
    unnamed x57, local copies, waits for them, and re-layouts  16.3 us
    all_to_all x1, blocking collectives, table_pass(): lax.all_to_all(mine, 'expert', split_axis=0, concat_axis=0, tiled=True)  9.24 us
    convert_element_type x9, other arithmetic, summed(): return total.astype(jnp.bfloat16)  4.04 us
    dot_general x1, matrix products, gram_of(): lax.dot_general(rows, rows, (((0,), (0,)), ((), ())), preferred_element_t...  3.16 us
  transfers between devices with their start and end apart: 33, of which 11 were waited for; matrix products, arithmetic and copies ran while one was open for 8% of the time, Pallas kernels for 19%

profile of v14, /device:TPU:0, one launch (start us, length us, event | category | flops | bytes accessed | tf_op | source)
XLA Modules:
  0.0 141.2 jit_solution(6708804411546904552)
XLA Ops:
  0.6 3.1 %collective-permute-start.1 = (bf16[128,2048]{1,0:T(8,128)(2,1)}, bf16[128,2048]{1,0:T(8,128)(2,1)}, u32[]{:S(2)}, u32[]{:S(2)}) collective-permute-start(bf16[128,2048]{1,0:T(8,128)(2,1)} %refs_0_.1), channel_id=1, source_target_pairs={{0,4},{1,5},{2,6},{3,7},{4,0},{5,1},{6,2},{7,3},{8,12},{9,13},{10,... | collective-permute-start | bytes 1572872 | tf_op jit(solution)/shard_map/ppermute | solution.py:210
  3.7 1.5 %collective-permute-start.3 = (bf16[128,2048]{1,0:T(8,128)(2,1)}, bf16[128,2048]{1,0:T(8,128)(2,1)}, u32[]{:S(2)}, u32[]{:S(2)}) collective-permute-start(bf16[128,2048]{1,0:T(8,128)(2,1)} %refs_0_.1), channel_id=1, source_target_pairs={{0,2},{1,3},{2,0},{3,1},{4,6},{5,7},{6,4},{7,5},{8,10},{9,11},{10,... | collective-permute-start | bytes 1572872 | tf_op jit(solution)/shard_map/ppermute | solution.py:210
  5.2 1.8 %fusion.11 = (bf16[64,2048]{1,0:T(8,128)(2,1)S(1)}, bf16[64,2048]{1,0:T(8,128)(2,1)}) fusion(bf16[128,2048]{1,0:T(8,128)(2,1)} %refs_0_.1), kind=kLoop, calls=%fused_computation.23 | loop fusion | bytes 1048576 | tf_op jit(solution)/shard_map/slice | solution.py:235
  7.0 2.6 %collective-permute-start.2 = (bf16[64,2048]{1,0:T(8,128)(2,1)S(1)}, bf16[64,2048]{1,0:T(8,128)(2,1)S(1)}, u32[]{:S(2)}, u32[]{:S(2)}) collective-permute-start(bf16[64,2048]{1,0:T(8,128)(2,1)S(1)} %get-tuple-element.118), channel_id=1, source_target_pairs={{0,8},{1,9},{2,10},{3,11},{4,12},{5,13},{6,14},{7,15},{8,0},{9,1},... | collective-permute-start | bytes 786440 | tf_op jit(solution)/shard_map/ppermute | solution.py:210
  9.6 1.9 %copy-done = bf16[1,2048,768]{2,1,0:T(8,128)(2,1)S(1)} copy-done((bf16[1,2048,768]{2,1,0:T(8,128)(2,1)S(1)}, bf16[1,2048,768]{2,1,0:T(8,128)(2,1)}, u32[]{:S(2)}) %copy-start) | copy-done | bytes 3145752
  11.5 1.9 %copy-done.3 = bf16[1,2048,768]{2,1,0:T(8,128)(2,1)S(1)} copy-done((bf16[1,2048,768]{2,1,0:T(8,128)(2,1)S(1)}, bf16[1,2048,768]{2,1,0:T(8,128)(2,1)}, u32[]{:S(2)}) %copy-start.3) | copy-done | bytes 3145752
  13.4 1.9 %copy-done.6 = bf16[1,768,2048]{2,1,0:T(8,128)(2,1)S(1)} copy-done((bf16[1,768,2048]{2,1,0:T(8,128)(2,1)S(1)}, bf16[1,768,2048]{2,1,0:T(8,128)(2,1)}, u32[]{:S(2)}) %copy-start.6) | copy-done | bytes 3145752
  15.3 0.7 copy-done.12
  16.0 0.7 copy-done.13
  16.7 9.2 %all_to_all.12 = f32[16,1,128]{2,1,0:T(1,128)S(1)} all-to-all(f32[16,1,128]{2,1,0:T(1,128)S(1)} %bitcast.41), channel_id=1, replica_groups=mesh['parts'=2,'expert'=16] {'expert'}, dimensions={0} | all-to-all | bytes 16384 | tf_op jit(solution)/shard_map/all_to_all | solution.py:48
  26.0 0.7 copy-done.26
  26.7 0.8 copy-done.15
  27.4 0.5 collective-permute-start.5
  28.0 0.2 collective-permute-start.6
  28.2 0.6 collective-permute-start
  28.9 0.8 collective-permute-done.7.refs_3_
  29.7 1.9 %copy-done.4 = bf16[1,2048,768]{2,1,0:T(8,128)(2,1)S(1)} copy-done((bf16[1,2048,768]{2,1,0:T(8,128)(2,1)S(1)}, bf16[1,2048,768]{2,1,0:T(8,128)(2,1)}, u32[]{:S(2)}) %copy-start.4) | copy-done | bytes 3145752
  31.6 1.9 %copy-done.7 = bf16[1,768,2048]{2,1,0:T(8,128)(2,1)S(1)} copy-done((bf16[1,768,2048]{2,1,0:T(8,128)(2,1)S(1)}, bf16[1,768,2048]{2,1,0:T(8,128)(2,1)}, u32[]{:S(2)}) %copy-start.7) | copy-done | bytes 3145752
  33.5 1.0 copy-done.11
  34.5 1.0 copy-done.16
  35.6 7.0 %shard_map.78 = (bf16[256,2048]{1,0:T(8,128)(2,1)S(1)}, bf16[256,2048]{1,0:T(8,128)(2,1)S(1)}, bf16[320,768]{1,0:T(8,128)(2,1)S(1)}, f32[8,512]{1,0:T(8,128)S(1)}) custom-call(s32[16]{0:T(128)S(1)} %stack.67.spots, f32[16,128]{1,0:T(8,128)S(1)} %bitcast.42, bf16[128,2048]{1,0:T(8,128)(2,1)S(1)} %copy-done.11, ...), custom_call_target="tpu_custom_call" | custom-call | flops 4362076160 | bytes 13631488 | tf_op jit(solution)/shard_map/pallas_call | solution.py:143
  42.5 1.0 copy-done.9
  43.8 1.2 constant_dynamic-update-slice_fusion.refs_0_
  45.0 0.3 collective-permute-start.10
  45.3 0.5 collective-permute-start.8
  45.8 0.8 collective-permute-start.9
  46.6 7.1 %shard_map.79 = (bf16[256,2048]{1,0:T(8,128)(2,1)S(1)}, bf16[128,2048]{1,0:T(8,128)(2,1)S(1)}, bf16[128,2048]{1,0:T(8,128)(2,1)S(1)}, bf16[320,768]{1,0:T(8,128)(2,1)S(1)}) custom-call(f32[8,512]{1,0:T(8,128)S(1)} %get-tuple-element.67.tables, bf16[128,2048]{1,0:T(8,128)(2,1)} %collective-permute-done.1.refs_0_, ...), custom_call_target="tpu_custom_call" | custom-call | flops 4362076160 | bytes 13631488 | tf_op jit(solution)/shard_map/pallas_call | solution.py:143
  53.7 0.2 collective-permute-start.12
  54.0 5.5 %collective-permute-done.8.refs_0_ = bf16[128,2048]{1,0:T(8,128)(2,1)S(1)} collective-permute-done((bf16[128,2048]{1,0:T(8,128)(2,1)S(1)}, bf16[128,2048]{1,0:T(8,128)(2,1)S(1)}, u32[]{:S(2)}, u32[]{:S(2)}) %collective-permute-start.8) | collective-permute-done | bytes 524320 | tf_op jit(solution)/shard_map/ppermute | solution.py:210
  59.7 1.5 %collective-permute-start.13 = (bf16[128,2048]{1,0:T(8,128)(2,1)S(1)}, bf16[128,2048]{1,0:T(8,128)(2,1)S(1)}, u32[]{:S(2)}, u32[]{:S(2)}) collective-permute-start(bf16[128,2048]{1,0:T(8,128)(2,1)S(1)} %collective-permute-done.9.refs_1_), channel_id=1, source_target_pairs={{0,4},{1,5},{2,6},{3,7},{4,0},{5,1},{6,2},{7,3},{8,12},{9,13},{10,... | collective-permute-start | bytes 1572872 | tf_op jit(solution)/shard_map/ppermute | solution.py:210
  61.3 1.1 collective-permute-start.14
  62.5 0.5 collective-permute-start.16
  63.0 5.6 %shard_map.80 = (bf16[256,2048]{1,0:T(8,128)(2,1)S(1)}, bf16[256,2048]{1,0:T(8,128)(2,1)S(1)}, bf16[320,768]{1,0:T(8,128)(2,1)S(1)}) custom-call(f32[8,512]{1,0:T(8,128)S(1)} %get-tuple-element.67.tables, bf16[128,2048]{1,0:T(8,128)(2,1)S(1)} %constant_dynamic-update-slice_fusion.refs_0_, bf16[128,2048]{1,0:T(8,128)(2,1)S(1)} %collective-permute-done.9.refs_1_, ...), custom_call_target="tpu_custom_call" | custom-call | flops 4362076160 | bytes 13631488 | tf_op jit(solution)/shard_map/pallas_call | solution.py:143
  68.6 6.8 %collective-permute-done.14 = bf16[128,2048]{1,0:T(8,128)(2,1)S(1)} collective-permute-done((bf16[128,2048]{1,0:T(8,128)(2,1)S(1)}, bf16[128,2048]{1,0:T(8,128)(2,1)S(1)}, u32[]{:S(2)}, u32[]{:S(2)}) %collective-permute-start.14) | collective-permute-done | bytes 524320 | tf_op jit(solution)/shard_map/ppermute | solution.py:210
  75.6 0.5 collective-permute-start.18
  76.0 0.2 add_convert_fusion.1
  76.3 0.6 collective-permute-start.20
  76.9 2.0 %collective-permute-done.18.refs_3_ = bf16[128,2048]{1,0:T(8,128)(2,1)S(1)} collective-permute-done((bf16[128,2048]{1,0:T(8,128)(2,1)S(1)}, bf16[128,2048]{1,0:T(8,128)(2,1)S(1)}, u32[]{:S(2)}, u32[]{:S(2)}) %collective-permute-start.18) | collective-permute-done | bytes 524320 | tf_op jit(solution)/shard_map/ppermute | solution.py:210
  79.0 6.4 %shard_map.81 = (bf16[256,2048]{1,0:T(8,128)(2,1)S(1)}, bf16[256,2048]{1,0:T(8,128)(2,1)}, bf16[320,768]{1,0:T(8,128)(2,1)S(1)}) custom-call(f32[8,512]{1,0:T(8,128)S(1)} %get-tuple-element.67.tables, bf16[128,2048]{1,0:T(8,128)(2,1)S(1)} %collective-permute-done.8.refs_0_, bf16[128,2048]{1,0:T(8,128)(2,1)S(1)} %collective-permute-done.13.refs_1_, ...), custom_call_target="tpu_custom_call" | custom-call | flops 4362076160 | bytes 13631488 | tf_op jit(solution)/shard_map/pallas_call | solution.py:143
  85.4 0.8 copy-done.21
  86.4 0.6 convert_reduce_fusion
  87.6 0.4 collective-permute-start.26
  88.1 1.1 collective-permute-start.24
  89.2 0.9 slice.77
  90.1 0.4 collective-permute-start.25
  90.6 1.0 add_convert_fusion.9
  91.5 1.2 collective-permute-start.23
  92.7 1.3 add_convert_fusion.5
  94.0 1.6 %collective-permute-start.22 = (bf16[80,2048]{1,0:T(8,128)(2,1)S(1)}, bf16[80,2048]{1,0:T(8,128)(2,1)S(1)}, u32[]{:S(2)}, u32[]{:S(2)}) collective-permute-start(bf16[80,2048]{1,0:T(8,128)(2,1)S(1)} %get-tuple-element.117), channel_id=1, source_target_pairs={{0,4},{1,5},{2,6},{3,7},{4,0},{5,1},{6,2},{7,3},{8,12},{9,13},{10,... | collective-permute-start | bytes 983048 | tf_op jit(solution)/shard_map/ppermute | solution.py:210
  95.9 3.4 %collective-permute-done.23.high3 = bf16[48,2048]{1,0:T(8,128)(2,1)S(1)} collective-permute-done((bf16[48,2048]{1,0:T(8,128)(2,1)S(1)}, bf16[48,2048]{1,0:T(8,128)(2,1)S(1)}, u32[]{:S(2)}, u32[]{:S(2)}) %collective-permute-start.23) | collective-permute-done | bytes 196640 | tf_op jit(solution)/shard_map/ppermute | solution.py:210
  99.3 3.7 %collective-permute-done.22 = bf16[80,2048]{1,0:T(8,128)(2,1)S(1)} collective-permute-done((bf16[80,2048]{1,0:T(8,128)(2,1)S(1)}, bf16[80,2048]{1,0:T(8,128)(2,1)S(1)}, u32[]{:S(2)}, u32[]{:S(2)}) %collective-permute-start.22) | collective-permute-done | bytes 327712 | tf_op jit(solution)/shard_map/ppermute | solution.py:210
  103.0 1.5 %shard_map.82 = bf16[96,2048]{1,0:T(8,128)(2,1)S(1)} custom-call(bf16[256,2048]{1,0:T(8,128)(2,1)S(1)} %get-tuple-element.93.keep3, bf16[256,2048]{1,0:T(8,128)(2,1)} %collective-permute-done.21.got3, bf16[48,2048]{1,0:T(8,128)(2,1)S(1)} %collective-permute-done.23.high3, bf16[256,2048]{1,0:T(8,128)(2,1)S(1)} %get-tuple-element.95.keep2, ...), custom_call_target="tpu_custom_call" | custom-call | tf_op jit(solution)/shard_map/pallas_call | solution.py:167
  104.5 1.5 %collective-permute-start.27 = (bf16[96,2048]{1,0:T(8,128)(2,1)S(1)}, bf16[96,2048]{1,0:T(8,128)(2,1)S(1)}, u32[]{:S(2)}, u32[]{:S(2)}) collective-permute-start(bf16[96,2048]{1,0:T(8,128)(2,1)S(1)} %shard_map.82), channel_id=1, source_target_pairs={{0,8},{1,9},{2,10},{3,11},{4,12},{5,13},{6,14},{7,15},{8,0},{9,1},... | collective-permute-start | bytes 1179656 | tf_op jit(solution)/shard_map/ppermute | solution.py:210
  106.0 1.5 %collective-permute-start.30 = (bf16[128,2048]{1,0:T(8,128)(2,1)S(1)}, bf16[128,2048]{1,0:T(8,128)(2,1)S(1)}, u32[]{:S(2)}, u32[]{:S(2)}) collective-permute-start(bf16[128,2048]{1,0:T(8,128)(2,1)S(1)} %add_convert_fusion), channel_id=1, source_target_pairs={{0,2},{1,3},{2,0},{3,1},{4,6},{5,7},{6,4},{7,5},{8,10},{9,11},{10,... | collective-permute-start | bytes 1572872 | tf_op jit(solution)/shard_map/ppermute | solution.py:210
  107.6 0.6 collective-permute-start.29
  108.3 1.5 %collective-permute-start.28 = (bf16[80,2048]{1,0:T(8,128)(2,1)S(1)}, bf16[80,2048]{1,0:T(8,128)(2,1)S(1)}, u32[]{:S(2)}, u32[]{:S(2)}) collective-permute-start(bf16[80,2048]{1,0:T(8,128)(2,1)S(1)} %get-tuple-element.102), channel_id=1, source_target_pairs={{0,4},{1,5},{2,6},{3,7},{4,0},{5,1},{6,2},{7,3},{8,12},{9,13},{10,... | collective-permute-start | bytes 983048 | tf_op jit(solution)/shard_map/ppermute | solution.py:210
  109.7 3.2 %broadcast_multiply_fusion = f32[768,768]{1,0:T(8,128)} fusion(f32[]{:T(128)S(6)} %div.24, bf16[320,768]{1,0:T(8,128)(2,1)S(1)} %copy-done.22, bf16[320,768]{1,0:T(8,128)(2,1)S(1)} %copy-done.20, bf16[320,768]{1,0:T(8,128)(2,1)S(1)} %copy-done.18, bf16[320,768]{1,0:T(8,128)(2,1)S(1)} %copy-done.24), kind=kOutput, calls=%fused_computation.8 | convolution fusion | flops 1518403584 | bytes 4325380 | tf_op jit(solution)/shard_map/dot_general | solution.py:12
  112.9 12.1 %collective-permute-done.29 = bf16[80,2048]{1,0:T(8,128)(2,1)S(1)} collective-permute-done((bf16[80,2048]{1,0:T(8,128)(2,1)S(1)}, bf16[80,2048]{1,0:T(8,128)(2,1)S(1)}, u32[]{:S(2)}, u32[]{:S(2)}) %collective-permute-start.29) | collective-permute-done | bytes 327712 | tf_op jit(solution)/shard_map/ppermute | solution.py:210
  125.2 1.5 %collective-permute-start.32 = (bf16[80,2048]{1,0:T(8,128)(2,1)S(1)}, bf16[80,2048]{1,0:T(8,128)(2,1)S(1)}, u32[]{:S(2)}, u32[]{:S(2)}) collective-permute-start(bf16[80,2048]{1,0:T(8,128)(2,1)S(1)} %add_convert_fusion.3), channel_id=1, source_target_pairs={{0,8},{1,9},{2,10},{3,11},{4,12},{5,13},{6,14},{7,15},{8,0},{9,1},... | collective-permute-start | bytes 983048 | tf_op jit(solution)/shard_map/ppermute | solution.py:210
  126.7 1.0 add_convert_fusion.7
  127.7 1.6 %collective-permute-start.31 = (bf16[48,2048]{1,0:T(8,128)(2,1)S(1)}, bf16[48,2048]{1,0:T(8,128)(2,1)S(1)}, u32[]{:S(2)}, u32[]{:S(2)}) collective-permute-start(bf16[48,2048]{1,0:T(8,128)(2,1)S(1)} %add_convert_fusion.7), channel_id=1, source_target_pairs={{0,4},{1,5},{2,6},{3,7},{4,0},{5,1},{6,2},{7,3},{8,12},{9,13},{10,... | collective-permute-start | bytes 589832 | tf_op jit(solution)/shard_map/ppermute | solution.py:210
  129.2 6.0 %collective-permute-done.31.near_high = bf16[48,2048]{1,0:T(8,128)(2,1)S(1)} collective-permute-done((bf16[48,2048]{1,0:T(8,128)(2,1)S(1)}, bf16[48,2048]{1,0:T(8,128)(2,1)S(1)}, u32[]{:S(2)}, u32[]{:S(2)}) %collective-permute-start.31) | collective-permute-done | bytes 196640 | tf_op jit(solution)/shard_map/ppermute | solution.py:210
  135.3 4.8 %collective-permute-done.32.far_low = bf16[80,2048]{1,0:T(8,128)(2,1)S(1)} collective-permute-done((bf16[80,2048]{1,0:T(8,128)(2,1)S(1)}, bf16[80,2048]{1,0:T(8,128)(2,1)S(1)}, u32[]{:S(2)}, u32[]{:S(2)}) %collective-permute-start.32) | collective-permute-done | bytes 327712 | tf_op jit(solution)/shard_map/ppermute | solution.py:210
  140.1 1.1 shard_map.83
  (83 shorter events, 1.8 us)
Async XLA Ops:
  0.6 25.3 %collective-permute-start.1 = (bf16[128,2048]{1,0:T(8,128)(2,1)}, bf16[128,2048]{1,0:T(8,128)(2,1)}, u32[]{:S(2)}, u32[]{:S(2)}) collective-permute-start(bf16[128,2048]{1,0:T(8,128)(2,1)} %refs_0_.1), channel_id=1, source_target_pairs={{0,4},{1,5},{2,6},{3,7},{4,0},{5,1},{6,2},{7,3},{8,12},{9,13},{10,... | collective-permute-start | bytes 1572872 | tf_op jit(solution)/shard_map/ppermute | solution.py:210
  3.7 22.2 %collective-permute-start.3 = (bf16[128,2048]{1,0:T(8,128)(2,1)}, bf16[128,2048]{1,0:T(8,128)(2,1)}, u32[]{:S(2)}, u32[]{:S(2)}) collective-permute-start(bf16[128,2048]{1,0:T(8,128)(2,1)} %refs_0_.1), channel_id=1, source_target_pairs={{0,2},{1,3},{2,0},{3,1},{4,6},{5,7},{6,4},{7,5},{8,10},{9,11},{10,... | collective-permute-start | bytes 1572872 | tf_op jit(solution)/shard_map/ppermute | solution.py:210
  5.2 20.7 %collective-permute-start.4 = (bf16[128,2048]{1,0:T(8,128)(2,1)}, bf16[128,2048]{1,0:T(8,128)(2,1)S(1)}, u32[]{:S(2)}, u32[]{:S(2)}) collective-permute-start(bf16[128,2048]{1,0:T(8,128)(2,1)} %refs_0_.1), channel_id=1, source_target_pairs={{0,1},{1,0},{2,3},{3,2},{4,5},{5,4},{6,7},{7,6},{8,9},{9,8},{10,11... | collective-permute-start | bytes 1572872 | tf_op jit(solution)/shard_map/ppermute | solution.py:210
  7.0 18.9 %collective-permute-start.2 = (bf16[64,2048]{1,0:T(8,128)(2,1)S(1)}, bf16[64,2048]{1,0:T(8,128)(2,1)S(1)}, u32[]{:S(2)}, u32[]{:S(2)}) collective-permute-start(bf16[64,2048]{1,0:T(8,128)(2,1)S(1)} %get-tuple-element.118), channel_id=1, source_target_pairs={{0,8},{1,9},{2,10},{3,11},{4,12},{5,13},{6,14},{7,15},{8,0},{9,1},... | collective-permute-start | bytes 786440 | tf_op jit(solution)/shard_map/ppermute | solution.py:210
  9.6 1.9 %copy-start = (bf16[1,2048,768]{2,1,0:T(8,128)(2,1)S(1)}, bf16[1,2048,768]{2,1,0:T(8,128)(2,1)}, u32[]{:S(2)}) copy-start(bf16[1,2048,768]{2,1,0:T(8,128)(2,1)} %param.9) | copy-start | bytes 9437188
  11.5 1.9 %copy-start.3 = (bf16[1,2048,768]{2,1,0:T(8,128)(2,1)S(1)}, bf16[1,2048,768]{2,1,0:T(8,128)(2,1)}, u32[]{:S(2)}) copy-start(bf16[1,2048,768]{2,1,0:T(8,128)(2,1)} %param.10) | copy-start | bytes 9437188
  13.4 1.9 %copy-start.6 = (bf16[1,768,2048]{2,1,0:T(8,128)(2,1)S(1)}, bf16[1,768,2048]{2,1,0:T(8,128)(2,1)}, u32[]{:S(2)}) copy-start(bf16[1,768,2048]{2,1,0:T(8,128)(2,1)} %param.11) | copy-start | bytes 9437188
  15.3 0.7 copy-start.12
  16.0 0.7 copy-start.13
  16.6 13.1 %copy-start.1 = (bf16[1,2048,768]{2,1,0:T(8,128)(2,1)S(1)}, bf16[1,2048,768]{2,1,0:T(8,128)(2,1)}, u32[]{:S(2)}) copy-start(bf16[1,2048,768]{2,1,0:T(8,128)(2,1)} %param.9) | copy-start | bytes 9437188
  25.9 0.7 copy-start.26
  26.7 0.8 copy-start.15
  27.4 2.3 %collective-permute-start.7 = (bf16[128,2048]{1,0:T(8,128)(2,1)}, bf16[128,2048]{1,0:T(8,128)(2,1)}, u32[]{:S(2)}, u32[]{:S(2)}) collective-permute-start(bf16[128,2048]{1,0:T(8,128)(2,1)} %collective-permute-done.3.refs_1_), channel_id=1, source_target_pairs={{0,1},{1,0},{2,3},{3,2},{4,5},{5,4},{6,7},{7,6},{8,9},{9,8},{10,11... | collective-permute-start | bytes 1572872 | tf_op jit(solution)/shard_map/ppermute | solution.py:210
  27.4 16.1 %collective-permute-start.5 = (bf16[128,2048]{1,0:T(8,128)(2,1)}, bf16[128,2048]{1,0:T(8,128)(2,1)}, u32[]{:S(2)}, u32[]{:S(2)}) collective-permute-start(bf16[128,2048]{1,0:T(8,128)(2,1)} %collective-permute-done.1.refs_0_), channel_id=1, source_target_pairs={{0,2},{1,3},{2,0},{3,1},{4,6},{5,7},{6,4},{7,5},{8,10},{9,11},{10,... | collective-permute-start | bytes 1572872 | tf_op jit(solution)/shard_map/ppermute | solution.py:210
  28.0 15.6 %collective-permute-start.6 = (bf16[128,2048]{1,0:T(8,128)(2,1)}, bf16[128,2048]{1,0:T(8,128)(2,1)}, u32[]{:S(2)}, u32[]{:S(2)}) collective-permute-start(bf16[128,2048]{1,0:T(8,128)(2,1)} %collective-permute-done.1.refs_0_), channel_id=1, source_target_pairs={{0,1},{1,0},{2,3},{3,2},{4,5},{5,4},{6,7},{7,6},{8,9},{9,8},{10,11... | collective-permute-start | bytes 1572872 | tf_op jit(solution)/shard_map/ppermute | solution.py:210
  28.2 15.4 %collective-permute-start = (bf16[64,2048]{1,0:T(8,128)(2,1)}, bf16[64,2048]{1,0:T(8,128)(2,1)}, u32[]{:S(2)}, u32[]{:S(2)}) collective-permute-start(bf16[64,2048]{1,0:T(8,128)(2,1)} %get-tuple-element.119), channel_id=1, source_target_pairs={{0,8},{1,9},{2,10},{3,11},{4,12},{5,13},{6,14},{7,15},{8,0},{9,1},... | collective-permute-start | bytes 786440 | tf_op jit(solution)/shard_map/ppermute | solution.py:210
  29.7 1.9 %copy-start.4 = (bf16[1,2048,768]{2,1,0:T(8,128)(2,1)S(1)}, bf16[1,2048,768]{2,1,0:T(8,128)(2,1)}, u32[]{:S(2)}) copy-start(bf16[1,2048,768]{2,1,0:T(8,128)(2,1)} %param.10) | copy-start | bytes 9437188
  31.6 1.9 %copy-start.7 = (bf16[1,768,2048]{2,1,0:T(8,128)(2,1)S(1)}, bf16[1,768,2048]{2,1,0:T(8,128)(2,1)}, u32[]{:S(2)}) copy-start(bf16[1,768,2048]{2,1,0:T(8,128)(2,1)} %param.11) | copy-start | bytes 9437188
  33.5 1.0 copy-start.11
  34.5 1.0 copy-start.16
  35.6 8.2 %copy-start.27 = (bf16[64,2048]{1,0:T(8,128)(2,1)S(1)}, bf16[64,2048]{1,0:T(8,128)(2,1)}, u32[]{:S(2)}) copy-start(bf16[64,2048]{1,0:T(8,128)(2,1)} %copy-done.26) | copy-start | bytes 786436
  42.5 1.0 copy-start.9
  43.6 3.0 %copy-start.14 = (bf16[256,2048]{1,0:T(8,128)(2,1)}, bf16[256,2048]{1,0:T(8,128)(2,1)S(1)}, u32[]{:S(2)}) copy-start(bf16[256,2048]{1,0:T(8,128)(2,1)S(1)} %get-tuple-element.99) | copy-start | bytes 3145732
  43.6 10.1 %copy-start.23 = (bf16[320,768]{1,0:T(8,128)(2,1)}, bf16[320,768]{1,0:T(8,128)(2,1)S(1)}, u32[]{:S(2)}) copy-start(bf16[320,768]{1,0:T(8,128)(2,1)S(1)} %get-tuple-element.105) | copy-start | bytes 1474564
  43.6 3.0 %collective-permute-start.11 = (bf16[128,2048]{1,0:T(8,128)(2,1)}, bf16[128,2048]{1,0:T(8,128)(2,1)S(1)}, u32[]{:S(2)}, u32[]{:S(2)}) collective-permute-start(bf16[128,2048]{1,0:T(8,128)(2,1)} %collective-permute-done.5.refs_1_), channel_id=1, source_target_pairs={{0,1},{1,0},{2,3},{3,2},{4,5},{5,4},{6,7},{7,6},{8,9},{9,8},{10,11... | collective-permute-start | bytes 1572872 | tf_op jit(solution)/shard_map/ppermute | solution.py:210
  45.0 18.0 %copy-start.2 = (bf16[1,2048,768]{2,1,0:T(8,128)(2,1)S(1)}, bf16[1,2048,768]{2,1,0:T(8,128)(2,1)}, u32[]{:S(2)}) copy-start(bf16[1,2048,768]{2,1,0:T(8,128)(2,1)} %param.9) | copy-start | bytes 9437188
  45.0 18.0 %copy-start.5 = (bf16[1,2048,768]{2,1,0:T(8,128)(2,1)S(1)}, bf16[1,2048,768]{2,1,0:T(8,128)(2,1)}, u32[]{:S(2)}) copy-start(bf16[1,2048,768]{2,1,0:T(8,128)(2,1)} %param.10) | copy-start | bytes 9437188
  45.0 8.9 %collective-permute-start.10 = (bf16[128,2048]{1,0:T(8,128)(2,1)S(1)}, bf16[128,2048]{1,0:T(8,128)(2,1)S(1)}, u32[]{:S(2)}, u32[]{:S(2)}) collective-permute-start(bf16[128,2048]{1,0:T(8,128)(2,1)S(1)} %constant_dynamic-update-slice_fusion.refs_0_), channel_id=1, source_target_pairs={{0,1},{1,0},{2,3},{3,2},{4,5},{5,4},{6,7},{7,6},{8,9},{9,8},{10,11... | collective-permute-start | bytes 1572872 | tf_op jit(solution)/shard_map/ppermute | solution.py:210
  45.3 14.1 %collective-permute-start.8 = (bf16[128,2048]{1,0:T(8,128)(2,1)S(1)}, bf16[128,2048]{1,0:T(8,128)(2,1)S(1)}, u32[]{:S(2)}, u32[]{:S(2)}) collective-permute-start(bf16[128,2048]{1,0:T(8,128)(2,1)S(1)} %constant_dynamic-update-slice_fusion.refs_0_), channel_id=1, source_target_pairs={{0,4},{1,5},{2,6},{3,7},{4,0},{5,1},{6,2},{7,3},{8,12},{9,13},{10,... | collective-permute-start | bytes 1572872 | tf_op jit(solution)/shard_map/ppermute | solution.py:210
  45.8 13.9 %collective-permute-start.9 = (bf16[128,2048]{1,0:T(8,128)(2,1)S(1)}, bf16[128,2048]{1,0:T(8,128)(2,1)S(1)}, u32[]{:S(2)}, u32[]{:S(2)}) collective-permute-start(bf16[128,2048]{1,0:T(8,128)(2,1)S(1)} %constant_dynamic-update-slice_fusion.refs_0_), channel_id=1, source_target_pairs={{0,2},{1,3},{2,0},{3,1},{4,6},{5,7},{6,4},{7,5},{8,10},{9,11},{10,... | collective-permute-start | bytes 1572872 | tf_op jit(solution)/shard_map/ppermute | solution.py:210
  53.7 9.3 %copy-start.17 = (bf16[320,768]{1,0:T(8,128)(2,1)}, bf16[320,768]{1,0:T(8,128)(2,1)S(1)}, u32[]{:S(2)}) copy-start(bf16[320,768]{1,0:T(8,128)(2,1)S(1)} %get-tuple-element.106) | copy-start | bytes 1474564
  53.7 6.0 %collective-permute-start.12 = (bf16[128,2048]{1,0:T(8,128)(2,1)S(1)}, bf16[128,2048]{1,0:T(8,128)(2,1)S(1)}, u32[]{:S(2)}, u32[]{:S(2)}) collective-permute-start(bf16[128,2048]{1,0:T(8,128)(2,1)S(1)} %get-tuple-element.75), channel_id=1, source_target_pairs={{0,1},{1,0},{2,3},{3,2},{4,5},{5,4},{6,7},{7,6},{8,9},{9,8},{10,11... | collective-permute-start | bytes 1572872 | tf_op jit(solution)/shard_map/ppermute | solution.py:210
  59.7 3.3 %collective-permute-start.17 = (bf16[128,2048]{1,0:T(8,128)(2,1)S(1)}, bf16[128,2048]{1,0:T(8,128)(2,1)S(1)}, u32[]{:S(2)}, u32[]{:S(2)}) collective-permute-start(bf16[128,2048]{1,0:T(8,128)(2,1)S(1)} %collective-permute-done.9.refs_1_), channel_id=1, source_target_pairs={{0,1},{1,0},{2,3},{3,2},{4,5},{5,4},{6,7},{7,6},{8,9},{9,8},{10,11... | collective-permute-start | bytes 1572872 | tf_op jit(solution)/shard_map/ppermute | solution.py:210
  59.7 15.8 %collective-permute-start.13 = (bf16[128,2048]{1,0:T(8,128)(2,1)S(1)}, bf16[128,2048]{1,0:T(8,128)(2,1)S(1)}, u32[]{:S(2)}, u32[]{:S(2)}) collective-permute-start(bf16[128,2048]{1,0:T(8,128)(2,1)S(1)} %collective-permute-done.9.refs_1_), channel_id=1, source_target_pairs={{0,4},{1,5},{2,6},{3,7},{4,0},{5,1},{6,2},{7,3},{8,12},{9,13},{10,... | collective-permute-start | bytes 1572872 | tf_op jit(solution)/shard_map/ppermute | solution.py:210
  61.3 17.6 %copy-start.8 = (bf16[1,768,2048]{2,1,0:T(8,128)(2,1)S(1)}, bf16[1,768,2048]{2,1,0:T(8,128)(2,1)}, u32[]{:S(2)}) copy-start(bf16[1,768,2048]{2,1,0:T(8,128)(2,1)} %param.11) | copy-start | bytes 9437188
  61.3 14.1 %collective-permute-start.14 = (bf16[128,2048]{1,0:T(8,128)(2,1)S(1)}, bf16[128,2048]{1,0:T(8,128)(2,1)S(1)}, u32[]{:S(2)}, u32[]{:S(2)}) collective-permute-start(bf16[128,2048]{1,0:T(8,128)(2,1)S(1)} %add_convert_fusion.2), channel_id=1, source_target_pairs={{0,2},{1,3},{2,0},{3,1},{4,6},{5,7},{6,4},{7,5},{8,10},{9,11},{10,... | collective-permute-start | bytes 1572872 | tf_op jit(solution)/shard_map/ppermute | solution.py:210
  62.5 13.0 %collective-permute-start.15 = (bf16[128,2048]{1,0:T(8,128)(2,1)S(1)}, bf16[128,2048]{1,0:T(8,128)(2,1)S(1)}, u32[]{:S(2)}, u32[]{:S(2)}) collective-permute-start(bf16[128,2048]{1,0:T(8,128)(2,1)S(1)} %collective-permute-done.8.refs_0_), channel_id=1, source_target_pairs={{0,1},{1,0},{2,3},{3,2},{4,5},{5,4},{6,7},{7,6},{8,9},{9,8},{10,11... | collective-permute-start | bytes 1572872 | tf_op jit(solution)/shard_map/ppermute | solution.py:210
  62.5 13.0 %collective-permute-start.16 = (bf16[128,2048]{1,0:T(8,128)(2,1)S(1)}, bf16[128,2048]{1,0:T(8,128)(2,1)S(1)}, u32[]{:S(2)}, u32[]{:S(2)}) collective-permute-start(bf16[128,2048]{1,0:T(8,128)(2,1)S(1)} %get-tuple-element.80), channel_id=1, source_target_pairs={{0,1},{1,0},{2,3},{3,2},{4,5},{5,4},{6,7},{7,6},{8,9},{9,8},{10,11... | collective-permute-start | bytes 1572872 | tf_op jit(solution)/shard_map/ppermute | solution.py:210
  68.6 16.8 %copy-start.19 = (bf16[320,768]{1,0:T(8,128)(2,1)}, bf16[320,768]{1,0:T(8,128)(2,1)S(1)}, u32[]{:S(2)}) copy-start(bf16[320,768]{1,0:T(8,128)(2,1)S(1)} %get-tuple-element.107) | copy-start | bytes 1474564
  75.5 10.7 %collective-permute-start.19 = (bf16[256,2048]{1,0:T(8,128)(2,1)S(1)}, bf16[256,2048]{1,0:T(8,128)(2,1)S(1)}, u32[]{:S(2)}, u32[]{:S(2)}) collective-permute-start(bf16[256,2048]{1,0:T(8,128)(2,1)S(1)} %get-tuple-element.90), channel_id=1, source_target_pairs={{0,1},{1,0},{2,3},{3,2},{4,5},{5,4},{6,7},{7,6},{8,9},{9,8},{10,11... | collective-permute-start | bytes 3145736 | tf_op jit(solution)/shard_map/ppermute | solution.py:210
  75.6 3.4 %collective-permute-start.18 = (bf16[128,2048]{1,0:T(8,128)(2,1)S(1)}, bf16[128,2048]{1,0:T(8,128)(2,1)S(1)}, u32[]{:S(2)}, u32[]{:S(2)}) collective-permute-start(bf16[128,2048]{1,0:T(8,128)(2,1)S(1)} %collective-permute-done.13.refs_1_), channel_id=1, source_target_pairs={{0,1},{1,0},{2,3},{3,2},{4,5},{5,4},{6,7},{7,6},{8,9},{9,8},{10,11... | collective-permute-start | bytes 1572872 | tf_op jit(solution)/shard_map/ppermute | solution.py:210
  76.3 9.9 %copy-start.25 = (bf16[128,2048]{1,0:T(8,128)(2,1)}, bf16[128,2048]{1,0:T(8,128)(2,1)S(1)}, u32[]{:S(2)}) copy-start(bf16[128,2048]{1,0:T(8,128)(2,1)S(1)} %add_convert_fusion.1) | copy-start | bytes 1572868
  76.3 9.9 %collective-permute-start.20 = (bf16[48,2048]{1,0:T(8,128)(2,1)S(1)}, bf16[48,2048]{1,0:T(8,128)(2,1)S(1)}, u32[]{:S(2)}, u32[]{:S(2)}) collective-permute-start(bf16[48,2048]{1,0:T(8,128)(2,1)S(1)} %slice.88), channel_id=1, source_target_pairs={{0,4},{1,5},{2,6},{3,7},{4,0},{5,1},{6,2},{7,3},{8,12},{9,13},{10,... | collective-permute-start | bytes 589832 | tf_op jit(solution)/shard_map/ppermute | solution.py:210
  85.4 0.8 copy-start.21
  86.2 4.4 %collective-permute-start.21 = (bf16[256,2048]{1,0:T(8,128)(2,1)}, bf16[256,2048]{1,0:T(8,128)(2,1)}, u32[]{:S(2)}, u32[]{:S(2)}) collective-permute-start(bf16[256,2048]{1,0:T(8,128)(2,1)} %get-tuple-element.94), channel_id=1, source_target_pairs={{0,1},{1,0},{2,3},{3,2},{4,5},{5,4},{6,7},{7,6},{8,9},{9,8},{10,11... | collective-permute-start | bytes 3145736 | tf_op jit(solution)/shard_map/ppermute | solution.py:210
  87.6 8.0 %copy-start.10 = (bf16[256,2048]{1,0:T(8,128)(2,1)S(1)}, bf16[256,2048]{1,0:T(8,128)(2,1)}, u32[]{:S(2)}) copy-start(bf16[256,2048]{1,0:T(8,128)(2,1)} %copy-done.9) | copy-start | bytes 3145732
  87.6 8.0 %collective-permute-start.26 = (bf16[256,2048]{1,0:T(8,128)(2,1)}, bf16[256,2048]{1,0:T(8,128)(2,1)S(1)}, u32[]{:S(2)}, u32[]{:S(2)}) collective-permute-start(bf16[256,2048]{1,0:T(8,128)(2,1)} %copy-done.14), channel_id=1, source_target_pairs={{0,1},{1,0},{2,3},{3,2},{4,5},{5,4},{6,7},{7,6},{8,9},{9,8},{10,11... | collective-permute-start | bytes 3145736 | tf_op jit(solution)/shard_map/ppermute | solution.py:210
  88.1 7.8 %collective-permute-start.24 = (bf16[48,2048]{1,0:T(8,128)(2,1)S(1)}, bf16[48,2048]{1,0:T(8,128)(2,1)S(1)}, u32[]{:S(2)}, u32[]{:S(2)}) collective-permute-start(bf16[48,2048]{1,0:T(8,128)(2,1)S(1)} %add_convert_fusion.8), channel_id=1, source_target_pairs={{0,2},{1,3},{2,0},{3,1},{4,6},{5,7},{6,4},{7,5},{8,10},{9,11},{10,... | collective-permute-start | bytes 589832 | tf_op jit(solution)/shard_map/ppermute | solution.py:210
  90.1 5.6 %collective-permute-start.25 = (bf16[32,2048]{1,0:T(8,128)(2,1)S(1)}, bf16[32,2048]{1,0:T(8,128)(2,1)S(1)}, u32[]{:S(2)}, u32[]{:S(2)}) collective-permute-start(bf16[32,2048]{1,0:T(8,128)(2,1)S(1)} %slice.77), channel_id=1, source_target_pairs={{0,4},{1,5},{2,6},{3,7},{4,0},{5,1},{6,2},{7,3},{8,12},{9,13},{10,... | collective-permute-start | bytes 393224 | tf_op jit(solution)/shard_map/ppermute | solution.py:210
  91.5 7.8 %collective-permute-start.23 = (bf16[48,2048]{1,0:T(8,128)(2,1)S(1)}, bf16[48,2048]{1,0:T(8,128)(2,1)S(1)}, u32[]{:S(2)}, u32[]{:S(2)}) collective-permute-start(bf16[48,2048]{1,0:T(8,128)(2,1)S(1)} %add_convert_fusion.9), channel_id=1, source_target_pairs={{0,2},{1,3},{2,0},{3,1},{4,6},{5,7},{6,4},{7,5},{8,10},{9,11},{10,... | collective-permute-start | bytes 589832 | tf_op jit(solution)/shard_map/ppermute | solution.py:210
  94.0 9.0 %collective-permute-start.22 = (bf16[80,2048]{1,0:T(8,128)(2,1)S(1)}, bf16[80,2048]{1,0:T(8,128)(2,1)S(1)}, u32[]{:S(2)}, u32[]{:S(2)}) collective-permute-start(bf16[80,2048]{1,0:T(8,128)(2,1)S(1)} %get-tuple-element.117), channel_id=1, source_target_pairs={{0,4},{1,5},{2,6},{3,7},{4,0},{5,1},{6,2},{7,3},{8,12},{9,13},{10,... | collective-permute-start | bytes 983048 | tf_op jit(solution)/shard_map/ppermute | solution.py:210
  103.0 6.7 %copy-start.18 = (bf16[320,768]{1,0:T(8,128)(2,1)S(1)}, bf16[320,768]{1,0:T(8,128)(2,1)}, u32[]{:S(2)}) copy-start(bf16[320,768]{1,0:T(8,128)(2,1)} %copy-done.17) | copy-start | bytes 1474564
  103.0 6.7 %copy-start.20 = (bf16[320,768]{1,0:T(8,128)(2,1)S(1)}, bf16[320,768]{1,0:T(8,128)(2,1)}, u32[]{:S(2)}) copy-start(bf16[320,768]{1,0:T(8,128)(2,1)} %copy-done.19) | copy-start | bytes 1474564
  103.0 6.7 %copy-start.22 = (bf16[320,768]{1,0:T(8,128)(2,1)S(1)}, bf16[320,768]{1,0:T(8,128)(2,1)}, u32[]{:S(2)}) copy-start(bf16[320,768]{1,0:T(8,128)(2,1)} %copy-done.21) | copy-start | bytes 1474564
  103.0 6.7 %copy-start.24 = (bf16[320,768]{1,0:T(8,128)(2,1)S(1)}, bf16[320,768]{1,0:T(8,128)(2,1)}, u32[]{:S(2)}) copy-start(bf16[320,768]{1,0:T(8,128)(2,1)} %copy-done.23) | copy-start | bytes 1474564
  104.5 20.5 %collective-permute-start.27 = (bf16[96,2048]{1,0:T(8,128)(2,1)S(1)}, bf16[96,2048]{1,0:T(8,128)(2,1)S(1)}, u32[]{:S(2)}, u32[]{:S(2)}) collective-permute-start(bf16[96,2048]{1,0:T(8,128)(2,1)S(1)} %shard_map.82), channel_id=1, source_target_pairs={{0,8},{1,9},{2,10},{3,11},{4,12},{5,13},{6,14},{7,15},{8,0},{9,1},... | collective-permute-start | bytes 1179656 | tf_op jit(solution)/shard_map/ppermute | solution.py:210
  106.0 18.9 %collective-permute-start.30 = (bf16[128,2048]{1,0:T(8,128)(2,1)S(1)}, bf16[128,2048]{1,0:T(8,128)(2,1)S(1)}, u32[]{:S(2)}, u32[]{:S(2)}) collective-permute-start(bf16[128,2048]{1,0:T(8,128)(2,1)S(1)} %add_convert_fusion), channel_id=1, source_target_pairs={{0,2},{1,3},{2,0},{3,1},{4,6},{5,7},{6,4},{7,5},{8,10},{9,11},{10,... | collective-permute-start | bytes 1572872 | tf_op jit(solution)/shard_map/ppermute | solution.py:210
  107.6 17.4 %collective-permute-start.29 = (bf16[80,2048]{1,0:T(8,128)(2,1)S(1)}, bf16[80,2048]{1,0:T(8,128)(2,1)S(1)}, u32[]{:S(2)}, u32[]{:S(2)}) collective-permute-start(bf16[80,2048]{1,0:T(8,128)(2,1)S(1)} %add_convert_fusion.4), channel_id=1, source_target_pairs={{0,2},{1,3},{2,0},{3,1},{4,6},{5,7},{6,4},{7,5},{8,10},{9,11},{10,... | collective-permute-start | bytes 983048 | tf_op jit(solution)/shard_map/ppermute | solution.py:210
  108.3 16.7 %collective-permute-start.28 = (bf16[80,2048]{1,0:T(8,128)(2,1)S(1)}, bf16[80,2048]{1,0:T(8,128)(2,1)S(1)}, u32[]{:S(2)}, u32[]{:S(2)}) collective-permute-start(bf16[80,2048]{1,0:T(8,128)(2,1)S(1)} %get-tuple-element.102), channel_id=1, source_target_pairs={{0,4},{1,5},{2,6},{3,7},{4,0},{5,1},{6,2},{7,3},{8,12},{9,13},{10,... | collective-permute-start | bytes 983048 | tf_op jit(solution)/shard_map/ppermute | solution.py:210
  125.2 14.9 %collective-permute-start.32 = (bf16[80,2048]{1,0:T(8,128)(2,1)S(1)}, bf16[80,2048]{1,0:T(8,128)(2,1)S(1)}, u32[]{:S(2)}, u32[]{:S(2)}) collective-permute-start(bf16[80,2048]{1,0:T(8,128)(2,1)S(1)} %add_convert_fusion.3), channel_id=1, source_target_pairs={{0,8},{1,9},{2,10},{3,11},{4,12},{5,13},{6,14},{7,15},{8,0},{9,1},... | collective-permute-start | bytes 983048 | tf_op jit(solution)/shard_map/ppermute | solution.py:210
  127.7 7.6 %collective-permute-start.31 = (bf16[48,2048]{1,0:T(8,128)(2,1)S(1)}, bf16[48,2048]{1,0:T(8,128)(2,1)S(1)}, u32[]{:S(2)}, u32[]{:S(2)}) collective-permute-start(bf16[48,2048]{1,0:T(8,128)(2,1)S(1)} %add_convert_fusion.7), channel_id=1, source_target_pairs={{0,4},{1,5},{2,6},{3,7},{4,0},{5,1},{6,2},{7,3},{8,12},{9,13},{10,... | collective-permute-start | bytes 589832 | tf_op jit(solution)/shard_map/ppermute | solution.py:210

commit v15 on v14

--- a/solution.py
+++ b/solution.py
@@ -28,7 +28,7 @@
     return lax.all_to_all(mine, "expert", split_axis=0, concat_axis=0, tiled=True)
 
 
-def table_kernel(routes, probs, w_gate, w_up, w_down, mine):
+def table_kernel(routes, probs, mine):
     names, shares = routes[...], probs[...]
     for e in range(mine.shape[0]):
         hit = (names == e).astype(jnp.float32)
@@ -37,14 +37,14 @@
         mine[pl.ds(e, 1), :] = jnp.where(named > 0.0, share, -1.0)
 
 
-def table_pass(routes, probs, experts, w_gate, w_up, w_down):
+def table_pass(routes, probs, experts):
     mine = pl.pallas_call(
         table_kernel,
         out_shape=jax.ShapeDtypeStruct((experts, routes.shape[0]), jnp.float32),
-        in_specs=[pl.BlockSpec(memory_space=pltpu.VMEM)] * 5,
+        in_specs=[pl.BlockSpec(memory_space=pltpu.VMEM)] * 2,
         out_specs=pl.BlockSpec(memory_space=pltpu.VMEM),
         compiler_params=pltpu.CompilerParams(vmem_limit_bytes=4 * 1024 * 1024),
-    )(routes.T, probs.T, w_gate, w_up, w_down)
+    )(routes.T, probs.T)
     return lax.all_to_all(mine, "expert", split_axis=0, concat_axis=0, tiled=True)
 
 
@@ -55,27 +55,43 @@
     return total.astype(jnp.bfloat16)
 
 
-def fill_tables(capacity, spots, weight, ranks, tables):
+def ranks_kernel(capacity, spots, weight, w_gate, w_up, w_down, tables, ranks):
     blocks, tok = weight.shape
+    planes = blocks // 4
     named = (weight[...] >= 0.0).astype(jnp.float32)
     lane = lax.broadcasted_iota(jnp.int32, (tok, tok), 0)
     below = (lane < lax.broadcasted_iota(jnp.int32, (tok, tok), 1)).astype(jnp.float32)
     within = jnp.dot(named, below, preferred_element_type=jnp.float32)
     totals = jnp.broadcast_to(jnp.sum(named, axis=1, keepdims=True), (blocks, tok))
     row = lax.broadcasted_iota(jnp.int32, (blocks, blocks), 0)
-    earlier = (lax.broadcasted_iota(jnp.int32, (blocks, blocks), 1) < row).astype(jnp.float32)
+    column = lax.broadcasted_iota(jnp.int32, (blocks, blocks), 1)
+    earlier = (column < row).astype(jnp.float32)
     before = jnp.dot(earlier, totals, preferred_element_type=jnp.float32)
     rank = within + before
     kept = (named > 0.0) & (rank < capacity)
-    first = lax.broadcasted_iota(jnp.int32, (blocks, blocks), 0) // 4 * 4
-    column = lax.broadcasted_iota(jnp.int32, (blocks, blocks), 1)
-    start = jnp.dot((column < first).astype(jnp.float32), totals, preferred_element_type=jnp.float32)
+    first = (column < row // 4 * 4).astype(jnp.float32)
+    start = jnp.dot(first, totals, preferred_element_type=jnp.float32)
     ranks[...] = jnp.where(kept, rank - start, -1.0)
-    for k in range(blocks // 4):
+    for k in range(planes):
         for i in range(4):
             span = pl.ds(i * tok, tok)
             tables[pl.ds(k, 1), span] = ranks[pl.ds(spots[4 * k + i], 1), :]
-            tables[pl.ds(blocks // 4 + k, 1), span] = weight[pl.ds(spots[4 * k + i], 1), :]
+            tables[pl.ds(planes + k, 1), span] = weight[pl.ds(spots[4 * k + i], 1), :]
+    count = jnp.minimum(jnp.sum(totals[:, :1], axis=0, keepdims=True), float(capacity))
+    tables[2 * planes :, :] = jnp.broadcast_to(2.0 / count, tables[2 * planes :, :].shape)
+
+
+def ranks_pass(capacity, spots, weight, w_gate, w_up, w_down):
+    blocks, tok = weight.shape
+    vmem = pl.BlockSpec(memory_space=pltpu.VMEM)
+    return pl.pallas_call(
+        functools.partial(ranks_kernel, capacity),
+        out_shape=jax.ShapeDtypeStruct((blocks // 4 * 2 + 8, 4 * tok), jnp.float32),
+        in_specs=[pl.BlockSpec(memory_space=pltpu.SMEM)] + [vmem] * 4,
+        out_specs=vmem,
+        scratch_shapes=[pltpu.VMEM(weight.shape, jnp.float32)],
+        compiler_params=pltpu.CompilerParams(vmem_limit_bytes=4 * 1024 * 1024),
+    )(spots, weight, w_gate, w_up, w_down)
 
 
 def plane_kernel(k, gives, tables, *refs):
@@ -86,7 +102,7 @@
     half, width = keep.shape[0], tables.shape[1]
     wide, cut = 256, 512
     place = tables[pl.ds(k, 1), :]
-    share = tables[pl.ds(tables.shape[0] // 2 + k, 1), :]
+    share = tables[pl.ds(4 + k, 1), :]
     slot = lax.broadcasted_iota(jnp.int32, (slots, width), 0).astype(jnp.float32)
     hits = slot == place
     scale = jnp.sum(jnp.where(hits, share, 0.0), axis=1, keepdims=True)
@@ -113,13 +129,7 @@
             start += give.shape[0]
 
 
-def first_kernel(capacity, spots, weight, *refs):
-    *plane, tables, rows, ranks = refs
-    fill_tables(capacity, spots, weight, ranks, tables)
-    plane_kernel(0, 1, tables, *plane, rows)
-
-
-def plane_pass(k, tables, xs, w_gate, w_up, w_down, slots, first=None, pieces=None):
+def plane_pass(k, tables, xs, w_gate, w_up, w_down, slots, pieces=None):
     tok, features = xs[0].shape
     hidden = w_gate.shape[1]
     rows = 4 * slots
@@ -128,29 +138,20 @@
         jax.ShapeDtypeStruct((some, features), jnp.bfloat16) for some in (2 * tok, *pieces)
     )
     outs += (jax.ShapeDtypeStruct((rows, hidden), jnp.bfloat16),)
-    scratch = [pltpu.VMEM((rows, features), jnp.bfloat16)]
     vmem = pl.BlockSpec(memory_space=pltpu.VMEM)
-    if first is None:
-        body, inputs, specs = functools.partial(plane_kernel, k, len(pieces)), (tables,), [vmem]
-    else:
-        capacity, spots, weight = first
-        body = functools.partial(first_kernel, capacity)
-        inputs, specs = (spots, weight), [pl.BlockSpec(memory_space=pltpu.SMEM), vmem]
-        outs += (jax.ShapeDtypeStruct((weight.shape[0] // 2, 4 * tok), jnp.float32),)
-        scratch.append(pltpu.VMEM(weight.shape, jnp.float32))
     flops = 2 * rows * (3 * features * hidden + 8 * tok * features)
     moved = 2 * (3 * features * hidden + 8 * tok * features)
     return pl.pallas_call(
-        body,
+        functools.partial(plane_kernel, k, len(pieces)),
         out_shape=outs,
-        in_specs=specs + [vmem] * (len(xs) + 3),
+        in_specs=[vmem] * (len(xs) + 4),
         out_specs=[vmem] * len(outs),
-        scratch_shapes=scratch,
+        scratch_shapes=[pltpu.VMEM((rows, features), jnp.bfloat16)],
         compiler_params=pltpu.CompilerParams(vmem_limit_bytes=12 * 1024 * 1024),
         cost_estimate=pl.CostEstimate(
             flops=flops, bytes_accessed=moved, transcendentals=rows * hidden
         ),
-    )(*inputs, *xs, w_gate, w_up, w_down)
+    )(tables, *xs, w_gate, w_up, w_down)
 
 
 def high_kernel(keep3, got3, high3, keep2, got2, high2, both):
@@ -173,11 +174,10 @@
     )(*parts)
 
 
-def mix_kernel(keep, got, side, near_low, near_mid, near_high, far_low, far_high, mixed):
-    least, most, tok = near_low.shape[0], far_low.shape[0], mixed.shape[0]
+def mix_kernel(keep, got, side, near_low, near_high, far_low, far_high, mixed):
+    most, tok = near_low.shape[0], mixed.shape[0]
     for start, stop, near, far in (
-        (0, least, near_low, far_low[:least, :]),
-        (least, most, near_mid, far_low[least:, :]),
+        (0, most, near_low, far_low[...]),
         (most, tok, near_high, far_high[tok - most :, :]),
     ):
         total = keep[start:stop, :].astype(jnp.float32) + got[start:stop, :].astype(jnp.float32)
@@ -226,30 +226,26 @@
         ]
     ).astype(jnp.int32)
 
-    def expert(k, tables, *xs, first=None, pieces=None):
-        return plane_pass(k, tables, xs, w_gate, w_up, w_down, slots, first, pieces)
-
-    weight = table_pass(routes, probs, size, w_gate, w_up, w_down)
-    a0 = tokens
-    a1, low, b0, c0, weight = together(
-        pair(a0), far(a0[:half]), column(a0), sibling(a0), weight
+    def expert(k, *xs, pieces=None):
+        return plane_pass(k, tables, xs, w_gate, w_up, w_down, slots, pieces)
+
+    a0, weight = together(tokens, table_pass(routes, probs, size))
+    tables = ranks_pass(capacity, spots, weight, w_gate, w_up, w_down)
+    a1, low, b0, c0, tables = together(
+        pair(a0), far(a0[:half]), column(a0), sibling(a0), tables
     )
     high = far(a0[half:])
     b1 = column(a1)
     d0 = sibling(b0)
     c1 = sibling(a1)
-    keep0, give0, act0, tables = expert(
-        0, None, a0, b0, c0, d0, first=(capacity, spots, weight)
-    )
-    high, b1, c1, keep0, give0, act0, tables = together(
-        high, b1, c1, keep0, give0, act0, tables
-    )
+    keep0, give0, act0 = expert(0, a0, b0, c0, d0)
+    high, b1, c1, keep0, give0, act0 = together(high, b1, c1, keep0, give0, act0)
     a2 = jnp.concatenate([low, high], axis=0)
     a3 = pair(a2)
     b2 = column(a2)
     d1 = sibling(b1)
     c2 = sibling(a2)
-    keep1, give1, *give1_side, act1 = expert(1, tables, a1, b1, c1, d1, pieces=(tok, tok))
+    keep1, give1, *give1_side, act1 = expert(1, a1, b1, c1, d1, pieces=(tok, tok))
     got1_side = [sibling(piece) for piece in give1_side]
     a3, b2, c2, keep1, give1, act1, *got1_side = together(
         a3, b2, c2, keep1, give1, act1, *got1_side
@@ -259,47 +255,42 @@
     got1 = sibling(give1)
     d2 = sibling(b2)
     c3 = sibling(a3)
-    keep2, give2, act2 = expert(2, tables, a2, b2, c2, d2)
+    keep2, give2, act2 = expert(2, a2, b2, c2, d2)
     b3, came1, c3, got1, keep2, give2, act2 = together(b3, came1, c3, got1, keep2, give2, act2)
     d3 = sibling(b3)
     near1 = summed(keep1[:tok], got1, came1)
     most = 5 * tok // 8
     least = tok - most
-    got2 = sibling(give2)
-    near1_low = pair(near1[:least])
-    keep3, give3, act3 = expert(3, tables, a3, b3, c3, d3)
-    keep3, give3, act3, got2, near1, near1_low = together(
-        keep3, give3, act3, got2, near1, near1_low
-    )
-    got0 = sibling(give0)
 
     def own(keep, got, start, stop, *more):
         return summed(keep[start:stop], got[start:stop], *more)
 
+    near1_low = pair(near1[:most])
+    got2 = sibling(give2)
+    side_high = column(own(keep2, got2, tok + most, 2 * tok))
+    keep3, give3, act3 = expert(3, a3, b3, c3, d3)
+    keep3, give3, act3, got2, near1, near1_low, side_high = together(
+        keep3, give3, act3, got2, near1, near1_low, side_high
+    )
+    got0 = sibling(give0)
     got3 = sibling(give3)
     low = pair(own(keep3, got3, tok, tok + most))
     high = column(own(keep3, got3, tok + most, 2 * tok))
-    side_high = column(own(keep2, got2, tok + most, 2 * tok))
-    near1_mid = pair(near1[least:most])
     sum3 = own(keep3, got3, 0, most)
     side0 = own(keep0, got0, tok, 2 * tok)
-    low, high, side_high, near1_mid, sum3, side0 = together(
-        low, high, side_high, near1_mid, sum3, side0
-    )
+    low, high, sum3, side0 = together(low, high, sum3, side0)
     far_high = far(high_pass(keep3, got3, high, keep2, got2, side_high))
     pair3_low = pair(sum3)
     side_low = column(own(keep2, got2, tok, tok + most, low))
-    last0 = column(side0)
-    acts = jnp.concatenate([act0, act1, act2, act3], axis=0)
-    count = jnp.minimum(jnp.sum((weight >= 0.0).astype(jnp.float32)), float(capacity))
-    gram = gram_of(acts) * (2.0 / count)
-    far_high, pair3_low, side_low, last0, gram = together(
-        far_high, pair3_low, side_low, last0, gram
+    gram = gram_of(jnp.concatenate([act0, act1, act2, act3], axis=0)) * tables[8, 0]
+    far_high, pair3_low, side_low, side0, gram = together(
+        far_high, pair3_low, side_low, side0, gram
     )
     far2_low = far(own(keep2, got2, 0, most, pair3_low, side_low))
     near1_high = pair(summed(near1[most:], far_high[:least]))
+    last0 = column(side0)
     mixed = mix_pass(
-        keep0, got0, last0, near1_low, near1_mid, near1_high, far2_low, far_high
+        keep0, got0, last0, near1_low, near1_high, far2_low, far_high
     )
 
     return gram[None], mixed

time: 142 us -> 143 us (level)
  waiting for transfers between devices: 45.6 us -> 73.1 us
  local copies, waits for them, and re-layouts: 20.2 us -> 8.83 us
  starting transfers between devices: 27.9 us -> 17.6 us
  Pallas kernels: 28.8 us -> 24.1 us
  blocking collectives: 9.24 us -> 13.6 us
  other arithmetic: 4.64 us -> 1.12 us
    ppermute x33 -> x32, waiting for transfers between devices: 45.6 us -> 73.1 us  [swapped(): return lax.ppermute(array, 'expert', [(i, i ^ bit) for i in range(size)])]
    ppermute x33 -> x32, starting transfers between devices: 27.9 us -> 17.6 us  [swapped(): return lax.ppermute(array, 'expert', [(i, i ^ bit) for i in range(size)])]
    unnamed x57 -> x19, local copies, waits for them, and re-layouts: 16.3 us -> 7.06 us
    all_to_all x1, blocking collectives: 9.24 us -> 13.6 us  [table_pass(): lax.all_to_all(mine, 'expert', split_axis=0, concat_axis=0, tiled=True)]
    pallas_call x4 -> x5, Pallas kernels: 26.2 us -> 22.8 us  [the longest x4 22 us: plane_pass(): pl.pallas_call(functools.partial(plane_kernel, k, len(pieces)), out_shape...]
    convert_element_type x9, other arithmetic: 4.04 us -> 1.12 us  [summed(): return total.astype(jnp.bfloat16)]
  transfers between devices with their start and end apart: 33 -> 32, of which waited for: 11 -> 19; matrix products, arithmetic and copies ran while one was open for 8% -> 5% of each run, Pallas kernels for 19% -> 16%
where the time goes in v15:
time: 143 us
  waiting for transfers between devices  73.1 us (51%)
  Pallas kernels  24.1 us (17%)
  starting transfers between devices  17.6 us (12%)
  blocking collectives  13.6 us (10%)
  local copies, waits for them, and re-layouts  8.83 us (6%)
  matrix products  3.8 us (3%)
    ppermute x32, waiting for transfers between devices, swapped(): return lax.ppermute(array, 'expert', [(i, i ^ bit) for i in range(size)])  73.1 us
    pallas_call x4, Pallas kernels, plane_pass(): pl.pallas_call(functools.partial(plane_kernel, k, len(pieces)), out_shape...  22 us
    ppermute x32, starting transfers between devices, swapped(): return lax.ppermute(array, 'expert', [(i, i ^ bit) for i in range(size)])  17.6 us
    all_to_all x1, blocking collectives, table_pass(): lax.all_to_all(mine, 'expert', split_axis=0, concat_axis=0, tiled=True)  13.6 us
    unnamed x19, local copies, waits for them, and re-layouts  7.06 us
    dot_general x1, matrix products, gram_of(): lax.dot_general(rows, rows, (((0,), (0,)), ((), ())), preferred_element_t...  3.8 us
  transfers between devices with their start and end apart: 32, of which 19 were waited for; matrix products, arithmetic and copies ran while one was open for 5% of the time, Pallas kernels for 16%

profile of v15, /device:TPU:0, one launch (start us, length us, event | category | flops | bytes accessed | tf_op | source)
XLA Modules:
  0.0 142.9 jit_solution(10376595551539851820)
XLA Ops:
  0.6 0.7 copy-done.7
  1.3 0.7 copy-done.8
  2.0 13.6 %all_to_all.12 = f32[16,1,128]{2,1,0:T(1,128)S(1)} all-to-all(f32[16,1,128]{2,1,0:T(1,128)S(1)} %bitcast.42), channel_id=1, replica_groups=mesh['parts'=2,'expert'=16] {'expert'}, dimensions={0} | all-to-all | bytes 16384 | tf_op jit(solution)/shard_map/all_to_all | solution.py:48
  15.6 0.5 collective-permute-start.2
  16.2 0.6 collective-permute-start
  16.7 1.1 fusion.11
  17.9 0.7 collective-permute-start.1
  18.6 1.9 %copy-done = bf16[1,2048,768]{2,1,0:T(8,128)(2,1)S(1)} copy-done((bf16[1,2048,768]{2,1,0:T(8,128)(2,1)S(1)}, bf16[1,2048,768]{2,1,0:T(8,128)(2,1)}, u32[]{:S(2)}) %copy-start) | copy-done | bytes 3145752
  20.5 1.9 %copy-done.2 = bf16[1,2048,768]{2,1,0:T(8,128)(2,1)S(1)} copy-done((bf16[1,2048,768]{2,1,0:T(8,128)(2,1)S(1)}, bf16[1,2048,768]{2,1,0:T(8,128)(2,1)}, u32[]{:S(2)}) %copy-start.2) | copy-done | bytes 3145752
  22.4 1.9 %copy-done.4 = bf16[1,768,2048]{2,1,0:T(8,128)(2,1)S(1)} copy-done((bf16[1,768,2048]{2,1,0:T(8,128)(2,1)S(1)}, bf16[1,768,2048]{2,1,0:T(8,128)(2,1)}, u32[]{:S(2)}) %copy-start.4) | copy-done | bytes 3145752
  24.3 0.7 shard_map.78.tables
  25.1 9.1 %collective-permute-done.1 = bf16[64,2048]{1,0:T(8,128)(2,1)S(1)} collective-permute-done((bf16[64,2048]{1,0:T(8,128)(2,1)S(1)}, bf16[64,2048]{1,0:T(8,128)(2,1)S(1)}, u32[]{:S(2)}, u32[]{:S(2)}) %collective-permute-start.1) | collective-permute-done | bytes 262176 | tf_op jit(solution)/shard_map/ppermute | solution.py:210
  34.1 1.9 %collective-permute-done.refs_0_ = bf16[128,2048]{1,0:T(8,128)(2,1)S(1)} collective-permute-done((bf16[128,2048]{1,0:T(8,128)(2,1)}, bf16[128,2048]{1,0:T(8,128)(2,1)S(1)}, u32[]{:S(2)}, u32[]{:S(2)}) %collective-permute-start) | collective-permute-done | bytes 524320 | tf_op jit(solution)/shard_map/ppermute | solution.py:210
  36.0 0.5 collective-permute-start.6
  36.5 1.5 %collective-permute-start.5 = (bf16[128,2048]{1,0:T(8,128)(2,1)S(1)}, bf16[128,2048]{1,0:T(8,128)(2,1)S(1)}, u32[]{:S(2)}, u32[]{:S(2)}) collective-permute-start(bf16[128,2048]{1,0:T(8,128)(2,1)S(1)} %collective-permute-done.refs_0_), channel_id=1, source_target_pairs={{0,2},{1,3},{2,0},{3,1},{4,6},{5,7},{6,4},{7,5},{8,10},{9,11},{10,... | collective-permute-start | bytes 1572872 | tf_op jit(solution)/shard_map/ppermute | solution.py:210
  38.1 1.5 %collective-permute-start.4 = (bf16[64,2048]{1,0:T(8,128)(2,1)S(1)}, bf16[64,2048]{1,0:T(8,128)(2,1)S(1)}, u32[]{:S(2)}, u32[]{:S(2)}) collective-permute-start(bf16[64,2048]{1,0:T(8,128)(2,1)S(1)} %get-tuple-element.116), channel_id=1, source_target_pairs={{0,8},{1,9},{2,10},{3,11},{4,12},{5,13},{6,14},{7,15},{8,0},{9,1},... | collective-permute-start | bytes 786440 | tf_op jit(solution)/shard_map/ppermute | solution.py:210
  39.6 5.5 %shard_map.79 = (bf16[256,2048]{1,0:T(8,128)(2,1)S(1)}, bf16[256,2048]{1,0:T(8,128)(2,1)S(1)}, bf16[320,768]{1,0:T(8,128)(2,1)S(1)}) custom-call(f32[16,512]{1,0:T(8,128)S(1)} %shard_map.78.tables, bf16[128,2048]{1,0:T(8,128)(2,1)S(1)} %copy-done.6, bf16[128,2048]{1,0:T(8,128)(2,1)S(1)} %collective-permute-done.2.refs_1_, ...), custom_call_target="tpu_custom_call" | custom-call | flops 4362076160 | bytes 13631488 | tf_op jit(solution)/shard_map/pallas_call | solution.py:144
  45.1 7.5 %collective-permute-done.4 = bf16[64,2048]{1,0:T(8,128)(2,1)S(1)} collective-permute-done((bf16[64,2048]{1,0:T(8,128)(2,1)S(1)}, bf16[64,2048]{1,0:T(8,128)(2,1)S(1)}, u32[]{:S(2)}, u32[]{:S(2)}) %collective-permute-start.4) | collective-permute-done | bytes 262176 | tf_op jit(solution)/shard_map/ppermute | solution.py:210
  52.6 0.6 collective-permute-start.10
  53.2 0.5 collective-permute-start.9
  53.7 0.8 collective-permute-done.11.refs_3_
  54.4 5.5 %shard_map.80 = (bf16[256,2048]{1,0:T(8,128)(2,1)S(1)}, bf16[128,2048]{1,0:T(8,128)(2,1)S(1)}, bf16[128,2048]{1,0:T(8,128)(2,1)S(1)}, bf16[320,768]{1,0:T(8,128)(2,1)S(1)}) custom-call(f32[16,512]{1,0:T(8,128)S(1)} %shard_map.78.tables, bf16[128,2048]{1,0:T(8,128)(2,1)S(1)} %collective-permute-done.refs_0_, ...), custom_call_target="tpu_custom_call" | custom-call | flops 4362076160 | bytes 13631488 | tf_op jit(solution)/shard_map/pallas_call | solution.py:144
  59.9 0.2 collective-permute-start.12
  60.1 6.9 %collective-permute-done.9.refs_1_ = bf16[128,2048]{1,0:T(8,128)(2,1)S(1)} collective-permute-done((bf16[128,2048]{1,0:T(8,128)(2,1)S(1)}, bf16[128,2048]{1,0:T(8,128)(2,1)S(1)}, u32[]{:S(2)}, u32[]{:S(2)}) %collective-permute-start.9) | collective-permute-done | bytes 524320 | tf_op jit(solution)/shard_map/ppermute | solution.py:210
  67.1 0.2 collective-permute-done.8.refs_0_
  67.3 0.1 add_convert_fusion.2
  67.4 1.6 %collective-permute-start.14 = (bf16[128,2048]{1,0:T(8,128)(2,1)S(1)}, bf16[128,2048]{1,0:T(8,128)(2,1)S(1)}, u32[]{:S(2)}, u32[]{:S(2)}) collective-permute-start(bf16[128,2048]{1,0:T(8,128)(2,1)S(1)} %add_convert_fusion.2), channel_id=1, source_target_pairs={{0,2},{1,3},{2,0},{3,1},{4,6},{5,7},{6,4},{7,5},{8,10},{9,11},{10,... | collective-permute-start | bytes 1572872 | tf_op jit(solution)/shard_map/ppermute | solution.py:210
  69.0 0.2 collective-permute-start.16
  69.2 0.3 collective-permute-start.15
  69.5 0.3 collective-permute-start.13
  69.8 5.6 %shard_map.81 = (bf16[256,2048]{1,0:T(8,128)(2,1)S(1)}, bf16[256,2048]{1,0:T(8,128)(2,1)S(1)}, bf16[320,768]{1,0:T(8,128)(2,1)S(1)}) custom-call(f32[16,512]{1,0:T(8,128)S(1)} %shard_map.78.tables, bf16[128,2048]{1,0:T(8,128)(2,1)S(1)} %constant_dynamic-update-slice_fusion.refs_0_, bf16[128,2048]{1,0:T(8,128)(2,1)S(1)} %collective-permute-done.9.refs_1_, ...), custom_call_target="tpu_custom_call" | custom-call | flops 4362076160 | bytes 13631488 | tf_op jit(solution)/shard_map/pallas_call | solution.py:144
  75.5 6.4 %collective-permute-done.14 = bf16[128,2048]{1,0:T(8,128)(2,1)S(1)} collective-permute-done((bf16[128,2048]{1,0:T(8,128)(2,1)S(1)}, bf16[128,2048]{1,0:T(8,128)(2,1)S(1)}, u32[]{:S(2)}, u32[]{:S(2)}) %collective-permute-start.14) | collective-permute-done | bytes 524320 | tf_op jit(solution)/shard_map/ppermute | solution.py:210
  81.8 1.7 %collective-permute-done.13.refs_1_ = bf16[128,2048]{1,0:T(8,128)(2,1)S(1)} collective-permute-done((bf16[128,2048]{1,0:T(8,128)(2,1)S(1)}, bf16[128,2048]{1,0:T(8,128)(2,1)S(1)}, u32[]{:S(2)}, u32[]{:S(2)}) %collective-permute-start.13) | collective-permute-done | bytes 524320 | tf_op jit(solution)/shard_map/ppermute | solution.py:210
  83.6 0.5 collective-permute-start.18
  84.1 0.2 add_convert_fusion.1
  84.4 0.3 collective-permute-start.20
  84.7 1.5 %collective-permute-done.19.got2 = bf16[256,2048]{1,0:T(8,128)(2,1)S(1)} collective-permute-done((bf16[256,2048]{1,0:T(8,128)(2,1)S(1)}, bf16[256,2048]{1,0:T(8,128)(2,1)S(1)}, u32[]{:S(2)}, u32[]{:S(2)}) %collective-permute-start.19) | collective-permute-done | bytes 1048608 | tf_op jit(solution)/shard_map/ppermute | solution.py:210
  86.3 0.6 collective-permute-start.21
  86.9 0.1 collective-permute-done.18.refs_3_
  87.0 5.5 %shard_map.82 = (bf16[256,2048]{1,0:T(8,128)(2,1)S(1)}, bf16[256,2048]{1,0:T(8,128)(2,1)S(1)}, bf16[320,768]{1,0:T(8,128)(2,1)S(1)}) custom-call(f32[16,512]{1,0:T(8,128)S(1)} %shard_map.78.tables, bf16[128,2048]{1,0:T(8,128)(2,1)S(1)} %collective-permute-done.8.refs_0_, bf16[128,2048]{1,0:T(8,128)(2,1)S(1)} %collective-permute-done.13.refs_1_, ...), custom_call_target="tpu_custom_call" | custom-call | flops 4362076160 | bytes 13631488 | tf_op jit(solution)/shard_map/pallas_call | solution.py:144
  92.5 1.6 %collective-permute-done.20.near_low = bf16[80,2048]{1,0:T(8,128)(2,1)S(1)} collective-permute-done((bf16[80,2048]{1,0:T(8,128)(2,1)S(1)}, bf16[80,2048]{1,0:T(8,128)(2,1)S(1)}, u32[]{:S(2)}, u32[]{:S(2)}) %collective-permute-start.20) | collective-permute-done | bytes 327712 | tf_op jit(solution)/shard_map/ppermute | solution.py:210
  94.1 0.5 collective-permute-start.25
  94.6 0.5 slice.83
  95.1 1.6 %collective-permute-done.22.got3 = bf16[256,2048]{1,0:T(8,128)(2,1)S(1)} collective-permute-done((bf16[256,2048]{1,0:T(8,128)(2,1)S(1)}, bf16[256,2048]{1,0:T(8,128)(2,1)S(1)}, u32[]{:S(2)}, u32[]{:S(2)}) %collective-permute-start.22) | collective-permute-done | bytes 1048608 | tf_op jit(solution)/shard_map/ppermute | solution.py:210
  96.8 0.6 collective-permute-start.24
  97.3 0.2 add_convert_fusion.5
  97.5 0.4 collective-permute-start.23
  97.9 0.3 collective-permute-done.25.got
  98.2 0.1 add_convert_fusion
  98.3 5.4 %collective-permute-done.24.high3 = bf16[48,2048]{1,0:T(8,128)(2,1)S(1)} collective-permute-done((bf16[48,2048]{1,0:T(8,128)(2,1)S(1)}, bf16[48,2048]{1,0:T(8,128)(2,1)S(1)}, u32[]{:S(2)}, u32[]{:S(2)}) %collective-permute-start.24) | collective-permute-done | bytes 196640 | tf_op jit(solution)/shard_map/ppermute | solution.py:210
  103.8 3.3 %collective-permute-done.23 = bf16[80,2048]{1,0:T(8,128)(2,1)S(1)} collective-permute-done((bf16[80,2048]{1,0:T(8,128)(2,1)S(1)}, bf16[80,2048]{1,0:T(8,128)(2,1)S(1)}, u32[]{:S(2)}, u32[]{:S(2)}) %collective-permute-start.23) | collective-permute-done | bytes 327712 | tf_op jit(solution)/shard_map/ppermute | solution.py:210
  107.1 0.1 shard_map.83
  107.2 0.5 collective-permute-start.26
  107.8 1.2 collective-permute-start.28
  109.0 1.1 collective-permute-start.27
  110.1 3.8 %broadcast_multiply_fusion = f32[768,768]{1,0:T(8,128)} fusion(f32[]{:T(128)} %bitcast.24, bf16[320,768]{1,0:T(8,128)(2,1)S(1)} %get-tuple-element.106, bf16[320,768]{1,0:T(8,128)(2,1)S(1)} %get-tuple-element.105, bf16[320,768]{1,0:T(8,128)(2,1)S(1)} %get-tuple-element.104, bf16[320,768]{1,0:T(8,128)(2,1)S(1)} %get-tuple-element.103), kind=kOutput, calls=%fused_computation.8 | convolution fusion | flops 1518403584 | bytes 4325380 | tf_op jit(solution)/shard_map/dot_general | solution.py:12
  113.9 2.3 %collective-permute-done.28 = bf16[80,2048]{1,0:T(8,128)(2,1)S(1)} collective-permute-done((bf16[80,2048]{1,0:T(8,128)(2,1)S(1)}, bf16[80,2048]{1,0:T(8,128)(2,1)S(1)}, u32[]{:S(2)}, u32[]{:S(2)}) %collective-permute-start.28) | collective-permute-done | bytes 327712 | tf_op jit(solution)/shard_map/ppermute | solution.py:210
  116.2 6.1 %collective-permute-done.27 = bf16[80,2048]{1,0:T(8,128)(2,1)S(1)} collective-permute-done((bf16[80,2048]{1,0:T(8,128)(2,1)S(1)}, bf16[80,2048]{1,0:T(8,128)(2,1)S(1)}, u32[]{:S(2)}, u32[]{:S(2)}) %collective-permute-start.27) | collective-permute-done | bytes 327712 | tf_op jit(solution)/shard_map/ppermute | solution.py:210
  122.3 4.0 %collective-permute-done.26.far_high = bf16[96,2048]{1,0:T(8,128)(2,1)S(1)} collective-permute-done((bf16[96,2048]{1,0:T(8,128)(2,1)S(1)}, bf16[96,2048]{1,0:T(8,128)(2,1)S(1)}, u32[]{:S(2)}, u32[]{:S(2)}) %collective-permute-start.26) | collective-permute-done | bytes 393248 | tf_op jit(solution)/shard_map/ppermute | solution.py:210
  126.4 0.2 add_convert_fusion.3
  126.6 1.6 %collective-permute-start.29 = (bf16[128,2048]{1,0:T(8,128)(2,1)S(1)}, bf16[128,2048]{1,0:T(8,128)(2,1)S(1)}, u32[]{:S(2)}, u32[]{:S(2)}) collective-permute-start(bf16[128,2048]{1,0:T(8,128)(2,1)S(1)} %add_convert_fusion), channel_id=1, source_target_pairs={{0,2},{1,3},{2,0},{3,1},{4,6},{5,7},{6,4},{7,5},{8,10},{9,11},{10,... | collective-permute-start | bytes 1572872 | tf_op jit(solution)/shard_map/ppermute | solution.py:210
  128.2 1.4 collective-permute-start.30
  129.6 12.2 %collective-permute-done.30.near_high = bf16[48,2048]{1,0:T(8,128)(2,1)S(1)} collective-permute-done((bf16[48,2048]{1,0:T(8,128)(2,1)S(1)}, bf16[48,2048]{1,0:T(8,128)(2,1)S(1)}, u32[]{:S(2)}, u32[]{:S(2)}) %collective-permute-start.30) | collective-permute-done | bytes 196640 | tf_op jit(solution)/shard_map/ppermute | solution.py:210
  141.8 1.1 shard_map.84
  (43 shorter events, 0.6 us)
Async XLA Ops:
  0.6 0.7 copy-start.7
  1.3 0.7 copy-start.8
  15.6 18.5 %collective-permute-start.3 = (bf16[128,2048]{1,0:T(8,128)(2,1)}, bf16[128,2048]{1,0:T(8,128)(2,1)S(1)}, u32[]{:S(2)}, u32[]{:S(2)}) collective-permute-start(bf16[128,2048]{1,0:T(8,128)(2,1)} %refs_0_), channel_id=1, source_target_pairs={{0,1},{1,0},{2,3},{3,2},{4,5},{5,4},{6,7},{7,6},{8,9},{9,8},{10,11... | collective-permute-start | bytes 1572872 | tf_op jit(solution)/shard_map/ppermute | solution.py:210
  15.6 18.5 %collective-permute-start.2 = (bf16[128,2048]{1,0:T(8,128)(2,1)}, bf16[128,2048]{1,0:T(8,128)(2,1)S(1)}, u32[]{:S(2)}, u32[]{:S(2)}) collective-permute-start(bf16[128,2048]{1,0:T(8,128)(2,1)} %refs_0_), channel_id=1, source_target_pairs={{0,2},{1,3},{2,0},{3,1},{4,6},{5,7},{6,4},{7,5},{8,10},{9,11},{10,... | collective-permute-start | bytes 1572872 | tf_op jit(solution)/shard_map/ppermute | solution.py:210
  16.2 19.9 %collective-permute-start = (bf16[128,2048]{1,0:T(8,128)(2,1)}, bf16[128,2048]{1,0:T(8,128)(2,1)S(1)}, u32[]{:S(2)}, u32[]{:S(2)}) collective-permute-start(bf16[128,2048]{1,0:T(8,128)(2,1)} %refs_0_), channel_id=1, source_target_pairs={{0,4},{1,5},{2,6},{3,7},{4,0},{5,1},{6,2},{7,3},{8,12},{9,13},{10,... | collective-permute-start | bytes 1572872 | tf_op jit(solution)/shard_map/ppermute | solution.py:210
  16.7 22.8 %copy-start.6 = (bf16[128,2048]{1,0:T(8,128)(2,1)S(1)}, bf16[128,2048]{1,0:T(8,128)(2,1)}, u32[]{:S(2)}) copy-start(bf16[128,2048]{1,0:T(8,128)(2,1)} %refs_0_) | copy-start | bytes 1572868
  17.9 16.3 %collective-permute-start.1 = (bf16[64,2048]{1,0:T(8,128)(2,1)S(1)}, bf16[64,2048]{1,0:T(8,128)(2,1)S(1)}, u32[]{:S(2)}, u32[]{:S(2)}) collective-permute-start(bf16[64,2048]{1,0:T(8,128)(2,1)S(1)} %get-tuple-element.117), channel_id=1, source_target_pairs={{0,8},{1,9},{2,10},{3,11},{4,12},{5,13},{6,14},{7,15},{8,0},{9,1},... | collective-permute-start | bytes 786440 | tf_op jit(solution)/shard_map/ppermute | solution.py:210
  18.6 1.9 %copy-start = (bf16[1,2048,768]{2,1,0:T(8,128)(2,1)S(1)}, bf16[1,2048,768]{2,1,0:T(8,128)(2,1)}, u32[]{:S(2)}) copy-start(bf16[1,2048,768]{2,1,0:T(8,128)(2,1)} %param.9) | copy-start | bytes 9437188
  20.5 1.9 %copy-start.2 = (bf16[1,2048,768]{2,1,0:T(8,128)(2,1)S(1)}, bf16[1,2048,768]{2,1,0:T(8,128)(2,1)}, u32[]{:S(2)}) copy-start(bf16[1,2048,768]{2,1,0:T(8,128)(2,1)} %param.10) | copy-start | bytes 9437188
  22.4 1.9 %copy-start.4 = (bf16[1,768,2048]{2,1,0:T(8,128)(2,1)S(1)}, bf16[1,768,2048]{2,1,0:T(8,128)(2,1)}, u32[]{:S(2)}) copy-start(bf16[1,768,2048]{2,1,0:T(8,128)(2,1)} %param.11) | copy-start | bytes 9437188
  24.3 15.3 %copy-start.1 = (bf16[1,2048,768]{2,1,0:T(8,128)(2,1)S(1)}, bf16[1,2048,768]{2,1,0:T(8,128)(2,1)}, u32[]{:S(2)}) copy-start(bf16[1,2048,768]{2,1,0:T(8,128)(2,1)} %param.9) | copy-start | bytes 9437188
  24.3 15.3 %copy-start.3 = (bf16[1,2048,768]{2,1,0:T(8,128)(2,1)S(1)}, bf16[1,2048,768]{2,1,0:T(8,128)(2,1)}, u32[]{:S(2)}) copy-start(bf16[1,2048,768]{2,1,0:T(8,128)(2,1)} %param.10) | copy-start | bytes 9437188
  24.3 15.3 %copy-start.5 = (bf16[1,768,2048]{2,1,0:T(8,128)(2,1)S(1)}, bf16[1,768,2048]{2,1,0:T(8,128)(2,1)}, u32[]{:S(2)}) copy-start(bf16[1,768,2048]{2,1,0:T(8,128)(2,1)} %param.11) | copy-start | bytes 9437188
  36.0 3.5 %collective-permute-start.7 = (bf16[128,2048]{1,0:T(8,128)(2,1)S(1)}, bf16[128,2048]{1,0:T(8,128)(2,1)S(1)}, u32[]{:S(2)}, u32[]{:S(2)}) collective-permute-start(bf16[128,2048]{1,0:T(8,128)(2,1)S(1)} %collective-permute-done.2.refs_1_), channel_id=1, source_target_pairs={{0,1},{1,0},{2,3},{3,2},{4,5},{5,4},{6,7},{7,6},{8,9},{9,8},{10,11... | collective-permute-start | bytes 1572872 | tf_op jit(solution)/shard_map/ppermute | solution.py:210
  36.0 16.5 %collective-permute-start.6 = (bf16[128,2048]{1,0:T(8,128)(2,1)S(1)}, bf16[128,2048]{1,0:T(8,128)(2,1)S(1)}, u32[]{:S(2)}, u32[]{:S(2)}) collective-permute-start(bf16[128,2048]{1,0:T(8,128)(2,1)S(1)} %collective-permute-done.refs_0_), channel_id=1, source_target_pairs={{0,1},{1,0},{2,3},{3,2},{4,5},{5,4},{6,7},{7,6},{8,9},{9,8},{10,11... | collective-permute-start | bytes 1572872 | tf_op jit(solution)/shard_map/ppermute | solution.py:210
  36.5 16.0 %collective-permute-start.5 = (bf16[128,2048]{1,0:T(8,128)(2,1)S(1)}, bf16[128,2048]{1,0:T(8,128)(2,1)S(1)}, u32[]{:S(2)}, u32[]{:S(2)}) collective-permute-start(bf16[128,2048]{1,0:T(8,128)(2,1)S(1)} %collective-permute-done.refs_0_), channel_id=1, source_target_pairs={{0,2},{1,3},{2,0},{3,1},{4,6},{5,7},{6,4},{7,5},{8,10},{9,11},{10,... | collective-permute-start | bytes 1572872 | tf_op jit(solution)/shard_map/ppermute | solution.py:210
  38.1 14.5 %collective-permute-start.4 = (bf16[64,2048]{1,0:T(8,128)(2,1)S(1)}, bf16[64,2048]{1,0:T(8,128)(2,1)S(1)}, u32[]{:S(2)}, u32[]{:S(2)}) collective-permute-start(bf16[64,2048]{1,0:T(8,128)(2,1)S(1)} %get-tuple-element.116), channel_id=1, source_target_pairs={{0,8},{1,9},{2,10},{3,11},{4,12},{5,13},{6,14},{7,15},{8,0},{9,1},... | collective-permute-start | bytes 786440 | tf_op jit(solution)/shard_map/ppermute | solution.py:210
  52.5 1.9 %collective-permute-start.11 = (bf16[128,2048]{1,0:T(8,128)(2,1)S(1)}, bf16[128,2048]{1,0:T(8,128)(2,1)S(1)}, u32[]{:S(2)}, u32[]{:S(2)}) collective-permute-start(bf16[128,2048]{1,0:T(8,128)(2,1)S(1)} %collective-permute-done.5.refs_1_), channel_id=1, source_target_pairs={{0,1},{1,0},{2,3},{3,2},{4,5},{5,4},{6,7},{7,6},{8,9},{9,8},{10,11... | collective-permute-start | bytes 1572872 | tf_op jit(solution)/shard_map/ppermute | solution.py:210
  52.6 7.5 %collective-permute-start.10 = (bf16[128,2048]{1,0:T(8,128)(2,1)S(1)}, bf16[128,2048]{1,0:T(8,128)(2,1)S(1)}, u32[]{:S(2)}, u32[]{:S(2)}) collective-permute-start(bf16[128,2048]{1,0:T(8,128)(2,1)S(1)} %constant_dynamic-update-slice_fusion.refs_0_), channel_id=1, source_target_pairs={{0,1},{1,0},{2,3},{3,2},{4,5},{5,4},{6,7},{7,6},{8,9},{9,8},{10,11... | collective-permute-start | bytes 1572872 | tf_op jit(solution)/shard_map/ppermute | solution.py:210
  53.2 13.9 %collective-permute-start.9 = (bf16[128,2048]{1,0:T(8,128)(2,1)S(1)}, bf16[128,2048]{1,0:T(8,128)(2,1)S(1)}, u32[]{:S(2)}, u32[]{:S(2)}) collective-permute-start(bf16[128,2048]{1,0:T(8,128)(2,1)S(1)} %constant_dynamic-update-slice_fusion.refs_0_), channel_id=1, source_target_pairs={{0,2},{1,3},{2,0},{3,1},{4,6},{5,7},{6,4},{7,5},{8,10},{9,11},{10,... | collective-permute-start | bytes 1572872 | tf_op jit(solution)/shard_map/ppermute | solution.py:210
  53.7 13.6 %collective-permute-start.8 = (bf16[128,2048]{1,0:T(8,128)(2,1)S(1)}, bf16[128,2048]{1,0:T(8,128)(2,1)S(1)}, u32[]{:S(2)}, u32[]{:S(2)}) collective-permute-start(bf16[128,2048]{1,0:T(8,128)(2,1)S(1)} %constant_dynamic-update-slice_fusion.refs_0_), channel_id=1, source_target_pairs={{0,4},{1,5},{2,6},{3,7},{4,0},{5,1},{6,2},{7,3},{8,12},{9,13},{10,... | collective-permute-start | bytes 1572872 | tf_op jit(solution)/shard_map/ppermute | solution.py:210
  59.9 7.4 %collective-permute-start.12 = (bf16[128,2048]{1,0:T(8,128)(2,1)S(1)}, bf16[128,2048]{1,0:T(8,128)(2,1)S(1)}, u32[]{:S(2)}, u32[]{:S(2)}) collective-permute-start(bf16[128,2048]{1,0:T(8,128)(2,1)S(1)} %get-tuple-element.74), channel_id=1, source_target_pairs={{0,1},{1,0},{2,3},{3,2},{4,5},{5,4},{6,7},{7,6},{8,9},{9,8},{10,11... | collective-permute-start | bytes 1572872 | tf_op jit(solution)/shard_map/ppermute | solution.py:210
  67.3 2.5 %collective-permute-start.17 = (bf16[128,2048]{1,0:T(8,128)(2,1)S(1)}, bf16[128,2048]{1,0:T(8,128)(2,1)S(1)}, u32[]{:S(2)}, u32[]{:S(2)}) collective-permute-start(bf16[128,2048]{1,0:T(8,128)(2,1)S(1)} %collective-permute-done.9.refs_1_), channel_id=1, source_target_pairs={{0,1},{1,0},{2,3},{3,2},{4,5},{5,4},{6,7},{7,6},{8,9},{9,8},{10,11... | collective-permute-start | bytes 1572872 | tf_op jit(solution)/shard_map/ppermute | solution.py:210
  67.4 14.4 %collective-permute-start.14 = (bf16[128,2048]{1,0:T(8,128)(2,1)S(1)}, bf16[128,2048]{1,0:T(8,128)(2,1)S(1)}, u32[]{:S(2)}, u32[]{:S(2)}) collective-permute-start(bf16[128,2048]{1,0:T(8,128)(2,1)S(1)} %add_convert_fusion.2), channel_id=1, source_target_pairs={{0,2},{1,3},{2,0},{3,1},{4,6},{5,7},{6,4},{7,5},{8,10},{9,11},{10,... | collective-permute-start | bytes 1572872 | tf_op jit(solution)/shard_map/ppermute | solution.py:210
  69.0 12.8 %collective-permute-start.16 = (bf16[128,2048]{1,0:T(8,128)(2,1)S(1)}, bf16[128,2048]{1,0:T(8,128)(2,1)S(1)}, u32[]{:S(2)}, u32[]{:S(2)}) collective-permute-start(bf16[128,2048]{1,0:T(8,128)(2,1)S(1)} %get-tuple-element.79), channel_id=1, source_target_pairs={{0,1},{1,0},{2,3},{3,2},{4,5},{5,4},{6,7},{7,6},{8,9},{9,8},{10,11... | collective-permute-start | bytes 1572872 | tf_op jit(solution)/shard_map/ppermute | solution.py:210
  69.2 12.6 %collective-permute-start.15 = (bf16[128,2048]{1,0:T(8,128)(2,1)S(1)}, bf16[128,2048]{1,0:T(8,128)(2,1)S(1)}, u32[]{:S(2)}, u32[]{:S(2)}) collective-permute-start(bf16[128,2048]{1,0:T(8,128)(2,1)S(1)} %collective-permute-done.8.refs_0_), channel_id=1, source_target_pairs={{0,1},{1,0},{2,3},{3,2},{4,5},{5,4},{6,7},{7,6},{8,9},{9,8},{10,11... | collective-permute-start | bytes 1572872 | tf_op jit(solution)/shard_map/ppermute | solution.py:210
  69.5 14.1 %collective-permute-start.13 = (bf16[128,2048]{1,0:T(8,128)(2,1)S(1)}, bf16[128,2048]{1,0:T(8,128)(2,1)S(1)}, u32[]{:S(2)}, u32[]{:S(2)}) collective-permute-start(bf16[128,2048]{1,0:T(8,128)(2,1)S(1)} %collective-permute-done.9.refs_1_), channel_id=1, source_target_pairs={{0,4},{1,5},{2,6},{3,7},{4,0},{5,1},{6,2},{7,3},{8,12},{9,13},{10,... | collective-permute-start | bytes 1572872 | tf_op jit(solution)/shard_map/ppermute | solution.py:210
  83.6 2.7 %collective-permute-start.19 = (bf16[256,2048]{1,0:T(8,128)(2,1)S(1)}, bf16[256,2048]{1,0:T(8,128)(2,1)S(1)}, u32[]{:S(2)}, u32[]{:S(2)}) collective-permute-start(bf16[256,2048]{1,0:T(8,128)(2,1)S(1)} %get-tuple-element.89), channel_id=1, source_target_pairs={{0,1},{1,0},{2,3},{3,2},{4,5},{5,4},{6,7},{7,6},{8,9},{9,8},{10,11... | collective-permute-start | bytes 3145736 | tf_op jit(solution)/shard_map/ppermute | solution.py:210
  83.6 3.4 %collective-permute-start.18 = (bf16[128,2048]{1,0:T(8,128)(2,1)S(1)}, bf16[128,2048]{1,0:T(8,128)(2,1)S(1)}, u32[]{:S(2)}, u32[]{:S(2)}) collective-permute-start(bf16[128,2048]{1,0:T(8,128)(2,1)S(1)} %collective-permute-done.13.refs_1_), channel_id=1, source_target_pairs={{0,1},{1,0},{2,3},{3,2},{4,5},{5,4},{6,7},{7,6},{8,9},{9,8},{10,11... | collective-permute-start | bytes 1572872 | tf_op jit(solution)/shard_map/ppermute | solution.py:210
  84.4 9.7 %collective-permute-start.20 = (bf16[80,2048]{1,0:T(8,128)(2,1)S(1)}, bf16[80,2048]{1,0:T(8,128)(2,1)S(1)}, u32[]{:S(2)}, u32[]{:S(2)}) collective-permute-start(bf16[80,2048]{1,0:T(8,128)(2,1)S(1)} %slice.88), channel_id=1, source_target_pairs={{0,4},{1,5},{2,6},{3,7},{4,0},{5,1},{6,2},{7,3},{8,12},{9,13},{10,... | collective-permute-start | bytes 983048 | tf_op jit(solution)/shard_map/ppermute | solution.py:210
  86.3 7.8 %collective-permute-start.21 = (bf16[48,2048]{1,0:T(8,128)(2,1)S(1)}, bf16[48,2048]{1,0:T(8,128)(2,1)S(1)}, u32[]{:S(2)}, u32[]{:S(2)}) collective-permute-start(bf16[48,2048]{1,0:T(8,128)(2,1)S(1)} %add_convert_fusion.9), channel_id=1, source_target_pairs={{0,2},{1,3},{2,0},{3,1},{4,6},{5,7},{6,4},{7,5},{8,10},{9,11},{10,... | collective-permute-start | bytes 589832 | tf_op jit(solution)/shard_map/ppermute | solution.py:210
  94.1 2.7 %collective-permute-start.22 = (bf16[256,2048]{1,0:T(8,128)(2,1)S(1)}, bf16[256,2048]{1,0:T(8,128)(2,1)S(1)}, u32[]{:S(2)}, u32[]{:S(2)}) collective-permute-start(bf16[256,2048]{1,0:T(8,128)(2,1)S(1)} %get-tuple-element.94), channel_id=1, source_target_pairs={{0,1},{1,0},{2,3},{3,2},{4,5},{5,4},{6,7},{7,6},{8,9},{9,8},{10,11... | collective-permute-start | bytes 3145736 | tf_op jit(solution)/shard_map/ppermute | solution.py:210
  94.1 4.2 %collective-permute-start.25 = (bf16[256,2048]{1,0:T(8,128)(2,1)S(1)}, bf16[256,2048]{1,0:T(8,128)(2,1)S(1)}, u32[]{:S(2)}, u32[]{:S(2)}) collective-permute-start(bf16[256,2048]{1,0:T(8,128)(2,1)S(1)} %get-tuple-element.96), channel_id=1, source_target_pairs={{0,1},{1,0},{2,3},{3,2},{4,5},{5,4},{6,7},{7,6},{8,9},{9,8},{10,11... | collective-permute-start | bytes 3145736 | tf_op jit(solution)/shard_map/ppermute | solution.py:210
  96.8 7.0 %collective-permute-start.24 = (bf16[48,2048]{1,0:T(8,128)(2,1)S(1)}, bf16[48,2048]{1,0:T(8,128)(2,1)S(1)}, u32[]{:S(2)}, u32[]{:S(2)}) collective-permute-start(bf16[48,2048]{1,0:T(8,128)(2,1)S(1)} %add_convert_fusion.8), channel_id=1, source_target_pairs={{0,2},{1,3},{2,0},{3,1},{4,6},{5,7},{6,4},{7,5},{8,10},{9,11},{10,... | collective-permute-start | bytes 589832 | tf_op jit(solution)/shard_map/ppermute | solution.py:210
  97.5 9.5 %collective-permute-start.23 = (bf16[80,2048]{1,0:T(8,128)(2,1)S(1)}, bf16[80,2048]{1,0:T(8,128)(2,1)S(1)}, u32[]{:S(2)}, u32[]{:S(2)}) collective-permute-start(bf16[80,2048]{1,0:T(8,128)(2,1)S(1)} %get-tuple-element.115), channel_id=1, source_target_pairs={{0,4},{1,5},{2,6},{3,7},{4,0},{5,1},{6,2},{7,3},{8,12},{9,13},{10,... | collective-permute-start | bytes 983048 | tf_op jit(solution)/shard_map/ppermute | solution.py:210
  107.2 19.1 %collective-permute-start.26 = (bf16[96,2048]{1,0:T(8,128)(2,1)S(1)}, bf16[96,2048]{1,0:T(8,128)(2,1)S(1)}, u32[]{:S(2)}, u32[]{:S(2)}) collective-permute-start(bf16[96,2048]{1,0:T(8,128)(2,1)S(1)} %shard_map.83), channel_id=1, source_target_pairs={{0,8},{1,9},{2,10},{3,11},{4,12},{5,13},{6,14},{7,15},{8,0},{9,1},... | collective-permute-start | bytes 1179656 | tf_op jit(solution)/shard_map/ppermute | solution.py:210
  107.8 8.4 %collective-permute-start.28 = (bf16[80,2048]{1,0:T(8,128)(2,1)S(1)}, bf16[80,2048]{1,0:T(8,128)(2,1)S(1)}, u32[]{:S(2)}, u32[]{:S(2)}) collective-permute-start(bf16[80,2048]{1,0:T(8,128)(2,1)S(1)} %add_convert_fusion.4), channel_id=1, source_target_pairs={{0,2},{1,3},{2,0},{3,1},{4,6},{5,7},{6,4},{7,5},{8,10},{9,11},{10,... | collective-permute-start | bytes 983048 | tf_op jit(solution)/shard_map/ppermute | solution.py:210
  109.0 13.3 %collective-permute-start.27 = (bf16[80,2048]{1,0:T(8,128)(2,1)S(1)}, bf16[80,2048]{1,0:T(8,128)(2,1)S(1)}, u32[]{:S(2)}, u32[]{:S(2)}) collective-permute-start(bf16[80,2048]{1,0:T(8,128)(2,1)S(1)} %get-tuple-element.100), channel_id=1, source_target_pairs={{0,4},{1,5},{2,6},{3,7},{4,0},{5,1},{6,2},{7,3},{8,12},{9,13},{10,... | collective-permute-start | bytes 983048 | tf_op jit(solution)/shard_map/ppermute | solution.py:210
  126.5 15.3 %collective-permute-start.31 = (bf16[80,2048]{1,0:T(8,128)(2,1)S(1)}, bf16[80,2048]{1,0:T(8,128)(2,1)S(1)}, u32[]{:S(2)}, u32[]{:S(2)}) collective-permute-start(bf16[80,2048]{1,0:T(8,128)(2,1)S(1)} %add_convert_fusion.3), channel_id=1, source_target_pairs={{0,8},{1,9},{2,10},{3,11},{4,12},{5,13},{6,14},{7,15},{8,0},{9,1},... | collective-permute-start | bytes 983048 | tf_op jit(solution)/shard_map/ppermute | solution.py:210
  126.6 15.2 %collective-permute-start.29 = (bf16[128,2048]{1,0:T(8,128)(2,1)S(1)}, bf16[128,2048]{1,0:T(8,128)(2,1)S(1)}, u32[]{:S(2)}, u32[]{:S(2)}) collective-permute-start(bf16[128,2048]{1,0:T(8,128)(2,1)S(1)} %add_convert_fusion), channel_id=1, source_target_pairs={{0,2},{1,3},{2,0},{3,1},{4,6},{5,7},{6,4},{7,5},{8,10},{9,11},{10,... | collective-permute-start | bytes 1572872 | tf_op jit(solution)/shard_map/ppermute | solution.py:210
  128.2 13.6 %collective-permute-start.30 = (bf16[48,2048]{1,0:T(8,128)(2,1)S(1)}, bf16[48,2048]{1,0:T(8,128)(2,1)S(1)}, u32[]{:S(2)}, u32[]{:S(2)}) collective-permute-start(bf16[48,2048]{1,0:T(8,128)(2,1)S(1)} %add_convert_fusion.7), channel_id=1, source_target_pairs={{0,4},{1,5},{2,6},{3,7},{4,0},{5,1},{6,2},{7,3},{8,12},{9,13},{10,... | collective-permute-start | bytes 589832 | tf_op jit(solution)/shard_map/ppermute | solution.py:210

commit v16 on v15

--- a/solution.py
+++ b/solution.py
@@ -154,35 +154,15 @@
     )(tables, *xs, w_gate, w_up, w_down)
 
 
-def high_kernel(keep3, got3, high3, keep2, got2, high2, both):
-    tok, least = keep3.shape[0] // 2, high3.shape[0]
-    for i, parts in enumerate(((keep3, got3, high3), (keep2, got2, high2))):
-        keep, got = (part[tok - least : tok, :].astype(jnp.float32) for part in parts[:2])
-        total = keep + got + parts[2][...].astype(jnp.float32)
-        both[i * least : (i + 1) * least, :] = total.astype(both.dtype)
-
-
-def high_pass(*parts):
-    least, features = parts[2].shape
-    vmem = pl.BlockSpec(memory_space=pltpu.VMEM)
-    return pl.pallas_call(
-        high_kernel,
-        out_shape=jax.ShapeDtypeStruct((2 * least, features), parts[2].dtype),
-        in_specs=[vmem] * len(parts),
-        out_specs=vmem,
-        compiler_params=pltpu.CompilerParams(vmem_limit_bytes=12 * 1024 * 1024),
-    )(*parts)
-
-
 def mix_kernel(keep, got, side, near_low, near_high, far_low, far_high, mixed):
     most, tok = near_low.shape[0], mixed.shape[0]
     for start, stop, near, far in (
-        (0, most, near_low, far_low[...]),
-        (most, tok, near_high, far_high[tok - most :, :]),
+        (0, most, near_low, far_low),
+        (most, tok, near_high, far_high),
     ):
         total = keep[start:stop, :].astype(jnp.float32) + got[start:stop, :].astype(jnp.float32)
         total = total + side[start:stop, :].astype(jnp.float32) + near[...].astype(jnp.float32)
-        mixed[start:stop, :] = (total + far.astype(jnp.float32)).astype(mixed.dtype)
+        mixed[start:stop, :] = (total + far[...].astype(jnp.float32)).astype(mixed.dtype)
 
 
 def mix_pass(*parts):
@@ -229,17 +209,20 @@
     def expert(k, *xs, pieces=None):
         return plane_pass(k, tables, xs, w_gate, w_up, w_down, slots, pieces)
 
-    a0, weight = together(tokens, table_pass(routes, probs, size))
+    weight = table_pass(routes, probs, size)
+    a0 = tokens
+    a1, low, b0, c0, weight = together(
+        pair(a0), far(a0[:half]), column(a0), sibling(a0), weight
+    )
     tables = ranks_pass(capacity, spots, weight, w_gate, w_up, w_down)
-    a1, low, b0, c0, tables = together(
-        pair(a0), far(a0[:half]), column(a0), sibling(a0), tables
-    )
     high = far(a0[half:])
     b1 = column(a1)
     d0 = sibling(b0)
     c1 = sibling(a1)
     keep0, give0, act0 = expert(0, a0, b0, c0, d0)
-    high, b1, c1, keep0, give0, act0 = together(high, b1, c1, keep0, give0, act0)
+    high, b1, c1, keep0, give0, act0, tables = together(
+        high, b1, c1, keep0, give0, act0, tables
+    )
     a2 = jnp.concatenate([low, high], axis=0)
     a3 = pair(a2)
     b2 = column(a2)
@@ -259,38 +242,37 @@
     b3, came1, c3, got1, keep2, give2, act2 = together(b3, came1, c3, got1, keep2, give2, act2)
     d3 = sibling(b3)
     near1 = summed(keep1[:tok], got1, came1)
-    most = 5 * tok // 8
-    least = tok - most
 
     def own(keep, got, start, stop, *more):
         return summed(keep[start:stop], got[start:stop], *more)
 
-    near1_low = pair(near1[:most])
+    near1_low = pair(near1[:half])
     got2 = sibling(give2)
-    side_high = column(own(keep2, got2, tok + most, 2 * tok))
+    side_high = column(own(keep2, got2, tok + half, 2 * tok))
     keep3, give3, act3 = expert(3, a3, b3, c3, d3)
     keep3, give3, act3, got2, near1, near1_low, side_high = together(
         keep3, give3, act3, got2, near1, near1_low, side_high
     )
+    far2_high = far(own(keep2, got2, half, tok, side_high))
     got0 = sibling(give0)
     got3 = sibling(give3)
-    low = pair(own(keep3, got3, tok, tok + most))
-    high = column(own(keep3, got3, tok + most, 2 * tok))
-    sum3 = own(keep3, got3, 0, most)
+    low = pair(own(keep3, got3, tok, tok + half))
+    high = column(own(keep3, got3, tok + half, 2 * tok))
+    sum3 = own(keep3, got3, 0, half)
     side0 = own(keep0, got0, tok, 2 * tok)
-    low, high, sum3, side0 = together(low, high, sum3, side0)
-    far_high = far(high_pass(keep3, got3, high, keep2, got2, side_high))
+    low, high, far2_high, sum3, side0 = together(low, high, far2_high, sum3, side0)
+    far3_high = far(own(keep3, got3, half, tok, high))
     pair3_low = pair(sum3)
-    side_low = column(own(keep2, got2, tok, tok + most, low))
+    side_low = column(own(keep2, got2, tok, tok + half, low))
     gram = gram_of(jnp.concatenate([act0, act1, act2, act3], axis=0)) * tables[8, 0]
-    far_high, pair3_low, side_low, side0, gram = together(
-        far_high, pair3_low, side_low, side0, gram
-    )
-    far2_low = far(own(keep2, got2, 0, most, pair3_low, side_low))
-    near1_high = pair(summed(near1[most:], far_high[:least]))
+    far3_high, pair3_low, side_low, side0, gram = together(
+        far3_high, pair3_low, side_low, side0, gram
+    )
+    far2_low = far(own(keep2, got2, 0, half, pair3_low, side_low))
+    near1_high = pair(summed(near1[half:], far3_high))
     last0 = column(side0)
     mixed = mix_pass(
-        keep0, got0, last0, near1_low, near1_high, far2_low, far_high
+        keep0, got0, last0, near1_low, near1_high, far2_low, far2_high
     )
 
     return gram[None], mixed

time: 143 us -> 134 us (0.937)
  waiting for transfers between devices: 73.1 us -> 44 us
  starting transfers between devices: 17.6 us -> 31.5 us
  local copies, waits for them, and re-layouts: 8.83 us -> 13.5 us
    ppermute x32 -> x33, waiting for transfers between devices: 73.1 us -> 44 us  [swapped(): return lax.ppermute(array, 'expert', [(i, i ^ bit) for i in range(size)])]
    ppermute x32 -> x33, starting transfers between devices: 17.6 us -> 31.5 us  [swapped(): return lax.ppermute(array, 'expert', [(i, i ^ bit) for i in range(size)])]
    unnamed x19, local copies, waits for them, and re-layouts: 7.06 us -> 10 us
  transfers between devices with their start and end apart: 32 -> 33, of which waited for: 19 -> 11; matrix products, arithmetic and copies ran while one was open for 5% -> 6% of each run, Pallas kernels for 16% -> 18%
where the time goes in v16:
time: 134 us
  waiting for transfers between devices  44 us (33%)
  starting transfers between devices  31.5 us (24%)
  Pallas kernels  25 us (19%)
  blocking collectives  13.6 us (10%)
  local copies, waits for them, and re-layouts  13.5 us (10%)
  matrix products  3.8 us (3%)
    ppermute x33, waiting for transfers between devices, swapped(): return lax.ppermute(array, 'expert', [(i, i ^ bit) for i in range(size)])  44 us
    ppermute x33, starting transfers between devices, swapped(): return lax.ppermute(array, 'expert', [(i, i ^ bit) for i in range(size)])  31.5 us
    pallas_call x4, Pallas kernels, plane_pass(): pl.pallas_call(functools.partial(plane_kernel, k, len(pieces)), out_shape...  23.1 us
    all_to_all x1, blocking collectives, table_pass(): lax.all_to_all(mine, 'expert', split_axis=0, concat_axis=0, tiled=True)  13.6 us
    unnamed x19, local copies, waits for them, and re-layouts  10 us
    dot_general x1, matrix products, gram_of(): lax.dot_general(rows, rows, (((0,), (0,)), ((), ())), preferred_element_t...  3.8 us
  transfers between devices with their start and end apart: 33, of which 11 were waited for; matrix products, arithmetic and copies ran while one was open for 6% of the time, Pallas kernels for 18%

profile of v16, /device:TPU:0, one launch (start us, length us, event | category | flops | bytes accessed | tf_op | source)
XLA Modules:
  0.0 133.6 jit_solution(5141618740427666914)
XLA Ops:
  0.6 3.1 %collective-permute-start.1 = (bf16[128,2048]{1,0:T(8,128)(2,1)}, bf16[128,2048]{1,0:T(8,128)(2,1)S(1)}, u32[]{:S(2)}, u32[]{:S(2)}) collective-permute-start(bf16[128,2048]{1,0:T(8,128)(2,1)} %refs_0_.1), channel_id=1, source_target_pairs={{0,4},{1,5},{2,6},{3,7},{4,0},{5,1},{6,2},{7,3},{8,12},{9,13},{10,... | collective-permute-start | bytes 1572872 | tf_op jit(solution)/shard_map/ppermute | solution.py:190
  3.7 1.5 %collective-permute-start.3 = (bf16[128,2048]{1,0:T(8,128)(2,1)}, bf16[128,2048]{1,0:T(8,128)(2,1)S(1)}, u32[]{:S(2)}, u32[]{:S(2)}) collective-permute-start(bf16[128,2048]{1,0:T(8,128)(2,1)} %refs_0_.1), channel_id=1, source_target_pairs={{0,2},{1,3},{2,0},{3,1},{4,6},{5,7},{6,4},{7,5},{8,10},{9,11},{10,... | collective-permute-start | bytes 1572872 | tf_op jit(solution)/shard_map/ppermute | solution.py:190
  5.2 1.8 %fusion.11 = (bf16[64,2048]{1,0:T(8,128)(2,1)S(1)}, bf16[64,2048]{1,0:T(8,128)(2,1)}) fusion(bf16[128,2048]{1,0:T(8,128)(2,1)} %refs_0_.1), kind=kLoop, calls=%fused_computation.24 | loop fusion | bytes 1048576 | tf_op jit(solution)/shard_map/slice | solution.py:215
  7.1 2.6 %collective-permute-start.2 = (bf16[64,2048]{1,0:T(8,128)(2,1)S(1)}, bf16[64,2048]{1,0:T(8,128)(2,1)S(1)}, u32[]{:S(2)}, u32[]{:S(2)}) collective-permute-start(bf16[64,2048]{1,0:T(8,128)(2,1)S(1)} %get-tuple-element.117), channel_id=1, source_target_pairs={{0,8},{1,9},{2,10},{3,11},{4,12},{5,13},{6,14},{7,15},{8,0},{9,1},... | collective-permute-start | bytes 786440 | tf_op jit(solution)/shard_map/ppermute | solution.py:190
  9.7 0.7 copy-done.7
  10.4 0.7 copy-done.8
  11.1 13.6 %all_to_all.12 = f32[16,1,128]{2,1,0:T(1,128)S(1)} all-to-all(f32[16,1,128]{2,1,0:T(1,128)S(1)} %bitcast.42), channel_id=1, replica_groups=mesh['parts'=2,'expert'=16] {'expert'}, dimensions={0} | all-to-all | bytes 16384 | tf_op jit(solution)/shard_map/all_to_all | solution.py:48
  24.8 0.5 collective-permute-start.6
  25.3 0.5 collective-permute-start.5
  25.8 0.6 collective-permute-start
  26.5 1.9 %copy-done = bf16[1,2048,768]{2,1,0:T(8,128)(2,1)S(1)} copy-done((bf16[1,2048,768]{2,1,0:T(8,128)(2,1)S(1)}, bf16[1,2048,768]{2,1,0:T(8,128)(2,1)}, u32[]{:S(2)}) %copy-start) | copy-done | bytes 3145752
  28.4 1.9 %copy-done.2 = bf16[1,2048,768]{2,1,0:T(8,128)(2,1)S(1)} copy-done((bf16[1,2048,768]{2,1,0:T(8,128)(2,1)S(1)}, bf16[1,2048,768]{2,1,0:T(8,128)(2,1)}, u32[]{:S(2)}) %copy-start.2) | copy-done | bytes 3145752
  30.3 1.9 %copy-done.4 = bf16[1,768,2048]{2,1,0:T(8,128)(2,1)S(1)} copy-done((bf16[1,768,2048]{2,1,0:T(8,128)(2,1)S(1)}, bf16[1,768,2048]{2,1,0:T(8,128)(2,1)}, u32[]{:S(2)}) %copy-start.4) | copy-done | bytes 3145752
  32.2 0.7 shard_map.78.tables
  33.0 1.1 copy-done.1
  34.1 1.0 copy-done.3
  35.0 0.9 copy-done.5
  35.9 6.5 %shard_map.79 = (bf16[256,2048]{1,0:T(8,128)(2,1)S(1)}, bf16[256,2048]{1,0:T(8,128)(2,1)S(1)}, bf16[320,768]{1,0:T(8,128)(2,1)S(1)}) custom-call(f32[16,512]{1,0:T(8,128)S(1)} %shard_map.78.tables, bf16[128,2048]{1,0:T(8,128)(2,1)S(1)} %copy-done.6, bf16[128,2048]{1,0:T(8,128)(2,1)S(1)} %collective-permute-done.3.refs_1_, ...), custom_call_target="tpu_custom_call" | custom-call | flops 4362076160 | bytes 13631488 | tf_op jit(solution)/shard_map/pallas_call | solution.py:144
  42.6 1.0 constant_dynamic-update-slice_fusion.refs_0_
  43.6 0.6 collective-permute-start.10
  44.1 1.5 %collective-permute-start.9 = (bf16[128,2048]{1,0:T(8,128)(2,1)S(1)}, bf16[128,2048]{1,0:T(8,128)(2,1)S(1)}, u32[]{:S(2)}, u32[]{:S(2)}) collective-permute-start(bf16[128,2048]{1,0:T(8,128)(2,1)S(1)} %constant_dynamic-update-slice_fusion.refs_0_), channel_id=1, source_target_pairs={{0,2},{1,3},{2,0},{3,1},{4,6},{5,7},{6,4},{7,5},{8,10},{9,11},{10,... | collective-permute-start | bytes 1572872 | tf_op jit(solution)/shard_map/ppermute | solution.py:190
  45.6 1.6 %collective-permute-start.8 = (bf16[128,2048]{1,0:T(8,128)(2,1)S(1)}, bf16[128,2048]{1,0:T(8,128)(2,1)S(1)}, u32[]{:S(2)}, u32[]{:S(2)}) collective-permute-start(bf16[128,2048]{1,0:T(8,128)(2,1)S(1)} %constant_dynamic-update-slice_fusion.refs_0_), channel_id=1, source_target_pairs={{0,4},{1,5},{2,6},{3,7},{4,0},{5,1},{6,2},{7,3},{8,12},{9,13},{10,... | collective-permute-start | bytes 1572872 | tf_op jit(solution)/shard_map/ppermute | solution.py:190
  47.2 5.5 %shard_map.80 = (bf16[256,2048]{1,0:T(8,128)(2,1)S(1)}, bf16[128,2048]{1,0:T(8,128)(2,1)S(1)}, bf16[128,2048]{1,0:T(8,128)(2,1)S(1)}, bf16[320,768]{1,0:T(8,128)(2,1)S(1)}) custom-call(f32[16,512]{1,0:T(8,128)S(1)} %shard_map.78.tables, bf16[128,2048]{1,0:T(8,128)(2,1)S(1)} %collective-permute-done.1.refs_0_, ...), custom_call_target="tpu_custom_call" | custom-call | flops 4362076160 | bytes 13631488 | tf_op jit(solution)/shard_map/pallas_call | solution.py:144
  52.8 5.3 %collective-permute-done.9.refs_1_ = bf16[128,2048]{1,0:T(8,128)(2,1)S(1)} collective-permute-done((bf16[128,2048]{1,0:T(8,128)(2,1)S(1)}, bf16[128,2048]{1,0:T(8,128)(2,1)S(1)}, u32[]{:S(2)}, u32[]{:S(2)}) %collective-permute-start.9) | collective-permute-done | bytes 524320 | tf_op jit(solution)/shard_map/ppermute | solution.py:190
  58.0 1.2 collective-permute-done.8.refs_0_
  59.2 0.1 add_convert_fusion.2
  59.3 0.6 collective-permute-start.14
  60.0 0.2 collective-permute-start.16
  60.2 0.3 collective-permute-start.15
  60.5 1.7 %collective-permute-start.13 = (bf16[128,2048]{1,0:T(8,128)(2,1)S(1)}, bf16[128,2048]{1,0:T(8,128)(2,1)S(1)}, u32[]{:S(2)}, u32[]{:S(2)}) collective-permute-start(bf16[128,2048]{1,0:T(8,128)(2,1)S(1)} %collective-permute-done.9.refs_1_), channel_id=1, source_target_pairs={{0,4},{1,5},{2,6},{3,7},{4,0},{5,1},{6,2},{7,3},{8,12},{9,13},{10,... | collective-permute-start | bytes 1572872 | tf_op jit(solution)/shard_map/ppermute | solution.py:190
  62.2 5.7 %shard_map.81 = (bf16[256,2048]{1,0:T(8,128)(2,1)S(1)}, bf16[256,2048]{1,0:T(8,128)(2,1)S(1)}, bf16[320,768]{1,0:T(8,128)(2,1)S(1)}) custom-call(f32[16,512]{1,0:T(8,128)S(1)} %shard_map.78.tables, bf16[128,2048]{1,0:T(8,128)(2,1)S(1)} %constant_dynamic-update-slice_fusion.refs_0_, bf16[128,2048]{1,0:T(8,128)(2,1)S(1)} %collective-permute-done.9.refs_1_, ...), custom_call_target="tpu_custom_call" | custom-call | flops 4362076160 | bytes 13631488 | tf_op jit(solution)/shard_map/pallas_call | solution.py:144
  67.9 5.9 %collective-permute-done.14 = bf16[128,2048]{1,0:T(8,128)(2,1)S(1)} collective-permute-done((bf16[128,2048]{1,0:T(8,128)(2,1)S(1)}, bf16[128,2048]{1,0:T(8,128)(2,1)S(1)}, u32[]{:S(2)}, u32[]{:S(2)}) %collective-permute-start.14) | collective-permute-done | bytes 524320 | tf_op jit(solution)/shard_map/ppermute | solution.py:190
  73.8 0.8 collective-permute-done.13.refs_1_
  74.5 0.5 collective-permute-start.18
  75.1 0.2 add_convert_fusion.1
  75.3 1.8 %collective-permute-start.20 = (bf16[64,2048]{1,0:T(8,128)(2,1)S(1)}, bf16[64,2048]{1,0:T(8,128)(2,1)S(1)}, u32[]{:S(2)}, u32[]{:S(2)}) collective-permute-start(bf16[64,2048]{1,0:T(8,128)(2,1)S(1)} %slice.100), channel_id=1, source_target_pairs={{0,4},{1,5},{2,6},{3,7},{4,0},{5,1},{6,2},{7,3},{8,12},{9,13},{10,... | collective-permute-start | bytes 786440 | tf_op jit(solution)/shard_map/ppermute | solution.py:190
  77.1 0.1 collective-permute-done.19
  77.3 1.5 %collective-permute-start.21 = (bf16[64,2048]{1,0:T(8,128)(2,1)S(1)}, bf16[64,2048]{1,0:T(8,128)(2,1)S(1)}, u32[]{:S(2)}, u32[]{:S(2)}) collective-permute-start(bf16[64,2048]{1,0:T(8,128)(2,1)S(1)} %add_convert_fusion.11), channel_id=1, source_target_pairs={{0,2},{1,3},{2,0},{3,1},{4,6},{5,7},{6,4},{7,5},{8,10},{9,11},{10,... | collective-permute-start | bytes 786440 | tf_op jit(solution)/shard_map/ppermute | solution.py:190
  78.8 5.5 %shard_map.82 = (bf16[256,2048]{1,0:T(8,128)(2,1)S(1)}, bf16[256,2048]{1,0:T(8,128)(2,1)S(1)}, bf16[320,768]{1,0:T(8,128)(2,1)S(1)}) custom-call(f32[16,512]{1,0:T(8,128)S(1)} %shard_map.78.tables, bf16[128,2048]{1,0:T(8,128)(2,1)S(1)} %collective-permute-done.8.refs_0_, bf16[128,2048]{1,0:T(8,128)(2,1)S(1)} %collective-permute-done.13.refs_1_, ...), custom_call_target="tpu_custom_call" | custom-call | flops 4362076160 | bytes 13631488 | tf_op jit(solution)/shard_map/pallas_call | solution.py:144
  84.3 1.4 %collective-permute-done.21 = bf16[64,2048]{1,0:T(8,128)(2,1)S(1)} collective-permute-done((bf16[64,2048]{1,0:T(8,128)(2,1)S(1)}, bf16[64,2048]{1,0:T(8,128)(2,1)S(1)}, u32[]{:S(2)}, u32[]{:S(2)}) %collective-permute-start.21) | collective-permute-done | bytes 262176 | tf_op jit(solution)/shard_map/ppermute | solution.py:190
  85.7 0.5 collective-permute-start.26
  86.2 0.5 slice.96
  86.7 0.1 add_convert_fusion.8
  86.8 2.4 %collective-permute-start.25 = (bf16[64,2048]{1,0:T(8,128)(2,1)S(1)}, bf16[64,2048]{1,0:T(8,128)(2,1)S(1)}, u32[]{:S(2)}, u32[]{:S(2)}) collective-permute-start(bf16[64,2048]{1,0:T(8,128)(2,1)S(1)} %add_convert_fusion.8), channel_id=1, source_target_pairs={{0,8},{1,9},{2,10},{3,11},{4,12},{5,13},{6,14},{7,15},{8,0},{9,1},... | collective-permute-start | bytes 786440 | tf_op jit(solution)/shard_map/ppermute | solution.py:190
  89.2 0.3 add_convert_fusion.7
  89.5 1.6 %collective-permute-start.24 = (bf16[64,2048]{1,0:T(8,128)(2,1)S(1)}, bf16[64,2048]{1,0:T(8,128)(2,1)S(1)}, u32[]{:S(2)}, u32[]{:S(2)}) collective-permute-start(bf16[64,2048]{1,0:T(8,128)(2,1)S(1)} %get-tuple-element.115), channel_id=1, source_target_pairs={{0,2},{1,3},{2,0},{3,1},{4,6},{5,7},{6,4},{7,5},{8,10},{9,11},{10,... | collective-permute-start | bytes 786440 | tf_op jit(solution)/shard_map/ppermute | solution.py:190
  91.1 0.7 collective-permute-start.23
  91.8 0.1 add_convert_fusion
  91.9 9.8 %collective-permute-done.25.far_high = bf16[64,2048]{1,0:T(8,128)(2,1)S(1)} collective-permute-done((bf16[64,2048]{1,0:T(8,128)(2,1)S(1)}, bf16[64,2048]{1,0:T(8,128)(2,1)S(1)}, u32[]{:S(2)}, u32[]{:S(2)}) %collective-permute-start.25) | collective-permute-done | bytes 262176 | tf_op jit(solution)/shard_map/ppermute | solution.py:190
  101.7 1.4 %collective-permute-done.23 = bf16[64,2048]{1,0:T(8,128)(2,1)S(1)} collective-permute-done((bf16[64,2048]{1,0:T(8,128)(2,1)S(1)}, bf16[64,2048]{1,0:T(8,128)(2,1)S(1)}, u32[]{:S(2)}, u32[]{:S(2)}) %collective-permute-start.23) | collective-permute-done | bytes 262176 | tf_op jit(solution)/shard_map/ppermute | solution.py:190
  103.1 0.1 add_convert_fusion.5
  103.2 0.6 collective-permute-start.29
  103.9 0.1 add_convert_fusion.6
  104.0 1.1 collective-permute-start.27
  105.1 1.6 %collective-permute-start.28 = (bf16[64,2048]{1,0:T(8,128)(2,1)S(1)}, bf16[64,2048]{1,0:T(8,128)(2,1)S(1)}, u32[]{:S(2)}, u32[]{:S(2)}) collective-permute-start(bf16[64,2048]{1,0:T(8,128)(2,1)S(1)} %get-tuple-element.99), channel_id=1, source_target_pairs={{0,4},{1,5},{2,6},{3,7},{4,0},{5,1},{6,2},{7,3},{8,12},{9,13},{10,... | collective-permute-start | bytes 786440 | tf_op jit(solution)/shard_map/ppermute | solution.py:190
  106.7 3.8 %broadcast_multiply_fusion = f32[768,768]{1,0:T(8,128)} fusion(f32[]{:T(128)} %bitcast.24, bf16[320,768]{1,0:T(8,128)(2,1)S(1)} %get-tuple-element.105, bf16[320,768]{1,0:T(8,128)(2,1)S(1)} %get-tuple-element.104, bf16[320,768]{1,0:T(8,128)(2,1)S(1)} %get-tuple-element.103, bf16[320,768]{1,0:T(8,128)(2,1)S(1)} %get-tuple-element.102), kind=kOutput, calls=%fused_computation.8 | convolution fusion | flops 1518403584 | bytes 4325380 | tf_op jit(solution)/shard_map/dot_general | solution.py:12
  110.5 6.6 %collective-permute-done.27 = bf16[64,2048]{1,0:T(8,128)(2,1)S(1)} collective-permute-done((bf16[64,2048]{1,0:T(8,128)(2,1)S(1)}, bf16[64,2048]{1,0:T(8,128)(2,1)S(1)}, u32[]{:S(2)}, u32[]{:S(2)}) %collective-permute-start.27) | collective-permute-done | bytes 262176 | tf_op jit(solution)/shard_map/ppermute | solution.py:190
  117.1 0.8 collective-permute-start.31
  117.9 0.6 collective-permute-start.30
  118.6 0.1 add_convert_fusion.3
  118.7 2.3 %collective-permute-start.32 = (bf16[64,2048]{1,0:T(8,128)(2,1)S(1)}, bf16[64,2048]{1,0:T(8,128)(2,1)S(1)}, u32[]{:S(2)}, u32[]{:S(2)}) collective-permute-start(bf16[64,2048]{1,0:T(8,128)(2,1)S(1)} %add_convert_fusion.3), channel_id=1, source_target_pairs={{0,8},{1,9},{2,10},{3,11},{4,12},{5,13},{6,14},{7,15},{8,0},{9,1},... | collective-permute-start | bytes 786440 | tf_op jit(solution)/shard_map/ppermute | solution.py:190
  121.0 8.1 %collective-permute-done.31.near_high = bf16[64,2048]{1,0:T(8,128)(2,1)S(1)} collective-permute-done((bf16[64,2048]{1,0:T(8,128)(2,1)S(1)}, bf16[64,2048]{1,0:T(8,128)(2,1)S(1)}, u32[]{:S(2)}, u32[]{:S(2)}) %collective-permute-start.31) | collective-permute-done | bytes 262176 | tf_op jit(solution)/shard_map/ppermute | solution.py:190
  129.1 3.4 %collective-permute-done.32.far_low = bf16[64,2048]{1,0:T(8,128)(2,1)S(1)} collective-permute-done((bf16[64,2048]{1,0:T(8,128)(2,1)S(1)}, bf16[64,2048]{1,0:T(8,128)(2,1)S(1)}, u32[]{:S(2)}, u32[]{:S(2)}) %collective-permute-start.32) | collective-permute-done | bytes 262176 | tf_op jit(solution)/shard_map/ppermute | solution.py:190
  132.5 1.1 shard_map.83
  (45 shorter events, 0.6 us)
Async XLA Ops:
  0.6 24.1 %collective-permute-start.1 = (bf16[128,2048]{1,0:T(8,128)(2,1)}, bf16[128,2048]{1,0:T(8,128)(2,1)S(1)}, u32[]{:S(2)}, u32[]{:S(2)}) collective-permute-start(bf16[128,2048]{1,0:T(8,128)(2,1)} %refs_0_.1), channel_id=1, source_target_pairs={{0,4},{1,5},{2,6},{3,7},{4,0},{5,1},{6,2},{7,3},{8,12},{9,13},{10,... | collective-permute-start | bytes 1572872 | tf_op jit(solution)/shard_map/ppermute | solution.py:190
  3.7 21.0 %collective-permute-start.3 = (bf16[128,2048]{1,0:T(8,128)(2,1)}, bf16[128,2048]{1,0:T(8,128)(2,1)S(1)}, u32[]{:S(2)}, u32[]{:S(2)}) collective-permute-start(bf16[128,2048]{1,0:T(8,128)(2,1)} %refs_0_.1), channel_id=1, source_target_pairs={{0,2},{1,3},{2,0},{3,1},{4,6},{5,7},{6,4},{7,5},{8,10},{9,11},{10,... | collective-permute-start | bytes 1572872 | tf_op jit(solution)/shard_map/ppermute | solution.py:190
  5.2 19.5 %collective-permute-start.4 = (bf16[128,2048]{1,0:T(8,128)(2,1)}, bf16[128,2048]{1,0:T(8,128)(2,1)S(1)}, u32[]{:S(2)}, u32[]{:S(2)}) collective-permute-start(bf16[128,2048]{1,0:T(8,128)(2,1)} %refs_0_.1), channel_id=1, source_target_pairs={{0,1},{1,0},{2,3},{3,2},{4,5},{5,4},{6,7},{7,6},{8,9},{9,8},{10,11... | collective-permute-start | bytes 1572872 | tf_op jit(solution)/shard_map/ppermute | solution.py:190
  5.2 27.7 %copy-start.6 = (bf16[128,2048]{1,0:T(8,128)(2,1)S(1)}, bf16[128,2048]{1,0:T(8,128)(2,1)}, u32[]{:S(2)}) copy-start(bf16[128,2048]{1,0:T(8,128)(2,1)} %refs_0_.1) | copy-start | bytes 1572868
  7.1 17.6 %collective-permute-start.2 = (bf16[64,2048]{1,0:T(8,128)(2,1)S(1)}, bf16[64,2048]{1,0:T(8,128)(2,1)S(1)}, u32[]{:S(2)}, u32[]{:S(2)}) collective-permute-start(bf16[64,2048]{1,0:T(8,128)(2,1)S(1)} %get-tuple-element.117), channel_id=1, source_target_pairs={{0,8},{1,9},{2,10},{3,11},{4,12},{5,13},{6,14},{7,15},{8,0},{9,1},... | collective-permute-start | bytes 786440 | tf_op jit(solution)/shard_map/ppermute | solution.py:190
  9.7 0.7 copy-start.7
  10.4 0.7 copy-start.8
  24.7 8.2 %collective-permute-start.7 = (bf16[128,2048]{1,0:T(8,128)(2,1)S(1)}, bf16[128,2048]{1,0:T(8,128)(2,1)}, u32[]{:S(2)}, u32[]{:S(2)}) collective-permute-start(bf16[128,2048]{1,0:T(8,128)(2,1)S(1)} %collective-permute-done.3.refs_1_), channel_id=1, source_target_pairs={{0,1},{1,0},{2,3},{3,2},{4,5},{5,4},{6,7},{7,6},{8,9},{9,8},{10,11... | collective-permute-start | bytes 1572872 | tf_op jit(solution)/shard_map/ppermute | solution.py:190
  24.8 17.6 %collective-permute-start.6 = (bf16[128,2048]{1,0:T(8,128)(2,1)S(1)}, bf16[128,2048]{1,0:T(8,128)(2,1)S(1)}, u32[]{:S(2)}, u32[]{:S(2)}) collective-permute-start(bf16[128,2048]{1,0:T(8,128)(2,1)S(1)} %collective-permute-done.1.refs_0_), channel_id=1, source_target_pairs={{0,1},{1,0},{2,3},{3,2},{4,5},{5,4},{6,7},{7,6},{8,9},{9,8},{10,11... | collective-permute-start | bytes 1572872 | tf_op jit(solution)/shard_map/ppermute | solution.py:190
  25.3 17.2 %collective-permute-start.5 = (bf16[128,2048]{1,0:T(8,128)(2,1)S(1)}, bf16[128,2048]{1,0:T(8,128)(2,1)S(1)}, u32[]{:S(2)}, u32[]{:S(2)}) collective-permute-start(bf16[128,2048]{1,0:T(8,128)(2,1)S(1)} %collective-permute-done.1.refs_0_), channel_id=1, source_target_pairs={{0,2},{1,3},{2,0},{3,1},{4,6},{5,7},{6,4},{7,5},{8,10},{9,11},{10,... | collective-permute-start | bytes 1572872 | tf_op jit(solution)/shard_map/ppermute | solution.py:190
  25.8 16.6 %collective-permute-start = (bf16[64,2048]{1,0:T(8,128)(2,1)}, bf16[64,2048]{1,0:T(8,128)(2,1)}, u32[]{:S(2)}, u32[]{:S(2)}) collective-permute-start(bf16[64,2048]{1,0:T(8,128)(2,1)} %get-tuple-element.118), channel_id=1, source_target_pairs={{0,8},{1,9},{2,10},{3,11},{4,12},{5,13},{6,14},{7,15},{8,0},{9,1},... | collective-permute-start | bytes 786440 | tf_op jit(solution)/shard_map/ppermute | solution.py:190
  26.5 1.9 %copy-start = (bf16[1,2048,768]{2,1,0:T(8,128)(2,1)S(1)}, bf16[1,2048,768]{2,1,0:T(8,128)(2,1)}, u32[]{:S(2)}) copy-start(bf16[1,2048,768]{2,1,0:T(8,128)(2,1)} %param.9) | copy-start | bytes 9437188
  28.4 1.9 %copy-start.2 = (bf16[1,2048,768]{2,1,0:T(8,128)(2,1)S(1)}, bf16[1,2048,768]{2,1,0:T(8,128)(2,1)}, u32[]{:S(2)}) copy-start(bf16[1,2048,768]{2,1,0:T(8,128)(2,1)} %param.10) | copy-start | bytes 9437188
  30.3 1.9 %copy-start.4 = (bf16[1,768,2048]{2,1,0:T(8,128)(2,1)S(1)}, bf16[1,768,2048]{2,1,0:T(8,128)(2,1)}, u32[]{:S(2)}) copy-start(bf16[1,768,2048]{2,1,0:T(8,128)(2,1)} %param.11) | copy-start | bytes 9437188
  32.2 1.9 %copy-start.1 = (bf16[1,2048,768]{2,1,0:T(8,128)(2,1)S(1)}, bf16[1,2048,768]{2,1,0:T(8,128)(2,1)}, u32[]{:S(2)}) copy-start(bf16[1,2048,768]{2,1,0:T(8,128)(2,1)} %param.9) | copy-start | bytes 9437188
  32.2 2.8 %copy-start.3 = (bf16[1,2048,768]{2,1,0:T(8,128)(2,1)S(1)}, bf16[1,2048,768]{2,1,0:T(8,128)(2,1)}, u32[]{:S(2)}) copy-start(bf16[1,2048,768]{2,1,0:T(8,128)(2,1)} %param.10) | copy-start | bytes 9437188
  32.2 3.8 %copy-start.5 = (bf16[1,768,2048]{2,1,0:T(8,128)(2,1)S(1)}, bf16[1,768,2048]{2,1,0:T(8,128)(2,1)}, u32[]{:S(2)}) copy-start(bf16[1,768,2048]{2,1,0:T(8,128)(2,1)} %param.11) | copy-start | bytes 9437188
  42.5 4.7 %collective-permute-start.11 = (bf16[128,2048]{1,0:T(8,128)(2,1)S(1)}, bf16[128,2048]{1,0:T(8,128)(2,1)S(1)}, u32[]{:S(2)}, u32[]{:S(2)}) collective-permute-start(bf16[128,2048]{1,0:T(8,128)(2,1)S(1)} %collective-permute-done.5.refs_1_), channel_id=1, source_target_pairs={{0,1},{1,0},{2,3},{3,2},{4,5},{5,4},{6,7},{7,6},{8,9},{9,8},{10,11... | collective-permute-start | bytes 1572872 | tf_op jit(solution)/shard_map/ppermute | solution.py:190
  43.6 9.2 %collective-permute-start.10 = (bf16[128,2048]{1,0:T(8,128)(2,1)S(1)}, bf16[128,2048]{1,0:T(8,128)(2,1)S(1)}, u32[]{:S(2)}, u32[]{:S(2)}) collective-permute-start(bf16[128,2048]{1,0:T(8,128)(2,1)S(1)} %constant_dynamic-update-slice_fusion.refs_0_), channel_id=1, source_target_pairs={{0,1},{1,0},{2,3},{3,2},{4,5},{5,4},{6,7},{7,6},{8,9},{9,8},{10,11... | collective-permute-start | bytes 1572872 | tf_op jit(solution)/shard_map/ppermute | solution.py:190
  44.1 13.9 %collective-permute-start.9 = (bf16[128,2048]{1,0:T(8,128)(2,1)S(1)}, bf16[128,2048]{1,0:T(8,128)(2,1)S(1)}, u32[]{:S(2)}, u32[]{:S(2)}) collective-permute-start(bf16[128,2048]{1,0:T(8,128)(2,1)S(1)} %constant_dynamic-update-slice_fusion.refs_0_), channel_id=1, source_target_pairs={{0,2},{1,3},{2,0},{3,1},{4,6},{5,7},{6,4},{7,5},{8,10},{9,11},{10,... | collective-permute-start | bytes 1572872 | tf_op jit(solution)/shard_map/ppermute | solution.py:190
  45.6 13.6 %collective-permute-start.8 = (bf16[128,2048]{1,0:T(8,128)(2,1)S(1)}, bf16[128,2048]{1,0:T(8,128)(2,1)S(1)}, u32[]{:S(2)}, u32[]{:S(2)}) collective-permute-start(bf16[128,2048]{1,0:T(8,128)(2,1)S(1)} %constant_dynamic-update-slice_fusion.refs_0_), channel_id=1, source_target_pairs={{0,4},{1,5},{2,6},{3,7},{4,0},{5,1},{6,2},{7,3},{8,12},{9,13},{10,... | collective-permute-start | bytes 1572872 | tf_op jit(solution)/shard_map/ppermute | solution.py:190
  52.7 6.5 %collective-permute-start.12 = (bf16[128,2048]{1,0:T(8,128)(2,1)S(1)}, bf16[128,2048]{1,0:T(8,128)(2,1)S(1)}, u32[]{:S(2)}, u32[]{:S(2)}) collective-permute-start(bf16[128,2048]{1,0:T(8,128)(2,1)S(1)} %get-tuple-element.73), channel_id=1, source_target_pairs={{0,1},{1,0},{2,3},{3,2},{4,5},{5,4},{6,7},{7,6},{8,9},{9,8},{10,11... | collective-permute-start | bytes 1572872 | tf_op jit(solution)/shard_map/ppermute | solution.py:190
  59.2 3.0 %collective-permute-start.17 = (bf16[128,2048]{1,0:T(8,128)(2,1)S(1)}, bf16[128,2048]{1,0:T(8,128)(2,1)S(1)}, u32[]{:S(2)}, u32[]{:S(2)}) collective-permute-start(bf16[128,2048]{1,0:T(8,128)(2,1)S(1)} %collective-permute-done.9.refs_1_), channel_id=1, source_target_pairs={{0,1},{1,0},{2,3},{3,2},{4,5},{5,4},{6,7},{7,6},{8,9},{9,8},{10,11... | collective-permute-start | bytes 1572872 | tf_op jit(solution)/shard_map/ppermute | solution.py:190
  59.3 14.4 %collective-permute-start.14 = (bf16[128,2048]{1,0:T(8,128)(2,1)S(1)}, bf16[128,2048]{1,0:T(8,128)(2,1)S(1)}, u32[]{:S(2)}, u32[]{:S(2)}) collective-permute-start(bf16[128,2048]{1,0:T(8,128)(2,1)S(1)} %add_convert_fusion.2), channel_id=1, source_target_pairs={{0,2},{1,3},{2,0},{3,1},{4,6},{5,7},{6,4},{7,5},{8,10},{9,11},{10,... | collective-permute-start | bytes 1572872 | tf_op jit(solution)/shard_map/ppermute | solution.py:190
  60.0 13.8 %collective-permute-start.16 = (bf16[128,2048]{1,0:T(8,128)(2,1)S(1)}, bf16[128,2048]{1,0:T(8,128)(2,1)S(1)}, u32[]{:S(2)}, u32[]{:S(2)}) collective-permute-start(bf16[128,2048]{1,0:T(8,128)(2,1)S(1)} %get-tuple-element.78), channel_id=1, source_target_pairs={{0,1},{1,0},{2,3},{3,2},{4,5},{5,4},{6,7},{7,6},{8,9},{9,8},{10,11... | collective-permute-start | bytes 1572872 | tf_op jit(solution)/shard_map/ppermute | solution.py:190
  60.2 13.5 %collective-permute-start.15 = (bf16[128,2048]{1,0:T(8,128)(2,1)S(1)}, bf16[128,2048]{1,0:T(8,128)(2,1)S(1)}, u32[]{:S(2)}, u32[]{:S(2)}) collective-permute-start(bf16[128,2048]{1,0:T(8,128)(2,1)S(1)} %collective-permute-done.8.refs_0_), channel_id=1, source_target_pairs={{0,1},{1,0},{2,3},{3,2},{4,5},{5,4},{6,7},{7,6},{8,9},{9,8},{10,11... | collective-permute-start | bytes 1572872 | tf_op jit(solution)/shard_map/ppermute | solution.py:190
  60.5 14.1 %collective-permute-start.13 = (bf16[128,2048]{1,0:T(8,128)(2,1)S(1)}, bf16[128,2048]{1,0:T(8,128)(2,1)S(1)}, u32[]{:S(2)}, u32[]{:S(2)}) collective-permute-start(bf16[128,2048]{1,0:T(8,128)(2,1)S(1)} %collective-permute-done.9.refs_1_), channel_id=1, source_target_pairs={{0,4},{1,5},{2,6},{3,7},{4,0},{5,1},{6,2},{7,3},{8,12},{9,13},{10,... | collective-permute-start | bytes 1572872 | tf_op jit(solution)/shard_map/ppermute | solution.py:190
  74.5 2.7 %collective-permute-start.19 = (bf16[256,2048]{1,0:T(8,128)(2,1)S(1)}, bf16[256,2048]{1,0:T(8,128)(2,1)S(1)}, u32[]{:S(2)}, u32[]{:S(2)}) collective-permute-start(bf16[256,2048]{1,0:T(8,128)(2,1)S(1)} %get-tuple-element.88), channel_id=1, source_target_pairs={{0,1},{1,0},{2,3},{3,2},{4,5},{5,4},{6,7},{7,6},{8,9},{9,8},{10,11... | collective-permute-start | bytes 3145736 | tf_op jit(solution)/shard_map/ppermute | solution.py:190
  74.5 4.3 %collective-permute-start.18 = (bf16[128,2048]{1,0:T(8,128)(2,1)S(1)}, bf16[128,2048]{1,0:T(8,128)(2,1)S(1)}, u32[]{:S(2)}, u32[]{:S(2)}) collective-permute-start(bf16[128,2048]{1,0:T(8,128)(2,1)S(1)} %collective-permute-done.13.refs_1_), channel_id=1, source_target_pairs={{0,1},{1,0},{2,3},{3,2},{4,5},{5,4},{6,7},{7,6},{8,9},{9,8},{10,11... | collective-permute-start | bytes 1572872 | tf_op jit(solution)/shard_map/ppermute | solution.py:190
  75.3 9.0 %collective-permute-start.20 = (bf16[64,2048]{1,0:T(8,128)(2,1)S(1)}, bf16[64,2048]{1,0:T(8,128)(2,1)S(1)}, u32[]{:S(2)}, u32[]{:S(2)}) collective-permute-start(bf16[64,2048]{1,0:T(8,128)(2,1)S(1)} %slice.100), channel_id=1, source_target_pairs={{0,4},{1,5},{2,6},{3,7},{4,0},{5,1},{6,2},{7,3},{8,12},{9,13},{10,... | collective-permute-start | bytes 786440 | tf_op jit(solution)/shard_map/ppermute | solution.py:190
  77.3 8.4 %collective-permute-start.21 = (bf16[64,2048]{1,0:T(8,128)(2,1)S(1)}, bf16[64,2048]{1,0:T(8,128)(2,1)S(1)}, u32[]{:S(2)}, u32[]{:S(2)}) collective-permute-start(bf16[64,2048]{1,0:T(8,128)(2,1)S(1)} %add_convert_fusion.11), channel_id=1, source_target_pairs={{0,2},{1,3},{2,0},{3,1},{4,6},{5,7},{6,4},{7,5},{8,10},{9,11},{10,... | collective-permute-start | bytes 786440 | tf_op jit(solution)/shard_map/ppermute | solution.py:190
  85.7 3.5 %collective-permute-start.22 = (bf16[256,2048]{1,0:T(8,128)(2,1)S(1)}, bf16[256,2048]{1,0:T(8,128)(2,1)S(1)}, u32[]{:S(2)}, u32[]{:S(2)}) collective-permute-start(bf16[256,2048]{1,0:T(8,128)(2,1)S(1)} %get-tuple-element.93), channel_id=1, source_target_pairs={{0,1},{1,0},{2,3},{3,2},{4,5},{5,4},{6,7},{7,6},{8,9},{9,8},{10,11... | collective-permute-start | bytes 3145736 | tf_op jit(solution)/shard_map/ppermute | solution.py:190
  85.7 6.1 %collective-permute-start.26 = (bf16[256,2048]{1,0:T(8,128)(2,1)S(1)}, bf16[256,2048]{1,0:T(8,128)(2,1)S(1)}, u32[]{:S(2)}, u32[]{:S(2)}) collective-permute-start(bf16[256,2048]{1,0:T(8,128)(2,1)S(1)} %get-tuple-element.97), channel_id=1, source_target_pairs={{0,1},{1,0},{2,3},{3,2},{4,5},{5,4},{6,7},{7,6},{8,9},{9,8},{10,11... | collective-permute-start | bytes 3145736 | tf_op jit(solution)/shard_map/ppermute | solution.py:190
  86.8 14.9 %collective-permute-start.25 = (bf16[64,2048]{1,0:T(8,128)(2,1)S(1)}, bf16[64,2048]{1,0:T(8,128)(2,1)S(1)}, u32[]{:S(2)}, u32[]{:S(2)}) collective-permute-start(bf16[64,2048]{1,0:T(8,128)(2,1)S(1)} %add_convert_fusion.8), channel_id=1, source_target_pairs={{0,8},{1,9},{2,10},{3,11},{4,12},{5,13},{6,14},{7,15},{8,0},{9,1},... | collective-permute-start | bytes 786440 | tf_op jit(solution)/shard_map/ppermute | solution.py:190
  89.5 12.2 %collective-permute-start.24 = (bf16[64,2048]{1,0:T(8,128)(2,1)S(1)}, bf16[64,2048]{1,0:T(8,128)(2,1)S(1)}, u32[]{:S(2)}, u32[]{:S(2)}) collective-permute-start(bf16[64,2048]{1,0:T(8,128)(2,1)S(1)} %get-tuple-element.115), channel_id=1, source_target_pairs={{0,2},{1,3},{2,0},{3,1},{4,6},{5,7},{6,4},{7,5},{8,10},{9,11},{10,... | collective-permute-start | bytes 786440 | tf_op jit(solution)/shard_map/ppermute | solution.py:190
  91.1 12.0 %collective-permute-start.23 = (bf16[64,2048]{1,0:T(8,128)(2,1)S(1)}, bf16[64,2048]{1,0:T(8,128)(2,1)S(1)}, u32[]{:S(2)}, u32[]{:S(2)}) collective-permute-start(bf16[64,2048]{1,0:T(8,128)(2,1)S(1)} %get-tuple-element.116), channel_id=1, source_target_pairs={{0,4},{1,5},{2,6},{3,7},{4,0},{5,1},{6,2},{7,3},{8,12},{9,13},{10,... | collective-permute-start | bytes 786440 | tf_op jit(solution)/shard_map/ppermute | solution.py:190
  103.2 7.2 %collective-permute-start.29 = (bf16[64,2048]{1,0:T(8,128)(2,1)S(1)}, bf16[64,2048]{1,0:T(8,128)(2,1)S(1)}, u32[]{:S(2)}, u32[]{:S(2)}) collective-permute-start(bf16[64,2048]{1,0:T(8,128)(2,1)S(1)} %add_convert_fusion.5), channel_id=1, source_target_pairs={{0,2},{1,3},{2,0},{3,1},{4,6},{5,7},{6,4},{7,5},{8,10},{9,11},{10,... | collective-permute-start | bytes 786440 | tf_op jit(solution)/shard_map/ppermute | solution.py:190
  104.0 13.1 %collective-permute-start.27 = (bf16[64,2048]{1,0:T(8,128)(2,1)S(1)}, bf16[64,2048]{1,0:T(8,128)(2,1)S(1)}, u32[]{:S(2)}, u32[]{:S(2)}) collective-permute-start(bf16[64,2048]{1,0:T(8,128)(2,1)S(1)} %add_convert_fusion.6), channel_id=1, source_target_pairs={{0,8},{1,9},{2,10},{3,11},{4,12},{5,13},{6,14},{7,15},{8,0},{9,1},... | collective-permute-start | bytes 786440 | tf_op jit(solution)/shard_map/ppermute | solution.py:190
  105.1 12.0 %collective-permute-start.28 = (bf16[64,2048]{1,0:T(8,128)(2,1)S(1)}, bf16[64,2048]{1,0:T(8,128)(2,1)S(1)}, u32[]{:S(2)}, u32[]{:S(2)}) collective-permute-start(bf16[64,2048]{1,0:T(8,128)(2,1)S(1)} %get-tuple-element.99), channel_id=1, source_target_pairs={{0,4},{1,5},{2,6},{3,7},{4,0},{5,1},{6,2},{7,3},{8,12},{9,13},{10,... | collective-permute-start | bytes 786440 | tf_op jit(solution)/shard_map/ppermute | solution.py:190
  117.1 12.0 %collective-permute-start.31 = (bf16[64,2048]{1,0:T(8,128)(2,1)S(1)}, bf16[64,2048]{1,0:T(8,128)(2,1)S(1)}, u32[]{:S(2)}, u32[]{:S(2)}) collective-permute-start(bf16[64,2048]{1,0:T(8,128)(2,1)S(1)} %add_convert_fusion.4), channel_id=1, source_target_pairs={{0,4},{1,5},{2,6},{3,7},{4,0},{5,1},{6,2},{7,3},{8,12},{9,13},{10,... | collective-permute-start | bytes 786440 | tf_op jit(solution)/shard_map/ppermute | solution.py:190
  117.9 14.6 %collective-permute-start.30 = (bf16[128,2048]{1,0:T(8,128)(2,1)S(1)}, bf16[128,2048]{1,0:T(8,128)(2,1)S(1)}, u32[]{:S(2)}, u32[]{:S(2)}) collective-permute-start(bf16[128,2048]{1,0:T(8,128)(2,1)S(1)} %add_convert_fusion), channel_id=1, source_target_pairs={{0,2},{1,3},{2,0},{3,1},{4,6},{5,7},{6,4},{7,5},{8,10},{9,11},{10,... | collective-permute-start | bytes 1572872 | tf_op jit(solution)/shard_map/ppermute | solution.py:190
  118.7 13.8 %collective-permute-start.32 = (bf16[64,2048]{1,0:T(8,128)(2,1)S(1)}, bf16[64,2048]{1,0:T(8,128)(2,1)S(1)}, u32[]{:S(2)}, u32[]{:S(2)}) collective-permute-start(bf16[64,2048]{1,0:T(8,128)(2,1)S(1)} %add_convert_fusion.3), channel_id=1, source_target_pairs={{0,8},{1,9},{2,10},{3,11},{4,12},{5,13},{6,14},{7,15},{8,0},{9,1},... | collective-permute-start | bytes 786440 | tf_op jit(solution)/shard_map/ppermute | solution.py:190

commit v17 on v16

--- a/solution.py
+++ b/solution.py
@@ -28,24 +28,44 @@
     return lax.all_to_all(mine, "expert", split_axis=0, concat_axis=0, tiled=True)
 
 
-def table_kernel(routes, probs, mine):
-    names, shares = routes[...], probs[...]
+def prepare_kernel(routes, probs, tokens, mine, low, high, names, shares, sems):
+    half = low.shape[0]
+    pairs = (
+        (routes, names),
+        (probs, shares),
+        (tokens.at[pl.ds(0, half), :], low),
+        (tokens.at[pl.ds(half, half), :], high),
+    )
+    copies = [pltpu.make_async_copy(*pair, sems.at[i]) for i, pair in enumerate(pairs)]
+    for copy in copies:
+        copy.start()
+    for copy in copies[:2]:
+        copy.wait()
     for e in range(mine.shape[0]):
-        hit = (names == e).astype(jnp.float32)
+        hit = (names[...] == e).astype(jnp.float32)
         named = jnp.sum(hit, axis=0, keepdims=True)
-        share = jnp.sum(hit * shares, axis=0, keepdims=True)
+        share = jnp.sum(hit * shares[...], axis=0, keepdims=True)
         mine[pl.ds(e, 1), :] = jnp.where(named > 0.0, share, -1.0)
-
-
-def table_pass(routes, probs, experts):
-    mine = pl.pallas_call(
-        table_kernel,
-        out_shape=jax.ShapeDtypeStruct((experts, routes.shape[0]), jnp.float32),
-        in_specs=[pl.BlockSpec(memory_space=pltpu.VMEM)] * 2,
-        out_specs=pl.BlockSpec(memory_space=pltpu.VMEM),
+    for copy in copies[2:]:
+        copy.wait()
+
+
+def prepare_pass(routes, probs, tokens, experts):
+    tok, top = routes.shape
+    half = jax.ShapeDtypeStruct((tok // 2, tokens.shape[1]), tokens.dtype)
+    vmem = pl.BlockSpec(memory_space=pltpu.VMEM)
+    return pl.pallas_call(
+        prepare_kernel,
+        out_shape=(jax.ShapeDtypeStruct((experts, tok), jnp.float32), half, half),
+        in_specs=[pl.BlockSpec(memory_space=pl.ANY)] * 3,
+        out_specs=[vmem] * 3,
+        scratch_shapes=[
+            pltpu.VMEM((top, tok), routes.dtype),
+            pltpu.VMEM((top, tok), probs.dtype),
+            pltpu.SemaphoreType.DMA((4,)),
+        ],
         compiler_params=pltpu.CompilerParams(vmem_limit_bytes=4 * 1024 * 1024),
-    )(routes.T, probs.T)
-    return lax.all_to_all(mine, "expert", split_axis=0, concat_axis=0, tiled=True)
+    )(routes.T, probs.T, tokens)
 
 
 def summed(*parts):
@@ -55,7 +75,7 @@
     return total.astype(jnp.bfloat16)
 
 
-def ranks_kernel(capacity, spots, weight, w_gate, w_up, w_down, tables, ranks):
+def ranks_kernel(capacity, spots, weight, tables, ranks):
     blocks, tok = weight.shape
     planes = blocks // 4
     named = (weight[...] >= 0.0).astype(jnp.float32)
@@ -81,17 +101,17 @@
     tables[2 * planes :, :] = jnp.broadcast_to(2.0 / count, tables[2 * planes :, :].shape)
 
 
-def ranks_pass(capacity, spots, weight, w_gate, w_up, w_down):
+def ranks_pass(capacity, spots, weight):
     blocks, tok = weight.shape
     vmem = pl.BlockSpec(memory_space=pltpu.VMEM)
     return pl.pallas_call(
         functools.partial(ranks_kernel, capacity),
         out_shape=jax.ShapeDtypeStruct((blocks // 4 * 2 + 8, 4 * tok), jnp.float32),
-        in_specs=[pl.BlockSpec(memory_space=pltpu.SMEM)] + [vmem] * 4,
+        in_specs=[pl.BlockSpec(memory_space=pltpu.SMEM), vmem],
         out_specs=vmem,
         scratch_shapes=[pltpu.VMEM(weight.shape, jnp.float32)],
         compiler_params=pltpu.CompilerParams(vmem_limit_bytes=4 * 1024 * 1024),
-    )(spots, weight, w_gate, w_up, w_down)
+    )(spots, weight)
 
 
 def plane_kernel(k, gives, tables, *refs):
@@ -209,13 +229,18 @@
     def expert(k, *xs, pieces=None):
         return plane_pass(k, tables, xs, w_gate, w_up, w_down, slots, pieces)
 
-    weight = table_pass(routes, probs, size)
+    mine, a0_low, a0_high = prepare_pass(routes, probs, tokens, size)
     a0 = tokens
-    a1, low, b0, c0, weight = together(
-        pair(a0), far(a0[:half]), column(a0), sibling(a0), weight
-    )
-    tables = ranks_pass(capacity, spots, weight, w_gate, w_up, w_down)
-    high = far(a0[half:])
+    a1, low, b0, c0, weight, a0_high = together(
+        pair(a0),
+        far(a0_low),
+        column(a0),
+        sibling(a0),
+        lax.all_to_all(mine, "expert", split_axis=0, concat_axis=0, tiled=True),
+        a0_high,
+    )
+    tables = ranks_pass(capacity, spots, weight)
+    high = far(a0_high)
     b1 = column(a1)
     d0 = sibling(b0)
     c1 = sibling(a1)
@@ -256,14 +281,13 @@
     far2_high = far(own(keep2, got2, half, tok, side_high))
     got0 = sibling(give0)
     got3 = sibling(give3)
-    low = pair(own(keep3, got3, tok, tok + half))
-    high = column(own(keep3, got3, tok + half, 2 * tok))
-    sum3 = own(keep3, got3, 0, half)
+    came3 = column(own(keep3, got3, tok, 2 * tok))
     side0 = own(keep0, got0, tok, 2 * tok)
-    low, high, far2_high, sum3, side0 = together(low, high, far2_high, sum3, side0)
-    far3_high = far(own(keep3, got3, half, tok, high))
-    pair3_low = pair(sum3)
-    side_low = column(own(keep2, got2, tok, tok + half, low))
+    side2 = own(keep2, got2, tok, tok + half)
+    came3, far2_high, side0, side2 = together(came3, far2_high, side0, side2)
+    far3_high = far(own(keep3, got3, half, tok, came3[half:]))
+    pair3_low = pair(own(keep3, got3, 0, half, came3[:half]))
+    side_low = column(side2)
     gram = gram_of(jnp.concatenate([act0, act1, act2, act3], axis=0)) * tables[8, 0]
     far3_high, pair3_low, side_low, side0, gram = together(
         far3_high, pair3_low, side_low, side0, gram

time: 134 us -> 133 us (level)
  waiting for transfers between devices: 44 us -> 50 us
  starting transfers between devices: 31.5 us -> 27.8 us
  local copies, waits for them, and re-layouts: 13.5 us -> 10.5 us
    ppermute x33 -> x32, waiting for transfers between devices: 44 us -> 50 us  [swapped(): return lax.ppermute(array, 'expert', [(i, i ^ bit) for i in range(size)])]
    ppermute x33 -> x32, starting transfers between devices: 31.5 us -> 27.8 us  [swapped(): return lax.ppermute(array, 'expert', [(i, i ^ bit) for i in range(size)])]
    slice x1 -> x0, local copies, waits for them, and re-layouts: 1.84 us -> none  [staged(): a0[:half]]
    unnamed x19 -> x25, local copies, waits for them, and re-layouts: 10 us -> 9.86 us
  transfers between devices with their start and end apart: 33 -> 32, of which waited for: 11 -> 12; matrix products, arithmetic and copies ran while one was open for 6% -> 4% of each run, Pallas kernels for 18% -> 17%
where the time goes in v17:
time: 133 us
  waiting for transfers between devices  50 us (38%)
  starting transfers between devices  27.8 us (21%)
  Pallas kernels  24 us (18%)
  blocking collectives  14.2 us (11%)
  local copies, waits for them, and re-layouts  10.5 us (8%)
  matrix products  3.8 us (3%)
    ppermute x32, waiting for transfers between devices, swapped(): return lax.ppermute(array, 'expert', [(i, i ^ bit) for i in range(size)])  50 us
    ppermute x32, starting transfers between devices, swapped(): return lax.ppermute(array, 'expert', [(i, i ^ bit) for i in range(size)])  27.8 us
    pallas_call x4, Pallas kernels, plane_pass(): pl.pallas_call(functools.partial(plane_kernel, k, len(pieces)), out_shape...  22 us
    all_to_all x1, blocking collectives, staged(): lax.all_to_all(mine, 'expert', split_axis=0, concat_axis=0, tiled=True)  14.2 us
    unnamed x25, local copies, waits for them, and re-layouts  9.86 us
    dot_general x1, matrix products, gram_of(): lax.dot_general(rows, rows, (((0,), (0,)), ((), ())), preferred_element_t...  3.8 us
  transfers between devices with their start and end apart: 32, of which 12 were waited for; matrix products, arithmetic and copies ran while one was open for 4% of the time, Pallas kernels for 17%

profile of v17, /device:TPU:0, one launch (start us, length us, event | category | flops | bytes accessed | tf_op | source)
XLA Modules:
  0.0 132.6 jit_solution(14078836104523487464)
XLA Ops:
  0.6 3.1 %collective-permute-start = (bf16[128,2048]{1,0:T(8,128)(2,1)}, bf16[128,2048]{1,0:T(8,128)(2,1)S(1)}, u32[]{:S(2)}, u32[]{:S(2)}) collective-permute-start(bf16[128,2048]{1,0:T(8,128)(2,1)} %refs_0_.1), channel_id=1, source_target_pairs={{0,4},{1,5},{2,6},{3,7},{4,0},{5,1},{6,2},{7,3},{8,12},{9,13},{10,... | collective-permute-start | bytes 1572872 | tf_op jit(solution)/shard_map/ppermute | solution.py:210
  3.7 1.5 %collective-permute-start.2 = (bf16[128,2048]{1,0:T(8,128)(2,1)}, bf16[128,2048]{1,0:T(8,128)(2,1)S(1)}, u32[]{:S(2)}, u32[]{:S(2)}) collective-permute-start(bf16[128,2048]{1,0:T(8,128)(2,1)} %refs_0_.1), channel_id=1, source_target_pairs={{0,2},{1,3},{2,0},{3,1},{4,6},{5,7},{6,4},{7,5},{8,10},{9,11},{10,... | collective-permute-start | bytes 1572872 | tf_op jit(solution)/shard_map/ppermute | solution.py:210
  5.2 1.1 copy-done
  6.3 0.7 copy-done.2
  7.0 0.7 copy-done.3
  7.7 0.1 shard_map.77
  7.8 2.7 %collective-permute-start.1 = (bf16[64,2048]{1,0:T(8,128)(2,1)S(1)}, bf16[64,2048]{1,0:T(8,128)(2,1)S(1)}, u32[]{:S(2)}, u32[]{:S(2)}) collective-permute-start(bf16[64,2048]{1,0:T(8,128)(2,1)S(1)} %get-tuple-element.61), channel_id=1, source_target_pairs={{0,8},{1,9},{2,10},{3,11},{4,12},{5,13},{6,14},{7,15},{8,0},{9,1},... | collective-permute-start | bytes 786440 | tf_op jit(solution)/shard_map/ppermute | solution.py:210
  10.5 14.2 %all_to_all.12 = f32[16,1,128]{2,1,0:T(1,128)S(1)} all-to-all(f32[16,1,128]{2,1,0:T(1,128)S(1)} %bitcast.28), channel_id=1, replica_groups=mesh['parts'=2,'expert'=16] {'expert'}, dimensions={0} | all-to-all | bytes 16384 | tf_op jit(solution)/shard_map/all_to_all | solution.py:239
  24.8 0.7 copy-done.10
  25.4 0.5 collective-permute-start.5
  25.9 0.2 collective-permute-start.6
  26.2 0.1 stack.67.spots
  26.3 1.1 collective-permute-start.4
  27.4 0.7 shard_map.78.tables
  28.2 1.0 copy-done.1
  29.2 1.9 %copy-done.4 = bf16[1,2048,768]{2,1,0:T(8,128)(2,1)S(1)} copy-done((bf16[1,2048,768]{2,1,0:T(8,128)(2,1)S(1)}, bf16[1,2048,768]{2,1,0:T(8,128)(2,1)}, u32[]{:S(2)}) %copy-start.4) | copy-done | bytes 3145752
  31.1 1.9 %copy-done.6 = bf16[1,2048,768]{2,1,0:T(8,128)(2,1)S(1)} copy-done((bf16[1,2048,768]{2,1,0:T(8,128)(2,1)S(1)}, bf16[1,2048,768]{2,1,0:T(8,128)(2,1)}, u32[]{:S(2)}) %copy-start.6) | copy-done | bytes 3145752
  33.0 1.9 %copy-done.8 = bf16[1,768,2048]{2,1,0:T(8,128)(2,1)S(1)} copy-done((bf16[1,768,2048]{2,1,0:T(8,128)(2,1)S(1)}, bf16[1,768,2048]{2,1,0:T(8,128)(2,1)}, u32[]{:S(2)}) %copy-start.8) | copy-done | bytes 3145752
  34.9 5.5 %shard_map.79 = (bf16[256,2048]{1,0:T(8,128)(2,1)S(1)}, bf16[256,2048]{1,0:T(8,128)(2,1)S(1)}, bf16[320,768]{1,0:T(8,128)(2,1)S(1)}) custom-call(f32[16,512]{1,0:T(8,128)S(1)} %shard_map.78.tables, bf16[128,2048]{1,0:T(8,128)(2,1)S(1)} %copy-done.1, bf16[128,2048]{1,0:T(8,128)(2,1)S(1)} %collective-permute-done.2.refs_1_, ...), custom_call_target="tpu_custom_call" | custom-call | flops 4362076160 | bytes 13631488 | tf_op jit(solution)/shard_map/pallas_call | solution.py:164
  40.4 1.0 collective-permute-done.4
  41.4 0.6 collective-permute-start.10
  42.0 0.6 collective-permute-start.8
  42.5 1.1 collective-permute-start.9
  43.7 5.5 %shard_map.80 = (bf16[256,2048]{1,0:T(8,128)(2,1)S(1)}, bf16[128,2048]{1,0:T(8,128)(2,1)S(1)}, bf16[128,2048]{1,0:T(8,128)(2,1)S(1)}, bf16[320,768]{1,0:T(8,128)(2,1)S(1)}) custom-call(f32[16,512]{1,0:T(8,128)S(1)} %shard_map.78.tables, bf16[128,2048]{1,0:T(8,128)(2,1)S(1)} %collective-permute-done.refs_0_, ...), custom_call_target="tpu_custom_call" | custom-call | flops 4362076160 | bytes 13631488 | tf_op jit(solution)/shard_map/pallas_call | solution.py:164
  49.2 0.1 collective-permute-start.12
  49.3 6.6 %collective-permute-done.8.refs_0_ = bf16[128,2048]{1,0:T(8,128)(2,1)S(1)} collective-permute-done((bf16[128,2048]{1,0:T(8,128)(2,1)S(1)}, bf16[128,2048]{1,0:T(8,128)(2,1)S(1)}, u32[]{:S(2)}, u32[]{:S(2)}) %collective-permute-start.8) | collective-permute-done | bytes 524320 | tf_op jit(solution)/shard_map/ppermute | solution.py:210
  55.9 0.3 collective-permute-done.9.refs_1_
  56.2 1.4 %collective-permute-start.13 = (bf16[128,2048]{1,0:T(8,128)(2,1)S(1)}, bf16[128,2048]{1,0:T(8,128)(2,1)S(1)}, u32[]{:S(2)}, u32[]{:S(2)}) collective-permute-start(bf16[128,2048]{1,0:T(8,128)(2,1)S(1)} %collective-permute-done.9.refs_1_), channel_id=1, source_target_pairs={{0,4},{1,5},{2,6},{3,7},{4,0},{5,1},{6,2},{7,3},{8,12},{9,13},{10,... | collective-permute-start | bytes 1572872 | tf_op jit(solution)/shard_map/ppermute | solution.py:210
  57.6 0.1 add_convert_fusion.3
  57.8 1.5 %collective-permute-start.14 = (bf16[128,2048]{1,0:T(8,128)(2,1)S(1)}, bf16[128,2048]{1,0:T(8,128)(2,1)S(1)}, u32[]{:S(2)}, u32[]{:S(2)}) collective-permute-start(bf16[128,2048]{1,0:T(8,128)(2,1)S(1)} %add_convert_fusion.3), channel_id=1, source_target_pairs={{0,2},{1,3},{2,0},{3,1},{4,6},{5,7},{6,4},{7,5},{8,10},{9,11},{10,... | collective-permute-start | bytes 1572872 | tf_op jit(solution)/shard_map/ppermute | solution.py:210
  59.3 0.5 collective-permute-start.16
  59.8 5.6 %shard_map.81 = (bf16[256,2048]{1,0:T(8,128)(2,1)S(1)}, bf16[256,2048]{1,0:T(8,128)(2,1)S(1)}, bf16[320,768]{1,0:T(8,128)(2,1)S(1)}) custom-call(f32[16,512]{1,0:T(8,128)S(1)} %shard_map.78.tables, bf16[128,2048]{1,0:T(8,128)(2,1)S(1)} %constant_dynamic-update-slice_fusion.refs_0_, bf16[128,2048]{1,0:T(8,128)(2,1)S(1)} %collective-permute-done.9.refs_1_, ...), custom_call_target="tpu_custom_call" | custom-call | flops 4362076160 | bytes 13631488 | tf_op jit(solution)/shard_map/pallas_call | solution.py:164
  65.4 6.4 %collective-permute-done.14 = bf16[128,2048]{1,0:T(8,128)(2,1)S(1)} collective-permute-done((bf16[128,2048]{1,0:T(8,128)(2,1)S(1)}, bf16[128,2048]{1,0:T(8,128)(2,1)S(1)}, u32[]{:S(2)}, u32[]{:S(2)}) %collective-permute-start.14) | collective-permute-done | bytes 524320 | tf_op jit(solution)/shard_map/ppermute | solution.py:210
  71.9 0.1 collective-permute-start.19
  72.0 0.5 collective-permute-start.18
  72.5 0.2 add_convert_fusion.2
  72.7 0.6 collective-permute-start.20
  73.4 1.2 collective-permute-done.19
  74.7 1.5 %collective-permute-start.21 = (bf16[64,2048]{1,0:T(8,128)(2,1)S(1)}, bf16[64,2048]{1,0:T(8,128)(2,1)S(1)}, u32[]{:S(2)}, u32[]{:S(2)}) collective-permute-start(bf16[64,2048]{1,0:T(8,128)(2,1)S(1)} %add_convert_fusion.10), channel_id=1, source_target_pairs={{0,2},{1,3},{2,0},{3,1},{4,6},{5,7},{6,4},{7,5},{8,10},{9,11},{10,... | collective-permute-start | bytes 786440 | tf_op jit(solution)/shard_map/ppermute | solution.py:210
  76.2 5.5 %shard_map.82 = (bf16[256,2048]{1,0:T(8,128)(2,1)S(1)}, bf16[256,2048]{1,0:T(8,128)(2,1)S(1)}, bf16[320,768]{1,0:T(8,128)(2,1)S(1)}) custom-call(f32[16,512]{1,0:T(8,128)S(1)} %shard_map.78.tables, bf16[128,2048]{1,0:T(8,128)(2,1)S(1)} %collective-permute-done.8.refs_0_, bf16[128,2048]{1,0:T(8,128)(2,1)S(1)} %collective-permute-done.13.refs_1_, ...), custom_call_target="tpu_custom_call" | custom-call | flops 4362076160 | bytes 13631488 | tf_op jit(solution)/shard_map/pallas_call | solution.py:164
  81.7 1.4 %collective-permute-done.21 = bf16[64,2048]{1,0:T(8,128)(2,1)S(1)} collective-permute-done((bf16[64,2048]{1,0:T(8,128)(2,1)S(1)}, bf16[64,2048]{1,0:T(8,128)(2,1)S(1)}, u32[]{:S(2)}, u32[]{:S(2)}) %collective-permute-start.21) | collective-permute-done | bytes 262176 | tf_op jit(solution)/shard_map/ppermute | solution.py:210
  83.1 0.5 collective-permute-start.25
  83.6 0.5 slice.88
  84.1 1.6 %collective-permute-done.22 = bf16[256,2048]{1,0:T(8,128)(2,1)S(1)} collective-permute-done((bf16[256,2048]{1,0:T(8,128)(2,1)S(1)}, bf16[256,2048]{1,0:T(8,128)(2,1)S(1)}, u32[]{:S(2)}, u32[]{:S(2)}) %collective-permute-start.22) | collective-permute-done | bytes 1048608 | tf_op jit(solution)/shard_map/ppermute | solution.py:210
  85.8 0.1 add_convert_fusion.1
  85.9 1.5 %collective-permute-start.23 = (bf16[128,2048]{1,0:T(8,128)(2,1)S(1)}, bf16[128,2048]{1,0:T(8,128)(2,1)S(1)}, u32[]{:S(2)}, u32[]{:S(2)}) collective-permute-start(bf16[128,2048]{1,0:T(8,128)(2,1)S(1)} %add_convert_fusion.1), channel_id=1, source_target_pairs={{0,2},{1,3},{2,0},{3,1},{4,6},{5,7},{6,4},{7,5},{8,10},{9,11},{10,... | collective-permute-start | bytes 1572872 | tf_op jit(solution)/shard_map/ppermute | solution.py:210
  87.4 0.2 add_convert_fusion.8
  87.6 1.1 collective-permute-start.24
  88.7 0.1 add_convert_fusion
  88.8 13.2 %collective-permute-done.24.far_high = bf16[64,2048]{1,0:T(8,128)(2,1)S(1)} collective-permute-done((bf16[64,2048]{1,0:T(8,128)(2,1)S(1)}, bf16[64,2048]{1,0:T(8,128)(2,1)S(1)}, u32[]{:S(2)}, u32[]{:S(2)}) %collective-permute-start.24) | collective-permute-done | bytes 262176 | tf_op jit(solution)/shard_map/ppermute | solution.py:210
  102.1 0.2 add_convert_fusion.6
  102.3 0.1 collective-permute-start.26
  102.4 2.2 %collective-permute-start.27 = (bf16[64,2048]{1,0:T(8,128)(2,1)S(1)}, bf16[64,2048]{1,0:T(8,128)(2,1)S(1)}, u32[]{:S(2)}, u32[]{:S(2)}) collective-permute-start(bf16[64,2048]{1,0:T(8,128)(2,1)S(1)} %get-tuple-element.120), channel_id=1, source_target_pairs={{0,4},{1,5},{2,6},{3,7},{4,0},{5,1},{6,2},{7,3},{8,12},{9,13},{10,... | collective-permute-start | bytes 786440 | tf_op jit(solution)/shard_map/ppermute | solution.py:210
  104.6 1.0 collective-permute-start.28
  105.6 3.8 %broadcast_multiply_fusion = f32[768,768]{1,0:T(8,128)} fusion(f32[]{:T(128)} %bitcast.24, bf16[320,768]{1,0:T(8,128)(2,1)S(1)} %get-tuple-element.111, bf16[320,768]{1,0:T(8,128)(2,1)S(1)} %get-tuple-element.110, bf16[320,768]{1,0:T(8,128)(2,1)S(1)} %get-tuple-element.109, bf16[320,768]{1,0:T(8,128)(2,1)S(1)} %get-tuple-element.108), kind=kOutput, calls=%fused_computation.8 | convolution fusion | flops 1518403584 | bytes 4325380 | tf_op jit(solution)/shard_map/dot_general | solution.py:12
  109.4 6.4 %collective-permute-done.26 = bf16[64,2048]{1,0:T(8,128)(2,1)S(1)} collective-permute-done((bf16[64,2048]{1,0:T(8,128)(2,1)S(1)}, bf16[64,2048]{1,0:T(8,128)(2,1)S(1)}, u32[]{:S(2)}, u32[]{:S(2)}) %collective-permute-start.26) | collective-permute-done | bytes 262176 | tf_op jit(solution)/shard_map/ppermute | solution.py:210
  115.8 0.5 collective-permute-done.27
  116.3 0.1 add_convert_fusion.4
  116.4 0.1 collective-permute-start.31
  116.5 1.4 %collective-permute-start.29 = (bf16[128,2048]{1,0:T(8,128)(2,1)S(1)}, bf16[128,2048]{1,0:T(8,128)(2,1)S(1)}, u32[]{:S(2)}, u32[]{:S(2)}) collective-permute-start(bf16[128,2048]{1,0:T(8,128)(2,1)S(1)} %add_convert_fusion), channel_id=1, source_target_pairs={{0,2},{1,3},{2,0},{3,1},{4,6},{5,7},{6,4},{7,5},{8,10},{9,11},{10,... | collective-permute-start | bytes 1572872 | tf_op jit(solution)/shard_map/ppermute | solution.py:210
  118.0 2.2 %collective-permute-start.30 = (bf16[64,2048]{1,0:T(8,128)(2,1)S(1)}, bf16[64,2048]{1,0:T(8,128)(2,1)S(1)}, u32[]{:S(2)}, u32[]{:S(2)}) collective-permute-start(bf16[64,2048]{1,0:T(8,128)(2,1)S(1)} %add_convert_fusion.5), channel_id=1, source_target_pairs={{0,4},{1,5},{2,6},{3,7},{4,0},{5,1},{6,2},{7,3},{8,12},{9,13},{10,... | collective-permute-start | bytes 786440 | tf_op jit(solution)/shard_map/ppermute | solution.py:210
  120.2 10.5 %collective-permute-done.31.far_low = bf16[64,2048]{1,0:T(8,128)(2,1)S(1)} collective-permute-done((bf16[64,2048]{1,0:T(8,128)(2,1)S(1)}, bf16[64,2048]{1,0:T(8,128)(2,1)S(1)}, u32[]{:S(2)}, u32[]{:S(2)}) %collective-permute-start.31) | collective-permute-done | bytes 262176 | tf_op jit(solution)/shard_map/ppermute | solution.py:210
  130.8 0.7 collective-permute-done.30.near_high
  131.5 1.1 shard_map.83
  (47 shorter events, 0.3 us)
Async XLA Ops:
  0.6 24.1 %collective-permute-start = (bf16[128,2048]{1,0:T(8,128)(2,1)}, bf16[128,2048]{1,0:T(8,128)(2,1)S(1)}, u32[]{:S(2)}, u32[]{:S(2)}) collective-permute-start(bf16[128,2048]{1,0:T(8,128)(2,1)} %refs_0_.1), channel_id=1, source_target_pairs={{0,4},{1,5},{2,6},{3,7},{4,0},{5,1},{6,2},{7,3},{8,12},{9,13},{10,... | collective-permute-start | bytes 1572872 | tf_op jit(solution)/shard_map/ppermute | solution.py:210
  3.7 21.0 %collective-permute-start.2 = (bf16[128,2048]{1,0:T(8,128)(2,1)}, bf16[128,2048]{1,0:T(8,128)(2,1)S(1)}, u32[]{:S(2)}, u32[]{:S(2)}) collective-permute-start(bf16[128,2048]{1,0:T(8,128)(2,1)} %refs_0_.1), channel_id=1, source_target_pairs={{0,2},{1,3},{2,0},{3,1},{4,6},{5,7},{6,4},{7,5},{8,10},{9,11},{10,... | collective-permute-start | bytes 1572872 | tf_op jit(solution)/shard_map/ppermute | solution.py:210
  5.2 19.5 %collective-permute-start.3 = (bf16[128,2048]{1,0:T(8,128)(2,1)}, bf16[128,2048]{1,0:T(8,128)(2,1)S(1)}, u32[]{:S(2)}, u32[]{:S(2)}) collective-permute-start(bf16[128,2048]{1,0:T(8,128)(2,1)} %refs_0_.1), channel_id=1, source_target_pairs={{0,1},{1,0},{2,3},{3,2},{4,5},{5,4},{6,7},{7,6},{8,9},{9,8},{10,11... | collective-permute-start | bytes 1572872 | tf_op jit(solution)/shard_map/ppermute | solution.py:210
  5.2 1.1 copy-start
  6.3 0.7 copy-start.2
  7.0 0.7 copy-start.3
  7.8 16.9 %collective-permute-start.1 = (bf16[64,2048]{1,0:T(8,128)(2,1)S(1)}, bf16[64,2048]{1,0:T(8,128)(2,1)S(1)}, u32[]{:S(2)}, u32[]{:S(2)}) collective-permute-start(bf16[64,2048]{1,0:T(8,128)(2,1)S(1)} %get-tuple-element.61), channel_id=1, source_target_pairs={{0,8},{1,9},{2,10},{3,11},{4,12},{5,13},{6,14},{7,15},{8,0},{9,1},... | collective-permute-start | bytes 786440 | tf_op jit(solution)/shard_map/ppermute | solution.py:210
  24.7 0.7 copy-start.10
  25.4 2.7 %collective-permute-start.7 = (bf16[128,2048]{1,0:T(8,128)(2,1)S(1)}, bf16[128,2048]{1,0:T(8,128)(2,1)S(1)}, u32[]{:S(2)}, u32[]{:S(2)}) collective-permute-start(bf16[128,2048]{1,0:T(8,128)(2,1)S(1)} %collective-permute-done.2.refs_1_), channel_id=1, source_target_pairs={{0,1},{1,0},{2,3},{3,2},{4,5},{5,4},{6,7},{7,6},{8,9},{9,8},{10,11... | collective-permute-start | bytes 1572872 | tf_op jit(solution)/shard_map/ppermute | solution.py:210
  25.4 15.9 %collective-permute-start.5 = (bf16[128,2048]{1,0:T(8,128)(2,1)S(1)}, bf16[128,2048]{1,0:T(8,128)(2,1)S(1)}, u32[]{:S(2)}, u32[]{:S(2)}) collective-permute-start(bf16[128,2048]{1,0:T(8,128)(2,1)S(1)} %collective-permute-done.refs_0_), channel_id=1, source_target_pairs={{0,2},{1,3},{2,0},{3,1},{4,6},{5,7},{6,4},{7,5},{8,10},{9,11},{10,... | collective-permute-start | bytes 1572872 | tf_op jit(solution)/shard_map/ppermute | solution.py:210
  25.9 15.4 %collective-permute-start.6 = (bf16[128,2048]{1,0:T(8,128)(2,1)S(1)}, bf16[128,2048]{1,0:T(8,128)(2,1)S(1)}, u32[]{:S(2)}, u32[]{:S(2)}) collective-permute-start(bf16[128,2048]{1,0:T(8,128)(2,1)S(1)} %collective-permute-done.refs_0_), channel_id=1, source_target_pairs={{0,1},{1,0},{2,3},{3,2},{4,5},{5,4},{6,7},{7,6},{8,9},{9,8},{10,11... | collective-permute-start | bytes 1572872 | tf_op jit(solution)/shard_map/ppermute | solution.py:210
  26.3 15.1 %collective-permute-start.4 = (bf16[64,2048]{1,0:T(8,128)(2,1)S(1)}, bf16[64,2048]{1,0:T(8,128)(2,1)S(1)}, u32[]{:S(2)}, u32[]{:S(2)}) collective-permute-start(bf16[64,2048]{1,0:T(8,128)(2,1)S(1)} %get-tuple-element.64), channel_id=1, source_target_pairs={{0,8},{1,9},{2,10},{3,11},{4,12},{5,13},{6,14},{7,15},{8,0},{9,1},... | collective-permute-start | bytes 786440 | tf_op jit(solution)/shard_map/ppermute | solution.py:210
  28.1 1.0 copy-start.1
  29.2 1.9 %copy-start.4 = (bf16[1,2048,768]{2,1,0:T(8,128)(2,1)S(1)}, bf16[1,2048,768]{2,1,0:T(8,128)(2,1)}, u32[]{:S(2)}) copy-start(bf16[1,2048,768]{2,1,0:T(8,128)(2,1)} %param.9) | copy-start | bytes 9437188
  31.1 1.9 %copy-start.6 = (bf16[1,2048,768]{2,1,0:T(8,128)(2,1)S(1)}, bf16[1,2048,768]{2,1,0:T(8,128)(2,1)}, u32[]{:S(2)}) copy-start(bf16[1,2048,768]{2,1,0:T(8,128)(2,1)} %param.10) | copy-start | bytes 9437188
  33.0 1.9 %copy-start.8 = (bf16[1,768,2048]{2,1,0:T(8,128)(2,1)S(1)}, bf16[1,768,2048]{2,1,0:T(8,128)(2,1)}, u32[]{:S(2)}) copy-start(bf16[1,768,2048]{2,1,0:T(8,128)(2,1)} %param.11) | copy-start | bytes 9437188
  34.9 6.5 %copy-start.11 = (bf16[64,2048]{1,0:T(8,128)(2,1)S(1)}, bf16[64,2048]{1,0:T(8,128)(2,1)}, u32[]{:S(2)}) copy-start(bf16[64,2048]{1,0:T(8,128)(2,1)} %copy-done.10) | copy-start | bytes 786436
  34.9 8.8 %copy-start.5 = (bf16[1,2048,768]{2,1,0:T(8,128)(2,1)S(1)}, bf16[1,2048,768]{2,1,0:T(8,128)(2,1)}, u32[]{:S(2)}) copy-start(bf16[1,2048,768]{2,1,0:T(8,128)(2,1)} %param.9) | copy-start | bytes 9437188
  34.9 8.8 %copy-start.7 = (bf16[1,2048,768]{2,1,0:T(8,128)(2,1)S(1)}, bf16[1,2048,768]{2,1,0:T(8,128)(2,1)}, u32[]{:S(2)}) copy-start(bf16[1,2048,768]{2,1,0:T(8,128)(2,1)} %param.10) | copy-start | bytes 9437188
  34.9 8.8 %copy-start.9 = (bf16[1,768,2048]{2,1,0:T(8,128)(2,1)S(1)}, bf16[1,768,2048]{2,1,0:T(8,128)(2,1)}, u32[]{:S(2)}) copy-start(bf16[1,768,2048]{2,1,0:T(8,128)(2,1)} %param.11) | copy-start | bytes 9437188
  41.3 2.3 %collective-permute-start.11 = (bf16[128,2048]{1,0:T(8,128)(2,1)S(1)}, bf16[128,2048]{1,0:T(8,128)(2,1)S(1)}, u32[]{:S(2)}, u32[]{:S(2)}) collective-permute-start(bf16[128,2048]{1,0:T(8,128)(2,1)S(1)} %collective-permute-done.5.refs_1_), channel_id=1, source_target_pairs={{0,1},{1,0},{2,3},{3,2},{4,5},{5,4},{6,7},{7,6},{8,9},{9,8},{10,11... | collective-permute-start | bytes 1572872 | tf_op jit(solution)/shard_map/ppermute | solution.py:210
  41.4 7.8 %collective-permute-start.10 = (bf16[128,2048]{1,0:T(8,128)(2,1)S(1)}, bf16[128,2048]{1,0:T(8,128)(2,1)S(1)}, u32[]{:S(2)}, u32[]{:S(2)}) collective-permute-start(bf16[128,2048]{1,0:T(8,128)(2,1)S(1)} %constant_dynamic-update-slice_fusion.refs_0_), channel_id=1, source_target_pairs={{0,1},{1,0},{2,3},{3,2},{4,5},{5,4},{6,7},{7,6},{8,9},{9,8},{10,11... | collective-permute-start | bytes 1572872 | tf_op jit(solution)/shard_map/ppermute | solution.py:210
  42.0 13.9 %collective-permute-start.8 = (bf16[128,2048]{1,0:T(8,128)(2,1)S(1)}, bf16[128,2048]{1,0:T(8,128)(2,1)S(1)}, u32[]{:S(2)}, u32[]{:S(2)}) collective-permute-start(bf16[128,2048]{1,0:T(8,128)(2,1)S(1)} %constant_dynamic-update-slice_fusion.refs_0_), channel_id=1, source_target_pairs={{0,4},{1,5},{2,6},{3,7},{4,0},{5,1},{6,2},{7,3},{8,12},{9,13},{10,... | collective-permute-start | bytes 1572872 | tf_op jit(solution)/shard_map/ppermute | solution.py:210
  42.5 13.6 %collective-permute-start.9 = (bf16[128,2048]{1,0:T(8,128)(2,1)S(1)}, bf16[128,2048]{1,0:T(8,128)(2,1)S(1)}, u32[]{:S(2)}, u32[]{:S(2)}) collective-permute-start(bf16[128,2048]{1,0:T(8,128)(2,1)S(1)} %constant_dynamic-update-slice_fusion.refs_0_), channel_id=1, source_target_pairs={{0,2},{1,3},{2,0},{3,1},{4,6},{5,7},{6,4},{7,5},{8,10},{9,11},{10,... | collective-permute-start | bytes 1572872 | tf_op jit(solution)/shard_map/ppermute | solution.py:210
  49.2 7.0 %collective-permute-start.12 = (bf16[128,2048]{1,0:T(8,128)(2,1)S(1)}, bf16[128,2048]{1,0:T(8,128)(2,1)S(1)}, u32[]{:S(2)}, u32[]{:S(2)}) collective-permute-start(bf16[128,2048]{1,0:T(8,128)(2,1)S(1)} %get-tuple-element.80), channel_id=1, source_target_pairs={{0,1},{1,0},{2,3},{3,2},{4,5},{5,4},{6,7},{7,6},{8,9},{9,8},{10,11... | collective-permute-start | bytes 1572872 | tf_op jit(solution)/shard_map/ppermute | solution.py:210
  56.2 3.6 %collective-permute-start.17 = (bf16[128,2048]{1,0:T(8,128)(2,1)S(1)}, bf16[128,2048]{1,0:T(8,128)(2,1)S(1)}, u32[]{:S(2)}, u32[]{:S(2)}) collective-permute-start(bf16[128,2048]{1,0:T(8,128)(2,1)S(1)} %collective-permute-done.9.refs_1_), channel_id=1, source_target_pairs={{0,1},{1,0},{2,3},{3,2},{4,5},{5,4},{6,7},{7,6},{8,9},{9,8},{10,11... | collective-permute-start | bytes 1572872 | tf_op jit(solution)/shard_map/ppermute | solution.py:210
  56.2 15.7 %collective-permute-start.13 = (bf16[128,2048]{1,0:T(8,128)(2,1)S(1)}, bf16[128,2048]{1,0:T(8,128)(2,1)S(1)}, u32[]{:S(2)}, u32[]{:S(2)}) collective-permute-start(bf16[128,2048]{1,0:T(8,128)(2,1)S(1)} %collective-permute-done.9.refs_1_), channel_id=1, source_target_pairs={{0,4},{1,5},{2,6},{3,7},{4,0},{5,1},{6,2},{7,3},{8,12},{9,13},{10,... | collective-permute-start | bytes 1572872 | tf_op jit(solution)/shard_map/ppermute | solution.py:210
  57.8 14.1 %collective-permute-start.14 = (bf16[128,2048]{1,0:T(8,128)(2,1)S(1)}, bf16[128,2048]{1,0:T(8,128)(2,1)S(1)}, u32[]{:S(2)}, u32[]{:S(2)}) collective-permute-start(bf16[128,2048]{1,0:T(8,128)(2,1)S(1)} %add_convert_fusion.3), channel_id=1, source_target_pairs={{0,2},{1,3},{2,0},{3,1},{4,6},{5,7},{6,4},{7,5},{8,10},{9,11},{10,... | collective-permute-start | bytes 1572872 | tf_op jit(solution)/shard_map/ppermute | solution.py:210
  59.3 12.6 %collective-permute-start.15 = (bf16[128,2048]{1,0:T(8,128)(2,1)S(1)}, bf16[128,2048]{1,0:T(8,128)(2,1)S(1)}, u32[]{:S(2)}, u32[]{:S(2)}) collective-permute-start(bf16[128,2048]{1,0:T(8,128)(2,1)S(1)} %collective-permute-done.8.refs_0_), channel_id=1, source_target_pairs={{0,1},{1,0},{2,3},{3,2},{4,5},{5,4},{6,7},{7,6},{8,9},{9,8},{10,11... | collective-permute-start | bytes 1572872 | tf_op jit(solution)/shard_map/ppermute | solution.py:210
  59.3 12.6 %collective-permute-start.16 = (bf16[128,2048]{1,0:T(8,128)(2,1)S(1)}, bf16[128,2048]{1,0:T(8,128)(2,1)S(1)}, u32[]{:S(2)}, u32[]{:S(2)}) collective-permute-start(bf16[128,2048]{1,0:T(8,128)(2,1)S(1)} %get-tuple-element.85), channel_id=1, source_target_pairs={{0,1},{1,0},{2,3},{3,2},{4,5},{5,4},{6,7},{7,6},{8,9},{9,8},{10,11... | collective-permute-start | bytes 1572872 | tf_op jit(solution)/shard_map/ppermute | solution.py:210
  71.9 2.7 %collective-permute-start.19 = (bf16[256,2048]{1,0:T(8,128)(2,1)S(1)}, bf16[256,2048]{1,0:T(8,128)(2,1)S(1)}, u32[]{:S(2)}, u32[]{:S(2)}) collective-permute-start(bf16[256,2048]{1,0:T(8,128)(2,1)S(1)} %get-tuple-element.95), channel_id=1, source_target_pairs={{0,1},{1,0},{2,3},{3,2},{4,5},{5,4},{6,7},{7,6},{8,9},{9,8},{10,11... | collective-permute-start | bytes 3145736 | tf_op jit(solution)/shard_map/ppermute | solution.py:210
  72.0 4.3 %collective-permute-start.18 = (bf16[128,2048]{1,0:T(8,128)(2,1)S(1)}, bf16[128,2048]{1,0:T(8,128)(2,1)S(1)}, u32[]{:S(2)}, u32[]{:S(2)}) collective-permute-start(bf16[128,2048]{1,0:T(8,128)(2,1)S(1)} %collective-permute-done.13.refs_1_), channel_id=1, source_target_pairs={{0,1},{1,0},{2,3},{3,2},{4,5},{5,4},{6,7},{7,6},{8,9},{9,8},{10,11... | collective-permute-start | bytes 1572872 | tf_op jit(solution)/shard_map/ppermute | solution.py:210
  72.7 9.0 %collective-permute-start.20 = (bf16[64,2048]{1,0:T(8,128)(2,1)S(1)}, bf16[64,2048]{1,0:T(8,128)(2,1)S(1)}, u32[]{:S(2)}, u32[]{:S(2)}) collective-permute-start(bf16[64,2048]{1,0:T(8,128)(2,1)S(1)} %slice.92), channel_id=1, source_target_pairs={{0,4},{1,5},{2,6},{3,7},{4,0},{5,1},{6,2},{7,3},{8,12},{9,13},{10,... | collective-permute-start | bytes 786440 | tf_op jit(solution)/shard_map/ppermute | solution.py:210
  74.7 8.4 %collective-permute-start.21 = (bf16[64,2048]{1,0:T(8,128)(2,1)S(1)}, bf16[64,2048]{1,0:T(8,128)(2,1)S(1)}, u32[]{:S(2)}, u32[]{:S(2)}) collective-permute-start(bf16[64,2048]{1,0:T(8,128)(2,1)S(1)} %add_convert_fusion.10), channel_id=1, source_target_pairs={{0,2},{1,3},{2,0},{3,1},{4,6},{5,7},{6,4},{7,5},{8,10},{9,11},{10,... | collective-permute-start | bytes 786440 | tf_op jit(solution)/shard_map/ppermute | solution.py:210
  83.1 2.7 %collective-permute-start.22 = (bf16[256,2048]{1,0:T(8,128)(2,1)S(1)}, bf16[256,2048]{1,0:T(8,128)(2,1)S(1)}, u32[]{:S(2)}, u32[]{:S(2)}) collective-permute-start(bf16[256,2048]{1,0:T(8,128)(2,1)S(1)} %get-tuple-element.100), channel_id=1, source_target_pairs={{0,1},{1,0},{2,3},{3,2},{4,5},{5,4},{6,7},{7,6},{8,9},{9,8},{10,11... | collective-permute-start | bytes 3145736 | tf_op jit(solution)/shard_map/ppermute | solution.py:210
  83.1 5.6 %collective-permute-start.25 = (bf16[256,2048]{1,0:T(8,128)(2,1)S(1)}, bf16[256,2048]{1,0:T(8,128)(2,1)S(1)}, u32[]{:S(2)}, u32[]{:S(2)}) collective-permute-start(bf16[256,2048]{1,0:T(8,128)(2,1)S(1)} %get-tuple-element.104), channel_id=1, source_target_pairs={{0,1},{1,0},{2,3},{3,2},{4,5},{5,4},{6,7},{7,6},{8,9},{9,8},{10,11... | collective-permute-start | bytes 3145736 | tf_op jit(solution)/shard_map/ppermute | solution.py:210
  85.9 16.2 %collective-permute-start.23 = (bf16[128,2048]{1,0:T(8,128)(2,1)S(1)}, bf16[128,2048]{1,0:T(8,128)(2,1)S(1)}, u32[]{:S(2)}, u32[]{:S(2)}) collective-permute-start(bf16[128,2048]{1,0:T(8,128)(2,1)S(1)} %add_convert_fusion.1), channel_id=1, source_target_pairs={{0,2},{1,3},{2,0},{3,1},{4,6},{5,7},{6,4},{7,5},{8,10},{9,11},{10,... | collective-permute-start | bytes 1572872 | tf_op jit(solution)/shard_map/ppermute | solution.py:210
  87.6 14.4 %collective-permute-start.24 = (bf16[64,2048]{1,0:T(8,128)(2,1)S(1)}, bf16[64,2048]{1,0:T(8,128)(2,1)S(1)}, u32[]{:S(2)}, u32[]{:S(2)}) collective-permute-start(bf16[64,2048]{1,0:T(8,128)(2,1)S(1)} %get-tuple-element.123), channel_id=1, source_target_pairs={{0,8},{1,9},{2,10},{3,11},{4,12},{5,13},{6,14},{7,15},{8,0},{9,1},... | collective-permute-start | bytes 786440 | tf_op jit(solution)/shard_map/ppermute | solution.py:210
  102.3 13.5 %collective-permute-start.26 = (bf16[64,2048]{1,0:T(8,128)(2,1)S(1)}, bf16[64,2048]{1,0:T(8,128)(2,1)S(1)}, u32[]{:S(2)}, u32[]{:S(2)}) collective-permute-start(bf16[64,2048]{1,0:T(8,128)(2,1)S(1)} %get-tuple-element.121), channel_id=1, source_target_pairs={{0,8},{1,9},{2,10},{3,11},{4,12},{5,13},{6,14},{7,15},{8,0},{9,1},... | collective-permute-start | bytes 786440 | tf_op jit(solution)/shard_map/ppermute | solution.py:210
  102.4 13.9 %collective-permute-start.27 = (bf16[64,2048]{1,0:T(8,128)(2,1)S(1)}, bf16[64,2048]{1,0:T(8,128)(2,1)S(1)}, u32[]{:S(2)}, u32[]{:S(2)}) collective-permute-start(bf16[64,2048]{1,0:T(8,128)(2,1)S(1)} %get-tuple-element.120), channel_id=1, source_target_pairs={{0,4},{1,5},{2,6},{3,7},{4,0},{5,1},{6,2},{7,3},{8,12},{9,13},{10,... | collective-permute-start | bytes 786440 | tf_op jit(solution)/shard_map/ppermute | solution.py:210
  104.6 11.7 %collective-permute-start.28 = (bf16[64,2048]{1,0:T(8,128)(2,1)S(1)}, bf16[64,2048]{1,0:T(8,128)(2,1)S(1)}, u32[]{:S(2)}, u32[]{:S(2)}) collective-permute-start(bf16[64,2048]{1,0:T(8,128)(2,1)S(1)} %get-tuple-element.106), channel_id=1, source_target_pairs={{0,2},{1,3},{2,0},{3,1},{4,6},{5,7},{6,4},{7,5},{8,10},{9,11},{10,... | collective-permute-start | bytes 786440 | tf_op jit(solution)/shard_map/ppermute | solution.py:210
  116.4 14.3 %collective-permute-start.31 = (bf16[64,2048]{1,0:T(8,128)(2,1)S(1)}, bf16[64,2048]{1,0:T(8,128)(2,1)S(1)}, u32[]{:S(2)}, u32[]{:S(2)}) collective-permute-start(bf16[64,2048]{1,0:T(8,128)(2,1)S(1)} %add_convert_fusion.4), channel_id=1, source_target_pairs={{0,8},{1,9},{2,10},{3,11},{4,12},{5,13},{6,14},{7,15},{8,0},{9,1},... | collective-permute-start | bytes 786440 | tf_op jit(solution)/shard_map/ppermute | solution.py:210
  116.5 14.9 %collective-permute-start.29 = (bf16[128,2048]{1,0:T(8,128)(2,1)S(1)}, bf16[128,2048]{1,0:T(8,128)(2,1)S(1)}, u32[]{:S(2)}, u32[]{:S(2)}) collective-permute-start(bf16[128,2048]{1,0:T(8,128)(2,1)S(1)} %add_convert_fusion), channel_id=1, source_target_pairs={{0,2},{1,3},{2,0},{3,1},{4,6},{5,7},{6,4},{7,5},{8,10},{9,11},{10,... | collective-permute-start | bytes 1572872 | tf_op jit(solution)/shard_map/ppermute | solution.py:210
  118.0 13.5 %collective-permute-start.30 = (bf16[64,2048]{1,0:T(8,128)(2,1)S(1)}, bf16[64,2048]{1,0:T(8,128)(2,1)S(1)}, u32[]{:S(2)}, u32[]{:S(2)}) collective-permute-start(bf16[64,2048]{1,0:T(8,128)(2,1)S(1)} %add_convert_fusion.5), channel_id=1, source_target_pairs={{0,4},{1,5},{2,6},{3,7},{4,0},{5,1},{6,2},{7,3},{8,12},{9,13},{10,... | collective-permute-start | bytes 786440 | tf_op jit(solution)/shard_map/ppermute | solution.py:210

commit v18 on v17

--- a/solution.py
+++ b/solution.py
@@ -75,7 +75,7 @@
     return total.astype(jnp.bfloat16)
 
 
-def ranks_kernel(capacity, spots, weight, tables, ranks):
+def ranks_kernel(capacity, spots, weight, tables, ranks, chip_ranks):
     blocks, tok = weight.shape
     planes = blocks // 4
     named = (weight[...] >= 0.0).astype(jnp.float32)
@@ -92,13 +92,20 @@
     first = (column < row // 4 * 4).astype(jnp.float32)
     start = jnp.dot(first, totals, preferred_element_type=jnp.float32)
     ranks[...] = jnp.where(kept, rank - start, -1.0)
+    first = (column < row // 2 * 2).astype(jnp.float32)
+    start = jnp.dot(first, totals, preferred_element_type=jnp.float32)
+    chip_ranks[...] = jnp.where(kept, rank - start, -1.0)
+    for i in range(4):
+        span = pl.ds(i * tok, tok)
+        tables[pl.ds(2 * planes, 1), span] = chip_ranks[pl.ds(spots[4 * planes - 4 + i], 1), :]
     for k in range(planes):
         for i in range(4):
             span = pl.ds(i * tok, tok)
             tables[pl.ds(k, 1), span] = ranks[pl.ds(spots[4 * k + i], 1), :]
             tables[pl.ds(planes + k, 1), span] = weight[pl.ds(spots[4 * k + i], 1), :]
     count = jnp.minimum(jnp.sum(totals[:, :1], axis=0, keepdims=True), float(capacity))
-    tables[2 * planes :, :] = jnp.broadcast_to(2.0 / count, tables[2 * planes :, :].shape)
+    rest = (tables.shape[0] - 2 * planes - 1, tables.shape[1])
+    tables[2 * planes + 1 :, :] = jnp.broadcast_to(2.0 / count, rest)
 
 
 def ranks_pass(capacity, spots, weight):
@@ -109,20 +116,27 @@
         out_shape=jax.ShapeDtypeStruct((blocks // 4 * 2 + 8, 4 * tok), jnp.float32),
         in_specs=[pl.BlockSpec(memory_space=pltpu.SMEM), vmem],
         out_specs=vmem,
-        scratch_shapes=[pltpu.VMEM(weight.shape, jnp.float32)],
+        scratch_shapes=[pltpu.VMEM(weight.shape, jnp.float32)] * 2,
         compiler_params=pltpu.CompilerParams(vmem_limit_bytes=4 * 1024 * 1024),
     )(spots, weight)
 
 
-def plane_kernel(k, gives, tables, *refs):
+def plane_kernel(k, picked, gives, tables, *refs):
     *xs, w_gate, w_up, w_down, keep = refs[: -gives - 2]
     *gives, act, rows = refs[-gives - 2 :]
     slots, hidden = act.shape
     features = rows.shape[1]
     half, width = keep.shape[0], tables.shape[1]
     wide, cut = 256, 512
-    place = tables[pl.ds(k, 1), :]
+    place = tables[pl.ds(8 if picked else k, 1), :]
     share = tables[pl.ds(4 + k, 1), :]
+    if picked:
+        tok = width // 4
+        place, share = (
+            jnp.concatenate([row[:, i * tok : (i + 1) * tok] for i in picked], axis=1)
+            for row in (place, share)
+        )
+        width = 2 * tok
     slot = lax.broadcasted_iota(jnp.int32, (slots, width), 0).astype(jnp.float32)
     hits = slot == place
     scale = jnp.sum(jnp.where(hits, share, 0.0), axis=1, keepdims=True)
@@ -149,20 +163,20 @@
             start += give.shape[0]
 
 
-def plane_pass(k, tables, xs, w_gate, w_up, w_down, slots, pieces=None):
+def plane_pass(k, tables, xs, w_gate, w_up, w_down, slots, pieces=None, picked=None):
     tok, features = xs[0].shape
     hidden = w_gate.shape[1]
-    rows = 4 * slots
-    pieces = pieces or (2 * tok,)
-    outs = tuple(
-        jax.ShapeDtypeStruct((some, features), jnp.bfloat16) for some in (2 * tok, *pieces)
-    )
+    blocks = 2 if picked else 4
+    rows = blocks * slots
+    half = blocks // 2 * tok
+    pieces = pieces or (half,)
+    outs = tuple(jax.ShapeDtypeStruct((some, features), jnp.bfloat16) for some in (half, *pieces))
     outs += (jax.ShapeDtypeStruct((rows, hidden), jnp.bfloat16),)
     vmem = pl.BlockSpec(memory_space=pltpu.VMEM)
-    flops = 2 * rows * (3 * features * hidden + 8 * tok * features)
-    moved = 2 * (3 * features * hidden + 8 * tok * features)
+    flops = 2 * rows * (3 * features * hidden + 2 * blocks * tok * features)
+    moved = 2 * (3 * features * hidden + 2 * blocks * tok * features)
     return pl.pallas_call(
-        functools.partial(plane_kernel, k, len(pieces)),
+        functools.partial(plane_kernel, k, picked, len(pieces)),
         out_shape=outs,
         in_specs=[vmem] * (len(xs) + 4),
         out_specs=[vmem] * len(outs),
@@ -172,6 +186,38 @@
             flops=flops, bytes_accessed=moved, transcendentals=rows * hidden
         ),
     )(tables, *xs, w_gate, w_up, w_down)
+
+
+def gram_kernel(tables, *refs):
+    *acts, gram = refs
+    wide = 256
+    scale = tables[9:10, :1]
+    rows = jnp.concatenate([act[...] for act in acts], axis=0)
+    for i in range(gram.shape[0] // wide):
+        some = rows[:, i * wide : (i + 1) * wide]
+        gram[pl.ds(i * wide, wide), :] = gram_of_two(some, rows) * scale
+
+
+def gram_of_two(left, right):
+    return lax.dot_general(left, right, (((0,), (0,)), ((), ())), preferred_element_type=jnp.float32)
+
+
+def gram_pass(tables, *acts):
+    hidden = acts[0].shape[1]
+    rows = sum(act.shape[0] for act in acts)
+    vmem = pl.BlockSpec(memory_space=pltpu.VMEM)
+    return pl.pallas_call(
+        gram_kernel,
+        out_shape=jax.ShapeDtypeStruct((hidden, hidden), jnp.float32),
+        in_specs=[vmem] * (len(acts) + 1),
+        out_specs=vmem,
+        compiler_params=pltpu.CompilerParams(vmem_limit_bytes=16 * 1024 * 1024),
+        cost_estimate=pl.CostEstimate(
+            flops=2 * rows * hidden * hidden,
+            bytes_accessed=4 * hidden * hidden + 2 * rows * hidden,
+            transcendentals=0,
+        ),
+    )(tables, *acts)
 
 
 def mix_kernel(keep, got, side, near_low, near_high, far_low, far_high, mixed):
@@ -226,8 +272,8 @@
         ]
     ).astype(jnp.int32)
 
-    def expert(k, *xs, pieces=None):
-        return plane_pass(k, tables, xs, w_gate, w_up, w_down, slots, pieces)
+    def expert(k, *xs, pieces=None, picked=None):
+        return plane_pass(k, tables, xs, w_gate, w_up, w_down, slots, pieces, picked)
 
     mine, a0_low, a0_high = prepare_pass(routes, probs, tokens, size)
     a0 = tokens
@@ -263,36 +309,39 @@
     got1 = sibling(give1)
     d2 = sibling(b2)
     c3 = sibling(a3)
-    keep2, give2, act2 = expert(2, a2, b2, c2, d2)
-    b3, came1, c3, got1, keep2, give2, act2 = together(b3, came1, c3, got1, keep2, give2, act2)
+    keep2, give2, give2_side, act2 = expert(2, a2, b2, c2, d2, pieces=(tok, tok))
+    got2_side = sibling(give2_side)
+    keep3, give3, act3 = expert(3, a3, c3, picked=(0, 2))
+    b3, came1, got1, got2_side, keep2, give2, act2, keep3, give3, act3 = together(
+        b3, came1, got1, got2_side, keep2, give2, act2, keep3, give3, act3
+    )
     d3 = sibling(b3)
     near1 = summed(keep1[:tok], got1, came1)
 
-    def own(keep, got, start, stop, *more):
-        return summed(keep[start:stop], got[start:stop], *more)
-
+    side_high = column(summed(keep2[tok + half :], got2_side[half:]))
+    got0, got2, got3 = sibling(give0), sibling(give2), sibling(give3)
+    keep3_side, give3_side, act4 = expert(3, b3, d3, picked=(1, 3))
+    keep3_side, give3_side, act4, got0, got2, got3, side_high, near1 = together(
+        keep3_side, give3_side, act4, got0, got2, got3, side_high, near1
+    )
+    far2_high = far(summed(keep2[half:tok], got2[half:], side_high))
+    got3_side = sibling(give3_side)
+    came3_low = column(summed(keep3_side[:half], got3_side[:half]))
+    came3_high = column(summed(keep3_side[half:], got3_side[half:]))
     near1_low = pair(near1[:half])
-    got2 = sibling(give2)
-    side_high = column(own(keep2, got2, tok + half, 2 * tok))
-    keep3, give3, act3 = expert(3, a3, b3, c3, d3)
-    keep3, give3, act3, got2, near1, near1_low, side_high = together(
-        keep3, give3, act3, got2, near1, near1_low, side_high
-    )
-    far2_high = far(own(keep2, got2, half, tok, side_high))
-    got0 = sibling(give0)
-    got3 = sibling(give3)
-    came3 = column(own(keep3, got3, tok, 2 * tok))
-    side0 = own(keep0, got0, tok, 2 * tok)
-    side2 = own(keep2, got2, tok, tok + half)
-    came3, far2_high, side0, side2 = together(came3, far2_high, side0, side2)
-    far3_high = far(own(keep3, got3, half, tok, came3[half:]))
-    pair3_low = pair(own(keep3, got3, 0, half, came3[:half]))
+    side0 = summed(keep0[tok:], got0[tok:])
+    side2 = summed(keep2[tok : tok + half], got2_side[:half])
+    came3_low, came3_high, far2_high, near1_low, side0, side2 = together(
+        came3_low, came3_high, far2_high, near1_low, side0, side2
+    )
+    far3_high = far(summed(keep3[half:], got3[half:], came3_high))
+    pair3_low = pair(summed(keep3[:half], got3[:half], came3_low))
     side_low = column(side2)
-    gram = gram_of(jnp.concatenate([act0, act1, act2, act3], axis=0)) * tables[8, 0]
+    gram = gram_pass(tables, act0, act1, act2, act3, act4)
     far3_high, pair3_low, side_low, side0, gram = together(
         far3_high, pair3_low, side_low, side0, gram
     )
-    far2_low = far(own(keep2, got2, 0, half, pair3_low, side_low))
+    far2_low = far(summed(keep2[:half], got2[:half], pair3_low, side_low))
     near1_high = pair(summed(near1[half:], far3_high))
     last0 = column(side0)
     mixed = mix_pass(

time: 133 us -> 129 us (0.970)
  waiting for transfers between devices: 50 us -> 45 us
  matrix products: 3.8 us -> 0 us
  Pallas kernels: 24 us -> 27.1 us
  starting transfers between devices: 27.8 us -> 30.1 us
    ppermute x32 -> x35, waiting for transfers between devices: 50 us -> 45 us  [swapped(): return lax.ppermute(array, 'expert', [(i, i ^ bit) for i in range(size)])]
    dot_general x1 -> x0, matrix products: 3.8 us -> none  [gram_of(): lax.dot_general(rows, rows, (((0,), (0,)), ((), ())), preferred_element_t...]
    pallas_call x4 -> x6, Pallas kernels: 22 us -> 25.1 us  [the longest x5 22 us: plane_pass(): pl.pallas_call(functools.partial(plane_kernel, k, picked, len(pieces)), o...]
    ppermute x32 -> x35, starting transfers between devices: 27.8 us -> 30.1 us  [swapped(): return lax.ppermute(array, 'expert', [(i, i ^ bit) for i in range(size)])]
  transfers between devices with their start and end apart: 32 -> 35, of which waited for: 12 -> 10; matrix products, arithmetic and copies ran while one was open for 4% -> 1% of each run, Pallas kernels for 17% -> 20%
where the time goes in v18:
time: 129 us
  waiting for transfers between devices  45 us (35%)
  starting transfers between devices  30.1 us (23%)
  Pallas kernels  27.1 us (21%)
  blocking collectives  14.2 us (11%)
  local copies, waits for them, and re-layouts  9.98 us (8%)
    ppermute x35, waiting for transfers between devices, swapped(): return lax.ppermute(array, 'expert', [(i, i ^ bit) for i in range(size)])  45 us
    ppermute x35, starting transfers between devices, swapped(): return lax.ppermute(array, 'expert', [(i, i ^ bit) for i in range(size)])  30.1 us
    pallas_call x5, Pallas kernels, plane_pass(): pl.pallas_call(functools.partial(plane_kernel, k, picked, len(pieces)), o...  22 us
    all_to_all x1, blocking collectives, staged(): lax.all_to_all(mine, 'expert', split_axis=0, concat_axis=0, tiled=True)  14.2 us
    unnamed x25, local copies, waits for them, and re-layouts  9.86 us
    pallas_call x1, Pallas kernels, gram_pass(): pl.pallas_call(gram_kernel, out_shape=jax.ShapeDtypeStruct((hidden, hidde...  3.14 us
  transfers between devices with their start and end apart: 35, of which 10 were waited for; matrix products, arithmetic and copies ran while one was open for 1% of the time, Pallas kernels for 20%

profile of v18, /device:TPU:0, one launch (start us, length us, event | category | flops | bytes accessed | tf_op | source)
XLA Modules:
  0.0 128.7 jit_solution(12814513577984451202)
XLA Ops:
  0.6 3.1 %collective-permute-start = (bf16[128,2048]{1,0:T(8,128)(2,1)}, bf16[128,2048]{1,0:T(8,128)(2,1)S(1)}, u32[]{:S(2)}, u32[]{:S(2)}) collective-permute-start(bf16[128,2048]{1,0:T(8,128)(2,1)} %refs_0_.1), channel_id=1, source_target_pairs={{0,4},{1,5},{2,6},{3,7},{4,0},{5,1},{6,2},{7,3},{8,12},{9,13},{10,... | collective-permute-start | bytes 1572872 | tf_op jit(solution)/shard_map/ppermute | solution.py:256
  3.7 1.5 %collective-permute-start.2 = (bf16[128,2048]{1,0:T(8,128)(2,1)}, bf16[128,2048]{1,0:T(8,128)(2,1)S(1)}, u32[]{:S(2)}, u32[]{:S(2)}) collective-permute-start(bf16[128,2048]{1,0:T(8,128)(2,1)} %refs_0_.1), channel_id=1, source_target_pairs={{0,2},{1,3},{2,0},{3,1},{4,6},{5,7},{6,4},{7,5},{8,10},{9,11},{10,... | collective-permute-start | bytes 1572872 | tf_op jit(solution)/shard_map/ppermute | solution.py:256
  5.2 1.1 copy-done.6
  6.3 0.7 copy-done.8
  7.0 0.7 copy-done.9
  7.7 0.1 shard_map.77
  7.8 2.7 %collective-permute-start.1 = (bf16[64,2048]{1,0:T(8,128)(2,1)S(1)}, bf16[64,2048]{1,0:T(8,128)(2,1)S(1)}, u32[]{:S(2)}, u32[]{:S(2)}) collective-permute-start(bf16[64,2048]{1,0:T(8,128)(2,1)S(1)} %get-tuple-element.71), channel_id=1, source_target_pairs={{0,8},{1,9},{2,10},{3,11},{4,12},{5,13},{6,14},{7,15},{8,0},{9,1},... | collective-permute-start | bytes 786440 | tf_op jit(solution)/shard_map/ppermute | solution.py:256
  10.5 14.2 %all_to_all.12 = f32[16,1,128]{2,1,0:T(1,128)S(1)} all-to-all(f32[16,1,128]{2,1,0:T(1,128)S(1)} %bitcast.42), channel_id=1, replica_groups=mesh['parts'=2,'expert'=16] {'expert'}, dimensions={0} | all-to-all | bytes 16384 | tf_op jit(solution)/shard_map/all_to_all | solution.py:285
  24.8 0.7 copy-done.10
  25.4 0.5 collective-permute-start.5
  25.9 0.2 collective-permute-start.6
  26.2 0.1 stack.67.spots
  26.3 1.1 collective-permute-start.4
  27.4 0.7 shard_map.78.tables
  28.2 1.9 %copy-done = bf16[1,2048,768]{2,1,0:T(8,128)(2,1)S(1)} copy-done((bf16[1,2048,768]{2,1,0:T(8,128)(2,1)S(1)}, bf16[1,2048,768]{2,1,0:T(8,128)(2,1)}, u32[]{:S(2)}) %copy-start) | copy-done | bytes 3145752
  30.0 1.9 %copy-done.2 = bf16[1,2048,768]{2,1,0:T(8,128)(2,1)S(1)} copy-done((bf16[1,2048,768]{2,1,0:T(8,128)(2,1)S(1)}, bf16[1,2048,768]{2,1,0:T(8,128)(2,1)}, u32[]{:S(2)}) %copy-start.2) | copy-done | bytes 3145752
  31.9 1.9 %copy-done.4 = bf16[1,768,2048]{2,1,0:T(8,128)(2,1)S(1)} copy-done((bf16[1,768,2048]{2,1,0:T(8,128)(2,1)S(1)}, bf16[1,768,2048]{2,1,0:T(8,128)(2,1)}, u32[]{:S(2)}) %copy-start.4) | copy-done | bytes 3145752
  33.8 1.0 copy-done.7
  34.9 5.5 %shard_map.79 = (bf16[256,2048]{1,0:T(8,128)(2,1)S(1)}, bf16[256,2048]{1,0:T(8,128)(2,1)S(1)}, bf16[320,768]{1,0:T(8,128)(2,1)S(1)}) custom-call(f32[16,512]{1,0:T(8,128)S(1)} %shard_map.78.tables, bf16[128,2048]{1,0:T(8,128)(2,1)S(1)} %copy-done.7, bf16[128,2048]{1,0:T(8,128)(2,1)S(1)} %collective-permute-done.2.refs_1_, ...), custom_call_target="tpu_custom_call" | custom-call | flops 4362076160 | bytes 13631488 | tf_op jit(solution)/shard_map/pallas_call | solution.py:178
  40.4 1.0 collective-permute-done.4
  41.4 0.6 collective-permute-start.10
  42.0 0.6 collective-permute-start.8
  42.6 1.1 collective-permute-start.9
  43.7 5.5 %shard_map.80 = (bf16[256,2048]{1,0:T(8,128)(2,1)S(1)}, bf16[128,2048]{1,0:T(8,128)(2,1)S(1)}, bf16[128,2048]{1,0:T(8,128)(2,1)S(1)}, bf16[320,768]{1,0:T(8,128)(2,1)S(1)}) custom-call(f32[16,512]{1,0:T(8,128)S(1)} %shard_map.78.tables, bf16[128,2048]{1,0:T(8,128)(2,1)S(1)} %collective-permute-done.refs_0_, ...), custom_call_target="tpu_custom_call" | custom-call | flops 4362076160 | bytes 13631488 | tf_op jit(solution)/shard_map/pallas_call | solution.py:178
  49.3 6.6 %collective-permute-done.8.refs_0_ = bf16[128,2048]{1,0:T(8,128)(2,1)S(1)} collective-permute-done((bf16[128,2048]{1,0:T(8,128)(2,1)S(1)}, bf16[128,2048]{1,0:T(8,128)(2,1)S(1)}, u32[]{:S(2)}, u32[]{:S(2)}) %collective-permute-start.8) | collective-permute-done | bytes 524320 | tf_op jit(solution)/shard_map/ppermute | solution.py:256
  55.9 0.3 collective-permute-done.9.refs_1_
  56.2 1.4 %collective-permute-start.13 = (bf16[128,2048]{1,0:T(8,128)(2,1)S(1)}, bf16[128,2048]{1,0:T(8,128)(2,1)S(1)}, u32[]{:S(2)}, u32[]{:S(2)}) collective-permute-start(bf16[128,2048]{1,0:T(8,128)(2,1)S(1)} %collective-permute-done.9.refs_1_), channel_id=1, source_target_pairs={{0,4},{1,5},{2,6},{3,7},{4,0},{5,1},{6,2},{7,3},{8,12},{9,13},{10,... | collective-permute-start | bytes 1572872 | tf_op jit(solution)/shard_map/ppermute | solution.py:256
  57.6 0.2 collective-permute-start.18
  57.9 0.1 add_convert_fusion.2
  58.0 1.5 %collective-permute-start.14 = (bf16[128,2048]{1,0:T(8,128)(2,1)S(1)}, bf16[128,2048]{1,0:T(8,128)(2,1)S(1)}, u32[]{:S(2)}, u32[]{:S(2)}) collective-permute-start(bf16[128,2048]{1,0:T(8,128)(2,1)S(1)} %add_convert_fusion.2), channel_id=1, source_target_pairs={{0,2},{1,3},{2,0},{3,1},{4,6},{5,7},{6,4},{7,5},{8,10},{9,11},{10,... | collective-permute-start | bytes 1572872 | tf_op jit(solution)/shard_map/ppermute | solution.py:256
  59.5 5.6 %shard_map.81 = (bf16[256,2048]{1,0:T(8,128)(2,1)S(1)}, bf16[128,2048]{1,0:T(8,128)(2,1)S(1)}, bf16[128,2048]{1,0:T(8,128)(2,1)S(1)}, bf16[320,768]{1,0:T(8,128)(2,1)S(1)}) custom-call(f32[16,512]{1,0:T(8,128)S(1)} %shard_map.78.tables, bf16[128,2048]{1,0:T(8,128)(2,1)S(1)} %constant_dynamic-update-slice_fusion.refs_0_, ...), custom_call_target="tpu_custom_call" | custom-call | flops 4362076160 | bytes 13631488 | tf_op jit(solution)/shard_map/pallas_call | solution.py:178
  65.2 0.6 collective-permute-start.17
  65.8 0.1 collective-permute-start.20
  65.8 2.7 %shard_map.82 = (bf16[128,2048]{1,0:T(8,128)(2,1)S(1)}, bf16[128,2048]{1,0:T(8,128)(2,1)S(1)}, bf16[160,768]{1,0:T(8,128)(2,1)S(1)}) custom-call(f32[16,512]{1,0:T(8,128)S(1)} %shard_map.78.tables, bf16[128,2048]{1,0:T(8,128)(2,1)S(1)} %collective-permute-done.8.refs_0_, bf16[128,2048]{1,0:T(8,128)(2,1)S(1)} %collective-permute-done.18.refs_1_, ...), custom_call_target="tpu_custom_call" | custom-call | flops 1845493760 | bytes 11534336 | tf_op jit(solution)/shard_map/pallas_call | solution.py:178
  68.5 3.6 %collective-permute-done.14 = bf16[128,2048]{1,0:T(8,128)(2,1)S(1)} collective-permute-done((bf16[128,2048]{1,0:T(8,128)(2,1)S(1)}, bf16[128,2048]{1,0:T(8,128)(2,1)S(1)}, u32[]{:S(2)}, u32[]{:S(2)}) %collective-permute-start.14) | collective-permute-done | bytes 524320 | tf_op jit(solution)/shard_map/ppermute | solution.py:256
  72.3 0.1 add_convert_fusion.7
  72.4 1.5 %collective-permute-start.23 = (bf16[64,2048]{1,0:T(8,128)(2,1)S(1)}, bf16[64,2048]{1,0:T(8,128)(2,1)S(1)}, u32[]{:S(2)}, u32[]{:S(2)}) collective-permute-start(bf16[64,2048]{1,0:T(8,128)(2,1)S(1)} %get-tuple-element.141), channel_id=1, source_target_pairs={{0,2},{1,3},{2,0},{3,1},{4,6},{5,7},{6,4},{7,5},{8,10},{9,11},{10,... | collective-permute-start | bytes 786440 | tf_op jit(solution)/shard_map/ppermute | solution.py:256
  73.9 0.2 collective-permute-start.21
  74.1 0.3 collective-permute-start.22
  74.4 0.2 add_convert_fusion.1
  74.7 2.7 %shard_map.83 = (bf16[128,2048]{1,0:T(8,128)(2,1)S(1)}, bf16[128,2048]{1,0:T(8,128)(2,1)S(1)}, bf16[160,768]{1,0:T(8,128)(2,1)S(1)}) custom-call(f32[16,512]{1,0:T(8,128)S(1)} %shard_map.78.tables, bf16[128,2048]{1,0:T(8,128)(2,1)S(1)} %collective-permute-done.13.refs_0_, bf16[128,2048]{1,0:T(8,128)(2,1)S(1)} %collective-permute-done.19.refs_1_, ...), custom_call_target="tpu_custom_call" | custom-call | flops 1845493760 | bytes 11534336 | tf_op jit(solution)/shard_map/pallas_call | solution.py:178
  77.4 3.7 %collective-permute-done.23 = bf16[64,2048]{1,0:T(8,128)(2,1)S(1)} collective-permute-done((bf16[64,2048]{1,0:T(8,128)(2,1)S(1)}, bf16[64,2048]{1,0:T(8,128)(2,1)S(1)}, u32[]{:S(2)}, u32[]{:S(2)}) %collective-permute-start.23) | collective-permute-done | bytes 262176 | tf_op jit(solution)/shard_map/ppermute | solution.py:256
  81.2 0.1 add_convert_fusion.8
  81.3 1.0 collective-permute-start.27
  82.3 1.6 %collective-permute-start.28 = (bf16[64,2048]{1,0:T(8,128)(2,1)S(1)}, bf16[64,2048]{1,0:T(8,128)(2,1)S(1)}, u32[]{:S(2)}, u32[]{:S(2)}) collective-permute-start(bf16[64,2048]{1,0:T(8,128)(2,1)S(1)} %slice.78), channel_id=1, source_target_pairs={{0,4},{1,5},{2,6},{3,7},{4,0},{5,1},{6,2},{7,3},{8,12},{9,13},{10,... | collective-permute-start | bytes 786440 | tf_op jit(solution)/shard_map/ppermute | solution.py:256
  84.0 0.1 add_convert_fusion.9
  84.1 1.0 collective-permute-start.25
  85.1 1.0 collective-permute-start.26
  86.2 0.1 add_convert_fusion
  86.3 10.3 %collective-permute-done.27.far_high = bf16[64,2048]{1,0:T(8,128)(2,1)S(1)} collective-permute-done((bf16[64,2048]{1,0:T(8,128)(2,1)S(1)}, bf16[64,2048]{1,0:T(8,128)(2,1)S(1)}, u32[]{:S(2)}, u32[]{:S(2)}) %collective-permute-start.27) | collective-permute-done | bytes 262176 | tf_op jit(solution)/shard_map/ppermute | solution.py:256
  96.6 1.3 %collective-permute-done.26 = bf16[64,2048]{1,0:T(8,128)(2,1)S(1)} collective-permute-done((bf16[64,2048]{1,0:T(8,128)(2,1)S(1)}, bf16[64,2048]{1,0:T(8,128)(2,1)S(1)}, u32[]{:S(2)}, u32[]{:S(2)}) %collective-permute-start.26) | collective-permute-done | bytes 262176 | tf_op jit(solution)/shard_map/ppermute | solution.py:256
  97.9 0.2 add_convert_fusion.5
  98.2 1.0 collective-permute-start.29
  99.2 1.4 %collective-permute-start.30 = (bf16[64,2048]{1,0:T(8,128)(2,1)S(1)}, bf16[64,2048]{1,0:T(8,128)(2,1)S(1)}, u32[]{:S(2)}, u32[]{:S(2)}) collective-permute-start(bf16[64,2048]{1,0:T(8,128)(2,1)S(1)} %get-tuple-element.142), channel_id=1, source_target_pairs={{0,4},{1,5},{2,6},{3,7},{4,0},{5,1},{6,2},{7,3},{8,12},{9,13},{10,... | collective-permute-start | bytes 786440 | tf_op jit(solution)/shard_map/ppermute | solution.py:256
  100.7 1.5 %collective-permute-start.31 = (bf16[64,2048]{1,0:T(8,128)(2,1)S(1)}, bf16[64,2048]{1,0:T(8,128)(2,1)S(1)}, u32[]{:S(2)}, u32[]{:S(2)}) collective-permute-start(bf16[64,2048]{1,0:T(8,128)(2,1)S(1)} %get-tuple-element.126), channel_id=1, source_target_pairs={{0,2},{1,3},{2,0},{3,1},{4,6},{5,7},{6,4},{7,5},{8,10},{9,11},{10,... | collective-permute-start | bytes 786440 | tf_op jit(solution)/shard_map/ppermute | solution.py:256
  102.1 3.1 %shard_map.84 = f32[768,768]{1,0:T(8,128)} custom-call(f32[16,512]{1,0:T(8,128)S(1)} %shard_map.78.tables, bf16[320,768]{1,0:T(8,128)(2,1)S(1)} %get-tuple-element.128.refs_0_, bf16[320,768]{1,0:T(8,128)(2,1)S(1)} %get-tuple-element.129.refs_1_, bf16[320,768]{1,0:T(8,128)(2,1)S(1)} %get-tuple-element.130.refs_2_, ...), custom_call_target="tpu_custom_call" | custom-call | flops 1509949440 | bytes 4325376 | tf_op jit(solution)/shard_map/pallas_call | solution.py:209
  105.3 6.7 %collective-permute-done.29 = bf16[64,2048]{1,0:T(8,128)(2,1)S(1)} collective-permute-done((bf16[64,2048]{1,0:T(8,128)(2,1)S(1)}, bf16[64,2048]{1,0:T(8,128)(2,1)S(1)}, u32[]{:S(2)}, u32[]{:S(2)}) %collective-permute-start.29) | collective-permute-done | bytes 262176 | tf_op jit(solution)/shard_map/ppermute | solution.py:256
  112.0 0.1 add_convert_fusion.3
  112.1 0.7 collective-permute-start.34
  112.8 1.5 %collective-permute-start.32 = (bf16[128,2048]{1,0:T(8,128)(2,1)S(1)}, bf16[128,2048]{1,0:T(8,128)(2,1)S(1)}, u32[]{:S(2)}, u32[]{:S(2)}) collective-permute-start(bf16[128,2048]{1,0:T(8,128)(2,1)S(1)} %add_convert_fusion), channel_id=1, source_target_pairs={{0,2},{1,3},{2,0},{3,1},{4,6},{5,7},{6,4},{7,5},{8,10},{9,11},{10,... | collective-permute-start | bytes 1572872 | tf_op jit(solution)/shard_map/ppermute | solution.py:256
  114.4 1.8 %collective-permute-start.33 = (bf16[64,2048]{1,0:T(8,128)(2,1)S(1)}, bf16[64,2048]{1,0:T(8,128)(2,1)S(1)}, u32[]{:S(2)}, u32[]{:S(2)}) collective-permute-start(bf16[64,2048]{1,0:T(8,128)(2,1)S(1)} %add_convert_fusion.4), channel_id=1, source_target_pairs={{0,4},{1,5},{2,6},{3,7},{4,0},{5,1},{6,2},{7,3},{8,12},{9,13},{10,... | collective-permute-start | bytes 786440 | tf_op jit(solution)/shard_map/ppermute | solution.py:256
  116.1 10.2 %collective-permute-done.34.far_low = bf16[64,2048]{1,0:T(8,128)(2,1)S(1)} collective-permute-done((bf16[64,2048]{1,0:T(8,128)(2,1)S(1)}, bf16[64,2048]{1,0:T(8,128)(2,1)S(1)}, u32[]{:S(2)}, u32[]{:S(2)}) %collective-permute-start.34) | collective-permute-done | bytes 262176 | tf_op jit(solution)/shard_map/ppermute | solution.py:256
  126.3 1.3 collective-permute-done.33.near_high
  127.6 1.1 shard_map.85
  (53 shorter events, 0.4 us)
Async XLA Ops:
  0.6 24.1 %collective-permute-start = (bf16[128,2048]{1,0:T(8,128)(2,1)}, bf16[128,2048]{1,0:T(8,128)(2,1)S(1)}, u32[]{:S(2)}, u32[]{:S(2)}) collective-permute-start(bf16[128,2048]{1,0:T(8,128)(2,1)} %refs_0_.1), channel_id=1, source_target_pairs={{0,4},{1,5},{2,6},{3,7},{4,0},{5,1},{6,2},{7,3},{8,12},{9,13},{10,... | collective-permute-start | bytes 1572872 | tf_op jit(solution)/shard_map/ppermute | solution.py:256
  3.7 21.0 %collective-permute-start.2 = (bf16[128,2048]{1,0:T(8,128)(2,1)}, bf16[128,2048]{1,0:T(8,128)(2,1)S(1)}, u32[]{:S(2)}, u32[]{:S(2)}) collective-permute-start(bf16[128,2048]{1,0:T(8,128)(2,1)} %refs_0_.1), channel_id=1, source_target_pairs={{0,2},{1,3},{2,0},{3,1},{4,6},{5,7},{6,4},{7,5},{8,10},{9,11},{10,... | collective-permute-start | bytes 1572872 | tf_op jit(solution)/shard_map/ppermute | solution.py:256
  5.2 19.5 %collective-permute-start.3 = (bf16[128,2048]{1,0:T(8,128)(2,1)}, bf16[128,2048]{1,0:T(8,128)(2,1)S(1)}, u32[]{:S(2)}, u32[]{:S(2)}) collective-permute-start(bf16[128,2048]{1,0:T(8,128)(2,1)} %refs_0_.1), channel_id=1, source_target_pairs={{0,1},{1,0},{2,3},{3,2},{4,5},{5,4},{6,7},{7,6},{8,9},{9,8},{10,11... | collective-permute-start | bytes 1572872 | tf_op jit(solution)/shard_map/ppermute | solution.py:256
  5.2 1.1 copy-start.6
  6.3 0.7 copy-start.8
  7.0 0.7 copy-start.9
  7.8 16.9 %collective-permute-start.1 = (bf16[64,2048]{1,0:T(8,128)(2,1)S(1)}, bf16[64,2048]{1,0:T(8,128)(2,1)S(1)}, u32[]{:S(2)}, u32[]{:S(2)}) collective-permute-start(bf16[64,2048]{1,0:T(8,128)(2,1)S(1)} %get-tuple-element.71), channel_id=1, source_target_pairs={{0,8},{1,9},{2,10},{3,11},{4,12},{5,13},{6,14},{7,15},{8,0},{9,1},... | collective-permute-start | bytes 786440 | tf_op jit(solution)/shard_map/ppermute | solution.py:256
  24.7 0.7 copy-start.10
  25.4 2.7 %collective-permute-start.7 = (bf16[128,2048]{1,0:T(8,128)(2,1)S(1)}, bf16[128,2048]{1,0:T(8,128)(2,1)S(1)}, u32[]{:S(2)}, u32[]{:S(2)}) collective-permute-start(bf16[128,2048]{1,0:T(8,128)(2,1)S(1)} %collective-permute-done.2.refs_1_), channel_id=1, source_target_pairs={{0,1},{1,0},{2,3},{3,2},{4,5},{5,4},{6,7},{7,6},{8,9},{9,8},{10,11... | collective-permute-start | bytes 1572872 | tf_op jit(solution)/shard_map/ppermute | solution.py:256
  25.4 15.9 %collective-permute-start.5 = (bf16[128,2048]{1,0:T(8,128)(2,1)S(1)}, bf16[128,2048]{1,0:T(8,128)(2,1)S(1)}, u32[]{:S(2)}, u32[]{:S(2)}) collective-permute-start(bf16[128,2048]{1,0:T(8,128)(2,1)S(1)} %collective-permute-done.refs_0_), channel_id=1, source_target_pairs={{0,2},{1,3},{2,0},{3,1},{4,6},{5,7},{6,4},{7,5},{8,10},{9,11},{10,... | collective-permute-start | bytes 1572872 | tf_op jit(solution)/shard_map/ppermute | solution.py:256
  25.9 15.4 %collective-permute-start.6 = (bf16[128,2048]{1,0:T(8,128)(2,1)S(1)}, bf16[128,2048]{1,0:T(8,128)(2,1)S(1)}, u32[]{:S(2)}, u32[]{:S(2)}) collective-permute-start(bf16[128,2048]{1,0:T(8,128)(2,1)S(1)} %collective-permute-done.refs_0_), channel_id=1, source_target_pairs={{0,1},{1,0},{2,3},{3,2},{4,5},{5,4},{6,7},{7,6},{8,9},{9,8},{10,11... | collective-permute-start | bytes 1572872 | tf_op jit(solution)/shard_map/ppermute | solution.py:256
  26.3 15.1 %collective-permute-start.4 = (bf16[64,2048]{1,0:T(8,128)(2,1)S(1)}, bf16[64,2048]{1,0:T(8,128)(2,1)S(1)}, u32[]{:S(2)}, u32[]{:S(2)}) collective-permute-start(bf16[64,2048]{1,0:T(8,128)(2,1)S(1)} %get-tuple-element.75), channel_id=1, source_target_pairs={{0,8},{1,9},{2,10},{3,11},{4,12},{5,13},{6,14},{7,15},{8,0},{9,1},... | collective-permute-start | bytes 786440 | tf_op jit(solution)/shard_map/ppermute | solution.py:256
  28.2 1.9 %copy-start = (bf16[1,2048,768]{2,1,0:T(8,128)(2,1)S(1)}, bf16[1,2048,768]{2,1,0:T(8,128)(2,1)}, u32[]{:S(2)}) copy-start(bf16[1,2048,768]{2,1,0:T(8,128)(2,1)} %param.9) | copy-start | bytes 9437188
  30.0 1.9 %copy-start.2 = (bf16[1,2048,768]{2,1,0:T(8,128)(2,1)S(1)}, bf16[1,2048,768]{2,1,0:T(8,128)(2,1)}, u32[]{:S(2)}) copy-start(bf16[1,2048,768]{2,1,0:T(8,128)(2,1)} %param.10) | copy-start | bytes 9437188
  31.9 1.9 %copy-start.4 = (bf16[1,768,2048]{2,1,0:T(8,128)(2,1)S(1)}, bf16[1,768,2048]{2,1,0:T(8,128)(2,1)}, u32[]{:S(2)}) copy-start(bf16[1,768,2048]{2,1,0:T(8,128)(2,1)} %param.11) | copy-start | bytes 9437188
  33.8 1.0 copy-start.7
  34.9 6.5 %copy-start.11 = (bf16[64,2048]{1,0:T(8,128)(2,1)S(1)}, bf16[64,2048]{1,0:T(8,128)(2,1)}, u32[]{:S(2)}) copy-start(bf16[64,2048]{1,0:T(8,128)(2,1)} %copy-done.10) | copy-start | bytes 786436
  34.9 8.8 %copy-start.1 = (bf16[1,2048,768]{2,1,0:T(8,128)(2,1)S(1)}, bf16[1,2048,768]{2,1,0:T(8,128)(2,1)}, u32[]{:S(2)}) copy-start(bf16[1,2048,768]{2,1,0:T(8,128)(2,1)} %param.9) | copy-start | bytes 9437188
  34.9 8.8 %copy-start.3 = (bf16[1,2048,768]{2,1,0:T(8,128)(2,1)S(1)}, bf16[1,2048,768]{2,1,0:T(8,128)(2,1)}, u32[]{:S(2)}) copy-start(bf16[1,2048,768]{2,1,0:T(8,128)(2,1)} %param.10) | copy-start | bytes 9437188
  34.9 8.8 %copy-start.5 = (bf16[1,768,2048]{2,1,0:T(8,128)(2,1)S(1)}, bf16[1,768,2048]{2,1,0:T(8,128)(2,1)}, u32[]{:S(2)}) copy-start(bf16[1,768,2048]{2,1,0:T(8,128)(2,1)} %param.11) | copy-start | bytes 9437188
  41.3 2.3 %collective-permute-start.11 = (bf16[128,2048]{1,0:T(8,128)(2,1)S(1)}, bf16[128,2048]{1,0:T(8,128)(2,1)S(1)}, u32[]{:S(2)}, u32[]{:S(2)}) collective-permute-start(bf16[128,2048]{1,0:T(8,128)(2,1)S(1)} %collective-permute-done.5.refs_1_), channel_id=1, source_target_pairs={{0,1},{1,0},{2,3},{3,2},{4,5},{5,4},{6,7},{7,6},{8,9},{9,8},{10,11... | collective-permute-start | bytes 1572872 | tf_op jit(solution)/shard_map/ppermute | solution.py:256
  41.4 7.8 %collective-permute-start.10 = (bf16[128,2048]{1,0:T(8,128)(2,1)S(1)}, bf16[128,2048]{1,0:T(8,128)(2,1)S(1)}, u32[]{:S(2)}, u32[]{:S(2)}) collective-permute-start(bf16[128,2048]{1,0:T(8,128)(2,1)S(1)} %constant_dynamic-update-slice_fusion.refs_0_), channel_id=1, source_target_pairs={{0,1},{1,0},{2,3},{3,2},{4,5},{5,4},{6,7},{7,6},{8,9},{9,8},{10,11... | collective-permute-start | bytes 1572872 | tf_op jit(solution)/shard_map/ppermute | solution.py:256
  42.0 13.9 %collective-permute-start.8 = (bf16[128,2048]{1,0:T(8,128)(2,1)S(1)}, bf16[128,2048]{1,0:T(8,128)(2,1)S(1)}, u32[]{:S(2)}, u32[]{:S(2)}) collective-permute-start(bf16[128,2048]{1,0:T(8,128)(2,1)S(1)} %constant_dynamic-update-slice_fusion.refs_0_), channel_id=1, source_target_pairs={{0,4},{1,5},{2,6},{3,7},{4,0},{5,1},{6,2},{7,3},{8,12},{9,13},{10,... | collective-permute-start | bytes 1572872 | tf_op jit(solution)/shard_map/ppermute | solution.py:256
  42.6 13.6 %collective-permute-start.9 = (bf16[128,2048]{1,0:T(8,128)(2,1)S(1)}, bf16[128,2048]{1,0:T(8,128)(2,1)S(1)}, u32[]{:S(2)}, u32[]{:S(2)}) collective-permute-start(bf16[128,2048]{1,0:T(8,128)(2,1)S(1)} %constant_dynamic-update-slice_fusion.refs_0_), channel_id=1, source_target_pairs={{0,2},{1,3},{2,0},{3,1},{4,6},{5,7},{6,4},{7,5},{8,10},{9,11},{10,... | collective-permute-start | bytes 1572872 | tf_op jit(solution)/shard_map/ppermute | solution.py:256
  49.2 7.0 %collective-permute-start.12 = (bf16[128,2048]{1,0:T(8,128)(2,1)S(1)}, bf16[128,2048]{1,0:T(8,128)(2,1)S(1)}, u32[]{:S(2)}, u32[]{:S(2)}) collective-permute-start(bf16[128,2048]{1,0:T(8,128)(2,1)S(1)} %get-tuple-element.90), channel_id=1, source_target_pairs={{0,1},{1,0},{2,3},{3,2},{4,5},{5,4},{6,7},{7,6},{8,9},{9,8},{10,11... | collective-permute-start | bytes 1572872 | tf_op jit(solution)/shard_map/ppermute | solution.py:256
  56.2 3.3 %collective-permute-start.16 = (bf16[128,2048]{1,0:T(8,128)(2,1)S(1)}, bf16[128,2048]{1,0:T(8,128)(2,1)S(1)}, u32[]{:S(2)}, u32[]{:S(2)}) collective-permute-start(bf16[128,2048]{1,0:T(8,128)(2,1)S(1)} %collective-permute-done.9.refs_1_), channel_id=1, source_target_pairs={{0,1},{1,0},{2,3},{3,2},{4,5},{5,4},{6,7},{7,6},{8,9},{9,8},{10,11... | collective-permute-start | bytes 1572872 | tf_op jit(solution)/shard_map/ppermute | solution.py:256
  56.2 16.0 %collective-permute-start.13 = (bf16[128,2048]{1,0:T(8,128)(2,1)S(1)}, bf16[128,2048]{1,0:T(8,128)(2,1)S(1)}, u32[]{:S(2)}, u32[]{:S(2)}) collective-permute-start(bf16[128,2048]{1,0:T(8,128)(2,1)S(1)} %collective-permute-done.9.refs_1_), channel_id=1, source_target_pairs={{0,4},{1,5},{2,6},{3,7},{4,0},{5,1},{6,2},{7,3},{8,12},{9,13},{10,... | collective-permute-start | bytes 1572872 | tf_op jit(solution)/shard_map/ppermute | solution.py:256
  57.6 8.1 %collective-permute-start.18 = (bf16[128,2048]{1,0:T(8,128)(2,1)S(1)}, bf16[128,2048]{1,0:T(8,128)(2,1)S(1)}, u32[]{:S(2)}, u32[]{:S(2)}) collective-permute-start(bf16[128,2048]{1,0:T(8,128)(2,1)S(1)} %collective-permute-done.8.refs_0_), channel_id=1, source_target_pairs={{0,1},{1,0},{2,3},{3,2},{4,5},{5,4},{6,7},{7,6},{8,9},{9,8},{10,11... | collective-permute-start | bytes 1572872 | tf_op jit(solution)/shard_map/ppermute | solution.py:256
  58.0 14.2 %collective-permute-start.14 = (bf16[128,2048]{1,0:T(8,128)(2,1)S(1)}, bf16[128,2048]{1,0:T(8,128)(2,1)S(1)}, u32[]{:S(2)}, u32[]{:S(2)}) collective-permute-start(bf16[128,2048]{1,0:T(8,128)(2,1)S(1)} %add_convert_fusion.2), channel_id=1, source_target_pairs={{0,2},{1,3},{2,0},{3,1},{4,6},{5,7},{6,4},{7,5},{8,10},{9,11},{10,... | collective-permute-start | bytes 1572872 | tf_op jit(solution)/shard_map/ppermute | solution.py:256
  59.5 12.7 %collective-permute-start.15 = (bf16[128,2048]{1,0:T(8,128)(2,1)S(1)}, bf16[128,2048]{1,0:T(8,128)(2,1)S(1)}, u32[]{:S(2)}, u32[]{:S(2)}) collective-permute-start(bf16[128,2048]{1,0:T(8,128)(2,1)S(1)} %get-tuple-element.94), channel_id=1, source_target_pairs={{0,1},{1,0},{2,3},{3,2},{4,5},{5,4},{6,7},{7,6},{8,9},{9,8},{10,11... | collective-permute-start | bytes 1572872 | tf_op jit(solution)/shard_map/ppermute | solution.py:256
  65.2 7.0 %collective-permute-start.17 = (bf16[128,2048]{1,0:T(8,128)(2,1)S(1)}, bf16[128,2048]{1,0:T(8,128)(2,1)S(1)}, u32[]{:S(2)}, u32[]{:S(2)}) collective-permute-start(bf16[128,2048]{1,0:T(8,128)(2,1)S(1)} %get-tuple-element.96), channel_id=1, source_target_pairs={{0,1},{1,0},{2,3},{3,2},{4,5},{5,4},{6,7},{7,6},{8,9},{9,8},{10,11... | collective-permute-start | bytes 1572872 | tf_op jit(solution)/shard_map/ppermute | solution.py:256
  65.8 11.7 %collective-permute-start.20 = (bf16[256,2048]{1,0:T(8,128)(2,1)S(1)}, bf16[256,2048]{1,0:T(8,128)(2,1)S(1)}, u32[]{:S(2)}, u32[]{:S(2)}) collective-permute-start(bf16[256,2048]{1,0:T(8,128)(2,1)S(1)} %get-tuple-element.109), channel_id=1, source_target_pairs={{0,1},{1,0},{2,3},{3,2},{4,5},{5,4},{6,7},{7,6},{8,9},{9,8},{10,11... | collective-permute-start | bytes 3145736 | tf_op jit(solution)/shard_map/ppermute | solution.py:256
  72.2 2.5 %collective-permute-start.19 = (bf16[128,2048]{1,0:T(8,128)(2,1)S(1)}, bf16[128,2048]{1,0:T(8,128)(2,1)S(1)}, u32[]{:S(2)}, u32[]{:S(2)}) collective-permute-start(bf16[128,2048]{1,0:T(8,128)(2,1)S(1)} %collective-permute-done.13.refs_0_), channel_id=1, source_target_pairs={{0,1},{1,0},{2,3},{3,2},{4,5},{5,4},{6,7},{7,6},{8,9},{9,8},{10,11... | collective-permute-start | bytes 1572872 | tf_op jit(solution)/shard_map/ppermute | solution.py:256
  72.4 8.8 %collective-permute-start.23 = (bf16[64,2048]{1,0:T(8,128)(2,1)S(1)}, bf16[64,2048]{1,0:T(8,128)(2,1)S(1)}, u32[]{:S(2)}, u32[]{:S(2)}) collective-permute-start(bf16[64,2048]{1,0:T(8,128)(2,1)S(1)} %get-tuple-element.141), channel_id=1, source_target_pairs={{0,2},{1,3},{2,0},{3,1},{4,6},{5,7},{6,4},{7,5},{8,10},{9,11},{10,... | collective-permute-start | bytes 786440 | tf_op jit(solution)/shard_map/ppermute | solution.py:256
  73.9 7.2 %collective-permute-start.21 = (bf16[128,2048]{1,0:T(8,128)(2,1)S(1)}, bf16[128,2048]{1,0:T(8,128)(2,1)S(1)}, u32[]{:S(2)}, u32[]{:S(2)}) collective-permute-start(bf16[128,2048]{1,0:T(8,128)(2,1)S(1)} %get-tuple-element.110), channel_id=1, source_target_pairs={{0,1},{1,0},{2,3},{3,2},{4,5},{5,4},{6,7},{7,6},{8,9},{9,8},{10,11... | collective-permute-start | bytes 1572872 | tf_op jit(solution)/shard_map/ppermute | solution.py:256
  74.1 7.0 %collective-permute-start.22 = (bf16[128,2048]{1,0:T(8,128)(2,1)S(1)}, bf16[128,2048]{1,0:T(8,128)(2,1)S(1)}, u32[]{:S(2)}, u32[]{:S(2)}) collective-permute-start(bf16[128,2048]{1,0:T(8,128)(2,1)S(1)} %get-tuple-element.111), channel_id=1, source_target_pairs={{0,1},{1,0},{2,3},{3,2},{4,5},{5,4},{6,7},{7,6},{8,9},{9,8},{10,11... | collective-permute-start | bytes 1572872 | tf_op jit(solution)/shard_map/ppermute | solution.py:256
  81.2 2.8 %collective-permute-start.24 = (bf16[128,2048]{1,0:T(8,128)(2,1)S(1)}, bf16[128,2048]{1,0:T(8,128)(2,1)S(1)}, u32[]{:S(2)}, u32[]{:S(2)}) collective-permute-start(bf16[128,2048]{1,0:T(8,128)(2,1)S(1)} %get-tuple-element.118), channel_id=1, source_target_pairs={{0,1},{1,0},{2,3},{3,2},{4,5},{5,4},{6,7},{7,6},{8,9},{9,8},{10,11... | collective-permute-start | bytes 1572872 | tf_op jit(solution)/shard_map/ppermute | solution.py:256
  81.3 15.3 %collective-permute-start.27 = (bf16[64,2048]{1,0:T(8,128)(2,1)S(1)}, bf16[64,2048]{1,0:T(8,128)(2,1)S(1)}, u32[]{:S(2)}, u32[]{:S(2)}) collective-permute-start(bf16[64,2048]{1,0:T(8,128)(2,1)S(1)} %add_convert_fusion.8), channel_id=1, source_target_pairs={{0,8},{1,9},{2,10},{3,11},{4,12},{5,13},{6,14},{7,15},{8,0},{9,1},... | collective-permute-start | bytes 786440 | tf_op jit(solution)/shard_map/ppermute | solution.py:256
  82.3 14.2 %collective-permute-start.28 = (bf16[64,2048]{1,0:T(8,128)(2,1)S(1)}, bf16[64,2048]{1,0:T(8,128)(2,1)S(1)}, u32[]{:S(2)}, u32[]{:S(2)}) collective-permute-start(bf16[64,2048]{1,0:T(8,128)(2,1)S(1)} %slice.78), channel_id=1, source_target_pairs={{0,4},{1,5},{2,6},{3,7},{4,0},{5,1},{6,2},{7,3},{8,12},{9,13},{10,... | collective-permute-start | bytes 786440 | tf_op jit(solution)/shard_map/ppermute | solution.py:256
  84.1 12.5 %collective-permute-start.25 = (bf16[64,2048]{1,0:T(8,128)(2,1)S(1)}, bf16[64,2048]{1,0:T(8,128)(2,1)S(1)}, u32[]{:S(2)}, u32[]{:S(2)}) collective-permute-start(bf16[64,2048]{1,0:T(8,128)(2,1)S(1)} %get-tuple-element.145), channel_id=1, source_target_pairs={{0,2},{1,3},{2,0},{3,1},{4,6},{5,7},{6,4},{7,5},{8,10},{9,11},{10,... | collective-permute-start | bytes 786440 | tf_op jit(solution)/shard_map/ppermute | solution.py:256
  85.1 12.8 %collective-permute-start.26 = (bf16[64,2048]{1,0:T(8,128)(2,1)S(1)}, bf16[64,2048]{1,0:T(8,128)(2,1)S(1)}, u32[]{:S(2)}, u32[]{:S(2)}) collective-permute-start(bf16[64,2048]{1,0:T(8,128)(2,1)S(1)} %get-tuple-element.144), channel_id=1, source_target_pairs={{0,2},{1,3},{2,0},{3,1},{4,6},{5,7},{6,4},{7,5},{8,10},{9,11},{10,... | collective-permute-start | bytes 786440 | tf_op jit(solution)/shard_map/ppermute | solution.py:256
  98.2 13.8 %collective-permute-start.29 = (bf16[64,2048]{1,0:T(8,128)(2,1)S(1)}, bf16[64,2048]{1,0:T(8,128)(2,1)S(1)}, u32[]{:S(2)}, u32[]{:S(2)}) collective-permute-start(bf16[64,2048]{1,0:T(8,128)(2,1)S(1)} %get-tuple-element.143), channel_id=1, source_target_pairs={{0,8},{1,9},{2,10},{3,11},{4,12},{5,13},{6,14},{7,15},{8,0},{9,1},... | collective-permute-start | bytes 786440 | tf_op jit(solution)/shard_map/ppermute | solution.py:256
  99.2 12.7 %collective-permute-start.30 = (bf16[64,2048]{1,0:T(8,128)(2,1)S(1)}, bf16[64,2048]{1,0:T(8,128)(2,1)S(1)}, u32[]{:S(2)}, u32[]{:S(2)}) collective-permute-start(bf16[64,2048]{1,0:T(8,128)(2,1)S(1)} %get-tuple-element.142), channel_id=1, source_target_pairs={{0,4},{1,5},{2,6},{3,7},{4,0},{5,1},{6,2},{7,3},{8,12},{9,13},{10,... | collective-permute-start | bytes 786440 | tf_op jit(solution)/shard_map/ppermute | solution.py:256
  100.7 11.3 %collective-permute-start.31 = (bf16[64,2048]{1,0:T(8,128)(2,1)S(1)}, bf16[64,2048]{1,0:T(8,128)(2,1)S(1)}, u32[]{:S(2)}, u32[]{:S(2)}) collective-permute-start(bf16[64,2048]{1,0:T(8,128)(2,1)S(1)} %get-tuple-element.126), channel_id=1, source_target_pairs={{0,2},{1,3},{2,0},{3,1},{4,6},{5,7},{6,4},{7,5},{8,10},{9,11},{10,... | collective-permute-start | bytes 786440 | tf_op jit(solution)/shard_map/ppermute | solution.py:256
  112.1 14.2 %collective-permute-start.34 = (bf16[64,2048]{1,0:T(8,128)(2,1)S(1)}, bf16[64,2048]{1,0:T(8,128)(2,1)S(1)}, u32[]{:S(2)}, u32[]{:S(2)}) collective-permute-start(bf16[64,2048]{1,0:T(8,128)(2,1)S(1)} %add_convert_fusion.3), channel_id=1, source_target_pairs={{0,8},{1,9},{2,10},{3,11},{4,12},{5,13},{6,14},{7,15},{8,0},{9,1},... | collective-permute-start | bytes 786440 | tf_op jit(solution)/shard_map/ppermute | solution.py:256
  112.8 14.8 %collective-permute-start.32 = (bf16[128,2048]{1,0:T(8,128)(2,1)S(1)}, bf16[128,2048]{1,0:T(8,128)(2,1)S(1)}, u32[]{:S(2)}, u32[]{:S(2)}) collective-permute-start(bf16[128,2048]{1,0:T(8,128)(2,1)S(1)} %add_convert_fusion), channel_id=1, source_target_pairs={{0,2},{1,3},{2,0},{3,1},{4,6},{5,7},{6,4},{7,5},{8,10},{9,11},{10,... | collective-permute-start | bytes 1572872 | tf_op jit(solution)/shard_map/ppermute | solution.py:256
  114.4 13.2 %collective-permute-start.33 = (bf16[64,2048]{1,0:T(8,128)(2,1)S(1)}, bf16[64,2048]{1,0:T(8,128)(2,1)S(1)}, u32[]{:S(2)}, u32[]{:S(2)}) collective-permute-start(bf16[64,2048]{1,0:T(8,128)(2,1)S(1)} %add_convert_fusion.4), channel_id=1, source_target_pairs={{0,4},{1,5},{2,6},{3,7},{4,0},{5,1},{6,2},{7,3},{8,12},{9,13},{10,... | collective-permute-start | bytes 786440 | tf_op jit(solution)/shard_map/ppermute | solution.py:256

commit v19 on v18

--- a/solution.py
+++ b/solution.py
@@ -75,7 +75,7 @@
     return total.astype(jnp.bfloat16)
 
 
-def ranks_kernel(capacity, spots, weight, tables, ranks, chip_ranks):
+def ranks_kernel(capacity, spots, weight, w_gate, w_up, w_down, tables, ranks, chip_ranks):
     blocks, tok = weight.shape
     planes = blocks // 4
     named = (weight[...] >= 0.0).astype(jnp.float32)
@@ -108,17 +108,17 @@
     tables[2 * planes + 1 :, :] = jnp.broadcast_to(2.0 / count, rest)
 
 
-def ranks_pass(capacity, spots, weight):
+def ranks_pass(capacity, spots, weight, w_gate, w_up, w_down):
     blocks, tok = weight.shape
     vmem = pl.BlockSpec(memory_space=pltpu.VMEM)
     return pl.pallas_call(
         functools.partial(ranks_kernel, capacity),
         out_shape=jax.ShapeDtypeStruct((blocks // 4 * 2 + 8, 4 * tok), jnp.float32),
-        in_specs=[pl.BlockSpec(memory_space=pltpu.SMEM), vmem],
+        in_specs=[pl.BlockSpec(memory_space=pltpu.SMEM)] + [vmem] * 4,
         out_specs=vmem,
         scratch_shapes=[pltpu.VMEM(weight.shape, jnp.float32)] * 2,
         compiler_params=pltpu.CompilerParams(vmem_limit_bytes=4 * 1024 * 1024),
-    )(spots, weight)
+    )(spots, weight, w_gate, w_up, w_down)
 
 
 def plane_kernel(k, picked, gives, tables, *refs):
@@ -188,6 +188,30 @@
     )(tables, *xs, w_gate, w_up, w_down)
 
 
+def late_kernel(keep3, got3, keep2, got2, side2, near1, low3, high3, high2, low1):
+    half, tok = low3.shape[0], keep3.shape[0]
+
+    def total(*parts):
+        return sum(part.astype(jnp.float32) for part in parts).astype(low3.dtype)
+
+    low3[...] = total(keep3[:half, :], got3[:half, :])
+    high3[...] = total(keep3[half:, :], got3[half:, :])
+    high2[...] = total(keep2[half:tok, :], got2[half:, :], side2[...])
+    low1[...] = near1[:half, :]
+
+
+def late_pass(*parts):
+    side = parts[4]
+    vmem = pl.BlockSpec(memory_space=pltpu.VMEM)
+    return pl.pallas_call(
+        late_kernel,
+        out_shape=[jax.ShapeDtypeStruct(side.shape, side.dtype)] * 4,
+        in_specs=[vmem] * len(parts),
+        out_specs=[vmem] * 4,
+        compiler_params=pltpu.CompilerParams(vmem_limit_bytes=12 * 1024 * 1024),
+    )(*parts)
+
+
 def gram_kernel(tables, *refs):
     *acts, gram = refs
     wide = 256
@@ -285,24 +309,22 @@
         lax.all_to_all(mine, "expert", split_axis=0, concat_axis=0, tiled=True),
         a0_high,
     )
-    tables = ranks_pass(capacity, spots, weight)
+    tables = ranks_pass(capacity, spots, weight, w_gate, w_up, w_down)
     high = far(a0_high)
     b1 = column(a1)
     d0 = sibling(b0)
     c1 = sibling(a1)
-    keep0, give0, act0 = expert(0, a0, b0, c0, d0)
-    high, b1, c1, keep0, give0, act0, tables = together(
-        high, b1, c1, keep0, give0, act0, tables
-    )
+    high, b1, c1, d0, tables = together(high, b1, c1, d0, tables)
     a2 = jnp.concatenate([low, high], axis=0)
     a3 = pair(a2)
     b2 = column(a2)
     d1 = sibling(b1)
     c2 = sibling(a2)
+    keep0, give0, act0 = expert(0, a0, b0, c0, d0)
     keep1, give1, *give1_side, act1 = expert(1, a1, b1, c1, d1, pieces=(tok, tok))
     got1_side = [sibling(piece) for piece in give1_side]
-    a3, b2, c2, keep1, give1, act1, *got1_side = together(
-        a3, b2, c2, keep1, give1, act1, *got1_side
+    a3, b2, c2, keep0, give0, act0, keep1, give1, act1, *got1_side = together(
+        a3, b2, c2, keep0, give0, act0, keep1, give1, act1, *got1_side
     )
     b3 = pair(b2)
     came1 = column(summed(keep1[tok:], jnp.concatenate(got1_side, axis=0)))
@@ -321,14 +343,16 @@
     side_high = column(summed(keep2[tok + half :], got2_side[half:]))
     got0, got2, got3 = sibling(give0), sibling(give2), sibling(give3)
     keep3_side, give3_side, act4 = expert(3, b3, d3, picked=(1, 3))
-    keep3_side, give3_side, act4, got0, got2, got3, side_high, near1 = together(
-        keep3_side, give3_side, act4, got0, got2, got3, side_high, near1
-    )
-    far2_high = far(summed(keep2[half:tok], got2[half:], side_high))
+    keep3_side, give3_side, act4, got0, got2, got3, near1 = together(
+        keep3_side, give3_side, act4, got0, got2, got3, near1
+    )
     got3_side = sibling(give3_side)
-    came3_low = column(summed(keep3_side[:half], got3_side[:half]))
-    came3_high = column(summed(keep3_side[half:], got3_side[half:]))
-    near1_low = pair(near1[:half])
+    came3_low, came3_high, far2_high, near1_low = late_pass(
+        keep3_side, got3_side, keep2, got2, side_high, near1
+    )
+    came3_low, came3_high = column(came3_low), column(came3_high)
+    far2_high = far(far2_high)
+    near1_low = pair(near1_low)
     side0 = summed(keep0[tok:], got0[tok:])
     side2 = summed(keep2[tok : tok + half], got2_side[:half])
     came3_low, came3_high, far2_high, near1_low, side0, side2 = together(

time: 129 us -> 135 us (1.047)
  waiting for transfers between devices: 45 us -> 50.1 us
    ppermute x35, waiting for transfers between devices: 45 us -> 50.1 us  [swapped(): return lax.ppermute(array, 'expert', [(i, i ^ bit) for i in range(size)])]
    unnamed x25 -> x23, local copies, waits for them, and re-layouts: 9.86 us -> 9.77 us
  transfers between devices with their start and end apart: 35 -> 35, of which waited for: 10 -> 13; matrix products, arithmetic and copies ran while one was open for 1% -> 2% of each run, Pallas kernels for 20% -> 19%
where the time goes in v19:
time: 135 us
  waiting for transfers between devices  50.1 us (37%)
  starting transfers between devices  30.5 us (23%)
  Pallas kernels  27.3 us (20%)
  blocking collectives  14.2 us (11%)
  local copies, waits for them, and re-layouts  10.8 us (8%)
    ppermute x35, waiting for transfers between devices, swapped(): return lax.ppermute(array, 'expert', [(i, i ^ bit) for i in range(size)])  50.1 us
    ppermute x35, starting transfers between devices, swapped(): return lax.ppermute(array, 'expert', [(i, i ^ bit) for i in range(size)])  30.5 us
    pallas_call x5, Pallas kernels, plane_pass(): pl.pallas_call(functools.partial(plane_kernel, k, picked, len(pieces)), o...  22 us
    all_to_all x1, blocking collectives, staged(): lax.all_to_all(mine, 'expert', split_axis=0, concat_axis=0, tiled=True)  14.2 us
    unnamed x23, local copies, waits for them, and re-layouts  9.77 us
    pallas_call x1, Pallas kernels, gram_pass(): pl.pallas_call(gram_kernel, out_shape=jax.ShapeDtypeStruct((hidden, hidde...  3.14 us
  transfers between devices with their start and end apart: 35, of which 13 were waited for; matrix products, arithmetic and copies ran while one was open for 2% of the time, Pallas kernels for 19%

profile of v19, /device:TPU:0, one launch (start us, length us, event | category | flops | bytes accessed | tf_op | source)
XLA Modules:
  0.0 134.9 jit_solution(6363474602729880979)
XLA Ops:
  0.6 3.1 %collective-permute-start = (bf16[128,2048]{1,0:T(8,128)(2,1)}, bf16[128,2048]{1,0:T(8,128)(2,1)S(1)}, u32[]{:S(2)}, u32[]{:S(2)}) collective-permute-start(bf16[128,2048]{1,0:T(8,128)(2,1)} %refs_0_.1), channel_id=1, source_target_pairs={{0,4},{1,5},{2,6},{3,7},{4,0},{5,1},{6,2},{7,3},{8,12},{9,13},{10,... | collective-permute-start | bytes 1572872 | tf_op jit(solution)/shard_map/ppermute | solution.py:280
  3.7 1.5 %collective-permute-start.2 = (bf16[128,2048]{1,0:T(8,128)(2,1)}, bf16[128,2048]{1,0:T(8,128)(2,1)S(1)}, u32[]{:S(2)}, u32[]{:S(2)}) collective-permute-start(bf16[128,2048]{1,0:T(8,128)(2,1)} %refs_0_.1), channel_id=1, source_target_pairs={{0,2},{1,3},{2,0},{3,1},{4,6},{5,7},{6,4},{7,5},{8,10},{9,11},{10,... | collective-permute-start | bytes 1572872 | tf_op jit(solution)/shard_map/ppermute | solution.py:280
  5.2 1.1 copy-done.6
  6.3 0.7 copy-done.8
  7.0 0.7 copy-done.9
  7.7 0.1 shard_map.77
  7.8 2.7 %collective-permute-start.1 = (bf16[64,2048]{1,0:T(8,128)(2,1)S(1)}, bf16[64,2048]{1,0:T(8,128)(2,1)S(1)}, u32[]{:S(2)}, u32[]{:S(2)}) collective-permute-start(bf16[64,2048]{1,0:T(8,128)(2,1)S(1)} %get-tuple-element.75), channel_id=1, source_target_pairs={{0,8},{1,9},{2,10},{3,11},{4,12},{5,13},{6,14},{7,15},{8,0},{9,1},... | collective-permute-start | bytes 786440 | tf_op jit(solution)/shard_map/ppermute | solution.py:280
  10.5 14.2 %all_to_all.12 = f32[16,1,128]{2,1,0:T(1,128)S(1)} all-to-all(f32[16,1,128]{2,1,0:T(1,128)S(1)} %bitcast.45), channel_id=1, replica_groups=mesh['parts'=2,'expert'=16] {'expert'}, dimensions={0} | all-to-all | bytes 16384 | tf_op jit(solution)/shard_map/all_to_all | solution.py:309
  24.8 0.7 copy-done.10
  25.4 0.5 collective-permute-start.5
  25.9 0.5 collective-permute-start.7
  26.4 1.1 collective-permute-start.4
  27.5 0.1 stack.67.spots
  27.6 1.9 %copy-done = bf16[1,2048,768]{2,1,0:T(8,128)(2,1)S(1)} copy-done((bf16[1,2048,768]{2,1,0:T(8,128)(2,1)S(1)}, bf16[1,2048,768]{2,1,0:T(8,128)(2,1)}, u32[]{:S(2)}) %copy-start) | copy-done | bytes 3145752
  29.5 1.9 %copy-done.2 = bf16[1,2048,768]{2,1,0:T(8,128)(2,1)S(1)} copy-done((bf16[1,2048,768]{2,1,0:T(8,128)(2,1)S(1)}, bf16[1,2048,768]{2,1,0:T(8,128)(2,1)}, u32[]{:S(2)}) %copy-start.2) | copy-done | bytes 3145752
  31.4 1.9 %copy-done.4 = bf16[1,768,2048]{2,1,0:T(8,128)(2,1)S(1)} copy-done((bf16[1,768,2048]{2,1,0:T(8,128)(2,1)S(1)}, bf16[1,768,2048]{2,1,0:T(8,128)(2,1)}, u32[]{:S(2)}) %copy-start.4) | copy-done | bytes 3145752
  33.3 0.7 shard_map.78.tables
  34.0 7.2 %collective-permute-done.4 = bf16[64,2048]{1,0:T(8,128)(2,1)} collective-permute-done((bf16[64,2048]{1,0:T(8,128)(2,1)S(1)}, bf16[64,2048]{1,0:T(8,128)(2,1)}, u32[]{:S(2)}, u32[]{:S(2)}) %collective-permute-start.4) | collective-permute-done | bytes 262176 | tf_op jit(solution)/shard_map/ppermute | solution.py:280
  41.4 1.0 constant_dynamic-update-slice_fusion.1
  42.3 1.0 constant_dynamic-update-slice_fusion.refs_0_
  43.3 0.6 collective-permute-start.10
  43.9 1.5 %collective-permute-start.9 = (bf16[128,2048]{1,0:T(8,128)(2,1)S(1)}, bf16[128,2048]{1,0:T(8,128)(2,1)S(1)}, u32[]{:S(2)}, u32[]{:S(2)}) collective-permute-start(bf16[128,2048]{1,0:T(8,128)(2,1)S(1)} %constant_dynamic-update-slice_fusion.refs_0_), channel_id=1, source_target_pairs={{0,2},{1,3},{2,0},{3,1},{4,6},{5,7},{6,4},{7,5},{8,10},{9,11},{10,... | collective-permute-start | bytes 1572872 | tf_op jit(solution)/shard_map/ppermute | solution.py:280
  45.4 5.5 %shard_map.80 = (bf16[256,2048]{1,0:T(8,128)(2,1)S(1)}, bf16[128,2048]{1,0:T(8,128)(2,1)S(1)}, bf16[128,2048]{1,0:T(8,128)(2,1)S(1)}, bf16[320,768]{1,0:T(8,128)(2,1)S(1)}) custom-call(f32[16,512]{1,0:T(8,128)S(1)} %shard_map.78.tables, bf16[128,2048]{1,0:T(8,128)(2,1)S(1)} %collective-permute-done.refs_0_, ...), custom_call_target="tpu_custom_call" | custom-call | flops 4362076160 | bytes 13631488 | tf_op jit(solution)/shard_map/pallas_call | solution.py:178
  50.9 5.5 %shard_map.79 = (bf16[256,2048]{1,0:T(8,128)(2,1)S(1)}, bf16[256,2048]{1,0:T(8,128)(2,1)S(1)}, bf16[320,768]{1,0:T(8,128)(2,1)S(1)}) custom-call(f32[16,512]{1,0:T(8,128)S(1)} %shard_map.78.tables, bf16[128,2048]{1,0:T(8,128)(2,1)S(1)} %copy-done.7, bf16[128,2048]{1,0:T(8,128)(2,1)S(1)} %collective-permute-done.2.refs_1_, ...), custom_call_target="tpu_custom_call" | custom-call | flops 4362076160 | bytes 13631488 | tf_op jit(solution)/shard_map/pallas_call | solution.py:178
  56.4 1.4 %collective-permute-done.8.refs_0_ = bf16[128,2048]{1,0:T(8,128)(2,1)S(1)} collective-permute-done((bf16[128,2048]{1,0:T(8,128)(2,1)S(1)}, bf16[128,2048]{1,0:T(8,128)(2,1)S(1)}, u32[]{:S(2)}, u32[]{:S(2)}) %collective-permute-start.8) | collective-permute-done | bytes 524320 | tf_op jit(solution)/shard_map/ppermute | solution.py:280
  57.9 1.7 %collective-permute-start.13 = (bf16[128,2048]{1,0:T(8,128)(2,1)S(1)}, bf16[128,2048]{1,0:T(8,128)(2,1)S(1)}, u32[]{:S(2)}, u32[]{:S(2)}) collective-permute-start(bf16[128,2048]{1,0:T(8,128)(2,1)S(1)} %collective-permute-done.9.refs_1_), channel_id=1, source_target_pairs={{0,4},{1,5},{2,6},{3,7},{4,0},{5,1},{6,2},{7,3},{8,12},{9,13},{10,... | collective-permute-start | bytes 1572872 | tf_op jit(solution)/shard_map/ppermute | solution.py:280
  59.5 0.2 collective-permute-start.18
  59.8 0.1 add_convert_fusion.2
  59.9 1.5 %collective-permute-start.14 = (bf16[128,2048]{1,0:T(8,128)(2,1)S(1)}, bf16[128,2048]{1,0:T(8,128)(2,1)S(1)}, u32[]{:S(2)}, u32[]{:S(2)}) collective-permute-start(bf16[128,2048]{1,0:T(8,128)(2,1)S(1)} %add_convert_fusion.2), channel_id=1, source_target_pairs={{0,2},{1,3},{2,0},{3,1},{4,6},{5,7},{6,4},{7,5},{8,10},{9,11},{10,... | collective-permute-start | bytes 1572872 | tf_op jit(solution)/shard_map/ppermute | solution.py:280
  61.4 5.6 %shard_map.81 = (bf16[256,2048]{1,0:T(8,128)(2,1)S(1)}, bf16[128,2048]{1,0:T(8,128)(2,1)S(1)}, bf16[128,2048]{1,0:T(8,128)(2,1)S(1)}, bf16[320,768]{1,0:T(8,128)(2,1)S(1)}) custom-call(f32[16,512]{1,0:T(8,128)S(1)} %shard_map.78.tables, bf16[128,2048]{1,0:T(8,128)(2,1)S(1)} %constant_dynamic-update-slice_fusion.refs_0_, ...), custom_call_target="tpu_custom_call" | custom-call | flops 4362076160 | bytes 13631488 | tf_op jit(solution)/shard_map/pallas_call | solution.py:178
  67.1 0.6 collective-permute-start.17
  67.8 2.7 %shard_map.82 = (bf16[128,2048]{1,0:T(8,128)(2,1)S(1)}, bf16[128,2048]{1,0:T(8,128)(2,1)S(1)}, bf16[160,768]{1,0:T(8,128)(2,1)S(1)}) custom-call(f32[16,512]{1,0:T(8,128)S(1)} %shard_map.78.tables, bf16[128,2048]{1,0:T(8,128)(2,1)S(1)} %collective-permute-done.8.refs_0_, bf16[128,2048]{1,0:T(8,128)(2,1)S(1)} %collective-permute-done.18.refs_1_, ...), custom_call_target="tpu_custom_call" | custom-call | flops 1845493760 | bytes 11534336 | tf_op jit(solution)/shard_map/pallas_call | solution.py:178
  70.5 3.6 %collective-permute-done.14 = bf16[128,2048]{1,0:T(8,128)(2,1)S(1)} collective-permute-done((bf16[128,2048]{1,0:T(8,128)(2,1)S(1)}, bf16[128,2048]{1,0:T(8,128)(2,1)S(1)}, u32[]{:S(2)}, u32[]{:S(2)}) %collective-permute-start.14) | collective-permute-done | bytes 524320 | tf_op jit(solution)/shard_map/ppermute | solution.py:280
  74.2 0.5 collective-permute-start.21
  74.8 0.2 add_convert_fusion.1.near1
  75.0 1.1 collective-permute-done.19.refs_1_
  76.1 2.7 %shard_map.83 = (bf16[128,2048]{1,0:T(8,128)(2,1)S(1)}, bf16[128,2048]{1,0:T(8,128)(2,1)S(1)}, bf16[160,768]{1,0:T(8,128)(2,1)S(1)}) custom-call(f32[16,512]{1,0:T(8,128)S(1)} %shard_map.78.tables, bf16[128,2048]{1,0:T(8,128)(2,1)S(1)} %collective-permute-done.13.refs_0_, bf16[128,2048]{1,0:T(8,128)(2,1)S(1)} %collective-permute-done.19.refs_1_, ...), custom_call_target="tpu_custom_call" | custom-call | flops 1845493760 | bytes 11534336 | tf_op jit(solution)/shard_map/pallas_call | solution.py:178
  78.8 0.2 collective-permute-start.23
  79.0 0.1 add_convert_fusion.7
  79.1 1.5 %collective-permute-start.24 = (bf16[64,2048]{1,0:T(8,128)(2,1)S(1)}, bf16[64,2048]{1,0:T(8,128)(2,1)S(1)}, u32[]{:S(2)}, u32[]{:S(2)}) collective-permute-start(bf16[64,2048]{1,0:T(8,128)(2,1)S(1)} %get-tuple-element.149), channel_id=1, source_target_pairs={{0,2},{1,3},{2,0},{3,1},{4,6},{5,7},{6,4},{7,5},{8,10},{9,11},{10,... | collective-permute-start | bytes 786440 | tf_op jit(solution)/shard_map/ppermute | solution.py:280
  80.7 7.1 %collective-permute-done.24.side2 = bf16[64,2048]{1,0:T(8,128)(2,1)S(1)} collective-permute-done((bf16[64,2048]{1,0:T(8,128)(2,1)S(1)}, bf16[64,2048]{1,0:T(8,128)(2,1)S(1)}, u32[]{:S(2)}, u32[]{:S(2)}) %collective-permute-start.24) | collective-permute-done | bytes 262176 | tf_op jit(solution)/shard_map/ppermute | solution.py:280
  87.8 0.2 shard_map.84
  88.0 1.5 %collective-permute-start.25 = (bf16[64,2048]{1,0:T(8,128)(2,1)S(1)}, bf16[64,2048]{1,0:T(8,128)(2,1)S(1)}, u32[]{:S(2)}, u32[]{:S(2)}) collective-permute-start(bf16[64,2048]{1,0:T(8,128)(2,1)S(1)} %get-tuple-element.126), channel_id=1, source_target_pairs={{0,2},{1,3},{2,0},{3,1},{4,6},{5,7},{6,4},{7,5},{8,10},{9,11},{10,... | collective-permute-start | bytes 786440 | tf_op jit(solution)/shard_map/ppermute | solution.py:280
  89.6 0.6 collective-permute-start.26
  90.1 0.9 collective-permute-start.27
  91.0 1.6 %collective-permute-start.28 = (bf16[64,2048]{1,0:T(8,128)(2,1)S(1)}, bf16[64,2048]{1,0:T(8,128)(2,1)S(1)}, u32[]{:S(2)}, u32[]{:S(2)}) collective-permute-start(bf16[64,2048]{1,0:T(8,128)(2,1)S(1)} %get-tuple-element.129), channel_id=1, source_target_pairs={{0,4},{1,5},{2,6},{3,7},{4,0},{5,1},{6,2},{7,3},{8,12},{9,13},{10,... | collective-permute-start | bytes 786440 | tf_op jit(solution)/shard_map/ppermute | solution.py:280
  92.6 0.1 add_convert_fusion
  92.8 4.5 %collective-permute-done.25 = bf16[64,2048]{1,0:T(8,128)(2,1)S(1)} collective-permute-done((bf16[64,2048]{1,0:T(8,128)(2,1)S(1)}, bf16[64,2048]{1,0:T(8,128)(2,1)S(1)}, u32[]{:S(2)}, u32[]{:S(2)}) %collective-permute-start.25) | collective-permute-done | bytes 262176 | tf_op jit(solution)/shard_map/ppermute | solution.py:280
  97.3 4.2 %collective-permute-done.26 = bf16[64,2048]{1,0:T(8,128)(2,1)S(1)} collective-permute-done((bf16[64,2048]{1,0:T(8,128)(2,1)S(1)}, bf16[64,2048]{1,0:T(8,128)(2,1)S(1)}, u32[]{:S(2)}, u32[]{:S(2)}) %collective-permute-start.26) | collective-permute-done | bytes 262176 | tf_op jit(solution)/shard_map/ppermute | solution.py:280
  101.5 2.2 %collective-permute-done.27.far_high = bf16[64,2048]{1,0:T(8,128)(2,1)S(1)} collective-permute-done((bf16[64,2048]{1,0:T(8,128)(2,1)S(1)}, bf16[64,2048]{1,0:T(8,128)(2,1)S(1)}, u32[]{:S(2)}, u32[]{:S(2)}) %collective-permute-start.27) | collective-permute-done | bytes 262176 | tf_op jit(solution)/shard_map/ppermute | solution.py:280
  103.7 0.2 add_convert_fusion.5
  103.9 0.7 collective-permute-start.29
  104.6 1.9 %collective-permute-start.30 = (bf16[64,2048]{1,0:T(8,128)(2,1)S(1)}, bf16[64,2048]{1,0:T(8,128)(2,1)S(1)}, u32[]{:S(2)}, u32[]{:S(2)}) collective-permute-start(bf16[64,2048]{1,0:T(8,128)(2,1)S(1)} %get-tuple-element.150), channel_id=1, source_target_pairs={{0,4},{1,5},{2,6},{3,7},{4,0},{5,1},{6,2},{7,3},{8,12},{9,13},{10,... | collective-permute-start | bytes 786440 | tf_op jit(solution)/shard_map/ppermute | solution.py:280
  106.5 1.2 collective-permute-start.31
  107.7 3.1 %shard_map.85 = f32[768,768]{1,0:T(8,128)} custom-call(f32[16,512]{1,0:T(8,128)S(1)} %shard_map.78.tables, bf16[320,768]{1,0:T(8,128)(2,1)S(1)} %get-tuple-element.136.refs_0_, bf16[320,768]{1,0:T(8,128)(2,1)S(1)} %get-tuple-element.137.refs_1_, bf16[320,768]{1,0:T(8,128)(2,1)S(1)} %get-tuple-element.138.refs_2_, ...), custom_call_target="tpu_custom_call" | custom-call | flops 1509949440 | bytes 4325376 | tf_op jit(solution)/shard_map/pallas_call | solution.py:233
  110.9 7.3 %collective-permute-done.29 = bf16[64,2048]{1,0:T(8,128)(2,1)S(1)} collective-permute-done((bf16[64,2048]{1,0:T(8,128)(2,1)S(1)}, bf16[64,2048]{1,0:T(8,128)(2,1)S(1)}, u32[]{:S(2)}, u32[]{:S(2)}) %collective-permute-start.29) | collective-permute-done | bytes 262176 | tf_op jit(solution)/shard_map/ppermute | solution.py:280
  118.1 0.2 collective-permute-done.30
  118.3 0.1 add_convert_fusion.3
  118.5 0.4 collective-permute-start.34
  118.9 1.1 collective-permute-start.32
  120.0 2.5 %collective-permute-start.33 = (bf16[64,2048]{1,0:T(8,128)(2,1)S(1)}, bf16[64,2048]{1,0:T(8,128)(2,1)S(1)}, u32[]{:S(2)}, u32[]{:S(2)}) collective-permute-start(bf16[64,2048]{1,0:T(8,128)(2,1)S(1)} %add_convert_fusion.4), channel_id=1, source_target_pairs={{0,4},{1,5},{2,6},{3,7},{4,0},{5,1},{6,2},{7,3},{8,12},{9,13},{10,... | collective-permute-start | bytes 786440 | tf_op jit(solution)/shard_map/ppermute | solution.py:280
  122.6 9.8 %collective-permute-done.34.far_low = bf16[64,2048]{1,0:T(8,128)(2,1)S(1)} collective-permute-done((bf16[64,2048]{1,0:T(8,128)(2,1)S(1)}, bf16[64,2048]{1,0:T(8,128)(2,1)S(1)}, u32[]{:S(2)}, u32[]{:S(2)}) %collective-permute-start.34) | collective-permute-done | bytes 262176 | tf_op jit(solution)/shard_map/ppermute | solution.py:280
  132.4 1.4 %collective-permute-done.33.near_high = bf16[64,2048]{1,0:T(8,128)(2,1)S(1)} collective-permute-done((bf16[64,2048]{1,0:T(8,128)(2,1)S(1)}, bf16[64,2048]{1,0:T(8,128)(2,1)S(1)}, u32[]{:S(2)}, u32[]{:S(2)}) %collective-permute-start.33) | collective-permute-done | bytes 262176 | tf_op jit(solution)/shard_map/ppermute | solution.py:280
  133.8 1.1 shard_map.86
  (49 shorter events, 0.6 us)
Async XLA Ops:
  0.6 24.1 %collective-permute-start = (bf16[128,2048]{1,0:T(8,128)(2,1)}, bf16[128,2048]{1,0:T(8,128)(2,1)S(1)}, u32[]{:S(2)}, u32[]{:S(2)}) collective-permute-start(bf16[128,2048]{1,0:T(8,128)(2,1)} %refs_0_.1), channel_id=1, source_target_pairs={{0,4},{1,5},{2,6},{3,7},{4,0},{5,1},{6,2},{7,3},{8,12},{9,13},{10,... | collective-permute-start | bytes 1572872 | tf_op jit(solution)/shard_map/ppermute | solution.py:280
  3.7 21.0 %collective-permute-start.2 = (bf16[128,2048]{1,0:T(8,128)(2,1)}, bf16[128,2048]{1,0:T(8,128)(2,1)S(1)}, u32[]{:S(2)}, u32[]{:S(2)}) collective-permute-start(bf16[128,2048]{1,0:T(8,128)(2,1)} %refs_0_.1), channel_id=1, source_target_pairs={{0,2},{1,3},{2,0},{3,1},{4,6},{5,7},{6,4},{7,5},{8,10},{9,11},{10,... | collective-permute-start | bytes 1572872 | tf_op jit(solution)/shard_map/ppermute | solution.py:280
  5.2 19.5 %collective-permute-start.3 = (bf16[128,2048]{1,0:T(8,128)(2,1)}, bf16[128,2048]{1,0:T(8,128)(2,1)S(1)}, u32[]{:S(2)}, u32[]{:S(2)}) collective-permute-start(bf16[128,2048]{1,0:T(8,128)(2,1)} %refs_0_.1), channel_id=1, source_target_pairs={{0,1},{1,0},{2,3},{3,2},{4,5},{5,4},{6,7},{7,6},{8,9},{9,8},{10,11... | collective-permute-start | bytes 1572872 | tf_op jit(solution)/shard_map/ppermute | solution.py:280
  5.2 1.1 copy-start.6
  6.3 0.7 copy-start.8
  7.0 0.7 copy-start.9
  7.8 16.9 %collective-permute-start.1 = (bf16[64,2048]{1,0:T(8,128)(2,1)S(1)}, bf16[64,2048]{1,0:T(8,128)(2,1)S(1)}, u32[]{:S(2)}, u32[]{:S(2)}) collective-permute-start(bf16[64,2048]{1,0:T(8,128)(2,1)S(1)} %get-tuple-element.75), channel_id=1, source_target_pairs={{0,8},{1,9},{2,10},{3,11},{4,12},{5,13},{6,14},{7,15},{8,0},{9,1},... | collective-permute-start | bytes 786440 | tf_op jit(solution)/shard_map/ppermute | solution.py:280
  24.7 0.7 copy-start.10
  25.4 15.9 %collective-permute-start.5 = (bf16[128,2048]{1,0:T(8,128)(2,1)S(1)}, bf16[128,2048]{1,0:T(8,128)(2,1)S(1)}, u32[]{:S(2)}, u32[]{:S(2)}) collective-permute-start(bf16[128,2048]{1,0:T(8,128)(2,1)S(1)} %collective-permute-done.refs_0_), channel_id=1, source_target_pairs={{0,2},{1,3},{2,0},{3,1},{4,6},{5,7},{6,4},{7,5},{8,10},{9,11},{10,... | collective-permute-start | bytes 1572872 | tf_op jit(solution)/shard_map/ppermute | solution.py:280
  25.9 15.4 %collective-permute-start.6 = (bf16[128,2048]{1,0:T(8,128)(2,1)S(1)}, bf16[128,2048]{1,0:T(8,128)(2,1)S(1)}, u32[]{:S(2)}, u32[]{:S(2)}) collective-permute-start(bf16[128,2048]{1,0:T(8,128)(2,1)S(1)} %collective-permute-done.refs_0_), channel_id=1, source_target_pairs={{0,1},{1,0},{2,3},{3,2},{4,5},{5,4},{6,7},{7,6},{8,9},{9,8},{10,11... | collective-permute-start | bytes 1572872 | tf_op jit(solution)/shard_map/ppermute | solution.py:280
  25.9 15.4 %collective-permute-start.7 = (bf16[128,2048]{1,0:T(8,128)(2,1)S(1)}, bf16[128,2048]{1,0:T(8,128)(2,1)S(1)}, u32[]{:S(2)}, u32[]{:S(2)}) collective-permute-start(bf16[128,2048]{1,0:T(8,128)(2,1)S(1)} %collective-permute-done.2.refs_1_), channel_id=1, source_target_pairs={{0,1},{1,0},{2,3},{3,2},{4,5},{5,4},{6,7},{7,6},{8,9},{9,8},{10,11... | collective-permute-start | bytes 1572872 | tf_op jit(solution)/shard_map/ppermute | solution.py:280
  26.4 14.8 %collective-permute-start.4 = (bf16[64,2048]{1,0:T(8,128)(2,1)S(1)}, bf16[64,2048]{1,0:T(8,128)(2,1)}, u32[]{:S(2)}, u32[]{:S(2)}) collective-permute-start(bf16[64,2048]{1,0:T(8,128)(2,1)S(1)} %get-tuple-element.79), channel_id=1, source_target_pairs={{0,8},{1,9},{2,10},{3,11},{4,12},{5,13},{6,14},{7,15},{8,0},{9,1},... | collective-permute-start | bytes 786440 | tf_op jit(solution)/shard_map/ppermute | solution.py:280
  27.6 1.9 %copy-start = (bf16[1,2048,768]{2,1,0:T(8,128)(2,1)S(1)}, bf16[1,2048,768]{2,1,0:T(8,128)(2,1)}, u32[]{:S(2)}) copy-start(bf16[1,2048,768]{2,1,0:T(8,128)(2,1)} %param.9) | copy-start | bytes 9437188
  29.5 1.9 %copy-start.2 = (bf16[1,2048,768]{2,1,0:T(8,128)(2,1)S(1)}, bf16[1,2048,768]{2,1,0:T(8,128)(2,1)}, u32[]{:S(2)}) copy-start(bf16[1,2048,768]{2,1,0:T(8,128)(2,1)} %param.10) | copy-start | bytes 9437188
  31.4 1.9 %copy-start.4 = (bf16[1,768,2048]{2,1,0:T(8,128)(2,1)S(1)}, bf16[1,768,2048]{2,1,0:T(8,128)(2,1)}, u32[]{:S(2)}) copy-start(bf16[1,768,2048]{2,1,0:T(8,128)(2,1)} %param.11) | copy-start | bytes 9437188
  33.3 12.1 %copy-start.1 = (bf16[1,2048,768]{2,1,0:T(8,128)(2,1)S(1)}, bf16[1,2048,768]{2,1,0:T(8,128)(2,1)}, u32[]{:S(2)}) copy-start(bf16[1,2048,768]{2,1,0:T(8,128)(2,1)} %param.9) | copy-start | bytes 9437188
  33.3 12.1 %copy-start.3 = (bf16[1,2048,768]{2,1,0:T(8,128)(2,1)S(1)}, bf16[1,2048,768]{2,1,0:T(8,128)(2,1)}, u32[]{:S(2)}) copy-start(bf16[1,2048,768]{2,1,0:T(8,128)(2,1)} %param.10) | copy-start | bytes 9437188
  33.3 12.1 %copy-start.5 = (bf16[1,768,2048]{2,1,0:T(8,128)(2,1)S(1)}, bf16[1,768,2048]{2,1,0:T(8,128)(2,1)}, u32[]{:S(2)}) copy-start(bf16[1,768,2048]{2,1,0:T(8,128)(2,1)} %param.11) | copy-start | bytes 9437188
  41.3 4.1 %collective-permute-start.11 = (bf16[128,2048]{1,0:T(8,128)(2,1)S(1)}, bf16[128,2048]{1,0:T(8,128)(2,1)S(1)}, u32[]{:S(2)}, u32[]{:S(2)}) collective-permute-start(bf16[128,2048]{1,0:T(8,128)(2,1)S(1)} %collective-permute-done.5.refs_1_), channel_id=1, source_target_pairs={{0,1},{1,0},{2,3},{3,2},{4,5},{5,4},{6,7},{7,6},{8,9},{9,8},{10,11... | collective-permute-start | bytes 1572872 | tf_op jit(solution)/shard_map/ppermute | solution.py:280
  43.3 7.6 %copy-start.7 = (bf16[128,2048]{1,0:T(8,128)(2,1)S(1)}, bf16[128,2048]{1,0:T(8,128)(2,1)}, u32[]{:S(2)}) copy-start(bf16[128,2048]{1,0:T(8,128)(2,1)} %refs_0_.1) | copy-start | bytes 1572868
  43.3 13.1 %collective-permute-start.10 = (bf16[128,2048]{1,0:T(8,128)(2,1)S(1)}, bf16[128,2048]{1,0:T(8,128)(2,1)S(1)}, u32[]{:S(2)}, u32[]{:S(2)}) collective-permute-start(bf16[128,2048]{1,0:T(8,128)(2,1)S(1)} %constant_dynamic-update-slice_fusion.refs_0_), channel_id=1, source_target_pairs={{0,1},{1,0},{2,3},{3,2},{4,5},{5,4},{6,7},{7,6},{8,9},{9,8},{10,11... | collective-permute-start | bytes 1572872 | tf_op jit(solution)/shard_map/ppermute | solution.py:280
  43.9 13.9 %collective-permute-start.8 = (bf16[128,2048]{1,0:T(8,128)(2,1)S(1)}, bf16[128,2048]{1,0:T(8,128)(2,1)S(1)}, u32[]{:S(2)}, u32[]{:S(2)}) collective-permute-start(bf16[128,2048]{1,0:T(8,128)(2,1)S(1)} %constant_dynamic-update-slice_fusion.refs_0_), channel_id=1, source_target_pairs={{0,4},{1,5},{2,6},{3,7},{4,0},{5,1},{6,2},{7,3},{8,12},{9,13},{10,... | collective-permute-start | bytes 1572872 | tf_op jit(solution)/shard_map/ppermute | solution.py:280
  43.9 14.0 %collective-permute-start.9 = (bf16[128,2048]{1,0:T(8,128)(2,1)S(1)}, bf16[128,2048]{1,0:T(8,128)(2,1)S(1)}, u32[]{:S(2)}, u32[]{:S(2)}) collective-permute-start(bf16[128,2048]{1,0:T(8,128)(2,1)S(1)} %constant_dynamic-update-slice_fusion.refs_0_), channel_id=1, source_target_pairs={{0,2},{1,3},{2,0},{3,1},{4,6},{5,7},{6,4},{7,5},{8,10},{9,11},{10,... | collective-permute-start | bytes 1572872 | tf_op jit(solution)/shard_map/ppermute | solution.py:280
  50.9 7.0 %collective-permute-start.12 = (bf16[128,2048]{1,0:T(8,128)(2,1)S(1)}, bf16[128,2048]{1,0:T(8,128)(2,1)S(1)}, u32[]{:S(2)}, u32[]{:S(2)}) collective-permute-start(bf16[128,2048]{1,0:T(8,128)(2,1)S(1)} %get-tuple-element.95), channel_id=1, source_target_pairs={{0,1},{1,0},{2,3},{3,2},{4,5},{5,4},{6,7},{7,6},{8,9},{9,8},{10,11... | collective-permute-start | bytes 1572872 | tf_op jit(solution)/shard_map/ppermute | solution.py:280
  57.9 3.6 %collective-permute-start.16 = (bf16[128,2048]{1,0:T(8,128)(2,1)S(1)}, bf16[128,2048]{1,0:T(8,128)(2,1)S(1)}, u32[]{:S(2)}, u32[]{:S(2)}) collective-permute-start(bf16[128,2048]{1,0:T(8,128)(2,1)S(1)} %collective-permute-done.9.refs_1_), channel_id=1, source_target_pairs={{0,1},{1,0},{2,3},{3,2},{4,5},{5,4},{6,7},{7,6},{8,9},{9,8},{10,11... | collective-permute-start | bytes 1572872 | tf_op jit(solution)/shard_map/ppermute | solution.py:280
  57.9 16.2 %collective-permute-start.13 = (bf16[128,2048]{1,0:T(8,128)(2,1)S(1)}, bf16[128,2048]{1,0:T(8,128)(2,1)S(1)}, u32[]{:S(2)}, u32[]{:S(2)}) collective-permute-start(bf16[128,2048]{1,0:T(8,128)(2,1)S(1)} %collective-permute-done.9.refs_1_), channel_id=1, source_target_pairs={{0,4},{1,5},{2,6},{3,7},{4,0},{5,1},{6,2},{7,3},{8,12},{9,13},{10,... | collective-permute-start | bytes 1572872 | tf_op jit(solution)/shard_map/ppermute | solution.py:280
  59.5 8.1 %collective-permute-start.18 = (bf16[128,2048]{1,0:T(8,128)(2,1)S(1)}, bf16[128,2048]{1,0:T(8,128)(2,1)S(1)}, u32[]{:S(2)}, u32[]{:S(2)}) collective-permute-start(bf16[128,2048]{1,0:T(8,128)(2,1)S(1)} %collective-permute-done.8.refs_0_), channel_id=1, source_target_pairs={{0,1},{1,0},{2,3},{3,2},{4,5},{5,4},{6,7},{7,6},{8,9},{9,8},{10,11... | collective-permute-start | bytes 1572872 | tf_op jit(solution)/shard_map/ppermute | solution.py:280
  59.9 14.2 %collective-permute-start.14 = (bf16[128,2048]{1,0:T(8,128)(2,1)S(1)}, bf16[128,2048]{1,0:T(8,128)(2,1)S(1)}, u32[]{:S(2)}, u32[]{:S(2)}) collective-permute-start(bf16[128,2048]{1,0:T(8,128)(2,1)S(1)} %add_convert_fusion.2), channel_id=1, source_target_pairs={{0,2},{1,3},{2,0},{3,1},{4,6},{5,7},{6,4},{7,5},{8,10},{9,11},{10,... | collective-permute-start | bytes 1572872 | tf_op jit(solution)/shard_map/ppermute | solution.py:280
  61.4 12.7 %collective-permute-start.15 = (bf16[128,2048]{1,0:T(8,128)(2,1)S(1)}, bf16[128,2048]{1,0:T(8,128)(2,1)S(1)}, u32[]{:S(2)}, u32[]{:S(2)}) collective-permute-start(bf16[128,2048]{1,0:T(8,128)(2,1)S(1)} %get-tuple-element.99), channel_id=1, source_target_pairs={{0,1},{1,0},{2,3},{3,2},{4,5},{5,4},{6,7},{7,6},{8,9},{9,8},{10,11... | collective-permute-start | bytes 1572872 | tf_op jit(solution)/shard_map/ppermute | solution.py:280
  67.1 7.0 %collective-permute-start.17 = (bf16[128,2048]{1,0:T(8,128)(2,1)S(1)}, bf16[128,2048]{1,0:T(8,128)(2,1)S(1)}, u32[]{:S(2)}, u32[]{:S(2)}) collective-permute-start(bf16[128,2048]{1,0:T(8,128)(2,1)S(1)} %get-tuple-element.101), channel_id=1, source_target_pairs={{0,1},{1,0},{2,3},{3,2},{4,5},{5,4},{6,7},{7,6},{8,9},{9,8},{10,11... | collective-permute-start | bytes 1572872 | tf_op jit(solution)/shard_map/ppermute | solution.py:280
  67.7 11.1 %collective-permute-start.20 = (bf16[256,2048]{1,0:T(8,128)(2,1)S(1)}, bf16[256,2048]{1,0:T(8,128)(2,1)S(1)}, u32[]{:S(2)}, u32[]{:S(2)}) collective-permute-start(bf16[256,2048]{1,0:T(8,128)(2,1)S(1)} %get-tuple-element.114), channel_id=1, source_target_pairs={{0,1},{1,0},{2,3},{3,2},{4,5},{5,4},{6,7},{7,6},{8,9},{9,8},{10,11... | collective-permute-start | bytes 3145736 | tf_op jit(solution)/shard_map/ppermute | solution.py:280
  74.1 2.0 %collective-permute-start.19 = (bf16[128,2048]{1,0:T(8,128)(2,1)S(1)}, bf16[128,2048]{1,0:T(8,128)(2,1)S(1)}, u32[]{:S(2)}, u32[]{:S(2)}) collective-permute-start(bf16[128,2048]{1,0:T(8,128)(2,1)S(1)} %collective-permute-done.13.refs_0_), channel_id=1, source_target_pairs={{0,1},{1,0},{2,3},{3,2},{4,5},{5,4},{6,7},{7,6},{8,9},{9,8},{10,11... | collective-permute-start | bytes 1572872 | tf_op jit(solution)/shard_map/ppermute | solution.py:280
  74.2 4.6 %collective-permute-start.21 = (bf16[128,2048]{1,0:T(8,128)(2,1)S(1)}, bf16[128,2048]{1,0:T(8,128)(2,1)S(1)}, u32[]{:S(2)}, u32[]{:S(2)}) collective-permute-start(bf16[128,2048]{1,0:T(8,128)(2,1)S(1)} %get-tuple-element.115), channel_id=1, source_target_pairs={{0,1},{1,0},{2,3},{3,2},{4,5},{5,4},{6,7},{7,6},{8,9},{9,8},{10,11... | collective-permute-start | bytes 1572872 | tf_op jit(solution)/shard_map/ppermute | solution.py:280
  74.7 4.1 %collective-permute-start.22 = (bf16[128,2048]{1,0:T(8,128)(2,1)S(1)}, bf16[128,2048]{1,0:T(8,128)(2,1)S(1)}, u32[]{:S(2)}, u32[]{:S(2)}) collective-permute-start(bf16[128,2048]{1,0:T(8,128)(2,1)S(1)} %get-tuple-element.116), channel_id=1, source_target_pairs={{0,1},{1,0},{2,3},{3,2},{4,5},{5,4},{6,7},{7,6},{8,9},{9,8},{10,11... | collective-permute-start | bytes 1572872 | tf_op jit(solution)/shard_map/ppermute | solution.py:280
  78.8 9.0 %collective-permute-start.23 = (bf16[128,2048]{1,0:T(8,128)(2,1)S(1)}, bf16[128,2048]{1,0:T(8,128)(2,1)S(1)}, u32[]{:S(2)}, u32[]{:S(2)}) collective-permute-start(bf16[128,2048]{1,0:T(8,128)(2,1)S(1)} %get-tuple-element.121), channel_id=1, source_target_pairs={{0,1},{1,0},{2,3},{3,2},{4,5},{5,4},{6,7},{7,6},{8,9},{9,8},{10,11... | collective-permute-start | bytes 1572872 | tf_op jit(solution)/shard_map/ppermute | solution.py:280
  79.1 8.7 %collective-permute-start.24 = (bf16[64,2048]{1,0:T(8,128)(2,1)S(1)}, bf16[64,2048]{1,0:T(8,128)(2,1)S(1)}, u32[]{:S(2)}, u32[]{:S(2)}) collective-permute-start(bf16[64,2048]{1,0:T(8,128)(2,1)S(1)} %get-tuple-element.149), channel_id=1, source_target_pairs={{0,2},{1,3},{2,0},{3,1},{4,6},{5,7},{6,4},{7,5},{8,10},{9,11},{10,... | collective-permute-start | bytes 786440 | tf_op jit(solution)/shard_map/ppermute | solution.py:280
  88.0 9.3 %collective-permute-start.25 = (bf16[64,2048]{1,0:T(8,128)(2,1)S(1)}, bf16[64,2048]{1,0:T(8,128)(2,1)S(1)}, u32[]{:S(2)}, u32[]{:S(2)}) collective-permute-start(bf16[64,2048]{1,0:T(8,128)(2,1)S(1)} %get-tuple-element.126), channel_id=1, source_target_pairs={{0,2},{1,3},{2,0},{3,1},{4,6},{5,7},{6,4},{7,5},{8,10},{9,11},{10,... | collective-permute-start | bytes 786440 | tf_op jit(solution)/shard_map/ppermute | solution.py:280
  89.6 11.9 %collective-permute-start.26 = (bf16[64,2048]{1,0:T(8,128)(2,1)S(1)}, bf16[64,2048]{1,0:T(8,128)(2,1)S(1)}, u32[]{:S(2)}, u32[]{:S(2)}) collective-permute-start(bf16[64,2048]{1,0:T(8,128)(2,1)S(1)} %get-tuple-element.127), channel_id=1, source_target_pairs={{0,2},{1,3},{2,0},{3,1},{4,6},{5,7},{6,4},{7,5},{8,10},{9,11},{10,... | collective-permute-start | bytes 786440 | tf_op jit(solution)/shard_map/ppermute | solution.py:280
  90.1 13.5 %collective-permute-start.27 = (bf16[64,2048]{1,0:T(8,128)(2,1)S(1)}, bf16[64,2048]{1,0:T(8,128)(2,1)S(1)}, u32[]{:S(2)}, u32[]{:S(2)}) collective-permute-start(bf16[64,2048]{1,0:T(8,128)(2,1)S(1)} %get-tuple-element.128), channel_id=1, source_target_pairs={{0,8},{1,9},{2,10},{3,11},{4,12},{5,13},{6,14},{7,15},{8,0},{9,1},... | collective-permute-start | bytes 786440 | tf_op jit(solution)/shard_map/ppermute | solution.py:280
  91.0 12.7 %collective-permute-start.28 = (bf16[64,2048]{1,0:T(8,128)(2,1)S(1)}, bf16[64,2048]{1,0:T(8,128)(2,1)S(1)}, u32[]{:S(2)}, u32[]{:S(2)}) collective-permute-start(bf16[64,2048]{1,0:T(8,128)(2,1)S(1)} %get-tuple-element.129), channel_id=1, source_target_pairs={{0,4},{1,5},{2,6},{3,7},{4,0},{5,1},{6,2},{7,3},{8,12},{9,13},{10,... | collective-permute-start | bytes 786440 | tf_op jit(solution)/shard_map/ppermute | solution.py:280
  103.9 14.2 %collective-permute-start.29 = (bf16[64,2048]{1,0:T(8,128)(2,1)S(1)}, bf16[64,2048]{1,0:T(8,128)(2,1)S(1)}, u32[]{:S(2)}, u32[]{:S(2)}) collective-permute-start(bf16[64,2048]{1,0:T(8,128)(2,1)S(1)} %get-tuple-element.151), channel_id=1, source_target_pairs={{0,8},{1,9},{2,10},{3,11},{4,12},{5,13},{6,14},{7,15},{8,0},{9,1},... | collective-permute-start | bytes 786440 | tf_op jit(solution)/shard_map/ppermute | solution.py:280
  104.6 13.7 %collective-permute-start.30 = (bf16[64,2048]{1,0:T(8,128)(2,1)S(1)}, bf16[64,2048]{1,0:T(8,128)(2,1)S(1)}, u32[]{:S(2)}, u32[]{:S(2)}) collective-permute-start(bf16[64,2048]{1,0:T(8,128)(2,1)S(1)} %get-tuple-element.150), channel_id=1, source_target_pairs={{0,4},{1,5},{2,6},{3,7},{4,0},{5,1},{6,2},{7,3},{8,12},{9,13},{10,... | collective-permute-start | bytes 786440 | tf_op jit(solution)/shard_map/ppermute | solution.py:280
  106.5 11.8 %collective-permute-start.31 = (bf16[64,2048]{1,0:T(8,128)(2,1)S(1)}, bf16[64,2048]{1,0:T(8,128)(2,1)S(1)}, u32[]{:S(2)}, u32[]{:S(2)}) collective-permute-start(bf16[64,2048]{1,0:T(8,128)(2,1)S(1)} %get-tuple-element.134), channel_id=1, source_target_pairs={{0,2},{1,3},{2,0},{3,1},{4,6},{5,7},{6,4},{7,5},{8,10},{9,11},{10,... | collective-permute-start | bytes 786440 | tf_op jit(solution)/shard_map/ppermute | solution.py:280
  118.5 13.9 %collective-permute-start.34 = (bf16[64,2048]{1,0:T(8,128)(2,1)S(1)}, bf16[64,2048]{1,0:T(8,128)(2,1)S(1)}, u32[]{:S(2)}, u32[]{:S(2)}) collective-permute-start(bf16[64,2048]{1,0:T(8,128)(2,1)S(1)} %add_convert_fusion.3), channel_id=1, source_target_pairs={{0,8},{1,9},{2,10},{3,11},{4,12},{5,13},{6,14},{7,15},{8,0},{9,1},... | collective-permute-start | bytes 786440 | tf_op jit(solution)/shard_map/ppermute | solution.py:280
  118.9 14.9 %collective-permute-start.32 = (bf16[128,2048]{1,0:T(8,128)(2,1)S(1)}, bf16[128,2048]{1,0:T(8,128)(2,1)S(1)}, u32[]{:S(2)}, u32[]{:S(2)}) collective-permute-start(bf16[128,2048]{1,0:T(8,128)(2,1)S(1)} %add_convert_fusion), channel_id=1, source_target_pairs={{0,2},{1,3},{2,0},{3,1},{4,6},{5,7},{6,4},{7,5},{8,10},{9,11},{10,... | collective-permute-start | bytes 1572872 | tf_op jit(solution)/shard_map/ppermute | solution.py:280
  120.0 13.8 %collective-permute-start.33 = (bf16[64,2048]{1,0:T(8,128)(2,1)S(1)}, bf16[64,2048]{1,0:T(8,128)(2,1)S(1)}, u32[]{:S(2)}, u32[]{:S(2)}) collective-permute-start(bf16[64,2048]{1,0:T(8,128)(2,1)S(1)} %add_convert_fusion.4), channel_id=1, source_target_pairs={{0,4},{1,5},{2,6},{3,7},{4,0},{5,1},{6,2},{7,3},{8,12},{9,13},{10,... | collective-permute-start | bytes 786440 | tf_op jit(solution)/shard_map/ppermute | solution.py:280

commit v20 on v18

--- a/solution.py
+++ b/solution.py
@@ -299,50 +299,59 @@
     b2 = column(a2)
     d1 = sibling(b1)
     c2 = sibling(a2)
-    keep1, give1, *give1_side, act1 = expert(1, a1, b1, c1, d1, pieces=(tok, tok))
-    got1_side = [sibling(piece) for piece in give1_side]
-    a3, b2, c2, keep1, give1, act1, *got1_side = together(
-        a3, b2, c2, keep1, give1, act1, *got1_side
+    keep1, give1, give1_side, act1 = expert(1, a1, b1, c1, d1, pieces=(tok, tok))
+    got1_side = sibling(give1_side)
+    a3, b2, c2, keep1, give1, act1, got1_side = together(
+        a3, b2, c2, keep1, give1, act1, got1_side
     )
     b3 = pair(b2)
-    came1 = column(summed(keep1[tok:], jnp.concatenate(got1_side, axis=0)))
+    came1_low = column(summed(keep1[tok : tok + half], got1_side[:half]))
     got1 = sibling(give1)
     d2 = sibling(b2)
     c3 = sibling(a3)
-    keep2, give2, give2_side, act2 = expert(2, a2, b2, c2, d2, pieces=(tok, tok))
-    got2_side = sibling(give2_side)
+    keep2, give2, give2_low, give2_high, act2 = expert(
+        2, a2, b2, c2, d2, pieces=(tok, half, half)
+    )
+    got2_high = sibling(give2_high)
     keep3, give3, act3 = expert(3, a3, c3, picked=(0, 2))
-    b3, came1, got1, got2_side, keep2, give2, act2, keep3, give3, act3 = together(
-        b3, came1, got1, got2_side, keep2, give2, act2, keep3, give3, act3
+    got0 = sibling(give0)
+    b3, came1_low, got0, got1, got2_high, keep2, give2, give2_low, act2, keep3, give3, act3 = (
+        together(
+            b3, came1_low, got0, got1, got2_high, keep2, give2, give2_low, act2, keep3, give3, act3
+        )
     )
     d3 = sibling(b3)
-    near1 = summed(keep1[:tok], got1, came1)
-
-    side_high = column(summed(keep2[tok + half :], got2_side[half:]))
-    got0, got2, got3 = sibling(give0), sibling(give2), sibling(give3)
+    near1 = summed(keep1[:half], got1[:half], came1_low)
+
+    side_high = column(summed(keep2[tok + half :], got2_high))
+    got2 = sibling(give2)
     keep3_side, give3_side, act4 = expert(3, b3, d3, picked=(1, 3))
-    keep3_side, give3_side, act4, got0, got2, got3, side_high, near1 = together(
-        keep3_side, give3_side, act4, got0, got2, got3, side_high, near1
-    )
+    keep3_side, give3_side, act4, got2, side_high, near1 = together(
+        keep3_side, give3_side, act4, got2, side_high, near1
+    )
+    got2_low, got3 = sibling(give2_low), sibling(give3)
     far2_high = far(summed(keep2[half:tok], got2[half:], side_high))
     got3_side = sibling(give3_side)
     came3_low = column(summed(keep3_side[:half], got3_side[:half]))
     came3_high = column(summed(keep3_side[half:], got3_side[half:]))
-    near1_low = pair(near1[:half])
+    near1_low = pair(near1)
     side0 = summed(keep0[tok:], got0[tok:])
-    side2 = summed(keep2[tok : tok + half], got2_side[:half])
-    came3_low, came3_high, far2_high, near1_low, side0, side2 = together(
-        came3_low, came3_high, far2_high, near1_low, side0, side2
+    side1 = summed(keep1[tok + half :], got1_side[half:])
+    came3_low, came3_high, far2_high, near1_low, side0, side1, got2_low, got3 = together(
+        came3_low, came3_high, far2_high, near1_low, side0, side1, got2_low, got3
     )
     far3_high = far(summed(keep3[half:], got3[half:], came3_high))
     pair3_low = pair(summed(keep3[:half], got3[:half], came3_low))
-    side_low = column(side2)
+    side_low = column(summed(keep2[tok : tok + half], got2_low))
+    came1_high = column(side1)
     gram = gram_pass(tables, act0, act1, act2, act3, act4)
-    far3_high, pair3_low, side_low, side0, gram = together(
-        far3_high, pair3_low, side_low, side0, gram
-    )
-    far2_low = far(summed(keep2[:half], got2[:half], pair3_low, side_low))
-    near1_high = pair(summed(near1[half:], far3_high))
+    far3_high, pair3_low, side_low, came1_high, side0, gram = together(
+        far3_high, pair3_low, side_low, came1_high, side0, gram
+    )
+    far2_low = summed(keep2[:half], got2[:half], pair3_low, side_low)
+    far2_low, far3_high, came1_high, side0 = together(far2_low, far3_high, came1_high, side0)
+    far2_low = far(far2_low)
+    near1_high = pair(summed(keep1[half:tok], got1[half:], came1_high, far3_high))
     last0 = column(side0)
     mixed = mix_pass(
         keep0, got0, last0, near1_low, near1_high, far2_low, far2_high

time: 129 us -> 129 us (level)
  waiting for transfers between devices: 45 us -> 43.5 us
    ppermute x35 -> x37, waiting for transfers between devices: 45 us -> 43.5 us  [swapped(): return lax.ppermute(array, 'expert', [(i, i ^ bit) for i in range(size)])]
    ppermute x35 -> x37, starting transfers between devices: 30.1 us -> 31.2 us  [swapped(): return lax.ppermute(array, 'expert', [(i, i ^ bit) for i in range(size)])]
  transfers between devices with their start and end apart: 35 -> 37, of which waited for: 10 -> 11; matrix products, arithmetic and copies ran while one was open for 1% -> 1% of each run, Pallas kernels for 20% -> 20%
where the time goes in v20:
time: 129 us; the launch traced here: 128 us
  waiting for transfers between devices  43.5 us (34%)
  starting transfers between devices  31.2 us (24%)
  Pallas kernels  27.1 us (21%)
  blocking collectives  14.2 us (11%)
  local copies, waits for them, and re-layouts  9.97 us (8%)
    ppermute x37, waiting for transfers between devices, swapped(): return lax.ppermute(array, 'expert', [(i, i ^ bit) for i in range(size)])  43.5 us
    ppermute x37, starting transfers between devices, swapped(): return lax.ppermute(array, 'expert', [(i, i ^ bit) for i in range(size)])  31.2 us
    pallas_call x5, Pallas kernels, plane_pass(): pl.pallas_call(functools.partial(plane_kernel, k, picked, len(pieces)), o...  22 us
    all_to_all x1, blocking collectives, staged(): lax.all_to_all(mine, 'expert', split_axis=0, concat_axis=0, tiled=True)  14.2 us
    unnamed x25, local copies, waits for them, and re-layouts  9.86 us
    pallas_call x1, Pallas kernels, gram_pass(): pl.pallas_call(gram_kernel, out_shape=jax.ShapeDtypeStruct((hidden, hidde...  3.14 us
  transfers between devices with their start and end apart: 37, of which 11 were waited for; matrix products, arithmetic and copies ran while one was open for 1% of the time, Pallas kernels for 20%

profile of v20, /device:TPU:0, one launch (start us, length us, event | category | flops | bytes accessed | tf_op | source)
XLA Modules:
  0.0 128.1 jit_solution(11684421015952798836)
XLA Ops:
  0.6 3.1 %collective-permute-start = (bf16[128,2048]{1,0:T(8,128)(2,1)}, bf16[128,2048]{1,0:T(8,128)(2,1)S(1)}, u32[]{:S(2)}, u32[]{:S(2)}) collective-permute-start(bf16[128,2048]{1,0:T(8,128)(2,1)} %refs_0_.1), channel_id=1, source_target_pairs={{0,4},{1,5},{2,6},{3,7},{4,0},{5,1},{6,2},{7,3},{8,12},{9,13},{10,... | collective-permute-start | bytes 1572872 | tf_op jit(solution)/shard_map/ppermute | solution.py:256
  3.7 1.5 %collective-permute-start.2 = (bf16[128,2048]{1,0:T(8,128)(2,1)}, bf16[128,2048]{1,0:T(8,128)(2,1)S(1)}, u32[]{:S(2)}, u32[]{:S(2)}) collective-permute-start(bf16[128,2048]{1,0:T(8,128)(2,1)} %refs_0_.1), channel_id=1, source_target_pairs={{0,2},{1,3},{2,0},{3,1},{4,6},{5,7},{6,4},{7,5},{8,10},{9,11},{10,... | collective-permute-start | bytes 1572872 | tf_op jit(solution)/shard_map/ppermute | solution.py:256
  5.2 1.1 copy-done.6
  6.3 0.7 copy-done.8
  7.0 0.7 copy-done.9
  7.7 0.1 shard_map.77
  7.8 2.7 %collective-permute-start.1 = (bf16[64,2048]{1,0:T(8,128)(2,1)S(1)}, bf16[64,2048]{1,0:T(8,128)(2,1)S(1)}, u32[]{:S(2)}, u32[]{:S(2)}) collective-permute-start(bf16[64,2048]{1,0:T(8,128)(2,1)S(1)} %get-tuple-element.79), channel_id=1, source_target_pairs={{0,8},{1,9},{2,10},{3,11},{4,12},{5,13},{6,14},{7,15},{8,0},{9,1},... | collective-permute-start | bytes 786440 | tf_op jit(solution)/shard_map/ppermute | solution.py:256
  10.5 14.2 %all_to_all.12 = f32[16,1,128]{2,1,0:T(1,128)S(1)} all-to-all(f32[16,1,128]{2,1,0:T(1,128)S(1)} %bitcast.42), channel_id=1, replica_groups=mesh['parts'=2,'expert'=16] {'expert'}, dimensions={0} | all-to-all | bytes 16384 | tf_op jit(solution)/shard_map/all_to_all | solution.py:285
  24.8 0.7 copy-done.10
  25.4 0.5 collective-permute-start.5
  25.9 0.2 collective-permute-start.6
  26.3 1.1 collective-permute-start.4
  27.4 0.7 shard_map.78.tables
  28.2 1.9 %copy-done = bf16[1,2048,768]{2,1,0:T(8,128)(2,1)S(1)} copy-done((bf16[1,2048,768]{2,1,0:T(8,128)(2,1)S(1)}, bf16[1,2048,768]{2,1,0:T(8,128)(2,1)}, u32[]{:S(2)}) %copy-start) | copy-done | bytes 3145752
  30.0 1.9 %copy-done.2 = bf16[1,2048,768]{2,1,0:T(8,128)(2,1)S(1)} copy-done((bf16[1,2048,768]{2,1,0:T(8,128)(2,1)S(1)}, bf16[1,2048,768]{2,1,0:T(8,128)(2,1)}, u32[]{:S(2)}) %copy-start.2) | copy-done | bytes 3145752
  31.9 1.9 %copy-done.4 = bf16[1,768,2048]{2,1,0:T(8,128)(2,1)S(1)} copy-done((bf16[1,768,2048]{2,1,0:T(8,128)(2,1)S(1)}, bf16[1,768,2048]{2,1,0:T(8,128)(2,1)}, u32[]{:S(2)}) %copy-start.4) | copy-done | bytes 3145752
  33.8 1.0 copy-done.7
  34.9 5.5 %shard_map.79 = (bf16[256,2048]{1,0:T(8,128)(2,1)S(1)}, bf16[256,2048]{1,0:T(8,128)(2,1)S(1)}, bf16[320,768]{1,0:T(8,128)(2,1)S(1)}) custom-call(f32[16,512]{1,0:T(8,128)S(1)} %shard_map.78.tables, bf16[128,2048]{1,0:T(8,128)(2,1)S(1)} %copy-done.7, bf16[128,2048]{1,0:T(8,128)(2,1)S(1)} %collective-permute-done.2.refs_1_, ...), custom_call_target="tpu_custom_call" | custom-call | flops 4362076160 | bytes 13631488 | tf_op jit(solution)/shard_map/pallas_call | solution.py:178
  40.4 1.0 collective-permute-done.4
  41.4 0.7 collective-permute-start.8
  42.1 1.1 collective-permute-start.9
  43.3 5.5 %shard_map.80 = (bf16[256,2048]{1,0:T(8,128)(2,1)S(1)}, bf16[128,2048]{1,0:T(8,128)(2,1)S(1)}, bf16[128,2048]{1,0:T(8,128)(2,1)S(1)}, bf16[320,768]{1,0:T(8,128)(2,1)S(1)}) custom-call(f32[16,512]{1,0:T(8,128)S(1)} %shard_map.78.tables, bf16[128,2048]{1,0:T(8,128)(2,1)S(1)} %collective-permute-done.refs_0_, ...), custom_call_target="tpu_custom_call" | custom-call | flops 4362076160 | bytes 13631488 | tf_op jit(solution)/shard_map/pallas_call | solution.py:178
  48.7 0.5 collective-permute-start.12
  49.3 6.5 %collective-permute-done.8.refs_0_ = bf16[128,2048]{1,0:T(8,128)(2,1)S(1)} collective-permute-done((bf16[128,2048]{1,0:T(8,128)(2,1)S(1)}, bf16[128,2048]{1,0:T(8,128)(2,1)S(1)}, u32[]{:S(2)}, u32[]{:S(2)}) %collective-permute-start.8) | collective-permute-done | bytes 524320 | tf_op jit(solution)/shard_map/ppermute | solution.py:256
  55.8 0.3 collective-permute-done.9.refs_1_
  56.1 0.5 collective-permute-start.15
  56.6 1.4 %collective-permute-start.13 = (bf16[128,2048]{1,0:T(8,128)(2,1)S(1)}, bf16[128,2048]{1,0:T(8,128)(2,1)S(1)}, u32[]{:S(2)}, u32[]{:S(2)}) collective-permute-start(bf16[128,2048]{1,0:T(8,128)(2,1)S(1)} %collective-permute-done.9.refs_1_), channel_id=1, source_target_pairs={{0,4},{1,5},{2,6},{3,7},{4,0},{5,1},{6,2},{7,3},{8,12},{9,13},{10,... | collective-permute-start | bytes 1572872 | tf_op jit(solution)/shard_map/ppermute | solution.py:256
  58.1 0.1 add_convert_fusion.6
  58.2 1.5 %collective-permute-start.14 = (bf16[64,2048]{1,0:T(8,128)(2,1)S(1)}, bf16[64,2048]{1,0:T(8,128)(2,1)S(1)}, u32[]{:S(2)}, u32[]{:S(2)}) collective-permute-start(bf16[64,2048]{1,0:T(8,128)(2,1)S(1)} %get-tuple-element.157), channel_id=1, source_target_pairs={{0,2},{1,3},{2,0},{3,1},{4,6},{5,7},{6,4},{7,5},{8,10},{9,11},{10,... | collective-permute-start | bytes 786440 | tf_op jit(solution)/shard_map/ppermute | solution.py:256
  59.7 0.2 collective-permute-start.16
  60.0 5.7 %shard_map.81 = (bf16[256,2048]{1,0:T(8,128)(2,1)S(1)}, bf16[128,2048]{1,0:T(8,128)(2,1)S(1)}, bf16[64,2048]{1,0:T(8,128)(2,1)S(1)}, bf16[64,2048]{1,0:T(8,128)(2,1)S(1)}, bf16[320,768]{1,0:T(8,128)(2,1)S(1)}) custom-call(f32[16,512]{1,0:T(8,128)S(1)} %shard_map.78.tables, bf16[128,2048]{1,0:T(8,128)(2,1)S(1)} %constant_dynamic-update-slice_fusion.refs_0_, ...), custom_call_target="tpu_custom_call" | custom-call | flops 4362076160 | bytes 13631488 | tf_op jit(solution)/shard_map/pallas_call | solution.py:178
  65.6 0.3 collective-permute-start.18
  66.0 2.7 %shard_map.82 = (bf16[128,2048]{1,0:T(8,128)(2,1)S(1)}, bf16[128,2048]{1,0:T(8,128)(2,1)S(1)}, bf16[160,768]{1,0:T(8,128)(2,1)S(1)}) custom-call(f32[16,512]{1,0:T(8,128)S(1)} %shard_map.78.tables, bf16[128,2048]{1,0:T(8,128)(2,1)S(1)} %collective-permute-done.8.refs_0_, bf16[128,2048]{1,0:T(8,128)(2,1)S(1)} %collective-permute-done.19.refs_1_, ...), custom_call_target="tpu_custom_call" | custom-call | flops 1845493760 | bytes 11534336 | tf_op jit(solution)/shard_map/pallas_call | solution.py:178
  68.7 1.8 %collective-permute-done.13.refs_0_ = bf16[128,2048]{1,0:T(8,128)(2,1)S(1)} collective-permute-done((bf16[128,2048]{1,0:T(8,128)(2,1)S(1)}, bf16[128,2048]{1,0:T(8,128)(2,1)S(1)}, u32[]{:S(2)}, u32[]{:S(2)}) %collective-permute-start.13) | collective-permute-done | bytes 524320 | tf_op jit(solution)/shard_map/ppermute | solution.py:256
  70.5 0.5 collective-permute-start.21
  71.1 1.3 %collective-permute-start.22 = (bf16[64,2048]{1,0:T(8,128)(2,1)S(1)}, bf16[64,2048]{1,0:T(8,128)(2,1)S(1)}, u32[]{:S(2)}, u32[]{:S(2)}) collective-permute-start(bf16[64,2048]{1,0:T(8,128)(2,1)S(1)} %add_convert_fusion.11), channel_id=1, source_target_pairs={{0,2},{1,3},{2,0},{3,1},{4,6},{5,7},{6,4},{7,5},{8,10},{9,11},{10,... | collective-permute-start | bytes 786440 | tf_op jit(solution)/shard_map/ppermute | solution.py:256
  72.6 2.7 %shard_map.83 = (bf16[128,2048]{1,0:T(8,128)(2,1)S(1)}, bf16[128,2048]{1,0:T(8,128)(2,1)S(1)}, bf16[160,768]{1,0:T(8,128)(2,1)S(1)}) custom-call(f32[16,512]{1,0:T(8,128)S(1)} %shard_map.78.tables, bf16[128,2048]{1,0:T(8,128)(2,1)S(1)} %collective-permute-done.13.refs_0_, bf16[128,2048]{1,0:T(8,128)(2,1)S(1)} %collective-permute-done.20.refs_1_, ...), custom_call_target="tpu_custom_call" | custom-call | flops 1845493760 | bytes 11534336 | tf_op jit(solution)/shard_map/pallas_call | solution.py:178
  75.3 4.2 %collective-permute-done.22 = bf16[64,2048]{1,0:T(8,128)(2,1)S(1)} collective-permute-done((bf16[64,2048]{1,0:T(8,128)(2,1)S(1)}, bf16[64,2048]{1,0:T(8,128)(2,1)S(1)}, u32[]{:S(2)}, u32[]{:S(2)}) %collective-permute-start.22) | collective-permute-done | bytes 262176 | tf_op jit(solution)/shard_map/ppermute | solution.py:256
  79.5 0.5 collective-permute-start.28
  80.0 0.1 add_convert_fusion.7
  80.1 2.0 %collective-permute-start.26 = (bf16[64,2048]{1,0:T(8,128)(2,1)S(1)}, bf16[64,2048]{1,0:T(8,128)(2,1)S(1)}, u32[]{:S(2)}, u32[]{:S(2)}) collective-permute-start(bf16[64,2048]{1,0:T(8,128)(2,1)S(1)} %add_convert_fusion.7), channel_id=1, source_target_pairs={{0,8},{1,9},{2,10},{3,11},{4,12},{5,13},{6,14},{7,15},{8,0},{9,1},... | collective-permute-start | bytes 786440 | tf_op jit(solution)/shard_map/ppermute | solution.py:256
  82.1 0.5 collective-permute-start.27
  82.6 0.1 add_convert_fusion.8
  82.7 1.6 %collective-permute-start.24 = (bf16[64,2048]{1,0:T(8,128)(2,1)S(1)}, bf16[64,2048]{1,0:T(8,128)(2,1)S(1)}, u32[]{:S(2)}, u32[]{:S(2)}) collective-permute-start(bf16[64,2048]{1,0:T(8,128)(2,1)S(1)} %get-tuple-element.161), channel_id=1, source_target_pairs={{0,2},{1,3},{2,0},{3,1},{4,6},{5,7},{6,4},{7,5},{8,10},{9,11},{10,... | collective-permute-start | bytes 786440 | tf_op jit(solution)/shard_map/ppermute | solution.py:256
  84.3 0.5 collective-permute-start.25
  84.8 0.1 add_convert_fusion
  84.9 10.4 %collective-permute-done.26.far_high = bf16[64,2048]{1,0:T(8,128)(2,1)S(1)} collective-permute-done((bf16[64,2048]{1,0:T(8,128)(2,1)S(1)}, bf16[64,2048]{1,0:T(8,128)(2,1)S(1)}, u32[]{:S(2)}, u32[]{:S(2)}) %collective-permute-start.26) | collective-permute-done | bytes 262176 | tf_op jit(solution)/shard_map/ppermute | solution.py:256
  95.4 1.1 collective-permute-done.25
  96.5 0.2 add_convert_fusion.4
  96.8 2.0 %collective-permute-start.30 = (bf16[64,2048]{1,0:T(8,128)(2,1)S(1)}, bf16[64,2048]{1,0:T(8,128)(2,1)S(1)}, u32[]{:S(2)}, u32[]{:S(2)}) collective-permute-start(bf16[64,2048]{1,0:T(8,128)(2,1)S(1)} %get-tuple-element.159), channel_id=1, source_target_pairs={{0,8},{1,9},{2,10},{3,11},{4,12},{5,13},{6,14},{7,15},{8,0},{9,1},... | collective-permute-start | bytes 786440 | tf_op jit(solution)/shard_map/ppermute | solution.py:256
  98.8 0.6 collective-permute-start.31
  99.4 1.3 %collective-permute-start.32 = (bf16[64,2048]{1,0:T(8,128)(2,1)S(1)}, bf16[64,2048]{1,0:T(8,128)(2,1)S(1)}, u32[]{:S(2)}, u32[]{:S(2)}) collective-permute-start(bf16[64,2048]{1,0:T(8,128)(2,1)S(1)} %add_convert_fusion.3), channel_id=1, source_target_pairs={{0,2},{1,3},{2,0},{3,1},{4,6},{5,7},{6,4},{7,5},{8,10},{9,11},{10,... | collective-permute-start | bytes 786440 | tf_op jit(solution)/shard_map/ppermute | solution.py:256
  100.8 0.8 collective-permute-start.33
  101.5 3.1 %shard_map.84 = f32[768,768]{1,0:T(8,128)} custom-call(f32[16,512]{1,0:T(8,128)S(1)} %shard_map.78.tables, bf16[320,768]{1,0:T(8,128)(2,1)S(1)} %get-tuple-element.139.refs_0_, bf16[320,768]{1,0:T(8,128)(2,1)S(1)} %get-tuple-element.140.refs_1_, bf16[320,768]{1,0:T(8,128)(2,1)S(1)} %get-tuple-element.141.refs_2_, ...), custom_call_target="tpu_custom_call" | custom-call | flops 1509949440 | bytes 4325376 | tf_op jit(solution)/shard_map/pallas_call | solution.py:209
  104.7 6.0 %collective-permute-done.30 = bf16[64,2048]{1,0:T(8,128)(2,1)S(1)} collective-permute-done((bf16[64,2048]{1,0:T(8,128)(2,1)S(1)}, bf16[64,2048]{1,0:T(8,128)(2,1)S(1)}, u32[]{:S(2)}, u32[]{:S(2)}) %collective-permute-start.30) | collective-permute-done | bytes 262176 | tf_op jit(solution)/shard_map/ppermute | solution.py:256
  110.7 1.2 collective-permute-done.33
  111.9 0.1 add_convert_fusion.2
  112.0 1.3 %collective-permute-start.34 = (bf16[128,2048]{1,0:T(8,128)(2,1)S(1)}, bf16[128,2048]{1,0:T(8,128)(2,1)S(1)}, u32[]{:S(2)}, u32[]{:S(2)}) collective-permute-start(bf16[128,2048]{1,0:T(8,128)(2,1)S(1)} %add_convert_fusion), channel_id=1, source_target_pairs={{0,2},{1,3},{2,0},{3,1},{4,6},{5,7},{6,4},{7,5},{8,10},{9,11},{10,... | collective-permute-start | bytes 1572872 | tf_op jit(solution)/shard_map/ppermute | solution.py:256
  113.3 0.1 add_convert_fusion.1
  113.5 1.7 %collective-permute-start.35 = (bf16[64,2048]{1,0:T(8,128)(2,1)S(1)}, bf16[64,2048]{1,0:T(8,128)(2,1)S(1)}, u32[]{:S(2)}, u32[]{:S(2)}) collective-permute-start(bf16[64,2048]{1,0:T(8,128)(2,1)S(1)} %add_convert_fusion.1), channel_id=1, source_target_pairs={{0,4},{1,5},{2,6},{3,7},{4,0},{5,1},{6,2},{7,3},{8,12},{9,13},{10,... | collective-permute-start | bytes 786440 | tf_op jit(solution)/shard_map/ppermute | solution.py:256
  115.2 1.0 collective-permute-start.36
  116.2 8.4 %collective-permute-done.35.near_high = bf16[64,2048]{1,0:T(8,128)(2,1)S(1)} collective-permute-done((bf16[64,2048]{1,0:T(8,128)(2,1)S(1)}, bf16[64,2048]{1,0:T(8,128)(2,1)S(1)}, u32[]{:S(2)}, u32[]{:S(2)}) %collective-permute-start.35) | collective-permute-done | bytes 262176 | tf_op jit(solution)/shard_map/ppermute | solution.py:256
  124.6 2.4 %collective-permute-done.36.far_low = bf16[64,2048]{1,0:T(8,128)(2,1)S(1)} collective-permute-done((bf16[64,2048]{1,0:T(8,128)(2,1)S(1)}, bf16[64,2048]{1,0:T(8,128)(2,1)S(1)}, u32[]{:S(2)}, u32[]{:S(2)}) %collective-permute-start.36) | collective-permute-done | bytes 262176 | tf_op jit(solution)/shard_map/ppermute | solution.py:256
  127.0 1.1 shard_map.85
  (57 shorter events, 0.5 us)
Async XLA Ops:
  0.6 24.1 %collective-permute-start = (bf16[128,2048]{1,0:T(8,128)(2,1)}, bf16[128,2048]{1,0:T(8,128)(2,1)S(1)}, u32[]{:S(2)}, u32[]{:S(2)}) collective-permute-start(bf16[128,2048]{1,0:T(8,128)(2,1)} %refs_0_.1), channel_id=1, source_target_pairs={{0,4},{1,5},{2,6},{3,7},{4,0},{5,1},{6,2},{7,3},{8,12},{9,13},{10,... | collective-permute-start | bytes 1572872 | tf_op jit(solution)/shard_map/ppermute | solution.py:256
  3.7 21.0 %collective-permute-start.2 = (bf16[128,2048]{1,0:T(8,128)(2,1)}, bf16[128,2048]{1,0:T(8,128)(2,1)S(1)}, u32[]{:S(2)}, u32[]{:S(2)}) collective-permute-start(bf16[128,2048]{1,0:T(8,128)(2,1)} %refs_0_.1), channel_id=1, source_target_pairs={{0,2},{1,3},{2,0},{3,1},{4,6},{5,7},{6,4},{7,5},{8,10},{9,11},{10,... | collective-permute-start | bytes 1572872 | tf_op jit(solution)/shard_map/ppermute | solution.py:256
  5.2 19.5 %collective-permute-start.3 = (bf16[128,2048]{1,0:T(8,128)(2,1)}, bf16[128,2048]{1,0:T(8,128)(2,1)S(1)}, u32[]{:S(2)}, u32[]{:S(2)}) collective-permute-start(bf16[128,2048]{1,0:T(8,128)(2,1)} %refs_0_.1), channel_id=1, source_target_pairs={{0,1},{1,0},{2,3},{3,2},{4,5},{5,4},{6,7},{7,6},{8,9},{9,8},{10,11... | collective-permute-start | bytes 1572872 | tf_op jit(solution)/shard_map/ppermute | solution.py:256
  5.2 1.1 copy-start.6
  6.3 0.7 copy-start.8
  7.0 0.7 copy-start.9
  7.8 16.9 %collective-permute-start.1 = (bf16[64,2048]{1,0:T(8,128)(2,1)S(1)}, bf16[64,2048]{1,0:T(8,128)(2,1)S(1)}, u32[]{:S(2)}, u32[]{:S(2)}) collective-permute-start(bf16[64,2048]{1,0:T(8,128)(2,1)S(1)} %get-tuple-element.79), channel_id=1, source_target_pairs={{0,8},{1,9},{2,10},{3,11},{4,12},{5,13},{6,14},{7,15},{8,0},{9,1},... | collective-permute-start | bytes 786440 | tf_op jit(solution)/shard_map/ppermute | solution.py:256
  24.7 0.7 copy-start.10
  25.4 2.7 %collective-permute-start.7 = (bf16[128,2048]{1,0:T(8,128)(2,1)S(1)}, bf16[128,2048]{1,0:T(8,128)(2,1)S(1)}, u32[]{:S(2)}, u32[]{:S(2)}) collective-permute-start(bf16[128,2048]{1,0:T(8,128)(2,1)S(1)} %collective-permute-done.2.refs_1_), channel_id=1, source_target_pairs={{0,1},{1,0},{2,3},{3,2},{4,5},{5,4},{6,7},{7,6},{8,9},{9,8},{10,11... | collective-permute-start | bytes 1572872 | tf_op jit(solution)/shard_map/ppermute | solution.py:256
  25.4 15.9 %collective-permute-start.5 = (bf16[128,2048]{1,0:T(8,128)(2,1)S(1)}, bf16[128,2048]{1,0:T(8,128)(2,1)S(1)}, u32[]{:S(2)}, u32[]{:S(2)}) collective-permute-start(bf16[128,2048]{1,0:T(8,128)(2,1)S(1)} %collective-permute-done.refs_0_), channel_id=1, source_target_pairs={{0,2},{1,3},{2,0},{3,1},{4,6},{5,7},{6,4},{7,5},{8,10},{9,11},{10,... | collective-permute-start | bytes 1572872 | tf_op jit(solution)/shard_map/ppermute | solution.py:256
  25.9 15.4 %collective-permute-start.6 = (bf16[128,2048]{1,0:T(8,128)(2,1)S(1)}, bf16[128,2048]{1,0:T(8,128)(2,1)S(1)}, u32[]{:S(2)}, u32[]{:S(2)}) collective-permute-start(bf16[128,2048]{1,0:T(8,128)(2,1)S(1)} %collective-permute-done.refs_0_), channel_id=1, source_target_pairs={{0,1},{1,0},{2,3},{3,2},{4,5},{5,4},{6,7},{7,6},{8,9},{9,8},{10,11... | collective-permute-start | bytes 1572872 | tf_op jit(solution)/shard_map/ppermute | solution.py:256
  26.3 15.1 %collective-permute-start.4 = (bf16[64,2048]{1,0:T(8,128)(2,1)S(1)}, bf16[64,2048]{1,0:T(8,128)(2,1)S(1)}, u32[]{:S(2)}, u32[]{:S(2)}) collective-permute-start(bf16[64,2048]{1,0:T(8,128)(2,1)S(1)} %get-tuple-element.83), channel_id=1, source_target_pairs={{0,8},{1,9},{2,10},{3,11},{4,12},{5,13},{6,14},{7,15},{8,0},{9,1},... | collective-permute-start | bytes 786440 | tf_op jit(solution)/shard_map/ppermute | solution.py:256
  28.2 1.9 %copy-start = (bf16[1,2048,768]{2,1,0:T(8,128)(2,1)S(1)}, bf16[1,2048,768]{2,1,0:T(8,128)(2,1)}, u32[]{:S(2)}) copy-start(bf16[1,2048,768]{2,1,0:T(8,128)(2,1)} %param.9) | copy-start | bytes 9437188
  30.0 1.9 %copy-start.2 = (bf16[1,2048,768]{2,1,0:T(8,128)(2,1)S(1)}, bf16[1,2048,768]{2,1,0:T(8,128)(2,1)}, u32[]{:S(2)}) copy-start(bf16[1,2048,768]{2,1,0:T(8,128)(2,1)} %param.10) | copy-start | bytes 9437188
  31.9 1.9 %copy-start.4 = (bf16[1,768,2048]{2,1,0:T(8,128)(2,1)S(1)}, bf16[1,768,2048]{2,1,0:T(8,128)(2,1)}, u32[]{:S(2)}) copy-start(bf16[1,768,2048]{2,1,0:T(8,128)(2,1)} %param.11) | copy-start | bytes 9437188
  33.8 1.0 copy-start.7
  34.9 6.5 %copy-start.11 = (bf16[64,2048]{1,0:T(8,128)(2,1)S(1)}, bf16[64,2048]{1,0:T(8,128)(2,1)}, u32[]{:S(2)}) copy-start(bf16[64,2048]{1,0:T(8,128)(2,1)} %copy-done.10) | copy-start | bytes 786436
  34.9 8.4 %copy-start.1 = (bf16[1,2048,768]{2,1,0:T(8,128)(2,1)S(1)}, bf16[1,2048,768]{2,1,0:T(8,128)(2,1)}, u32[]{:S(2)}) copy-start(bf16[1,2048,768]{2,1,0:T(8,128)(2,1)} %param.9) | copy-start | bytes 9437188
  34.9 8.4 %copy-start.3 = (bf16[1,2048,768]{2,1,0:T(8,128)(2,1)S(1)}, bf16[1,2048,768]{2,1,0:T(8,128)(2,1)}, u32[]{:S(2)}) copy-start(bf16[1,2048,768]{2,1,0:T(8,128)(2,1)} %param.10) | copy-start | bytes 9437188
  34.9 8.4 %copy-start.5 = (bf16[1,768,2048]{2,1,0:T(8,128)(2,1)S(1)}, bf16[1,768,2048]{2,1,0:T(8,128)(2,1)}, u32[]{:S(2)}) copy-start(bf16[1,768,2048]{2,1,0:T(8,128)(2,1)} %param.11) | copy-start | bytes 9437188
  41.3 1.9 %collective-permute-start.11 = (bf16[128,2048]{1,0:T(8,128)(2,1)S(1)}, bf16[128,2048]{1,0:T(8,128)(2,1)S(1)}, u32[]{:S(2)}, u32[]{:S(2)}) collective-permute-start(bf16[128,2048]{1,0:T(8,128)(2,1)S(1)} %collective-permute-done.5.refs_1_), channel_id=1, source_target_pairs={{0,1},{1,0},{2,3},{3,2},{4,5},{5,4},{6,7},{7,6},{8,9},{9,8},{10,11... | collective-permute-start | bytes 1572872 | tf_op jit(solution)/shard_map/ppermute | solution.py:256
  41.4 14.4 %collective-permute-start.8 = (bf16[128,2048]{1,0:T(8,128)(2,1)S(1)}, bf16[128,2048]{1,0:T(8,128)(2,1)S(1)}, u32[]{:S(2)}, u32[]{:S(2)}) collective-permute-start(bf16[128,2048]{1,0:T(8,128)(2,1)S(1)} %constant_dynamic-update-slice_fusion.refs_0_), channel_id=1, source_target_pairs={{0,4},{1,5},{2,6},{3,7},{4,0},{5,1},{6,2},{7,3},{8,12},{9,13},{10,... | collective-permute-start | bytes 1572872 | tf_op jit(solution)/shard_map/ppermute | solution.py:256
  42.1 14.0 %collective-permute-start.9 = (bf16[128,2048]{1,0:T(8,128)(2,1)S(1)}, bf16[128,2048]{1,0:T(8,128)(2,1)S(1)}, u32[]{:S(2)}, u32[]{:S(2)}) collective-permute-start(bf16[128,2048]{1,0:T(8,128)(2,1)S(1)} %constant_dynamic-update-slice_fusion.refs_0_), channel_id=1, source_target_pairs={{0,2},{1,3},{2,0},{3,1},{4,6},{5,7},{6,4},{7,5},{8,10},{9,11},{10,... | collective-permute-start | bytes 1572872 | tf_op jit(solution)/shard_map/ppermute | solution.py:256
  43.2 12.9 %collective-permute-start.10 = (bf16[128,2048]{1,0:T(8,128)(2,1)S(1)}, bf16[128,2048]{1,0:T(8,128)(2,1)S(1)}, u32[]{:S(2)}, u32[]{:S(2)}) collective-permute-start(bf16[128,2048]{1,0:T(8,128)(2,1)S(1)} %constant_dynamic-update-slice_fusion.refs_0_), channel_id=1, source_target_pairs={{0,1},{1,0},{2,3},{3,2},{4,5},{5,4},{6,7},{7,6},{8,9},{9,8},{10,11... | collective-permute-start | bytes 1572872 | tf_op jit(solution)/shard_map/ppermute | solution.py:256
  48.7 7.4 %collective-permute-start.12 = (bf16[128,2048]{1,0:T(8,128)(2,1)S(1)}, bf16[128,2048]{1,0:T(8,128)(2,1)S(1)}, u32[]{:S(2)}, u32[]{:S(2)}) collective-permute-start(bf16[128,2048]{1,0:T(8,128)(2,1)S(1)} %get-tuple-element.98), channel_id=1, source_target_pairs={{0,1},{1,0},{2,3},{3,2},{4,5},{5,4},{6,7},{7,6},{8,9},{9,8},{10,11... | collective-permute-start | bytes 1572872 | tf_op jit(solution)/shard_map/ppermute | solution.py:256
  56.1 3.6 %collective-permute-start.17 = (bf16[128,2048]{1,0:T(8,128)(2,1)S(1)}, bf16[128,2048]{1,0:T(8,128)(2,1)S(1)}, u32[]{:S(2)}, u32[]{:S(2)}) collective-permute-start(bf16[128,2048]{1,0:T(8,128)(2,1)S(1)} %collective-permute-done.9.refs_1_), channel_id=1, source_target_pairs={{0,1},{1,0},{2,3},{3,2},{4,5},{5,4},{6,7},{7,6},{8,9},{9,8},{10,11... | collective-permute-start | bytes 1572872 | tf_op jit(solution)/shard_map/ppermute | solution.py:256
  56.1 12.6 %collective-permute-start.15 = (bf16[256,2048]{1,0:T(8,128)(2,1)S(1)}, bf16[256,2048]{1,0:T(8,128)(2,1)S(1)}, u32[]{:S(2)}, u32[]{:S(2)}) collective-permute-start(bf16[256,2048]{1,0:T(8,128)(2,1)S(1)} %get-tuple-element.102), channel_id=1, source_target_pairs={{0,1},{1,0},{2,3},{3,2},{4,5},{5,4},{6,7},{7,6},{8,9},{9,8},{10,11... | collective-permute-start | bytes 3145736 | tf_op jit(solution)/shard_map/ppermute | solution.py:256
  56.6 13.9 %collective-permute-start.13 = (bf16[128,2048]{1,0:T(8,128)(2,1)S(1)}, bf16[128,2048]{1,0:T(8,128)(2,1)S(1)}, u32[]{:S(2)}, u32[]{:S(2)}) collective-permute-start(bf16[128,2048]{1,0:T(8,128)(2,1)S(1)} %collective-permute-done.9.refs_1_), channel_id=1, source_target_pairs={{0,4},{1,5},{2,6},{3,7},{4,0},{5,1},{6,2},{7,3},{8,12},{9,13},{10,... | collective-permute-start | bytes 1572872 | tf_op jit(solution)/shard_map/ppermute | solution.py:256
  58.1 7.6 %collective-permute-start.19 = (bf16[128,2048]{1,0:T(8,128)(2,1)S(1)}, bf16[128,2048]{1,0:T(8,128)(2,1)S(1)}, u32[]{:S(2)}, u32[]{:S(2)}) collective-permute-start(bf16[128,2048]{1,0:T(8,128)(2,1)S(1)} %collective-permute-done.8.refs_0_), channel_id=1, source_target_pairs={{0,1},{1,0},{2,3},{3,2},{4,5},{5,4},{6,7},{7,6},{8,9},{9,8},{10,11... | collective-permute-start | bytes 1572872 | tf_op jit(solution)/shard_map/ppermute | solution.py:256
  58.2 10.5 %collective-permute-start.14 = (bf16[64,2048]{1,0:T(8,128)(2,1)S(1)}, bf16[64,2048]{1,0:T(8,128)(2,1)S(1)}, u32[]{:S(2)}, u32[]{:S(2)}) collective-permute-start(bf16[64,2048]{1,0:T(8,128)(2,1)S(1)} %get-tuple-element.157), channel_id=1, source_target_pairs={{0,2},{1,3},{2,0},{3,1},{4,6},{5,7},{6,4},{7,5},{8,10},{9,11},{10,... | collective-permute-start | bytes 786440 | tf_op jit(solution)/shard_map/ppermute | solution.py:256
  59.7 10.8 %collective-permute-start.16 = (bf16[128,2048]{1,0:T(8,128)(2,1)S(1)}, bf16[128,2048]{1,0:T(8,128)(2,1)S(1)}, u32[]{:S(2)}, u32[]{:S(2)}) collective-permute-start(bf16[128,2048]{1,0:T(8,128)(2,1)S(1)} %get-tuple-element.103), channel_id=1, source_target_pairs={{0,1},{1,0},{2,3},{3,2},{4,5},{5,4},{6,7},{7,6},{8,9},{9,8},{10,11... | collective-permute-start | bytes 1572872 | tf_op jit(solution)/shard_map/ppermute | solution.py:256
  65.6 4.9 %collective-permute-start.18 = (bf16[64,2048]{1,0:T(8,128)(2,1)S(1)}, bf16[64,2048]{1,0:T(8,128)(2,1)S(1)}, u32[]{:S(2)}, u32[]{:S(2)}) collective-permute-start(bf16[64,2048]{1,0:T(8,128)(2,1)S(1)} %get-tuple-element.105), channel_id=1, source_target_pairs={{0,1},{1,0},{2,3},{3,2},{4,5},{5,4},{6,7},{7,6},{8,9},{9,8},{10,11... | collective-permute-start | bytes 786440 | tf_op jit(solution)/shard_map/ppermute | solution.py:256
  70.5 2.0 %collective-permute-start.20 = (bf16[128,2048]{1,0:T(8,128)(2,1)S(1)}, bf16[128,2048]{1,0:T(8,128)(2,1)S(1)}, u32[]{:S(2)}, u32[]{:S(2)}) collective-permute-start(bf16[128,2048]{1,0:T(8,128)(2,1)S(1)} %collective-permute-done.13.refs_0_), channel_id=1, source_target_pairs={{0,1},{1,0},{2,3},{3,2},{4,5},{5,4},{6,7},{7,6},{8,9},{9,8},{10,11... | collective-permute-start | bytes 1572872 | tf_op jit(solution)/shard_map/ppermute | solution.py:256
  70.5 8.9 %collective-permute-start.21 = (bf16[128,2048]{1,0:T(8,128)(2,1)S(1)}, bf16[128,2048]{1,0:T(8,128)(2,1)S(1)}, u32[]{:S(2)}, u32[]{:S(2)}) collective-permute-start(bf16[128,2048]{1,0:T(8,128)(2,1)S(1)} %get-tuple-element.119), channel_id=1, source_target_pairs={{0,1},{1,0},{2,3},{3,2},{4,5},{5,4},{6,7},{7,6},{8,9},{9,8},{10,11... | collective-permute-start | bytes 1572872 | tf_op jit(solution)/shard_map/ppermute | solution.py:256
  71.1 8.3 %collective-permute-start.22 = (bf16[64,2048]{1,0:T(8,128)(2,1)S(1)}, bf16[64,2048]{1,0:T(8,128)(2,1)S(1)}, u32[]{:S(2)}, u32[]{:S(2)}) collective-permute-start(bf16[64,2048]{1,0:T(8,128)(2,1)S(1)} %add_convert_fusion.11), channel_id=1, source_target_pairs={{0,2},{1,3},{2,0},{3,1},{4,6},{5,7},{6,4},{7,5},{8,10},{9,11},{10,... | collective-permute-start | bytes 786440 | tf_op jit(solution)/shard_map/ppermute | solution.py:256
  79.5 3.1 %collective-permute-start.23 = (bf16[128,2048]{1,0:T(8,128)(2,1)S(1)}, bf16[128,2048]{1,0:T(8,128)(2,1)S(1)}, u32[]{:S(2)}, u32[]{:S(2)}) collective-permute-start(bf16[128,2048]{1,0:T(8,128)(2,1)S(1)} %get-tuple-element.125), channel_id=1, source_target_pairs={{0,1},{1,0},{2,3},{3,2},{4,5},{5,4},{6,7},{7,6},{8,9},{9,8},{10,11... | collective-permute-start | bytes 1572872 | tf_op jit(solution)/shard_map/ppermute | solution.py:256
  79.5 4.8 %collective-permute-start.28 = (bf16[64,2048]{1,0:T(8,128)(2,1)S(1)}, bf16[64,2048]{1,0:T(8,128)(2,1)S(1)}, u32[]{:S(2)}, u32[]{:S(2)}) collective-permute-start(bf16[64,2048]{1,0:T(8,128)(2,1)S(1)} %get-tuple-element.131), channel_id=1, source_target_pairs={{0,1},{1,0},{2,3},{3,2},{4,5},{5,4},{6,7},{7,6},{8,9},{9,8},{10,11... | collective-permute-start | bytes 786440 | tf_op jit(solution)/shard_map/ppermute | solution.py:256
  80.0 5.0 %collective-permute-start.29 = (bf16[128,2048]{1,0:T(8,128)(2,1)S(1)}, bf16[128,2048]{1,0:T(8,128)(2,1)S(1)}, u32[]{:S(2)}, u32[]{:S(2)}) collective-permute-start(bf16[128,2048]{1,0:T(8,128)(2,1)S(1)} %get-tuple-element.132), channel_id=1, source_target_pairs={{0,1},{1,0},{2,3},{3,2},{4,5},{5,4},{6,7},{7,6},{8,9},{9,8},{10,11... | collective-permute-start | bytes 1572872 | tf_op jit(solution)/shard_map/ppermute | solution.py:256
  80.1 15.3 %collective-permute-start.26 = (bf16[64,2048]{1,0:T(8,128)(2,1)S(1)}, bf16[64,2048]{1,0:T(8,128)(2,1)S(1)}, u32[]{:S(2)}, u32[]{:S(2)}) collective-permute-start(bf16[64,2048]{1,0:T(8,128)(2,1)S(1)} %add_convert_fusion.7), channel_id=1, source_target_pairs={{0,8},{1,9},{2,10},{3,11},{4,12},{5,13},{6,14},{7,15},{8,0},{9,1},... | collective-permute-start | bytes 786440 | tf_op jit(solution)/shard_map/ppermute | solution.py:256
  82.1 13.3 %collective-permute-start.27 = (bf16[64,2048]{1,0:T(8,128)(2,1)S(1)}, bf16[64,2048]{1,0:T(8,128)(2,1)S(1)}, u32[]{:S(2)}, u32[]{:S(2)}) collective-permute-start(bf16[64,2048]{1,0:T(8,128)(2,1)S(1)} %add_convert_fusion.10), channel_id=1, source_target_pairs={{0,4},{1,5},{2,6},{3,7},{4,0},{5,1},{6,2},{7,3},{8,12},{9,13},{10,... | collective-permute-start | bytes 786440 | tf_op jit(solution)/shard_map/ppermute | solution.py:256
  82.7 12.7 %collective-permute-start.24 = (bf16[64,2048]{1,0:T(8,128)(2,1)S(1)}, bf16[64,2048]{1,0:T(8,128)(2,1)S(1)}, u32[]{:S(2)}, u32[]{:S(2)}) collective-permute-start(bf16[64,2048]{1,0:T(8,128)(2,1)S(1)} %get-tuple-element.161), channel_id=1, source_target_pairs={{0,2},{1,3},{2,0},{3,1},{4,6},{5,7},{6,4},{7,5},{8,10},{9,11},{10,... | collective-permute-start | bytes 786440 | tf_op jit(solution)/shard_map/ppermute | solution.py:256
  84.3 12.3 %collective-permute-start.25 = (bf16[64,2048]{1,0:T(8,128)(2,1)S(1)}, bf16[64,2048]{1,0:T(8,128)(2,1)S(1)}, u32[]{:S(2)}, u32[]{:S(2)}) collective-permute-start(bf16[64,2048]{1,0:T(8,128)(2,1)S(1)} %get-tuple-element.160), channel_id=1, source_target_pairs={{0,2},{1,3},{2,0},{3,1},{4,6},{5,7},{6,4},{7,5},{8,10},{9,11},{10,... | collective-permute-start | bytes 786440 | tf_op jit(solution)/shard_map/ppermute | solution.py:256
  96.8 13.9 %collective-permute-start.30 = (bf16[64,2048]{1,0:T(8,128)(2,1)S(1)}, bf16[64,2048]{1,0:T(8,128)(2,1)S(1)}, u32[]{:S(2)}, u32[]{:S(2)}) collective-permute-start(bf16[64,2048]{1,0:T(8,128)(2,1)S(1)} %get-tuple-element.159), channel_id=1, source_target_pairs={{0,8},{1,9},{2,10},{3,11},{4,12},{5,13},{6,14},{7,15},{8,0},{9,1},... | collective-permute-start | bytes 786440 | tf_op jit(solution)/shard_map/ppermute | solution.py:256
  98.8 11.9 %collective-permute-start.31 = (bf16[64,2048]{1,0:T(8,128)(2,1)S(1)}, bf16[64,2048]{1,0:T(8,128)(2,1)S(1)}, u32[]{:S(2)}, u32[]{:S(2)}) collective-permute-start(bf16[64,2048]{1,0:T(8,128)(2,1)S(1)} %get-tuple-element.158), channel_id=1, source_target_pairs={{0,4},{1,5},{2,6},{3,7},{4,0},{5,1},{6,2},{7,3},{8,12},{9,13},{10,... | collective-permute-start | bytes 786440 | tf_op jit(solution)/shard_map/ppermute | solution.py:256
  99.4 11.2 %collective-permute-start.32 = (bf16[64,2048]{1,0:T(8,128)(2,1)S(1)}, bf16[64,2048]{1,0:T(8,128)(2,1)S(1)}, u32[]{:S(2)}, u32[]{:S(2)}) collective-permute-start(bf16[64,2048]{1,0:T(8,128)(2,1)S(1)} %add_convert_fusion.3), channel_id=1, source_target_pairs={{0,2},{1,3},{2,0},{3,1},{4,6},{5,7},{6,4},{7,5},{8,10},{9,11},{10,... | collective-permute-start | bytes 786440 | tf_op jit(solution)/shard_map/ppermute | solution.py:256
  100.8 11.1 %collective-permute-start.33 = (bf16[64,2048]{1,0:T(8,128)(2,1)S(1)}, bf16[64,2048]{1,0:T(8,128)(2,1)S(1)}, u32[]{:S(2)}, u32[]{:S(2)}) collective-permute-start(bf16[64,2048]{1,0:T(8,128)(2,1)S(1)} %get-tuple-element.137), channel_id=1, source_target_pairs={{0,2},{1,3},{2,0},{3,1},{4,6},{5,7},{6,4},{7,5},{8,10},{9,11},{10,... | collective-permute-start | bytes 786440 | tf_op jit(solution)/shard_map/ppermute | solution.py:256
  112.0 15.0 %collective-permute-start.34 = (bf16[128,2048]{1,0:T(8,128)(2,1)S(1)}, bf16[128,2048]{1,0:T(8,128)(2,1)S(1)}, u32[]{:S(2)}, u32[]{:S(2)}) collective-permute-start(bf16[128,2048]{1,0:T(8,128)(2,1)S(1)} %add_convert_fusion), channel_id=1, source_target_pairs={{0,2},{1,3},{2,0},{3,1},{4,6},{5,7},{6,4},{7,5},{8,10},{9,11},{10,... | collective-permute-start | bytes 1572872 | tf_op jit(solution)/shard_map/ppermute | solution.py:256
  113.5 11.1 %collective-permute-start.35 = (bf16[64,2048]{1,0:T(8,128)(2,1)S(1)}, bf16[64,2048]{1,0:T(8,128)(2,1)S(1)}, u32[]{:S(2)}, u32[]{:S(2)}) collective-permute-start(bf16[64,2048]{1,0:T(8,128)(2,1)S(1)} %add_convert_fusion.1), channel_id=1, source_target_pairs={{0,4},{1,5},{2,6},{3,7},{4,0},{5,1},{6,2},{7,3},{8,12},{9,13},{10,... | collective-permute-start | bytes 786440 | tf_op jit(solution)/shard_map/ppermute | solution.py:256
  115.2 11.8 %collective-permute-start.36 = (bf16[64,2048]{1,0:T(8,128)(2,1)S(1)}, bf16[64,2048]{1,0:T(8,128)(2,1)S(1)}, u32[]{:S(2)}, u32[]{:S(2)}) collective-permute-start(bf16[64,2048]{1,0:T(8,128)(2,1)S(1)} %add_convert_fusion.2), channel_id=1, source_target_pairs={{0,8},{1,9},{2,10},{3,11},{4,12},{5,13},{6,14},{7,15},{8,0},{9,1},... | collective-permute-start | bytes 786440 | tf_op jit(solution)/shard_map/ppermute | solution.py:256

commit v21 on v20

--- a/solution.py
+++ b/solution.py
@@ -220,23 +220,26 @@
     )(tables, *acts)
 
 
-def mix_kernel(keep, got, side, near_low, near_high, far_low, far_high, mixed):
+def mix_kernel(
+    keep, got, side_low, side_high, near_low, near_high, far_low, far_high, mixed
+):
     most, tok = near_low.shape[0], mixed.shape[0]
-    for start, stop, near, far in (
-        (0, most, near_low, far_low),
-        (most, tok, near_high, far_high),
+    for start, stop, *parts in (
+        (0, most, side_low, near_low, far_low),
+        (most, tok, side_high, near_high, far_high),
     ):
         total = keep[start:stop, :].astype(jnp.float32) + got[start:stop, :].astype(jnp.float32)
-        total = total + side[start:stop, :].astype(jnp.float32) + near[...].astype(jnp.float32)
-        mixed[start:stop, :] = (total + far[...].astype(jnp.float32)).astype(mixed.dtype)
+        for part in parts:
+            total = total + part[...].astype(jnp.float32)
+        mixed[start:stop, :] = total.astype(mixed.dtype)
 
 
 def mix_pass(*parts):
-    side = parts[2]
+    tok = 2 * parts[2].shape[0]
     vmem = pl.BlockSpec(memory_space=pltpu.VMEM)
     return pl.pallas_call(
         mix_kernel,
-        out_shape=jax.ShapeDtypeStruct(side.shape, side.dtype),
+        out_shape=jax.ShapeDtypeStruct((tok, parts[2].shape[1]), parts[2].dtype),
         in_specs=[vmem] * len(parts),
         out_specs=vmem,
         compiler_params=pltpu.CompilerParams(vmem_limit_bytes=12 * 1024 * 1024),
@@ -277,23 +280,16 @@
 
     mine, a0_low, a0_high = prepare_pass(routes, probs, tokens, size)
     a0 = tokens
-    a1, low, b0, c0, weight, a0_high = together(
-        pair(a0),
-        far(a0_low),
-        column(a0),
-        sibling(a0),
-        lax.all_to_all(mine, "expert", split_axis=0, concat_axis=0, tiled=True),
-        a0_high,
-    )
-    tables = ranks_pass(capacity, spots, weight)
+    a1, low, b0, c0, a0_high, mine = together(
+        pair(a0), far(a0_low), column(a0), sibling(a0), a0_high, mine
+    )
+    weight = lax.all_to_all(mine, "expert", split_axis=0, concat_axis=0, tiled=True)
     high = far(a0_high)
     b1 = column(a1)
     d0 = sibling(b0)
     c1 = sibling(a1)
-    keep0, give0, act0 = expert(0, a0, b0, c0, d0)
-    high, b1, c1, keep0, give0, act0, tables = together(
-        high, b1, c1, keep0, give0, act0, tables
-    )
+    high, b1, c1, d0, weight = together(high, b1, c1, d0, weight)
+    tables = ranks_pass(capacity, spots, weight)
     a2 = jnp.concatenate([low, high], axis=0)
     a3 = pair(a2)
     b2 = column(a2)
@@ -301,8 +297,8 @@
     c2 = sibling(a2)
     keep1, give1, give1_side, act1 = expert(1, a1, b1, c1, d1, pieces=(tok, tok))
     got1_side = sibling(give1_side)
-    a3, b2, c2, keep1, give1, act1, got1_side = together(
-        a3, b2, c2, keep1, give1, act1, got1_side
+    a3, b2, c2, keep1, give1, act1, got1_side, tables = together(
+        a3, b2, c2, keep1, give1, act1, got1_side, tables
     )
     b3 = pair(b2)
     came1_low = column(summed(keep1[tok : tok + half], got1_side[:half]))
@@ -314,10 +310,9 @@
     )
     got2_high = sibling(give2_high)
     keep3, give3, act3 = expert(3, a3, c3, picked=(0, 2))
-    got0 = sibling(give0)
-    b3, came1_low, got0, got1, got2_high, keep2, give2, give2_low, act2, keep3, give3, act3 = (
+    b3, came1_low, got1, got2_high, keep2, give2, give2_low, act2, keep3, give3, act3 = (
         together(
-            b3, came1_low, got0, got1, got2_high, keep2, give2, give2_low, act2, keep3, give3, act3
+            b3, came1_low, got1, got2_high, keep2, give2, give2_low, act2, keep3, give3, act3
         )
     )
     d3 = sibling(b3)
@@ -335,26 +330,30 @@
     came3_low = column(summed(keep3_side[:half], got3_side[:half]))
     came3_high = column(summed(keep3_side[half:], got3_side[half:]))
     near1_low = pair(near1)
-    side0 = summed(keep0[tok:], got0[tok:])
+    keep0, give0, act0 = expert(0, a0, b0, c0, d0)
     side1 = summed(keep1[tok + half :], got1_side[half:])
-    came3_low, came3_high, far2_high, near1_low, side0, side1, got2_low, got3 = together(
-        came3_low, came3_high, far2_high, near1_low, side0, side1, got2_low, got3
-    )
+    came3_low, came3_high, far2_high, near1_low, side1, got2_low, got3, keep0, give0, act0 = (
+        together(
+            came3_low, came3_high, far2_high, near1_low, side1, got2_low, got3, keep0, give0, act0
+        )
+    )
+    got0 = sibling(give0)
     far3_high = far(summed(keep3[half:], got3[half:], came3_high))
     pair3_low = pair(summed(keep3[:half], got3[:half], came3_low))
     side_low = column(summed(keep2[tok : tok + half], got2_low))
     came1_high = column(side1)
     gram = gram_pass(tables, act0, act1, act2, act3, act4)
-    far3_high, pair3_low, side_low, came1_high, side0, gram = together(
-        far3_high, pair3_low, side_low, came1_high, side0, gram
+    far3_high, pair3_low, side_low, came1_high, got0, gram = together(
+        far3_high, pair3_low, side_low, came1_high, got0, gram
     )
     far2_low = summed(keep2[:half], got2[:half], pair3_low, side_low)
-    far2_low, far3_high, came1_high, side0 = together(far2_low, far3_high, came1_high, side0)
+    far2_low, far3_high, came1_high, got0 = together(far2_low, far3_high, came1_high, got0)
     far2_low = far(far2_low)
     near1_high = pair(summed(keep1[half:tok], got1[half:], came1_high, far3_high))
-    last0 = column(side0)
+    last0_low = column(summed(keep0[tok : tok + half], got0[tok : tok + half]))
+    last0_high = column(summed(keep0[tok + half :], got0[tok + half :]))
     mixed = mix_pass(
-        keep0, got0, last0, near1_low, near1_high, far2_low, far2_high
+        keep0, got0, last0_low, last0_high, near1_low, near1_high, far2_low, far2_high
     )
 
     return gram[None], mixed

time: 129 us -> 134 us (1.039)
  waiting for transfers between devices: 43.5 us -> 49.2 us
    ppermute x37 -> x38, waiting for transfers between devices: 43.5 us -> 49.2 us  [swapped(): return lax.ppermute(array, 'expert', [(i, i ^ bit) for i in range(size)])]
    unnamed x25 -> x19, local copies, waits for them, and re-layouts: 9.86 us -> 8.81 us
    ppermute x37 -> x38, starting transfers between devices: 31.2 us -> 31 us  [swapped(): return lax.ppermute(array, 'expert', [(i, i ^ bit) for i in range(size)])]
  transfers between devices with their start and end apart: 37 -> 38, of which waited for: 11 -> 14; matrix products, arithmetic and copies ran while one was open for 1% -> 2% of each run, Pallas kernels for 20% -> 20%
where the time goes in v21:
time: 134 us
  waiting for transfers between devices  49.2 us (37%)
  starting transfers between devices  31 us (23%)
  Pallas kernels  28.3 us (21%)
  blocking collectives  13 us (10%)
  local copies, waits for them, and re-layouts  9.87 us (7%)
    ppermute x38, waiting for transfers between devices, swapped(): return lax.ppermute(array, 'expert', [(i, i ^ bit) for i in range(size)])  49.2 us
    ppermute x38, starting transfers between devices, swapped(): return lax.ppermute(array, 'expert', [(i, i ^ bit) for i in range(size)])  31 us
    pallas_call x5, Pallas kernels, plane_pass(): pl.pallas_call(functools.partial(plane_kernel, k, picked, len(pieces)), o...  23.2 us
    all_to_all x1, blocking collectives, staged(): lax.all_to_all(mine, 'expert', split_axis=0, concat_axis=0, tiled=True)  13 us
    unnamed x19, local copies, waits for them, and re-layouts  8.81 us
    pallas_call x1, Pallas kernels, gram_pass(): pl.pallas_call(gram_kernel, out_shape=jax.ShapeDtypeStruct((hidden, hidde...  3.15 us
  transfers between devices with their start and end apart: 38, of which 14 were waited for; matrix products, arithmetic and copies ran while one was open for 2% of the time, Pallas kernels for 20%

profile of v21, /device:TPU:0, one launch (start us, length us, event | category | flops | bytes accessed | tf_op | source)
XLA Modules:
  0.0 133.5 jit_solution(1202084113111347112)
XLA Ops:
  0.6 3.0 %collective-permute-start.2 = (bf16[128,2048]{1,0:T(8,128)(2,1)}, bf16[128,2048]{1,0:T(8,128)(2,1)S(1)}, u32[]{:S(2)}, u32[]{:S(2)}) collective-permute-start(bf16[128,2048]{1,0:T(8,128)(2,1)} %refs_0_.1), channel_id=1, source_target_pairs={{0,2},{1,3},{2,0},{3,1},{4,6},{5,7},{6,4},{7,5},{8,10},{9,11},{10,... | collective-permute-start | bytes 1572872 | tf_op jit(solution)/shard_map/ppermute | solution.py:259
  3.7 1.6 %collective-permute-start = (bf16[128,2048]{1,0:T(8,128)(2,1)}, bf16[128,2048]{1,0:T(8,128)(2,1)S(1)}, u32[]{:S(2)}, u32[]{:S(2)}) collective-permute-start(bf16[128,2048]{1,0:T(8,128)(2,1)} %refs_0_.1), channel_id=1, source_target_pairs={{0,4},{1,5},{2,6},{3,7},{4,0},{5,1},{6,2},{7,3},{8,12},{9,13},{10,... | collective-permute-start | bytes 1572872 | tf_op jit(solution)/shard_map/ppermute | solution.py:259
  5.2 1.1 copy-done.4
  6.3 0.7 copy-done.6
  7.0 0.7 copy-done.7
  7.8 2.7 %collective-permute-start.1 = (bf16[64,2048]{1,0:T(8,128)(2,1)S(1)}, bf16[64,2048]{1,0:T(8,128)(2,1)S(1)}, u32[]{:S(2)}, u32[]{:S(2)}) collective-permute-start(bf16[64,2048]{1,0:T(8,128)(2,1)S(1)} %get-tuple-element.79), channel_id=1, source_target_pairs={{0,8},{1,9},{2,10},{3,11},{4,12},{5,13},{6,14},{7,15},{8,0},{9,1},... | collective-permute-start | bytes 786440 | tf_op jit(solution)/shard_map/ppermute | solution.py:259
  10.5 11.5 %collective-permute-done.1 = bf16[64,2048]{1,0:T(8,128)(2,1)S(1)} collective-permute-done((bf16[64,2048]{1,0:T(8,128)(2,1)S(1)}, bf16[64,2048]{1,0:T(8,128)(2,1)S(1)}, u32[]{:S(2)}, u32[]{:S(2)}) %collective-permute-start.1) | collective-permute-done | bytes 262176 | tf_op jit(solution)/shard_map/ppermute | solution.py:259
  22.0 0.9 collective-permute-done.refs_0_
  22.9 0.5 collective-permute-start.6
  23.4 0.4 collective-permute-start.5
  23.8 2.7 %collective-permute-start.4 = (bf16[64,2048]{1,0:T(8,128)(2,1)S(1)}, bf16[64,2048]{1,0:T(8,128)(2,1)S(1)}, u32[]{:S(2)}, u32[]{:S(2)}) collective-permute-start(bf16[64,2048]{1,0:T(8,128)(2,1)S(1)} %get-tuple-element.83), channel_id=1, source_target_pairs={{0,8},{1,9},{2,10},{3,11},{4,12},{5,13},{6,14},{7,15},{8,0},{9,1},... | collective-permute-start | bytes 786440 | tf_op jit(solution)/shard_map/ppermute | solution.py:259
  26.4 13.0 %all_to_all.12 = f32[16,1,128]{2,1,0:T(1,128)S(1)} all-to-all(f32[16,1,128]{2,1,0:T(1,128)S(1)} %bitcast.42), channel_id=1, replica_groups=mesh['parts'=2,'expert'=16] {'expert'}, dimensions={0} | all-to-all | bytes 16384 | tf_op jit(solution)/shard_map/all_to_all | solution.py:286
  39.4 0.7 copy-done.8
  40.2 1.0 constant_dynamic-update-slice_fusion.refs_0_
  41.2 0.6 collective-permute-start.10
  41.8 0.7 collective-permute-start.9
  42.4 0.7 collective-permute-start.8
  43.2 0.7 shard_map.78.tables
  44.0 1.9 %copy-done = bf16[1,2048,768]{2,1,0:T(8,128)(2,1)S(1)} copy-done((bf16[1,2048,768]{2,1,0:T(8,128)(2,1)S(1)}, bf16[1,2048,768]{2,1,0:T(8,128)(2,1)}, u32[]{:S(2)}) %copy-start) | copy-done | bytes 3145752
  45.9 1.9 %copy-done.2 = bf16[1,2048,768]{2,1,0:T(8,128)(2,1)S(1)} copy-done((bf16[1,2048,768]{2,1,0:T(8,128)(2,1)S(1)}, bf16[1,2048,768]{2,1,0:T(8,128)(2,1)}, u32[]{:S(2)}) %copy-start.2) | copy-done | bytes 3145752
  47.7 1.9 %copy-done.3 = bf16[1,768,2048]{2,1,0:T(8,128)(2,1)S(1)} copy-done((bf16[1,768,2048]{2,1,0:T(8,128)(2,1)S(1)}, bf16[1,768,2048]{2,1,0:T(8,128)(2,1)}, u32[]{:S(2)}) %copy-start.3) | copy-done | bytes 3145752
  49.6 6.7 %shard_map.79 = (bf16[256,2048]{1,0:T(8,128)(2,1)S(1)}, bf16[128,2048]{1,0:T(8,128)(2,1)S(1)}, bf16[128,2048]{1,0:T(8,128)(2,1)S(1)}, bf16[320,768]{1,0:T(8,128)(2,1)S(1)}) custom-call(f32[16,512]{1,0:T(8,128)S(1)} %shard_map.78.tables, bf16[128,2048]{1,0:T(8,128)(2,1)S(1)} %collective-permute-done.refs_0_, ...), custom_call_target="tpu_custom_call" | custom-call | flops 4362076160 | bytes 13631488 | tf_op jit(solution)/shard_map/pallas_call | solution.py:178
  56.4 1.9 %collective-permute-done.12 = bf16[128,2048]{1,0:T(8,128)(2,1)S(1)} collective-permute-done((bf16[128,2048]{1,0:T(8,128)(2,1)S(1)}, bf16[128,2048]{1,0:T(8,128)(2,1)S(1)}, u32[]{:S(2)}, u32[]{:S(2)}) %collective-permute-start.12) | collective-permute-done | bytes 524320 | tf_op jit(solution)/shard_map/ppermute | solution.py:259
  58.3 0.1 collective-permute-start.16
  58.4 1.3 collective-permute-start.13
  59.8 0.1 add_convert_fusion.7
  59.9 1.4 %collective-permute-start.14 = (bf16[64,2048]{1,0:T(8,128)(2,1)S(1)}, bf16[64,2048]{1,0:T(8,128)(2,1)S(1)}, u32[]{:S(2)}, u32[]{:S(2)}) collective-permute-start(bf16[64,2048]{1,0:T(8,128)(2,1)S(1)} %get-tuple-element.159), channel_id=1, source_target_pairs={{0,2},{1,3},{2,0},{3,1},{4,6},{5,7},{6,4},{7,5},{8,10},{9,11},{10,... | collective-permute-start | bytes 786440 | tf_op jit(solution)/shard_map/ppermute | solution.py:259
  61.4 0.2 collective-permute-start.15
  61.5 5.5 %shard_map.80 = (bf16[256,2048]{1,0:T(8,128)(2,1)S(1)}, bf16[128,2048]{1,0:T(8,128)(2,1)S(1)}, bf16[64,2048]{1,0:T(8,128)(2,1)S(1)}, bf16[64,2048]{1,0:T(8,128)(2,1)S(1)}, bf16[320,768]{1,0:T(8,128)(2,1)S(1)}) custom-call(f32[16,512]{1,0:T(8,128)S(1)} %shard_map.78.tables, bf16[128,2048]{1,0:T(8,128)(2,1)S(1)} %constant_dynamic-update-slice_fusion.refs_0_, ...), custom_call_target="tpu_custom_call" | custom-call | flops 4362076160 | bytes 13631488 | tf_op jit(solution)/shard_map/pallas_call | solution.py:178
  67.0 0.4 collective-permute-start.17
  67.4 2.7 %shard_map.81 = (bf16[128,2048]{1,0:T(8,128)(2,1)S(1)}, bf16[128,2048]{1,0:T(8,128)(2,1)S(1)}, bf16[160,768]{1,0:T(8,128)(2,1)S(1)}) custom-call(f32[16,512]{1,0:T(8,128)S(1)} %shard_map.78.tables, bf16[128,2048]{1,0:T(8,128)(2,1)S(1)} %collective-permute-done.8.refs_0_, bf16[128,2048]{1,0:T(8,128)(2,1)S(1)} %collective-permute-done.18.refs_1_, ...), custom_call_target="tpu_custom_call" | custom-call | flops 1845493760 | bytes 11534336 | tf_op jit(solution)/shard_map/pallas_call | solution.py:178
  70.1 2.5 %collective-permute-done.13.refs_0_ = bf16[128,2048]{1,0:T(8,128)(2,1)S(1)} collective-permute-done((bf16[128,2048]{1,0:T(8,128)(2,1)S(1)}, bf16[128,2048]{1,0:T(8,128)(2,1)S(1)}, u32[]{:S(2)}, u32[]{:S(2)}) %collective-permute-start.13) | collective-permute-done | bytes 524320 | tf_op jit(solution)/shard_map/ppermute | solution.py:259
  72.7 1.4 %collective-permute-start.21 = (bf16[64,2048]{1,0:T(8,128)(2,1)S(1)}, bf16[64,2048]{1,0:T(8,128)(2,1)S(1)}, u32[]{:S(2)}, u32[]{:S(2)}) collective-permute-start(bf16[64,2048]{1,0:T(8,128)(2,1)S(1)} %add_convert_fusion.12), channel_id=1, source_target_pairs={{0,2},{1,3},{2,0},{3,1},{4,6},{5,7},{6,4},{7,5},{8,10},{9,11},{10,... | collective-permute-start | bytes 786440 | tf_op jit(solution)/shard_map/ppermute | solution.py:259
  74.1 0.2 collective-permute-start.20
  74.5 2.9 %shard_map.82 = (bf16[128,2048]{1,0:T(8,128)(2,1)S(1)}, bf16[128,2048]{1,0:T(8,128)(2,1)S(1)}, bf16[160,768]{1,0:T(8,128)(2,1)S(1)}) custom-call(f32[16,512]{1,0:T(8,128)S(1)} %shard_map.78.tables, bf16[128,2048]{1,0:T(8,128)(2,1)S(1)} %collective-permute-done.13.refs_0_, bf16[128,2048]{1,0:T(8,128)(2,1)S(1)} %collective-permute-done.19.refs_1_, ...), custom_call_target="tpu_custom_call" | custom-call | flops 1845493760 | bytes 11534336 | tf_op jit(solution)/shard_map/pallas_call | solution.py:178
  77.4 4.0 %collective-permute-done.21 = bf16[64,2048]{1,0:T(8,128)(2,1)S(1)} collective-permute-done((bf16[64,2048]{1,0:T(8,128)(2,1)S(1)}, bf16[64,2048]{1,0:T(8,128)(2,1)S(1)}, u32[]{:S(2)}, u32[]{:S(2)}) %collective-permute-start.21) | collective-permute-done | bytes 262176 | tf_op jit(solution)/shard_map/ppermute | solution.py:259
  81.5 0.5 collective-permute-start.27
  82.1 3.4 %collective-permute-start.25 = (bf16[64,2048]{1,0:T(8,128)(2,1)S(1)}, bf16[64,2048]{1,0:T(8,128)(2,1)S(1)}, u32[]{:S(2)}, u32[]{:S(2)}) collective-permute-start(bf16[64,2048]{1,0:T(8,128)(2,1)S(1)} %add_convert_fusion.8), channel_id=1, source_target_pairs={{0,8},{1,9},{2,10},{3,11},{4,12},{5,13},{6,14},{7,15},{8,0},{9,1},... | collective-permute-start | bytes 786440 | tf_op jit(solution)/shard_map/ppermute | solution.py:259
  85.5 0.5 collective-permute-start.26
  86.0 0.1 add_convert_fusion.9
  86.1 1.6 %collective-permute-start.24 = (bf16[64,2048]{1,0:T(8,128)(2,1)S(1)}, bf16[64,2048]{1,0:T(8,128)(2,1)S(1)}, u32[]{:S(2)}, u32[]{:S(2)}) collective-permute-start(bf16[64,2048]{1,0:T(8,128)(2,1)S(1)} %get-tuple-element.162), channel_id=1, source_target_pairs={{0,2},{1,3},{2,0},{3,1},{4,6},{5,7},{6,4},{7,5},{8,10},{9,11},{10,... | collective-permute-start | bytes 786440 | tf_op jit(solution)/shard_map/ppermute | solution.py:259
  87.7 0.5 collective-permute-start.23
  88.2 5.5 %shard_map.83 = (bf16[256,2048]{1,0:T(8,128)(2,1)S(1)}, bf16[256,2048]{1,0:T(8,128)(2,1)S(1)}, bf16[320,768]{1,0:T(8,128)(2,1)S(1)}) custom-call(f32[16,512]{1,0:T(8,128)S(1)} %shard_map.78.tables, bf16[128,2048]{1,0:T(8,128)(2,1)S(1)} %copy-done.5, bf16[128,2048]{1,0:T(8,128)(2,1)S(1)} %collective-permute-done.2.refs_1_, ...), custom_call_target="tpu_custom_call" | custom-call | flops 4362076160 | bytes 13631488 | tf_op jit(solution)/shard_map/pallas_call | solution.py:178
  93.7 4.5 %collective-permute-done.25.far_high = bf16[64,2048]{1,0:T(8,128)(2,1)S(1)} collective-permute-done((bf16[64,2048]{1,0:T(8,128)(2,1)S(1)}, bf16[64,2048]{1,0:T(8,128)(2,1)S(1)}, u32[]{:S(2)}, u32[]{:S(2)}) %collective-permute-start.25) | collective-permute-done | bytes 262176 | tf_op jit(solution)/shard_map/ppermute | solution.py:259
  98.2 1.2 collective-permute-done.26.near_low
  99.5 0.5 collective-permute-done.23
  100.0 1.6 %collective-permute-start.31 = (bf16[64,2048]{1,0:T(8,128)(2,1)S(1)}, bf16[64,2048]{1,0:T(8,128)(2,1)S(1)}, u32[]{:S(2)}, u32[]{:S(2)}) collective-permute-start(bf16[64,2048]{1,0:T(8,128)(2,1)S(1)} %add_convert_fusion.4), channel_id=1, source_target_pairs={{0,2},{1,3},{2,0},{3,1},{4,6},{5,7},{6,4},{7,5},{8,10},{9,11},{10,... | collective-permute-start | bytes 786440 | tf_op jit(solution)/shard_map/ppermute | solution.py:259
  101.6 0.2 add_convert_fusion.5
  101.8 1.5 %collective-permute-start.30 = (bf16[64,2048]{1,0:T(8,128)(2,1)S(1)}, bf16[64,2048]{1,0:T(8,128)(2,1)S(1)}, u32[]{:S(2)}, u32[]{:S(2)}) collective-permute-start(bf16[64,2048]{1,0:T(8,128)(2,1)S(1)} %get-tuple-element.160), channel_id=1, source_target_pairs={{0,4},{1,5},{2,6},{3,7},{4,0},{5,1},{6,2},{7,3},{8,12},{9,13},{10,... | collective-permute-start | bytes 786440 | tf_op jit(solution)/shard_map/ppermute | solution.py:259
  103.3 0.4 collective-permute-start.29
  103.7 0.7 collective-permute-start.32
  104.3 3.1 %shard_map.84 = f32[768,768]{1,0:T(8,128)} custom-call(f32[16,512]{1,0:T(8,128)S(1)} %shard_map.78.tables, bf16[320,768]{1,0:T(8,128)(2,1)S(1)} %get-tuple-element.138.refs_0_, bf16[320,768]{1,0:T(8,128)(2,1)S(1)} %get-tuple-element.139.refs_1_, bf16[320,768]{1,0:T(8,128)(2,1)S(1)} %get-tuple-element.140.refs_2_, ...), custom_call_target="tpu_custom_call" | custom-call | flops 1509949440 | bytes 4325376 | tf_op jit(solution)/shard_map/pallas_call | solution.py:209
  107.5 1.7 %collective-permute-done.31 = bf16[64,2048]{1,0:T(8,128)(2,1)S(1)} collective-permute-done((bf16[64,2048]{1,0:T(8,128)(2,1)S(1)}, bf16[64,2048]{1,0:T(8,128)(2,1)S(1)}, u32[]{:S(2)}, u32[]{:S(2)}) %collective-permute-start.31) | collective-permute-done | bytes 262176 | tf_op jit(solution)/shard_map/ppermute | solution.py:259
  109.2 5.0 %collective-permute-done.30 = bf16[64,2048]{1,0:T(8,128)(2,1)S(1)} collective-permute-done((bf16[64,2048]{1,0:T(8,128)(2,1)S(1)}, bf16[64,2048]{1,0:T(8,128)(2,1)S(1)}, u32[]{:S(2)}, u32[]{:S(2)}) %collective-permute-start.30) | collective-permute-done | bytes 262176 | tf_op jit(solution)/shard_map/ppermute | solution.py:259
  114.2 3.8 %collective-permute-done.29 = bf16[64,2048]{1,0:T(8,128)(2,1)S(1)} collective-permute-done((bf16[64,2048]{1,0:T(8,128)(2,1)S(1)}, bf16[64,2048]{1,0:T(8,128)(2,1)S(1)}, u32[]{:S(2)}, u32[]{:S(2)}) %collective-permute-start.29) | collective-permute-done | bytes 262176 | tf_op jit(solution)/shard_map/ppermute | solution.py:259
  118.1 0.1 add_convert_fusion.3
  118.2 0.1 add_convert_fusion
  118.4 0.3 collective-permute-start.37
  118.7 0.1 add_convert_fusion.1
  118.9 0.7 collective-permute-start.35
  119.6 1.4 %collective-permute-start.34 = (bf16[64,2048]{1,0:T(8,128)(2,1)S(1)}, bf16[64,2048]{1,0:T(8,128)(2,1)S(1)}, u32[]{:S(2)}, u32[]{:S(2)}) collective-permute-start(bf16[64,2048]{1,0:T(8,128)(2,1)S(1)} %get-tuple-element.157), channel_id=1, source_target_pairs={{0,2},{1,3},{2,0},{3,1},{4,6},{5,7},{6,4},{7,5},{8,10},{9,11},{10,... | collective-permute-start | bytes 786440 | tf_op jit(solution)/shard_map/ppermute | solution.py:259
  120.9 9.4 %collective-permute-done.36.near_high = bf16[64,2048]{1,0:T(8,128)(2,1)S(1)} collective-permute-done((bf16[64,2048]{1,0:T(8,128)(2,1)S(1)}, bf16[64,2048]{1,0:T(8,128)(2,1)S(1)}, u32[]{:S(2)}, u32[]{:S(2)}) %collective-permute-start.36) | collective-permute-done | bytes 262176 | tf_op jit(solution)/shard_map/ppermute | solution.py:259
  130.4 2.0 %collective-permute-done.37.far_low = bf16[64,2048]{1,0:T(8,128)(2,1)S(1)} collective-permute-done((bf16[64,2048]{1,0:T(8,128)(2,1)S(1)}, bf16[64,2048]{1,0:T(8,128)(2,1)S(1)}, u32[]{:S(2)}, u32[]{:S(2)}) %collective-permute-start.37) | collective-permute-done | bytes 262176 | tf_op jit(solution)/shard_map/ppermute | solution.py:259
  132.4 1.1 shard_map.85
  (53 shorter events, 1.0 us)
Async XLA Ops:
  0.6 21.3 %collective-permute-start.2 = (bf16[128,2048]{1,0:T(8,128)(2,1)}, bf16[128,2048]{1,0:T(8,128)(2,1)S(1)}, u32[]{:S(2)}, u32[]{:S(2)}) collective-permute-start(bf16[128,2048]{1,0:T(8,128)(2,1)} %refs_0_.1), channel_id=1, source_target_pairs={{0,2},{1,3},{2,0},{3,1},{4,6},{5,7},{6,4},{7,5},{8,10},{9,11},{10,... | collective-permute-start | bytes 1572872 | tf_op jit(solution)/shard_map/ppermute | solution.py:259
  3.7 19.2 %collective-permute-start = (bf16[128,2048]{1,0:T(8,128)(2,1)}, bf16[128,2048]{1,0:T(8,128)(2,1)S(1)}, u32[]{:S(2)}, u32[]{:S(2)}) collective-permute-start(bf16[128,2048]{1,0:T(8,128)(2,1)} %refs_0_.1), channel_id=1, source_target_pairs={{0,4},{1,5},{2,6},{3,7},{4,0},{5,1},{6,2},{7,3},{8,12},{9,13},{10,... | collective-permute-start | bytes 1572872 | tf_op jit(solution)/shard_map/ppermute | solution.py:259
  5.2 17.6 %collective-permute-start.3 = (bf16[128,2048]{1,0:T(8,128)(2,1)}, bf16[128,2048]{1,0:T(8,128)(2,1)S(1)}, u32[]{:S(2)}, u32[]{:S(2)}) collective-permute-start(bf16[128,2048]{1,0:T(8,128)(2,1)} %refs_0_.1), channel_id=1, source_target_pairs={{0,1},{1,0},{2,3},{3,2},{4,5},{5,4},{6,7},{7,6},{8,9},{9,8},{10,11... | collective-permute-start | bytes 1572872 | tf_op jit(solution)/shard_map/ppermute | solution.py:259
  5.2 1.1 copy-start.4
  6.3 0.7 copy-start.6
  7.0 0.7 copy-start.7
  7.8 14.2 %collective-permute-start.1 = (bf16[64,2048]{1,0:T(8,128)(2,1)S(1)}, bf16[64,2048]{1,0:T(8,128)(2,1)S(1)}, u32[]{:S(2)}, u32[]{:S(2)}) collective-permute-start(bf16[64,2048]{1,0:T(8,128)(2,1)S(1)} %get-tuple-element.79), channel_id=1, source_target_pairs={{0,8},{1,9},{2,10},{3,11},{4,12},{5,13},{6,14},{7,15},{8,0},{9,1},... | collective-permute-start | bytes 786440 | tf_op jit(solution)/shard_map/ppermute | solution.py:259
  22.9 16.5 %collective-permute-start.7 = (bf16[128,2048]{1,0:T(8,128)(2,1)S(1)}, bf16[128,2048]{1,0:T(8,128)(2,1)S(1)}, u32[]{:S(2)}, u32[]{:S(2)}) collective-permute-start(bf16[128,2048]{1,0:T(8,128)(2,1)S(1)} %collective-permute-done.2.refs_1_), channel_id=1, source_target_pairs={{0,1},{1,0},{2,3},{3,2},{4,5},{5,4},{6,7},{7,6},{8,9},{9,8},{10,11... | collective-permute-start | bytes 1572872 | tf_op jit(solution)/shard_map/ppermute | solution.py:259
  22.9 16.5 %collective-permute-start.6 = (bf16[128,2048]{1,0:T(8,128)(2,1)S(1)}, bf16[128,2048]{1,0:T(8,128)(2,1)S(1)}, u32[]{:S(2)}, u32[]{:S(2)}) collective-permute-start(bf16[128,2048]{1,0:T(8,128)(2,1)S(1)} %collective-permute-done.refs_0_), channel_id=1, source_target_pairs={{0,1},{1,0},{2,3},{3,2},{4,5},{5,4},{6,7},{7,6},{8,9},{9,8},{10,11... | collective-permute-start | bytes 1572872 | tf_op jit(solution)/shard_map/ppermute | solution.py:259
  23.4 16.0 %collective-permute-start.5 = (bf16[128,2048]{1,0:T(8,128)(2,1)S(1)}, bf16[128,2048]{1,0:T(8,128)(2,1)S(1)}, u32[]{:S(2)}, u32[]{:S(2)}) collective-permute-start(bf16[128,2048]{1,0:T(8,128)(2,1)S(1)} %collective-permute-done.refs_0_), channel_id=1, source_target_pairs={{0,2},{1,3},{2,0},{3,1},{4,6},{5,7},{6,4},{7,5},{8,10},{9,11},{10,... | collective-permute-start | bytes 1572872 | tf_op jit(solution)/shard_map/ppermute | solution.py:259
  23.8 15.7 %collective-permute-start.4 = (bf16[64,2048]{1,0:T(8,128)(2,1)S(1)}, bf16[64,2048]{1,0:T(8,128)(2,1)S(1)}, u32[]{:S(2)}, u32[]{:S(2)}) collective-permute-start(bf16[64,2048]{1,0:T(8,128)(2,1)S(1)} %get-tuple-element.83), channel_id=1, source_target_pairs={{0,8},{1,9},{2,10},{3,11},{4,12},{5,13},{6,14},{7,15},{8,0},{9,1},... | collective-permute-start | bytes 786440 | tf_op jit(solution)/shard_map/ppermute | solution.py:259
  39.4 0.7 copy-start.8
  40.1 3.8 %collective-permute-start.11 = (bf16[128,2048]{1,0:T(8,128)(2,1)S(1)}, bf16[128,2048]{1,0:T(8,128)(2,1)}, u32[]{:S(2)}, u32[]{:S(2)}) collective-permute-start(bf16[128,2048]{1,0:T(8,128)(2,1)S(1)} %collective-permute-done.5.refs_1_), channel_id=1, source_target_pairs={{0,1},{1,0},{2,3},{3,2},{4,5},{5,4},{6,7},{7,6},{8,9},{9,8},{10,11... | collective-permute-start | bytes 1572872 | tf_op jit(solution)/shard_map/ppermute | solution.py:259
  41.2 15.2 %collective-permute-start.10 = (bf16[128,2048]{1,0:T(8,128)(2,1)S(1)}, bf16[128,2048]{1,0:T(8,128)(2,1)S(1)}, u32[]{:S(2)}, u32[]{:S(2)}) collective-permute-start(bf16[128,2048]{1,0:T(8,128)(2,1)S(1)} %constant_dynamic-update-slice_fusion.refs_0_), channel_id=1, source_target_pairs={{0,1},{1,0},{2,3},{3,2},{4,5},{5,4},{6,7},{7,6},{8,9},{9,8},{10,11... | collective-permute-start | bytes 1572872 | tf_op jit(solution)/shard_map/ppermute | solution.py:259
  41.8 14.6 %collective-permute-start.9 = (bf16[128,2048]{1,0:T(8,128)(2,1)S(1)}, bf16[128,2048]{1,0:T(8,128)(2,1)S(1)}, u32[]{:S(2)}, u32[]{:S(2)}) collective-permute-start(bf16[128,2048]{1,0:T(8,128)(2,1)S(1)} %constant_dynamic-update-slice_fusion.refs_0_), channel_id=1, source_target_pairs={{0,2},{1,3},{2,0},{3,1},{4,6},{5,7},{6,4},{7,5},{8,10},{9,11},{10,... | collective-permute-start | bytes 1572872 | tf_op jit(solution)/shard_map/ppermute | solution.py:259
  42.4 14.0 %collective-permute-start.8 = (bf16[128,2048]{1,0:T(8,128)(2,1)S(1)}, bf16[128,2048]{1,0:T(8,128)(2,1)S(1)}, u32[]{:S(2)}, u32[]{:S(2)}) collective-permute-start(bf16[128,2048]{1,0:T(8,128)(2,1)S(1)} %constant_dynamic-update-slice_fusion.refs_0_), channel_id=1, source_target_pairs={{0,4},{1,5},{2,6},{3,7},{4,0},{5,1},{6,2},{7,3},{8,12},{9,13},{10,... | collective-permute-start | bytes 1572872 | tf_op jit(solution)/shard_map/ppermute | solution.py:259
  44.0 1.9 %copy-start = (bf16[1,2048,768]{2,1,0:T(8,128)(2,1)S(1)}, bf16[1,2048,768]{2,1,0:T(8,128)(2,1)}, u32[]{:S(2)}) copy-start(bf16[1,2048,768]{2,1,0:T(8,128)(2,1)} %param.9) | copy-start | bytes 9437188
  45.9 1.9 %copy-start.2 = (bf16[1,2048,768]{2,1,0:T(8,128)(2,1)S(1)}, bf16[1,2048,768]{2,1,0:T(8,128)(2,1)}, u32[]{:S(2)}) copy-start(bf16[1,2048,768]{2,1,0:T(8,128)(2,1)} %param.10) | copy-start | bytes 9437188
  47.7 1.9 %copy-start.3 = (bf16[1,768,2048]{2,1,0:T(8,128)(2,1)S(1)}, bf16[1,768,2048]{2,1,0:T(8,128)(2,1)}, u32[]{:S(2)}) copy-start(bf16[1,768,2048]{2,1,0:T(8,128)(2,1)} %param.11) | copy-start | bytes 9437188
  49.6 11.9 %copy-start.1 = (bf16[1,2048,768]{2,1,0:T(8,128)(2,1)S(1)}, bf16[1,2048,768]{2,1,0:T(8,128)(2,1)}, u32[]{:S(2)}) copy-start(bf16[1,2048,768]{2,1,0:T(8,128)(2,1)} %param.9) | copy-start | bytes 9437188
  56.3 2.0 %collective-permute-start.12 = (bf16[128,2048]{1,0:T(8,128)(2,1)S(1)}, bf16[128,2048]{1,0:T(8,128)(2,1)S(1)}, u32[]{:S(2)}, u32[]{:S(2)}) collective-permute-start(bf16[128,2048]{1,0:T(8,128)(2,1)S(1)} %get-tuple-element.94), channel_id=1, source_target_pairs={{0,1},{1,0},{2,3},{3,2},{4,5},{5,4},{6,7},{7,6},{8,9},{9,8},{10,11... | collective-permute-start | bytes 1572872 | tf_op jit(solution)/shard_map/ppermute | solution.py:259
  58.3 3.2 %collective-permute-start.16 = (bf16[128,2048]{1,0:T(8,128)(2,1)S(1)}, bf16[128,2048]{1,0:T(8,128)(2,1)S(1)}, u32[]{:S(2)}, u32[]{:S(2)}) collective-permute-start(bf16[128,2048]{1,0:T(8,128)(2,1)S(1)} %collective-permute-done.9.refs_1_), channel_id=1, source_target_pairs={{0,1},{1,0},{2,3},{3,2},{4,5},{5,4},{6,7},{7,6},{8,9},{9,8},{10,11... | collective-permute-start | bytes 1572872 | tf_op jit(solution)/shard_map/ppermute | solution.py:259
  58.4 14.2 %collective-permute-start.13 = (bf16[128,2048]{1,0:T(8,128)(2,1)S(1)}, bf16[128,2048]{1,0:T(8,128)(2,1)S(1)}, u32[]{:S(2)}, u32[]{:S(2)}) collective-permute-start(bf16[128,2048]{1,0:T(8,128)(2,1)S(1)} %collective-permute-done.9.refs_1_), channel_id=1, source_target_pairs={{0,4},{1,5},{2,6},{3,7},{4,0},{5,1},{6,2},{7,3},{8,12},{9,13},{10,... | collective-permute-start | bytes 1572872 | tf_op jit(solution)/shard_map/ppermute | solution.py:259
  59.7 7.7 %collective-permute-start.18 = (bf16[128,2048]{1,0:T(8,128)(2,1)S(1)}, bf16[128,2048]{1,0:T(8,128)(2,1)S(1)}, u32[]{:S(2)}, u32[]{:S(2)}) collective-permute-start(bf16[128,2048]{1,0:T(8,128)(2,1)S(1)} %collective-permute-done.8.refs_0_), channel_id=1, source_target_pairs={{0,1},{1,0},{2,3},{3,2},{4,5},{5,4},{6,7},{7,6},{8,9},{9,8},{10,11... | collective-permute-start | bytes 1572872 | tf_op jit(solution)/shard_map/ppermute | solution.py:259
  59.9 10.2 %collective-permute-start.14 = (bf16[64,2048]{1,0:T(8,128)(2,1)S(1)}, bf16[64,2048]{1,0:T(8,128)(2,1)S(1)}, u32[]{:S(2)}, u32[]{:S(2)}) collective-permute-start(bf16[64,2048]{1,0:T(8,128)(2,1)S(1)} %get-tuple-element.159), channel_id=1, source_target_pairs={{0,2},{1,3},{2,0},{3,1},{4,6},{5,7},{6,4},{7,5},{8,10},{9,11},{10,... | collective-permute-start | bytes 786440 | tf_op jit(solution)/shard_map/ppermute | solution.py:259
  61.4 8.8 %collective-permute-start.15 = (bf16[128,2048]{1,0:T(8,128)(2,1)S(1)}, bf16[128,2048]{1,0:T(8,128)(2,1)S(1)}, u32[]{:S(2)}, u32[]{:S(2)}) collective-permute-start(bf16[128,2048]{1,0:T(8,128)(2,1)S(1)} %get-tuple-element.98), channel_id=1, source_target_pairs={{0,1},{1,0},{2,3},{3,2},{4,5},{5,4},{6,7},{7,6},{8,9},{9,8},{10,11... | collective-permute-start | bytes 1572872 | tf_op jit(solution)/shard_map/ppermute | solution.py:259
  67.0 5.6 %collective-permute-start.17 = (bf16[64,2048]{1,0:T(8,128)(2,1)S(1)}, bf16[64,2048]{1,0:T(8,128)(2,1)S(1)}, u32[]{:S(2)}, u32[]{:S(2)}) collective-permute-start(bf16[64,2048]{1,0:T(8,128)(2,1)S(1)} %get-tuple-element.101), channel_id=1, source_target_pairs={{0,1},{1,0},{2,3},{3,2},{4,5},{5,4},{6,7},{7,6},{8,9},{9,8},{10,11... | collective-permute-start | bytes 786440 | tf_op jit(solution)/shard_map/ppermute | solution.py:259
  72.6 1.9 %collective-permute-start.19 = (bf16[128,2048]{1,0:T(8,128)(2,1)S(1)}, bf16[128,2048]{1,0:T(8,128)(2,1)S(1)}, u32[]{:S(2)}, u32[]{:S(2)}) collective-permute-start(bf16[128,2048]{1,0:T(8,128)(2,1)S(1)} %collective-permute-done.13.refs_0_), channel_id=1, source_target_pairs={{0,1},{1,0},{2,3},{3,2},{4,5},{5,4},{6,7},{7,6},{8,9},{9,8},{10,11... | collective-permute-start | bytes 1572872 | tf_op jit(solution)/shard_map/ppermute | solution.py:259
  72.7 8.8 %collective-permute-start.21 = (bf16[64,2048]{1,0:T(8,128)(2,1)S(1)}, bf16[64,2048]{1,0:T(8,128)(2,1)S(1)}, u32[]{:S(2)}, u32[]{:S(2)}) collective-permute-start(bf16[64,2048]{1,0:T(8,128)(2,1)S(1)} %add_convert_fusion.12), channel_id=1, source_target_pairs={{0,2},{1,3},{2,0},{3,1},{4,6},{5,7},{6,4},{7,5},{8,10},{9,11},{10,... | collective-permute-start | bytes 786440 | tf_op jit(solution)/shard_map/ppermute | solution.py:259
  74.1 7.4 %collective-permute-start.20 = (bf16[128,2048]{1,0:T(8,128)(2,1)S(1)}, bf16[128,2048]{1,0:T(8,128)(2,1)S(1)}, u32[]{:S(2)}, u32[]{:S(2)}) collective-permute-start(bf16[128,2048]{1,0:T(8,128)(2,1)S(1)} %get-tuple-element.115), channel_id=1, source_target_pairs={{0,1},{1,0},{2,3},{3,2},{4,5},{5,4},{6,7},{7,6},{8,9},{9,8},{10,11... | collective-permute-start | bytes 1572872 | tf_op jit(solution)/shard_map/ppermute | solution.py:259
  74.4 13.8 %copy-start.5 = (bf16[128,2048]{1,0:T(8,128)(2,1)S(1)}, bf16[128,2048]{1,0:T(8,128)(2,1)}, u32[]{:S(2)}) copy-start(bf16[128,2048]{1,0:T(8,128)(2,1)} %refs_0_.1) | copy-start | bytes 1572868
  81.5 4.5 %collective-permute-start.22 = (bf16[128,2048]{1,0:T(8,128)(2,1)S(1)}, bf16[128,2048]{1,0:T(8,128)(2,1)S(1)}, u32[]{:S(2)}, u32[]{:S(2)}) collective-permute-start(bf16[128,2048]{1,0:T(8,128)(2,1)S(1)} %get-tuple-element.121), channel_id=1, source_target_pairs={{0,1},{1,0},{2,3},{3,2},{4,5},{5,4},{6,7},{7,6},{8,9},{9,8},{10,11... | collective-permute-start | bytes 1572872 | tf_op jit(solution)/shard_map/ppermute | solution.py:259
  81.5 6.2 %collective-permute-start.27 = (bf16[64,2048]{1,0:T(8,128)(2,1)S(1)}, bf16[64,2048]{1,0:T(8,128)(2,1)S(1)}, u32[]{:S(2)}, u32[]{:S(2)}) collective-permute-start(bf16[64,2048]{1,0:T(8,128)(2,1)S(1)} %get-tuple-element.125), channel_id=1, source_target_pairs={{0,1},{1,0},{2,3},{3,2},{4,5},{5,4},{6,7},{7,6},{8,9},{9,8},{10,11... | collective-permute-start | bytes 786440 | tf_op jit(solution)/shard_map/ppermute | solution.py:259
  82.0 11.7 %collective-permute-start.28 = (bf16[128,2048]{1,0:T(8,128)(2,1)S(1)}, bf16[128,2048]{1,0:T(8,128)(2,1)S(1)}, u32[]{:S(2)}, u32[]{:S(2)}) collective-permute-start(bf16[128,2048]{1,0:T(8,128)(2,1)S(1)} %get-tuple-element.126), channel_id=1, source_target_pairs={{0,1},{1,0},{2,3},{3,2},{4,5},{5,4},{6,7},{7,6},{8,9},{9,8},{10,11... | collective-permute-start | bytes 1572872 | tf_op jit(solution)/shard_map/ppermute | solution.py:259
  82.1 16.1 %collective-permute-start.25 = (bf16[64,2048]{1,0:T(8,128)(2,1)S(1)}, bf16[64,2048]{1,0:T(8,128)(2,1)S(1)}, u32[]{:S(2)}, u32[]{:S(2)}) collective-permute-start(bf16[64,2048]{1,0:T(8,128)(2,1)S(1)} %add_convert_fusion.8), channel_id=1, source_target_pairs={{0,8},{1,9},{2,10},{3,11},{4,12},{5,13},{6,14},{7,15},{8,0},{9,1},... | collective-permute-start | bytes 786440 | tf_op jit(solution)/shard_map/ppermute | solution.py:259
  85.5 13.9 %collective-permute-start.26 = (bf16[64,2048]{1,0:T(8,128)(2,1)S(1)}, bf16[64,2048]{1,0:T(8,128)(2,1)S(1)}, u32[]{:S(2)}, u32[]{:S(2)}) collective-permute-start(bf16[64,2048]{1,0:T(8,128)(2,1)S(1)} %add_convert_fusion.11), channel_id=1, source_target_pairs={{0,4},{1,5},{2,6},{3,7},{4,0},{5,1},{6,2},{7,3},{8,12},{9,13},{10,... | collective-permute-start | bytes 786440 | tf_op jit(solution)/shard_map/ppermute | solution.py:259
  86.1 13.3 %collective-permute-start.24 = (bf16[64,2048]{1,0:T(8,128)(2,1)S(1)}, bf16[64,2048]{1,0:T(8,128)(2,1)S(1)}, u32[]{:S(2)}, u32[]{:S(2)}) collective-permute-start(bf16[64,2048]{1,0:T(8,128)(2,1)S(1)} %get-tuple-element.162), channel_id=1, source_target_pairs={{0,2},{1,3},{2,0},{3,1},{4,6},{5,7},{6,4},{7,5},{8,10},{9,11},{10,... | collective-permute-start | bytes 786440 | tf_op jit(solution)/shard_map/ppermute | solution.py:259
  87.7 12.3 %collective-permute-start.23 = (bf16[64,2048]{1,0:T(8,128)(2,1)S(1)}, bf16[64,2048]{1,0:T(8,128)(2,1)S(1)}, u32[]{:S(2)}, u32[]{:S(2)}) collective-permute-start(bf16[64,2048]{1,0:T(8,128)(2,1)S(1)} %get-tuple-element.163), channel_id=1, source_target_pairs={{0,2},{1,3},{2,0},{3,1},{4,6},{5,7},{6,4},{7,5},{8,10},{9,11},{10,... | collective-permute-start | bytes 786440 | tf_op jit(solution)/shard_map/ppermute | solution.py:259
  100.0 18.1 %collective-permute-start.33 = (bf16[256,2048]{1,0:T(8,128)(2,1)S(1)}, bf16[256,2048]{1,0:T(8,128)(2,1)S(1)}, u32[]{:S(2)}, u32[]{:S(2)}) collective-permute-start(bf16[256,2048]{1,0:T(8,128)(2,1)S(1)} %get-tuple-element.137), channel_id=1, source_target_pairs={{0,1},{1,0},{2,3},{3,2},{4,5},{5,4},{6,7},{7,6},{8,9},{9,8},{10,11... | collective-permute-start | bytes 3145736 | tf_op jit(solution)/shard_map/ppermute | solution.py:259
  100.0 9.2 %collective-permute-start.31 = (bf16[64,2048]{1,0:T(8,128)(2,1)S(1)}, bf16[64,2048]{1,0:T(8,128)(2,1)S(1)}, u32[]{:S(2)}, u32[]{:S(2)}) collective-permute-start(bf16[64,2048]{1,0:T(8,128)(2,1)S(1)} %add_convert_fusion.4), channel_id=1, source_target_pairs={{0,2},{1,3},{2,0},{3,1},{4,6},{5,7},{6,4},{7,5},{8,10},{9,11},{10,... | collective-permute-start | bytes 786440 | tf_op jit(solution)/shard_map/ppermute | solution.py:259
  101.8 12.4 %collective-permute-start.30 = (bf16[64,2048]{1,0:T(8,128)(2,1)S(1)}, bf16[64,2048]{1,0:T(8,128)(2,1)S(1)}, u32[]{:S(2)}, u32[]{:S(2)}) collective-permute-start(bf16[64,2048]{1,0:T(8,128)(2,1)S(1)} %get-tuple-element.160), channel_id=1, source_target_pairs={{0,4},{1,5},{2,6},{3,7},{4,0},{5,1},{6,2},{7,3},{8,12},{9,13},{10,... | collective-permute-start | bytes 786440 | tf_op jit(solution)/shard_map/ppermute | solution.py:259
  103.3 14.7 %collective-permute-start.29 = (bf16[64,2048]{1,0:T(8,128)(2,1)S(1)}, bf16[64,2048]{1,0:T(8,128)(2,1)S(1)}, u32[]{:S(2)}, u32[]{:S(2)}) collective-permute-start(bf16[64,2048]{1,0:T(8,128)(2,1)S(1)} %get-tuple-element.161), channel_id=1, source_target_pairs={{0,8},{1,9},{2,10},{3,11},{4,12},{5,13},{6,14},{7,15},{8,0},{9,1},... | collective-permute-start | bytes 786440 | tf_op jit(solution)/shard_map/ppermute | solution.py:259
  103.7 14.4 %collective-permute-start.32 = (bf16[64,2048]{1,0:T(8,128)(2,1)S(1)}, bf16[64,2048]{1,0:T(8,128)(2,1)S(1)}, u32[]{:S(2)}, u32[]{:S(2)}) collective-permute-start(bf16[64,2048]{1,0:T(8,128)(2,1)S(1)} %get-tuple-element.136), channel_id=1, source_target_pairs={{0,2},{1,3},{2,0},{3,1},{4,6},{5,7},{6,4},{7,5},{8,10},{9,11},{10,... | collective-permute-start | bytes 786440 | tf_op jit(solution)/shard_map/ppermute | solution.py:259
  118.3 12.0 %collective-permute-start.36 = (bf16[64,2048]{1,0:T(8,128)(2,1)S(1)}, bf16[64,2048]{1,0:T(8,128)(2,1)S(1)}, u32[]{:S(2)}, u32[]{:S(2)}) collective-permute-start(bf16[64,2048]{1,0:T(8,128)(2,1)S(1)} %add_convert_fusion), channel_id=1, source_target_pairs={{0,4},{1,5},{2,6},{3,7},{4,0},{5,1},{6,2},{7,3},{8,12},{9,13},{10,... | collective-permute-start | bytes 786440 | tf_op jit(solution)/shard_map/ppermute | solution.py:259
  118.4 14.0 %collective-permute-start.37 = (bf16[64,2048]{1,0:T(8,128)(2,1)S(1)}, bf16[64,2048]{1,0:T(8,128)(2,1)S(1)}, u32[]{:S(2)}, u32[]{:S(2)}) collective-permute-start(bf16[64,2048]{1,0:T(8,128)(2,1)S(1)} %add_convert_fusion.3), channel_id=1, source_target_pairs={{0,8},{1,9},{2,10},{3,11},{4,12},{5,13},{6,14},{7,15},{8,0},{9,1},... | collective-permute-start | bytes 786440 | tf_op jit(solution)/shard_map/ppermute | solution.py:259
  118.9 13.5 %collective-permute-start.35 = (bf16[64,2048]{1,0:T(8,128)(2,1)S(1)}, bf16[64,2048]{1,0:T(8,128)(2,1)S(1)}, u32[]{:S(2)}, u32[]{:S(2)}) collective-permute-start(bf16[64,2048]{1,0:T(8,128)(2,1)S(1)} %get-tuple-element.156), channel_id=1, source_target_pairs={{0,2},{1,3},{2,0},{3,1},{4,6},{5,7},{6,4},{7,5},{8,10},{9,11},{10,... | collective-permute-start | bytes 786440 | tf_op jit(solution)/shard_map/ppermute | solution.py:259
  119.6 12.8 %collective-permute-start.34 = (bf16[64,2048]{1,0:T(8,128)(2,1)S(1)}, bf16[64,2048]{1,0:T(8,128)(2,1)S(1)}, u32[]{:S(2)}, u32[]{:S(2)}) collective-permute-start(bf16[64,2048]{1,0:T(8,128)(2,1)S(1)} %get-tuple-element.157), channel_id=1, source_target_pairs={{0,2},{1,3},{2,0},{3,1},{4,6},{5,7},{6,4},{7,5},{8,10},{9,11},{10,... | collective-permute-start | bytes 786440 | tf_op jit(solution)/shard_map/ppermute | solution.py:259

commit v22 on v20

--- a/solution.py
+++ b/solution.py
@@ -220,7 +220,7 @@
     )(tables, *acts)
 
 
-def mix_kernel(keep, got, side, near_low, near_high, far_low, far_high, mixed):
+def mix_kernel(far_low, far_high, near_high, near_low, side, keep, got, mixed):
     most, tok = near_low.shape[0], mixed.shape[0]
     for start, stop, near, far in (
         (0, most, near_low, far_low),
@@ -232,7 +232,7 @@
 
 
 def mix_pass(*parts):
-    side = parts[2]
+    side = parts[4]
     vmem = pl.BlockSpec(memory_space=pltpu.VMEM)
     return pl.pallas_call(
         mix_kernel,
@@ -354,7 +354,7 @@
     near1_high = pair(summed(keep1[half:tok], got1[half:], came1_high, far3_high))
     last0 = column(side0)
     mixed = mix_pass(
-        keep0, got0, last0, near1_low, near1_high, far2_low, far2_high
+        far2_low, far2_high, near1_high, near1_low, last0, keep0, got0
     )
 
     return gram[None], mixed

time: 129 us -> 127 us (0.984)
  waiting for transfers between devices: 43.5 us -> 41.7 us
    ppermute x37, waiting for transfers between devices: 43.5 us -> 41.7 us  [swapped(): return lax.ppermute(array, 'expert', [(i, i ^ bit) for i in range(size)])]
  transfers between devices with their start and end apart: 37 -> 37, of which waited for: 11 -> 11; matrix products, arithmetic and copies ran while one was open for 1% -> 1% of each run, Pallas kernels for 20% -> 21%
where the time goes in v22:
time: 127 us; the launch traced here: 126 us
  waiting for transfers between devices  41.7 us (33%)
  starting transfers between devices  31.2 us (25%)
  Pallas kernels  27.1 us (21%)
  blocking collectives  14.2 us (11%)
  local copies, waits for them, and re-layouts  9.97 us (8%)
    ppermute x37, waiting for transfers between devices, swapped(): return lax.ppermute(array, 'expert', [(i, i ^ bit) for i in range(size)])  41.7 us
    ppermute x37, starting transfers between devices, swapped(): return lax.ppermute(array, 'expert', [(i, i ^ bit) for i in range(size)])  31.2 us
    pallas_call x5, Pallas kernels, plane_pass(): pl.pallas_call(functools.partial(plane_kernel, k, picked, len(pieces)), o...  22 us
    all_to_all x1, blocking collectives, staged(): lax.all_to_all(mine, 'expert', split_axis=0, concat_axis=0, tiled=True)  14.2 us
    unnamed x25, local copies, waits for them, and re-layouts  9.86 us
    pallas_call x1, Pallas kernels, gram_pass(): pl.pallas_call(gram_kernel, out_shape=jax.ShapeDtypeStruct((hidden, hidde...  3.14 us
  transfers between devices with their start and end apart: 37, of which 11 were waited for; matrix products, arithmetic and copies ran while one was open for 1% of the time, Pallas kernels for 21%

profile of v22, /device:TPU:0, one launch (start us, length us, event | category | flops | bytes accessed | tf_op | source)
XLA Modules:
  0.0 126.4 jit_solution(6191867067194875628)
XLA Ops:
  0.6 3.1 %collective-permute-start = (bf16[128,2048]{1,0:T(8,128)(2,1)}, bf16[128,2048]{1,0:T(8,128)(2,1)S(1)}, u32[]{:S(2)}, u32[]{:S(2)}) collective-permute-start(bf16[128,2048]{1,0:T(8,128)(2,1)} %refs_0_.1), channel_id=1, source_target_pairs={{0,4},{1,5},{2,6},{3,7},{4,0},{5,1},{6,2},{7,3},{8,12},{9,13},{10,... | collective-permute-start | bytes 1572872 | tf_op jit(solution)/shard_map/ppermute | solution.py:256
  3.7 1.5 %collective-permute-start.2 = (bf16[128,2048]{1,0:T(8,128)(2,1)}, bf16[128,2048]{1,0:T(8,128)(2,1)S(1)}, u32[]{:S(2)}, u32[]{:S(2)}) collective-permute-start(bf16[128,2048]{1,0:T(8,128)(2,1)} %refs_0_.1), channel_id=1, source_target_pairs={{0,2},{1,3},{2,0},{3,1},{4,6},{5,7},{6,4},{7,5},{8,10},{9,11},{10,... | collective-permute-start | bytes 1572872 | tf_op jit(solution)/shard_map/ppermute | solution.py:256
  5.2 1.1 copy-done.6
  6.3 0.7 copy-done.8
  7.0 0.7 copy-done.9
  7.7 0.1 shard_map.77
  7.8 2.7 %collective-permute-start.1 = (bf16[64,2048]{1,0:T(8,128)(2,1)S(1)}, bf16[64,2048]{1,0:T(8,128)(2,1)S(1)}, u32[]{:S(2)}, u32[]{:S(2)}) collective-permute-start(bf16[64,2048]{1,0:T(8,128)(2,1)S(1)} %get-tuple-element.79), channel_id=1, source_target_pairs={{0,8},{1,9},{2,10},{3,11},{4,12},{5,13},{6,14},{7,15},{8,0},{9,1},... | collective-permute-start | bytes 786440 | tf_op jit(solution)/shard_map/ppermute | solution.py:256
  10.5 14.2 %all_to_all.12 = f32[16,1,128]{2,1,0:T(1,128)S(1)} all-to-all(f32[16,1,128]{2,1,0:T(1,128)S(1)} %bitcast.42), channel_id=1, replica_groups=mesh['parts'=2,'expert'=16] {'expert'}, dimensions={0} | all-to-all | bytes 16384 | tf_op jit(solution)/shard_map/all_to_all | solution.py:285
  24.8 0.7 copy-done.10
  25.4 0.5 collective-permute-start.5
  25.9 0.2 collective-permute-start.6
  26.3 1.1 collective-permute-start.4
  27.4 0.7 shard_map.78.tables
  28.2 1.9 %copy-done = bf16[1,2048,768]{2,1,0:T(8,128)(2,1)S(1)} copy-done((bf16[1,2048,768]{2,1,0:T(8,128)(2,1)S(1)}, bf16[1,2048,768]{2,1,0:T(8,128)(2,1)}, u32[]{:S(2)}) %copy-start) | copy-done | bytes 3145752
  30.0 1.9 %copy-done.2 = bf16[1,2048,768]{2,1,0:T(8,128)(2,1)S(1)} copy-done((bf16[1,2048,768]{2,1,0:T(8,128)(2,1)S(1)}, bf16[1,2048,768]{2,1,0:T(8,128)(2,1)}, u32[]{:S(2)}) %copy-start.2) | copy-done | bytes 3145752
  31.9 1.9 %copy-done.4 = bf16[1,768,2048]{2,1,0:T(8,128)(2,1)S(1)} copy-done((bf16[1,768,2048]{2,1,0:T(8,128)(2,1)S(1)}, bf16[1,768,2048]{2,1,0:T(8,128)(2,1)}, u32[]{:S(2)}) %copy-start.4) | copy-done | bytes 3145752
  33.8 1.0 copy-done.7
  34.9 5.5 %shard_map.79 = (bf16[256,2048]{1,0:T(8,128)(2,1)S(1)}, bf16[256,2048]{1,0:T(8,128)(2,1)S(1)}, bf16[320,768]{1,0:T(8,128)(2,1)S(1)}) custom-call(f32[16,512]{1,0:T(8,128)S(1)} %shard_map.78.tables, bf16[128,2048]{1,0:T(8,128)(2,1)S(1)} %copy-done.7, bf16[128,2048]{1,0:T(8,128)(2,1)S(1)} %collective-permute-done.2.refs_1_, ...), custom_call_target="tpu_custom_call" | custom-call | flops 4362076160 | bytes 13631488 | tf_op jit(solution)/shard_map/pallas_call | solution.py:178
  40.4 1.0 collective-permute-done.4
  41.4 0.7 collective-permute-start.8
  42.1 1.1 collective-permute-start.9
  43.3 5.5 %shard_map.80 = (bf16[256,2048]{1,0:T(8,128)(2,1)S(1)}, bf16[128,2048]{1,0:T(8,128)(2,1)S(1)}, bf16[128,2048]{1,0:T(8,128)(2,1)S(1)}, bf16[320,768]{1,0:T(8,128)(2,1)S(1)}) custom-call(f32[16,512]{1,0:T(8,128)S(1)} %shard_map.78.tables, bf16[128,2048]{1,0:T(8,128)(2,1)S(1)} %collective-permute-done.refs_0_, ...), custom_call_target="tpu_custom_call" | custom-call | flops 4362076160 | bytes 13631488 | tf_op jit(solution)/shard_map/pallas_call | solution.py:178
  48.7 0.5 collective-permute-start.12
  49.3 6.5 %collective-permute-done.8.refs_0_ = bf16[128,2048]{1,0:T(8,128)(2,1)S(1)} collective-permute-done((bf16[128,2048]{1,0:T(8,128)(2,1)S(1)}, bf16[128,2048]{1,0:T(8,128)(2,1)S(1)}, u32[]{:S(2)}, u32[]{:S(2)}) %collective-permute-start.8) | collective-permute-done | bytes 524320 | tf_op jit(solution)/shard_map/ppermute | solution.py:256
  55.8 0.3 collective-permute-done.9.refs_1_
  56.1 0.5 collective-permute-start.15
  56.6 1.4 %collective-permute-start.13 = (bf16[128,2048]{1,0:T(8,128)(2,1)S(1)}, bf16[128,2048]{1,0:T(8,128)(2,1)S(1)}, u32[]{:S(2)}, u32[]{:S(2)}) collective-permute-start(bf16[128,2048]{1,0:T(8,128)(2,1)S(1)} %collective-permute-done.9.refs_1_), channel_id=1, source_target_pairs={{0,4},{1,5},{2,6},{3,7},{4,0},{5,1},{6,2},{7,3},{8,12},{9,13},{10,... | collective-permute-start | bytes 1572872 | tf_op jit(solution)/shard_map/ppermute | solution.py:256
  58.1 0.1 add_convert_fusion.6
  58.2 1.5 %collective-permute-start.14 = (bf16[64,2048]{1,0:T(8,128)(2,1)S(1)}, bf16[64,2048]{1,0:T(8,128)(2,1)S(1)}, u32[]{:S(2)}, u32[]{:S(2)}) collective-permute-start(bf16[64,2048]{1,0:T(8,128)(2,1)S(1)} %get-tuple-element.157), channel_id=1, source_target_pairs={{0,2},{1,3},{2,0},{3,1},{4,6},{5,7},{6,4},{7,5},{8,10},{9,11},{10,... | collective-permute-start | bytes 786440 | tf_op jit(solution)/shard_map/ppermute | solution.py:256
  59.7 0.2 collective-permute-start.16
  60.0 5.7 %shard_map.81 = (bf16[256,2048]{1,0:T(8,128)(2,1)S(1)}, bf16[128,2048]{1,0:T(8,128)(2,1)S(1)}, bf16[64,2048]{1,0:T(8,128)(2,1)S(1)}, bf16[64,2048]{1,0:T(8,128)(2,1)S(1)}, bf16[320,768]{1,0:T(8,128)(2,1)S(1)}) custom-call(f32[16,512]{1,0:T(8,128)S(1)} %shard_map.78.tables, bf16[128,2048]{1,0:T(8,128)(2,1)S(1)} %constant_dynamic-update-slice_fusion.refs_0_, ...), custom_call_target="tpu_custom_call" | custom-call | flops 4362076160 | bytes 13631488 | tf_op jit(solution)/shard_map/pallas_call | solution.py:178
  65.6 0.3 collective-permute-start.18
  66.0 2.7 %shard_map.82 = (bf16[128,2048]{1,0:T(8,128)(2,1)S(1)}, bf16[128,2048]{1,0:T(8,128)(2,1)S(1)}, bf16[160,768]{1,0:T(8,128)(2,1)S(1)}) custom-call(f32[16,512]{1,0:T(8,128)S(1)} %shard_map.78.tables, bf16[128,2048]{1,0:T(8,128)(2,1)S(1)} %collective-permute-done.8.refs_0_, bf16[128,2048]{1,0:T(8,128)(2,1)S(1)} %collective-permute-done.19.refs_1_, ...), custom_call_target="tpu_custom_call" | custom-call | flops 1845493760 | bytes 11534336 | tf_op jit(solution)/shard_map/pallas_call | solution.py:178
  68.7 1.8 %collective-permute-done.13.refs_0_ = bf16[128,2048]{1,0:T(8,128)(2,1)S(1)} collective-permute-done((bf16[128,2048]{1,0:T(8,128)(2,1)S(1)}, bf16[128,2048]{1,0:T(8,128)(2,1)S(1)}, u32[]{:S(2)}, u32[]{:S(2)}) %collective-permute-start.13) | collective-permute-done | bytes 524320 | tf_op jit(solution)/shard_map/ppermute | solution.py:256
  70.5 0.5 collective-permute-start.21
  71.1 1.3 %collective-permute-start.22 = (bf16[64,2048]{1,0:T(8,128)(2,1)S(1)}, bf16[64,2048]{1,0:T(8,128)(2,1)S(1)}, u32[]{:S(2)}, u32[]{:S(2)}) collective-permute-start(bf16[64,2048]{1,0:T(8,128)(2,1)S(1)} %add_convert_fusion.11), channel_id=1, source_target_pairs={{0,2},{1,3},{2,0},{3,1},{4,6},{5,7},{6,4},{7,5},{8,10},{9,11},{10,... | collective-permute-start | bytes 786440 | tf_op jit(solution)/shard_map/ppermute | solution.py:256
  72.6 2.7 %shard_map.83 = (bf16[128,2048]{1,0:T(8,128)(2,1)S(1)}, bf16[128,2048]{1,0:T(8,128)(2,1)S(1)}, bf16[160,768]{1,0:T(8,128)(2,1)S(1)}) custom-call(f32[16,512]{1,0:T(8,128)S(1)} %shard_map.78.tables, bf16[128,2048]{1,0:T(8,128)(2,1)S(1)} %collective-permute-done.13.refs_0_, bf16[128,2048]{1,0:T(8,128)(2,1)S(1)} %collective-permute-done.20.refs_1_, ...), custom_call_target="tpu_custom_call" | custom-call | flops 1845493760 | bytes 11534336 | tf_op jit(solution)/shard_map/pallas_call | solution.py:178
  75.3 4.2 %collective-permute-done.22 = bf16[64,2048]{1,0:T(8,128)(2,1)S(1)} collective-permute-done((bf16[64,2048]{1,0:T(8,128)(2,1)S(1)}, bf16[64,2048]{1,0:T(8,128)(2,1)S(1)}, u32[]{:S(2)}, u32[]{:S(2)}) %collective-permute-start.22) | collective-permute-done | bytes 262176 | tf_op jit(solution)/shard_map/ppermute | solution.py:256
  79.5 0.5 collective-permute-start.28
  80.0 0.1 add_convert_fusion.7
  80.1 2.0 %collective-permute-start.26 = (bf16[64,2048]{1,0:T(8,128)(2,1)S(1)}, bf16[64,2048]{1,0:T(8,128)(2,1)S(1)}, u32[]{:S(2)}, u32[]{:S(2)}) collective-permute-start(bf16[64,2048]{1,0:T(8,128)(2,1)S(1)} %add_convert_fusion.7), channel_id=1, source_target_pairs={{0,8},{1,9},{2,10},{3,11},{4,12},{5,13},{6,14},{7,15},{8,0},{9,1},... | collective-permute-start | bytes 786440 | tf_op jit(solution)/shard_map/ppermute | solution.py:256
  82.1 0.5 collective-permute-start.27
  82.6 0.1 add_convert_fusion.8
  82.7 1.6 %collective-permute-start.24 = (bf16[64,2048]{1,0:T(8,128)(2,1)S(1)}, bf16[64,2048]{1,0:T(8,128)(2,1)S(1)}, u32[]{:S(2)}, u32[]{:S(2)}) collective-permute-start(bf16[64,2048]{1,0:T(8,128)(2,1)S(1)} %get-tuple-element.161), channel_id=1, source_target_pairs={{0,2},{1,3},{2,0},{3,1},{4,6},{5,7},{6,4},{7,5},{8,10},{9,11},{10,... | collective-permute-start | bytes 786440 | tf_op jit(solution)/shard_map/ppermute | solution.py:256
  84.3 0.5 collective-permute-start.25
  84.8 0.1 add_convert_fusion
  84.9 10.4 %collective-permute-done.26.far_high = bf16[64,2048]{1,0:T(8,128)(2,1)S(1)} collective-permute-done((bf16[64,2048]{1,0:T(8,128)(2,1)S(1)}, bf16[64,2048]{1,0:T(8,128)(2,1)S(1)}, u32[]{:S(2)}, u32[]{:S(2)}) %collective-permute-start.26) | collective-permute-done | bytes 262176 | tf_op jit(solution)/shard_map/ppermute | solution.py:256
  95.4 1.1 collective-permute-done.25
  96.5 0.2 add_convert_fusion.4
  96.8 2.0 %collective-permute-start.30 = (bf16[64,2048]{1,0:T(8,128)(2,1)S(1)}, bf16[64,2048]{1,0:T(8,128)(2,1)S(1)}, u32[]{:S(2)}, u32[]{:S(2)}) collective-permute-start(bf16[64,2048]{1,0:T(8,128)(2,1)S(1)} %get-tuple-element.159), channel_id=1, source_target_pairs={{0,8},{1,9},{2,10},{3,11},{4,12},{5,13},{6,14},{7,15},{8,0},{9,1},... | collective-permute-start | bytes 786440 | tf_op jit(solution)/shard_map/ppermute | solution.py:256
  98.8 0.6 collective-permute-start.31
  99.4 1.3 %collective-permute-start.32 = (bf16[64,2048]{1,0:T(8,128)(2,1)S(1)}, bf16[64,2048]{1,0:T(8,128)(2,1)S(1)}, u32[]{:S(2)}, u32[]{:S(2)}) collective-permute-start(bf16[64,2048]{1,0:T(8,128)(2,1)S(1)} %add_convert_fusion.3), channel_id=1, source_target_pairs={{0,2},{1,3},{2,0},{3,1},{4,6},{5,7},{6,4},{7,5},{8,10},{9,11},{10,... | collective-permute-start | bytes 786440 | tf_op jit(solution)/shard_map/ppermute | solution.py:256
  100.8 0.8 collective-permute-start.33
  101.5 3.1 %shard_map.84 = f32[768,768]{1,0:T(8,128)} custom-call(f32[16,512]{1,0:T(8,128)S(1)} %shard_map.78.tables, bf16[320,768]{1,0:T(8,128)(2,1)S(1)} %get-tuple-element.139.refs_0_, bf16[320,768]{1,0:T(8,128)(2,1)S(1)} %get-tuple-element.140.refs_1_, bf16[320,768]{1,0:T(8,128)(2,1)S(1)} %get-tuple-element.141.refs_2_, ...), custom_call_target="tpu_custom_call" | custom-call | flops 1509949440 | bytes 4325376 | tf_op jit(solution)/shard_map/pallas_call | solution.py:209
  104.7 6.0 %collective-permute-done.30 = bf16[64,2048]{1,0:T(8,128)(2,1)S(1)} collective-permute-done((bf16[64,2048]{1,0:T(8,128)(2,1)S(1)}, bf16[64,2048]{1,0:T(8,128)(2,1)S(1)}, u32[]{:S(2)}, u32[]{:S(2)}) %collective-permute-start.30) | collective-permute-done | bytes 262176 | tf_op jit(solution)/shard_map/ppermute | solution.py:256
  110.7 1.2 collective-permute-done.33
  111.9 0.1 add_convert_fusion.2
  112.0 2.0 %collective-permute-start.34 = (bf16[64,2048]{1,0:T(8,128)(2,1)S(1)}, bf16[64,2048]{1,0:T(8,128)(2,1)S(1)}, u32[]{:S(2)}, u32[]{:S(2)}) collective-permute-start(bf16[64,2048]{1,0:T(8,128)(2,1)S(1)} %add_convert_fusion.2), channel_id=1, source_target_pairs={{0,8},{1,9},{2,10},{3,11},{4,12},{5,13},{6,14},{7,15},{8,0},{9,1},... | collective-permute-start | bytes 786440 | tf_op jit(solution)/shard_map/ppermute | solution.py:256
  114.0 1.0 collective-permute-start.36
  115.0 0.1 add_convert_fusion.1
  115.1 1.1 collective-permute-start.35
  116.2 8.5 %collective-permute-done.34.far_low = bf16[64,2048]{1,0:T(8,128)(2,1)S(1)} collective-permute-done((bf16[64,2048]{1,0:T(8,128)(2,1)S(1)}, bf16[64,2048]{1,0:T(8,128)(2,1)S(1)}, u32[]{:S(2)}, u32[]{:S(2)}) %collective-permute-start.34) | collective-permute-done | bytes 262176 | tf_op jit(solution)/shard_map/ppermute | solution.py:256
  124.7 0.6 collective-permute-done.35.near_high
  125.3 1.1 shard_map.85
  (57 shorter events, 0.5 us)
Async XLA Ops:
  0.6 24.1 %collective-permute-start = (bf16[128,2048]{1,0:T(8,128)(2,1)}, bf16[128,2048]{1,0:T(8,128)(2,1)S(1)}, u32[]{:S(2)}, u32[]{:S(2)}) collective-permute-start(bf16[128,2048]{1,0:T(8,128)(2,1)} %refs_0_.1), channel_id=1, source_target_pairs={{0,4},{1,5},{2,6},{3,7},{4,0},{5,1},{6,2},{7,3},{8,12},{9,13},{10,... | collective-permute-start | bytes 1572872 | tf_op jit(solution)/shard_map/ppermute | solution.py:256
  3.7 21.0 %collective-permute-start.2 = (bf16[128,2048]{1,0:T(8,128)(2,1)}, bf16[128,2048]{1,0:T(8,128)(2,1)S(1)}, u32[]{:S(2)}, u32[]{:S(2)}) collective-permute-start(bf16[128,2048]{1,0:T(8,128)(2,1)} %refs_0_.1), channel_id=1, source_target_pairs={{0,2},{1,3},{2,0},{3,1},{4,6},{5,7},{6,4},{7,5},{8,10},{9,11},{10,... | collective-permute-start | bytes 1572872 | tf_op jit(solution)/shard_map/ppermute | solution.py:256
  5.2 19.5 %collective-permute-start.3 = (bf16[128,2048]{1,0:T(8,128)(2,1)}, bf16[128,2048]{1,0:T(8,128)(2,1)S(1)}, u32[]{:S(2)}, u32[]{:S(2)}) collective-permute-start(bf16[128,2048]{1,0:T(8,128)(2,1)} %refs_0_.1), channel_id=1, source_target_pairs={{0,1},{1,0},{2,3},{3,2},{4,5},{5,4},{6,7},{7,6},{8,9},{9,8},{10,11... | collective-permute-start | bytes 1572872 | tf_op jit(solution)/shard_map/ppermute | solution.py:256
  5.2 1.1 copy-start.6
  6.3 0.7 copy-start.8
  7.0 0.7 copy-start.9
  7.8 16.9 %collective-permute-start.1 = (bf16[64,2048]{1,0:T(8,128)(2,1)S(1)}, bf16[64,2048]{1,0:T(8,128)(2,1)S(1)}, u32[]{:S(2)}, u32[]{:S(2)}) collective-permute-start(bf16[64,2048]{1,0:T(8,128)(2,1)S(1)} %get-tuple-element.79), channel_id=1, source_target_pairs={{0,8},{1,9},{2,10},{3,11},{4,12},{5,13},{6,14},{7,15},{8,0},{9,1},... | collective-permute-start | bytes 786440 | tf_op jit(solution)/shard_map/ppermute | solution.py:256
  24.7 0.7 copy-start.10
  25.4 2.7 %collective-permute-start.7 = (bf16[128,2048]{1,0:T(8,128)(2,1)S(1)}, bf16[128,2048]{1,0:T(8,128)(2,1)S(1)}, u32[]{:S(2)}, u32[]{:S(2)}) collective-permute-start(bf16[128,2048]{1,0:T(8,128)(2,1)S(1)} %collective-permute-done.2.refs_1_), channel_id=1, source_target_pairs={{0,1},{1,0},{2,3},{3,2},{4,5},{5,4},{6,7},{7,6},{8,9},{9,8},{10,11... | collective-permute-start | bytes 1572872 | tf_op jit(solution)/shard_map/ppermute | solution.py:256
  25.4 15.9 %collective-permute-start.5 = (bf16[128,2048]{1,0:T(8,128)(2,1)S(1)}, bf16[128,2048]{1,0:T(8,128)(2,1)S(1)}, u32[]{:S(2)}, u32[]{:S(2)}) collective-permute-start(bf16[128,2048]{1,0:T(8,128)(2,1)S(1)} %collective-permute-done.refs_0_), channel_id=1, source_target_pairs={{0,2},{1,3},{2,0},{3,1},{4,6},{5,7},{6,4},{7,5},{8,10},{9,11},{10,... | collective-permute-start | bytes 1572872 | tf_op jit(solution)/shard_map/ppermute | solution.py:256
  25.9 15.4 %collective-permute-start.6 = (bf16[128,2048]{1,0:T(8,128)(2,1)S(1)}, bf16[128,2048]{1,0:T(8,128)(2,1)S(1)}, u32[]{:S(2)}, u32[]{:S(2)}) collective-permute-start(bf16[128,2048]{1,0:T(8,128)(2,1)S(1)} %collective-permute-done.refs_0_), channel_id=1, source_target_pairs={{0,1},{1,0},{2,3},{3,2},{4,5},{5,4},{6,7},{7,6},{8,9},{9,8},{10,11... | collective-permute-start | bytes 1572872 | tf_op jit(solution)/shard_map/ppermute | solution.py:256
  26.3 15.1 %collective-permute-start.4 = (bf16[64,2048]{1,0:T(8,128)(2,1)S(1)}, bf16[64,2048]{1,0:T(8,128)(2,1)S(1)}, u32[]{:S(2)}, u32[]{:S(2)}) collective-permute-start(bf16[64,2048]{1,0:T(8,128)(2,1)S(1)} %get-tuple-element.83), channel_id=1, source_target_pairs={{0,8},{1,9},{2,10},{3,11},{4,12},{5,13},{6,14},{7,15},{8,0},{9,1},... | collective-permute-start | bytes 786440 | tf_op jit(solution)/shard_map/ppermute | solution.py:256
  28.2 1.9 %copy-start = (bf16[1,2048,768]{2,1,0:T(8,128)(2,1)S(1)}, bf16[1,2048,768]{2,1,0:T(8,128)(2,1)}, u32[]{:S(2)}) copy-start(bf16[1,2048,768]{2,1,0:T(8,128)(2,1)} %param.9) | copy-start | bytes 9437188
  30.0 1.9 %copy-start.2 = (bf16[1,2048,768]{2,1,0:T(8,128)(2,1)S(1)}, bf16[1,2048,768]{2,1,0:T(8,128)(2,1)}, u32[]{:S(2)}) copy-start(bf16[1,2048,768]{2,1,0:T(8,128)(2,1)} %param.10) | copy-start | bytes 9437188
  31.9 1.9 %copy-start.4 = (bf16[1,768,2048]{2,1,0:T(8,128)(2,1)S(1)}, bf16[1,768,2048]{2,1,0:T(8,128)(2,1)}, u32[]{:S(2)}) copy-start(bf16[1,768,2048]{2,1,0:T(8,128)(2,1)} %param.11) | copy-start | bytes 9437188
  33.8 1.0 copy-start.7
  34.9 6.5 %copy-start.11 = (bf16[64,2048]{1,0:T(8,128)(2,1)S(1)}, bf16[64,2048]{1,0:T(8,128)(2,1)}, u32[]{:S(2)}) copy-start(bf16[64,2048]{1,0:T(8,128)(2,1)} %copy-done.10) | copy-start | bytes 786436
  34.9 8.4 %copy-start.1 = (bf16[1,2048,768]{2,1,0:T(8,128)(2,1)S(1)}, bf16[1,2048,768]{2,1,0:T(8,128)(2,1)}, u32[]{:S(2)}) copy-start(bf16[1,2048,768]{2,1,0:T(8,128)(2,1)} %param.9) | copy-start | bytes 9437188
  34.9 8.4 %copy-start.3 = (bf16[1,2048,768]{2,1,0:T(8,128)(2,1)S(1)}, bf16[1,2048,768]{2,1,0:T(8,128)(2,1)}, u32[]{:S(2)}) copy-start(bf16[1,2048,768]{2,1,0:T(8,128)(2,1)} %param.10) | copy-start | bytes 9437188
  34.9 8.4 %copy-start.5 = (bf16[1,768,2048]{2,1,0:T(8,128)(2,1)S(1)}, bf16[1,768,2048]{2,1,0:T(8,128)(2,1)}, u32[]{:S(2)}) copy-start(bf16[1,768,2048]{2,1,0:T(8,128)(2,1)} %param.11) | copy-start | bytes 9437188
  41.3 1.9 %collective-permute-start.11 = (bf16[128,2048]{1,0:T(8,128)(2,1)S(1)}, bf16[128,2048]{1,0:T(8,128)(2,1)S(1)}, u32[]{:S(2)}, u32[]{:S(2)}) collective-permute-start(bf16[128,2048]{1,0:T(8,128)(2,1)S(1)} %collective-permute-done.5.refs_1_), channel_id=1, source_target_pairs={{0,1},{1,0},{2,3},{3,2},{4,5},{5,4},{6,7},{7,6},{8,9},{9,8},{10,11... | collective-permute-start | bytes 1572872 | tf_op jit(solution)/shard_map/ppermute | solution.py:256
  41.4 14.4 %collective-permute-start.8 = (bf16[128,2048]{1,0:T(8,128)(2,1)S(1)}, bf16[128,2048]{1,0:T(8,128)(2,1)S(1)}, u32[]{:S(2)}, u32[]{:S(2)}) collective-permute-start(bf16[128,2048]{1,0:T(8,128)(2,1)S(1)} %constant_dynamic-update-slice_fusion.refs_0_), channel_id=1, source_target_pairs={{0,4},{1,5},{2,6},{3,7},{4,0},{5,1},{6,2},{7,3},{8,12},{9,13},{10,... | collective-permute-start | bytes 1572872 | tf_op jit(solution)/shard_map/ppermute | solution.py:256
  42.1 14.0 %collective-permute-start.9 = (bf16[128,2048]{1,0:T(8,128)(2,1)S(1)}, bf16[128,2048]{1,0:T(8,128)(2,1)S(1)}, u32[]{:S(2)}, u32[]{:S(2)}) collective-permute-start(bf16[128,2048]{1,0:T(8,128)(2,1)S(1)} %constant_dynamic-update-slice_fusion.refs_0_), channel_id=1, source_target_pairs={{0,2},{1,3},{2,0},{3,1},{4,6},{5,7},{6,4},{7,5},{8,10},{9,11},{10,... | collective-permute-start | bytes 1572872 | tf_op jit(solution)/shard_map/ppermute | solution.py:256
  43.2 12.9 %collective-permute-start.10 = (bf16[128,2048]{1,0:T(8,128)(2,1)S(1)}, bf16[128,2048]{1,0:T(8,128)(2,1)S(1)}, u32[]{:S(2)}, u32[]{:S(2)}) collective-permute-start(bf16[128,2048]{1,0:T(8,128)(2,1)S(1)} %constant_dynamic-update-slice_fusion.refs_0_), channel_id=1, source_target_pairs={{0,1},{1,0},{2,3},{3,2},{4,5},{5,4},{6,7},{7,6},{8,9},{9,8},{10,11... | collective-permute-start | bytes 1572872 | tf_op jit(solution)/shard_map/ppermute | solution.py:256
  48.7 7.4 %collective-permute-start.12 = (bf16[128,2048]{1,0:T(8,128)(2,1)S(1)}, bf16[128,2048]{1,0:T(8,128)(2,1)S(1)}, u32[]{:S(2)}, u32[]{:S(2)}) collective-permute-start(bf16[128,2048]{1,0:T(8,128)(2,1)S(1)} %get-tuple-element.98), channel_id=1, source_target_pairs={{0,1},{1,0},{2,3},{3,2},{4,5},{5,4},{6,7},{7,6},{8,9},{9,8},{10,11... | collective-permute-start | bytes 1572872 | tf_op jit(solution)/shard_map/ppermute | solution.py:256
  56.1 3.6 %collective-permute-start.17 = (bf16[128,2048]{1,0:T(8,128)(2,1)S(1)}, bf16[128,2048]{1,0:T(8,128)(2,1)S(1)}, u32[]{:S(2)}, u32[]{:S(2)}) collective-permute-start(bf16[128,2048]{1,0:T(8,128)(2,1)S(1)} %collective-permute-done.9.refs_1_), channel_id=1, source_target_pairs={{0,1},{1,0},{2,3},{3,2},{4,5},{5,4},{6,7},{7,6},{8,9},{9,8},{10,11... | collective-permute-start | bytes 1572872 | tf_op jit(solution)/shard_map/ppermute | solution.py:256
  56.1 12.6 %collective-permute-start.15 = (bf16[256,2048]{1,0:T(8,128)(2,1)S(1)}, bf16[256,2048]{1,0:T(8,128)(2,1)S(1)}, u32[]{:S(2)}, u32[]{:S(2)}) collective-permute-start(bf16[256,2048]{1,0:T(8,128)(2,1)S(1)} %get-tuple-element.102), channel_id=1, source_target_pairs={{0,1},{1,0},{2,3},{3,2},{4,5},{5,4},{6,7},{7,6},{8,9},{9,8},{10,11... | collective-permute-start | bytes 3145736 | tf_op jit(solution)/shard_map/ppermute | solution.py:256
  56.6 13.9 %collective-permute-start.13 = (bf16[128,2048]{1,0:T(8,128)(2,1)S(1)}, bf16[128,2048]{1,0:T(8,128)(2,1)S(1)}, u32[]{:S(2)}, u32[]{:S(2)}) collective-permute-start(bf16[128,2048]{1,0:T(8,128)(2,1)S(1)} %collective-permute-done.9.refs_1_), channel_id=1, source_target_pairs={{0,4},{1,5},{2,6},{3,7},{4,0},{5,1},{6,2},{7,3},{8,12},{9,13},{10,... | collective-permute-start | bytes 1572872 | tf_op jit(solution)/shard_map/ppermute | solution.py:256
  58.1 7.6 %collective-permute-start.19 = (bf16[128,2048]{1,0:T(8,128)(2,1)S(1)}, bf16[128,2048]{1,0:T(8,128)(2,1)S(1)}, u32[]{:S(2)}, u32[]{:S(2)}) collective-permute-start(bf16[128,2048]{1,0:T(8,128)(2,1)S(1)} %collective-permute-done.8.refs_0_), channel_id=1, source_target_pairs={{0,1},{1,0},{2,3},{3,2},{4,5},{5,4},{6,7},{7,6},{8,9},{9,8},{10,11... | collective-permute-start | bytes 1572872 | tf_op jit(solution)/shard_map/ppermute | solution.py:256
  58.2 10.5 %collective-permute-start.14 = (bf16[64,2048]{1,0:T(8,128)(2,1)S(1)}, bf16[64,2048]{1,0:T(8,128)(2,1)S(1)}, u32[]{:S(2)}, u32[]{:S(2)}) collective-permute-start(bf16[64,2048]{1,0:T(8,128)(2,1)S(1)} %get-tuple-element.157), channel_id=1, source_target_pairs={{0,2},{1,3},{2,0},{3,1},{4,6},{5,7},{6,4},{7,5},{8,10},{9,11},{10,... | collective-permute-start | bytes 786440 | tf_op jit(solution)/shard_map/ppermute | solution.py:256
  59.7 10.8 %collective-permute-start.16 = (bf16[128,2048]{1,0:T(8,128)(2,1)S(1)}, bf16[128,2048]{1,0:T(8,128)(2,1)S(1)}, u32[]{:S(2)}, u32[]{:S(2)}) collective-permute-start(bf16[128,2048]{1,0:T(8,128)(2,1)S(1)} %get-tuple-element.103), channel_id=1, source_target_pairs={{0,1},{1,0},{2,3},{3,2},{4,5},{5,4},{6,7},{7,6},{8,9},{9,8},{10,11... | collective-permute-start | bytes 1572872 | tf_op jit(solution)/shard_map/ppermute | solution.py:256
  65.6 4.9 %collective-permute-start.18 = (bf16[64,2048]{1,0:T(8,128)(2,1)S(1)}, bf16[64,2048]{1,0:T(8,128)(2,1)S(1)}, u32[]{:S(2)}, u32[]{:S(2)}) collective-permute-start(bf16[64,2048]{1,0:T(8,128)(2,1)S(1)} %get-tuple-element.105), channel_id=1, source_target_pairs={{0,1},{1,0},{2,3},{3,2},{4,5},{5,4},{6,7},{7,6},{8,9},{9,8},{10,11... | collective-permute-start | bytes 786440 | tf_op jit(solution)/shard_map/ppermute | solution.py:256
  70.5 2.0 %collective-permute-start.20 = (bf16[128,2048]{1,0:T(8,128)(2,1)S(1)}, bf16[128,2048]{1,0:T(8,128)(2,1)S(1)}, u32[]{:S(2)}, u32[]{:S(2)}) collective-permute-start(bf16[128,2048]{1,0:T(8,128)(2,1)S(1)} %collective-permute-done.13.refs_0_), channel_id=1, source_target_pairs={{0,1},{1,0},{2,3},{3,2},{4,5},{5,4},{6,7},{7,6},{8,9},{9,8},{10,11... | collective-permute-start | bytes 1572872 | tf_op jit(solution)/shard_map/ppermute | solution.py:256
  70.5 8.9 %collective-permute-start.21 = (bf16[128,2048]{1,0:T(8,128)(2,1)S(1)}, bf16[128,2048]{1,0:T(8,128)(2,1)S(1)}, u32[]{:S(2)}, u32[]{:S(2)}) collective-permute-start(bf16[128,2048]{1,0:T(8,128)(2,1)S(1)} %get-tuple-element.119), channel_id=1, source_target_pairs={{0,1},{1,0},{2,3},{3,2},{4,5},{5,4},{6,7},{7,6},{8,9},{9,8},{10,11... | collective-permute-start | bytes 1572872 | tf_op jit(solution)/shard_map/ppermute | solution.py:256
  71.1 8.3 %collective-permute-start.22 = (bf16[64,2048]{1,0:T(8,128)(2,1)S(1)}, bf16[64,2048]{1,0:T(8,128)(2,1)S(1)}, u32[]{:S(2)}, u32[]{:S(2)}) collective-permute-start(bf16[64,2048]{1,0:T(8,128)(2,1)S(1)} %add_convert_fusion.11), channel_id=1, source_target_pairs={{0,2},{1,3},{2,0},{3,1},{4,6},{5,7},{6,4},{7,5},{8,10},{9,11},{10,... | collective-permute-start | bytes 786440 | tf_op jit(solution)/shard_map/ppermute | solution.py:256
  79.5 3.1 %collective-permute-start.23 = (bf16[128,2048]{1,0:T(8,128)(2,1)S(1)}, bf16[128,2048]{1,0:T(8,128)(2,1)S(1)}, u32[]{:S(2)}, u32[]{:S(2)}) collective-permute-start(bf16[128,2048]{1,0:T(8,128)(2,1)S(1)} %get-tuple-element.125), channel_id=1, source_target_pairs={{0,1},{1,0},{2,3},{3,2},{4,5},{5,4},{6,7},{7,6},{8,9},{9,8},{10,11... | collective-permute-start | bytes 1572872 | tf_op jit(solution)/shard_map/ppermute | solution.py:256
  79.5 4.8 %collective-permute-start.28 = (bf16[64,2048]{1,0:T(8,128)(2,1)S(1)}, bf16[64,2048]{1,0:T(8,128)(2,1)S(1)}, u32[]{:S(2)}, u32[]{:S(2)}) collective-permute-start(bf16[64,2048]{1,0:T(8,128)(2,1)S(1)} %get-tuple-element.131), channel_id=1, source_target_pairs={{0,1},{1,0},{2,3},{3,2},{4,5},{5,4},{6,7},{7,6},{8,9},{9,8},{10,11... | collective-permute-start | bytes 786440 | tf_op jit(solution)/shard_map/ppermute | solution.py:256
  80.0 5.0 %collective-permute-start.29 = (bf16[128,2048]{1,0:T(8,128)(2,1)S(1)}, bf16[128,2048]{1,0:T(8,128)(2,1)S(1)}, u32[]{:S(2)}, u32[]{:S(2)}) collective-permute-start(bf16[128,2048]{1,0:T(8,128)(2,1)S(1)} %get-tuple-element.132), channel_id=1, source_target_pairs={{0,1},{1,0},{2,3},{3,2},{4,5},{5,4},{6,7},{7,6},{8,9},{9,8},{10,11... | collective-permute-start | bytes 1572872 | tf_op jit(solution)/shard_map/ppermute | solution.py:256
  80.1 15.3 %collective-permute-start.26 = (bf16[64,2048]{1,0:T(8,128)(2,1)S(1)}, bf16[64,2048]{1,0:T(8,128)(2,1)S(1)}, u32[]{:S(2)}, u32[]{:S(2)}) collective-permute-start(bf16[64,2048]{1,0:T(8,128)(2,1)S(1)} %add_convert_fusion.7), channel_id=1, source_target_pairs={{0,8},{1,9},{2,10},{3,11},{4,12},{5,13},{6,14},{7,15},{8,0},{9,1},... | collective-permute-start | bytes 786440 | tf_op jit(solution)/shard_map/ppermute | solution.py:256
  82.1 13.3 %collective-permute-start.27 = (bf16[64,2048]{1,0:T(8,128)(2,1)S(1)}, bf16[64,2048]{1,0:T(8,128)(2,1)S(1)}, u32[]{:S(2)}, u32[]{:S(2)}) collective-permute-start(bf16[64,2048]{1,0:T(8,128)(2,1)S(1)} %add_convert_fusion.10), channel_id=1, source_target_pairs={{0,4},{1,5},{2,6},{3,7},{4,0},{5,1},{6,2},{7,3},{8,12},{9,13},{10,... | collective-permute-start | bytes 786440 | tf_op jit(solution)/shard_map/ppermute | solution.py:256
  82.7 12.7 %collective-permute-start.24 = (bf16[64,2048]{1,0:T(8,128)(2,1)S(1)}, bf16[64,2048]{1,0:T(8,128)(2,1)S(1)}, u32[]{:S(2)}, u32[]{:S(2)}) collective-permute-start(bf16[64,2048]{1,0:T(8,128)(2,1)S(1)} %get-tuple-element.161), channel_id=1, source_target_pairs={{0,2},{1,3},{2,0},{3,1},{4,6},{5,7},{6,4},{7,5},{8,10},{9,11},{10,... | collective-permute-start | bytes 786440 | tf_op jit(solution)/shard_map/ppermute | solution.py:256
  84.3 12.3 %collective-permute-start.25 = (bf16[64,2048]{1,0:T(8,128)(2,1)S(1)}, bf16[64,2048]{1,0:T(8,128)(2,1)S(1)}, u32[]{:S(2)}, u32[]{:S(2)}) collective-permute-start(bf16[64,2048]{1,0:T(8,128)(2,1)S(1)} %get-tuple-element.160), channel_id=1, source_target_pairs={{0,2},{1,3},{2,0},{3,1},{4,6},{5,7},{6,4},{7,5},{8,10},{9,11},{10,... | collective-permute-start | bytes 786440 | tf_op jit(solution)/shard_map/ppermute | solution.py:256
  96.8 13.9 %collective-permute-start.30 = (bf16[64,2048]{1,0:T(8,128)(2,1)S(1)}, bf16[64,2048]{1,0:T(8,128)(2,1)S(1)}, u32[]{:S(2)}, u32[]{:S(2)}) collective-permute-start(bf16[64,2048]{1,0:T(8,128)(2,1)S(1)} %get-tuple-element.159), channel_id=1, source_target_pairs={{0,8},{1,9},{2,10},{3,11},{4,12},{5,13},{6,14},{7,15},{8,0},{9,1},... | collective-permute-start | bytes 786440 | tf_op jit(solution)/shard_map/ppermute | solution.py:256
  98.8 11.9 %collective-permute-start.31 = (bf16[64,2048]{1,0:T(8,128)(2,1)S(1)}, bf16[64,2048]{1,0:T(8,128)(2,1)S(1)}, u32[]{:S(2)}, u32[]{:S(2)}) collective-permute-start(bf16[64,2048]{1,0:T(8,128)(2,1)S(1)} %get-tuple-element.158), channel_id=1, source_target_pairs={{0,4},{1,5},{2,6},{3,7},{4,0},{5,1},{6,2},{7,3},{8,12},{9,13},{10,... | collective-permute-start | bytes 786440 | tf_op jit(solution)/shard_map/ppermute | solution.py:256
  99.4 11.2 %collective-permute-start.32 = (bf16[64,2048]{1,0:T(8,128)(2,1)S(1)}, bf16[64,2048]{1,0:T(8,128)(2,1)S(1)}, u32[]{:S(2)}, u32[]{:S(2)}) collective-permute-start(bf16[64,2048]{1,0:T(8,128)(2,1)S(1)} %add_convert_fusion.3), channel_id=1, source_target_pairs={{0,2},{1,3},{2,0},{3,1},{4,6},{5,7},{6,4},{7,5},{8,10},{9,11},{10,... | collective-permute-start | bytes 786440 | tf_op jit(solution)/shard_map/ppermute | solution.py:256
  100.8 11.1 %collective-permute-start.33 = (bf16[64,2048]{1,0:T(8,128)(2,1)S(1)}, bf16[64,2048]{1,0:T(8,128)(2,1)S(1)}, u32[]{:S(2)}, u32[]{:S(2)}) collective-permute-start(bf16[64,2048]{1,0:T(8,128)(2,1)S(1)} %get-tuple-element.137), channel_id=1, source_target_pairs={{0,2},{1,3},{2,0},{3,1},{4,6},{5,7},{6,4},{7,5},{8,10},{9,11},{10,... | collective-permute-start | bytes 786440 | tf_op jit(solution)/shard_map/ppermute | solution.py:256
  112.0 12.7 %collective-permute-start.34 = (bf16[64,2048]{1,0:T(8,128)(2,1)S(1)}, bf16[64,2048]{1,0:T(8,128)(2,1)S(1)}, u32[]{:S(2)}, u32[]{:S(2)}) collective-permute-start(bf16[64,2048]{1,0:T(8,128)(2,1)S(1)} %add_convert_fusion.2), channel_id=1, source_target_pairs={{0,8},{1,9},{2,10},{3,11},{4,12},{5,13},{6,14},{7,15},{8,0},{9,1},... | collective-permute-start | bytes 786440 | tf_op jit(solution)/shard_map/ppermute | solution.py:256
  114.0 11.2 %collective-permute-start.36 = (bf16[128,2048]{1,0:T(8,128)(2,1)S(1)}, bf16[128,2048]{1,0:T(8,128)(2,1)S(1)}, u32[]{:S(2)}, u32[]{:S(2)}) collective-permute-start(bf16[128,2048]{1,0:T(8,128)(2,1)S(1)} %add_convert_fusion), channel_id=1, source_target_pairs={{0,2},{1,3},{2,0},{3,1},{4,6},{5,7},{6,4},{7,5},{8,10},{9,11},{10,... | collective-permute-start | bytes 1572872 | tf_op jit(solution)/shard_map/ppermute | solution.py:256
  115.1 10.1 %collective-permute-start.35 = (bf16[64,2048]{1,0:T(8,128)(2,1)S(1)}, bf16[64,2048]{1,0:T(8,128)(2,1)S(1)}, u32[]{:S(2)}, u32[]{:S(2)}) collective-permute-start(bf16[64,2048]{1,0:T(8,128)(2,1)S(1)} %add_convert_fusion.1), channel_id=1, source_target_pairs={{0,4},{1,5},{2,6},{3,7},{4,0},{5,1},{6,2},{7,3},{8,12},{9,13},{10,... | collective-permute-start | bytes 786440 | tf_op jit(solution)/shard_map/ppermute | solution.py:256

commit v23 on v22

--- a/solution.py
+++ b/solution.py
@@ -28,44 +28,24 @@
     return lax.all_to_all(mine, "expert", split_axis=0, concat_axis=0, tiled=True)
 
 
-def prepare_kernel(routes, probs, tokens, mine, low, high, names, shares, sems):
-    half = low.shape[0]
-    pairs = (
-        (routes, names),
-        (probs, shares),
-        (tokens.at[pl.ds(0, half), :], low),
-        (tokens.at[pl.ds(half, half), :], high),
-    )
-    copies = [pltpu.make_async_copy(*pair, sems.at[i]) for i, pair in enumerate(pairs)]
-    for copy in copies:
-        copy.start()
-    for copy in copies[:2]:
-        copy.wait()
+def table_kernel(routes, probs, mine):
+    names, shares = routes[...], probs[...]
     for e in range(mine.shape[0]):
-        hit = (names[...] == e).astype(jnp.float32)
+        hit = (names == e).astype(jnp.float32)
         named = jnp.sum(hit, axis=0, keepdims=True)
-        share = jnp.sum(hit * shares[...], axis=0, keepdims=True)
+        share = jnp.sum(hit * shares, axis=0, keepdims=True)
         mine[pl.ds(e, 1), :] = jnp.where(named > 0.0, share, -1.0)
-    for copy in copies[2:]:
-        copy.wait()
-
-
-def prepare_pass(routes, probs, tokens, experts):
-    tok, top = routes.shape
-    half = jax.ShapeDtypeStruct((tok // 2, tokens.shape[1]), tokens.dtype)
-    vmem = pl.BlockSpec(memory_space=pltpu.VMEM)
-    return pl.pallas_call(
-        prepare_kernel,
-        out_shape=(jax.ShapeDtypeStruct((experts, tok), jnp.float32), half, half),
-        in_specs=[pl.BlockSpec(memory_space=pl.ANY)] * 3,
-        out_specs=[vmem] * 3,
-        scratch_shapes=[
-            pltpu.VMEM((top, tok), routes.dtype),
-            pltpu.VMEM((top, tok), probs.dtype),
-            pltpu.SemaphoreType.DMA((4,)),
-        ],
+
+
+def table_pass(routes, probs, experts):
+    vmem = pl.BlockSpec(memory_space=pltpu.VMEM)
+    return pl.pallas_call(
+        table_kernel,
+        out_shape=jax.ShapeDtypeStruct((experts, routes.shape[0]), jnp.float32),
+        in_specs=[vmem] * 2,
+        out_specs=vmem,
         compiler_params=pltpu.CompilerParams(vmem_limit_bytes=4 * 1024 * 1024),
-    )(routes.T, probs.T, tokens)
+    )(routes.T, probs.T)
 
 
 def summed(*parts):
@@ -275,26 +255,29 @@
     def expert(k, *xs, pieces=None, picked=None):
         return plane_pass(k, tables, xs, w_gate, w_up, w_down, slots, pieces, picked)
 
-    mine, a0_low, a0_high = prepare_pass(routes, probs, tokens, size)
+    def far_of(which, array):
+        pairs = [(i, i ^ 8) for i in range(size) if i % 2 == which]
+        return lax.ppermute(array, "expert", pairs)
+
+    mine = table_pass(routes, probs, size)
     a0 = tokens
-    a1, low, b0, c0, weight, a0_high = together(
+    a1, far_0, b0, c0, weight = together(
         pair(a0),
-        far(a0_low),
+        far_of(0, a0),
         column(a0),
         sibling(a0),
         lax.all_to_all(mine, "expert", split_axis=0, concat_axis=0, tiled=True),
-        a0_high,
     )
     tables = ranks_pass(capacity, spots, weight)
-    high = far(a0_high)
+    far_1 = far_of(1, a0)
     b1 = column(a1)
     d0 = sibling(b0)
     c1 = sibling(a1)
     keep0, give0, act0 = expert(0, a0, b0, c0, d0)
-    high, b1, c1, keep0, give0, act0, tables = together(
-        high, b1, c1, keep0, give0, act0, tables
-    )
-    a2 = jnp.concatenate([low, high], axis=0)
+    far_1, b1, c1, keep0, give0, act0, tables = together(
+        far_1, b1, c1, keep0, give0, act0, tables
+    )
+    a2 = jnp.where(core == 0, far_0, far_1)
     a3 = pair(a2)
     b2 = column(a2)
     d1 = sibling(b1)

time: 127 us -> 138 us (1.087)
  local copies, waits for them, and re-layouts: 9.97 us -> 20.2 us
  waiting for transfers between devices: 41.7 us -> 38.8 us
  starting transfers between devices: 31.2 us -> 33.1 us
  Pallas kernels: 27.1 us -> 28.7 us
    unnamed x25 -> x44, local copies, waits for them, and re-layouts: 9.86 us -> 20.1 us
    ppermute x0 -> x2, starting transfers between devices: none -> 5.94 us  [far_of(): return lax.ppermute(array, 'expert', pairs)]
    ppermute x37 -> x35, starting transfers between devices: 31.2 us -> 27.2 us  [swapped(): return lax.ppermute(array, 'expert', [(i, i ^ bit) for i in range(size)])]
    ppermute x37 -> x35, waiting for transfers between devices: 41.7 us -> 38.8 us  [swapped(): return lax.ppermute(array, 'expert', [(i, i ^ bit) for i in range(size)])]
    pallas_call x5, Pallas kernels: 22 us -> 23.7 us  [plane_pass(): pl.pallas_call(functools.partial(plane_kernel, k, picked, len(pieces)), o...]
  transfers between devices with their start and end apart: 37 -> 37, of which waited for: 11 -> 12; matrix products, arithmetic and copies ran while one was open for 1% -> 2% of each run, Pallas kernels for 21% -> 20%
where the time goes in v23:
time: 138 us
  waiting for transfers between devices  38.8 us (28%)
  starting transfers between devices  33.1 us (24%)
  Pallas kernels  28.7 us (21%)
  local copies, waits for them, and re-layouts  20.2 us (15%)
  blocking collectives  13.5 us (10%)
  other arithmetic  2.4 us (2%)
    ppermute x35, waiting for transfers between devices, swapped(): return lax.ppermute(array, 'expert', [(i, i ^ bit) for i in range(size)])  38.8 us
    ppermute x35, starting transfers between devices, swapped(): return lax.ppermute(array, 'expert', [(i, i ^ bit) for i in range(size)])  27.2 us
    pallas_call x5, Pallas kernels, plane_pass(): pl.pallas_call(functools.partial(plane_kernel, k, picked, len(pieces)), o...  23.7 us
    unnamed x44, local copies, waits for them, and re-layouts  20.1 us
    all_to_all x1, blocking collectives, staged(): lax.all_to_all(mine, 'expert', split_axis=0, concat_axis=0, tiled=True)  13.5 us
    ppermute x2, starting transfers between devices, far_of(): return lax.ppermute(array, 'expert', pairs)  5.94 us
    pallas_call x1, Pallas kernels, gram_pass(): pl.pallas_call(gram_kernel, out_shape=jax.ShapeDtypeStruct((hidden, hidde...  3.15 us
  transfers between devices with their start and end apart: 37, of which 12 were waited for; matrix products, arithmetic and copies ran while one was open for 2% of the time, Pallas kernels for 20%

profile of v23, /device:TPU:0, one launch (start us, length us, event | category | flops | bytes accessed | tf_op | source)
XLA Modules:
  0.0 137.7 jit_solution(8800593708463926481)
XLA Ops:
  0.6 3.1 %collective-permute-start = (bf16[128,2048]{1,0:T(8,128)(2,1)}, bf16[128,2048]{1,0:T(8,128)(2,1)}, u32[]{:S(2)}, u32[]{:S(2)}) collective-permute-start(bf16[128,2048]{1,0:T(8,128)(2,1)} %refs_0_.1), channel_id=1, source_target_pairs={{0,4},{1,5},{2,6},{3,7},{4,0},{5,1},{6,2},{7,3},{8,12},{9,13},{10,... | collective-permute-start | bytes 1572872 | tf_op jit(solution)/shard_map/ppermute | solution.py:236
  3.7 4.5 %collective-permute-start.1 = (bf16[128,2048]{1,0:T(8,128)(2,1)}, bf16[128,2048]{1,0:T(8,128)(2,1)}, u32[]{:S(2)}, u32[]{:S(2)}) collective-permute-start(bf16[128,2048]{1,0:T(8,128)(2,1)} %refs_0_.1), channel_id=1, source_target_pairs={{0,8},{2,10},{4,12},{6,14},{8,0},{10,2},{12,4},{14,6},{16,24},{18,... | collective-permute-start | bytes 1572872 | tf_op jit(solution)/shard_map/ppermute | solution.py:260
  8.2 1.6 %collective-permute-start.2 = (bf16[128,2048]{1,0:T(8,128)(2,1)}, bf16[128,2048]{1,0:T(8,128)(2,1)S(1)}, u32[]{:S(2)}, u32[]{:S(2)}) collective-permute-start(bf16[128,2048]{1,0:T(8,128)(2,1)} %refs_0_.1), channel_id=1, source_target_pairs={{0,2},{1,3},{2,0},{3,1},{4,6},{5,7},{6,4},{7,5},{8,10},{9,11},{10,... | collective-permute-start | bytes 1572872 | tf_op jit(solution)/shard_map/ppermute | solution.py:236
  9.8 0.7 copy-done.9
  10.5 0.7 copy-done.10
  11.2 13.5 %all_to_all.12 = f32[16,1,128]{2,1,0:T(1,128)S(1)} all-to-all(f32[16,1,128]{2,1,0:T(1,128)S(1)} %bitcast.41), channel_id=1, replica_groups=mesh['parts'=2,'expert'=16] {'expert'}, dimensions={0} | all-to-all | bytes 16384 | tf_op jit(solution)/shard_map/all_to_all | solution.py:269
  24.8 0.8 copy-done.16
  25.5 0.8 copy-done.14
  26.3 1.4 %collective-permute-start.4 = (bf16[128,2048]{1,0:T(8,128)(2,1)}, bf16[128,2048]{1,0:T(8,128)(2,1)}, u32[]{:S(2)}, u32[]{:S(2)}) collective-permute-start(bf16[128,2048]{1,0:T(8,128)(2,1)} %refs_0_.1), channel_id=1, source_target_pairs={{1,9},{3,11},{5,13},{7,15},{9,1},{11,3},{13,5},{15,7},{17,25},{19,... | collective-permute-start | bytes 1572872 | tf_op jit(solution)/shard_map/ppermute | solution.py:260
  27.8 0.5 collective-permute-start.5
  28.3 1.1 collective-permute-start.6
  29.5 0.8 shard_map.78.tables
  30.3 0.8 copy-done.18
  31.0 1.9 %copy-done = bf16[1,2048,768]{2,1,0:T(8,128)(2,1)S(1)} copy-done((bf16[1,2048,768]{2,1,0:T(8,128)(2,1)S(1)}, bf16[1,2048,768]{2,1,0:T(8,128)(2,1)}, u32[]{:S(2)}) %copy-start) | copy-done | bytes 3145752
  32.9 1.9 %copy-done.2 = bf16[1,2048,768]{2,1,0:T(8,128)(2,1)S(1)} copy-done((bf16[1,2048,768]{2,1,0:T(8,128)(2,1)S(1)}, bf16[1,2048,768]{2,1,0:T(8,128)(2,1)}, u32[]{:S(2)}) %copy-start.2) | copy-done | bytes 3145752
  34.8 1.9 %copy-done.5 = bf16[1,768,2048]{2,1,0:T(8,128)(2,1)S(1)} copy-done((bf16[1,768,2048]{2,1,0:T(8,128)(2,1)S(1)}, bf16[1,768,2048]{2,1,0:T(8,128)(2,1)}, u32[]{:S(2)}) %copy-start.5) | copy-done | bytes 3145752
  36.7 1.0 copy-done.13
  37.8 1.0 copy-done.15
  38.8 1.0 copy-done.17
  39.8 1.0 copy-done.19
  40.9 5.5 %shard_map.79 = (bf16[256,2048]{1,0:T(8,128)(2,1)S(1)}, bf16[256,2048]{1,0:T(8,128)(2,1)S(1)}, bf16[320,768]{1,0:T(8,128)(2,1)S(1)}) custom-call(f32[16,512]{1,0:T(8,128)S(1)} %shard_map.78.tables, bf16[128,2048]{1,0:T(8,128)(2,1)S(1)} %copy-done.13, bf16[128,2048]{1,0:T(8,128)(2,1)S(1)} %copy-done.15, bf16[128,2048]{1,0:T(8,128)(2,1)S(1)} %copy-done.17, ...), custom_call_target="tpu_custom_call" | custom-call | flops 4362076160 | bytes 13631488 | tf_op jit(solution)/shard_map/pallas_call | solution.py:158
  46.4 1.0 copy-done.7
  47.4 1.0 copy-done.11
  48.3 0.8 copy-done.20
  49.2 1.2 broadcast_select_fusion.refs_0_
  50.4 1.8 %collective-permute-start.8 = (bf16[128,2048]{1,0:T(8,128)(2,1)S(1)}, bf16[128,2048]{1,0:T(8,128)(2,1)S(1)}, u32[]{:S(2)}, u32[]{:S(2)}) collective-permute-start(bf16[128,2048]{1,0:T(8,128)(2,1)S(1)} %broadcast_select_fusion.refs_0_), channel_id=1, source_target_pairs={{0,4},{1,5},{2,6},{3,7},{4,0},{5,1},{6,2},{7,3},{8,12},{9,13},{10,... | collective-permute-start | bytes 1572872 | tf_op jit(solution)/shard_map/ppermute | solution.py:236
  52.2 1.3 collective-permute-start.9
  53.6 1.9 %copy-done.3 = bf16[1,2048,768]{2,1,0:T(8,128)(2,1)S(1)} copy-done((bf16[1,2048,768]{2,1,0:T(8,128)(2,1)S(1)}, bf16[1,2048,768]{2,1,0:T(8,128)(2,1)}, u32[]{:S(2)}) %copy-start.3) | copy-done | bytes 3145752
  55.4 1.9 %copy-done.6 = bf16[1,768,2048]{2,1,0:T(8,128)(2,1)S(1)} copy-done((bf16[1,768,2048]{2,1,0:T(8,128)(2,1)S(1)}, bf16[1,768,2048]{2,1,0:T(8,128)(2,1)}, u32[]{:S(2)}) %copy-start.6) | copy-done | bytes 3145752
  57.3 7.1 %shard_map.80 = (bf16[256,2048]{1,0:T(8,128)(2,1)S(1)}, bf16[128,2048]{1,0:T(8,128)(2,1)S(1)}, bf16[128,2048]{1,0:T(8,128)(2,1)S(1)}, bf16[320,768]{1,0:T(8,128)(2,1)S(1)}) custom-call(f32[16,512]{1,0:T(8,128)S(1)} %shard_map.78.tables, bf16[128,2048]{1,0:T(8,128)(2,1)} %collective-permute-done.refs_0_, bf16[128,2048]{1,0:T(8,128)(2,1)} %collective-permute-done.5.refs_1_, ...), custom_call_target="tpu_custom_call" | custom-call | flops 4362076160 | bytes 13631488 | tf_op jit(solution)/shard_map/pallas_call | solution.py:158
  64.5 0.6 collective-permute-start.12
  65.0 1.2 collective-permute-done.9.refs_1_
  66.2 0.4 collective-permute-done.12
  66.6 0.4 collective-permute-start.17
  67.1 0.4 collective-permute-start.13
  67.7 1.0 collective-permute-start.14
  68.9 5.7 %shard_map.81 = (bf16[256,2048]{1,0:T(8,128)(2,1)S(1)}, bf16[128,2048]{1,0:T(8,128)(2,1)S(1)}, bf16[64,2048]{1,0:T(8,128)(2,1)S(1)}, bf16[64,2048]{1,0:T(8,128)(2,1)S(1)}, bf16[320,768]{1,0:T(8,128)(2,1)S(1)}) custom-call(f32[16,512]{1,0:T(8,128)S(1)} %shard_map.78.tables, bf16[128,2048]{1,0:T(8,128)(2,1)S(1)} %broadcast_select_fusion.refs_0_, ...), custom_call_target="tpu_custom_call" | custom-call | flops 4362076160 | bytes 13631488 | tf_op jit(solution)/shard_map/pallas_call | solution.py:158
  75.0 2.7 %shard_map.82 = (bf16[128,2048]{1,0:T(8,128)(2,1)S(1)}, bf16[128,2048]{1,0:T(8,128)(2,1)S(1)}, bf16[160,768]{1,0:T(8,128)(2,1)S(1)}) custom-call(f32[16,512]{1,0:T(8,128)S(1)} %shard_map.78.tables, bf16[128,2048]{1,0:T(8,128)(2,1)S(1)} %collective-permute-done.8.refs_0_, bf16[128,2048]{1,0:T(8,128)(2,1)S(1)} %collective-permute-done.19.refs_1_, ...), custom_call_target="tpu_custom_call" | custom-call | flops 1845493760 | bytes 11534336 | tf_op jit(solution)/shard_map/pallas_call | solution.py:158
  77.7 3.6 %collective-permute-done.13.refs_0_ = bf16[128,2048]{1,0:T(8,128)(2,1)S(1)} collective-permute-done((bf16[128,2048]{1,0:T(8,128)(2,1)S(1)}, bf16[128,2048]{1,0:T(8,128)(2,1)S(1)}, u32[]{:S(2)}, u32[]{:S(2)}) %collective-permute-start.13) | collective-permute-done | bytes 524320 | tf_op jit(solution)/shard_map/ppermute | solution.py:236
  81.3 0.5 collective-permute-start.21
  81.9 0.8 collective-permute-start.22
  82.8 0.5 collective-permute-done.20.refs_1_
  83.2 2.7 %shard_map.83 = (bf16[128,2048]{1,0:T(8,128)(2,1)S(1)}, bf16[128,2048]{1,0:T(8,128)(2,1)S(1)}, bf16[160,768]{1,0:T(8,128)(2,1)S(1)}) custom-call(f32[16,512]{1,0:T(8,128)S(1)} %shard_map.78.tables, bf16[128,2048]{1,0:T(8,128)(2,1)S(1)} %collective-permute-done.13.refs_0_, bf16[128,2048]{1,0:T(8,128)(2,1)S(1)} %collective-permute-done.20.refs_1_, ...), custom_call_target="tpu_custom_call" | custom-call | flops 1845493760 | bytes 11534336 | tf_op jit(solution)/shard_map/pallas_call | solution.py:158
  85.9 4.3 %collective-permute-done.22 = bf16[64,2048]{1,0:T(8,128)(2,1)S(1)} collective-permute-done((bf16[64,2048]{1,0:T(8,128)(2,1)S(1)}, bf16[64,2048]{1,0:T(8,128)(2,1)S(1)}, u32[]{:S(2)}, u32[]{:S(2)}) %collective-permute-start.22) | collective-permute-done | bytes 262176 | tf_op jit(solution)/shard_map/ppermute | solution.py:236
  90.2 0.5 collective-permute-start.28
  90.9 1.4 %collective-permute-start.26 = (bf16[64,2048]{1,0:T(8,128)(2,1)S(1)}, bf16[64,2048]{1,0:T(8,128)(2,1)S(1)}, u32[]{:S(2)}, u32[]{:S(2)}) collective-permute-start(bf16[64,2048]{1,0:T(8,128)(2,1)S(1)} %add_convert_fusion.7), channel_id=1, source_target_pairs={{0,8},{1,9},{2,10},{3,11},{4,12},{5,13},{6,14},{7,15},{8,0},{9,1},... | collective-permute-start | bytes 786440 | tf_op jit(solution)/shard_map/ppermute | solution.py:236
  92.3 1.5 %collective-permute-start.27 = (bf16[64,2048]{1,0:T(8,128)(2,1)S(1)}, bf16[64,2048]{1,0:T(8,128)(2,1)S(1)}, u32[]{:S(2)}, u32[]{:S(2)}) collective-permute-start(bf16[64,2048]{1,0:T(8,128)(2,1)S(1)} %add_convert_fusion.10), channel_id=1, source_target_pairs={{0,4},{1,5},{2,6},{3,7},{4,0},{5,1},{6,2},{7,3},{8,12},{9,13},{10,... | collective-permute-start | bytes 786440 | tf_op jit(solution)/shard_map/ppermute | solution.py:236
  93.9 0.8 collective-permute-start.24
  94.6 1.3 collective-permute-start.25
  96.1 10.0 %collective-permute-done.26.far_high = bf16[64,2048]{1,0:T(8,128)(2,1)S(1)} collective-permute-done((bf16[64,2048]{1,0:T(8,128)(2,1)S(1)}, bf16[64,2048]{1,0:T(8,128)(2,1)S(1)}, u32[]{:S(2)}, u32[]{:S(2)}) %collective-permute-start.26) | collective-permute-done | bytes 262176 | tf_op jit(solution)/shard_map/ppermute | solution.py:236
  106.3 1.4 %collective-permute-done.25 = bf16[64,2048]{1,0:T(8,128)(2,1)S(1)} collective-permute-done((bf16[64,2048]{1,0:T(8,128)(2,1)S(1)}, bf16[64,2048]{1,0:T(8,128)(2,1)S(1)}, u32[]{:S(2)}, u32[]{:S(2)}) %collective-permute-start.25) | collective-permute-done | bytes 262176 | tf_op jit(solution)/shard_map/ppermute | solution.py:236
  108.0 0.6 collective-permute-start.30
  108.5 1.6 %collective-permute-start.31 = (bf16[64,2048]{1,0:T(8,128)(2,1)S(1)}, bf16[64,2048]{1,0:T(8,128)(2,1)S(1)}, u32[]{:S(2)}, u32[]{:S(2)}) collective-permute-start(bf16[64,2048]{1,0:T(8,128)(2,1)S(1)} %get-tuple-element.150), channel_id=1, source_target_pairs={{0,4},{1,5},{2,6},{3,7},{4,0},{5,1},{6,2},{7,3},{8,12},{9,13},{10,... | collective-permute-start | bytes 786440 | tf_op jit(solution)/shard_map/ppermute | solution.py:236
  110.2 0.8 collective-permute-start.32
  111.0 1.3 collective-permute-start.33
  112.3 3.1 %shard_map.84 = f32[768,768]{1,0:T(8,128)} custom-call(f32[16,512]{1,0:T(8,128)S(1)} %shard_map.78.tables, bf16[320,768]{1,0:T(8,128)(2,1)S(1)} %copy-done.21, bf16[320,768]{1,0:T(8,128)(2,1)S(1)} %get-tuple-element.132.refs_1_, bf16[320,768]{1,0:T(8,128)(2,1)S(1)} %get-tuple-element.133.refs_2_, bf16[160,768]{1,0:T(8,128)(2,1)S(1)} %get-tuple-element.134.refs_3_, ...), custom_call_target="tpu_custom_call" | custom-call | flops 1509949440 | bytes 4325376 | tf_op jit(solution)/shard_map/pallas_call | solution.py:189
  115.5 6.3 %collective-permute-done.30 = bf16[64,2048]{1,0:T(8,128)(2,1)S(1)} collective-permute-done((bf16[64,2048]{1,0:T(8,128)(2,1)S(1)}, bf16[64,2048]{1,0:T(8,128)(2,1)S(1)}, u32[]{:S(2)}, u32[]{:S(2)}) %collective-permute-start.30) | collective-permute-done | bytes 262176 | tf_op jit(solution)/shard_map/ppermute | solution.py:236
  121.8 0.9 collective-permute-done.33
  122.9 1.3 collective-permute-start.34
  124.2 0.7 collective-permute-start.36
  125.0 1.6 %collective-permute-start.35 = (bf16[64,2048]{1,0:T(8,128)(2,1)S(1)}, bf16[64,2048]{1,0:T(8,128)(2,1)S(1)}, u32[]{:S(2)}, u32[]{:S(2)}) collective-permute-start(bf16[64,2048]{1,0:T(8,128)(2,1)S(1)} %add_convert_fusion.1), channel_id=1, source_target_pairs={{0,4},{1,5},{2,6},{3,7},{4,0},{5,1},{6,2},{7,3},{8,12},{9,13},{10,... | collective-permute-start | bytes 786440 | tf_op jit(solution)/shard_map/ppermute | solution.py:236
  126.6 9.1 %collective-permute-done.34.far_low = bf16[64,2048]{1,0:T(8,128)(2,1)S(1)} collective-permute-done((bf16[64,2048]{1,0:T(8,128)(2,1)S(1)}, bf16[64,2048]{1,0:T(8,128)(2,1)S(1)}, u32[]{:S(2)}, u32[]{:S(2)}) %collective-permute-start.34) | collective-permute-done | bytes 262176 | tf_op jit(solution)/shard_map/ppermute | solution.py:236
  135.7 0.9 collective-permute-done.35.near_high
  136.6 1.1 shard_map.85
  (76 shorter events, 2.5 us)
Async XLA Ops:
  0.6 24.1 %collective-permute-start = (bf16[128,2048]{1,0:T(8,128)(2,1)}, bf16[128,2048]{1,0:T(8,128)(2,1)}, u32[]{:S(2)}, u32[]{:S(2)}) collective-permute-start(bf16[128,2048]{1,0:T(8,128)(2,1)} %refs_0_.1), channel_id=1, source_target_pairs={{0,4},{1,5},{2,6},{3,7},{4,0},{5,1},{6,2},{7,3},{8,12},{9,13},{10,... | collective-permute-start | bytes 1572872 | tf_op jit(solution)/shard_map/ppermute | solution.py:236
  3.7 21.0 %collective-permute-start.1 = (bf16[128,2048]{1,0:T(8,128)(2,1)}, bf16[128,2048]{1,0:T(8,128)(2,1)}, u32[]{:S(2)}, u32[]{:S(2)}) collective-permute-start(bf16[128,2048]{1,0:T(8,128)(2,1)} %refs_0_.1), channel_id=1, source_target_pairs={{0,8},{2,10},{4,12},{6,14},{8,0},{10,2},{12,4},{14,6},{16,24},{18,... | collective-permute-start | bytes 1572872 | tf_op jit(solution)/shard_map/ppermute | solution.py:260
  8.2 16.5 %collective-permute-start.2 = (bf16[128,2048]{1,0:T(8,128)(2,1)}, bf16[128,2048]{1,0:T(8,128)(2,1)S(1)}, u32[]{:S(2)}, u32[]{:S(2)}) collective-permute-start(bf16[128,2048]{1,0:T(8,128)(2,1)} %refs_0_.1), channel_id=1, source_target_pairs={{0,2},{1,3},{2,0},{3,1},{4,6},{5,7},{6,4},{7,5},{8,10},{9,11},{10,... | collective-permute-start | bytes 1572872 | tf_op jit(solution)/shard_map/ppermute | solution.py:236
  9.8 14.9 %collective-permute-start.3 = (bf16[128,2048]{1,0:T(8,128)(2,1)}, bf16[128,2048]{1,0:T(8,128)(2,1)S(1)}, u32[]{:S(2)}, u32[]{:S(2)}) collective-permute-start(bf16[128,2048]{1,0:T(8,128)(2,1)} %refs_0_.1), channel_id=1, source_target_pairs={{0,1},{1,0},{2,3},{3,2},{4,5},{5,4},{6,7},{7,6},{8,9},{9,8},{10,11... | collective-permute-start | bytes 1572872 | tf_op jit(solution)/shard_map/ppermute | solution.py:236
  9.8 0.7 copy-start.9
  10.5 0.7 copy-start.10
  24.7 0.8 copy-start.16
  25.5 4.7 %collective-permute-start.7 = (bf16[128,2048]{1,0:T(8,128)(2,1)S(1)}, bf16[128,2048]{1,0:T(8,128)(2,1)S(1)}, u32[]{:S(2)}, u32[]{:S(2)}) collective-permute-start(bf16[128,2048]{1,0:T(8,128)(2,1)S(1)} %collective-permute-done.2.refs_1_), channel_id=1, source_target_pairs={{0,1},{1,0},{2,3},{3,2},{4,5},{5,4},{6,7},{7,6},{8,9},{9,8},{10,11... | collective-permute-start | bytes 1572872 | tf_op jit(solution)/shard_map/ppermute | solution.py:236
  25.5 0.8 copy-start.14
  26.3 22.8 %collective-permute-start.4 = (bf16[128,2048]{1,0:T(8,128)(2,1)}, bf16[128,2048]{1,0:T(8,128)(2,1)}, u32[]{:S(2)}, u32[]{:S(2)}) collective-permute-start(bf16[128,2048]{1,0:T(8,128)(2,1)} %refs_0_.1), channel_id=1, source_target_pairs={{1,9},{3,11},{5,13},{7,15},{9,1},{11,3},{13,5},{15,7},{17,25},{19,... | collective-permute-start | bytes 1572872 | tf_op jit(solution)/shard_map/ppermute | solution.py:260
  27.8 21.3 %collective-permute-start.5 = (bf16[128,2048]{1,0:T(8,128)(2,1)}, bf16[128,2048]{1,0:T(8,128)(2,1)}, u32[]{:S(2)}, u32[]{:S(2)}) collective-permute-start(bf16[128,2048]{1,0:T(8,128)(2,1)} %collective-permute-done.refs_0_), channel_id=1, source_target_pairs={{0,2},{1,3},{2,0},{3,1},{4,6},{5,7},{6,4},{7,5},{8,10},{9,11},{10,... | collective-permute-start | bytes 1572872 | tf_op jit(solution)/shard_map/ppermute | solution.py:236
  28.3 20.8 %collective-permute-start.6 = (bf16[128,2048]{1,0:T(8,128)(2,1)}, bf16[128,2048]{1,0:T(8,128)(2,1)}, u32[]{:S(2)}, u32[]{:S(2)}) collective-permute-start(bf16[128,2048]{1,0:T(8,128)(2,1)} %collective-permute-done.refs_0_), channel_id=1, source_target_pairs={{0,1},{1,0},{2,3},{3,2},{4,5},{5,4},{6,7},{7,6},{8,9},{9,8},{10,11... | collective-permute-start | bytes 1572872 | tf_op jit(solution)/shard_map/ppermute | solution.py:236
  30.2 0.8 copy-start.18
  31.0 1.9 %copy-start = (bf16[1,2048,768]{2,1,0:T(8,128)(2,1)S(1)}, bf16[1,2048,768]{2,1,0:T(8,128)(2,1)}, u32[]{:S(2)}) copy-start(bf16[1,2048,768]{2,1,0:T(8,128)(2,1)} %param.9) | copy-start | bytes 9437188
  32.9 1.9 %copy-start.2 = (bf16[1,2048,768]{2,1,0:T(8,128)(2,1)S(1)}, bf16[1,2048,768]{2,1,0:T(8,128)(2,1)}, u32[]{:S(2)}) copy-start(bf16[1,2048,768]{2,1,0:T(8,128)(2,1)} %param.10) | copy-start | bytes 9437188
  34.8 1.9 %copy-start.5 = (bf16[1,768,2048]{2,1,0:T(8,128)(2,1)S(1)}, bf16[1,768,2048]{2,1,0:T(8,128)(2,1)}, u32[]{:S(2)}) copy-start(bf16[1,768,2048]{2,1,0:T(8,128)(2,1)} %param.11) | copy-start | bytes 9437188
  36.7 1.0 copy-start.13
  37.8 1.0 copy-start.15
  38.8 1.0 copy-start.17
  39.8 1.0 copy-start.19
  40.9 12.7 %copy-start.1 = (bf16[1,2048,768]{2,1,0:T(8,128)(2,1)S(1)}, bf16[1,2048,768]{2,1,0:T(8,128)(2,1)}, u32[]{:S(2)}) copy-start(bf16[1,2048,768]{2,1,0:T(8,128)(2,1)} %param.9) | copy-start | bytes 9437188
  46.4 1.0 copy-start.7
  47.4 1.0 copy-start.11
  48.3 0.8 copy-start.20
  49.1 4.4 %collective-permute-start.11 = (bf16[128,2048]{1,0:T(8,128)(2,1)}, bf16[128,2048]{1,0:T(8,128)(2,1)}, u32[]{:S(2)}, u32[]{:S(2)}) collective-permute-start(bf16[128,2048]{1,0:T(8,128)(2,1)} %collective-permute-done.5.refs_1_), channel_id=1, source_target_pairs={{0,1},{1,0},{2,3},{3,2},{4,5},{5,4},{6,7},{7,6},{8,9},{9,8},{10,11... | collective-permute-start | bytes 1572872 | tf_op jit(solution)/shard_map/ppermute | solution.py:236
  49.2 17.7 %copy-start.12 = (bf16[256,2048]{1,0:T(8,128)(2,1)S(1)}, bf16[256,2048]{1,0:T(8,128)(2,1)}, u32[]{:S(2)}) copy-start(bf16[256,2048]{1,0:T(8,128)(2,1)} %copy-done.11) | copy-start | bytes 3145732
  50.4 14.6 %collective-permute-start.8 = (bf16[128,2048]{1,0:T(8,128)(2,1)S(1)}, bf16[128,2048]{1,0:T(8,128)(2,1)S(1)}, u32[]{:S(2)}, u32[]{:S(2)}) collective-permute-start(bf16[128,2048]{1,0:T(8,128)(2,1)S(1)} %broadcast_select_fusion.refs_0_), channel_id=1, source_target_pairs={{0,4},{1,5},{2,6},{3,7},{4,0},{5,1},{6,2},{7,3},{8,12},{9,13},{10,... | collective-permute-start | bytes 1572872 | tf_op jit(solution)/shard_map/ppermute | solution.py:236
  52.2 14.0 %collective-permute-start.9 = (bf16[128,2048]{1,0:T(8,128)(2,1)S(1)}, bf16[128,2048]{1,0:T(8,128)(2,1)S(1)}, u32[]{:S(2)}, u32[]{:S(2)}) collective-permute-start(bf16[128,2048]{1,0:T(8,128)(2,1)S(1)} %broadcast_select_fusion.refs_0_), channel_id=1, source_target_pairs={{0,2},{1,3},{2,0},{3,1},{4,6},{5,7},{6,4},{7,5},{8,10},{9,11},{10,... | collective-permute-start | bytes 1572872 | tf_op jit(solution)/shard_map/ppermute | solution.py:236
  53.5 12.7 %collective-permute-start.10 = (bf16[128,2048]{1,0:T(8,128)(2,1)S(1)}, bf16[128,2048]{1,0:T(8,128)(2,1)S(1)}, u32[]{:S(2)}, u32[]{:S(2)}) collective-permute-start(bf16[128,2048]{1,0:T(8,128)(2,1)S(1)} %broadcast_select_fusion.refs_0_), channel_id=1, source_target_pairs={{0,1},{1,0},{2,3},{3,2},{4,5},{5,4},{6,7},{7,6},{8,9},{9,8},{10,11... | collective-permute-start | bytes 1572872 | tf_op jit(solution)/shard_map/ppermute | solution.py:236
  53.6 1.9 %copy-start.3 = (bf16[1,2048,768]{2,1,0:T(8,128)(2,1)S(1)}, bf16[1,2048,768]{2,1,0:T(8,128)(2,1)}, u32[]{:S(2)}) copy-start(bf16[1,2048,768]{2,1,0:T(8,128)(2,1)} %param.10) | copy-start | bytes 9437188
  55.4 1.9 %copy-start.6 = (bf16[1,768,2048]{2,1,0:T(8,128)(2,1)S(1)}, bf16[1,768,2048]{2,1,0:T(8,128)(2,1)}, u32[]{:S(2)}) copy-start(bf16[1,768,2048]{2,1,0:T(8,128)(2,1)} %param.11) | copy-start | bytes 9437188
  57.3 11.6 %copy-start.4 = (bf16[1,2048,768]{2,1,0:T(8,128)(2,1)S(1)}, bf16[1,2048,768]{2,1,0:T(8,128)(2,1)}, u32[]{:S(2)}) copy-start(bf16[1,2048,768]{2,1,0:T(8,128)(2,1)} %param.10) | copy-start | bytes 9437188
  64.5 2.1 %collective-permute-start.12 = (bf16[128,2048]{1,0:T(8,128)(2,1)S(1)}, bf16[128,2048]{1,0:T(8,128)(2,1)S(1)}, u32[]{:S(2)}, u32[]{:S(2)}) collective-permute-start(bf16[128,2048]{1,0:T(8,128)(2,1)S(1)} %get-tuple-element.90), channel_id=1, source_target_pairs={{0,1},{1,0},{2,3},{3,2},{4,5},{5,4},{6,7},{7,6},{8,9},{9,8},{10,11... | collective-permute-start | bytes 1572872 | tf_op jit(solution)/shard_map/ppermute | solution.py:236
  66.6 2.1 %collective-permute-start.17 = (bf16[128,2048]{1,0:T(8,128)(2,1)S(1)}, bf16[128,2048]{1,0:T(8,128)(2,1)S(1)}, u32[]{:S(2)}, u32[]{:S(2)}) collective-permute-start(bf16[128,2048]{1,0:T(8,128)(2,1)S(1)} %collective-permute-done.9.refs_1_), channel_id=1, source_target_pairs={{0,1},{1,0},{2,3},{3,2},{4,5},{5,4},{6,7},{7,6},{8,9},{9,8},{10,11... | collective-permute-start | bytes 1572872 | tf_op jit(solution)/shard_map/ppermute | solution.py:236
  67.0 10.7 %collective-permute-start.15 = (bf16[256,2048]{1,0:T(8,128)(2,1)S(1)}, bf16[256,2048]{1,0:T(8,128)(2,1)S(1)}, u32[]{:S(2)}, u32[]{:S(2)}) collective-permute-start(bf16[256,2048]{1,0:T(8,128)(2,1)S(1)} %copy-done.12), channel_id=1, source_target_pairs={{0,1},{1,0},{2,3},{3,2},{4,5},{5,4},{6,7},{7,6},{8,9},{9,8},{10,11... | collective-permute-start | bytes 3145736 | tf_op jit(solution)/shard_map/ppermute | solution.py:236
  67.1 14.2 %collective-permute-start.13 = (bf16[128,2048]{1,0:T(8,128)(2,1)S(1)}, bf16[128,2048]{1,0:T(8,128)(2,1)S(1)}, u32[]{:S(2)}, u32[]{:S(2)}) collective-permute-start(bf16[128,2048]{1,0:T(8,128)(2,1)S(1)} %collective-permute-done.9.refs_1_), channel_id=1, source_target_pairs={{0,4},{1,5},{2,6},{3,7},{4,0},{5,1},{6,2},{7,3},{8,12},{9,13},{10,... | collective-permute-start | bytes 1572872 | tf_op jit(solution)/shard_map/ppermute | solution.py:236
  67.5 7.1 %collective-permute-start.19 = (bf16[128,2048]{1,0:T(8,128)(2,1)S(1)}, bf16[128,2048]{1,0:T(8,128)(2,1)S(1)}, u32[]{:S(2)}, u32[]{:S(2)}) collective-permute-start(bf16[128,2048]{1,0:T(8,128)(2,1)S(1)} %collective-permute-done.8.refs_0_), channel_id=1, source_target_pairs={{0,1},{1,0},{2,3},{3,2},{4,5},{5,4},{6,7},{7,6},{8,9},{9,8},{10,11... | collective-permute-start | bytes 1572872 | tf_op jit(solution)/shard_map/ppermute | solution.py:236
  67.7 10.0 %collective-permute-start.14 = (bf16[64,2048]{1,0:T(8,128)(2,1)S(1)}, bf16[64,2048]{1,0:T(8,128)(2,1)S(1)}, u32[]{:S(2)}, u32[]{:S(2)}) collective-permute-start(bf16[64,2048]{1,0:T(8,128)(2,1)S(1)} %get-tuple-element.149), channel_id=1, source_target_pairs={{0,2},{1,3},{2,0},{3,1},{4,6},{5,7},{6,4},{7,5},{8,10},{9,11},{10,... | collective-permute-start | bytes 786440 | tf_op jit(solution)/shard_map/ppermute | solution.py:236
  68.7 12.6 %collective-permute-start.16 = (bf16[128,2048]{1,0:T(8,128)(2,1)S(1)}, bf16[128,2048]{1,0:T(8,128)(2,1)S(1)}, u32[]{:S(2)}, u32[]{:S(2)}) collective-permute-start(bf16[128,2048]{1,0:T(8,128)(2,1)S(1)} %get-tuple-element.95), channel_id=1, source_target_pairs={{0,1},{1,0},{2,3},{3,2},{4,5},{5,4},{6,7},{7,6},{8,9},{9,8},{10,11... | collective-permute-start | bytes 1572872 | tf_op jit(solution)/shard_map/ppermute | solution.py:236
  74.6 6.7 %collective-permute-start.18 = (bf16[64,2048]{1,0:T(8,128)(2,1)S(1)}, bf16[64,2048]{1,0:T(8,128)(2,1)S(1)}, u32[]{:S(2)}, u32[]{:S(2)}) collective-permute-start(bf16[64,2048]{1,0:T(8,128)(2,1)S(1)} %get-tuple-element.97), channel_id=1, source_target_pairs={{0,1},{1,0},{2,3},{3,2},{4,5},{5,4},{6,7},{7,6},{8,9},{9,8},{10,11... | collective-permute-start | bytes 786440 | tf_op jit(solution)/shard_map/ppermute | solution.py:236
  81.3 1.9 %collective-permute-start.20 = (bf16[128,2048]{1,0:T(8,128)(2,1)S(1)}, bf16[128,2048]{1,0:T(8,128)(2,1)S(1)}, u32[]{:S(2)}, u32[]{:S(2)}) collective-permute-start(bf16[128,2048]{1,0:T(8,128)(2,1)S(1)} %collective-permute-done.13.refs_0_), channel_id=1, source_target_pairs={{0,1},{1,0},{2,3},{3,2},{4,5},{5,4},{6,7},{7,6},{8,9},{9,8},{10,11... | collective-permute-start | bytes 1572872 | tf_op jit(solution)/shard_map/ppermute | solution.py:236
  81.3 8.9 %collective-permute-start.21 = (bf16[128,2048]{1,0:T(8,128)(2,1)S(1)}, bf16[128,2048]{1,0:T(8,128)(2,1)S(1)}, u32[]{:S(2)}, u32[]{:S(2)}) collective-permute-start(bf16[128,2048]{1,0:T(8,128)(2,1)S(1)} %get-tuple-element.111), channel_id=1, source_target_pairs={{0,1},{1,0},{2,3},{3,2},{4,5},{5,4},{6,7},{7,6},{8,9},{9,8},{10,11... | collective-permute-start | bytes 1572872 | tf_op jit(solution)/shard_map/ppermute | solution.py:236
  81.9 8.3 %collective-permute-start.22 = (bf16[64,2048]{1,0:T(8,128)(2,1)S(1)}, bf16[64,2048]{1,0:T(8,128)(2,1)S(1)}, u32[]{:S(2)}, u32[]{:S(2)}) collective-permute-start(bf16[64,2048]{1,0:T(8,128)(2,1)S(1)} %add_convert_fusion.11), channel_id=1, source_target_pairs={{0,2},{1,3},{2,0},{3,1},{4,6},{5,7},{6,4},{7,5},{8,10},{9,11},{10,... | collective-permute-start | bytes 786440 | tf_op jit(solution)/shard_map/ppermute | solution.py:236
  82.7 13.2 %copy-start.8 = (bf16[256,2048]{1,0:T(8,128)(2,1)S(1)}, bf16[256,2048]{1,0:T(8,128)(2,1)}, u32[]{:S(2)}) copy-start(bf16[256,2048]{1,0:T(8,128)(2,1)} %copy-done.7) | copy-start | bytes 3145732
  90.2 3.5 %collective-permute-start.23 = (bf16[128,2048]{1,0:T(8,128)(2,1)S(1)}, bf16[128,2048]{1,0:T(8,128)(2,1)S(1)}, u32[]{:S(2)}, u32[]{:S(2)}) collective-permute-start(bf16[128,2048]{1,0:T(8,128)(2,1)S(1)} %get-tuple-element.117), channel_id=1, source_target_pairs={{0,1},{1,0},{2,3},{3,2},{4,5},{5,4},{6,7},{7,6},{8,9},{9,8},{10,11... | collective-permute-start | bytes 1572872 | tf_op jit(solution)/shard_map/ppermute | solution.py:236
  90.2 4.4 %collective-permute-start.28 = (bf16[64,2048]{1,0:T(8,128)(2,1)S(1)}, bf16[64,2048]{1,0:T(8,128)(2,1)S(1)}, u32[]{:S(2)}, u32[]{:S(2)}) collective-permute-start(bf16[64,2048]{1,0:T(8,128)(2,1)S(1)} %get-tuple-element.123), channel_id=1, source_target_pairs={{0,1},{1,0},{2,3},{3,2},{4,5},{5,4},{6,7},{7,6},{8,9},{9,8},{10,11... | collective-permute-start | bytes 786440 | tf_op jit(solution)/shard_map/ppermute | solution.py:236
  90.7 5.4 %collective-permute-start.29 = (bf16[128,2048]{1,0:T(8,128)(2,1)S(1)}, bf16[128,2048]{1,0:T(8,128)(2,1)S(1)}, u32[]{:S(2)}, u32[]{:S(2)}) collective-permute-start(bf16[128,2048]{1,0:T(8,128)(2,1)S(1)} %get-tuple-element.124), channel_id=1, source_target_pairs={{0,1},{1,0},{2,3},{3,2},{4,5},{5,4},{6,7},{7,6},{8,9},{9,8},{10,11... | collective-permute-start | bytes 1572872 | tf_op jit(solution)/shard_map/ppermute | solution.py:236
  90.9 21.5 %copy-start.21 = (bf16[320,768]{1,0:T(8,128)(2,1)S(1)}, bf16[320,768]{1,0:T(8,128)(2,1)}, u32[]{:S(2)}) copy-start(bf16[320,768]{1,0:T(8,128)(2,1)} %copy-done.20) | copy-start | bytes 1474564
  90.9 15.3 %collective-permute-start.26 = (bf16[64,2048]{1,0:T(8,128)(2,1)S(1)}, bf16[64,2048]{1,0:T(8,128)(2,1)S(1)}, u32[]{:S(2)}, u32[]{:S(2)}) collective-permute-start(bf16[64,2048]{1,0:T(8,128)(2,1)S(1)} %add_convert_fusion.7), channel_id=1, source_target_pairs={{0,8},{1,9},{2,10},{3,11},{4,12},{5,13},{6,14},{7,15},{8,0},{9,1},... | collective-permute-start | bytes 786440 | tf_op jit(solution)/shard_map/ppermute | solution.py:236
  92.3 14.0 %collective-permute-start.27 = (bf16[64,2048]{1,0:T(8,128)(2,1)S(1)}, bf16[64,2048]{1,0:T(8,128)(2,1)S(1)}, u32[]{:S(2)}, u32[]{:S(2)}) collective-permute-start(bf16[64,2048]{1,0:T(8,128)(2,1)S(1)} %add_convert_fusion.10), channel_id=1, source_target_pairs={{0,4},{1,5},{2,6},{3,7},{4,0},{5,1},{6,2},{7,3},{8,12},{9,13},{10,... | collective-permute-start | bytes 786440 | tf_op jit(solution)/shard_map/ppermute | solution.py:236
  93.9 12.4 %collective-permute-start.24 = (bf16[64,2048]{1,0:T(8,128)(2,1)S(1)}, bf16[64,2048]{1,0:T(8,128)(2,1)S(1)}, u32[]{:S(2)}, u32[]{:S(2)}) collective-permute-start(bf16[64,2048]{1,0:T(8,128)(2,1)S(1)} %get-tuple-element.153), channel_id=1, source_target_pairs={{0,2},{1,3},{2,0},{3,1},{4,6},{5,7},{6,4},{7,5},{8,10},{9,11},{10,... | collective-permute-start | bytes 786440 | tf_op jit(solution)/shard_map/ppermute | solution.py:236
  94.6 13.1 %collective-permute-start.25 = (bf16[64,2048]{1,0:T(8,128)(2,1)S(1)}, bf16[64,2048]{1,0:T(8,128)(2,1)S(1)}, u32[]{:S(2)}, u32[]{:S(2)}) collective-permute-start(bf16[64,2048]{1,0:T(8,128)(2,1)S(1)} %get-tuple-element.152), channel_id=1, source_target_pairs={{0,2},{1,3},{2,0},{3,1},{4,6},{5,7},{6,4},{7,5},{8,10},{9,11},{10,... | collective-permute-start | bytes 786440 | tf_op jit(solution)/shard_map/ppermute | solution.py:236
  108.0 13.8 %collective-permute-start.30 = (bf16[64,2048]{1,0:T(8,128)(2,1)S(1)}, bf16[64,2048]{1,0:T(8,128)(2,1)S(1)}, u32[]{:S(2)}, u32[]{:S(2)}) collective-permute-start(bf16[64,2048]{1,0:T(8,128)(2,1)S(1)} %get-tuple-element.151), channel_id=1, source_target_pairs={{0,8},{1,9},{2,10},{3,11},{4,12},{5,13},{6,14},{7,15},{8,0},{9,1},... | collective-permute-start | bytes 786440 | tf_op jit(solution)/shard_map/ppermute | solution.py:236
  108.5 13.2 %collective-permute-start.31 = (bf16[64,2048]{1,0:T(8,128)(2,1)S(1)}, bf16[64,2048]{1,0:T(8,128)(2,1)S(1)}, u32[]{:S(2)}, u32[]{:S(2)}) collective-permute-start(bf16[64,2048]{1,0:T(8,128)(2,1)S(1)} %get-tuple-element.150), channel_id=1, source_target_pairs={{0,4},{1,5},{2,6},{3,7},{4,0},{5,1},{6,2},{7,3},{8,12},{9,13},{10,... | collective-permute-start | bytes 786440 | tf_op jit(solution)/shard_map/ppermute | solution.py:236
  110.2 11.6 %collective-permute-start.32 = (bf16[64,2048]{1,0:T(8,128)(2,1)S(1)}, bf16[64,2048]{1,0:T(8,128)(2,1)S(1)}, u32[]{:S(2)}, u32[]{:S(2)}) collective-permute-start(bf16[64,2048]{1,0:T(8,128)(2,1)S(1)} %add_convert_fusion.3), channel_id=1, source_target_pairs={{0,2},{1,3},{2,0},{3,1},{4,6},{5,7},{6,4},{7,5},{8,10},{9,11},{10,... | collective-permute-start | bytes 786440 | tf_op jit(solution)/shard_map/ppermute | solution.py:236
  111.0 11.7 %collective-permute-start.33 = (bf16[64,2048]{1,0:T(8,128)(2,1)S(1)}, bf16[64,2048]{1,0:T(8,128)(2,1)S(1)}, u32[]{:S(2)}, u32[]{:S(2)}) collective-permute-start(bf16[64,2048]{1,0:T(8,128)(2,1)S(1)} %get-tuple-element.129), channel_id=1, source_target_pairs={{0,2},{1,3},{2,0},{3,1},{4,6},{5,7},{6,4},{7,5},{8,10},{9,11},{10,... | collective-permute-start | bytes 786440 | tf_op jit(solution)/shard_map/ppermute | solution.py:236
  122.9 12.8 %collective-permute-start.34 = (bf16[64,2048]{1,0:T(8,128)(2,1)S(1)}, bf16[64,2048]{1,0:T(8,128)(2,1)S(1)}, u32[]{:S(2)}, u32[]{:S(2)}) collective-permute-start(bf16[64,2048]{1,0:T(8,128)(2,1)S(1)} %add_convert_fusion.2), channel_id=1, source_target_pairs={{0,8},{1,9},{2,10},{3,11},{4,12},{5,13},{6,14},{7,15},{8,0},{9,1},... | collective-permute-start | bytes 786440 | tf_op jit(solution)/shard_map/ppermute | solution.py:236
  124.2 12.4 %collective-permute-start.36 = (bf16[128,2048]{1,0:T(8,128)(2,1)S(1)}, bf16[128,2048]{1,0:T(8,128)(2,1)S(1)}, u32[]{:S(2)}, u32[]{:S(2)}) collective-permute-start(bf16[128,2048]{1,0:T(8,128)(2,1)S(1)} %add_convert_fusion), channel_id=1, source_target_pairs={{0,2},{1,3},{2,0},{3,1},{4,6},{5,7},{6,4},{7,5},{8,10},{9,11},{10,... | collective-permute-start | bytes 1572872 | tf_op jit(solution)/shard_map/ppermute | solution.py:236
  125.0 11.6 %collective-permute-start.35 = (bf16[64,2048]{1,0:T(8,128)(2,1)S(1)}, bf16[64,2048]{1,0:T(8,128)(2,1)S(1)}, u32[]{:S(2)}, u32[]{:S(2)}) collective-permute-start(bf16[64,2048]{1,0:T(8,128)(2,1)S(1)} %add_convert_fusion.1), channel_id=1, source_target_pairs={{0,4},{1,5},{2,6},{3,7},{4,0},{5,1},{6,2},{7,3},{8,12},{9,13},{10,... | collective-permute-start | bytes 786440 | tf_op jit(solution)/shard_map/ppermute | solution.py:236

commit v24 on v22

--- a/solution.py
+++ b/solution.py
@@ -325,15 +325,17 @@
 
     side_high = column(summed(keep2[tok + half :], got2_high))
     got2 = sibling(give2)
-    keep3_side, give3_side, act4 = expert(3, b3, d3, picked=(1, 3))
-    keep3_side, give3_side, act4, got2, side_high, near1 = together(
-        keep3_side, give3_side, act4, got2, side_high, near1
+    keep3_side, give3_low, give3_high, act4 = expert(
+        3, b3, d3, pieces=(half, half), picked=(1, 3)
+    )
+    got3_low, got3_high = sibling(give3_low), sibling(give3_high)
+    keep3_side, got3_low, got3_high, act4, got2, side_high, near1 = together(
+        keep3_side, got3_low, got3_high, act4, got2, side_high, near1
     )
     got2_low, got3 = sibling(give2_low), sibling(give3)
     far2_high = far(summed(keep2[half:tok], got2[half:], side_high))
-    got3_side = sibling(give3_side)
-    came3_low = column(summed(keep3_side[:half], got3_side[:half]))
-    came3_high = column(summed(keep3_side[half:], got3_side[half:]))
+    came3_low = column(summed(keep3_side[:half], got3_low))
+    came3_high = column(summed(keep3_side[half:], got3_high))
     near1_low = pair(near1)
     side0 = summed(keep0[tok:], got0[tok:])
     side1 = summed(keep1[tok + half :], got1_side[half:])

time: 127 us -> 129 us (1.016)
  waiting for transfers between devices: 41.7 us -> 43.9 us
    ppermute x37 -> x38, waiting for transfers between devices: 41.7 us -> 43.9 us  [swapped(): return lax.ppermute(array, 'expert', [(i, i ^ bit) for i in range(size)])]
    ppermute x37 -> x38, starting transfers between devices: 31.2 us -> 30.8 us  [swapped(): return lax.ppermute(array, 'expert', [(i, i ^ bit) for i in range(size)])]
  transfers between devices with their start and end apart: 37 -> 38, of which waited for: 11 -> 12; matrix products, arithmetic and copies ran while one was open for 1% -> 1% of each run, Pallas kernels for 21% -> 20%
where the time goes in v24:
time: 129 us; the launch traced here: 128 us
  waiting for transfers between devices  43.9 us (34%)
  starting transfers between devices  30.8 us (24%)
  Pallas kernels  27.1 us (21%)
  blocking collectives  14.2 us (11%)
  local copies, waits for them, and re-layouts  9.97 us (8%)
    ppermute x38, waiting for transfers between devices, swapped(): return lax.ppermute(array, 'expert', [(i, i ^ bit) for i in range(size)])  43.9 us
    ppermute x38, starting transfers between devices, swapped(): return lax.ppermute(array, 'expert', [(i, i ^ bit) for i in range(size)])  30.8 us
    pallas_call x5, Pallas kernels, plane_pass(): pl.pallas_call(functools.partial(plane_kernel, k, picked, len(pieces)), o...  22 us
    all_to_all x1, blocking collectives, staged(): lax.all_to_all(mine, 'expert', split_axis=0, concat_axis=0, tiled=True)  14.2 us
    unnamed x25, local copies, waits for them, and re-layouts  9.86 us
    pallas_call x1, Pallas kernels, gram_pass(): pl.pallas_call(gram_kernel, out_shape=jax.ShapeDtypeStruct((hidden, hidde...  3.15 us
  transfers between devices with their start and end apart: 38, of which 12 were waited for; matrix products, arithmetic and copies ran while one was open for 1% of the time, Pallas kernels for 20%

profile of v24, /device:TPU:0, one launch (start us, length us, event | category | flops | bytes accessed | tf_op | source)
XLA Modules:
  0.0 128.1 jit_solution(10406007825566412798)
XLA Ops:
  0.6 3.1 %collective-permute-start = (bf16[128,2048]{1,0:T(8,128)(2,1)}, bf16[128,2048]{1,0:T(8,128)(2,1)S(1)}, u32[]{:S(2)}, u32[]{:S(2)}) collective-permute-start(bf16[128,2048]{1,0:T(8,128)(2,1)} %refs_0_.1), channel_id=1, source_target_pairs={{0,4},{1,5},{2,6},{3,7},{4,0},{5,1},{6,2},{7,3},{8,12},{9,13},{10,... | collective-permute-start | bytes 1572872 | tf_op jit(solution)/shard_map/ppermute | solution.py:256
  3.7 1.5 %collective-permute-start.2 = (bf16[128,2048]{1,0:T(8,128)(2,1)}, bf16[128,2048]{1,0:T(8,128)(2,1)S(1)}, u32[]{:S(2)}, u32[]{:S(2)}) collective-permute-start(bf16[128,2048]{1,0:T(8,128)(2,1)} %refs_0_.1), channel_id=1, source_target_pairs={{0,2},{1,3},{2,0},{3,1},{4,6},{5,7},{6,4},{7,5},{8,10},{9,11},{10,... | collective-permute-start | bytes 1572872 | tf_op jit(solution)/shard_map/ppermute | solution.py:256
  5.2 1.1 copy-done.6
  6.3 0.7 copy-done.8
  7.0 0.7 copy-done.9
  7.7 0.1 shard_map.77
  7.8 2.7 %collective-permute-start.1 = (bf16[64,2048]{1,0:T(8,128)(2,1)S(1)}, bf16[64,2048]{1,0:T(8,128)(2,1)S(1)}, u32[]{:S(2)}, u32[]{:S(2)}) collective-permute-start(bf16[64,2048]{1,0:T(8,128)(2,1)S(1)} %get-tuple-element.81), channel_id=1, source_target_pairs={{0,8},{1,9},{2,10},{3,11},{4,12},{5,13},{6,14},{7,15},{8,0},{9,1},... | collective-permute-start | bytes 786440 | tf_op jit(solution)/shard_map/ppermute | solution.py:256
  10.5 14.2 %all_to_all.12 = f32[16,1,128]{2,1,0:T(1,128)S(1)} all-to-all(f32[16,1,128]{2,1,0:T(1,128)S(1)} %bitcast.42), channel_id=1, replica_groups=mesh['parts'=2,'expert'=16] {'expert'}, dimensions={0} | all-to-all | bytes 16384 | tf_op jit(solution)/shard_map/all_to_all | solution.py:285
  24.8 0.7 copy-done.10
  25.4 0.5 collective-permute-start.5
  25.9 0.2 collective-permute-start.6
  26.3 1.1 collective-permute-start.4
  27.4 0.7 shard_map.78.tables
  28.2 1.9 %copy-done = bf16[1,2048,768]{2,1,0:T(8,128)(2,1)S(1)} copy-done((bf16[1,2048,768]{2,1,0:T(8,128)(2,1)S(1)}, bf16[1,2048,768]{2,1,0:T(8,128)(2,1)}, u32[]{:S(2)}) %copy-start) | copy-done | bytes 3145752
  30.0 1.9 %copy-done.2 = bf16[1,2048,768]{2,1,0:T(8,128)(2,1)S(1)} copy-done((bf16[1,2048,768]{2,1,0:T(8,128)(2,1)S(1)}, bf16[1,2048,768]{2,1,0:T(8,128)(2,1)}, u32[]{:S(2)}) %copy-start.2) | copy-done | bytes 3145752
  31.9 1.9 %copy-done.4 = bf16[1,768,2048]{2,1,0:T(8,128)(2,1)S(1)} copy-done((bf16[1,768,2048]{2,1,0:T(8,128)(2,1)S(1)}, bf16[1,768,2048]{2,1,0:T(8,128)(2,1)}, u32[]{:S(2)}) %copy-start.4) | copy-done | bytes 3145752
  33.8 1.0 copy-done.7
  34.9 5.5 %shard_map.79 = (bf16[256,2048]{1,0:T(8,128)(2,1)S(1)}, bf16[256,2048]{1,0:T(8,128)(2,1)S(1)}, bf16[320,768]{1,0:T(8,128)(2,1)S(1)}) custom-call(f32[16,512]{1,0:T(8,128)S(1)} %shard_map.78.tables, bf16[128,2048]{1,0:T(8,128)(2,1)S(1)} %copy-done.7, bf16[128,2048]{1,0:T(8,128)(2,1)S(1)} %collective-permute-done.2.refs_1_, ...), custom_call_target="tpu_custom_call" | custom-call | flops 4362076160 | bytes 13631488 | tf_op jit(solution)/shard_map/pallas_call | solution.py:178
  40.4 1.0 collective-permute-done.4
  41.4 0.7 collective-permute-start.8
  42.1 1.1 collective-permute-start.9
  43.3 5.5 %shard_map.80 = (bf16[256,2048]{1,0:T(8,128)(2,1)S(1)}, bf16[128,2048]{1,0:T(8,128)(2,1)S(1)}, bf16[128,2048]{1,0:T(8,128)(2,1)S(1)}, bf16[320,768]{1,0:T(8,128)(2,1)S(1)}) custom-call(f32[16,512]{1,0:T(8,128)S(1)} %shard_map.78.tables, bf16[128,2048]{1,0:T(8,128)(2,1)S(1)} %collective-permute-done.refs_0_, ...), custom_call_target="tpu_custom_call" | custom-call | flops 4362076160 | bytes 13631488 | tf_op jit(solution)/shard_map/pallas_call | solution.py:178
  48.7 0.5 collective-permute-start.12
  49.3 6.5 %collective-permute-done.8.refs_0_ = bf16[128,2048]{1,0:T(8,128)(2,1)S(1)} collective-permute-done((bf16[128,2048]{1,0:T(8,128)(2,1)S(1)}, bf16[128,2048]{1,0:T(8,128)(2,1)S(1)}, u32[]{:S(2)}, u32[]{:S(2)}) %collective-permute-start.8) | collective-permute-done | bytes 524320 | tf_op jit(solution)/shard_map/ppermute | solution.py:256
  55.8 0.3 collective-permute-done.9.refs_1_
  56.1 0.5 collective-permute-start.15
  56.6 1.4 %collective-permute-start.13 = (bf16[128,2048]{1,0:T(8,128)(2,1)S(1)}, bf16[128,2048]{1,0:T(8,128)(2,1)S(1)}, u32[]{:S(2)}, u32[]{:S(2)}) collective-permute-start(bf16[128,2048]{1,0:T(8,128)(2,1)S(1)} %collective-permute-done.9.refs_1_), channel_id=1, source_target_pairs={{0,4},{1,5},{2,6},{3,7},{4,0},{5,1},{6,2},{7,3},{8,12},{9,13},{10,... | collective-permute-start | bytes 1572872 | tf_op jit(solution)/shard_map/ppermute | solution.py:256
  58.1 0.1 add_convert_fusion.6
  58.2 1.5 %collective-permute-start.14 = (bf16[64,2048]{1,0:T(8,128)(2,1)S(1)}, bf16[64,2048]{1,0:T(8,128)(2,1)S(1)}, u32[]{:S(2)}, u32[]{:S(2)}) collective-permute-start(bf16[64,2048]{1,0:T(8,128)(2,1)S(1)} %get-tuple-element.161), channel_id=1, source_target_pairs={{0,2},{1,3},{2,0},{3,1},{4,6},{5,7},{6,4},{7,5},{8,10},{9,11},{10,... | collective-permute-start | bytes 786440 | tf_op jit(solution)/shard_map/ppermute | solution.py:256
  59.7 0.2 collective-permute-start.16
  60.0 5.7 %shard_map.81 = (bf16[256,2048]{1,0:T(8,128)(2,1)S(1)}, bf16[128,2048]{1,0:T(8,128)(2,1)S(1)}, bf16[64,2048]{1,0:T(8,128)(2,1)S(1)}, bf16[64,2048]{1,0:T(8,128)(2,1)S(1)}, bf16[320,768]{1,0:T(8,128)(2,1)S(1)}) custom-call(f32[16,512]{1,0:T(8,128)S(1)} %shard_map.78.tables, bf16[128,2048]{1,0:T(8,128)(2,1)S(1)} %constant_dynamic-update-slice_fusion.refs_0_, ...), custom_call_target="tpu_custom_call" | custom-call | flops 4362076160 | bytes 13631488 | tf_op jit(solution)/shard_map/pallas_call | solution.py:178
  65.6 0.3 collective-permute-start.18
  66.0 2.7 %shard_map.82 = (bf16[128,2048]{1,0:T(8,128)(2,1)S(1)}, bf16[128,2048]{1,0:T(8,128)(2,1)S(1)}, bf16[160,768]{1,0:T(8,128)(2,1)S(1)}) custom-call(f32[16,512]{1,0:T(8,128)S(1)} %shard_map.78.tables, bf16[128,2048]{1,0:T(8,128)(2,1)S(1)} %collective-permute-done.8.refs_0_, bf16[128,2048]{1,0:T(8,128)(2,1)S(1)} %collective-permute-done.19.refs_1_, ...), custom_call_target="tpu_custom_call" | custom-call | flops 1845493760 | bytes 11534336 | tf_op jit(solution)/shard_map/pallas_call | solution.py:178
  68.7 1.8 %collective-permute-done.13.refs_0_ = bf16[128,2048]{1,0:T(8,128)(2,1)S(1)} collective-permute-done((bf16[128,2048]{1,0:T(8,128)(2,1)S(1)}, bf16[128,2048]{1,0:T(8,128)(2,1)S(1)}, u32[]{:S(2)}, u32[]{:S(2)}) %collective-permute-start.13) | collective-permute-done | bytes 524320 | tf_op jit(solution)/shard_map/ppermute | solution.py:256
  70.5 0.5 collective-permute-start.23
  71.1 1.3 %collective-permute-start.24 = (bf16[64,2048]{1,0:T(8,128)(2,1)S(1)}, bf16[64,2048]{1,0:T(8,128)(2,1)S(1)}, u32[]{:S(2)}, u32[]{:S(2)}) collective-permute-start(bf16[64,2048]{1,0:T(8,128)(2,1)S(1)} %add_convert_fusion.11), channel_id=1, source_target_pairs={{0,2},{1,3},{2,0},{3,1},{4,6},{5,7},{6,4},{7,5},{8,10},{9,11},{10,... | collective-permute-start | bytes 786440 | tf_op jit(solution)/shard_map/ppermute | solution.py:256
  72.5 2.7 %shard_map.83 = (bf16[128,2048]{1,0:T(8,128)(2,1)S(1)}, bf16[64,2048]{1,0:T(8,128)(2,1)S(1)}, bf16[64,2048]{1,0:T(8,128)(2,1)S(1)}, bf16[160,768]{1,0:T(8,128)(2,1)S(1)}) custom-call(f32[16,512]{1,0:T(8,128)S(1)} %shard_map.78.tables, bf16[128,2048]{1,0:T(8,128)(2,1)S(1)} %collective-permute-done.13.refs_0_, ...), custom_call_target="tpu_custom_call" | custom-call | flops 1845493760 | bytes 11534336 | tf_op jit(solution)/shard_map/pallas_call | solution.py:178
  75.2 0.6 collective-permute-start.21
  75.9 3.5 %collective-permute-done.24 = bf16[64,2048]{1,0:T(8,128)(2,1)S(1)} collective-permute-done((bf16[64,2048]{1,0:T(8,128)(2,1)S(1)}, bf16[64,2048]{1,0:T(8,128)(2,1)S(1)}, u32[]{:S(2)}, u32[]{:S(2)}) %collective-permute-start.24) | collective-permute-done | bytes 262176 | tf_op jit(solution)/shard_map/ppermute | solution.py:256
  79.5 0.1 add_convert_fusion.8
  79.6 1.3 %collective-permute-start.25 = (bf16[64,2048]{1,0:T(8,128)(2,1)S(1)}, bf16[64,2048]{1,0:T(8,128)(2,1)S(1)}, u32[]{:S(2)}, u32[]{:S(2)}) collective-permute-start(bf16[64,2048]{1,0:T(8,128)(2,1)S(1)} %get-tuple-element.165), channel_id=1, source_target_pairs={{0,2},{1,3},{2,0},{3,1},{4,6},{5,7},{6,4},{7,5},{8,10},{9,11},{10,... | collective-permute-start | bytes 786440 | tf_op jit(solution)/shard_map/ppermute | solution.py:256
  81.0 0.8 collective-permute-start.26
  81.8 2.0 %collective-permute-start.27 = (bf16[64,2048]{1,0:T(8,128)(2,1)S(1)}, bf16[64,2048]{1,0:T(8,128)(2,1)S(1)}, u32[]{:S(2)}, u32[]{:S(2)}) collective-permute-start(bf16[64,2048]{1,0:T(8,128)(2,1)S(1)} %add_convert_fusion.7), channel_id=1, source_target_pairs={{0,8},{1,9},{2,10},{3,11},{4,12},{5,13},{6,14},{7,15},{8,0},{9,1},... | collective-permute-start | bytes 786440 | tf_op jit(solution)/shard_map/ppermute | solution.py:256
  83.8 0.5 collective-permute-start.28
  84.3 0.1 add_convert_fusion
  84.4 4.3 %collective-permute-done.25 = bf16[64,2048]{1,0:T(8,128)(2,1)S(1)} collective-permute-done((bf16[64,2048]{1,0:T(8,128)(2,1)S(1)}, bf16[64,2048]{1,0:T(8,128)(2,1)S(1)}, u32[]{:S(2)}, u32[]{:S(2)}) %collective-permute-start.25) | collective-permute-done | bytes 262176 | tf_op jit(solution)/shard_map/ppermute | solution.py:256
  88.8 5.2 %collective-permute-done.26 = bf16[64,2048]{1,0:T(8,128)(2,1)S(1)} collective-permute-done((bf16[64,2048]{1,0:T(8,128)(2,1)S(1)}, bf16[64,2048]{1,0:T(8,128)(2,1)S(1)}, u32[]{:S(2)}, u32[]{:S(2)}) %collective-permute-start.26) | collective-permute-done | bytes 262176 | tf_op jit(solution)/shard_map/ppermute | solution.py:256
  94.0 2.5 %collective-permute-done.27.far_high = bf16[64,2048]{1,0:T(8,128)(2,1)S(1)} collective-permute-done((bf16[64,2048]{1,0:T(8,128)(2,1)S(1)}, bf16[64,2048]{1,0:T(8,128)(2,1)S(1)}, u32[]{:S(2)}, u32[]{:S(2)}) %collective-permute-start.27) | collective-permute-done | bytes 262176 | tf_op jit(solution)/shard_map/ppermute | solution.py:256
  96.5 0.2 add_convert_fusion.4
  96.8 1.5 %collective-permute-start.31 = (bf16[64,2048]{1,0:T(8,128)(2,1)S(1)}, bf16[64,2048]{1,0:T(8,128)(2,1)S(1)}, u32[]{:S(2)}, u32[]{:S(2)}) collective-permute-start(bf16[64,2048]{1,0:T(8,128)(2,1)S(1)} %get-tuple-element.163), channel_id=1, source_target_pairs={{0,8},{1,9},{2,10},{3,11},{4,12},{5,13},{6,14},{7,15},{8,0},{9,1},... | collective-permute-start | bytes 786440 | tf_op jit(solution)/shard_map/ppermute | solution.py:256
  98.3 0.9 collective-permute-start.32
  99.3 1.8 %collective-permute-start.33 = (bf16[64,2048]{1,0:T(8,128)(2,1)S(1)}, bf16[64,2048]{1,0:T(8,128)(2,1)S(1)}, u32[]{:S(2)}, u32[]{:S(2)}) collective-permute-start(bf16[64,2048]{1,0:T(8,128)(2,1)S(1)} %add_convert_fusion.3), channel_id=1, source_target_pairs={{0,2},{1,3},{2,0},{3,1},{4,6},{5,7},{6,4},{7,5},{8,10},{9,11},{10,... | collective-permute-start | bytes 786440 | tf_op jit(solution)/shard_map/ppermute | solution.py:256
  101.1 0.3 collective-permute-start.34
  101.4 3.1 %shard_map.84 = f32[768,768]{1,0:T(8,128)} custom-call(f32[16,512]{1,0:T(8,128)S(1)} %shard_map.78.tables, bf16[320,768]{1,0:T(8,128)(2,1)S(1)} %get-tuple-element.143.refs_0_, bf16[320,768]{1,0:T(8,128)(2,1)S(1)} %get-tuple-element.144.refs_1_, bf16[320,768]{1,0:T(8,128)(2,1)S(1)} %get-tuple-element.145.refs_2_, ...), custom_call_target="tpu_custom_call" | custom-call | flops 1509949440 | bytes 4325376 | tf_op jit(solution)/shard_map/pallas_call | solution.py:209
  104.6 6.1 %collective-permute-done.31 = bf16[64,2048]{1,0:T(8,128)(2,1)S(1)} collective-permute-done((bf16[64,2048]{1,0:T(8,128)(2,1)S(1)}, bf16[64,2048]{1,0:T(8,128)(2,1)S(1)}, u32[]{:S(2)}, u32[]{:S(2)}) %collective-permute-start.31) | collective-permute-done | bytes 262176 | tf_op jit(solution)/shard_map/ppermute | solution.py:256
  110.7 1.3 %collective-permute-done.34 = bf16[64,2048]{1,0:T(8,128)(2,1)S(1)} collective-permute-done((bf16[64,2048]{1,0:T(8,128)(2,1)S(1)}, bf16[64,2048]{1,0:T(8,128)(2,1)S(1)}, u32[]{:S(2)}, u32[]{:S(2)}) %collective-permute-start.34) | collective-permute-done | bytes 262176 | tf_op jit(solution)/shard_map/ppermute | solution.py:256
  112.1 0.1 add_convert_fusion.2
  112.2 1.4 %collective-permute-start.35 = (bf16[64,2048]{1,0:T(8,128)(2,1)S(1)}, bf16[64,2048]{1,0:T(8,128)(2,1)S(1)}, u32[]{:S(2)}, u32[]{:S(2)}) collective-permute-start(bf16[64,2048]{1,0:T(8,128)(2,1)S(1)} %add_convert_fusion.2), channel_id=1, source_target_pairs={{0,8},{1,9},{2,10},{3,11},{4,12},{5,13},{6,14},{7,15},{8,0},{9,1},... | collective-permute-start | bytes 786440 | tf_op jit(solution)/shard_map/ppermute | solution.py:256
  113.6 1.0 collective-permute-start.37
  114.6 0.1 add_convert_fusion.1
  114.7 1.3 collective-permute-start.36
  116.0 9.0 %collective-permute-done.35.far_low = bf16[64,2048]{1,0:T(8,128)(2,1)S(1)} collective-permute-done((bf16[64,2048]{1,0:T(8,128)(2,1)S(1)}, bf16[64,2048]{1,0:T(8,128)(2,1)S(1)}, u32[]{:S(2)}, u32[]{:S(2)}) %collective-permute-start.35) | collective-permute-done | bytes 262176 | tf_op jit(solution)/shard_map/ppermute | solution.py:256
  125.0 2.0 %collective-permute-done.36.near_high = bf16[64,2048]{1,0:T(8,128)(2,1)S(1)} collective-permute-done((bf16[64,2048]{1,0:T(8,128)(2,1)S(1)}, bf16[64,2048]{1,0:T(8,128)(2,1)S(1)}, u32[]{:S(2)}, u32[]{:S(2)}) %collective-permute-start.36) | collective-permute-done | bytes 262176 | tf_op jit(solution)/shard_map/ppermute | solution.py:256
  127.0 1.1 shard_map.85
  (59 shorter events, 0.7 us)
Async XLA Ops:
  0.6 24.1 %collective-permute-start = (bf16[128,2048]{1,0:T(8,128)(2,1)}, bf16[128,2048]{1,0:T(8,128)(2,1)S(1)}, u32[]{:S(2)}, u32[]{:S(2)}) collective-permute-start(bf16[128,2048]{1,0:T(8,128)(2,1)} %refs_0_.1), channel_id=1, source_target_pairs={{0,4},{1,5},{2,6},{3,7},{4,0},{5,1},{6,2},{7,3},{8,12},{9,13},{10,... | collective-permute-start | bytes 1572872 | tf_op jit(solution)/shard_map/ppermute | solution.py:256
  3.7 21.0 %collective-permute-start.2 = (bf16[128,2048]{1,0:T(8,128)(2,1)}, bf16[128,2048]{1,0:T(8,128)(2,1)S(1)}, u32[]{:S(2)}, u32[]{:S(2)}) collective-permute-start(bf16[128,2048]{1,0:T(8,128)(2,1)} %refs_0_.1), channel_id=1, source_target_pairs={{0,2},{1,3},{2,0},{3,1},{4,6},{5,7},{6,4},{7,5},{8,10},{9,11},{10,... | collective-permute-start | bytes 1572872 | tf_op jit(solution)/shard_map/ppermute | solution.py:256
  5.2 19.5 %collective-permute-start.3 = (bf16[128,2048]{1,0:T(8,128)(2,1)}, bf16[128,2048]{1,0:T(8,128)(2,1)S(1)}, u32[]{:S(2)}, u32[]{:S(2)}) collective-permute-start(bf16[128,2048]{1,0:T(8,128)(2,1)} %refs_0_.1), channel_id=1, source_target_pairs={{0,1},{1,0},{2,3},{3,2},{4,5},{5,4},{6,7},{7,6},{8,9},{9,8},{10,11... | collective-permute-start | bytes 1572872 | tf_op jit(solution)/shard_map/ppermute | solution.py:256
  5.2 1.1 copy-start.6
  6.3 0.7 copy-start.8
  7.0 0.7 copy-start.9
  7.8 16.9 %collective-permute-start.1 = (bf16[64,2048]{1,0:T(8,128)(2,1)S(1)}, bf16[64,2048]{1,0:T(8,128)(2,1)S(1)}, u32[]{:S(2)}, u32[]{:S(2)}) collective-permute-start(bf16[64,2048]{1,0:T(8,128)(2,1)S(1)} %get-tuple-element.81), channel_id=1, source_target_pairs={{0,8},{1,9},{2,10},{3,11},{4,12},{5,13},{6,14},{7,15},{8,0},{9,1},... | collective-permute-start | bytes 786440 | tf_op jit(solution)/shard_map/ppermute | solution.py:256
  24.7 0.7 copy-start.10
  25.4 2.7 %collective-permute-start.7 = (bf16[128,2048]{1,0:T(8,128)(2,1)S(1)}, bf16[128,2048]{1,0:T(8,128)(2,1)S(1)}, u32[]{:S(2)}, u32[]{:S(2)}) collective-permute-start(bf16[128,2048]{1,0:T(8,128)(2,1)S(1)} %collective-permute-done.2.refs_1_), channel_id=1, source_target_pairs={{0,1},{1,0},{2,3},{3,2},{4,5},{5,4},{6,7},{7,6},{8,9},{9,8},{10,11... | collective-permute-start | bytes 1572872 | tf_op jit(solution)/shard_map/ppermute | solution.py:256
  25.4 15.9 %collective-permute-start.5 = (bf16[128,2048]{1,0:T(8,128)(2,1)S(1)}, bf16[128,2048]{1,0:T(8,128)(2,1)S(1)}, u32[]{:S(2)}, u32[]{:S(2)}) collective-permute-start(bf16[128,2048]{1,0:T(8,128)(2,1)S(1)} %collective-permute-done.refs_0_), channel_id=1, source_target_pairs={{0,2},{1,3},{2,0},{3,1},{4,6},{5,7},{6,4},{7,5},{8,10},{9,11},{10,... | collective-permute-start | bytes 1572872 | tf_op jit(solution)/shard_map/ppermute | solution.py:256
  25.9 15.4 %collective-permute-start.6 = (bf16[128,2048]{1,0:T(8,128)(2,1)S(1)}, bf16[128,2048]{1,0:T(8,128)(2,1)S(1)}, u32[]{:S(2)}, u32[]{:S(2)}) collective-permute-start(bf16[128,2048]{1,0:T(8,128)(2,1)S(1)} %collective-permute-done.refs_0_), channel_id=1, source_target_pairs={{0,1},{1,0},{2,3},{3,2},{4,5},{5,4},{6,7},{7,6},{8,9},{9,8},{10,11... | collective-permute-start | bytes 1572872 | tf_op jit(solution)/shard_map/ppermute | solution.py:256
  26.3 15.1 %collective-permute-start.4 = (bf16[64,2048]{1,0:T(8,128)(2,1)S(1)}, bf16[64,2048]{1,0:T(8,128)(2,1)S(1)}, u32[]{:S(2)}, u32[]{:S(2)}) collective-permute-start(bf16[64,2048]{1,0:T(8,128)(2,1)S(1)} %get-tuple-element.85), channel_id=1, source_target_pairs={{0,8},{1,9},{2,10},{3,11},{4,12},{5,13},{6,14},{7,15},{8,0},{9,1},... | collective-permute-start | bytes 786440 | tf_op jit(solution)/shard_map/ppermute | solution.py:256
  28.2 1.9 %copy-start = (bf16[1,2048,768]{2,1,0:T(8,128)(2,1)S(1)}, bf16[1,2048,768]{2,1,0:T(8,128)(2,1)}, u32[]{:S(2)}) copy-start(bf16[1,2048,768]{2,1,0:T(8,128)(2,1)} %param.9) | copy-start | bytes 9437188
  30.0 1.9 %copy-start.2 = (bf16[1,2048,768]{2,1,0:T(8,128)(2,1)S(1)}, bf16[1,2048,768]{2,1,0:T(8,128)(2,1)}, u32[]{:S(2)}) copy-start(bf16[1,2048,768]{2,1,0:T(8,128)(2,1)} %param.10) | copy-start | bytes 9437188
  31.9 1.9 %copy-start.4 = (bf16[1,768,2048]{2,1,0:T(8,128)(2,1)S(1)}, bf16[1,768,2048]{2,1,0:T(8,128)(2,1)}, u32[]{:S(2)}) copy-start(bf16[1,768,2048]{2,1,0:T(8,128)(2,1)} %param.11) | copy-start | bytes 9437188
  33.8 1.0 copy-start.7
  34.9 6.5 %copy-start.11 = (bf16[64,2048]{1,0:T(8,128)(2,1)S(1)}, bf16[64,2048]{1,0:T(8,128)(2,1)}, u32[]{:S(2)}) copy-start(bf16[64,2048]{1,0:T(8,128)(2,1)} %copy-done.10) | copy-start | bytes 786436
  34.9 8.4 %copy-start.1 = (bf16[1,2048,768]{2,1,0:T(8,128)(2,1)S(1)}, bf16[1,2048,768]{2,1,0:T(8,128)(2,1)}, u32[]{:S(2)}) copy-start(bf16[1,2048,768]{2,1,0:T(8,128)(2,1)} %param.9) | copy-start | bytes 9437188
  34.9 8.4 %copy-start.3 = (bf16[1,2048,768]{2,1,0:T(8,128)(2,1)S(1)}, bf16[1,2048,768]{2,1,0:T(8,128)(2,1)}, u32[]{:S(2)}) copy-start(bf16[1,2048,768]{2,1,0:T(8,128)(2,1)} %param.10) | copy-start | bytes 9437188
  34.9 8.4 %copy-start.5 = (bf16[1,768,2048]{2,1,0:T(8,128)(2,1)S(1)}, bf16[1,768,2048]{2,1,0:T(8,128)(2,1)}, u32[]{:S(2)}) copy-start(bf16[1,768,2048]{2,1,0:T(8,128)(2,1)} %param.11) | copy-start | bytes 9437188
  41.3 1.9 %collective-permute-start.11 = (bf16[128,2048]{1,0:T(8,128)(2,1)S(1)}, bf16[128,2048]{1,0:T(8,128)(2,1)S(1)}, u32[]{:S(2)}, u32[]{:S(2)}) collective-permute-start(bf16[128,2048]{1,0:T(8,128)(2,1)S(1)} %collective-permute-done.5.refs_1_), channel_id=1, source_target_pairs={{0,1},{1,0},{2,3},{3,2},{4,5},{5,4},{6,7},{7,6},{8,9},{9,8},{10,11... | collective-permute-start | bytes 1572872 | tf_op jit(solution)/shard_map/ppermute | solution.py:256
  41.4 14.4 %collective-permute-start.8 = (bf16[128,2048]{1,0:T(8,128)(2,1)S(1)}, bf16[128,2048]{1,0:T(8,128)(2,1)S(1)}, u32[]{:S(2)}, u32[]{:S(2)}) collective-permute-start(bf16[128,2048]{1,0:T(8,128)(2,1)S(1)} %constant_dynamic-update-slice_fusion.refs_0_), channel_id=1, source_target_pairs={{0,4},{1,5},{2,6},{3,7},{4,0},{5,1},{6,2},{7,3},{8,12},{9,13},{10,... | collective-permute-start | bytes 1572872 | tf_op jit(solution)/shard_map/ppermute | solution.py:256
  42.1 14.0 %collective-permute-start.9 = (bf16[128,2048]{1,0:T(8,128)(2,1)S(1)}, bf16[128,2048]{1,0:T(8,128)(2,1)S(1)}, u32[]{:S(2)}, u32[]{:S(2)}) collective-permute-start(bf16[128,2048]{1,0:T(8,128)(2,1)S(1)} %constant_dynamic-update-slice_fusion.refs_0_), channel_id=1, source_target_pairs={{0,2},{1,3},{2,0},{3,1},{4,6},{5,7},{6,4},{7,5},{8,10},{9,11},{10,... | collective-permute-start | bytes 1572872 | tf_op jit(solution)/shard_map/ppermute | solution.py:256
  43.2 12.9 %collective-permute-start.10 = (bf16[128,2048]{1,0:T(8,128)(2,1)S(1)}, bf16[128,2048]{1,0:T(8,128)(2,1)S(1)}, u32[]{:S(2)}, u32[]{:S(2)}) collective-permute-start(bf16[128,2048]{1,0:T(8,128)(2,1)S(1)} %constant_dynamic-update-slice_fusion.refs_0_), channel_id=1, source_target_pairs={{0,1},{1,0},{2,3},{3,2},{4,5},{5,4},{6,7},{7,6},{8,9},{9,8},{10,11... | collective-permute-start | bytes 1572872 | tf_op jit(solution)/shard_map/ppermute | solution.py:256
  48.7 7.4 %collective-permute-start.12 = (bf16[128,2048]{1,0:T(8,128)(2,1)S(1)}, bf16[128,2048]{1,0:T(8,128)(2,1)S(1)}, u32[]{:S(2)}, u32[]{:S(2)}) collective-permute-start(bf16[128,2048]{1,0:T(8,128)(2,1)S(1)} %get-tuple-element.100), channel_id=1, source_target_pairs={{0,1},{1,0},{2,3},{3,2},{4,5},{5,4},{6,7},{7,6},{8,9},{9,8},{10,11... | collective-permute-start | bytes 1572872 | tf_op jit(solution)/shard_map/ppermute | solution.py:256
  56.1 3.6 %collective-permute-start.17 = (bf16[128,2048]{1,0:T(8,128)(2,1)S(1)}, bf16[128,2048]{1,0:T(8,128)(2,1)S(1)}, u32[]{:S(2)}, u32[]{:S(2)}) collective-permute-start(bf16[128,2048]{1,0:T(8,128)(2,1)S(1)} %collective-permute-done.9.refs_1_), channel_id=1, source_target_pairs={{0,1},{1,0},{2,3},{3,2},{4,5},{5,4},{6,7},{7,6},{8,9},{9,8},{10,11... | collective-permute-start | bytes 1572872 | tf_op jit(solution)/shard_map/ppermute | solution.py:256
  56.1 12.6 %collective-permute-start.15 = (bf16[256,2048]{1,0:T(8,128)(2,1)S(1)}, bf16[256,2048]{1,0:T(8,128)(2,1)S(1)}, u32[]{:S(2)}, u32[]{:S(2)}) collective-permute-start(bf16[256,2048]{1,0:T(8,128)(2,1)S(1)} %get-tuple-element.104), channel_id=1, source_target_pairs={{0,1},{1,0},{2,3},{3,2},{4,5},{5,4},{6,7},{7,6},{8,9},{9,8},{10,11... | collective-permute-start | bytes 3145736 | tf_op jit(solution)/shard_map/ppermute | solution.py:256
  56.6 13.9 %collective-permute-start.13 = (bf16[128,2048]{1,0:T(8,128)(2,1)S(1)}, bf16[128,2048]{1,0:T(8,128)(2,1)S(1)}, u32[]{:S(2)}, u32[]{:S(2)}) collective-permute-start(bf16[128,2048]{1,0:T(8,128)(2,1)S(1)} %collective-permute-done.9.refs_1_), channel_id=1, source_target_pairs={{0,4},{1,5},{2,6},{3,7},{4,0},{5,1},{6,2},{7,3},{8,12},{9,13},{10,... | collective-permute-start | bytes 1572872 | tf_op jit(solution)/shard_map/ppermute | solution.py:256
  58.1 7.6 %collective-permute-start.19 = (bf16[128,2048]{1,0:T(8,128)(2,1)S(1)}, bf16[128,2048]{1,0:T(8,128)(2,1)S(1)}, u32[]{:S(2)}, u32[]{:S(2)}) collective-permute-start(bf16[128,2048]{1,0:T(8,128)(2,1)S(1)} %collective-permute-done.8.refs_0_), channel_id=1, source_target_pairs={{0,1},{1,0},{2,3},{3,2},{4,5},{5,4},{6,7},{7,6},{8,9},{9,8},{10,11... | collective-permute-start | bytes 1572872 | tf_op jit(solution)/shard_map/ppermute | solution.py:256
  58.2 10.5 %collective-permute-start.14 = (bf16[64,2048]{1,0:T(8,128)(2,1)S(1)}, bf16[64,2048]{1,0:T(8,128)(2,1)S(1)}, u32[]{:S(2)}, u32[]{:S(2)}) collective-permute-start(bf16[64,2048]{1,0:T(8,128)(2,1)S(1)} %get-tuple-element.161), channel_id=1, source_target_pairs={{0,2},{1,3},{2,0},{3,1},{4,6},{5,7},{6,4},{7,5},{8,10},{9,11},{10,... | collective-permute-start | bytes 786440 | tf_op jit(solution)/shard_map/ppermute | solution.py:256
  59.7 10.8 %collective-permute-start.16 = (bf16[128,2048]{1,0:T(8,128)(2,1)S(1)}, bf16[128,2048]{1,0:T(8,128)(2,1)S(1)}, u32[]{:S(2)}, u32[]{:S(2)}) collective-permute-start(bf16[128,2048]{1,0:T(8,128)(2,1)S(1)} %get-tuple-element.105), channel_id=1, source_target_pairs={{0,1},{1,0},{2,3},{3,2},{4,5},{5,4},{6,7},{7,6},{8,9},{9,8},{10,11... | collective-permute-start | bytes 1572872 | tf_op jit(solution)/shard_map/ppermute | solution.py:256
  65.6 4.9 %collective-permute-start.18 = (bf16[64,2048]{1,0:T(8,128)(2,1)S(1)}, bf16[64,2048]{1,0:T(8,128)(2,1)S(1)}, u32[]{:S(2)}, u32[]{:S(2)}) collective-permute-start(bf16[64,2048]{1,0:T(8,128)(2,1)S(1)} %get-tuple-element.107), channel_id=1, source_target_pairs={{0,1},{1,0},{2,3},{3,2},{4,5},{5,4},{6,7},{7,6},{8,9},{9,8},{10,11... | collective-permute-start | bytes 786440 | tf_op jit(solution)/shard_map/ppermute | solution.py:256
  70.5 1.9 %collective-permute-start.20 = (bf16[128,2048]{1,0:T(8,128)(2,1)S(1)}, bf16[128,2048]{1,0:T(8,128)(2,1)S(1)}, u32[]{:S(2)}, u32[]{:S(2)}) collective-permute-start(bf16[128,2048]{1,0:T(8,128)(2,1)S(1)} %collective-permute-done.13.refs_0_), channel_id=1, source_target_pairs={{0,1},{1,0},{2,3},{3,2},{4,5},{5,4},{6,7},{7,6},{8,9},{9,8},{10,11... | collective-permute-start | bytes 1572872 | tf_op jit(solution)/shard_map/ppermute | solution.py:256
  70.5 8.9 %collective-permute-start.23 = (bf16[128,2048]{1,0:T(8,128)(2,1)S(1)}, bf16[128,2048]{1,0:T(8,128)(2,1)S(1)}, u32[]{:S(2)}, u32[]{:S(2)}) collective-permute-start(bf16[128,2048]{1,0:T(8,128)(2,1)S(1)} %get-tuple-element.122), channel_id=1, source_target_pairs={{0,1},{1,0},{2,3},{3,2},{4,5},{5,4},{6,7},{7,6},{8,9},{9,8},{10,11... | collective-permute-start | bytes 1572872 | tf_op jit(solution)/shard_map/ppermute | solution.py:256
  71.1 8.3 %collective-permute-start.24 = (bf16[64,2048]{1,0:T(8,128)(2,1)S(1)}, bf16[64,2048]{1,0:T(8,128)(2,1)S(1)}, u32[]{:S(2)}, u32[]{:S(2)}) collective-permute-start(bf16[64,2048]{1,0:T(8,128)(2,1)S(1)} %add_convert_fusion.11), channel_id=1, source_target_pairs={{0,2},{1,3},{2,0},{3,1},{4,6},{5,7},{6,4},{7,5},{8,10},{9,11},{10,... | collective-permute-start | bytes 786440 | tf_op jit(solution)/shard_map/ppermute | solution.py:256
  72.4 11.4 %collective-permute-start.29 = (bf16[64,2048]{1,0:T(8,128)(2,1)S(1)}, bf16[64,2048]{1,0:T(8,128)(2,1)S(1)}, u32[]{:S(2)}, u32[]{:S(2)}) collective-permute-start(bf16[64,2048]{1,0:T(8,128)(2,1)S(1)} %get-tuple-element.135), channel_id=1, source_target_pairs={{0,1},{1,0},{2,3},{3,2},{4,5},{5,4},{6,7},{7,6},{8,9},{9,8},{10,11... | collective-permute-start | bytes 786440 | tf_op jit(solution)/shard_map/ppermute | solution.py:256
  75.2 4.3 %collective-permute-start.21 = (bf16[64,2048]{1,0:T(8,128)(2,1)S(1)}, bf16[64,2048]{1,0:T(8,128)(2,1)S(1)}, u32[]{:S(2)}, u32[]{:S(2)}) collective-permute-start(bf16[64,2048]{1,0:T(8,128)(2,1)S(1)} %get-tuple-element.119), channel_id=1, source_target_pairs={{0,1},{1,0},{2,3},{3,2},{4,5},{5,4},{6,7},{7,6},{8,9},{9,8},{10,11... | collective-permute-start | bytes 786440 | tf_op jit(solution)/shard_map/ppermute | solution.py:256
  75.7 3.7 %collective-permute-start.22 = (bf16[64,2048]{1,0:T(8,128)(2,1)S(1)}, bf16[64,2048]{1,0:T(8,128)(2,1)S(1)}, u32[]{:S(2)}, u32[]{:S(2)}) collective-permute-start(bf16[64,2048]{1,0:T(8,128)(2,1)S(1)} %get-tuple-element.120), channel_id=1, source_target_pairs={{0,1},{1,0},{2,3},{3,2},{4,5},{5,4},{6,7},{7,6},{8,9},{9,8},{10,11... | collective-permute-start | bytes 786440 | tf_op jit(solution)/shard_map/ppermute | solution.py:256
  79.5 5.0 %collective-permute-start.30 = (bf16[128,2048]{1,0:T(8,128)(2,1)S(1)}, bf16[128,2048]{1,0:T(8,128)(2,1)S(1)}, u32[]{:S(2)}, u32[]{:S(2)}) collective-permute-start(bf16[128,2048]{1,0:T(8,128)(2,1)S(1)} %get-tuple-element.136), channel_id=1, source_target_pairs={{0,1},{1,0},{2,3},{3,2},{4,5},{5,4},{6,7},{7,6},{8,9},{9,8},{10,11... | collective-permute-start | bytes 1572872 | tf_op jit(solution)/shard_map/ppermute | solution.py:256
  79.6 9.2 %collective-permute-start.25 = (bf16[64,2048]{1,0:T(8,128)(2,1)S(1)}, bf16[64,2048]{1,0:T(8,128)(2,1)S(1)}, u32[]{:S(2)}, u32[]{:S(2)}) collective-permute-start(bf16[64,2048]{1,0:T(8,128)(2,1)S(1)} %get-tuple-element.165), channel_id=1, source_target_pairs={{0,2},{1,3},{2,0},{3,1},{4,6},{5,7},{6,4},{7,5},{8,10},{9,11},{10,... | collective-permute-start | bytes 786440 | tf_op jit(solution)/shard_map/ppermute | solution.py:256
  81.0 13.1 %collective-permute-start.26 = (bf16[64,2048]{1,0:T(8,128)(2,1)S(1)}, bf16[64,2048]{1,0:T(8,128)(2,1)S(1)}, u32[]{:S(2)}, u32[]{:S(2)}) collective-permute-start(bf16[64,2048]{1,0:T(8,128)(2,1)S(1)} %get-tuple-element.164), channel_id=1, source_target_pairs={{0,2},{1,3},{2,0},{3,1},{4,6},{5,7},{6,4},{7,5},{8,10},{9,11},{10,... | collective-permute-start | bytes 786440 | tf_op jit(solution)/shard_map/ppermute | solution.py:256
  81.8 14.7 %collective-permute-start.27 = (bf16[64,2048]{1,0:T(8,128)(2,1)S(1)}, bf16[64,2048]{1,0:T(8,128)(2,1)S(1)}, u32[]{:S(2)}, u32[]{:S(2)}) collective-permute-start(bf16[64,2048]{1,0:T(8,128)(2,1)S(1)} %add_convert_fusion.7), channel_id=1, source_target_pairs={{0,8},{1,9},{2,10},{3,11},{4,12},{5,13},{6,14},{7,15},{8,0},{9,1},... | collective-permute-start | bytes 786440 | tf_op jit(solution)/shard_map/ppermute | solution.py:256
  83.8 12.7 %collective-permute-start.28 = (bf16[64,2048]{1,0:T(8,128)(2,1)S(1)}, bf16[64,2048]{1,0:T(8,128)(2,1)S(1)}, u32[]{:S(2)}, u32[]{:S(2)}) collective-permute-start(bf16[64,2048]{1,0:T(8,128)(2,1)S(1)} %add_convert_fusion.10), channel_id=1, source_target_pairs={{0,4},{1,5},{2,6},{3,7},{4,0},{5,1},{6,2},{7,3},{8,12},{9,13},{10,... | collective-permute-start | bytes 786440 | tf_op jit(solution)/shard_map/ppermute | solution.py:256
  96.8 13.9 %collective-permute-start.31 = (bf16[64,2048]{1,0:T(8,128)(2,1)S(1)}, bf16[64,2048]{1,0:T(8,128)(2,1)S(1)}, u32[]{:S(2)}, u32[]{:S(2)}) collective-permute-start(bf16[64,2048]{1,0:T(8,128)(2,1)S(1)} %get-tuple-element.163), channel_id=1, source_target_pairs={{0,8},{1,9},{2,10},{3,11},{4,12},{5,13},{6,14},{7,15},{8,0},{9,1},... | collective-permute-start | bytes 786440 | tf_op jit(solution)/shard_map/ppermute | solution.py:256
  98.3 12.4 %collective-permute-start.32 = (bf16[64,2048]{1,0:T(8,128)(2,1)S(1)}, bf16[64,2048]{1,0:T(8,128)(2,1)S(1)}, u32[]{:S(2)}, u32[]{:S(2)}) collective-permute-start(bf16[64,2048]{1,0:T(8,128)(2,1)S(1)} %get-tuple-element.162), channel_id=1, source_target_pairs={{0,4},{1,5},{2,6},{3,7},{4,0},{5,1},{6,2},{7,3},{8,12},{9,13},{10,... | collective-permute-start | bytes 786440 | tf_op jit(solution)/shard_map/ppermute | solution.py:256
  99.3 11.4 %collective-permute-start.33 = (bf16[64,2048]{1,0:T(8,128)(2,1)S(1)}, bf16[64,2048]{1,0:T(8,128)(2,1)S(1)}, u32[]{:S(2)}, u32[]{:S(2)}) collective-permute-start(bf16[64,2048]{1,0:T(8,128)(2,1)S(1)} %add_convert_fusion.3), channel_id=1, source_target_pairs={{0,2},{1,3},{2,0},{3,1},{4,6},{5,7},{6,4},{7,5},{8,10},{9,11},{10,... | collective-permute-start | bytes 786440 | tf_op jit(solution)/shard_map/ppermute | solution.py:256
  101.1 11.0 %collective-permute-start.34 = (bf16[64,2048]{1,0:T(8,128)(2,1)S(1)}, bf16[64,2048]{1,0:T(8,128)(2,1)S(1)}, u32[]{:S(2)}, u32[]{:S(2)}) collective-permute-start(bf16[64,2048]{1,0:T(8,128)(2,1)S(1)} %get-tuple-element.141), channel_id=1, source_target_pairs={{0,2},{1,3},{2,0},{3,1},{4,6},{5,7},{6,4},{7,5},{8,10},{9,11},{10,... | collective-permute-start | bytes 786440 | tf_op jit(solution)/shard_map/ppermute | solution.py:256
  112.2 12.8 %collective-permute-start.35 = (bf16[64,2048]{1,0:T(8,128)(2,1)S(1)}, bf16[64,2048]{1,0:T(8,128)(2,1)S(1)}, u32[]{:S(2)}, u32[]{:S(2)}) collective-permute-start(bf16[64,2048]{1,0:T(8,128)(2,1)S(1)} %add_convert_fusion.2), channel_id=1, source_target_pairs={{0,8},{1,9},{2,10},{3,11},{4,12},{5,13},{6,14},{7,15},{8,0},{9,1},... | collective-permute-start | bytes 786440 | tf_op jit(solution)/shard_map/ppermute | solution.py:256
  113.6 13.4 %collective-permute-start.37 = (bf16[128,2048]{1,0:T(8,128)(2,1)S(1)}, bf16[128,2048]{1,0:T(8,128)(2,1)S(1)}, u32[]{:S(2)}, u32[]{:S(2)}) collective-permute-start(bf16[128,2048]{1,0:T(8,128)(2,1)S(1)} %add_convert_fusion), channel_id=1, source_target_pairs={{0,2},{1,3},{2,0},{3,1},{4,6},{5,7},{6,4},{7,5},{8,10},{9,11},{10,... | collective-permute-start | bytes 1572872 | tf_op jit(solution)/shard_map/ppermute | solution.py:256
  114.7 12.3 %collective-permute-start.36 = (bf16[64,2048]{1,0:T(8,128)(2,1)S(1)}, bf16[64,2048]{1,0:T(8,128)(2,1)S(1)}, u32[]{:S(2)}, u32[]{:S(2)}) collective-permute-start(bf16[64,2048]{1,0:T(8,128)(2,1)S(1)} %add_convert_fusion.1), channel_id=1, source_target_pairs={{0,4},{1,5},{2,6},{3,7},{4,0},{5,1},{6,2},{7,3},{8,12},{9,13},{10,... | collective-permute-start | bytes 786440 | tf_op jit(solution)/shard_map/ppermute | solution.py:256

commit v25 on v24

--- a/solution.py
+++ b/solution.py
@@ -339,8 +339,8 @@
     near1_low = pair(near1)
     side0 = summed(keep0[tok:], got0[tok:])
     side1 = summed(keep1[tok + half :], got1_side[half:])
-    came3_low, came3_high, far2_high, near1_low, side0, side1, got2_low, got3 = together(
-        came3_low, came3_high, far2_high, near1_low, side0, side1, got2_low, got3
+    far2_high, came3_low, came3_high, near1_low, side0, side1, got2_low, got3 = together(
+        far2_high, came3_low, came3_high, near1_low, side0, side1, got2_low, got3
     )
     far3_high = far(summed(keep3[half:], got3[half:], came3_high))
     pair3_low = pair(summed(keep3[:half], got3[:half], came3_low))

time: 129 us -> 127 us (0.984)
  no operation moved by 1% of the time
where the time goes in v25:
time: 127 us
  waiting for transfers between devices  42.8 us (34%)
  starting transfers between devices  30.8 us (24%)
  Pallas kernels  27.1 us (21%)
  blocking collectives  14.2 us (11%)
  local copies, waits for them, and re-layouts  9.97 us (8%)
    ppermute x38, waiting for transfers between devices, swapped(): return lax.ppermute(array, 'expert', [(i, i ^ bit) for i in range(size)])  42.8 us
    ppermute x38, starting transfers between devices, swapped(): return lax.ppermute(array, 'expert', [(i, i ^ bit) for i in range(size)])  30.8 us
    pallas_call x5, Pallas kernels, plane_pass(): pl.pallas_call(functools.partial(plane_kernel, k, picked, len(pieces)), o...  22 us
    all_to_all x1, blocking collectives, staged(): lax.all_to_all(mine, 'expert', split_axis=0, concat_axis=0, tiled=True)  14.2 us
    unnamed x25, local copies, waits for them, and re-layouts  9.86 us
    pallas_call x1, Pallas kernels, gram_pass(): pl.pallas_call(gram_kernel, out_shape=jax.ShapeDtypeStruct((hidden, hidde...  3.14 us
  transfers between devices with their start and end apart: 38, of which 12 were waited for; matrix products, arithmetic and copies ran while one was open for 1% of the time, Pallas kernels for 20%

profile of v25, /device:TPU:0, one launch (start us, length us, event | category | flops | bytes accessed | tf_op | source)
XLA Modules:
  0.0 127.1 jit_solution(14265564924030089542)
XLA Ops:
  0.6 3.1 %collective-permute-start = (bf16[128,2048]{1,0:T(8,128)(2,1)}, bf16[128,2048]{1,0:T(8,128)(2,1)S(1)}, u32[]{:S(2)}, u32[]{:S(2)}) collective-permute-start(bf16[128,2048]{1,0:T(8,128)(2,1)} %refs_0_.1), channel_id=1, source_target_pairs={{0,4},{1,5},{2,6},{3,7},{4,0},{5,1},{6,2},{7,3},{8,12},{9,13},{10,... | collective-permute-start | bytes 1572872 | tf_op jit(solution)/shard_map/ppermute | solution.py:256
  3.7 1.5 %collective-permute-start.2 = (bf16[128,2048]{1,0:T(8,128)(2,1)}, bf16[128,2048]{1,0:T(8,128)(2,1)S(1)}, u32[]{:S(2)}, u32[]{:S(2)}) collective-permute-start(bf16[128,2048]{1,0:T(8,128)(2,1)} %refs_0_.1), channel_id=1, source_target_pairs={{0,2},{1,3},{2,0},{3,1},{4,6},{5,7},{6,4},{7,5},{8,10},{9,11},{10,... | collective-permute-start | bytes 1572872 | tf_op jit(solution)/shard_map/ppermute | solution.py:256
  5.2 1.1 copy-done.6
  6.3 0.7 copy-done.8
  7.0 0.7 copy-done.9
  7.7 0.1 shard_map.77
  7.8 2.7 %collective-permute-start.1 = (bf16[64,2048]{1,0:T(8,128)(2,1)S(1)}, bf16[64,2048]{1,0:T(8,128)(2,1)S(1)}, u32[]{:S(2)}, u32[]{:S(2)}) collective-permute-start(bf16[64,2048]{1,0:T(8,128)(2,1)S(1)} %get-tuple-element.81), channel_id=1, source_target_pairs={{0,8},{1,9},{2,10},{3,11},{4,12},{5,13},{6,14},{7,15},{8,0},{9,1},... | collective-permute-start | bytes 786440 | tf_op jit(solution)/shard_map/ppermute | solution.py:256
  10.5 14.2 %all_to_all.12 = f32[16,1,128]{2,1,0:T(1,128)S(1)} all-to-all(f32[16,1,128]{2,1,0:T(1,128)S(1)} %bitcast.42), channel_id=1, replica_groups=mesh['parts'=2,'expert'=16] {'expert'}, dimensions={0} | all-to-all | bytes 16384 | tf_op jit(solution)/shard_map/all_to_all | solution.py:285
  24.8 0.7 copy-done.10
  25.4 0.5 collective-permute-start.5
  25.9 0.2 collective-permute-start.6
  26.3 1.1 collective-permute-start.4
  27.4 0.7 shard_map.78.tables
  28.2 1.9 %copy-done = bf16[1,2048,768]{2,1,0:T(8,128)(2,1)S(1)} copy-done((bf16[1,2048,768]{2,1,0:T(8,128)(2,1)S(1)}, bf16[1,2048,768]{2,1,0:T(8,128)(2,1)}, u32[]{:S(2)}) %copy-start) | copy-done | bytes 3145752
  30.0 1.9 %copy-done.2 = bf16[1,2048,768]{2,1,0:T(8,128)(2,1)S(1)} copy-done((bf16[1,2048,768]{2,1,0:T(8,128)(2,1)S(1)}, bf16[1,2048,768]{2,1,0:T(8,128)(2,1)}, u32[]{:S(2)}) %copy-start.2) | copy-done | bytes 3145752
  31.9 1.9 %copy-done.4 = bf16[1,768,2048]{2,1,0:T(8,128)(2,1)S(1)} copy-done((bf16[1,768,2048]{2,1,0:T(8,128)(2,1)S(1)}, bf16[1,768,2048]{2,1,0:T(8,128)(2,1)}, u32[]{:S(2)}) %copy-start.4) | copy-done | bytes 3145752
  33.8 1.0 copy-done.7
  34.9 5.5 %shard_map.79 = (bf16[256,2048]{1,0:T(8,128)(2,1)S(1)}, bf16[256,2048]{1,0:T(8,128)(2,1)S(1)}, bf16[320,768]{1,0:T(8,128)(2,1)S(1)}) custom-call(f32[16,512]{1,0:T(8,128)S(1)} %shard_map.78.tables, bf16[128,2048]{1,0:T(8,128)(2,1)S(1)} %copy-done.7, bf16[128,2048]{1,0:T(8,128)(2,1)S(1)} %collective-permute-done.2.refs_1_, ...), custom_call_target="tpu_custom_call" | custom-call | flops 4362076160 | bytes 13631488 | tf_op jit(solution)/shard_map/pallas_call | solution.py:178
  40.4 1.0 collective-permute-done.4
  41.4 0.7 collective-permute-start.8
  42.1 1.1 collective-permute-start.9
  43.3 5.5 %shard_map.80 = (bf16[256,2048]{1,0:T(8,128)(2,1)S(1)}, bf16[128,2048]{1,0:T(8,128)(2,1)S(1)}, bf16[128,2048]{1,0:T(8,128)(2,1)S(1)}, bf16[320,768]{1,0:T(8,128)(2,1)S(1)}) custom-call(f32[16,512]{1,0:T(8,128)S(1)} %shard_map.78.tables, bf16[128,2048]{1,0:T(8,128)(2,1)S(1)} %collective-permute-done.refs_0_, ...), custom_call_target="tpu_custom_call" | custom-call | flops 4362076160 | bytes 13631488 | tf_op jit(solution)/shard_map/pallas_call | solution.py:178
  48.7 0.5 collective-permute-start.12
  49.3 6.5 %collective-permute-done.8.refs_0_ = bf16[128,2048]{1,0:T(8,128)(2,1)S(1)} collective-permute-done((bf16[128,2048]{1,0:T(8,128)(2,1)S(1)}, bf16[128,2048]{1,0:T(8,128)(2,1)S(1)}, u32[]{:S(2)}, u32[]{:S(2)}) %collective-permute-start.8) | collective-permute-done | bytes 524320 | tf_op jit(solution)/shard_map/ppermute | solution.py:256
  55.8 0.3 collective-permute-done.9.refs_1_
  56.1 0.5 collective-permute-start.15
  56.6 1.4 %collective-permute-start.13 = (bf16[128,2048]{1,0:T(8,128)(2,1)S(1)}, bf16[128,2048]{1,0:T(8,128)(2,1)S(1)}, u32[]{:S(2)}, u32[]{:S(2)}) collective-permute-start(bf16[128,2048]{1,0:T(8,128)(2,1)S(1)} %collective-permute-done.9.refs_1_), channel_id=1, source_target_pairs={{0,4},{1,5},{2,6},{3,7},{4,0},{5,1},{6,2},{7,3},{8,12},{9,13},{10,... | collective-permute-start | bytes 1572872 | tf_op jit(solution)/shard_map/ppermute | solution.py:256
  58.1 0.1 add_convert_fusion.6
  58.2 1.5 %collective-permute-start.14 = (bf16[64,2048]{1,0:T(8,128)(2,1)S(1)}, bf16[64,2048]{1,0:T(8,128)(2,1)S(1)}, u32[]{:S(2)}, u32[]{:S(2)}) collective-permute-start(bf16[64,2048]{1,0:T(8,128)(2,1)S(1)} %get-tuple-element.161), channel_id=1, source_target_pairs={{0,2},{1,3},{2,0},{3,1},{4,6},{5,7},{6,4},{7,5},{8,10},{9,11},{10,... | collective-permute-start | bytes 786440 | tf_op jit(solution)/shard_map/ppermute | solution.py:256
  59.7 0.2 collective-permute-start.16
  60.0 5.7 %shard_map.81 = (bf16[256,2048]{1,0:T(8,128)(2,1)S(1)}, bf16[128,2048]{1,0:T(8,128)(2,1)S(1)}, bf16[64,2048]{1,0:T(8,128)(2,1)S(1)}, bf16[64,2048]{1,0:T(8,128)(2,1)S(1)}, bf16[320,768]{1,0:T(8,128)(2,1)S(1)}) custom-call(f32[16,512]{1,0:T(8,128)S(1)} %shard_map.78.tables, bf16[128,2048]{1,0:T(8,128)(2,1)S(1)} %constant_dynamic-update-slice_fusion.refs_0_, ...), custom_call_target="tpu_custom_call" | custom-call | flops 4362076160 | bytes 13631488 | tf_op jit(solution)/shard_map/pallas_call | solution.py:178
  65.6 0.3 collective-permute-start.18
  66.0 2.7 %shard_map.82 = (bf16[128,2048]{1,0:T(8,128)(2,1)S(1)}, bf16[128,2048]{1,0:T(8,128)(2,1)S(1)}, bf16[160,768]{1,0:T(8,128)(2,1)S(1)}) custom-call(f32[16,512]{1,0:T(8,128)S(1)} %shard_map.78.tables, bf16[128,2048]{1,0:T(8,128)(2,1)S(1)} %collective-permute-done.8.refs_0_, bf16[128,2048]{1,0:T(8,128)(2,1)S(1)} %collective-permute-done.19.refs_1_, ...), custom_call_target="tpu_custom_call" | custom-call | flops 1845493760 | bytes 11534336 | tf_op jit(solution)/shard_map/pallas_call | solution.py:178
  68.7 1.8 %collective-permute-done.13.refs_0_ = bf16[128,2048]{1,0:T(8,128)(2,1)S(1)} collective-permute-done((bf16[128,2048]{1,0:T(8,128)(2,1)S(1)}, bf16[128,2048]{1,0:T(8,128)(2,1)S(1)}, u32[]{:S(2)}, u32[]{:S(2)}) %collective-permute-start.13) | collective-permute-done | bytes 524320 | tf_op jit(solution)/shard_map/ppermute | solution.py:256
  70.5 0.5 collective-permute-start.23
  71.1 1.3 %collective-permute-start.24 = (bf16[64,2048]{1,0:T(8,128)(2,1)S(1)}, bf16[64,2048]{1,0:T(8,128)(2,1)S(1)}, u32[]{:S(2)}, u32[]{:S(2)}) collective-permute-start(bf16[64,2048]{1,0:T(8,128)(2,1)S(1)} %add_convert_fusion.11), channel_id=1, source_target_pairs={{0,2},{1,3},{2,0},{3,1},{4,6},{5,7},{6,4},{7,5},{8,10},{9,11},{10,... | collective-permute-start | bytes 786440 | tf_op jit(solution)/shard_map/ppermute | solution.py:256
  72.5 2.7 %shard_map.83 = (bf16[128,2048]{1,0:T(8,128)(2,1)S(1)}, bf16[64,2048]{1,0:T(8,128)(2,1)S(1)}, bf16[64,2048]{1,0:T(8,128)(2,1)S(1)}, bf16[160,768]{1,0:T(8,128)(2,1)S(1)}) custom-call(f32[16,512]{1,0:T(8,128)S(1)} %shard_map.78.tables, bf16[128,2048]{1,0:T(8,128)(2,1)S(1)} %collective-permute-done.13.refs_0_, ...), custom_call_target="tpu_custom_call" | custom-call | flops 1845493760 | bytes 11534336 | tf_op jit(solution)/shard_map/pallas_call | solution.py:178
  75.2 0.6 collective-permute-start.21
  75.8 0.1 add_convert_fusion.10
  75.9 3.5 %collective-permute-done.24 = bf16[64,2048]{1,0:T(8,128)(2,1)S(1)} collective-permute-done((bf16[64,2048]{1,0:T(8,128)(2,1)S(1)}, bf16[64,2048]{1,0:T(8,128)(2,1)S(1)}, u32[]{:S(2)}, u32[]{:S(2)}) %collective-permute-start.24) | collective-permute-done | bytes 262176 | tf_op jit(solution)/shard_map/ppermute | solution.py:256
  79.6 2.0 %collective-permute-start.25 = (bf16[64,2048]{1,0:T(8,128)(2,1)S(1)}, bf16[64,2048]{1,0:T(8,128)(2,1)S(1)}, u32[]{:S(2)}, u32[]{:S(2)}) collective-permute-start(bf16[64,2048]{1,0:T(8,128)(2,1)S(1)} %add_convert_fusion.9), channel_id=1, source_target_pairs={{0,8},{1,9},{2,10},{3,11},{4,12},{5,13},{6,14},{7,15},{8,0},{9,1},... | collective-permute-start | bytes 786440 | tf_op jit(solution)/shard_map/ppermute | solution.py:256
  81.6 0.1 add_convert_fusion.7
  81.7 1.0 collective-permute-start.26
  82.8 1.0 collective-permute-start.27
  83.8 0.5 collective-permute-start.28
  84.3 0.1 add_convert_fusion
  84.4 10.6 %collective-permute-done.25.far_high = bf16[64,2048]{1,0:T(8,128)(2,1)S(1)} collective-permute-done((bf16[64,2048]{1,0:T(8,128)(2,1)S(1)}, bf16[64,2048]{1,0:T(8,128)(2,1)S(1)}, u32[]{:S(2)}, u32[]{:S(2)}) %collective-permute-start.25) | collective-permute-done | bytes 262176 | tf_op jit(solution)/shard_map/ppermute | solution.py:256
  95.0 0.8 collective-permute-done.27
  95.8 0.5 collective-permute-done.28.near_low
  96.3 0.2 add_convert_fusion.4
  96.6 0.6 collective-permute-start.31
  97.1 1.8 %collective-permute-start.32 = (bf16[64,2048]{1,0:T(8,128)(2,1)S(1)}, bf16[64,2048]{1,0:T(8,128)(2,1)S(1)}, u32[]{:S(2)}, u32[]{:S(2)}) collective-permute-start(bf16[64,2048]{1,0:T(8,128)(2,1)S(1)} %get-tuple-element.162), channel_id=1, source_target_pairs={{0,4},{1,5},{2,6},{3,7},{4,0},{5,1},{6,2},{7,3},{8,12},{9,13},{10,... | collective-permute-start | bytes 786440 | tf_op jit(solution)/shard_map/ppermute | solution.py:256
  99.0 2.1 %collective-permute-start.33 = (bf16[64,2048]{1,0:T(8,128)(2,1)S(1)}, bf16[64,2048]{1,0:T(8,128)(2,1)S(1)}, u32[]{:S(2)}, u32[]{:S(2)}) collective-permute-start(bf16[64,2048]{1,0:T(8,128)(2,1)S(1)} %add_convert_fusion.3), channel_id=1, source_target_pairs={{0,2},{1,3},{2,0},{3,1},{4,6},{5,7},{6,4},{7,5},{8,10},{9,11},{10,... | collective-permute-start | bytes 786440 | tf_op jit(solution)/shard_map/ppermute | solution.py:256
  101.2 3.1 %shard_map.84 = f32[768,768]{1,0:T(8,128)} custom-call(f32[16,512]{1,0:T(8,128)S(1)} %shard_map.78.tables, bf16[320,768]{1,0:T(8,128)(2,1)S(1)} %get-tuple-element.143.refs_0_, bf16[320,768]{1,0:T(8,128)(2,1)S(1)} %get-tuple-element.144.refs_1_, bf16[320,768]{1,0:T(8,128)(2,1)S(1)} %get-tuple-element.145.refs_2_, ...), custom_call_target="tpu_custom_call" | custom-call | flops 1509949440 | bytes 4325376 | tf_op jit(solution)/shard_map/pallas_call | solution.py:209
  104.3 5.9 %collective-permute-done.31 = bf16[64,2048]{1,0:T(8,128)(2,1)S(1)} collective-permute-done((bf16[64,2048]{1,0:T(8,128)(2,1)S(1)}, bf16[64,2048]{1,0:T(8,128)(2,1)S(1)}, u32[]{:S(2)}, u32[]{:S(2)}) %collective-permute-start.31) | collective-permute-done | bytes 262176 | tf_op jit(solution)/shard_map/ppermute | solution.py:256
  110.2 1.2 collective-permute-done.34
  111.4 0.1 add_convert_fusion.2
  111.5 1.0 collective-permute-start.35
  112.6 1.5 %collective-permute-start.37 = (bf16[128,2048]{1,0:T(8,128)(2,1)S(1)}, bf16[128,2048]{1,0:T(8,128)(2,1)S(1)}, u32[]{:S(2)}, u32[]{:S(2)}) collective-permute-start(bf16[128,2048]{1,0:T(8,128)(2,1)S(1)} %add_convert_fusion), channel_id=1, source_target_pairs={{0,2},{1,3},{2,0},{3,1},{4,6},{5,7},{6,4},{7,5},{8,10},{9,11},{10,... | collective-permute-start | bytes 1572872 | tf_op jit(solution)/shard_map/ppermute | solution.py:256
  114.1 0.1 add_convert_fusion.1
  114.2 1.1 collective-permute-start.36
  115.3 9.2 %collective-permute-done.35.far_low = bf16[64,2048]{1,0:T(8,128)(2,1)S(1)} collective-permute-done((bf16[64,2048]{1,0:T(8,128)(2,1)S(1)}, bf16[64,2048]{1,0:T(8,128)(2,1)S(1)}, u32[]{:S(2)}, u32[]{:S(2)}) %collective-permute-start.35) | collective-permute-done | bytes 262176 | tf_op jit(solution)/shard_map/ppermute | solution.py:256
  124.5 1.4 %collective-permute-done.36.near_high = bf16[64,2048]{1,0:T(8,128)(2,1)S(1)} collective-permute-done((bf16[64,2048]{1,0:T(8,128)(2,1)S(1)}, bf16[64,2048]{1,0:T(8,128)(2,1)S(1)}, u32[]{:S(2)}, u32[]{:S(2)}) %collective-permute-start.36) | collective-permute-done | bytes 262176 | tf_op jit(solution)/shard_map/ppermute | solution.py:256
  125.9 1.1 shard_map.85
  (59 shorter events, 0.7 us)
Async XLA Ops:
  0.6 24.1 %collective-permute-start = (bf16[128,2048]{1,0:T(8,128)(2,1)}, bf16[128,2048]{1,0:T(8,128)(2,1)S(1)}, u32[]{:S(2)}, u32[]{:S(2)}) collective-permute-start(bf16[128,2048]{1,0:T(8,128)(2,1)} %refs_0_.1), channel_id=1, source_target_pairs={{0,4},{1,5},{2,6},{3,7},{4,0},{5,1},{6,2},{7,3},{8,12},{9,13},{10,... | collective-permute-start | bytes 1572872 | tf_op jit(solution)/shard_map/ppermute | solution.py:256
  3.7 21.0 %collective-permute-start.2 = (bf16[128,2048]{1,0:T(8,128)(2,1)}, bf16[128,2048]{1,0:T(8,128)(2,1)S(1)}, u32[]{:S(2)}, u32[]{:S(2)}) collective-permute-start(bf16[128,2048]{1,0:T(8,128)(2,1)} %refs_0_.1), channel_id=1, source_target_pairs={{0,2},{1,3},{2,0},{3,1},{4,6},{5,7},{6,4},{7,5},{8,10},{9,11},{10,... | collective-permute-start | bytes 1572872 | tf_op jit(solution)/shard_map/ppermute | solution.py:256
  5.2 19.5 %collective-permute-start.3 = (bf16[128,2048]{1,0:T(8,128)(2,1)}, bf16[128,2048]{1,0:T(8,128)(2,1)S(1)}, u32[]{:S(2)}, u32[]{:S(2)}) collective-permute-start(bf16[128,2048]{1,0:T(8,128)(2,1)} %refs_0_.1), channel_id=1, source_target_pairs={{0,1},{1,0},{2,3},{3,2},{4,5},{5,4},{6,7},{7,6},{8,9},{9,8},{10,11... | collective-permute-start | bytes 1572872 | tf_op jit(solution)/shard_map/ppermute | solution.py:256
  5.2 1.1 copy-start.6
  6.3 0.7 copy-start.8
  7.0 0.7 copy-start.9
  7.8 16.9 %collective-permute-start.1 = (bf16[64,2048]{1,0:T(8,128)(2,1)S(1)}, bf16[64,2048]{1,0:T(8,128)(2,1)S(1)}, u32[]{:S(2)}, u32[]{:S(2)}) collective-permute-start(bf16[64,2048]{1,0:T(8,128)(2,1)S(1)} %get-tuple-element.81), channel_id=1, source_target_pairs={{0,8},{1,9},{2,10},{3,11},{4,12},{5,13},{6,14},{7,15},{8,0},{9,1},... | collective-permute-start | bytes 786440 | tf_op jit(solution)/shard_map/ppermute | solution.py:256
  24.7 0.7 copy-start.10
  25.4 2.7 %collective-permute-start.7 = (bf16[128,2048]{1,0:T(8,128)(2,1)S(1)}, bf16[128,2048]{1,0:T(8,128)(2,1)S(1)}, u32[]{:S(2)}, u32[]{:S(2)}) collective-permute-start(bf16[128,2048]{1,0:T(8,128)(2,1)S(1)} %collective-permute-done.2.refs_1_), channel_id=1, source_target_pairs={{0,1},{1,0},{2,3},{3,2},{4,5},{5,4},{6,7},{7,6},{8,9},{9,8},{10,11... | collective-permute-start | bytes 1572872 | tf_op jit(solution)/shard_map/ppermute | solution.py:256
  25.4 15.9 %collective-permute-start.5 = (bf16[128,2048]{1,0:T(8,128)(2,1)S(1)}, bf16[128,2048]{1,0:T(8,128)(2,1)S(1)}, u32[]{:S(2)}, u32[]{:S(2)}) collective-permute-start(bf16[128,2048]{1,0:T(8,128)(2,1)S(1)} %collective-permute-done.refs_0_), channel_id=1, source_target_pairs={{0,2},{1,3},{2,0},{3,1},{4,6},{5,7},{6,4},{7,5},{8,10},{9,11},{10,... | collective-permute-start | bytes 1572872 | tf_op jit(solution)/shard_map/ppermute | solution.py:256
  25.9 15.4 %collective-permute-start.6 = (bf16[128,2048]{1,0:T(8,128)(2,1)S(1)}, bf16[128,2048]{1,0:T(8,128)(2,1)S(1)}, u32[]{:S(2)}, u32[]{:S(2)}) collective-permute-start(bf16[128,2048]{1,0:T(8,128)(2,1)S(1)} %collective-permute-done.refs_0_), channel_id=1, source_target_pairs={{0,1},{1,0},{2,3},{3,2},{4,5},{5,4},{6,7},{7,6},{8,9},{9,8},{10,11... | collective-permute-start | bytes 1572872 | tf_op jit(solution)/shard_map/ppermute | solution.py:256
  26.3 15.1 %collective-permute-start.4 = (bf16[64,2048]{1,0:T(8,128)(2,1)S(1)}, bf16[64,2048]{1,0:T(8,128)(2,1)S(1)}, u32[]{:S(2)}, u32[]{:S(2)}) collective-permute-start(bf16[64,2048]{1,0:T(8,128)(2,1)S(1)} %get-tuple-element.85), channel_id=1, source_target_pairs={{0,8},{1,9},{2,10},{3,11},{4,12},{5,13},{6,14},{7,15},{8,0},{9,1},... | collective-permute-start | bytes 786440 | tf_op jit(solution)/shard_map/ppermute | solution.py:256
  28.2 1.9 %copy-start = (bf16[1,2048,768]{2,1,0:T(8,128)(2,1)S(1)}, bf16[1,2048,768]{2,1,0:T(8,128)(2,1)}, u32[]{:S(2)}) copy-start(bf16[1,2048,768]{2,1,0:T(8,128)(2,1)} %param.9) | copy-start | bytes 9437188
  30.0 1.9 %copy-start.2 = (bf16[1,2048,768]{2,1,0:T(8,128)(2,1)S(1)}, bf16[1,2048,768]{2,1,0:T(8,128)(2,1)}, u32[]{:S(2)}) copy-start(bf16[1,2048,768]{2,1,0:T(8,128)(2,1)} %param.10) | copy-start | bytes 9437188
  31.9 1.9 %copy-start.4 = (bf16[1,768,2048]{2,1,0:T(8,128)(2,1)S(1)}, bf16[1,768,2048]{2,1,0:T(8,128)(2,1)}, u32[]{:S(2)}) copy-start(bf16[1,768,2048]{2,1,0:T(8,128)(2,1)} %param.11) | copy-start | bytes 9437188
  33.8 1.0 copy-start.7
  34.9 6.5 %copy-start.11 = (bf16[64,2048]{1,0:T(8,128)(2,1)S(1)}, bf16[64,2048]{1,0:T(8,128)(2,1)}, u32[]{:S(2)}) copy-start(bf16[64,2048]{1,0:T(8,128)(2,1)} %copy-done.10) | copy-start | bytes 786436
  34.9 8.4 %copy-start.1 = (bf16[1,2048,768]{2,1,0:T(8,128)(2,1)S(1)}, bf16[1,2048,768]{2,1,0:T(8,128)(2,1)}, u32[]{:S(2)}) copy-start(bf16[1,2048,768]{2,1,0:T(8,128)(2,1)} %param.9) | copy-start | bytes 9437188
  34.9 8.4 %copy-start.3 = (bf16[1,2048,768]{2,1,0:T(8,128)(2,1)S(1)}, bf16[1,2048,768]{2,1,0:T(8,128)(2,1)}, u32[]{:S(2)}) copy-start(bf16[1,2048,768]{2,1,0:T(8,128)(2,1)} %param.10) | copy-start | bytes 9437188
  34.9 8.4 %copy-start.5 = (bf16[1,768,2048]{2,1,0:T(8,128)(2,1)S(1)}, bf16[1,768,2048]{2,1,0:T(8,128)(2,1)}, u32[]{:S(2)}) copy-start(bf16[1,768,2048]{2,1,0:T(8,128)(2,1)} %param.11) | copy-start | bytes 9437188
  41.3 1.9 %collective-permute-start.11 = (bf16[128,2048]{1,0:T(8,128)(2,1)S(1)}, bf16[128,2048]{1,0:T(8,128)(2,1)S(1)}, u32[]{:S(2)}, u32[]{:S(2)}) collective-permute-start(bf16[128,2048]{1,0:T(8,128)(2,1)S(1)} %collective-permute-done.5.refs_1_), channel_id=1, source_target_pairs={{0,1},{1,0},{2,3},{3,2},{4,5},{5,4},{6,7},{7,6},{8,9},{9,8},{10,11... | collective-permute-start | bytes 1572872 | tf_op jit(solution)/shard_map/ppermute | solution.py:256
  41.4 14.4 %collective-permute-start.8 = (bf16[128,2048]{1,0:T(8,128)(2,1)S(1)}, bf16[128,2048]{1,0:T(8,128)(2,1)S(1)}, u32[]{:S(2)}, u32[]{:S(2)}) collective-permute-start(bf16[128,2048]{1,0:T(8,128)(2,1)S(1)} %constant_dynamic-update-slice_fusion.refs_0_), channel_id=1, source_target_pairs={{0,4},{1,5},{2,6},{3,7},{4,0},{5,1},{6,2},{7,3},{8,12},{9,13},{10,... | collective-permute-start | bytes 1572872 | tf_op jit(solution)/shard_map/ppermute | solution.py:256
  42.1 14.0 %collective-permute-start.9 = (bf16[128,2048]{1,0:T(8,128)(2,1)S(1)}, bf16[128,2048]{1,0:T(8,128)(2,1)S(1)}, u32[]{:S(2)}, u32[]{:S(2)}) collective-permute-start(bf16[128,2048]{1,0:T(8,128)(2,1)S(1)} %constant_dynamic-update-slice_fusion.refs_0_), channel_id=1, source_target_pairs={{0,2},{1,3},{2,0},{3,1},{4,6},{5,7},{6,4},{7,5},{8,10},{9,11},{10,... | collective-permute-start | bytes 1572872 | tf_op jit(solution)/shard_map/ppermute | solution.py:256
  43.2 12.9 %collective-permute-start.10 = (bf16[128,2048]{1,0:T(8,128)(2,1)S(1)}, bf16[128,2048]{1,0:T(8,128)(2,1)S(1)}, u32[]{:S(2)}, u32[]{:S(2)}) collective-permute-start(bf16[128,2048]{1,0:T(8,128)(2,1)S(1)} %constant_dynamic-update-slice_fusion.refs_0_), channel_id=1, source_target_pairs={{0,1},{1,0},{2,3},{3,2},{4,5},{5,4},{6,7},{7,6},{8,9},{9,8},{10,11... | collective-permute-start | bytes 1572872 | tf_op jit(solution)/shard_map/ppermute | solution.py:256
  48.7 7.4 %collective-permute-start.12 = (bf16[128,2048]{1,0:T(8,128)(2,1)S(1)}, bf16[128,2048]{1,0:T(8,128)(2,1)S(1)}, u32[]{:S(2)}, u32[]{:S(2)}) collective-permute-start(bf16[128,2048]{1,0:T(8,128)(2,1)S(1)} %get-tuple-element.100), channel_id=1, source_target_pairs={{0,1},{1,0},{2,3},{3,2},{4,5},{5,4},{6,7},{7,6},{8,9},{9,8},{10,11... | collective-permute-start | bytes 1572872 | tf_op jit(solution)/shard_map/ppermute | solution.py:256
  56.1 3.6 %collective-permute-start.17 = (bf16[128,2048]{1,0:T(8,128)(2,1)S(1)}, bf16[128,2048]{1,0:T(8,128)(2,1)S(1)}, u32[]{:S(2)}, u32[]{:S(2)}) collective-permute-start(bf16[128,2048]{1,0:T(8,128)(2,1)S(1)} %collective-permute-done.9.refs_1_), channel_id=1, source_target_pairs={{0,1},{1,0},{2,3},{3,2},{4,5},{5,4},{6,7},{7,6},{8,9},{9,8},{10,11... | collective-permute-start | bytes 1572872 | tf_op jit(solution)/shard_map/ppermute | solution.py:256
  56.1 12.6 %collective-permute-start.15 = (bf16[256,2048]{1,0:T(8,128)(2,1)S(1)}, bf16[256,2048]{1,0:T(8,128)(2,1)S(1)}, u32[]{:S(2)}, u32[]{:S(2)}) collective-permute-start(bf16[256,2048]{1,0:T(8,128)(2,1)S(1)} %get-tuple-element.104), channel_id=1, source_target_pairs={{0,1},{1,0},{2,3},{3,2},{4,5},{5,4},{6,7},{7,6},{8,9},{9,8},{10,11... | collective-permute-start | bytes 3145736 | tf_op jit(solution)/shard_map/ppermute | solution.py:256
  56.6 13.9 %collective-permute-start.13 = (bf16[128,2048]{1,0:T(8,128)(2,1)S(1)}, bf16[128,2048]{1,0:T(8,128)(2,1)S(1)}, u32[]{:S(2)}, u32[]{:S(2)}) collective-permute-start(bf16[128,2048]{1,0:T(8,128)(2,1)S(1)} %collective-permute-done.9.refs_1_), channel_id=1, source_target_pairs={{0,4},{1,5},{2,6},{3,7},{4,0},{5,1},{6,2},{7,3},{8,12},{9,13},{10,... | collective-permute-start | bytes 1572872 | tf_op jit(solution)/shard_map/ppermute | solution.py:256
  58.1 7.6 %collective-permute-start.19 = (bf16[128,2048]{1,0:T(8,128)(2,1)S(1)}, bf16[128,2048]{1,0:T(8,128)(2,1)S(1)}, u32[]{:S(2)}, u32[]{:S(2)}) collective-permute-start(bf16[128,2048]{1,0:T(8,128)(2,1)S(1)} %collective-permute-done.8.refs_0_), channel_id=1, source_target_pairs={{0,1},{1,0},{2,3},{3,2},{4,5},{5,4},{6,7},{7,6},{8,9},{9,8},{10,11... | collective-permute-start | bytes 1572872 | tf_op jit(solution)/shard_map/ppermute | solution.py:256
  58.2 10.5 %collective-permute-start.14 = (bf16[64,2048]{1,0:T(8,128)(2,1)S(1)}, bf16[64,2048]{1,0:T(8,128)(2,1)S(1)}, u32[]{:S(2)}, u32[]{:S(2)}) collective-permute-start(bf16[64,2048]{1,0:T(8,128)(2,1)S(1)} %get-tuple-element.161), channel_id=1, source_target_pairs={{0,2},{1,3},{2,0},{3,1},{4,6},{5,7},{6,4},{7,5},{8,10},{9,11},{10,... | collective-permute-start | bytes 786440 | tf_op jit(solution)/shard_map/ppermute | solution.py:256
  59.7 10.8 %collective-permute-start.16 = (bf16[128,2048]{1,0:T(8,128)(2,1)S(1)}, bf16[128,2048]{1,0:T(8,128)(2,1)S(1)}, u32[]{:S(2)}, u32[]{:S(2)}) collective-permute-start(bf16[128,2048]{1,0:T(8,128)(2,1)S(1)} %get-tuple-element.105), channel_id=1, source_target_pairs={{0,1},{1,0},{2,3},{3,2},{4,5},{5,4},{6,7},{7,6},{8,9},{9,8},{10,11... | collective-permute-start | bytes 1572872 | tf_op jit(solution)/shard_map/ppermute | solution.py:256
  65.6 4.9 %collective-permute-start.18 = (bf16[64,2048]{1,0:T(8,128)(2,1)S(1)}, bf16[64,2048]{1,0:T(8,128)(2,1)S(1)}, u32[]{:S(2)}, u32[]{:S(2)}) collective-permute-start(bf16[64,2048]{1,0:T(8,128)(2,1)S(1)} %get-tuple-element.107), channel_id=1, source_target_pairs={{0,1},{1,0},{2,3},{3,2},{4,5},{5,4},{6,7},{7,6},{8,9},{9,8},{10,11... | collective-permute-start | bytes 786440 | tf_op jit(solution)/shard_map/ppermute | solution.py:256
  70.5 1.9 %collective-permute-start.20 = (bf16[128,2048]{1,0:T(8,128)(2,1)S(1)}, bf16[128,2048]{1,0:T(8,128)(2,1)S(1)}, u32[]{:S(2)}, u32[]{:S(2)}) collective-permute-start(bf16[128,2048]{1,0:T(8,128)(2,1)S(1)} %collective-permute-done.13.refs_0_), channel_id=1, source_target_pairs={{0,1},{1,0},{2,3},{3,2},{4,5},{5,4},{6,7},{7,6},{8,9},{9,8},{10,11... | collective-permute-start | bytes 1572872 | tf_op jit(solution)/shard_map/ppermute | solution.py:256
  70.5 8.9 %collective-permute-start.23 = (bf16[128,2048]{1,0:T(8,128)(2,1)S(1)}, bf16[128,2048]{1,0:T(8,128)(2,1)S(1)}, u32[]{:S(2)}, u32[]{:S(2)}) collective-permute-start(bf16[128,2048]{1,0:T(8,128)(2,1)S(1)} %get-tuple-element.123), channel_id=1, source_target_pairs={{0,1},{1,0},{2,3},{3,2},{4,5},{5,4},{6,7},{7,6},{8,9},{9,8},{10,11... | collective-permute-start | bytes 1572872 | tf_op jit(solution)/shard_map/ppermute | solution.py:256
  71.1 8.3 %collective-permute-start.24 = (bf16[64,2048]{1,0:T(8,128)(2,1)S(1)}, bf16[64,2048]{1,0:T(8,128)(2,1)S(1)}, u32[]{:S(2)}, u32[]{:S(2)}) collective-permute-start(bf16[64,2048]{1,0:T(8,128)(2,1)S(1)} %add_convert_fusion.11), channel_id=1, source_target_pairs={{0,2},{1,3},{2,0},{3,1},{4,6},{5,7},{6,4},{7,5},{8,10},{9,11},{10,... | collective-permute-start | bytes 786440 | tf_op jit(solution)/shard_map/ppermute | solution.py:256
  72.4 11.4 %collective-permute-start.29 = (bf16[64,2048]{1,0:T(8,128)(2,1)S(1)}, bf16[64,2048]{1,0:T(8,128)(2,1)S(1)}, u32[]{:S(2)}, u32[]{:S(2)}) collective-permute-start(bf16[64,2048]{1,0:T(8,128)(2,1)S(1)} %get-tuple-element.135), channel_id=1, source_target_pairs={{0,1},{1,0},{2,3},{3,2},{4,5},{5,4},{6,7},{7,6},{8,9},{9,8},{10,11... | collective-permute-start | bytes 786440 | tf_op jit(solution)/shard_map/ppermute | solution.py:256
  75.2 4.3 %collective-permute-start.21 = (bf16[64,2048]{1,0:T(8,128)(2,1)S(1)}, bf16[64,2048]{1,0:T(8,128)(2,1)S(1)}, u32[]{:S(2)}, u32[]{:S(2)}) collective-permute-start(bf16[64,2048]{1,0:T(8,128)(2,1)S(1)} %get-tuple-element.120), channel_id=1, source_target_pairs={{0,1},{1,0},{2,3},{3,2},{4,5},{5,4},{6,7},{7,6},{8,9},{9,8},{10,11... | collective-permute-start | bytes 786440 | tf_op jit(solution)/shard_map/ppermute | solution.py:256
  75.7 3.7 %collective-permute-start.22 = (bf16[64,2048]{1,0:T(8,128)(2,1)S(1)}, bf16[64,2048]{1,0:T(8,128)(2,1)S(1)}, u32[]{:S(2)}, u32[]{:S(2)}) collective-permute-start(bf16[64,2048]{1,0:T(8,128)(2,1)S(1)} %get-tuple-element.121), channel_id=1, source_target_pairs={{0,1},{1,0},{2,3},{3,2},{4,5},{5,4},{6,7},{7,6},{8,9},{9,8},{10,11... | collective-permute-start | bytes 786440 | tf_op jit(solution)/shard_map/ppermute | solution.py:256
  79.5 5.0 %collective-permute-start.30 = (bf16[128,2048]{1,0:T(8,128)(2,1)S(1)}, bf16[128,2048]{1,0:T(8,128)(2,1)S(1)}, u32[]{:S(2)}, u32[]{:S(2)}) collective-permute-start(bf16[128,2048]{1,0:T(8,128)(2,1)S(1)} %get-tuple-element.136), channel_id=1, source_target_pairs={{0,1},{1,0},{2,3},{3,2},{4,5},{5,4},{6,7},{7,6},{8,9},{9,8},{10,11... | collective-permute-start | bytes 1572872 | tf_op jit(solution)/shard_map/ppermute | solution.py:256
  79.6 15.4 %collective-permute-start.25 = (bf16[64,2048]{1,0:T(8,128)(2,1)S(1)}, bf16[64,2048]{1,0:T(8,128)(2,1)S(1)}, u32[]{:S(2)}, u32[]{:S(2)}) collective-permute-start(bf16[64,2048]{1,0:T(8,128)(2,1)S(1)} %add_convert_fusion.9), channel_id=1, source_target_pairs={{0,8},{1,9},{2,10},{3,11},{4,12},{5,13},{6,14},{7,15},{8,0},{9,1},... | collective-permute-start | bytes 786440 | tf_op jit(solution)/shard_map/ppermute | solution.py:256
  81.7 13.3 %collective-permute-start.26 = (bf16[64,2048]{1,0:T(8,128)(2,1)S(1)}, bf16[64,2048]{1,0:T(8,128)(2,1)S(1)}, u32[]{:S(2)}, u32[]{:S(2)}) collective-permute-start(bf16[64,2048]{1,0:T(8,128)(2,1)S(1)} %get-tuple-element.165), channel_id=1, source_target_pairs={{0,2},{1,3},{2,0},{3,1},{4,6},{5,7},{6,4},{7,5},{8,10},{9,11},{10,... | collective-permute-start | bytes 786440 | tf_op jit(solution)/shard_map/ppermute | solution.py:256
  82.8 13.1 %collective-permute-start.27 = (bf16[64,2048]{1,0:T(8,128)(2,1)S(1)}, bf16[64,2048]{1,0:T(8,128)(2,1)S(1)}, u32[]{:S(2)}, u32[]{:S(2)}) collective-permute-start(bf16[64,2048]{1,0:T(8,128)(2,1)S(1)} %get-tuple-element.164), channel_id=1, source_target_pairs={{0,2},{1,3},{2,0},{3,1},{4,6},{5,7},{6,4},{7,5},{8,10},{9,11},{10,... | collective-permute-start | bytes 786440 | tf_op jit(solution)/shard_map/ppermute | solution.py:256
  83.8 12.5 %collective-permute-start.28 = (bf16[64,2048]{1,0:T(8,128)(2,1)S(1)}, bf16[64,2048]{1,0:T(8,128)(2,1)S(1)}, u32[]{:S(2)}, u32[]{:S(2)}) collective-permute-start(bf16[64,2048]{1,0:T(8,128)(2,1)S(1)} %add_convert_fusion.10), channel_id=1, source_target_pairs={{0,4},{1,5},{2,6},{3,7},{4,0},{5,1},{6,2},{7,3},{8,12},{9,13},{10,... | collective-permute-start | bytes 786440 | tf_op jit(solution)/shard_map/ppermute | solution.py:256
  96.6 13.6 %collective-permute-start.31 = (bf16[64,2048]{1,0:T(8,128)(2,1)S(1)}, bf16[64,2048]{1,0:T(8,128)(2,1)S(1)}, u32[]{:S(2)}, u32[]{:S(2)}) collective-permute-start(bf16[64,2048]{1,0:T(8,128)(2,1)S(1)} %get-tuple-element.163), channel_id=1, source_target_pairs={{0,8},{1,9},{2,10},{3,11},{4,12},{5,13},{6,14},{7,15},{8,0},{9,1},... | collective-permute-start | bytes 786440 | tf_op jit(solution)/shard_map/ppermute | solution.py:256
  97.1 13.1 %collective-permute-start.32 = (bf16[64,2048]{1,0:T(8,128)(2,1)S(1)}, bf16[64,2048]{1,0:T(8,128)(2,1)S(1)}, u32[]{:S(2)}, u32[]{:S(2)}) collective-permute-start(bf16[64,2048]{1,0:T(8,128)(2,1)S(1)} %get-tuple-element.162), channel_id=1, source_target_pairs={{0,4},{1,5},{2,6},{3,7},{4,0},{5,1},{6,2},{7,3},{8,12},{9,13},{10,... | collective-permute-start | bytes 786440 | tf_op jit(solution)/shard_map/ppermute | solution.py:256
  99.0 11.2 %collective-permute-start.33 = (bf16[64,2048]{1,0:T(8,128)(2,1)S(1)}, bf16[64,2048]{1,0:T(8,128)(2,1)S(1)}, u32[]{:S(2)}, u32[]{:S(2)}) collective-permute-start(bf16[64,2048]{1,0:T(8,128)(2,1)S(1)} %add_convert_fusion.3), channel_id=1, source_target_pairs={{0,2},{1,3},{2,0},{3,1},{4,6},{5,7},{6,4},{7,5},{8,10},{9,11},{10,... | collective-permute-start | bytes 786440 | tf_op jit(solution)/shard_map/ppermute | solution.py:256
  101.1 10.3 %collective-permute-start.34 = (bf16[64,2048]{1,0:T(8,128)(2,1)S(1)}, bf16[64,2048]{1,0:T(8,128)(2,1)S(1)}, u32[]{:S(2)}, u32[]{:S(2)}) collective-permute-start(bf16[64,2048]{1,0:T(8,128)(2,1)S(1)} %get-tuple-element.141), channel_id=1, source_target_pairs={{0,2},{1,3},{2,0},{3,1},{4,6},{5,7},{6,4},{7,5},{8,10},{9,11},{10,... | collective-permute-start | bytes 786440 | tf_op jit(solution)/shard_map/ppermute | solution.py:256
  111.5 13.0 %collective-permute-start.35 = (bf16[64,2048]{1,0:T(8,128)(2,1)S(1)}, bf16[64,2048]{1,0:T(8,128)(2,1)S(1)}, u32[]{:S(2)}, u32[]{:S(2)}) collective-permute-start(bf16[64,2048]{1,0:T(8,128)(2,1)S(1)} %add_convert_fusion.2), channel_id=1, source_target_pairs={{0,8},{1,9},{2,10},{3,11},{4,12},{5,13},{6,14},{7,15},{8,0},{9,1},... | collective-permute-start | bytes 786440 | tf_op jit(solution)/shard_map/ppermute | solution.py:256
  112.6 13.4 %collective-permute-start.37 = (bf16[128,2048]{1,0:T(8,128)(2,1)S(1)}, bf16[128,2048]{1,0:T(8,128)(2,1)S(1)}, u32[]{:S(2)}, u32[]{:S(2)}) collective-permute-start(bf16[128,2048]{1,0:T(8,128)(2,1)S(1)} %add_convert_fusion), channel_id=1, source_target_pairs={{0,2},{1,3},{2,0},{3,1},{4,6},{5,7},{6,4},{7,5},{8,10},{9,11},{10,... | collective-permute-start | bytes 1572872 | tf_op jit(solution)/shard_map/ppermute | solution.py:256
  114.2 11.7 %collective-permute-start.36 = (bf16[64,2048]{1,0:T(8,128)(2,1)S(1)}, bf16[64,2048]{1,0:T(8,128)(2,1)S(1)}, u32[]{:S(2)}, u32[]{:S(2)}) collective-permute-start(bf16[64,2048]{1,0:T(8,128)(2,1)S(1)} %add_convert_fusion.1), channel_id=1, source_target_pairs={{0,4},{1,5},{2,6},{3,7},{4,0},{5,1},{6,2},{7,3},{8,12},{9,13},{10,... | collective-permute-start | bytes 786440 | tf_op jit(solution)/shard_map/ppermute | solution.py:256

commit v26 on v25

--- a/solution.py
+++ b/solution.py
@@ -329,18 +329,18 @@
         3, b3, d3, pieces=(half, half), picked=(1, 3)
     )
     got3_low, got3_high = sibling(give3_low), sibling(give3_high)
-    keep3_side, got3_low, got3_high, act4, got2, side_high, near1 = together(
-        keep3_side, got3_low, got3_high, act4, got2, side_high, near1
+    near1_low = pair(near1)
+    side_high, near1_low, keep3_side, got3_low, got3_high, act4, got2 = together(
+        side_high, near1_low, keep3_side, got3_low, got3_high, act4, got2
     )
     got2_low, got3 = sibling(give2_low), sibling(give3)
     far2_high = far(summed(keep2[half:tok], got2[half:], side_high))
     came3_low = column(summed(keep3_side[:half], got3_low))
     came3_high = column(summed(keep3_side[half:], got3_high))
-    near1_low = pair(near1)
     side0 = summed(keep0[tok:], got0[tok:])
     side1 = summed(keep1[tok + half :], got1_side[half:])
-    far2_high, came3_low, came3_high, near1_low, side0, side1, got2_low, got3 = together(
-        far2_high, came3_low, came3_high, near1_low, side0, side1, got2_low, got3
+    far2_high, came3_low, came3_high, side0, side1, got2_low, got3 = together(
+        far2_high, came3_low, came3_high, side0, side1, got2_low, got3
     )
     far3_high = far(summed(keep3[half:], got3[half:], came3_high))
     pair3_low = pair(summed(keep3[:half], got3[:half], came3_low))

time: 127 us -> 128 us (level)
  no operation moved by 1% of the time
where the time goes in v26:
time: 128 us
  waiting for transfers between devices  42.8 us (33%)
  starting transfers between devices  31.5 us (25%)
  Pallas kernels  27.1 us (21%)
  blocking collectives  14.2 us (11%)
  local copies, waits for them, and re-layouts  9.97 us (8%)
    ppermute x38, waiting for transfers between devices, swapped(): return lax.ppermute(array, 'expert', [(i, i ^ bit) for i in range(size)])  42.8 us
    ppermute x38, starting transfers between devices, swapped(): return lax.ppermute(array, 'expert', [(i, i ^ bit) for i in range(size)])  31.5 us
    pallas_call x5, Pallas kernels, plane_pass(): pl.pallas_call(functools.partial(plane_kernel, k, picked, len(pieces)), o...  22 us
    all_to_all x1, blocking collectives, staged(): lax.all_to_all(mine, 'expert', split_axis=0, concat_axis=0, tiled=True)  14.2 us
    unnamed x25, local copies, waits for them, and re-layouts  9.86 us
    pallas_call x1, Pallas kernels, gram_pass(): pl.pallas_call(gram_kernel, out_shape=jax.ShapeDtypeStruct((hidden, hidde...  3.14 us
  transfers between devices with their start and end apart: 38, of which 12 were waited for; matrix products, arithmetic and copies ran while one was open for 1% of the time, Pallas kernels for 20%

profile of v26, /device:TPU:0, one launch (start us, length us, event | category | flops | bytes accessed | tf_op | source)
XLA Modules:
  0.0 127.7 jit_solution(3865252213681831577)
XLA Ops:
  0.6 3.1 %collective-permute-start = (bf16[128,2048]{1,0:T(8,128)(2,1)}, bf16[128,2048]{1,0:T(8,128)(2,1)S(1)}, u32[]{:S(2)}, u32[]{:S(2)}) collective-permute-start(bf16[128,2048]{1,0:T(8,128)(2,1)} %refs_0_.1), channel_id=1, source_target_pairs={{0,4},{1,5},{2,6},{3,7},{4,0},{5,1},{6,2},{7,3},{8,12},{9,13},{10,... | collective-permute-start | bytes 1572872 | tf_op jit(solution)/shard_map/ppermute | solution.py:256
  3.7 1.5 %collective-permute-start.2 = (bf16[128,2048]{1,0:T(8,128)(2,1)}, bf16[128,2048]{1,0:T(8,128)(2,1)S(1)}, u32[]{:S(2)}, u32[]{:S(2)}) collective-permute-start(bf16[128,2048]{1,0:T(8,128)(2,1)} %refs_0_.1), channel_id=1, source_target_pairs={{0,2},{1,3},{2,0},{3,1},{4,6},{5,7},{6,4},{7,5},{8,10},{9,11},{10,... | collective-permute-start | bytes 1572872 | tf_op jit(solution)/shard_map/ppermute | solution.py:256
  5.2 1.1 copy-done.6
  6.3 0.7 copy-done.8
  7.0 0.7 copy-done.9
  7.7 0.1 shard_map.77
  7.8 2.7 %collective-permute-start.1 = (bf16[64,2048]{1,0:T(8,128)(2,1)S(1)}, bf16[64,2048]{1,0:T(8,128)(2,1)S(1)}, u32[]{:S(2)}, u32[]{:S(2)}) collective-permute-start(bf16[64,2048]{1,0:T(8,128)(2,1)S(1)} %get-tuple-element.80), channel_id=1, source_target_pairs={{0,8},{1,9},{2,10},{3,11},{4,12},{5,13},{6,14},{7,15},{8,0},{9,1},... | collective-permute-start | bytes 786440 | tf_op jit(solution)/shard_map/ppermute | solution.py:256
  10.5 14.2 %all_to_all.12 = f32[16,1,128]{2,1,0:T(1,128)S(1)} all-to-all(f32[16,1,128]{2,1,0:T(1,128)S(1)} %bitcast.42), channel_id=1, replica_groups=mesh['parts'=2,'expert'=16] {'expert'}, dimensions={0} | all-to-all | bytes 16384 | tf_op jit(solution)/shard_map/all_to_all | solution.py:285
  24.8 0.7 copy-done.10
  25.4 0.5 collective-permute-start.5
  25.9 0.2 collective-permute-start.6
  26.3 1.1 collective-permute-start.4
  27.4 0.7 shard_map.78.tables
  28.2 1.9 %copy-done = bf16[1,2048,768]{2,1,0:T(8,128)(2,1)S(1)} copy-done((bf16[1,2048,768]{2,1,0:T(8,128)(2,1)S(1)}, bf16[1,2048,768]{2,1,0:T(8,128)(2,1)}, u32[]{:S(2)}) %copy-start) | copy-done | bytes 3145752
  30.0 1.9 %copy-done.2 = bf16[1,2048,768]{2,1,0:T(8,128)(2,1)S(1)} copy-done((bf16[1,2048,768]{2,1,0:T(8,128)(2,1)S(1)}, bf16[1,2048,768]{2,1,0:T(8,128)(2,1)}, u32[]{:S(2)}) %copy-start.2) | copy-done | bytes 3145752
  31.9 1.9 %copy-done.4 = bf16[1,768,2048]{2,1,0:T(8,128)(2,1)S(1)} copy-done((bf16[1,768,2048]{2,1,0:T(8,128)(2,1)S(1)}, bf16[1,768,2048]{2,1,0:T(8,128)(2,1)}, u32[]{:S(2)}) %copy-start.4) | copy-done | bytes 3145752
  33.8 1.0 copy-done.7
  34.9 5.5 %shard_map.79 = (bf16[256,2048]{1,0:T(8,128)(2,1)S(1)}, bf16[256,2048]{1,0:T(8,128)(2,1)S(1)}, bf16[320,768]{1,0:T(8,128)(2,1)S(1)}) custom-call(f32[16,512]{1,0:T(8,128)S(1)} %shard_map.78.tables, bf16[128,2048]{1,0:T(8,128)(2,1)S(1)} %copy-done.7, bf16[128,2048]{1,0:T(8,128)(2,1)S(1)} %collective-permute-done.2.refs_1_, ...), custom_call_target="tpu_custom_call" | custom-call | flops 4362076160 | bytes 13631488 | tf_op jit(solution)/shard_map/pallas_call | solution.py:178
  40.4 1.0 collective-permute-done.4
  41.4 0.7 collective-permute-start.8
  42.1 1.1 collective-permute-start.9
  43.3 5.5 %shard_map.80 = (bf16[256,2048]{1,0:T(8,128)(2,1)S(1)}, bf16[128,2048]{1,0:T(8,128)(2,1)S(1)}, bf16[128,2048]{1,0:T(8,128)(2,1)S(1)}, bf16[320,768]{1,0:T(8,128)(2,1)S(1)}) custom-call(f32[16,512]{1,0:T(8,128)S(1)} %shard_map.78.tables, bf16[128,2048]{1,0:T(8,128)(2,1)S(1)} %collective-permute-done.refs_0_, ...), custom_call_target="tpu_custom_call" | custom-call | flops 4362076160 | bytes 13631488 | tf_op jit(solution)/shard_map/pallas_call | solution.py:178
  48.7 0.5 collective-permute-start.12
  49.3 6.5 %collective-permute-done.8.refs_0_ = bf16[128,2048]{1,0:T(8,128)(2,1)S(1)} collective-permute-done((bf16[128,2048]{1,0:T(8,128)(2,1)S(1)}, bf16[128,2048]{1,0:T(8,128)(2,1)S(1)}, u32[]{:S(2)}, u32[]{:S(2)}) %collective-permute-start.8) | collective-permute-done | bytes 524320 | tf_op jit(solution)/shard_map/ppermute | solution.py:256
  55.8 0.3 collective-permute-done.9.refs_1_
  56.1 0.5 collective-permute-start.15
  56.6 1.4 %collective-permute-start.13 = (bf16[128,2048]{1,0:T(8,128)(2,1)S(1)}, bf16[128,2048]{1,0:T(8,128)(2,1)S(1)}, u32[]{:S(2)}, u32[]{:S(2)}) collective-permute-start(bf16[128,2048]{1,0:T(8,128)(2,1)S(1)} %collective-permute-done.9.refs_1_), channel_id=1, source_target_pairs={{0,4},{1,5},{2,6},{3,7},{4,0},{5,1},{6,2},{7,3},{8,12},{9,13},{10,... | collective-permute-start | bytes 1572872 | tf_op jit(solution)/shard_map/ppermute | solution.py:256
  58.1 0.1 add_convert_fusion.6
  58.2 1.5 %collective-permute-start.14 = (bf16[64,2048]{1,0:T(8,128)(2,1)S(1)}, bf16[64,2048]{1,0:T(8,128)(2,1)S(1)}, u32[]{:S(2)}, u32[]{:S(2)}) collective-permute-start(bf16[64,2048]{1,0:T(8,128)(2,1)S(1)} %get-tuple-element.159), channel_id=1, source_target_pairs={{0,2},{1,3},{2,0},{3,1},{4,6},{5,7},{6,4},{7,5},{8,10},{9,11},{10,... | collective-permute-start | bytes 786440 | tf_op jit(solution)/shard_map/ppermute | solution.py:256
  59.7 0.2 collective-permute-start.16
  60.0 5.7 %shard_map.81 = (bf16[256,2048]{1,0:T(8,128)(2,1)S(1)}, bf16[128,2048]{1,0:T(8,128)(2,1)S(1)}, bf16[64,2048]{1,0:T(8,128)(2,1)S(1)}, bf16[64,2048]{1,0:T(8,128)(2,1)S(1)}, bf16[320,768]{1,0:T(8,128)(2,1)S(1)}) custom-call(f32[16,512]{1,0:T(8,128)S(1)} %shard_map.78.tables, bf16[128,2048]{1,0:T(8,128)(2,1)S(1)} %constant_dynamic-update-slice_fusion.refs_0_, ...), custom_call_target="tpu_custom_call" | custom-call | flops 4362076160 | bytes 13631488 | tf_op jit(solution)/shard_map/pallas_call | solution.py:178
  65.6 0.3 collective-permute-start.18
  66.0 2.7 %shard_map.82 = (bf16[128,2048]{1,0:T(8,128)(2,1)S(1)}, bf16[128,2048]{1,0:T(8,128)(2,1)S(1)}, bf16[160,768]{1,0:T(8,128)(2,1)S(1)}) custom-call(f32[16,512]{1,0:T(8,128)S(1)} %shard_map.78.tables, bf16[128,2048]{1,0:T(8,128)(2,1)S(1)} %collective-permute-done.8.refs_0_, bf16[128,2048]{1,0:T(8,128)(2,1)S(1)} %collective-permute-done.19.refs_1_, ...), custom_call_target="tpu_custom_call" | custom-call | flops 1845493760 | bytes 11534336 | tf_op jit(solution)/shard_map/pallas_call | solution.py:178
  68.7 1.8 %collective-permute-done.13.refs_0_ = bf16[128,2048]{1,0:T(8,128)(2,1)S(1)} collective-permute-done((bf16[128,2048]{1,0:T(8,128)(2,1)S(1)}, bf16[128,2048]{1,0:T(8,128)(2,1)S(1)}, u32[]{:S(2)}, u32[]{:S(2)}) %collective-permute-start.13) | collective-permute-done | bytes 524320 | tf_op jit(solution)/shard_map/ppermute | solution.py:256
  70.6 1.3 %collective-permute-start.20 = (bf16[64,2048]{1,0:T(8,128)(2,1)S(1)}, bf16[64,2048]{1,0:T(8,128)(2,1)S(1)}, u32[]{:S(2)}, u32[]{:S(2)}) collective-permute-start(bf16[64,2048]{1,0:T(8,128)(2,1)S(1)} %add_convert_fusion.11), channel_id=1, source_target_pairs={{0,2},{1,3},{2,0},{3,1},{4,6},{5,7},{6,4},{7,5},{8,10},{9,11},{10,... | collective-permute-start | bytes 786440 | tf_op jit(solution)/shard_map/ppermute | solution.py:256
  71.9 0.2 collective-permute-start.25
  72.3 1.7 %collective-permute-start.21 = (bf16[64,2048]{1,0:T(8,128)(2,1)S(1)}, bf16[64,2048]{1,0:T(8,128)(2,1)S(1)}, u32[]{:S(2)}, u32[]{:S(2)}) collective-permute-start(bf16[64,2048]{1,0:T(8,128)(2,1)S(1)} %add_convert_fusion.10), channel_id=1, source_target_pairs={{0,4},{1,5},{2,6},{3,7},{4,0},{5,1},{6,2},{7,3},{8,12},{9,13},{10,... | collective-permute-start | bytes 786440 | tf_op jit(solution)/shard_map/ppermute | solution.py:256
  74.0 2.7 %shard_map.83 = (bf16[128,2048]{1,0:T(8,128)(2,1)S(1)}, bf16[64,2048]{1,0:T(8,128)(2,1)S(1)}, bf16[64,2048]{1,0:T(8,128)(2,1)S(1)}, bf16[160,768]{1,0:T(8,128)(2,1)S(1)}) custom-call(f32[16,512]{1,0:T(8,128)S(1)} %shard_map.78.tables, bf16[128,2048]{1,0:T(8,128)(2,1)S(1)} %collective-permute-done.13.refs_0_, ...), custom_call_target="tpu_custom_call" | custom-call | flops 1845493760 | bytes 11534336 | tf_op jit(solution)/shard_map/pallas_call | solution.py:178
  76.8 0.5 collective-permute-start.24
  77.3 2.1 %collective-permute-done.20 = bf16[64,2048]{1,0:T(8,128)(2,1)S(1)} collective-permute-done((bf16[64,2048]{1,0:T(8,128)(2,1)S(1)}, bf16[64,2048]{1,0:T(8,128)(2,1)S(1)}, u32[]{:S(2)}, u32[]{:S(2)}) %collective-permute-start.20) | collective-permute-done | bytes 262176 | tf_op jit(solution)/shard_map/ppermute | solution.py:256
  79.4 1.4 %collective-permute-done.21.near_low = bf16[64,2048]{1,0:T(8,128)(2,1)S(1)} collective-permute-done((bf16[64,2048]{1,0:T(8,128)(2,1)S(1)}, bf16[64,2048]{1,0:T(8,128)(2,1)S(1)}, u32[]{:S(2)}, u32[]{:S(2)}) %collective-permute-start.21) | collective-permute-done | bytes 262176 | tf_op jit(solution)/shard_map/ppermute | solution.py:256
  81.0 1.7 %collective-permute-start.26 = (bf16[64,2048]{1,0:T(8,128)(2,1)S(1)}, bf16[64,2048]{1,0:T(8,128)(2,1)S(1)}, u32[]{:S(2)}, u32[]{:S(2)}) collective-permute-start(bf16[64,2048]{1,0:T(8,128)(2,1)S(1)} %add_convert_fusion.9), channel_id=1, source_target_pairs={{0,8},{1,9},{2,10},{3,11},{4,12},{5,13},{6,14},{7,15},{8,0},{9,1},... | collective-permute-start | bytes 786440 | tf_op jit(solution)/shard_map/ppermute | solution.py:256
  82.7 0.1 add_convert_fusion.7
  82.8 1.1 collective-permute-start.27
  83.9 1.0 collective-permute-start.28
  84.9 0.1 add_convert_fusion
  85.1 11.2 %collective-permute-done.26.far_high = bf16[64,2048]{1,0:T(8,128)(2,1)S(1)} collective-permute-done((bf16[64,2048]{1,0:T(8,128)(2,1)S(1)}, bf16[64,2048]{1,0:T(8,128)(2,1)S(1)}, u32[]{:S(2)}, u32[]{:S(2)}) %collective-permute-start.26) | collective-permute-done | bytes 262176 | tf_op jit(solution)/shard_map/ppermute | solution.py:256
  96.3 0.7 collective-permute-done.28
  96.9 0.2 add_convert_fusion.4
  97.2 1.3 %collective-permute-start.31 = (bf16[64,2048]{1,0:T(8,128)(2,1)S(1)}, bf16[64,2048]{1,0:T(8,128)(2,1)S(1)}, u32[]{:S(2)}, u32[]{:S(2)}) collective-permute-start(bf16[64,2048]{1,0:T(8,128)(2,1)S(1)} %get-tuple-element.161), channel_id=1, source_target_pairs={{0,8},{1,9},{2,10},{3,11},{4,12},{5,13},{6,14},{7,15},{8,0},{9,1},... | collective-permute-start | bytes 786440 | tf_op jit(solution)/shard_map/ppermute | solution.py:256
  98.5 1.6 %collective-permute-start.32 = (bf16[64,2048]{1,0:T(8,128)(2,1)S(1)}, bf16[64,2048]{1,0:T(8,128)(2,1)S(1)}, u32[]{:S(2)}, u32[]{:S(2)}) collective-permute-start(bf16[64,2048]{1,0:T(8,128)(2,1)S(1)} %get-tuple-element.160), channel_id=1, source_target_pairs={{0,4},{1,5},{2,6},{3,7},{4,0},{5,1},{6,2},{7,3},{8,12},{9,13},{10,... | collective-permute-start | bytes 786440 | tf_op jit(solution)/shard_map/ppermute | solution.py:256
  100.2 0.6 collective-permute-start.33
  100.8 1.5 %collective-permute-start.34 = (bf16[64,2048]{1,0:T(8,128)(2,1)S(1)}, bf16[64,2048]{1,0:T(8,128)(2,1)S(1)}, u32[]{:S(2)}, u32[]{:S(2)}) collective-permute-start(bf16[64,2048]{1,0:T(8,128)(2,1)S(1)} %get-tuple-element.139), channel_id=1, source_target_pairs={{0,2},{1,3},{2,0},{3,1},{4,6},{5,7},{6,4},{7,5},{8,10},{9,11},{10,... | collective-permute-start | bytes 786440 | tf_op jit(solution)/shard_map/ppermute | solution.py:256
  102.3 3.1 %shard_map.84 = f32[768,768]{1,0:T(8,128)} custom-call(f32[16,512]{1,0:T(8,128)S(1)} %shard_map.78.tables, bf16[320,768]{1,0:T(8,128)(2,1)S(1)} %get-tuple-element.141.refs_0_, bf16[320,768]{1,0:T(8,128)(2,1)S(1)} %get-tuple-element.142.refs_1_, bf16[320,768]{1,0:T(8,128)(2,1)S(1)} %get-tuple-element.143.refs_2_, ...), custom_call_target="tpu_custom_call" | custom-call | flops 1509949440 | bytes 4325376 | tf_op jit(solution)/shard_map/pallas_call | solution.py:209
  105.5 5.9 %collective-permute-done.31 = bf16[64,2048]{1,0:T(8,128)(2,1)S(1)} collective-permute-done((bf16[64,2048]{1,0:T(8,128)(2,1)S(1)}, bf16[64,2048]{1,0:T(8,128)(2,1)S(1)}, u32[]{:S(2)}, u32[]{:S(2)}) %collective-permute-start.31) | collective-permute-done | bytes 262176 | tf_op jit(solution)/shard_map/ppermute | solution.py:256
  111.4 1.6 %collective-permute-done.34 = bf16[64,2048]{1,0:T(8,128)(2,1)S(1)} collective-permute-done((bf16[64,2048]{1,0:T(8,128)(2,1)S(1)}, bf16[64,2048]{1,0:T(8,128)(2,1)S(1)}, u32[]{:S(2)}, u32[]{:S(2)}) %collective-permute-start.34) | collective-permute-done | bytes 262176 | tf_op jit(solution)/shard_map/ppermute | solution.py:256
  113.0 0.1 add_convert_fusion.2
  113.1 1.1 collective-permute-start.35
  114.2 0.5 collective-permute-start.37
  114.7 0.1 add_convert_fusion.1
  114.8 1.6 %collective-permute-start.36 = (bf16[64,2048]{1,0:T(8,128)(2,1)S(1)}, bf16[64,2048]{1,0:T(8,128)(2,1)S(1)}, u32[]{:S(2)}, u32[]{:S(2)}) collective-permute-start(bf16[64,2048]{1,0:T(8,128)(2,1)S(1)} %add_convert_fusion.1), channel_id=1, source_target_pairs={{0,4},{1,5},{2,6},{3,7},{4,0},{5,1},{6,2},{7,3},{8,12},{9,13},{10,... | collective-permute-start | bytes 786440 | tf_op jit(solution)/shard_map/ppermute | solution.py:256
  116.4 9.5 %collective-permute-done.35.far_low = bf16[64,2048]{1,0:T(8,128)(2,1)S(1)} collective-permute-done((bf16[64,2048]{1,0:T(8,128)(2,1)S(1)}, bf16[64,2048]{1,0:T(8,128)(2,1)S(1)}, u32[]{:S(2)}, u32[]{:S(2)}) %collective-permute-start.35) | collective-permute-done | bytes 262176 | tf_op jit(solution)/shard_map/ppermute | solution.py:256
  125.9 0.7 collective-permute-done.36.near_high
  126.6 1.1 shard_map.85
  (59 shorter events, 0.7 us)
Async XLA Ops:
  0.6 24.1 %collective-permute-start = (bf16[128,2048]{1,0:T(8,128)(2,1)}, bf16[128,2048]{1,0:T(8,128)(2,1)S(1)}, u32[]{:S(2)}, u32[]{:S(2)}) collective-permute-start(bf16[128,2048]{1,0:T(8,128)(2,1)} %refs_0_.1), channel_id=1, source_target_pairs={{0,4},{1,5},{2,6},{3,7},{4,0},{5,1},{6,2},{7,3},{8,12},{9,13},{10,... | collective-permute-start | bytes 1572872 | tf_op jit(solution)/shard_map/ppermute | solution.py:256
  3.7 21.0 %collective-permute-start.2 = (bf16[128,2048]{1,0:T(8,128)(2,1)}, bf16[128,2048]{1,0:T(8,128)(2,1)S(1)}, u32[]{:S(2)}, u32[]{:S(2)}) collective-permute-start(bf16[128,2048]{1,0:T(8,128)(2,1)} %refs_0_.1), channel_id=1, source_target_pairs={{0,2},{1,3},{2,0},{3,1},{4,6},{5,7},{6,4},{7,5},{8,10},{9,11},{10,... | collective-permute-start | bytes 1572872 | tf_op jit(solution)/shard_map/ppermute | solution.py:256
  5.2 19.5 %collective-permute-start.3 = (bf16[128,2048]{1,0:T(8,128)(2,1)}, bf16[128,2048]{1,0:T(8,128)(2,1)S(1)}, u32[]{:S(2)}, u32[]{:S(2)}) collective-permute-start(bf16[128,2048]{1,0:T(8,128)(2,1)} %refs_0_.1), channel_id=1, source_target_pairs={{0,1},{1,0},{2,3},{3,2},{4,5},{5,4},{6,7},{7,6},{8,9},{9,8},{10,11... | collective-permute-start | bytes 1572872 | tf_op jit(solution)/shard_map/ppermute | solution.py:256
  5.2 1.1 copy-start.6
  6.3 0.7 copy-start.8
  7.0 0.7 copy-start.9
  7.8 16.9 %collective-permute-start.1 = (bf16[64,2048]{1,0:T(8,128)(2,1)S(1)}, bf16[64,2048]{1,0:T(8,128)(2,1)S(1)}, u32[]{:S(2)}, u32[]{:S(2)}) collective-permute-start(bf16[64,2048]{1,0:T(8,128)(2,1)S(1)} %get-tuple-element.80), channel_id=1, source_target_pairs={{0,8},{1,9},{2,10},{3,11},{4,12},{5,13},{6,14},{7,15},{8,0},{9,1},... | collective-permute-start | bytes 786440 | tf_op jit(solution)/shard_map/ppermute | solution.py:256
  24.7 0.7 copy-start.10
  25.4 2.7 %collective-permute-start.7 = (bf16[128,2048]{1,0:T(8,128)(2,1)S(1)}, bf16[128,2048]{1,0:T(8,128)(2,1)S(1)}, u32[]{:S(2)}, u32[]{:S(2)}) collective-permute-start(bf16[128,2048]{1,0:T(8,128)(2,1)S(1)} %collective-permute-done.2.refs_1_), channel_id=1, source_target_pairs={{0,1},{1,0},{2,3},{3,2},{4,5},{5,4},{6,7},{7,6},{8,9},{9,8},{10,11... | collective-permute-start | bytes 1572872 | tf_op jit(solution)/shard_map/ppermute | solution.py:256
  25.4 15.9 %collective-permute-start.5 = (bf16[128,2048]{1,0:T(8,128)(2,1)S(1)}, bf16[128,2048]{1,0:T(8,128)(2,1)S(1)}, u32[]{:S(2)}, u32[]{:S(2)}) collective-permute-start(bf16[128,2048]{1,0:T(8,128)(2,1)S(1)} %collective-permute-done.refs_0_), channel_id=1, source_target_pairs={{0,2},{1,3},{2,0},{3,1},{4,6},{5,7},{6,4},{7,5},{8,10},{9,11},{10,... | collective-permute-start | bytes 1572872 | tf_op jit(solution)/shard_map/ppermute | solution.py:256
  25.9 15.4 %collective-permute-start.6 = (bf16[128,2048]{1,0:T(8,128)(2,1)S(1)}, bf16[128,2048]{1,0:T(8,128)(2,1)S(1)}, u32[]{:S(2)}, u32[]{:S(2)}) collective-permute-start(bf16[128,2048]{1,0:T(8,128)(2,1)S(1)} %collective-permute-done.refs_0_), channel_id=1, source_target_pairs={{0,1},{1,0},{2,3},{3,2},{4,5},{5,4},{6,7},{7,6},{8,9},{9,8},{10,11... | collective-permute-start | bytes 1572872 | tf_op jit(solution)/shard_map/ppermute | solution.py:256
  26.3 15.1 %collective-permute-start.4 = (bf16[64,2048]{1,0:T(8,128)(2,1)S(1)}, bf16[64,2048]{1,0:T(8,128)(2,1)S(1)}, u32[]{:S(2)}, u32[]{:S(2)}) collective-permute-start(bf16[64,2048]{1,0:T(8,128)(2,1)S(1)} %get-tuple-element.84), channel_id=1, source_target_pairs={{0,8},{1,9},{2,10},{3,11},{4,12},{5,13},{6,14},{7,15},{8,0},{9,1},... | collective-permute-start | bytes 786440 | tf_op jit(solution)/shard_map/ppermute | solution.py:256
  28.2 1.9 %copy-start = (bf16[1,2048,768]{2,1,0:T(8,128)(2,1)S(1)}, bf16[1,2048,768]{2,1,0:T(8,128)(2,1)}, u32[]{:S(2)}) copy-start(bf16[1,2048,768]{2,1,0:T(8,128)(2,1)} %param.9) | copy-start | bytes 9437188
  30.0 1.9 %copy-start.2 = (bf16[1,2048,768]{2,1,0:T(8,128)(2,1)S(1)}, bf16[1,2048,768]{2,1,0:T(8,128)(2,1)}, u32[]{:S(2)}) copy-start(bf16[1,2048,768]{2,1,0:T(8,128)(2,1)} %param.10) | copy-start | bytes 9437188
  31.9 1.9 %copy-start.4 = (bf16[1,768,2048]{2,1,0:T(8,128)(2,1)S(1)}, bf16[1,768,2048]{2,1,0:T(8,128)(2,1)}, u32[]{:S(2)}) copy-start(bf16[1,768,2048]{2,1,0:T(8,128)(2,1)} %param.11) | copy-start | bytes 9437188
  33.8 1.0 copy-start.7
  34.9 6.5 %copy-start.11 = (bf16[64,2048]{1,0:T(8,128)(2,1)S(1)}, bf16[64,2048]{1,0:T(8,128)(2,1)}, u32[]{:S(2)}) copy-start(bf16[64,2048]{1,0:T(8,128)(2,1)} %copy-done.10) | copy-start | bytes 786436
  34.9 8.4 %copy-start.1 = (bf16[1,2048,768]{2,1,0:T(8,128)(2,1)S(1)}, bf16[1,2048,768]{2,1,0:T(8,128)(2,1)}, u32[]{:S(2)}) copy-start(bf16[1,2048,768]{2,1,0:T(8,128)(2,1)} %param.9) | copy-start | bytes 9437188
  34.9 8.4 %copy-start.3 = (bf16[1,2048,768]{2,1,0:T(8,128)(2,1)S(1)}, bf16[1,2048,768]{2,1,0:T(8,128)(2,1)}, u32[]{:S(2)}) copy-start(bf16[1,2048,768]{2,1,0:T(8,128)(2,1)} %param.10) | copy-start | bytes 9437188
  34.9 8.4 %copy-start.5 = (bf16[1,768,2048]{2,1,0:T(8,128)(2,1)S(1)}, bf16[1,768,2048]{2,1,0:T(8,128)(2,1)}, u32[]{:S(2)}) copy-start(bf16[1,768,2048]{2,1,0:T(8,128)(2,1)} %param.11) | copy-start | bytes 9437188
  41.3 1.9 %collective-permute-start.11 = (bf16[128,2048]{1,0:T(8,128)(2,1)S(1)}, bf16[128,2048]{1,0:T(8,128)(2,1)S(1)}, u32[]{:S(2)}, u32[]{:S(2)}) collective-permute-start(bf16[128,2048]{1,0:T(8,128)(2,1)S(1)} %collective-permute-done.5.refs_1_), channel_id=1, source_target_pairs={{0,1},{1,0},{2,3},{3,2},{4,5},{5,4},{6,7},{7,6},{8,9},{9,8},{10,11... | collective-permute-start | bytes 1572872 | tf_op jit(solution)/shard_map/ppermute | solution.py:256
  41.4 14.4 %collective-permute-start.8 = (bf16[128,2048]{1,0:T(8,128)(2,1)S(1)}, bf16[128,2048]{1,0:T(8,128)(2,1)S(1)}, u32[]{:S(2)}, u32[]{:S(2)}) collective-permute-start(bf16[128,2048]{1,0:T(8,128)(2,1)S(1)} %constant_dynamic-update-slice_fusion.refs_0_), channel_id=1, source_target_pairs={{0,4},{1,5},{2,6},{3,7},{4,0},{5,1},{6,2},{7,3},{8,12},{9,13},{10,... | collective-permute-start | bytes 1572872 | tf_op jit(solution)/shard_map/ppermute | solution.py:256
  42.1 14.0 %collective-permute-start.9 = (bf16[128,2048]{1,0:T(8,128)(2,1)S(1)}, bf16[128,2048]{1,0:T(8,128)(2,1)S(1)}, u32[]{:S(2)}, u32[]{:S(2)}) collective-permute-start(bf16[128,2048]{1,0:T(8,128)(2,1)S(1)} %constant_dynamic-update-slice_fusion.refs_0_), channel_id=1, source_target_pairs={{0,2},{1,3},{2,0},{3,1},{4,6},{5,7},{6,4},{7,5},{8,10},{9,11},{10,... | collective-permute-start | bytes 1572872 | tf_op jit(solution)/shard_map/ppermute | solution.py:256
  43.2 12.9 %collective-permute-start.10 = (bf16[128,2048]{1,0:T(8,128)(2,1)S(1)}, bf16[128,2048]{1,0:T(8,128)(2,1)S(1)}, u32[]{:S(2)}, u32[]{:S(2)}) collective-permute-start(bf16[128,2048]{1,0:T(8,128)(2,1)S(1)} %constant_dynamic-update-slice_fusion.refs_0_), channel_id=1, source_target_pairs={{0,1},{1,0},{2,3},{3,2},{4,5},{5,4},{6,7},{7,6},{8,9},{9,8},{10,11... | collective-permute-start | bytes 1572872 | tf_op jit(solution)/shard_map/ppermute | solution.py:256
  48.7 7.4 %collective-permute-start.12 = (bf16[128,2048]{1,0:T(8,128)(2,1)S(1)}, bf16[128,2048]{1,0:T(8,128)(2,1)S(1)}, u32[]{:S(2)}, u32[]{:S(2)}) collective-permute-start(bf16[128,2048]{1,0:T(8,128)(2,1)S(1)} %get-tuple-element.99), channel_id=1, source_target_pairs={{0,1},{1,0},{2,3},{3,2},{4,5},{5,4},{6,7},{7,6},{8,9},{9,8},{10,11... | collective-permute-start | bytes 1572872 | tf_op jit(solution)/shard_map/ppermute | solution.py:256
  56.1 3.6 %collective-permute-start.17 = (bf16[128,2048]{1,0:T(8,128)(2,1)S(1)}, bf16[128,2048]{1,0:T(8,128)(2,1)S(1)}, u32[]{:S(2)}, u32[]{:S(2)}) collective-permute-start(bf16[128,2048]{1,0:T(8,128)(2,1)S(1)} %collective-permute-done.9.refs_1_), channel_id=1, source_target_pairs={{0,1},{1,0},{2,3},{3,2},{4,5},{5,4},{6,7},{7,6},{8,9},{9,8},{10,11... | collective-permute-start | bytes 1572872 | tf_op jit(solution)/shard_map/ppermute | solution.py:256
  56.1 12.6 %collective-permute-start.15 = (bf16[256,2048]{1,0:T(8,128)(2,1)S(1)}, bf16[256,2048]{1,0:T(8,128)(2,1)S(1)}, u32[]{:S(2)}, u32[]{:S(2)}) collective-permute-start(bf16[256,2048]{1,0:T(8,128)(2,1)S(1)} %get-tuple-element.103), channel_id=1, source_target_pairs={{0,1},{1,0},{2,3},{3,2},{4,5},{5,4},{6,7},{7,6},{8,9},{9,8},{10,11... | collective-permute-start | bytes 3145736 | tf_op jit(solution)/shard_map/ppermute | solution.py:256
  56.6 13.9 %collective-permute-start.13 = (bf16[128,2048]{1,0:T(8,128)(2,1)S(1)}, bf16[128,2048]{1,0:T(8,128)(2,1)S(1)}, u32[]{:S(2)}, u32[]{:S(2)}) collective-permute-start(bf16[128,2048]{1,0:T(8,128)(2,1)S(1)} %collective-permute-done.9.refs_1_), channel_id=1, source_target_pairs={{0,4},{1,5},{2,6},{3,7},{4,0},{5,1},{6,2},{7,3},{8,12},{9,13},{10,... | collective-permute-start | bytes 1572872 | tf_op jit(solution)/shard_map/ppermute | solution.py:256
  58.1 7.6 %collective-permute-start.19 = (bf16[128,2048]{1,0:T(8,128)(2,1)S(1)}, bf16[128,2048]{1,0:T(8,128)(2,1)S(1)}, u32[]{:S(2)}, u32[]{:S(2)}) collective-permute-start(bf16[128,2048]{1,0:T(8,128)(2,1)S(1)} %collective-permute-done.8.refs_0_), channel_id=1, source_target_pairs={{0,1},{1,0},{2,3},{3,2},{4,5},{5,4},{6,7},{7,6},{8,9},{9,8},{10,11... | collective-permute-start | bytes 1572872 | tf_op jit(solution)/shard_map/ppermute | solution.py:256
  58.2 10.5 %collective-permute-start.14 = (bf16[64,2048]{1,0:T(8,128)(2,1)S(1)}, bf16[64,2048]{1,0:T(8,128)(2,1)S(1)}, u32[]{:S(2)}, u32[]{:S(2)}) collective-permute-start(bf16[64,2048]{1,0:T(8,128)(2,1)S(1)} %get-tuple-element.159), channel_id=1, source_target_pairs={{0,2},{1,3},{2,0},{3,1},{4,6},{5,7},{6,4},{7,5},{8,10},{9,11},{10,... | collective-permute-start | bytes 786440 | tf_op jit(solution)/shard_map/ppermute | solution.py:256
  59.7 10.8 %collective-permute-start.16 = (bf16[128,2048]{1,0:T(8,128)(2,1)S(1)}, bf16[128,2048]{1,0:T(8,128)(2,1)S(1)}, u32[]{:S(2)}, u32[]{:S(2)}) collective-permute-start(bf16[128,2048]{1,0:T(8,128)(2,1)S(1)} %get-tuple-element.104), channel_id=1, source_target_pairs={{0,1},{1,0},{2,3},{3,2},{4,5},{5,4},{6,7},{7,6},{8,9},{9,8},{10,11... | collective-permute-start | bytes 1572872 | tf_op jit(solution)/shard_map/ppermute | solution.py:256
  65.6 4.9 %collective-permute-start.18 = (bf16[64,2048]{1,0:T(8,128)(2,1)S(1)}, bf16[64,2048]{1,0:T(8,128)(2,1)S(1)}, u32[]{:S(2)}, u32[]{:S(2)}) collective-permute-start(bf16[64,2048]{1,0:T(8,128)(2,1)S(1)} %get-tuple-element.106), channel_id=1, source_target_pairs={{0,1},{1,0},{2,3},{3,2},{4,5},{5,4},{6,7},{7,6},{8,9},{9,8},{10,11... | collective-permute-start | bytes 786440 | tf_op jit(solution)/shard_map/ppermute | solution.py:256
  70.5 3.4 %collective-permute-start.22 = (bf16[128,2048]{1,0:T(8,128)(2,1)S(1)}, bf16[128,2048]{1,0:T(8,128)(2,1)S(1)}, u32[]{:S(2)}, u32[]{:S(2)}) collective-permute-start(bf16[128,2048]{1,0:T(8,128)(2,1)S(1)} %collective-permute-done.13.refs_0_), channel_id=1, source_target_pairs={{0,1},{1,0},{2,3},{3,2},{4,5},{5,4},{6,7},{7,6},{8,9},{9,8},{10,11... | collective-permute-start | bytes 1572872 | tf_op jit(solution)/shard_map/ppermute | solution.py:256
  70.6 8.8 %collective-permute-start.20 = (bf16[64,2048]{1,0:T(8,128)(2,1)S(1)}, bf16[64,2048]{1,0:T(8,128)(2,1)S(1)}, u32[]{:S(2)}, u32[]{:S(2)}) collective-permute-start(bf16[64,2048]{1,0:T(8,128)(2,1)S(1)} %add_convert_fusion.11), channel_id=1, source_target_pairs={{0,2},{1,3},{2,0},{3,1},{4,6},{5,7},{6,4},{7,5},{8,10},{9,11},{10,... | collective-permute-start | bytes 786440 | tf_op jit(solution)/shard_map/ppermute | solution.py:256
  71.9 8.9 %collective-permute-start.25 = (bf16[128,2048]{1,0:T(8,128)(2,1)S(1)}, bf16[128,2048]{1,0:T(8,128)(2,1)S(1)}, u32[]{:S(2)}, u32[]{:S(2)}) collective-permute-start(bf16[128,2048]{1,0:T(8,128)(2,1)S(1)} %get-tuple-element.125), channel_id=1, source_target_pairs={{0,1},{1,0},{2,3},{3,2},{4,5},{5,4},{6,7},{7,6},{8,9},{9,8},{10,11... | collective-permute-start | bytes 1572872 | tf_op jit(solution)/shard_map/ppermute | solution.py:256
  72.3 8.6 %collective-permute-start.21 = (bf16[64,2048]{1,0:T(8,128)(2,1)S(1)}, bf16[64,2048]{1,0:T(8,128)(2,1)S(1)}, u32[]{:S(2)}, u32[]{:S(2)}) collective-permute-start(bf16[64,2048]{1,0:T(8,128)(2,1)S(1)} %add_convert_fusion.10), channel_id=1, source_target_pairs={{0,4},{1,5},{2,6},{3,7},{4,0},{5,1},{6,2},{7,3},{8,12},{9,13},{10,... | collective-permute-start | bytes 786440 | tf_op jit(solution)/shard_map/ppermute | solution.py:256
  76.7 4.2 %collective-permute-start.23 = (bf16[64,2048]{1,0:T(8,128)(2,1)S(1)}, bf16[64,2048]{1,0:T(8,128)(2,1)S(1)}, u32[]{:S(2)}, u32[]{:S(2)}) collective-permute-start(bf16[64,2048]{1,0:T(8,128)(2,1)S(1)} %get-tuple-element.122), channel_id=1, source_target_pairs={{0,1},{1,0},{2,3},{3,2},{4,5},{5,4},{6,7},{7,6},{8,9},{9,8},{10,11... | collective-permute-start | bytes 786440 | tf_op jit(solution)/shard_map/ppermute | solution.py:256
  76.8 4.1 %collective-permute-start.24 = (bf16[64,2048]{1,0:T(8,128)(2,1)S(1)}, bf16[64,2048]{1,0:T(8,128)(2,1)S(1)}, u32[]{:S(2)}, u32[]{:S(2)}) collective-permute-start(bf16[64,2048]{1,0:T(8,128)(2,1)S(1)} %get-tuple-element.123), channel_id=1, source_target_pairs={{0,1},{1,0},{2,3},{3,2},{4,5},{5,4},{6,7},{7,6},{8,9},{9,8},{10,11... | collective-permute-start | bytes 786440 | tf_op jit(solution)/shard_map/ppermute | solution.py:256
  79.4 5.7 %collective-permute-start.29 = (bf16[64,2048]{1,0:T(8,128)(2,1)S(1)}, bf16[64,2048]{1,0:T(8,128)(2,1)S(1)}, u32[]{:S(2)}, u32[]{:S(2)}) collective-permute-start(bf16[64,2048]{1,0:T(8,128)(2,1)S(1)} %get-tuple-element.133), channel_id=1, source_target_pairs={{0,1},{1,0},{2,3},{3,2},{4,5},{5,4},{6,7},{7,6},{8,9},{9,8},{10,11... | collective-permute-start | bytes 786440 | tf_op jit(solution)/shard_map/ppermute | solution.py:256
  80.8 4.2 %collective-permute-start.30 = (bf16[128,2048]{1,0:T(8,128)(2,1)S(1)}, bf16[128,2048]{1,0:T(8,128)(2,1)S(1)}, u32[]{:S(2)}, u32[]{:S(2)}) collective-permute-start(bf16[128,2048]{1,0:T(8,128)(2,1)S(1)} %get-tuple-element.134), channel_id=1, source_target_pairs={{0,1},{1,0},{2,3},{3,2},{4,5},{5,4},{6,7},{7,6},{8,9},{9,8},{10,11... | collective-permute-start | bytes 1572872 | tf_op jit(solution)/shard_map/ppermute | solution.py:256
  81.0 15.3 %collective-permute-start.26 = (bf16[64,2048]{1,0:T(8,128)(2,1)S(1)}, bf16[64,2048]{1,0:T(8,128)(2,1)S(1)}, u32[]{:S(2)}, u32[]{:S(2)}) collective-permute-start(bf16[64,2048]{1,0:T(8,128)(2,1)S(1)} %add_convert_fusion.9), channel_id=1, source_target_pairs={{0,8},{1,9},{2,10},{3,11},{4,12},{5,13},{6,14},{7,15},{8,0},{9,1},... | collective-permute-start | bytes 786440 | tf_op jit(solution)/shard_map/ppermute | solution.py:256
  82.8 13.5 %collective-permute-start.27 = (bf16[64,2048]{1,0:T(8,128)(2,1)S(1)}, bf16[64,2048]{1,0:T(8,128)(2,1)S(1)}, u32[]{:S(2)}, u32[]{:S(2)}) collective-permute-start(bf16[64,2048]{1,0:T(8,128)(2,1)S(1)} %get-tuple-element.163), channel_id=1, source_target_pairs={{0,2},{1,3},{2,0},{3,1},{4,6},{5,7},{6,4},{7,5},{8,10},{9,11},{10,... | collective-permute-start | bytes 786440 | tf_op jit(solution)/shard_map/ppermute | solution.py:256
  83.9 13.0 %collective-permute-start.28 = (bf16[64,2048]{1,0:T(8,128)(2,1)S(1)}, bf16[64,2048]{1,0:T(8,128)(2,1)S(1)}, u32[]{:S(2)}, u32[]{:S(2)}) collective-permute-start(bf16[64,2048]{1,0:T(8,128)(2,1)S(1)} %get-tuple-element.162), channel_id=1, source_target_pairs={{0,2},{1,3},{2,0},{3,1},{4,6},{5,7},{6,4},{7,5},{8,10},{9,11},{10,... | collective-permute-start | bytes 786440 | tf_op jit(solution)/shard_map/ppermute | solution.py:256
  97.2 14.2 %collective-permute-start.31 = (bf16[64,2048]{1,0:T(8,128)(2,1)S(1)}, bf16[64,2048]{1,0:T(8,128)(2,1)S(1)}, u32[]{:S(2)}, u32[]{:S(2)}) collective-permute-start(bf16[64,2048]{1,0:T(8,128)(2,1)S(1)} %get-tuple-element.161), channel_id=1, source_target_pairs={{0,8},{1,9},{2,10},{3,11},{4,12},{5,13},{6,14},{7,15},{8,0},{9,1},... | collective-permute-start | bytes 786440 | tf_op jit(solution)/shard_map/ppermute | solution.py:256
  98.5 12.9 %collective-permute-start.32 = (bf16[64,2048]{1,0:T(8,128)(2,1)S(1)}, bf16[64,2048]{1,0:T(8,128)(2,1)S(1)}, u32[]{:S(2)}, u32[]{:S(2)}) collective-permute-start(bf16[64,2048]{1,0:T(8,128)(2,1)S(1)} %get-tuple-element.160), channel_id=1, source_target_pairs={{0,4},{1,5},{2,6},{3,7},{4,0},{5,1},{6,2},{7,3},{8,12},{9,13},{10,... | collective-permute-start | bytes 786440 | tf_op jit(solution)/shard_map/ppermute | solution.py:256
  100.2 11.2 %collective-permute-start.33 = (bf16[64,2048]{1,0:T(8,128)(2,1)S(1)}, bf16[64,2048]{1,0:T(8,128)(2,1)S(1)}, u32[]{:S(2)}, u32[]{:S(2)}) collective-permute-start(bf16[64,2048]{1,0:T(8,128)(2,1)S(1)} %add_convert_fusion.3), channel_id=1, source_target_pairs={{0,2},{1,3},{2,0},{3,1},{4,6},{5,7},{6,4},{7,5},{8,10},{9,11},{10,... | collective-permute-start | bytes 786440 | tf_op jit(solution)/shard_map/ppermute | solution.py:256
  100.8 12.1 %collective-permute-start.34 = (bf16[64,2048]{1,0:T(8,128)(2,1)S(1)}, bf16[64,2048]{1,0:T(8,128)(2,1)S(1)}, u32[]{:S(2)}, u32[]{:S(2)}) collective-permute-start(bf16[64,2048]{1,0:T(8,128)(2,1)S(1)} %get-tuple-element.139), channel_id=1, source_target_pairs={{0,2},{1,3},{2,0},{3,1},{4,6},{5,7},{6,4},{7,5},{8,10},{9,11},{10,... | collective-permute-start | bytes 786440 | tf_op jit(solution)/shard_map/ppermute | solution.py:256
  113.1 12.8 %collective-permute-start.35 = (bf16[64,2048]{1,0:T(8,128)(2,1)S(1)}, bf16[64,2048]{1,0:T(8,128)(2,1)S(1)}, u32[]{:S(2)}, u32[]{:S(2)}) collective-permute-start(bf16[64,2048]{1,0:T(8,128)(2,1)S(1)} %add_convert_fusion.2), channel_id=1, source_target_pairs={{0,8},{1,9},{2,10},{3,11},{4,12},{5,13},{6,14},{7,15},{8,0},{9,1},... | collective-permute-start | bytes 786440 | tf_op jit(solution)/shard_map/ppermute | solution.py:256
  114.2 12.4 %collective-permute-start.37 = (bf16[128,2048]{1,0:T(8,128)(2,1)S(1)}, bf16[128,2048]{1,0:T(8,128)(2,1)S(1)}, u32[]{:S(2)}, u32[]{:S(2)}) collective-permute-start(bf16[128,2048]{1,0:T(8,128)(2,1)S(1)} %add_convert_fusion), channel_id=1, source_target_pairs={{0,2},{1,3},{2,0},{3,1},{4,6},{5,7},{6,4},{7,5},{8,10},{9,11},{10,... | collective-permute-start | bytes 1572872 | tf_op jit(solution)/shard_map/ppermute | solution.py:256
  114.8 11.8 %collective-permute-start.36 = (bf16[64,2048]{1,0:T(8,128)(2,1)S(1)}, bf16[64,2048]{1,0:T(8,128)(2,1)S(1)}, u32[]{:S(2)}, u32[]{:S(2)}) collective-permute-start(bf16[64,2048]{1,0:T(8,128)(2,1)S(1)} %add_convert_fusion.1), channel_id=1, source_target_pairs={{0,4},{1,5},{2,6},{3,7},{4,0},{5,1},{6,2},{7,3},{8,12},{9,13},{10,... | collective-permute-start | bytes 786440 | tf_op jit(solution)/shard_map/ppermute | solution.py:256

commit v27 on v22

--- a/solution.py
+++ b/solution.py
@@ -277,14 +277,11 @@
 
     mine, a0_low, a0_high = prepare_pass(routes, probs, tokens, size)
     a0 = tokens
-    a1, low, b0, c0, weight, a0_high = together(
-        pair(a0),
-        far(a0_low),
-        column(a0),
-        sibling(a0),
-        lax.all_to_all(mine, "expert", split_axis=0, concat_axis=0, tiled=True),
-        a0_high,
-    )
+    all_mine = lax.all_gather(mine, "expert")
+    a1, low, b0, c0, a0_high = together(
+        pair(a0), far(a0_low), column(a0), sibling(a0), a0_high
+    )
+    weight = lax.dynamic_index_in_dim(all_mine, me, 1, False)
     tables = ranks_pass(capacity, spots, weight)
     high = far(a0_high)
     b1 = column(a1)

time: 127 us -> 146 us (1.15)
  waiting for transfers between devices: 41.7 us -> 52.6 us
  blocking collectives: 14.2 us -> 22.2 us
    all_gather x0 -> x1, blocking collectives: none -> 22.2 us  [staged(): all_mine = lax.all_gather(mine, 'expert')]
    all_to_all x1 -> x0, blocking collectives: 14.2 us -> none  [staged(): lax.all_to_all(mine, 'expert', split_axis=0, concat_axis=0, tiled=True)]
    ppermute x37, waiting for transfers between devices: 41.7 us -> 52.6 us  [swapped(): return lax.ppermute(array, 'expert', [(i, i ^ bit) for i in range(size)])]
  transfers between devices with their start and end apart: 37 -> 37, of which waited for: 11 -> 13; matrix products, arithmetic and copies ran while one was open for 1% -> 1% of each run, Pallas kernels for 21% -> 18%
where the time goes in v27:
time: 146 us; the launch traced here: 145 us
  waiting for transfers between devices  52.6 us (36%)
  starting transfers between devices  31.9 us (22%)
  Pallas kernels  27.2 us (19%)
  blocking collectives  22.2 us (15%)
  local copies, waits for them, and re-layouts  9.31 us (6%)
    ppermute x37, waiting for transfers between devices, swapped(): return lax.ppermute(array, 'expert', [(i, i ^ bit) for i in range(size)])  52.6 us
    ppermute x37, starting transfers between devices, swapped(): return lax.ppermute(array, 'expert', [(i, i ^ bit) for i in range(size)])  31.9 us
    all_gather x1, blocking collectives, staged(): all_mine = lax.all_gather(mine, 'expert')  22.2 us
    pallas_call x5, Pallas kernels, plane_pass(): pl.pallas_call(functools.partial(plane_kernel, k, picked, len(pieces)), o...  22 us
    unnamed x25, local copies, waits for them, and re-layouts  9.18 us
    pallas_call x1, Pallas kernels, gram_pass(): pl.pallas_call(gram_kernel, out_shape=jax.ShapeDtypeStruct((hidden, hidde...  3.14 us
  transfers between devices with their start and end apart: 37, of which 13 were waited for; matrix products, arithmetic and copies ran while one was open for 1% of the time, Pallas kernels for 18%

profile of v27, /device:TPU:0, one launch (start us, length us, event | category | flops | bytes accessed | tf_op | source)
XLA Modules:
  0.0 145.4 jit_solution(6006594292611012286)
XLA Ops:
  0.6 3.1 %collective-permute-start = (bf16[128,2048]{1,0:T(8,128)(2,1)}, bf16[128,2048]{1,0:T(8,128)(2,1)S(1)}, u32[]{:S(2)}, u32[]{:S(2)}) collective-permute-start(bf16[128,2048]{1,0:T(8,128)(2,1)} %refs_0_.1), channel_id=1, source_target_pairs={{0,4},{1,5},{2,6},{3,7},{4,0},{5,1},{6,2},{7,3},{8,12},{9,13},{10,... | collective-permute-start | bytes 1572872 | tf_op jit(solution)/shard_map/ppermute | solution.py:256
  3.7 1.5 %collective-permute-start.2 = (bf16[128,2048]{1,0:T(8,128)(2,1)}, bf16[128,2048]{1,0:T(8,128)(2,1)S(1)}, u32[]{:S(2)}, u32[]{:S(2)}) collective-permute-start(bf16[128,2048]{1,0:T(8,128)(2,1)} %refs_0_.1), channel_id=1, source_target_pairs={{0,2},{1,3},{2,0},{3,1},{4,6},{5,7},{6,4},{7,5},{8,10},{9,11},{10,... | collective-permute-start | bytes 1572872 | tf_op jit(solution)/shard_map/ppermute | solution.py:256
  5.2 1.1 copy-done.6
  6.3 0.7 copy-done.8
  7.0 0.7 copy-done.9
  7.7 0.1 shard_map.77
  7.8 2.7 %collective-permute-start.1 = (bf16[64,2048]{1,0:T(8,128)(2,1)S(1)}, bf16[64,2048]{1,0:T(8,128)(2,1)S(1)}, u32[]{:S(2)}, u32[]{:S(2)}) collective-permute-start(bf16[64,2048]{1,0:T(8,128)(2,1)S(1)} %get-tuple-element.78), channel_id=1, source_target_pairs={{0,8},{1,9},{2,10},{3,11},{4,12},{5,13},{6,14},{7,15},{8,0},{9,1},... | collective-permute-start | bytes 786440 | tf_op jit(solution)/shard_map/ppermute | solution.py:256
  10.5 10.3 %collective-permute-done.1 = bf16[64,2048]{1,0:T(8,128)(2,1)S(1)} collective-permute-done((bf16[64,2048]{1,0:T(8,128)(2,1)S(1)}, bf16[64,2048]{1,0:T(8,128)(2,1)S(1)}, u32[]{:S(2)}, u32[]{:S(2)}) %collective-permute-start.1) | collective-permute-done | bytes 262176 | tf_op jit(solution)/shard_map/ppermute | solution.py:256
  20.8 0.7 collective-permute-done.refs_0_
  21.6 22.2 %all-gather = f32[256,128]{1,0:T(8,128)S(1)} all-gather(f32[16,128]{1,0:T(8,128)S(1)} %get-tuple-element.83), channel_id=2, replica_groups=mesh['parts'=2,'expert'=16] {'expert'}, dimensions={0}, use_global_device_ids=true | all-gather | bytes 139264 | tf_op jit(solution)/shard_map/all_gather | solution.py:280
  43.8 0.3 collective-permute-start.6
  44.2 0.8 shard_map.78.tables
  45.1 1.9 %copy-done = bf16[1,2048,768]{2,1,0:T(8,128)(2,1)S(1)} copy-done((bf16[1,2048,768]{2,1,0:T(8,128)(2,1)S(1)}, bf16[1,2048,768]{2,1,0:T(8,128)(2,1)}, u32[]{:S(2)}) %copy-start) | copy-done | bytes 3145752
  47.0 1.9 %copy-done.2 = bf16[1,2048,768]{2,1,0:T(8,128)(2,1)S(1)} copy-done((bf16[1,2048,768]{2,1,0:T(8,128)(2,1)S(1)}, bf16[1,2048,768]{2,1,0:T(8,128)(2,1)}, u32[]{:S(2)}) %copy-start.2) | copy-done | bytes 3145752
  48.9 1.9 %copy-done.4 = bf16[1,768,2048]{2,1,0:T(8,128)(2,1)S(1)} copy-done((bf16[1,768,2048]{2,1,0:T(8,128)(2,1)S(1)}, bf16[1,768,2048]{2,1,0:T(8,128)(2,1)}, u32[]{:S(2)}) %copy-start.4) | copy-done | bytes 3145752
  50.8 1.0 copy-done.7
  51.8 5.5 %shard_map.79 = (bf16[256,2048]{1,0:T(8,128)(2,1)S(1)}, bf16[256,2048]{1,0:T(8,128)(2,1)S(1)}, bf16[320,768]{1,0:T(8,128)(2,1)S(1)}) custom-call(f32[16,512]{1,0:T(8,128)S(1)} %shard_map.78.tables, bf16[128,2048]{1,0:T(8,128)(2,1)S(1)} %copy-done.7, bf16[128,2048]{1,0:T(8,128)(2,1)S(1)} %collective-permute-done.2.refs_1_, ...), custom_call_target="tpu_custom_call" | custom-call | flops 4362076160 | bytes 13631488 | tf_op jit(solution)/shard_map/pallas_call | solution.py:178
  57.3 0.9 collective-permute-done.4
  58.3 2.1 %collective-permute-start.9 = (bf16[128,2048]{1,0:T(8,128)(2,1)S(1)}, bf16[128,2048]{1,0:T(8,128)(2,1)S(1)}, u32[]{:S(2)}, u32[]{:S(2)}) collective-permute-start(bf16[128,2048]{1,0:T(8,128)(2,1)S(1)} %constant_dynamic-update-slice_fusion.refs_0_), channel_id=1, source_target_pairs={{0,2},{1,3},{2,0},{3,1},{4,6},{5,7},{6,4},{7,5},{8,10},{9,11},{10,... | collective-permute-start | bytes 1572872 | tf_op jit(solution)/shard_map/ppermute | solution.py:256
  60.5 0.2 collective-permute-start.10
  60.7 5.5 %shard_map.80 = (bf16[256,2048]{1,0:T(8,128)(2,1)S(1)}, bf16[128,2048]{1,0:T(8,128)(2,1)S(1)}, bf16[128,2048]{1,0:T(8,128)(2,1)S(1)}, bf16[320,768]{1,0:T(8,128)(2,1)S(1)}) custom-call(f32[16,512]{1,0:T(8,128)S(1)} %shard_map.78.tables, bf16[128,2048]{1,0:T(8,128)(2,1)S(1)} %collective-permute-done.refs_0_, ...), custom_call_target="tpu_custom_call" | custom-call | flops 4362076160 | bytes 13631488 | tf_op jit(solution)/shard_map/pallas_call | solution.py:178
  66.1 0.4 collective-permute-start.12
  66.5 6.1 %collective-permute-done.8.refs_0_ = bf16[128,2048]{1,0:T(8,128)(2,1)S(1)} collective-permute-done((bf16[128,2048]{1,0:T(8,128)(2,1)S(1)}, bf16[128,2048]{1,0:T(8,128)(2,1)S(1)}, u32[]{:S(2)}, u32[]{:S(2)}) %collective-permute-start.8) | collective-permute-done | bytes 524320 | tf_op jit(solution)/shard_map/ppermute | solution.py:256
  72.6 0.4 collective-permute-done.9.refs_1_
  73.0 0.5 collective-permute-start.15
  73.5 1.7 %collective-permute-start.13 = (bf16[128,2048]{1,0:T(8,128)(2,1)S(1)}, bf16[128,2048]{1,0:T(8,128)(2,1)S(1)}, u32[]{:S(2)}, u32[]{:S(2)}) collective-permute-start(bf16[128,2048]{1,0:T(8,128)(2,1)S(1)} %collective-permute-done.9.refs_1_), channel_id=1, source_target_pairs={{0,4},{1,5},{2,6},{3,7},{4,0},{5,1},{6,2},{7,3},{8,12},{9,13},{10,... | collective-permute-start | bytes 1572872 | tf_op jit(solution)/shard_map/ppermute | solution.py:256
  75.2 0.1 add_convert_fusion.6
  75.3 1.8 %collective-permute-start.14 = (bf16[64,2048]{1,0:T(8,128)(2,1)S(1)}, bf16[64,2048]{1,0:T(8,128)(2,1)S(1)}, u32[]{:S(2)}, u32[]{:S(2)}) collective-permute-start(bf16[64,2048]{1,0:T(8,128)(2,1)S(1)} %get-tuple-element.155), channel_id=1, source_target_pairs={{0,2},{1,3},{2,0},{3,1},{4,6},{5,7},{6,4},{7,5},{8,10},{9,11},{10,... | collective-permute-start | bytes 786440 | tf_op jit(solution)/shard_map/ppermute | solution.py:256
  77.1 0.2 collective-permute-start.16
  77.4 5.7 %shard_map.81 = (bf16[256,2048]{1,0:T(8,128)(2,1)S(1)}, bf16[128,2048]{1,0:T(8,128)(2,1)S(1)}, bf16[64,2048]{1,0:T(8,128)(2,1)S(1)}, bf16[64,2048]{1,0:T(8,128)(2,1)S(1)}, bf16[320,768]{1,0:T(8,128)(2,1)S(1)}) custom-call(f32[16,512]{1,0:T(8,128)S(1)} %shard_map.78.tables, bf16[128,2048]{1,0:T(8,128)(2,1)S(1)} %constant_dynamic-update-slice_fusion.refs_0_, ...), custom_call_target="tpu_custom_call" | custom-call | flops 4362076160 | bytes 13631488 | tf_op jit(solution)/shard_map/pallas_call | solution.py:178
  83.0 0.3 collective-permute-start.18
  83.4 2.7 %shard_map.82 = (bf16[128,2048]{1,0:T(8,128)(2,1)S(1)}, bf16[128,2048]{1,0:T(8,128)(2,1)S(1)}, bf16[160,768]{1,0:T(8,128)(2,1)S(1)}) custom-call(f32[16,512]{1,0:T(8,128)S(1)} %shard_map.78.tables, bf16[128,2048]{1,0:T(8,128)(2,1)S(1)} %collective-permute-done.8.refs_0_, bf16[128,2048]{1,0:T(8,128)(2,1)S(1)} %collective-permute-done.19.refs_1_, ...), custom_call_target="tpu_custom_call" | custom-call | flops 1845493760 | bytes 11534336 | tf_op jit(solution)/shard_map/pallas_call | solution.py:178
  86.1 1.3 collective-permute-done.13.refs_0_
  87.4 0.5 collective-permute-start.21
  88.0 1.8 %collective-permute-start.22 = (bf16[64,2048]{1,0:T(8,128)(2,1)S(1)}, bf16[64,2048]{1,0:T(8,128)(2,1)S(1)}, u32[]{:S(2)}, u32[]{:S(2)}) collective-permute-start(bf16[64,2048]{1,0:T(8,128)(2,1)S(1)} %add_convert_fusion.11), channel_id=1, source_target_pairs={{0,2},{1,3},{2,0},{3,1},{4,6},{5,7},{6,4},{7,5},{8,10},{9,11},{10,... | collective-permute-start | bytes 786440 | tf_op jit(solution)/shard_map/ppermute | solution.py:256
  89.8 0.1 add_convert_fusion.10
  90.0 2.7 %shard_map.83 = (bf16[128,2048]{1,0:T(8,128)(2,1)S(1)}, bf16[128,2048]{1,0:T(8,128)(2,1)S(1)}, bf16[160,768]{1,0:T(8,128)(2,1)S(1)}) custom-call(f32[16,512]{1,0:T(8,128)S(1)} %shard_map.78.tables, bf16[128,2048]{1,0:T(8,128)(2,1)S(1)} %collective-permute-done.13.refs_0_, bf16[128,2048]{1,0:T(8,128)(2,1)S(1)} %collective-permute-done.20.refs_1_, ...), custom_call_target="tpu_custom_call" | custom-call | flops 1845493760 | bytes 11534336 | tf_op jit(solution)/shard_map/pallas_call | solution.py:178
  92.7 3.7 %collective-permute-done.22 = bf16[64,2048]{1,0:T(8,128)(2,1)S(1)} collective-permute-done((bf16[64,2048]{1,0:T(8,128)(2,1)S(1)}, bf16[64,2048]{1,0:T(8,128)(2,1)S(1)}, u32[]{:S(2)}, u32[]{:S(2)}) %collective-permute-start.22) | collective-permute-done | bytes 262176 | tf_op jit(solution)/shard_map/ppermute | solution.py:256
  96.4 0.5 collective-permute-start.28
  96.9 0.1 add_convert_fusion.7
  97.0 1.9 %collective-permute-start.26 = (bf16[64,2048]{1,0:T(8,128)(2,1)S(1)}, bf16[64,2048]{1,0:T(8,128)(2,1)S(1)}, u32[]{:S(2)}, u32[]{:S(2)}) collective-permute-start(bf16[64,2048]{1,0:T(8,128)(2,1)S(1)} %add_convert_fusion.7), channel_id=1, source_target_pairs={{0,8},{1,9},{2,10},{3,11},{4,12},{5,13},{6,14},{7,15},{8,0},{9,1},... | collective-permute-start | bytes 786440 | tf_op jit(solution)/shard_map/ppermute | solution.py:256
  98.9 1.6 %collective-permute-start.27 = (bf16[64,2048]{1,0:T(8,128)(2,1)S(1)}, bf16[64,2048]{1,0:T(8,128)(2,1)S(1)}, u32[]{:S(2)}, u32[]{:S(2)}) collective-permute-start(bf16[64,2048]{1,0:T(8,128)(2,1)S(1)} %add_convert_fusion.10), channel_id=1, source_target_pairs={{0,4},{1,5},{2,6},{3,7},{4,0},{5,1},{6,2},{7,3},{8,12},{9,13},{10,... | collective-permute-start | bytes 786440 | tf_op jit(solution)/shard_map/ppermute | solution.py:256
  100.6 0.1 add_convert_fusion.8
  100.7 1.8 %collective-permute-start.24 = (bf16[64,2048]{1,0:T(8,128)(2,1)S(1)}, bf16[64,2048]{1,0:T(8,128)(2,1)S(1)}, u32[]{:S(2)}, u32[]{:S(2)}) collective-permute-start(bf16[64,2048]{1,0:T(8,128)(2,1)S(1)} %get-tuple-element.159), channel_id=1, source_target_pairs={{0,2},{1,3},{2,0},{3,1},{4,6},{5,7},{6,4},{7,5},{8,10},{9,11},{10,... | collective-permute-start | bytes 786440 | tf_op jit(solution)/shard_map/ppermute | solution.py:256
  102.5 0.3 collective-permute-start.25
  102.8 0.1 add_convert_fusion
  102.9 9.4 %collective-permute-done.26.far_high = bf16[64,2048]{1,0:T(8,128)(2,1)S(1)} collective-permute-done((bf16[64,2048]{1,0:T(8,128)(2,1)S(1)}, bf16[64,2048]{1,0:T(8,128)(2,1)S(1)}, u32[]{:S(2)}, u32[]{:S(2)}) %collective-permute-start.26) | collective-permute-done | bytes 262176 | tf_op jit(solution)/shard_map/ppermute | solution.py:256
  112.3 2.2 %collective-permute-done.25 = bf16[64,2048]{1,0:T(8,128)(2,1)S(1)} collective-permute-done((bf16[64,2048]{1,0:T(8,128)(2,1)S(1)}, bf16[64,2048]{1,0:T(8,128)(2,1)S(1)}, u32[]{:S(2)}, u32[]{:S(2)}) %collective-permute-start.25) | collective-permute-done | bytes 262176 | tf_op jit(solution)/shard_map/ppermute | solution.py:256
  114.5 0.2 add_convert_fusion.4
  114.8 1.1 collective-permute-start.30
  115.9 0.4 collective-permute-start.31
  116.4 1.8 %collective-permute-start.32 = (bf16[64,2048]{1,0:T(8,128)(2,1)S(1)}, bf16[64,2048]{1,0:T(8,128)(2,1)S(1)}, u32[]{:S(2)}, u32[]{:S(2)}) collective-permute-start(bf16[64,2048]{1,0:T(8,128)(2,1)S(1)} %add_convert_fusion.3), channel_id=1, source_target_pairs={{0,2},{1,3},{2,0},{3,1},{4,6},{5,7},{6,4},{7,5},{8,10},{9,11},{10,... | collective-permute-start | bytes 786440 | tf_op jit(solution)/shard_map/ppermute | solution.py:256
  118.2 0.3 collective-permute-start.33
  118.5 3.1 %shard_map.84 = f32[768,768]{1,0:T(8,128)} custom-call(f32[16,512]{1,0:T(8,128)S(1)} %shard_map.78.tables, bf16[320,768]{1,0:T(8,128)(2,1)S(1)} %get-tuple-element.137.refs_0_, bf16[320,768]{1,0:T(8,128)(2,1)S(1)} %get-tuple-element.138.refs_1_, bf16[320,768]{1,0:T(8,128)(2,1)S(1)} %get-tuple-element.139.refs_2_, ...), custom_call_target="tpu_custom_call" | custom-call | flops 1509949440 | bytes 4325376 | tf_op jit(solution)/shard_map/pallas_call | solution.py:209
  121.6 6.9 %collective-permute-done.30 = bf16[64,2048]{1,0:T(8,128)(2,1)S(1)} collective-permute-done((bf16[64,2048]{1,0:T(8,128)(2,1)S(1)}, bf16[64,2048]{1,0:T(8,128)(2,1)S(1)}, u32[]{:S(2)}, u32[]{:S(2)}) %collective-permute-start.30) | collective-permute-done | bytes 262176 | tf_op jit(solution)/shard_map/ppermute | solution.py:256
  128.6 0.9 collective-permute-done.33
  129.4 0.1 add_convert_fusion.2
  129.6 1.3 collective-permute-start.34
  130.8 1.7 %collective-permute-start.36 = (bf16[128,2048]{1,0:T(8,128)(2,1)S(1)}, bf16[128,2048]{1,0:T(8,128)(2,1)S(1)}, u32[]{:S(2)}, u32[]{:S(2)}) collective-permute-start(bf16[128,2048]{1,0:T(8,128)(2,1)S(1)} %add_convert_fusion), channel_id=1, source_target_pairs={{0,2},{1,3},{2,0},{3,1},{4,6},{5,7},{6,4},{7,5},{8,10},{9,11},{10,... | collective-permute-start | bytes 1572872 | tf_op jit(solution)/shard_map/ppermute | solution.py:256
  132.6 0.1 add_convert_fusion.1
  132.7 1.7 %collective-permute-start.35 = (bf16[64,2048]{1,0:T(8,128)(2,1)S(1)}, bf16[64,2048]{1,0:T(8,128)(2,1)S(1)}, u32[]{:S(2)}, u32[]{:S(2)}) collective-permute-start(bf16[64,2048]{1,0:T(8,128)(2,1)S(1)} %add_convert_fusion.1), channel_id=1, source_target_pairs={{0,4},{1,5},{2,6},{3,7},{4,0},{5,1},{6,2},{7,3},{8,12},{9,13},{10,... | collective-permute-start | bytes 786440 | tf_op jit(solution)/shard_map/ppermute | solution.py:256
  134.4 8.1 %collective-permute-done.34.far_low = bf16[64,2048]{1,0:T(8,128)(2,1)S(1)} collective-permute-done((bf16[64,2048]{1,0:T(8,128)(2,1)S(1)}, bf16[64,2048]{1,0:T(8,128)(2,1)S(1)}, u32[]{:S(2)}, u32[]{:S(2)}) %collective-permute-start.34) | collective-permute-done | bytes 262176 | tf_op jit(solution)/shard_map/ppermute | solution.py:256
  142.5 1.7 %collective-permute-done.35.near_high = bf16[64,2048]{1,0:T(8,128)(2,1)S(1)} collective-permute-done((bf16[64,2048]{1,0:T(8,128)(2,1)S(1)}, bf16[64,2048]{1,0:T(8,128)(2,1)S(1)}, u32[]{:S(2)}, u32[]{:S(2)}) %collective-permute-start.35) | collective-permute-done | bytes 262176 | tf_op jit(solution)/shard_map/ppermute | solution.py:256
  144.2 1.1 shard_map.85
  (58 shorter events, 0.6 us)
Async XLA Ops:
  0.6 20.8 %collective-permute-start = (bf16[128,2048]{1,0:T(8,128)(2,1)}, bf16[128,2048]{1,0:T(8,128)(2,1)S(1)}, u32[]{:S(2)}, u32[]{:S(2)}) collective-permute-start(bf16[128,2048]{1,0:T(8,128)(2,1)} %refs_0_.1), channel_id=1, source_target_pairs={{0,4},{1,5},{2,6},{3,7},{4,0},{5,1},{6,2},{7,3},{8,12},{9,13},{10,... | collective-permute-start | bytes 1572872 | tf_op jit(solution)/shard_map/ppermute | solution.py:256
  3.7 17.8 %collective-permute-start.2 = (bf16[128,2048]{1,0:T(8,128)(2,1)}, bf16[128,2048]{1,0:T(8,128)(2,1)S(1)}, u32[]{:S(2)}, u32[]{:S(2)}) collective-permute-start(bf16[128,2048]{1,0:T(8,128)(2,1)} %refs_0_.1), channel_id=1, source_target_pairs={{0,2},{1,3},{2,0},{3,1},{4,6},{5,7},{6,4},{7,5},{8,10},{9,11},{10,... | collective-permute-start | bytes 1572872 | tf_op jit(solution)/shard_map/ppermute | solution.py:256
  5.2 16.2 %collective-permute-start.3 = (bf16[128,2048]{1,0:T(8,128)(2,1)}, bf16[128,2048]{1,0:T(8,128)(2,1)S(1)}, u32[]{:S(2)}, u32[]{:S(2)}) collective-permute-start(bf16[128,2048]{1,0:T(8,128)(2,1)} %refs_0_.1), channel_id=1, source_target_pairs={{0,1},{1,0},{2,3},{3,2},{4,5},{5,4},{6,7},{7,6},{8,9},{9,8},{10,11... | collective-permute-start | bytes 1572872 | tf_op jit(solution)/shard_map/ppermute | solution.py:256
  5.2 1.1 copy-start.6
  6.3 0.7 copy-start.8
  7.0 0.7 copy-start.9
  7.8 13.0 %collective-permute-start.1 = (bf16[64,2048]{1,0:T(8,128)(2,1)S(1)}, bf16[64,2048]{1,0:T(8,128)(2,1)S(1)}, u32[]{:S(2)}, u32[]{:S(2)}) collective-permute-start(bf16[64,2048]{1,0:T(8,128)(2,1)S(1)} %get-tuple-element.78), channel_id=1, source_target_pairs={{0,8},{1,9},{2,10},{3,11},{4,12},{5,13},{6,14},{7,15},{8,0},{9,1},... | collective-permute-start | bytes 786440 | tf_op jit(solution)/shard_map/ppermute | solution.py:256
  20.8 0.7 copy-start.10
  21.5 23.6 %collective-permute-start.7 = (bf16[128,2048]{1,0:T(8,128)(2,1)S(1)}, bf16[128,2048]{1,0:T(8,128)(2,1)S(1)}, u32[]{:S(2)}, u32[]{:S(2)}) collective-permute-start(bf16[128,2048]{1,0:T(8,128)(2,1)S(1)} %collective-permute-done.2.refs_1_), channel_id=1, source_target_pairs={{0,1},{1,0},{2,3},{3,2},{4,5},{5,4},{6,7},{7,6},{8,9},{9,8},{10,11... | collective-permute-start | bytes 1572872 | tf_op jit(solution)/shard_map/ppermute | solution.py:256
  43.8 14.4 %collective-permute-start.5 = (bf16[128,2048]{1,0:T(8,128)(2,1)S(1)}, bf16[128,2048]{1,0:T(8,128)(2,1)S(1)}, u32[]{:S(2)}, u32[]{:S(2)}) collective-permute-start(bf16[128,2048]{1,0:T(8,128)(2,1)S(1)} %collective-permute-done.refs_0_), channel_id=1, source_target_pairs={{0,2},{1,3},{2,0},{3,1},{4,6},{5,7},{6,4},{7,5},{8,10},{9,11},{10,... | collective-permute-start | bytes 1572872 | tf_op jit(solution)/shard_map/ppermute | solution.py:256
  43.8 14.4 %collective-permute-start.6 = (bf16[128,2048]{1,0:T(8,128)(2,1)S(1)}, bf16[128,2048]{1,0:T(8,128)(2,1)S(1)}, u32[]{:S(2)}, u32[]{:S(2)}) collective-permute-start(bf16[128,2048]{1,0:T(8,128)(2,1)S(1)} %collective-permute-done.refs_0_), channel_id=1, source_target_pairs={{0,1},{1,0},{2,3},{3,2},{4,5},{5,4},{6,7},{7,6},{8,9},{9,8},{10,11... | collective-permute-start | bytes 1572872 | tf_op jit(solution)/shard_map/ppermute | solution.py:256
  45.0 13.2 %collective-permute-start.4 = (bf16[64,2048]{1,0:T(8,128)(2,1)S(1)}, bf16[64,2048]{1,0:T(8,128)(2,1)S(1)}, u32[]{:S(2)}, u32[]{:S(2)}) collective-permute-start(bf16[64,2048]{1,0:T(8,128)(2,1)S(1)} %get-tuple-element.81), channel_id=1, source_target_pairs={{0,8},{1,9},{2,10},{3,11},{4,12},{5,13},{6,14},{7,15},{8,0},{9,1},... | collective-permute-start | bytes 786440 | tf_op jit(solution)/shard_map/ppermute | solution.py:256
  45.1 1.9 %copy-start = (bf16[1,2048,768]{2,1,0:T(8,128)(2,1)S(1)}, bf16[1,2048,768]{2,1,0:T(8,128)(2,1)}, u32[]{:S(2)}) copy-start(bf16[1,2048,768]{2,1,0:T(8,128)(2,1)} %param.9) | copy-start | bytes 9437188
  47.0 1.9 %copy-start.2 = (bf16[1,2048,768]{2,1,0:T(8,128)(2,1)S(1)}, bf16[1,2048,768]{2,1,0:T(8,128)(2,1)}, u32[]{:S(2)}) copy-start(bf16[1,2048,768]{2,1,0:T(8,128)(2,1)} %param.10) | copy-start | bytes 9437188
  48.9 1.9 %copy-start.4 = (bf16[1,768,2048]{2,1,0:T(8,128)(2,1)S(1)}, bf16[1,768,2048]{2,1,0:T(8,128)(2,1)}, u32[]{:S(2)}) copy-start(bf16[1,768,2048]{2,1,0:T(8,128)(2,1)} %param.11) | copy-start | bytes 9437188
  50.8 1.0 copy-start.7
  51.8 6.4 %copy-start.11 = (bf16[64,2048]{1,0:T(8,128)(2,1)S(1)}, bf16[64,2048]{1,0:T(8,128)(2,1)}, u32[]{:S(2)}) copy-start(bf16[64,2048]{1,0:T(8,128)(2,1)} %copy-done.10) | copy-start | bytes 786436
  51.8 8.8 %copy-start.1 = (bf16[1,2048,768]{2,1,0:T(8,128)(2,1)S(1)}, bf16[1,2048,768]{2,1,0:T(8,128)(2,1)}, u32[]{:S(2)}) copy-start(bf16[1,2048,768]{2,1,0:T(8,128)(2,1)} %param.9) | copy-start | bytes 9437188
  51.8 8.8 %copy-start.3 = (bf16[1,2048,768]{2,1,0:T(8,128)(2,1)S(1)}, bf16[1,2048,768]{2,1,0:T(8,128)(2,1)}, u32[]{:S(2)}) copy-start(bf16[1,2048,768]{2,1,0:T(8,128)(2,1)} %param.10) | copy-start | bytes 9437188
  51.8 8.8 %copy-start.5 = (bf16[1,768,2048]{2,1,0:T(8,128)(2,1)S(1)}, bf16[1,768,2048]{2,1,0:T(8,128)(2,1)}, u32[]{:S(2)}) copy-start(bf16[1,768,2048]{2,1,0:T(8,128)(2,1)} %param.11) | copy-start | bytes 9437188
  58.2 2.5 %collective-permute-start.11 = (bf16[128,2048]{1,0:T(8,128)(2,1)S(1)}, bf16[128,2048]{1,0:T(8,128)(2,1)S(1)}, u32[]{:S(2)}, u32[]{:S(2)}) collective-permute-start(bf16[128,2048]{1,0:T(8,128)(2,1)S(1)} %collective-permute-done.5.refs_1_), channel_id=1, source_target_pairs={{0,1},{1,0},{2,3},{3,2},{4,5},{5,4},{6,7},{7,6},{8,9},{9,8},{10,11... | collective-permute-start | bytes 1572872 | tf_op jit(solution)/shard_map/ppermute | solution.py:256
  58.3 14.4 %collective-permute-start.8 = (bf16[128,2048]{1,0:T(8,128)(2,1)S(1)}, bf16[128,2048]{1,0:T(8,128)(2,1)S(1)}, u32[]{:S(2)}, u32[]{:S(2)}) collective-permute-start(bf16[128,2048]{1,0:T(8,128)(2,1)S(1)} %constant_dynamic-update-slice_fusion.refs_0_), channel_id=1, source_target_pairs={{0,4},{1,5},{2,6},{3,7},{4,0},{5,1},{6,2},{7,3},{8,12},{9,13},{10,... | collective-permute-start | bytes 1572872 | tf_op jit(solution)/shard_map/ppermute | solution.py:256
  58.3 14.6 %collective-permute-start.9 = (bf16[128,2048]{1,0:T(8,128)(2,1)S(1)}, bf16[128,2048]{1,0:T(8,128)(2,1)S(1)}, u32[]{:S(2)}, u32[]{:S(2)}) collective-permute-start(bf16[128,2048]{1,0:T(8,128)(2,1)S(1)} %constant_dynamic-update-slice_fusion.refs_0_), channel_id=1, source_target_pairs={{0,2},{1,3},{2,0},{3,1},{4,6},{5,7},{6,4},{7,5},{8,10},{9,11},{10,... | collective-permute-start | bytes 1572872 | tf_op jit(solution)/shard_map/ppermute | solution.py:256
  60.5 12.5 %collective-permute-start.10 = (bf16[128,2048]{1,0:T(8,128)(2,1)S(1)}, bf16[128,2048]{1,0:T(8,128)(2,1)S(1)}, u32[]{:S(2)}, u32[]{:S(2)}) collective-permute-start(bf16[128,2048]{1,0:T(8,128)(2,1)S(1)} %constant_dynamic-update-slice_fusion.refs_0_), channel_id=1, source_target_pairs={{0,1},{1,0},{2,3},{3,2},{4,5},{5,4},{6,7},{7,6},{8,9},{9,8},{10,11... | collective-permute-start | bytes 1572872 | tf_op jit(solution)/shard_map/ppermute | solution.py:256
  66.1 6.9 %collective-permute-start.12 = (bf16[128,2048]{1,0:T(8,128)(2,1)S(1)}, bf16[128,2048]{1,0:T(8,128)(2,1)S(1)}, u32[]{:S(2)}, u32[]{:S(2)}) collective-permute-start(bf16[128,2048]{1,0:T(8,128)(2,1)S(1)} %get-tuple-element.96), channel_id=1, source_target_pairs={{0,1},{1,0},{2,3},{3,2},{4,5},{5,4},{6,7},{7,6},{8,9},{9,8},{10,11... | collective-permute-start | bytes 1572872 | tf_op jit(solution)/shard_map/ppermute | solution.py:256
  73.0 4.1 %collective-permute-start.17 = (bf16[128,2048]{1,0:T(8,128)(2,1)S(1)}, bf16[128,2048]{1,0:T(8,128)(2,1)S(1)}, u32[]{:S(2)}, u32[]{:S(2)}) collective-permute-start(bf16[128,2048]{1,0:T(8,128)(2,1)S(1)} %collective-permute-done.9.refs_1_), channel_id=1, source_target_pairs={{0,1},{1,0},{2,3},{3,2},{4,5},{5,4},{6,7},{7,6},{8,9},{9,8},{10,11... | collective-permute-start | bytes 1572872 | tf_op jit(solution)/shard_map/ppermute | solution.py:256
  73.0 13.1 %collective-permute-start.15 = (bf16[256,2048]{1,0:T(8,128)(2,1)S(1)}, bf16[256,2048]{1,0:T(8,128)(2,1)S(1)}, u32[]{:S(2)}, u32[]{:S(2)}) collective-permute-start(bf16[256,2048]{1,0:T(8,128)(2,1)S(1)} %get-tuple-element.100), channel_id=1, source_target_pairs={{0,1},{1,0},{2,3},{3,2},{4,5},{5,4},{6,7},{7,6},{8,9},{9,8},{10,11... | collective-permute-start | bytes 3145736 | tf_op jit(solution)/shard_map/ppermute | solution.py:256
  73.5 13.9 %collective-permute-start.13 = (bf16[128,2048]{1,0:T(8,128)(2,1)S(1)}, bf16[128,2048]{1,0:T(8,128)(2,1)S(1)}, u32[]{:S(2)}, u32[]{:S(2)}) collective-permute-start(bf16[128,2048]{1,0:T(8,128)(2,1)S(1)} %collective-permute-done.9.refs_1_), channel_id=1, source_target_pairs={{0,4},{1,5},{2,6},{3,7},{4,0},{5,1},{6,2},{7,3},{8,12},{9,13},{10,... | collective-permute-start | bytes 1572872 | tf_op jit(solution)/shard_map/ppermute | solution.py:256
  75.2 7.9 %collective-permute-start.19 = (bf16[128,2048]{1,0:T(8,128)(2,1)S(1)}, bf16[128,2048]{1,0:T(8,128)(2,1)S(1)}, u32[]{:S(2)}, u32[]{:S(2)}) collective-permute-start(bf16[128,2048]{1,0:T(8,128)(2,1)S(1)} %collective-permute-done.8.refs_0_), channel_id=1, source_target_pairs={{0,1},{1,0},{2,3},{3,2},{4,5},{5,4},{6,7},{7,6},{8,9},{9,8},{10,11... | collective-permute-start | bytes 1572872 | tf_op jit(solution)/shard_map/ppermute | solution.py:256
  75.3 10.8 %collective-permute-start.14 = (bf16[64,2048]{1,0:T(8,128)(2,1)S(1)}, bf16[64,2048]{1,0:T(8,128)(2,1)S(1)}, u32[]{:S(2)}, u32[]{:S(2)}) collective-permute-start(bf16[64,2048]{1,0:T(8,128)(2,1)S(1)} %get-tuple-element.155), channel_id=1, source_target_pairs={{0,2},{1,3},{2,0},{3,1},{4,6},{5,7},{6,4},{7,5},{8,10},{9,11},{10,... | collective-permute-start | bytes 786440 | tf_op jit(solution)/shard_map/ppermute | solution.py:256
  77.1 10.3 %collective-permute-start.16 = (bf16[128,2048]{1,0:T(8,128)(2,1)S(1)}, bf16[128,2048]{1,0:T(8,128)(2,1)S(1)}, u32[]{:S(2)}, u32[]{:S(2)}) collective-permute-start(bf16[128,2048]{1,0:T(8,128)(2,1)S(1)} %get-tuple-element.101), channel_id=1, source_target_pairs={{0,1},{1,0},{2,3},{3,2},{4,5},{5,4},{6,7},{7,6},{8,9},{9,8},{10,11... | collective-permute-start | bytes 1572872 | tf_op jit(solution)/shard_map/ppermute | solution.py:256
  83.0 4.4 %collective-permute-start.18 = (bf16[64,2048]{1,0:T(8,128)(2,1)S(1)}, bf16[64,2048]{1,0:T(8,128)(2,1)S(1)}, u32[]{:S(2)}, u32[]{:S(2)}) collective-permute-start(bf16[64,2048]{1,0:T(8,128)(2,1)S(1)} %get-tuple-element.103), channel_id=1, source_target_pairs={{0,1},{1,0},{2,3},{3,2},{4,5},{5,4},{6,7},{7,6},{8,9},{9,8},{10,11... | collective-permute-start | bytes 786440 | tf_op jit(solution)/shard_map/ppermute | solution.py:256
  87.4 2.5 %collective-permute-start.20 = (bf16[128,2048]{1,0:T(8,128)(2,1)S(1)}, bf16[128,2048]{1,0:T(8,128)(2,1)S(1)}, u32[]{:S(2)}, u32[]{:S(2)}) collective-permute-start(bf16[128,2048]{1,0:T(8,128)(2,1)S(1)} %collective-permute-done.13.refs_0_), channel_id=1, source_target_pairs={{0,1},{1,0},{2,3},{3,2},{4,5},{5,4},{6,7},{7,6},{8,9},{9,8},{10,11... | collective-permute-start | bytes 1572872 | tf_op jit(solution)/shard_map/ppermute | solution.py:256
  87.4 9.0 %collective-permute-start.21 = (bf16[128,2048]{1,0:T(8,128)(2,1)S(1)}, bf16[128,2048]{1,0:T(8,128)(2,1)S(1)}, u32[]{:S(2)}, u32[]{:S(2)}) collective-permute-start(bf16[128,2048]{1,0:T(8,128)(2,1)S(1)} %get-tuple-element.117), channel_id=1, source_target_pairs={{0,1},{1,0},{2,3},{3,2},{4,5},{5,4},{6,7},{7,6},{8,9},{9,8},{10,11... | collective-permute-start | bytes 1572872 | tf_op jit(solution)/shard_map/ppermute | solution.py:256
  88.0 8.4 %collective-permute-start.22 = (bf16[64,2048]{1,0:T(8,128)(2,1)S(1)}, bf16[64,2048]{1,0:T(8,128)(2,1)S(1)}, u32[]{:S(2)}, u32[]{:S(2)}) collective-permute-start(bf16[64,2048]{1,0:T(8,128)(2,1)S(1)} %add_convert_fusion.11), channel_id=1, source_target_pairs={{0,2},{1,3},{2,0},{3,1},{4,6},{5,7},{6,4},{7,5},{8,10},{9,11},{10,... | collective-permute-start | bytes 786440 | tf_op jit(solution)/shard_map/ppermute | solution.py:256
  96.4 4.2 %collective-permute-start.23 = (bf16[128,2048]{1,0:T(8,128)(2,1)S(1)}, bf16[128,2048]{1,0:T(8,128)(2,1)S(1)}, u32[]{:S(2)}, u32[]{:S(2)}) collective-permute-start(bf16[128,2048]{1,0:T(8,128)(2,1)S(1)} %get-tuple-element.123), channel_id=1, source_target_pairs={{0,1},{1,0},{2,3},{3,2},{4,5},{5,4},{6,7},{7,6},{8,9},{9,8},{10,11... | collective-permute-start | bytes 1572872 | tf_op jit(solution)/shard_map/ppermute | solution.py:256
  96.4 6.1 %collective-permute-start.28 = (bf16[64,2048]{1,0:T(8,128)(2,1)S(1)}, bf16[64,2048]{1,0:T(8,128)(2,1)S(1)}, u32[]{:S(2)}, u32[]{:S(2)}) collective-permute-start(bf16[64,2048]{1,0:T(8,128)(2,1)S(1)} %get-tuple-element.129), channel_id=1, source_target_pairs={{0,1},{1,0},{2,3},{3,2},{4,5},{5,4},{6,7},{7,6},{8,9},{9,8},{10,11... | collective-permute-start | bytes 786440 | tf_op jit(solution)/shard_map/ppermute | solution.py:256
  96.9 6.0 %collective-permute-start.29 = (bf16[128,2048]{1,0:T(8,128)(2,1)S(1)}, bf16[128,2048]{1,0:T(8,128)(2,1)S(1)}, u32[]{:S(2)}, u32[]{:S(2)}) collective-permute-start(bf16[128,2048]{1,0:T(8,128)(2,1)S(1)} %get-tuple-element.130), channel_id=1, source_target_pairs={{0,1},{1,0},{2,3},{3,2},{4,5},{5,4},{6,7},{7,6},{8,9},{9,8},{10,11... | collective-permute-start | bytes 1572872 | tf_op jit(solution)/shard_map/ppermute | solution.py:256
  97.0 15.3 %collective-permute-start.26 = (bf16[64,2048]{1,0:T(8,128)(2,1)S(1)}, bf16[64,2048]{1,0:T(8,128)(2,1)S(1)}, u32[]{:S(2)}, u32[]{:S(2)}) collective-permute-start(bf16[64,2048]{1,0:T(8,128)(2,1)S(1)} %add_convert_fusion.7), channel_id=1, source_target_pairs={{0,8},{1,9},{2,10},{3,11},{4,12},{5,13},{6,14},{7,15},{8,0},{9,1},... | collective-permute-start | bytes 786440 | tf_op jit(solution)/shard_map/ppermute | solution.py:256
  98.9 13.4 %collective-permute-start.27 = (bf16[64,2048]{1,0:T(8,128)(2,1)S(1)}, bf16[64,2048]{1,0:T(8,128)(2,1)S(1)}, u32[]{:S(2)}, u32[]{:S(2)}) collective-permute-start(bf16[64,2048]{1,0:T(8,128)(2,1)S(1)} %add_convert_fusion.10), channel_id=1, source_target_pairs={{0,4},{1,5},{2,6},{3,7},{4,0},{5,1},{6,2},{7,3},{8,12},{9,13},{10,... | collective-permute-start | bytes 786440 | tf_op jit(solution)/shard_map/ppermute | solution.py:256
  100.7 11.6 %collective-permute-start.24 = (bf16[64,2048]{1,0:T(8,128)(2,1)S(1)}, bf16[64,2048]{1,0:T(8,128)(2,1)S(1)}, u32[]{:S(2)}, u32[]{:S(2)}) collective-permute-start(bf16[64,2048]{1,0:T(8,128)(2,1)S(1)} %get-tuple-element.159), channel_id=1, source_target_pairs={{0,2},{1,3},{2,0},{3,1},{4,6},{5,7},{6,4},{7,5},{8,10},{9,11},{10,... | collective-permute-start | bytes 786440 | tf_op jit(solution)/shard_map/ppermute | solution.py:256
  102.5 12.0 %collective-permute-start.25 = (bf16[64,2048]{1,0:T(8,128)(2,1)S(1)}, bf16[64,2048]{1,0:T(8,128)(2,1)S(1)}, u32[]{:S(2)}, u32[]{:S(2)}) collective-permute-start(bf16[64,2048]{1,0:T(8,128)(2,1)S(1)} %get-tuple-element.158), channel_id=1, source_target_pairs={{0,2},{1,3},{2,0},{3,1},{4,6},{5,7},{6,4},{7,5},{8,10},{9,11},{10,... | collective-permute-start | bytes 786440 | tf_op jit(solution)/shard_map/ppermute | solution.py:256
  114.8 13.8 %collective-permute-start.30 = (bf16[64,2048]{1,0:T(8,128)(2,1)S(1)}, bf16[64,2048]{1,0:T(8,128)(2,1)S(1)}, u32[]{:S(2)}, u32[]{:S(2)}) collective-permute-start(bf16[64,2048]{1,0:T(8,128)(2,1)S(1)} %get-tuple-element.157), channel_id=1, source_target_pairs={{0,8},{1,9},{2,10},{3,11},{4,12},{5,13},{6,14},{7,15},{8,0},{9,1},... | collective-permute-start | bytes 786440 | tf_op jit(solution)/shard_map/ppermute | solution.py:256
  115.9 12.6 %collective-permute-start.31 = (bf16[64,2048]{1,0:T(8,128)(2,1)S(1)}, bf16[64,2048]{1,0:T(8,128)(2,1)S(1)}, u32[]{:S(2)}, u32[]{:S(2)}) collective-permute-start(bf16[64,2048]{1,0:T(8,128)(2,1)S(1)} %get-tuple-element.156), channel_id=1, source_target_pairs={{0,4},{1,5},{2,6},{3,7},{4,0},{5,1},{6,2},{7,3},{8,12},{9,13},{10,... | collective-permute-start | bytes 786440 | tf_op jit(solution)/shard_map/ppermute | solution.py:256
  116.4 12.2 %collective-permute-start.32 = (bf16[64,2048]{1,0:T(8,128)(2,1)S(1)}, bf16[64,2048]{1,0:T(8,128)(2,1)S(1)}, u32[]{:S(2)}, u32[]{:S(2)}) collective-permute-start(bf16[64,2048]{1,0:T(8,128)(2,1)S(1)} %add_convert_fusion.3), channel_id=1, source_target_pairs={{0,2},{1,3},{2,0},{3,1},{4,6},{5,7},{6,4},{7,5},{8,10},{9,11},{10,... | collective-permute-start | bytes 786440 | tf_op jit(solution)/shard_map/ppermute | solution.py:256
  118.2 11.2 %collective-permute-start.33 = (bf16[64,2048]{1,0:T(8,128)(2,1)S(1)}, bf16[64,2048]{1,0:T(8,128)(2,1)S(1)}, u32[]{:S(2)}, u32[]{:S(2)}) collective-permute-start(bf16[64,2048]{1,0:T(8,128)(2,1)S(1)} %get-tuple-element.135), channel_id=1, source_target_pairs={{0,2},{1,3},{2,0},{3,1},{4,6},{5,7},{6,4},{7,5},{8,10},{9,11},{10,... | collective-permute-start | bytes 786440 | tf_op jit(solution)/shard_map/ppermute | solution.py:256
  129.6 12.9 %collective-permute-start.34 = (bf16[64,2048]{1,0:T(8,128)(2,1)S(1)}, bf16[64,2048]{1,0:T(8,128)(2,1)S(1)}, u32[]{:S(2)}, u32[]{:S(2)}) collective-permute-start(bf16[64,2048]{1,0:T(8,128)(2,1)S(1)} %add_convert_fusion.2), channel_id=1, source_target_pairs={{0,8},{1,9},{2,10},{3,11},{4,12},{5,13},{6,14},{7,15},{8,0},{9,1},... | collective-permute-start | bytes 786440 | tf_op jit(solution)/shard_map/ppermute | solution.py:256
  130.8 13.4 %collective-permute-start.36 = (bf16[128,2048]{1,0:T(8,128)(2,1)S(1)}, bf16[128,2048]{1,0:T(8,128)(2,1)S(1)}, u32[]{:S(2)}, u32[]{:S(2)}) collective-permute-start(bf16[128,2048]{1,0:T(8,128)(2,1)S(1)} %add_convert_fusion), channel_id=1, source_target_pairs={{0,2},{1,3},{2,0},{3,1},{4,6},{5,7},{6,4},{7,5},{8,10},{9,11},{10,... | collective-permute-start | bytes 1572872 | tf_op jit(solution)/shard_map/ppermute | solution.py:256
  132.7 11.5 %collective-permute-start.35 = (bf16[64,2048]{1,0:T(8,128)(2,1)S(1)}, bf16[64,2048]{1,0:T(8,128)(2,1)S(1)}, u32[]{:S(2)}, u32[]{:S(2)}) collective-permute-start(bf16[64,2048]{1,0:T(8,128)(2,1)S(1)} %add_convert_fusion.1), channel_id=1, source_target_pairs={{0,4},{1,5},{2,6},{3,7},{4,0},{5,1},{6,2},{7,3},{8,12},{9,13},{10,... | collective-permute-start | bytes 786440 | tf_op jit(solution)/shard_map/ppermute | solution.py:256

commit v28 on v22

--- a/solution.py
+++ b/solution.py
@@ -64,7 +64,7 @@
             pltpu.VMEM((top, tok), probs.dtype),
             pltpu.SemaphoreType.DMA((4,)),
         ],
-        compiler_params=pltpu.CompilerParams(vmem_limit_bytes=4 * 1024 * 1024),
+        compiler_params=pltpu.CompilerParams(vmem_limit_bytes=58 * 1024 * 1024),
     )(routes.T, probs.T, tokens)
 
 

time: 127 us -> 126 us (level)
  local copies, waits for them, and re-layouts: 9.97 us -> 6.84 us
  Pallas kernels: 27.1 us -> 28.9 us
    unnamed x25 -> x15, local copies, waits for them, and re-layouts: 9.86 us -> 6.73 us
    pallas_call x1, Pallas kernels: 0.12 us -> 1.89 us  [prepare_pass(): pl.pallas_call(prepare_kernel, out_shape=(jax.ShapeDtypeStruct((experts,...]
  transfers between devices with their start and end apart: 37 -> 37, of which waited for: 11 -> 11; matrix products, arithmetic and copies ran while one was open for 1% -> 1% of each run, Pallas kernels for 21% -> 22%
where the time goes in v28:
time: 126 us
  waiting for transfers between devices  42.1 us (33%)
  starting transfers between devices  31.1 us (25%)
  Pallas kernels  28.9 us (23%)
  blocking collectives  14.9 us (12%)
  local copies, waits for them, and re-layouts  6.84 us (5%)
    ppermute x37, waiting for transfers between devices, swapped(): return lax.ppermute(array, 'expert', [(i, i ^ bit) for i in range(size)])  42.1 us
    ppermute x37, starting transfers between devices, swapped(): return lax.ppermute(array, 'expert', [(i, i ^ bit) for i in range(size)])  31.1 us
    pallas_call x5, Pallas kernels, plane_pass(): pl.pallas_call(functools.partial(plane_kernel, k, picked, len(pieces)), o...  22 us
    all_to_all x1, blocking collectives, staged(): lax.all_to_all(mine, 'expert', split_axis=0, concat_axis=0, tiled=True)  14.9 us
    unnamed x15, local copies, waits for them, and re-layouts  6.73 us
    pallas_call x1, Pallas kernels, gram_pass(): pl.pallas_call(gram_kernel, out_shape=jax.ShapeDtypeStruct((hidden, hidde...  3.15 us
  transfers between devices with their start and end apart: 37, of which 11 were waited for; matrix products, arithmetic and copies ran while one was open for 1% of the time, Pallas kernels for 22%

profile of v28, /device:TPU:0, one launch (start us, length us, event | category | flops | bytes accessed | tf_op | source)
XLA Modules:
  0.0 126.0 jit_solution(17307191884493280387)
XLA Ops:
  0.6 3.1 %collective-permute-start = (bf16[128,2048]{1,0:T(8,128)(2,1)}, bf16[128,2048]{1,0:T(8,128)(2,1)S(1)}, u32[]{:S(2)}, u32[]{:S(2)}) collective-permute-start(bf16[128,2048]{1,0:T(8,128)(2,1)} %refs_0_.1), channel_id=1, source_target_pairs={{0,4},{1,5},{2,6},{3,7},{4,0},{5,1},{6,2},{7,3},{8,12},{9,13},{10,... | collective-permute-start | bytes 1572872 | tf_op jit(solution)/shard_map/ppermute | solution.py:256
  3.7 1.5 %collective-permute-start.2 = (bf16[128,2048]{1,0:T(8,128)(2,1)}, bf16[128,2048]{1,0:T(8,128)(2,1)S(1)}, u32[]{:S(2)}, u32[]{:S(2)}) collective-permute-start(bf16[128,2048]{1,0:T(8,128)(2,1)} %refs_0_.1), channel_id=1, source_target_pairs={{0,2},{1,3},{2,0},{3,1},{4,6},{5,7},{6,4},{7,5},{8,10},{9,11},{10,... | collective-permute-start | bytes 1572872 | tf_op jit(solution)/shard_map/ppermute | solution.py:256
  5.2 1.9 %shard_map.77 = (f32[16,128]{1,0:T(8,128)}, bf16[64,2048]{1,0:T(8,128)(2,1)}, bf16[64,2048]{1,0:T(8,128)(2,1)}) custom-call(s32[8,128]{1,0:T(8,128)} %bitcast.43, f32[8,128]{1,0:T(8,128)} %bitcast.44, bf16[128,2048]{1,0:T(8,128)(2,1)} %refs_0_.1), custom_call_target="tpu_custom_call" | custom-call | tf_op jit(solution)/shard_map/pallas_call | solution.py:57
  7.1 2.7 %collective-permute-start.1 = (bf16[64,2048]{1,0:T(8,128)(2,1)}, bf16[64,2048]{1,0:T(8,128)(2,1)S(1)}, u32[]{:S(2)}, u32[]{:S(2)}) collective-permute-start(bf16[64,2048]{1,0:T(8,128)(2,1)} %get-tuple-element.79), channel_id=1, source_target_pairs={{0,8},{1,9},{2,10},{3,11},{4,12},{5,13},{6,14},{7,15},{8,0},{9,1},... | collective-permute-start | bytes 786440 | tf_op jit(solution)/shard_map/ppermute | solution.py:256
  9.8 14.9 %all_to_all.12 = f32[16,1,128]{2,1,0:T(1,128)S(1)} all-to-all(f32[16,1,128]{2,1,0:T(1,128)} %bitcast.42), channel_id=1, replica_groups=mesh['parts'=2,'expert'=16] {'expert'}, dimensions={0} | all-to-all | bytes 16384 | tf_op jit(solution)/shard_map/all_to_all | solution.py:285
  24.7 0.1 collective-permute-start.7
  24.8 0.6 collective-permute-start.5
  25.4 0.2 collective-permute-start.6
  25.6 0.1 stack.67.spots
  25.6 0.7 collective-permute-start.4
  26.3 0.7 shard_map.78.tables
  27.1 1.9 %copy-done = bf16[1,2048,768]{2,1,0:T(8,128)(2,1)S(1)} copy-done((bf16[1,2048,768]{2,1,0:T(8,128)(2,1)S(1)}, bf16[1,2048,768]{2,1,0:T(8,128)(2,1)}, u32[]{:S(2)}) %copy-start) | copy-done | bytes 3145752
  29.0 1.9 %copy-done.2 = bf16[1,2048,768]{2,1,0:T(8,128)(2,1)S(1)} copy-done((bf16[1,2048,768]{2,1,0:T(8,128)(2,1)S(1)}, bf16[1,2048,768]{2,1,0:T(8,128)(2,1)}, u32[]{:S(2)}) %copy-start.2) | copy-done | bytes 3145752
  30.9 1.9 %copy-done.4 = bf16[1,768,2048]{2,1,0:T(8,128)(2,1)S(1)} copy-done((bf16[1,768,2048]{2,1,0:T(8,128)(2,1)S(1)}, bf16[1,768,2048]{2,1,0:T(8,128)(2,1)}, u32[]{:S(2)}) %copy-start.4) | copy-done | bytes 3145752
  32.8 1.0 copy-done.6
  33.8 5.5 %shard_map.79 = (bf16[256,2048]{1,0:T(8,128)(2,1)S(1)}, bf16[256,2048]{1,0:T(8,128)(2,1)S(1)}, bf16[320,768]{1,0:T(8,128)(2,1)S(1)}) custom-call(f32[16,512]{1,0:T(8,128)S(1)} %shard_map.78.tables, bf16[128,2048]{1,0:T(8,128)(2,1)S(1)} %copy-done.6, bf16[128,2048]{1,0:T(8,128)(2,1)S(1)} %collective-permute-done.2.refs_1_, ...), custom_call_target="tpu_custom_call" | custom-call | flops 4362076160 | bytes 13631488 | tf_op jit(solution)/shard_map/pallas_call | solution.py:178
  39.3 1.7 %collective-permute-done.4 = bf16[64,2048]{1,0:T(8,128)(2,1)S(1)} collective-permute-done((bf16[64,2048]{1,0:T(8,128)(2,1)}, bf16[64,2048]{1,0:T(8,128)(2,1)S(1)}, u32[]{:S(2)}, u32[]{:S(2)}) %collective-permute-start.4) | collective-permute-done | bytes 262176 | tf_op jit(solution)/shard_map/ppermute | solution.py:256
  41.1 0.2 collective-permute-start.8
  41.2 1.5 %collective-permute-start.9 = (bf16[128,2048]{1,0:T(8,128)(2,1)S(1)}, bf16[128,2048]{1,0:T(8,128)(2,1)S(1)}, u32[]{:S(2)}, u32[]{:S(2)}) collective-permute-start(bf16[128,2048]{1,0:T(8,128)(2,1)S(1)} %constant_dynamic-update-slice_fusion.refs_0_), channel_id=1, source_target_pairs={{0,2},{1,3},{2,0},{3,1},{4,6},{5,7},{6,4},{7,5},{8,10},{9,11},{10,... | collective-permute-start | bytes 1572872 | tf_op jit(solution)/shard_map/ppermute | solution.py:256
  42.7 0.2 collective-permute-start.10
  42.9 5.5 %shard_map.80 = (bf16[256,2048]{1,0:T(8,128)(2,1)S(1)}, bf16[128,2048]{1,0:T(8,128)(2,1)S(1)}, bf16[128,2048]{1,0:T(8,128)(2,1)S(1)}, bf16[320,768]{1,0:T(8,128)(2,1)S(1)}) custom-call(f32[16,512]{1,0:T(8,128)S(1)} %shard_map.78.tables, bf16[128,2048]{1,0:T(8,128)(2,1)S(1)} %collective-permute-done.refs_0_, ...), custom_call_target="tpu_custom_call" | custom-call | flops 4362076160 | bytes 13631488 | tf_op jit(solution)/shard_map/pallas_call | solution.py:178
  48.4 0.4 collective-permute-start.12
  48.8 6.7 %collective-permute-done.8.refs_0_ = bf16[128,2048]{1,0:T(8,128)(2,1)S(1)} collective-permute-done((bf16[128,2048]{1,0:T(8,128)(2,1)S(1)}, bf16[128,2048]{1,0:T(8,128)(2,1)S(1)}, u32[]{:S(2)}, u32[]{:S(2)}) %collective-permute-start.8) | collective-permute-done | bytes 524320 | tf_op jit(solution)/shard_map/ppermute | solution.py:256
  55.5 0.1 collective-permute-done.9.refs_1_
  55.6 0.5 collective-permute-start.15
  56.1 1.6 %collective-permute-start.13 = (bf16[128,2048]{1,0:T(8,128)(2,1)S(1)}, bf16[128,2048]{1,0:T(8,128)(2,1)S(1)}, u32[]{:S(2)}, u32[]{:S(2)}) collective-permute-start(bf16[128,2048]{1,0:T(8,128)(2,1)S(1)} %collective-permute-done.9.refs_1_), channel_id=1, source_target_pairs={{0,4},{1,5},{2,6},{3,7},{4,0},{5,1},{6,2},{7,3},{8,12},{9,13},{10,... | collective-permute-start | bytes 1572872 | tf_op jit(solution)/shard_map/ppermute | solution.py:256
  57.7 0.1 add_convert_fusion.6
  57.9 1.5 %collective-permute-start.14 = (bf16[64,2048]{1,0:T(8,128)(2,1)S(1)}, bf16[64,2048]{1,0:T(8,128)(2,1)S(1)}, u32[]{:S(2)}, u32[]{:S(2)}) collective-permute-start(bf16[64,2048]{1,0:T(8,128)(2,1)S(1)} %get-tuple-element.157), channel_id=1, source_target_pairs={{0,2},{1,3},{2,0},{3,1},{4,6},{5,7},{6,4},{7,5},{8,10},{9,11},{10,... | collective-permute-start | bytes 786440 | tf_op jit(solution)/shard_map/ppermute | solution.py:256
  59.4 0.2 collective-permute-start.16
  59.6 5.7 %shard_map.81 = (bf16[256,2048]{1,0:T(8,128)(2,1)S(1)}, bf16[128,2048]{1,0:T(8,128)(2,1)S(1)}, bf16[64,2048]{1,0:T(8,128)(2,1)S(1)}, bf16[64,2048]{1,0:T(8,128)(2,1)S(1)}, bf16[320,768]{1,0:T(8,128)(2,1)S(1)}) custom-call(f32[16,512]{1,0:T(8,128)S(1)} %shard_map.78.tables, bf16[128,2048]{1,0:T(8,128)(2,1)S(1)} %constant_dynamic-update-slice_fusion.refs_0_, ...), custom_call_target="tpu_custom_call" | custom-call | flops 4362076160 | bytes 13631488 | tf_op jit(solution)/shard_map/pallas_call | solution.py:178
  65.3 0.3 collective-permute-start.18
  65.6 2.7 %shard_map.82 = (bf16[128,2048]{1,0:T(8,128)(2,1)S(1)}, bf16[128,2048]{1,0:T(8,128)(2,1)S(1)}, bf16[160,768]{1,0:T(8,128)(2,1)S(1)}) custom-call(f32[16,512]{1,0:T(8,128)S(1)} %shard_map.78.tables, bf16[128,2048]{1,0:T(8,128)(2,1)S(1)} %collective-permute-done.8.refs_0_, bf16[128,2048]{1,0:T(8,128)(2,1)S(1)} %collective-permute-done.19.refs_1_, ...), custom_call_target="tpu_custom_call" | custom-call | flops 1845493760 | bytes 11534336 | tf_op jit(solution)/shard_map/pallas_call | solution.py:178
  68.4 1.6 %collective-permute-done.13.refs_0_ = bf16[128,2048]{1,0:T(8,128)(2,1)S(1)} collective-permute-done((bf16[128,2048]{1,0:T(8,128)(2,1)S(1)}, bf16[128,2048]{1,0:T(8,128)(2,1)S(1)}, u32[]{:S(2)}, u32[]{:S(2)}) %collective-permute-start.13) | collective-permute-done | bytes 524320 | tf_op jit(solution)/shard_map/ppermute | solution.py:256
  70.0 0.5 collective-permute-start.21
  70.6 1.5 %collective-permute-start.22 = (bf16[64,2048]{1,0:T(8,128)(2,1)S(1)}, bf16[64,2048]{1,0:T(8,128)(2,1)S(1)}, u32[]{:S(2)}, u32[]{:S(2)}) collective-permute-start(bf16[64,2048]{1,0:T(8,128)(2,1)S(1)} %add_convert_fusion.11), channel_id=1, source_target_pairs={{0,2},{1,3},{2,0},{3,1},{4,6},{5,7},{6,4},{7,5},{8,10},{9,11},{10,... | collective-permute-start | bytes 786440 | tf_op jit(solution)/shard_map/ppermute | solution.py:256
  72.1 0.1 add_convert_fusion.10
  72.2 2.7 %shard_map.83 = (bf16[128,2048]{1,0:T(8,128)(2,1)S(1)}, bf16[128,2048]{1,0:T(8,128)(2,1)S(1)}, bf16[160,768]{1,0:T(8,128)(2,1)S(1)}) custom-call(f32[16,512]{1,0:T(8,128)S(1)} %shard_map.78.tables, bf16[128,2048]{1,0:T(8,128)(2,1)S(1)} %collective-permute-done.13.refs_0_, bf16[128,2048]{1,0:T(8,128)(2,1)S(1)} %collective-permute-done.20.refs_1_, ...), custom_call_target="tpu_custom_call" | custom-call | flops 1845493760 | bytes 11534336 | tf_op jit(solution)/shard_map/pallas_call | solution.py:178
  74.9 4.0 %collective-permute-done.22 = bf16[64,2048]{1,0:T(8,128)(2,1)S(1)} collective-permute-done((bf16[64,2048]{1,0:T(8,128)(2,1)S(1)}, bf16[64,2048]{1,0:T(8,128)(2,1)S(1)}, u32[]{:S(2)}, u32[]{:S(2)}) %collective-permute-start.22) | collective-permute-done | bytes 262176 | tf_op jit(solution)/shard_map/ppermute | solution.py:256
  78.9 0.5 collective-permute-start.28
  79.4 0.1 add_convert_fusion.7
  79.6 1.8 %collective-permute-start.26 = (bf16[64,2048]{1,0:T(8,128)(2,1)S(1)}, bf16[64,2048]{1,0:T(8,128)(2,1)S(1)}, u32[]{:S(2)}, u32[]{:S(2)}) collective-permute-start(bf16[64,2048]{1,0:T(8,128)(2,1)S(1)} %add_convert_fusion.7), channel_id=1, source_target_pairs={{0,8},{1,9},{2,10},{3,11},{4,12},{5,13},{6,14},{7,15},{8,0},{9,1},... | collective-permute-start | bytes 786440 | tf_op jit(solution)/shard_map/ppermute | solution.py:256
  81.3 0.6 collective-permute-start.27
  82.0 0.1 add_convert_fusion.8
  82.1 1.6 %collective-permute-start.24 = (bf16[64,2048]{1,0:T(8,128)(2,1)S(1)}, bf16[64,2048]{1,0:T(8,128)(2,1)S(1)}, u32[]{:S(2)}, u32[]{:S(2)}) collective-permute-start(bf16[64,2048]{1,0:T(8,128)(2,1)S(1)} %get-tuple-element.161), channel_id=1, source_target_pairs={{0,2},{1,3},{2,0},{3,1},{4,6},{5,7},{6,4},{7,5},{8,10},{9,11},{10,... | collective-permute-start | bytes 786440 | tf_op jit(solution)/shard_map/ppermute | solution.py:256
  83.7 0.5 collective-permute-start.25
  84.2 0.1 add_convert_fusion
  84.3 10.5 %collective-permute-done.26.far_high = bf16[64,2048]{1,0:T(8,128)(2,1)S(1)} collective-permute-done((bf16[64,2048]{1,0:T(8,128)(2,1)S(1)}, bf16[64,2048]{1,0:T(8,128)(2,1)S(1)}, u32[]{:S(2)}, u32[]{:S(2)}) %collective-permute-start.26) | collective-permute-done | bytes 262176 | tf_op jit(solution)/shard_map/ppermute | solution.py:256
  94.9 1.1 collective-permute-done.25
  95.9 0.2 add_convert_fusion.4
  96.2 2.3 %collective-permute-start.30 = (bf16[64,2048]{1,0:T(8,128)(2,1)S(1)}, bf16[64,2048]{1,0:T(8,128)(2,1)S(1)}, u32[]{:S(2)}, u32[]{:S(2)}) collective-permute-start(bf16[64,2048]{1,0:T(8,128)(2,1)S(1)} %get-tuple-element.159), channel_id=1, source_target_pairs={{0,8},{1,9},{2,10},{3,11},{4,12},{5,13},{6,14},{7,15},{8,0},{9,1},... | collective-permute-start | bytes 786440 | tf_op jit(solution)/shard_map/ppermute | solution.py:256
  98.5 0.4 collective-permute-start.31
  98.9 1.5 %collective-permute-start.32 = (bf16[64,2048]{1,0:T(8,128)(2,1)S(1)}, bf16[64,2048]{1,0:T(8,128)(2,1)S(1)}, u32[]{:S(2)}, u32[]{:S(2)}) collective-permute-start(bf16[64,2048]{1,0:T(8,128)(2,1)S(1)} %add_convert_fusion.3), channel_id=1, source_target_pairs={{0,2},{1,3},{2,0},{3,1},{4,6},{5,7},{6,4},{7,5},{8,10},{9,11},{10,... | collective-permute-start | bytes 786440 | tf_op jit(solution)/shard_map/ppermute | solution.py:256
  100.5 0.6 collective-permute-start.33
  101.0 3.1 %shard_map.84 = f32[768,768]{1,0:T(8,128)} custom-call(f32[16,512]{1,0:T(8,128)S(1)} %shard_map.78.tables, bf16[320,768]{1,0:T(8,128)(2,1)S(1)} %get-tuple-element.139.refs_0_, bf16[320,768]{1,0:T(8,128)(2,1)S(1)} %get-tuple-element.140.refs_1_, bf16[320,768]{1,0:T(8,128)(2,1)S(1)} %get-tuple-element.141.refs_2_, ...), custom_call_target="tpu_custom_call" | custom-call | flops 1509949440 | bytes 4325376 | tf_op jit(solution)/shard_map/pallas_call | solution.py:209
  104.2 6.0 %collective-permute-done.30 = bf16[64,2048]{1,0:T(8,128)(2,1)S(1)} collective-permute-done((bf16[64,2048]{1,0:T(8,128)(2,1)S(1)}, bf16[64,2048]{1,0:T(8,128)(2,1)S(1)}, u32[]{:S(2)}, u32[]{:S(2)}) %collective-permute-start.30) | collective-permute-done | bytes 262176 | tf_op jit(solution)/shard_map/ppermute | solution.py:256
  110.2 1.2 collective-permute-done.33
  111.3 0.1 add_convert_fusion.2
  111.5 1.8 %collective-permute-start.34 = (bf16[64,2048]{1,0:T(8,128)(2,1)S(1)}, bf16[64,2048]{1,0:T(8,128)(2,1)S(1)}, u32[]{:S(2)}, u32[]{:S(2)}) collective-permute-start(bf16[64,2048]{1,0:T(8,128)(2,1)S(1)} %add_convert_fusion.2), channel_id=1, source_target_pairs={{0,8},{1,9},{2,10},{3,11},{4,12},{5,13},{6,14},{7,15},{8,0},{9,1},... | collective-permute-start | bytes 786440 | tf_op jit(solution)/shard_map/ppermute | solution.py:256
  113.2 1.4 %collective-permute-start.36 = (bf16[128,2048]{1,0:T(8,128)(2,1)S(1)}, bf16[128,2048]{1,0:T(8,128)(2,1)S(1)}, u32[]{:S(2)}, u32[]{:S(2)}) collective-permute-start(bf16[128,2048]{1,0:T(8,128)(2,1)S(1)} %add_convert_fusion), channel_id=1, source_target_pairs={{0,2},{1,3},{2,0},{3,1},{4,6},{5,7},{6,4},{7,5},{8,10},{9,11},{10,... | collective-permute-start | bytes 1572872 | tf_op jit(solution)/shard_map/ppermute | solution.py:256
  114.7 0.1 add_convert_fusion.1
  114.8 0.8 collective-permute-start.35
  115.6 8.7 %collective-permute-done.34.far_low = bf16[64,2048]{1,0:T(8,128)(2,1)S(1)} collective-permute-done((bf16[64,2048]{1,0:T(8,128)(2,1)S(1)}, bf16[64,2048]{1,0:T(8,128)(2,1)S(1)}, u32[]{:S(2)}, u32[]{:S(2)}) %collective-permute-start.34) | collective-permute-done | bytes 262176 | tf_op jit(solution)/shard_map/ppermute | solution.py:256
  124.3 0.6 collective-permute-done.35.near_high
  124.8 1.1 shard_map.85
  (47 shorter events, 0.3 us)
Async XLA Ops:
  0.6 24.1 %collective-permute-start = (bf16[128,2048]{1,0:T(8,128)(2,1)}, bf16[128,2048]{1,0:T(8,128)(2,1)S(1)}, u32[]{:S(2)}, u32[]{:S(2)}) collective-permute-start(bf16[128,2048]{1,0:T(8,128)(2,1)} %refs_0_.1), channel_id=1, source_target_pairs={{0,4},{1,5},{2,6},{3,7},{4,0},{5,1},{6,2},{7,3},{8,12},{9,13},{10,... | collective-permute-start | bytes 1572872 | tf_op jit(solution)/shard_map/ppermute | solution.py:256
  3.7 21.0 %collective-permute-start.2 = (bf16[128,2048]{1,0:T(8,128)(2,1)}, bf16[128,2048]{1,0:T(8,128)(2,1)S(1)}, u32[]{:S(2)}, u32[]{:S(2)}) collective-permute-start(bf16[128,2048]{1,0:T(8,128)(2,1)} %refs_0_.1), channel_id=1, source_target_pairs={{0,2},{1,3},{2,0},{3,1},{4,6},{5,7},{6,4},{7,5},{8,10},{9,11},{10,... | collective-permute-start | bytes 1572872 | tf_op jit(solution)/shard_map/ppermute | solution.py:256
  5.2 19.5 %collective-permute-start.3 = (bf16[128,2048]{1,0:T(8,128)(2,1)}, bf16[128,2048]{1,0:T(8,128)(2,1)S(1)}, u32[]{:S(2)}, u32[]{:S(2)}) collective-permute-start(bf16[128,2048]{1,0:T(8,128)(2,1)} %refs_0_.1), channel_id=1, source_target_pairs={{0,1},{1,0},{2,3},{3,2},{4,5},{5,4},{6,7},{7,6},{8,9},{9,8},{10,11... | collective-permute-start | bytes 1572872 | tf_op jit(solution)/shard_map/ppermute | solution.py:256
  7.1 17.6 %collective-permute-start.1 = (bf16[64,2048]{1,0:T(8,128)(2,1)}, bf16[64,2048]{1,0:T(8,128)(2,1)S(1)}, u32[]{:S(2)}, u32[]{:S(2)}) collective-permute-start(bf16[64,2048]{1,0:T(8,128)(2,1)} %get-tuple-element.79), channel_id=1, source_target_pairs={{0,8},{1,9},{2,10},{3,11},{4,12},{5,13},{6,14},{7,15},{8,0},{9,1},... | collective-permute-start | bytes 786440 | tf_op jit(solution)/shard_map/ppermute | solution.py:256
  24.7 2.4 %collective-permute-start.7 = (bf16[128,2048]{1,0:T(8,128)(2,1)S(1)}, bf16[128,2048]{1,0:T(8,128)(2,1)S(1)}, u32[]{:S(2)}, u32[]{:S(2)}) collective-permute-start(bf16[128,2048]{1,0:T(8,128)(2,1)S(1)} %collective-permute-done.2.refs_1_), channel_id=1, source_target_pairs={{0,1},{1,0},{2,3},{3,2},{4,5},{5,4},{6,7},{7,6},{8,9},{9,8},{10,11... | collective-permute-start | bytes 1572872 | tf_op jit(solution)/shard_map/ppermute | solution.py:256
  24.8 16.2 %collective-permute-start.5 = (bf16[128,2048]{1,0:T(8,128)(2,1)S(1)}, bf16[128,2048]{1,0:T(8,128)(2,1)S(1)}, u32[]{:S(2)}, u32[]{:S(2)}) collective-permute-start(bf16[128,2048]{1,0:T(8,128)(2,1)S(1)} %collective-permute-done.refs_0_), channel_id=1, source_target_pairs={{0,2},{1,3},{2,0},{3,1},{4,6},{5,7},{6,4},{7,5},{8,10},{9,11},{10,... | collective-permute-start | bytes 1572872 | tf_op jit(solution)/shard_map/ppermute | solution.py:256
  25.4 15.6 %collective-permute-start.6 = (bf16[128,2048]{1,0:T(8,128)(2,1)S(1)}, bf16[128,2048]{1,0:T(8,128)(2,1)S(1)}, u32[]{:S(2)}, u32[]{:S(2)}) collective-permute-start(bf16[128,2048]{1,0:T(8,128)(2,1)S(1)} %collective-permute-done.refs_0_), channel_id=1, source_target_pairs={{0,1},{1,0},{2,3},{3,2},{4,5},{5,4},{6,7},{7,6},{8,9},{9,8},{10,11... | collective-permute-start | bytes 1572872 | tf_op jit(solution)/shard_map/ppermute | solution.py:256
  25.6 15.3 %collective-permute-start.4 = (bf16[64,2048]{1,0:T(8,128)(2,1)}, bf16[64,2048]{1,0:T(8,128)(2,1)S(1)}, u32[]{:S(2)}, u32[]{:S(2)}) collective-permute-start(bf16[64,2048]{1,0:T(8,128)(2,1)} %get-tuple-element.83), channel_id=1, source_target_pairs={{0,8},{1,9},{2,10},{3,11},{4,12},{5,13},{6,14},{7,15},{8,0},{9,1},... | collective-permute-start | bytes 786440 | tf_op jit(solution)/shard_map/ppermute | solution.py:256
  27.1 1.9 %copy-start = (bf16[1,2048,768]{2,1,0:T(8,128)(2,1)S(1)}, bf16[1,2048,768]{2,1,0:T(8,128)(2,1)}, u32[]{:S(2)}) copy-start(bf16[1,2048,768]{2,1,0:T(8,128)(2,1)} %param.9) | copy-start | bytes 9437188
  29.0 1.9 %copy-start.2 = (bf16[1,2048,768]{2,1,0:T(8,128)(2,1)S(1)}, bf16[1,2048,768]{2,1,0:T(8,128)(2,1)}, u32[]{:S(2)}) copy-start(bf16[1,2048,768]{2,1,0:T(8,128)(2,1)} %param.10) | copy-start | bytes 9437188
  30.9 1.9 %copy-start.4 = (bf16[1,768,2048]{2,1,0:T(8,128)(2,1)S(1)}, bf16[1,768,2048]{2,1,0:T(8,128)(2,1)}, u32[]{:S(2)}) copy-start(bf16[1,768,2048]{2,1,0:T(8,128)(2,1)} %param.11) | copy-start | bytes 9437188
  32.8 1.0 copy-start.6
  33.8 9.1 %copy-start.1 = (bf16[1,2048,768]{2,1,0:T(8,128)(2,1)S(1)}, bf16[1,2048,768]{2,1,0:T(8,128)(2,1)}, u32[]{:S(2)}) copy-start(bf16[1,2048,768]{2,1,0:T(8,128)(2,1)} %param.9) | copy-start | bytes 9437188
  33.8 9.1 %copy-start.3 = (bf16[1,2048,768]{2,1,0:T(8,128)(2,1)S(1)}, bf16[1,2048,768]{2,1,0:T(8,128)(2,1)}, u32[]{:S(2)}) copy-start(bf16[1,2048,768]{2,1,0:T(8,128)(2,1)} %param.10) | copy-start | bytes 9437188
  33.8 9.1 %copy-start.5 = (bf16[1,768,2048]{2,1,0:T(8,128)(2,1)S(1)}, bf16[1,768,2048]{2,1,0:T(8,128)(2,1)}, u32[]{:S(2)}) copy-start(bf16[1,768,2048]{2,1,0:T(8,128)(2,1)} %param.11) | copy-start | bytes 9437188
  41.0 1.9 %collective-permute-start.11 = (bf16[128,2048]{1,0:T(8,128)(2,1)S(1)}, bf16[128,2048]{1,0:T(8,128)(2,1)S(1)}, u32[]{:S(2)}, u32[]{:S(2)}) collective-permute-start(bf16[128,2048]{1,0:T(8,128)(2,1)S(1)} %collective-permute-done.5.refs_1_), channel_id=1, source_target_pairs={{0,1},{1,0},{2,3},{3,2},{4,5},{5,4},{6,7},{7,6},{8,9},{9,8},{10,11... | collective-permute-start | bytes 1572872 | tf_op jit(solution)/shard_map/ppermute | solution.py:256
  41.1 14.4 %collective-permute-start.8 = (bf16[128,2048]{1,0:T(8,128)(2,1)S(1)}, bf16[128,2048]{1,0:T(8,128)(2,1)S(1)}, u32[]{:S(2)}, u32[]{:S(2)}) collective-permute-start(bf16[128,2048]{1,0:T(8,128)(2,1)S(1)} %constant_dynamic-update-slice_fusion.refs_0_), channel_id=1, source_target_pairs={{0,4},{1,5},{2,6},{3,7},{4,0},{5,1},{6,2},{7,3},{8,12},{9,13},{10,... | collective-permute-start | bytes 1572872 | tf_op jit(solution)/shard_map/ppermute | solution.py:256
  41.2 14.3 %collective-permute-start.9 = (bf16[128,2048]{1,0:T(8,128)(2,1)S(1)}, bf16[128,2048]{1,0:T(8,128)(2,1)S(1)}, u32[]{:S(2)}, u32[]{:S(2)}) collective-permute-start(bf16[128,2048]{1,0:T(8,128)(2,1)S(1)} %constant_dynamic-update-slice_fusion.refs_0_), channel_id=1, source_target_pairs={{0,2},{1,3},{2,0},{3,1},{4,6},{5,7},{6,4},{7,5},{8,10},{9,11},{10,... | collective-permute-start | bytes 1572872 | tf_op jit(solution)/shard_map/ppermute | solution.py:256
  42.7 12.8 %collective-permute-start.10 = (bf16[128,2048]{1,0:T(8,128)(2,1)S(1)}, bf16[128,2048]{1,0:T(8,128)(2,1)S(1)}, u32[]{:S(2)}, u32[]{:S(2)}) collective-permute-start(bf16[128,2048]{1,0:T(8,128)(2,1)S(1)} %constant_dynamic-update-slice_fusion.refs_0_), channel_id=1, source_target_pairs={{0,1},{1,0},{2,3},{3,2},{4,5},{5,4},{6,7},{7,6},{8,9},{9,8},{10,11... | collective-permute-start | bytes 1572872 | tf_op jit(solution)/shard_map/ppermute | solution.py:256
  48.4 7.1 %collective-permute-start.12 = (bf16[128,2048]{1,0:T(8,128)(2,1)S(1)}, bf16[128,2048]{1,0:T(8,128)(2,1)S(1)}, u32[]{:S(2)}, u32[]{:S(2)}) collective-permute-start(bf16[128,2048]{1,0:T(8,128)(2,1)S(1)} %get-tuple-element.98), channel_id=1, source_target_pairs={{0,1},{1,0},{2,3},{3,2},{4,5},{5,4},{6,7},{7,6},{8,9},{9,8},{10,11... | collective-permute-start | bytes 1572872 | tf_op jit(solution)/shard_map/ppermute | solution.py:256
  55.5 3.9 %collective-permute-start.17 = (bf16[128,2048]{1,0:T(8,128)(2,1)S(1)}, bf16[128,2048]{1,0:T(8,128)(2,1)S(1)}, u32[]{:S(2)}, u32[]{:S(2)}) collective-permute-start(bf16[128,2048]{1,0:T(8,128)(2,1)S(1)} %collective-permute-done.9.refs_1_), channel_id=1, source_target_pairs={{0,1},{1,0},{2,3},{3,2},{4,5},{5,4},{6,7},{7,6},{8,9},{9,8},{10,11... | collective-permute-start | bytes 1572872 | tf_op jit(solution)/shard_map/ppermute | solution.py:256
  55.6 12.8 %collective-permute-start.15 = (bf16[256,2048]{1,0:T(8,128)(2,1)S(1)}, bf16[256,2048]{1,0:T(8,128)(2,1)S(1)}, u32[]{:S(2)}, u32[]{:S(2)}) collective-permute-start(bf16[256,2048]{1,0:T(8,128)(2,1)S(1)} %get-tuple-element.102), channel_id=1, source_target_pairs={{0,1},{1,0},{2,3},{3,2},{4,5},{5,4},{6,7},{7,6},{8,9},{9,8},{10,11... | collective-permute-start | bytes 3145736 | tf_op jit(solution)/shard_map/ppermute | solution.py:256
  56.1 13.9 %collective-permute-start.13 = (bf16[128,2048]{1,0:T(8,128)(2,1)S(1)}, bf16[128,2048]{1,0:T(8,128)(2,1)S(1)}, u32[]{:S(2)}, u32[]{:S(2)}) collective-permute-start(bf16[128,2048]{1,0:T(8,128)(2,1)S(1)} %collective-permute-done.9.refs_1_), channel_id=1, source_target_pairs={{0,4},{1,5},{2,6},{3,7},{4,0},{5,1},{6,2},{7,3},{8,12},{9,13},{10,... | collective-permute-start | bytes 1572872 | tf_op jit(solution)/shard_map/ppermute | solution.py:256
  57.7 7.6 %collective-permute-start.19 = (bf16[128,2048]{1,0:T(8,128)(2,1)S(1)}, bf16[128,2048]{1,0:T(8,128)(2,1)S(1)}, u32[]{:S(2)}, u32[]{:S(2)}) collective-permute-start(bf16[128,2048]{1,0:T(8,128)(2,1)S(1)} %collective-permute-done.8.refs_0_), channel_id=1, source_target_pairs={{0,1},{1,0},{2,3},{3,2},{4,5},{5,4},{6,7},{7,6},{8,9},{9,8},{10,11... | collective-permute-start | bytes 1572872 | tf_op jit(solution)/shard_map/ppermute | solution.py:256
  57.9 10.5 %collective-permute-start.14 = (bf16[64,2048]{1,0:T(8,128)(2,1)S(1)}, bf16[64,2048]{1,0:T(8,128)(2,1)S(1)}, u32[]{:S(2)}, u32[]{:S(2)}) collective-permute-start(bf16[64,2048]{1,0:T(8,128)(2,1)S(1)} %get-tuple-element.157), channel_id=1, source_target_pairs={{0,2},{1,3},{2,0},{3,1},{4,6},{5,7},{6,4},{7,5},{8,10},{9,11},{10,... | collective-permute-start | bytes 786440 | tf_op jit(solution)/shard_map/ppermute | solution.py:256
  59.4 10.6 %collective-permute-start.16 = (bf16[128,2048]{1,0:T(8,128)(2,1)S(1)}, bf16[128,2048]{1,0:T(8,128)(2,1)S(1)}, u32[]{:S(2)}, u32[]{:S(2)}) collective-permute-start(bf16[128,2048]{1,0:T(8,128)(2,1)S(1)} %get-tuple-element.103), channel_id=1, source_target_pairs={{0,1},{1,0},{2,3},{3,2},{4,5},{5,4},{6,7},{7,6},{8,9},{9,8},{10,11... | collective-permute-start | bytes 1572872 | tf_op jit(solution)/shard_map/ppermute | solution.py:256
  65.3 4.7 %collective-permute-start.18 = (bf16[64,2048]{1,0:T(8,128)(2,1)S(1)}, bf16[64,2048]{1,0:T(8,128)(2,1)S(1)}, u32[]{:S(2)}, u32[]{:S(2)}) collective-permute-start(bf16[64,2048]{1,0:T(8,128)(2,1)S(1)} %get-tuple-element.105), channel_id=1, source_target_pairs={{0,1},{1,0},{2,3},{3,2},{4,5},{5,4},{6,7},{7,6},{8,9},{9,8},{10,11... | collective-permute-start | bytes 786440 | tf_op jit(solution)/shard_map/ppermute | solution.py:256
  70.0 2.2 %collective-permute-start.20 = (bf16[128,2048]{1,0:T(8,128)(2,1)S(1)}, bf16[128,2048]{1,0:T(8,128)(2,1)S(1)}, u32[]{:S(2)}, u32[]{:S(2)}) collective-permute-start(bf16[128,2048]{1,0:T(8,128)(2,1)S(1)} %collective-permute-done.13.refs_0_), channel_id=1, source_target_pairs={{0,1},{1,0},{2,3},{3,2},{4,5},{5,4},{6,7},{7,6},{8,9},{9,8},{10,11... | collective-permute-start | bytes 1572872 | tf_op jit(solution)/shard_map/ppermute | solution.py:256
  70.0 8.9 %collective-permute-start.21 = (bf16[128,2048]{1,0:T(8,128)(2,1)S(1)}, bf16[128,2048]{1,0:T(8,128)(2,1)S(1)}, u32[]{:S(2)}, u32[]{:S(2)}) collective-permute-start(bf16[128,2048]{1,0:T(8,128)(2,1)S(1)} %get-tuple-element.119), channel_id=1, source_target_pairs={{0,1},{1,0},{2,3},{3,2},{4,5},{5,4},{6,7},{7,6},{8,9},{9,8},{10,11... | collective-permute-start | bytes 1572872 | tf_op jit(solution)/shard_map/ppermute | solution.py:256
  70.6 8.3 %collective-permute-start.22 = (bf16[64,2048]{1,0:T(8,128)(2,1)S(1)}, bf16[64,2048]{1,0:T(8,128)(2,1)S(1)}, u32[]{:S(2)}, u32[]{:S(2)}) collective-permute-start(bf16[64,2048]{1,0:T(8,128)(2,1)S(1)} %add_convert_fusion.11), channel_id=1, source_target_pairs={{0,2},{1,3},{2,0},{3,1},{4,6},{5,7},{6,4},{7,5},{8,10},{9,11},{10,... | collective-permute-start | bytes 786440 | tf_op jit(solution)/shard_map/ppermute | solution.py:256
  78.9 3.0 %collective-permute-start.23 = (bf16[128,2048]{1,0:T(8,128)(2,1)S(1)}, bf16[128,2048]{1,0:T(8,128)(2,1)S(1)}, u32[]{:S(2)}, u32[]{:S(2)}) collective-permute-start(bf16[128,2048]{1,0:T(8,128)(2,1)S(1)} %get-tuple-element.125), channel_id=1, source_target_pairs={{0,1},{1,0},{2,3},{3,2},{4,5},{5,4},{6,7},{7,6},{8,9},{9,8},{10,11... | collective-permute-start | bytes 1572872 | tf_op jit(solution)/shard_map/ppermute | solution.py:256
  78.9 4.7 %collective-permute-start.28 = (bf16[64,2048]{1,0:T(8,128)(2,1)S(1)}, bf16[64,2048]{1,0:T(8,128)(2,1)S(1)}, u32[]{:S(2)}, u32[]{:S(2)}) collective-permute-start(bf16[64,2048]{1,0:T(8,128)(2,1)S(1)} %get-tuple-element.131), channel_id=1, source_target_pairs={{0,1},{1,0},{2,3},{3,2},{4,5},{5,4},{6,7},{7,6},{8,9},{9,8},{10,11... | collective-permute-start | bytes 786440 | tf_op jit(solution)/shard_map/ppermute | solution.py:256
  79.4 4.9 %collective-permute-start.29 = (bf16[128,2048]{1,0:T(8,128)(2,1)S(1)}, bf16[128,2048]{1,0:T(8,128)(2,1)S(1)}, u32[]{:S(2)}, u32[]{:S(2)}) collective-permute-start(bf16[128,2048]{1,0:T(8,128)(2,1)S(1)} %get-tuple-element.132), channel_id=1, source_target_pairs={{0,1},{1,0},{2,3},{3,2},{4,5},{5,4},{6,7},{7,6},{8,9},{9,8},{10,11... | collective-permute-start | bytes 1572872 | tf_op jit(solution)/shard_map/ppermute | solution.py:256
  79.6 15.3 %collective-permute-start.26 = (bf16[64,2048]{1,0:T(8,128)(2,1)S(1)}, bf16[64,2048]{1,0:T(8,128)(2,1)S(1)}, u32[]{:S(2)}, u32[]{:S(2)}) collective-permute-start(bf16[64,2048]{1,0:T(8,128)(2,1)S(1)} %add_convert_fusion.7), channel_id=1, source_target_pairs={{0,8},{1,9},{2,10},{3,11},{4,12},{5,13},{6,14},{7,15},{8,0},{9,1},... | collective-permute-start | bytes 786440 | tf_op jit(solution)/shard_map/ppermute | solution.py:256
  81.3 13.5 %collective-permute-start.27 = (bf16[64,2048]{1,0:T(8,128)(2,1)S(1)}, bf16[64,2048]{1,0:T(8,128)(2,1)S(1)}, u32[]{:S(2)}, u32[]{:S(2)}) collective-permute-start(bf16[64,2048]{1,0:T(8,128)(2,1)S(1)} %add_convert_fusion.10), channel_id=1, source_target_pairs={{0,4},{1,5},{2,6},{3,7},{4,0},{5,1},{6,2},{7,3},{8,12},{9,13},{10,... | collective-permute-start | bytes 786440 | tf_op jit(solution)/shard_map/ppermute | solution.py:256
  82.1 12.8 %collective-permute-start.24 = (bf16[64,2048]{1,0:T(8,128)(2,1)S(1)}, bf16[64,2048]{1,0:T(8,128)(2,1)S(1)}, u32[]{:S(2)}, u32[]{:S(2)}) collective-permute-start(bf16[64,2048]{1,0:T(8,128)(2,1)S(1)} %get-tuple-element.161), channel_id=1, source_target_pairs={{0,2},{1,3},{2,0},{3,1},{4,6},{5,7},{6,4},{7,5},{8,10},{9,11},{10,... | collective-permute-start | bytes 786440 | tf_op jit(solution)/shard_map/ppermute | solution.py:256
  83.7 12.3 %collective-permute-start.25 = (bf16[64,2048]{1,0:T(8,128)(2,1)S(1)}, bf16[64,2048]{1,0:T(8,128)(2,1)S(1)}, u32[]{:S(2)}, u32[]{:S(2)}) collective-permute-start(bf16[64,2048]{1,0:T(8,128)(2,1)S(1)} %get-tuple-element.160), channel_id=1, source_target_pairs={{0,2},{1,3},{2,0},{3,1},{4,6},{5,7},{6,4},{7,5},{8,10},{9,11},{10,... | collective-permute-start | bytes 786440 | tf_op jit(solution)/shard_map/ppermute | solution.py:256
  96.2 14.0 %collective-permute-start.30 = (bf16[64,2048]{1,0:T(8,128)(2,1)S(1)}, bf16[64,2048]{1,0:T(8,128)(2,1)S(1)}, u32[]{:S(2)}, u32[]{:S(2)}) collective-permute-start(bf16[64,2048]{1,0:T(8,128)(2,1)S(1)} %get-tuple-element.159), channel_id=1, source_target_pairs={{0,8},{1,9},{2,10},{3,11},{4,12},{5,13},{6,14},{7,15},{8,0},{9,1},... | collective-permute-start | bytes 786440 | tf_op jit(solution)/shard_map/ppermute | solution.py:256
  98.5 11.7 %collective-permute-start.31 = (bf16[64,2048]{1,0:T(8,128)(2,1)S(1)}, bf16[64,2048]{1,0:T(8,128)(2,1)S(1)}, u32[]{:S(2)}, u32[]{:S(2)}) collective-permute-start(bf16[64,2048]{1,0:T(8,128)(2,1)S(1)} %get-tuple-element.158), channel_id=1, source_target_pairs={{0,4},{1,5},{2,6},{3,7},{4,0},{5,1},{6,2},{7,3},{8,12},{9,13},{10,... | collective-permute-start | bytes 786440 | tf_op jit(solution)/shard_map/ppermute | solution.py:256
  98.9 11.3 %collective-permute-start.32 = (bf16[64,2048]{1,0:T(8,128)(2,1)S(1)}, bf16[64,2048]{1,0:T(8,128)(2,1)S(1)}, u32[]{:S(2)}, u32[]{:S(2)}) collective-permute-start(bf16[64,2048]{1,0:T(8,128)(2,1)S(1)} %add_convert_fusion.3), channel_id=1, source_target_pairs={{0,2},{1,3},{2,0},{3,1},{4,6},{5,7},{6,4},{7,5},{8,10},{9,11},{10,... | collective-permute-start | bytes 786440 | tf_op jit(solution)/shard_map/ppermute | solution.py:256
  100.5 10.9 %collective-permute-start.33 = (bf16[64,2048]{1,0:T(8,128)(2,1)S(1)}, bf16[64,2048]{1,0:T(8,128)(2,1)S(1)}, u32[]{:S(2)}, u32[]{:S(2)}) collective-permute-start(bf16[64,2048]{1,0:T(8,128)(2,1)S(1)} %get-tuple-element.137), channel_id=1, source_target_pairs={{0,2},{1,3},{2,0},{3,1},{4,6},{5,7},{6,4},{7,5},{8,10},{9,11},{10,... | collective-permute-start | bytes 786440 | tf_op jit(solution)/shard_map/ppermute | solution.py:256
  111.5 12.8 %collective-permute-start.34 = (bf16[64,2048]{1,0:T(8,128)(2,1)S(1)}, bf16[64,2048]{1,0:T(8,128)(2,1)S(1)}, u32[]{:S(2)}, u32[]{:S(2)}) collective-permute-start(bf16[64,2048]{1,0:T(8,128)(2,1)S(1)} %add_convert_fusion.2), channel_id=1, source_target_pairs={{0,8},{1,9},{2,10},{3,11},{4,12},{5,13},{6,14},{7,15},{8,0},{9,1},... | collective-permute-start | bytes 786440 | tf_op jit(solution)/shard_map/ppermute | solution.py:256
  113.2 11.6 %collective-permute-start.36 = (bf16[128,2048]{1,0:T(8,128)(2,1)S(1)}, bf16[128,2048]{1,0:T(8,128)(2,1)S(1)}, u32[]{:S(2)}, u32[]{:S(2)}) collective-permute-start(bf16[128,2048]{1,0:T(8,128)(2,1)S(1)} %add_convert_fusion), channel_id=1, source_target_pairs={{0,2},{1,3},{2,0},{3,1},{4,6},{5,7},{6,4},{7,5},{8,10},{9,11},{10,... | collective-permute-start | bytes 1572872 | tf_op jit(solution)/shard_map/ppermute | solution.py:256
  114.8 10.0 %collective-permute-start.35 = (bf16[64,2048]{1,0:T(8,128)(2,1)S(1)}, bf16[64,2048]{1,0:T(8,128)(2,1)S(1)}, u32[]{:S(2)}, u32[]{:S(2)}) collective-permute-start(bf16[64,2048]{1,0:T(8,128)(2,1)S(1)} %add_convert_fusion.1), channel_id=1, source_target_pairs={{0,4},{1,5},{2,6},{3,7},{4,0},{5,1},{6,2},{7,3},{8,12},{9,13},{10,... | collective-permute-start | bytes 786440 | tf_op jit(solution)/shard_map/ppermute | solution.py:256

commit v29 on v28

--- a/solution.py
+++ b/solution.py
@@ -314,10 +314,9 @@
     )
     got2_high = sibling(give2_high)
     keep3, give3, act3 = expert(3, a3, c3, picked=(0, 2))
-    got0 = sibling(give0)
-    b3, came1_low, got0, got1, got2_high, keep2, give2, give2_low, act2, keep3, give3, act3 = (
+    b3, came1_low, got1, got2_high, keep2, give2, give2_low, act2, keep3, give3, act3 = (
         together(
-            b3, came1_low, got0, got1, got2_high, keep2, give2, give2_low, act2, keep3, give3, act3
+            b3, came1_low, got1, got2_high, keep2, give2, give2_low, act2, keep3, give3, act3
         )
     )
     d3 = sibling(b3)
@@ -335,15 +334,16 @@
     came3_low = column(summed(keep3_side[:half], got3_side[:half]))
     came3_high = column(summed(keep3_side[half:], got3_side[half:]))
     near1_low = pair(near1)
-    side0 = summed(keep0[tok:], got0[tok:])
+    got0 = sibling(give0)
     side1 = summed(keep1[tok + half :], got1_side[half:])
-    came3_low, came3_high, far2_high, near1_low, side0, side1, got2_low, got3 = together(
-        came3_low, came3_high, far2_high, near1_low, side0, side1, got2_low, got3
+    came3_low, came3_high, far2_high, near1_low, got0, side1, got2_low, got3 = together(
+        came3_low, came3_high, far2_high, near1_low, got0, side1, got2_low, got3
     )
     far3_high = far(summed(keep3[half:], got3[half:], came3_high))
     pair3_low = pair(summed(keep3[:half], got3[:half], came3_low))
     side_low = column(summed(keep2[tok : tok + half], got2_low))
     came1_high = column(side1)
+    side0 = summed(keep0[tok:], got0[tok:])
     gram = gram_pass(tables, act0, act1, act2, act3, act4)
     far3_high, pair3_low, side_low, came1_high, side0, gram = together(
         far3_high, pair3_low, side_low, came1_high, side0, gram

time: 126 us -> 127 us (level)
  no operation moved by 1% of the time
where the time goes in v29:
time: 127 us
  waiting for transfers between devices  42.7 us (34%)
  starting transfers between devices  31.2 us (25%)
  Pallas kernels  28.8 us (23%)
  blocking collectives  14.9 us (12%)
  local copies, waits for them, and re-layouts  6.84 us (5%)
    ppermute x37, waiting for transfers between devices, swapped(): return lax.ppermute(array, 'expert', [(i, i ^ bit) for i in range(size)])  42.7 us
    ppermute x37, starting transfers between devices, swapped(): return lax.ppermute(array, 'expert', [(i, i ^ bit) for i in range(size)])  31.2 us
    pallas_call x5, Pallas kernels, plane_pass(): pl.pallas_call(functools.partial(plane_kernel, k, picked, len(pieces)), o...  21.9 us
    all_to_all x1, blocking collectives, staged(): lax.all_to_all(mine, 'expert', split_axis=0, concat_axis=0, tiled=True)  14.9 us
    unnamed x15, local copies, waits for them, and re-layouts  6.73 us
    pallas_call x1, Pallas kernels, gram_pass(): pl.pallas_call(gram_kernel, out_shape=jax.ShapeDtypeStruct((hidden, hidde...  3.14 us
  transfers between devices with their start and end apart: 37, of which 11 were waited for; matrix products, arithmetic and copies ran while one was open for 1% of the time, Pallas kernels for 22%

profile of v29, /device:TPU:0, one launch (start us, length us, event | category | flops | bytes accessed | tf_op | source)
XLA Modules:
  0.0 126.6 jit_solution(9259004445028090454)
XLA Ops:
  0.6 3.1 %collective-permute-start = (bf16[128,2048]{1,0:T(8,128)(2,1)}, bf16[128,2048]{1,0:T(8,128)(2,1)S(1)}, u32[]{:S(2)}, u32[]{:S(2)}) collective-permute-start(bf16[128,2048]{1,0:T(8,128)(2,1)} %refs_0_.1), channel_id=1, source_target_pairs={{0,4},{1,5},{2,6},{3,7},{4,0},{5,1},{6,2},{7,3},{8,12},{9,13},{10,... | collective-permute-start | bytes 1572872 | tf_op jit(solution)/shard_map/ppermute | solution.py:256
  3.7 1.5 %collective-permute-start.2 = (bf16[128,2048]{1,0:T(8,128)(2,1)}, bf16[128,2048]{1,0:T(8,128)(2,1)S(1)}, u32[]{:S(2)}, u32[]{:S(2)}) collective-permute-start(bf16[128,2048]{1,0:T(8,128)(2,1)} %refs_0_.1), channel_id=1, source_target_pairs={{0,2},{1,3},{2,0},{3,1},{4,6},{5,7},{6,4},{7,5},{8,10},{9,11},{10,... | collective-permute-start | bytes 1572872 | tf_op jit(solution)/shard_map/ppermute | solution.py:256
  5.2 1.9 %shard_map.77 = (f32[16,128]{1,0:T(8,128)}, bf16[64,2048]{1,0:T(8,128)(2,1)}, bf16[64,2048]{1,0:T(8,128)(2,1)}) custom-call(s32[8,128]{1,0:T(8,128)} %bitcast.43, f32[8,128]{1,0:T(8,128)} %bitcast.44, bf16[128,2048]{1,0:T(8,128)(2,1)} %refs_0_.1), custom_call_target="tpu_custom_call" | custom-call | tf_op jit(solution)/shard_map/pallas_call | solution.py:57
  7.1 2.7 %collective-permute-start.1 = (bf16[64,2048]{1,0:T(8,128)(2,1)}, bf16[64,2048]{1,0:T(8,128)(2,1)S(1)}, u32[]{:S(2)}, u32[]{:S(2)}) collective-permute-start(bf16[64,2048]{1,0:T(8,128)(2,1)} %get-tuple-element.78), channel_id=1, source_target_pairs={{0,8},{1,9},{2,10},{3,11},{4,12},{5,13},{6,14},{7,15},{8,0},{9,1},... | collective-permute-start | bytes 786440 | tf_op jit(solution)/shard_map/ppermute | solution.py:256
  9.8 14.9 %all_to_all.12 = f32[16,1,128]{2,1,0:T(1,128)S(1)} all-to-all(f32[16,1,128]{2,1,0:T(1,128)} %bitcast.42), channel_id=1, replica_groups=mesh['parts'=2,'expert'=16] {'expert'}, dimensions={0} | all-to-all | bytes 16384 | tf_op jit(solution)/shard_map/all_to_all | solution.py:285
  24.8 0.6 collective-permute-start.5
  25.4 0.2 collective-permute-start.6
  25.6 0.1 stack.67.spots
  25.6 0.7 collective-permute-start.4
  26.3 0.7 shard_map.78.tables
  27.1 1.9 %copy-done = bf16[1,2048,768]{2,1,0:T(8,128)(2,1)S(1)} copy-done((bf16[1,2048,768]{2,1,0:T(8,128)(2,1)S(1)}, bf16[1,2048,768]{2,1,0:T(8,128)(2,1)}, u32[]{:S(2)}) %copy-start) | copy-done | bytes 3145752
  29.0 1.9 %copy-done.2 = bf16[1,2048,768]{2,1,0:T(8,128)(2,1)S(1)} copy-done((bf16[1,2048,768]{2,1,0:T(8,128)(2,1)S(1)}, bf16[1,2048,768]{2,1,0:T(8,128)(2,1)}, u32[]{:S(2)}) %copy-start.2) | copy-done | bytes 3145752
  30.9 1.9 %copy-done.4 = bf16[1,768,2048]{2,1,0:T(8,128)(2,1)S(1)} copy-done((bf16[1,768,2048]{2,1,0:T(8,128)(2,1)S(1)}, bf16[1,768,2048]{2,1,0:T(8,128)(2,1)}, u32[]{:S(2)}) %copy-start.4) | copy-done | bytes 3145752
  32.8 1.0 copy-done.6
  33.8 5.5 %shard_map.79 = (bf16[256,2048]{1,0:T(8,128)(2,1)S(1)}, bf16[256,2048]{1,0:T(8,128)(2,1)S(1)}, bf16[320,768]{1,0:T(8,128)(2,1)S(1)}) custom-call(f32[16,512]{1,0:T(8,128)S(1)} %shard_map.78.tables, bf16[128,2048]{1,0:T(8,128)(2,1)S(1)} %copy-done.6, bf16[128,2048]{1,0:T(8,128)(2,1)S(1)} %collective-permute-done.2.refs_1_, ...), custom_call_target="tpu_custom_call" | custom-call | flops 4362076160 | bytes 13631488 | tf_op jit(solution)/shard_map/pallas_call | solution.py:178
  39.3 1.7 %collective-permute-done.4 = bf16[64,2048]{1,0:T(8,128)(2,1)S(1)} collective-permute-done((bf16[64,2048]{1,0:T(8,128)(2,1)}, bf16[64,2048]{1,0:T(8,128)(2,1)S(1)}, u32[]{:S(2)}, u32[]{:S(2)}) %collective-permute-start.4) | collective-permute-done | bytes 262176 | tf_op jit(solution)/shard_map/ppermute | solution.py:256
  41.1 0.2 collective-permute-start.8
  41.2 1.5 %collective-permute-start.9 = (bf16[128,2048]{1,0:T(8,128)(2,1)S(1)}, bf16[128,2048]{1,0:T(8,128)(2,1)S(1)}, u32[]{:S(2)}, u32[]{:S(2)}) collective-permute-start(bf16[128,2048]{1,0:T(8,128)(2,1)S(1)} %constant_dynamic-update-slice_fusion.refs_0_), channel_id=1, source_target_pairs={{0,2},{1,3},{2,0},{3,1},{4,6},{5,7},{6,4},{7,5},{8,10},{9,11},{10,... | collective-permute-start | bytes 1572872 | tf_op jit(solution)/shard_map/ppermute | solution.py:256
  42.7 0.2 collective-permute-start.10
  42.9 5.5 %shard_map.80 = (bf16[256,2048]{1,0:T(8,128)(2,1)S(1)}, bf16[128,2048]{1,0:T(8,128)(2,1)S(1)}, bf16[128,2048]{1,0:T(8,128)(2,1)S(1)}, bf16[320,768]{1,0:T(8,128)(2,1)S(1)}) custom-call(f32[16,512]{1,0:T(8,128)S(1)} %shard_map.78.tables, bf16[128,2048]{1,0:T(8,128)(2,1)S(1)} %collective-permute-done.refs_0_, ...), custom_call_target="tpu_custom_call" | custom-call | flops 4362076160 | bytes 13631488 | tf_op jit(solution)/shard_map/pallas_call | solution.py:178
  48.4 0.4 collective-permute-start.12
  48.8 6.7 %collective-permute-done.8.refs_0_ = bf16[128,2048]{1,0:T(8,128)(2,1)S(1)} collective-permute-done((bf16[128,2048]{1,0:T(8,128)(2,1)S(1)}, bf16[128,2048]{1,0:T(8,128)(2,1)S(1)}, u32[]{:S(2)}, u32[]{:S(2)}) %collective-permute-start.8) | collective-permute-done | bytes 524320 | tf_op jit(solution)/shard_map/ppermute | solution.py:256
  55.5 0.1 collective-permute-done.9.refs_1_
  55.6 1.7 %collective-permute-start.13 = (bf16[128,2048]{1,0:T(8,128)(2,1)S(1)}, bf16[128,2048]{1,0:T(8,128)(2,1)S(1)}, u32[]{:S(2)}, u32[]{:S(2)}) collective-permute-start(bf16[128,2048]{1,0:T(8,128)(2,1)S(1)} %collective-permute-done.9.refs_1_), channel_id=1, source_target_pairs={{0,4},{1,5},{2,6},{3,7},{4,0},{5,1},{6,2},{7,3},{8,12},{9,13},{10,... | collective-permute-start | bytes 1572872 | tf_op jit(solution)/shard_map/ppermute | solution.py:256
  57.3 0.2 collective-permute-start.18
  57.4 0.1 add_convert_fusion.6
  57.6 1.5 %collective-permute-start.14 = (bf16[64,2048]{1,0:T(8,128)(2,1)S(1)}, bf16[64,2048]{1,0:T(8,128)(2,1)S(1)}, u32[]{:S(2)}, u32[]{:S(2)}) collective-permute-start(bf16[64,2048]{1,0:T(8,128)(2,1)S(1)} %get-tuple-element.155), channel_id=1, source_target_pairs={{0,2},{1,3},{2,0},{3,1},{4,6},{5,7},{6,4},{7,5},{8,10},{9,11},{10,... | collective-permute-start | bytes 786440 | tf_op jit(solution)/shard_map/ppermute | solution.py:256
  59.1 0.1 collective-permute-start.15
  59.2 5.6 %shard_map.81 = (bf16[256,2048]{1,0:T(8,128)(2,1)S(1)}, bf16[128,2048]{1,0:T(8,128)(2,1)S(1)}, bf16[64,2048]{1,0:T(8,128)(2,1)S(1)}, bf16[64,2048]{1,0:T(8,128)(2,1)S(1)}, bf16[320,768]{1,0:T(8,128)(2,1)S(1)}) custom-call(f32[16,512]{1,0:T(8,128)S(1)} %shard_map.78.tables, bf16[128,2048]{1,0:T(8,128)(2,1)S(1)} %constant_dynamic-update-slice_fusion.refs_0_, ...), custom_call_target="tpu_custom_call" | custom-call | flops 4362076160 | bytes 13631488 | tf_op jit(solution)/shard_map/pallas_call | solution.py:178
  64.8 0.5 collective-permute-start.17
  65.3 0.1 collective-permute-start.27
  65.4 2.7 %shard_map.82 = (bf16[128,2048]{1,0:T(8,128)(2,1)S(1)}, bf16[128,2048]{1,0:T(8,128)(2,1)S(1)}, bf16[160,768]{1,0:T(8,128)(2,1)S(1)}) custom-call(f32[16,512]{1,0:T(8,128)S(1)} %shard_map.78.tables, bf16[128,2048]{1,0:T(8,128)(2,1)S(1)} %collective-permute-done.8.refs_0_, bf16[128,2048]{1,0:T(8,128)(2,1)S(1)} %collective-permute-done.18.refs_1_, ...), custom_call_target="tpu_custom_call" | custom-call | flops 1845493760 | bytes 11534336 | tf_op jit(solution)/shard_map/pallas_call | solution.py:178
  68.1 1.8 %collective-permute-done.13.refs_0_ = bf16[128,2048]{1,0:T(8,128)(2,1)S(1)} collective-permute-done((bf16[128,2048]{1,0:T(8,128)(2,1)S(1)}, bf16[128,2048]{1,0:T(8,128)(2,1)S(1)}, u32[]{:S(2)}, u32[]{:S(2)}) %collective-permute-start.13) | collective-permute-done | bytes 524320 | tf_op jit(solution)/shard_map/ppermute | solution.py:256
  69.9 0.5 collective-permute-start.20
  70.5 1.5 %collective-permute-start.21 = (bf16[64,2048]{1,0:T(8,128)(2,1)S(1)}, bf16[64,2048]{1,0:T(8,128)(2,1)S(1)}, u32[]{:S(2)}, u32[]{:S(2)}) collective-permute-start(bf16[64,2048]{1,0:T(8,128)(2,1)S(1)} %add_convert_fusion.11), channel_id=1, source_target_pairs={{0,2},{1,3},{2,0},{3,1},{4,6},{5,7},{6,4},{7,5},{8,10},{9,11},{10,... | collective-permute-start | bytes 786440 | tf_op jit(solution)/shard_map/ppermute | solution.py:256
  72.0 0.1 add_convert_fusion.10
  72.2 2.7 %shard_map.83 = (bf16[128,2048]{1,0:T(8,128)(2,1)S(1)}, bf16[128,2048]{1,0:T(8,128)(2,1)S(1)}, bf16[160,768]{1,0:T(8,128)(2,1)S(1)}) custom-call(f32[16,512]{1,0:T(8,128)S(1)} %shard_map.78.tables, bf16[128,2048]{1,0:T(8,128)(2,1)S(1)} %collective-permute-done.13.refs_0_, bf16[128,2048]{1,0:T(8,128)(2,1)S(1)} %collective-permute-done.19.refs_1_, ...), custom_call_target="tpu_custom_call" | custom-call | flops 1845493760 | bytes 11534336 | tf_op jit(solution)/shard_map/pallas_call | solution.py:178
  74.9 4.0 %collective-permute-done.21 = bf16[64,2048]{1,0:T(8,128)(2,1)S(1)} collective-permute-done((bf16[64,2048]{1,0:T(8,128)(2,1)S(1)}, bf16[64,2048]{1,0:T(8,128)(2,1)S(1)}, u32[]{:S(2)}, u32[]{:S(2)}) %collective-permute-start.21) | collective-permute-done | bytes 262176 | tf_op jit(solution)/shard_map/ppermute | solution.py:256
  78.9 0.5 collective-permute-start.28
  79.4 0.1 add_convert_fusion.7
  79.5 1.8 %collective-permute-start.25 = (bf16[64,2048]{1,0:T(8,128)(2,1)S(1)}, bf16[64,2048]{1,0:T(8,128)(2,1)S(1)}, u32[]{:S(2)}, u32[]{:S(2)}) collective-permute-start(bf16[64,2048]{1,0:T(8,128)(2,1)S(1)} %add_convert_fusion.7), channel_id=1, source_target_pairs={{0,8},{1,9},{2,10},{3,11},{4,12},{5,13},{6,14},{7,15},{8,0},{9,1},... | collective-permute-start | bytes 786440 | tf_op jit(solution)/shard_map/ppermute | solution.py:256
  81.2 1.2 collective-permute-start.26
  82.4 0.1 add_convert_fusion.8
  82.6 1.5 %collective-permute-start.23 = (bf16[64,2048]{1,0:T(8,128)(2,1)S(1)}, bf16[64,2048]{1,0:T(8,128)(2,1)S(1)}, u32[]{:S(2)}, u32[]{:S(2)}) collective-permute-start(bf16[64,2048]{1,0:T(8,128)(2,1)S(1)} %get-tuple-element.159), channel_id=1, source_target_pairs={{0,2},{1,3},{2,0},{3,1},{4,6},{5,7},{6,4},{7,5},{8,10},{9,11},{10,... | collective-permute-start | bytes 786440 | tf_op jit(solution)/shard_map/ppermute | solution.py:256
  84.1 0.6 collective-permute-start.24
  84.6 3.1 %shard_map.84 = f32[768,768]{1,0:T(8,128)} custom-call(f32[16,512]{1,0:T(8,128)S(1)} %shard_map.78.tables, bf16[320,768]{1,0:T(8,128)(2,1)S(1)} %get-tuple-element.137.refs_0_, bf16[320,768]{1,0:T(8,128)(2,1)S(1)} %get-tuple-element.138.refs_1_, bf16[320,768]{1,0:T(8,128)(2,1)S(1)} %get-tuple-element.139.refs_2_, ...), custom_call_target="tpu_custom_call" | custom-call | flops 1509949440 | bytes 4325376 | tf_op jit(solution)/shard_map/pallas_call | solution.py:209
  87.8 7.0 %collective-permute-done.25.far_high = bf16[64,2048]{1,0:T(8,128)(2,1)S(1)} collective-permute-done((bf16[64,2048]{1,0:T(8,128)(2,1)S(1)}, bf16[64,2048]{1,0:T(8,128)(2,1)S(1)}, u32[]{:S(2)}, u32[]{:S(2)}) %collective-permute-start.25) | collective-permute-done | bytes 262176 | tf_op jit(solution)/shard_map/ppermute | solution.py:256
  94.8 1.5 %collective-permute-done.24 = bf16[64,2048]{1,0:T(8,128)(2,1)S(1)} collective-permute-done((bf16[64,2048]{1,0:T(8,128)(2,1)S(1)}, bf16[64,2048]{1,0:T(8,128)(2,1)S(1)}, u32[]{:S(2)}, u32[]{:S(2)}) %collective-permute-start.24) | collective-permute-done | bytes 262176 | tf_op jit(solution)/shard_map/ppermute | solution.py:256
  96.3 0.2 add_convert_fusion.4
  96.5 1.9 %collective-permute-start.30 = (bf16[64,2048]{1,0:T(8,128)(2,1)S(1)}, bf16[64,2048]{1,0:T(8,128)(2,1)S(1)}, u32[]{:S(2)}, u32[]{:S(2)}) collective-permute-start(bf16[64,2048]{1,0:T(8,128)(2,1)S(1)} %get-tuple-element.157), channel_id=1, source_target_pairs={{0,8},{1,9},{2,10},{3,11},{4,12},{5,13},{6,14},{7,15},{8,0},{9,1},... | collective-permute-start | bytes 786440 | tf_op jit(solution)/shard_map/ppermute | solution.py:256
  98.4 0.4 collective-permute-start.31
  98.9 1.5 %collective-permute-start.32 = (bf16[64,2048]{1,0:T(8,128)(2,1)S(1)}, bf16[64,2048]{1,0:T(8,128)(2,1)S(1)}, u32[]{:S(2)}, u32[]{:S(2)}) collective-permute-start(bf16[64,2048]{1,0:T(8,128)(2,1)S(1)} %add_convert_fusion.3), channel_id=1, source_target_pairs={{0,2},{1,3},{2,0},{3,1},{4,6},{5,7},{6,4},{7,5},{8,10},{9,11},{10,... | collective-permute-start | bytes 786440 | tf_op jit(solution)/shard_map/ppermute | solution.py:256
  100.4 0.6 collective-permute-start.33
  101.0 0.1 add_convert_fusion
  101.1 9.3 %collective-permute-done.30 = bf16[64,2048]{1,0:T(8,128)(2,1)S(1)} collective-permute-done((bf16[64,2048]{1,0:T(8,128)(2,1)S(1)}, bf16[64,2048]{1,0:T(8,128)(2,1)S(1)}, u32[]{:S(2)}, u32[]{:S(2)}) %collective-permute-start.30) | collective-permute-done | bytes 262176 | tf_op jit(solution)/shard_map/ppermute | solution.py:256
  110.5 0.8 collective-permute-done.33
  111.3 0.1 add_convert_fusion.2
  111.4 1.8 %collective-permute-start.34 = (bf16[64,2048]{1,0:T(8,128)(2,1)S(1)}, bf16[64,2048]{1,0:T(8,128)(2,1)S(1)}, u32[]{:S(2)}, u32[]{:S(2)}) collective-permute-start(bf16[64,2048]{1,0:T(8,128)(2,1)S(1)} %add_convert_fusion.2), channel_id=1, source_target_pairs={{0,8},{1,9},{2,10},{3,11},{4,12},{5,13},{6,14},{7,15},{8,0},{9,1},... | collective-permute-start | bytes 786440 | tf_op jit(solution)/shard_map/ppermute | solution.py:256
  113.2 1.4 %collective-permute-start.36 = (bf16[128,2048]{1,0:T(8,128)(2,1)S(1)}, bf16[128,2048]{1,0:T(8,128)(2,1)S(1)}, u32[]{:S(2)}, u32[]{:S(2)}) collective-permute-start(bf16[128,2048]{1,0:T(8,128)(2,1)S(1)} %add_convert_fusion), channel_id=1, source_target_pairs={{0,2},{1,3},{2,0},{3,1},{4,6},{5,7},{6,4},{7,5},{8,10},{9,11},{10,... | collective-permute-start | bytes 1572872 | tf_op jit(solution)/shard_map/ppermute | solution.py:256
  114.6 0.1 add_convert_fusion.1
  114.7 1.1 collective-permute-start.35
  115.8 9.1 %collective-permute-done.34.far_low = bf16[64,2048]{1,0:T(8,128)(2,1)S(1)} collective-permute-done((bf16[64,2048]{1,0:T(8,128)(2,1)S(1)}, bf16[64,2048]{1,0:T(8,128)(2,1)S(1)}, u32[]{:S(2)}, u32[]{:S(2)}) %collective-permute-start.34) | collective-permute-done | bytes 262176 | tf_op jit(solution)/shard_map/ppermute | solution.py:256
  124.9 0.6 collective-permute-done.35.near_high
  125.5 1.1 shard_map.85
  (47 shorter events, 0.4 us)
Async XLA Ops:
  0.6 24.1 %collective-permute-start = (bf16[128,2048]{1,0:T(8,128)(2,1)}, bf16[128,2048]{1,0:T(8,128)(2,1)S(1)}, u32[]{:S(2)}, u32[]{:S(2)}) collective-permute-start(bf16[128,2048]{1,0:T(8,128)(2,1)} %refs_0_.1), channel_id=1, source_target_pairs={{0,4},{1,5},{2,6},{3,7},{4,0},{5,1},{6,2},{7,3},{8,12},{9,13},{10,... | collective-permute-start | bytes 1572872 | tf_op jit(solution)/shard_map/ppermute | solution.py:256
  3.7 21.0 %collective-permute-start.2 = (bf16[128,2048]{1,0:T(8,128)(2,1)}, bf16[128,2048]{1,0:T(8,128)(2,1)S(1)}, u32[]{:S(2)}, u32[]{:S(2)}) collective-permute-start(bf16[128,2048]{1,0:T(8,128)(2,1)} %refs_0_.1), channel_id=1, source_target_pairs={{0,2},{1,3},{2,0},{3,1},{4,6},{5,7},{6,4},{7,5},{8,10},{9,11},{10,... | collective-permute-start | bytes 1572872 | tf_op jit(solution)/shard_map/ppermute | solution.py:256
  5.2 19.5 %collective-permute-start.3 = (bf16[128,2048]{1,0:T(8,128)(2,1)}, bf16[128,2048]{1,0:T(8,128)(2,1)S(1)}, u32[]{:S(2)}, u32[]{:S(2)}) collective-permute-start(bf16[128,2048]{1,0:T(8,128)(2,1)} %refs_0_.1), channel_id=1, source_target_pairs={{0,1},{1,0},{2,3},{3,2},{4,5},{5,4},{6,7},{7,6},{8,9},{9,8},{10,11... | collective-permute-start | bytes 1572872 | tf_op jit(solution)/shard_map/ppermute | solution.py:256
  7.1 17.6 %collective-permute-start.1 = (bf16[64,2048]{1,0:T(8,128)(2,1)}, bf16[64,2048]{1,0:T(8,128)(2,1)S(1)}, u32[]{:S(2)}, u32[]{:S(2)}) collective-permute-start(bf16[64,2048]{1,0:T(8,128)(2,1)} %get-tuple-element.78), channel_id=1, source_target_pairs={{0,8},{1,9},{2,10},{3,11},{4,12},{5,13},{6,14},{7,15},{8,0},{9,1},... | collective-permute-start | bytes 786440 | tf_op jit(solution)/shard_map/ppermute | solution.py:256
  24.7 2.4 %collective-permute-start.7 = (bf16[128,2048]{1,0:T(8,128)(2,1)S(1)}, bf16[128,2048]{1,0:T(8,128)(2,1)S(1)}, u32[]{:S(2)}, u32[]{:S(2)}) collective-permute-start(bf16[128,2048]{1,0:T(8,128)(2,1)S(1)} %collective-permute-done.2.refs_1_), channel_id=1, source_target_pairs={{0,1},{1,0},{2,3},{3,2},{4,5},{5,4},{6,7},{7,6},{8,9},{9,8},{10,11... | collective-permute-start | bytes 1572872 | tf_op jit(solution)/shard_map/ppermute | solution.py:256
  24.8 16.2 %collective-permute-start.5 = (bf16[128,2048]{1,0:T(8,128)(2,1)S(1)}, bf16[128,2048]{1,0:T(8,128)(2,1)S(1)}, u32[]{:S(2)}, u32[]{:S(2)}) collective-permute-start(bf16[128,2048]{1,0:T(8,128)(2,1)S(1)} %collective-permute-done.refs_0_), channel_id=1, source_target_pairs={{0,2},{1,3},{2,0},{3,1},{4,6},{5,7},{6,4},{7,5},{8,10},{9,11},{10,... | collective-permute-start | bytes 1572872 | tf_op jit(solution)/shard_map/ppermute | solution.py:256
  25.4 15.6 %collective-permute-start.6 = (bf16[128,2048]{1,0:T(8,128)(2,1)S(1)}, bf16[128,2048]{1,0:T(8,128)(2,1)S(1)}, u32[]{:S(2)}, u32[]{:S(2)}) collective-permute-start(bf16[128,2048]{1,0:T(8,128)(2,1)S(1)} %collective-permute-done.refs_0_), channel_id=1, source_target_pairs={{0,1},{1,0},{2,3},{3,2},{4,5},{5,4},{6,7},{7,6},{8,9},{9,8},{10,11... | collective-permute-start | bytes 1572872 | tf_op jit(solution)/shard_map/ppermute | solution.py:256
  25.6 15.3 %collective-permute-start.4 = (bf16[64,2048]{1,0:T(8,128)(2,1)}, bf16[64,2048]{1,0:T(8,128)(2,1)S(1)}, u32[]{:S(2)}, u32[]{:S(2)}) collective-permute-start(bf16[64,2048]{1,0:T(8,128)(2,1)} %get-tuple-element.82), channel_id=1, source_target_pairs={{0,8},{1,9},{2,10},{3,11},{4,12},{5,13},{6,14},{7,15},{8,0},{9,1},... | collective-permute-start | bytes 786440 | tf_op jit(solution)/shard_map/ppermute | solution.py:256
  27.1 1.9 %copy-start = (bf16[1,2048,768]{2,1,0:T(8,128)(2,1)S(1)}, bf16[1,2048,768]{2,1,0:T(8,128)(2,1)}, u32[]{:S(2)}) copy-start(bf16[1,2048,768]{2,1,0:T(8,128)(2,1)} %param.9) | copy-start | bytes 9437188
  29.0 1.9 %copy-start.2 = (bf16[1,2048,768]{2,1,0:T(8,128)(2,1)S(1)}, bf16[1,2048,768]{2,1,0:T(8,128)(2,1)}, u32[]{:S(2)}) copy-start(bf16[1,2048,768]{2,1,0:T(8,128)(2,1)} %param.10) | copy-start | bytes 9437188
  30.9 1.9 %copy-start.4 = (bf16[1,768,2048]{2,1,0:T(8,128)(2,1)S(1)}, bf16[1,768,2048]{2,1,0:T(8,128)(2,1)}, u32[]{:S(2)}) copy-start(bf16[1,768,2048]{2,1,0:T(8,128)(2,1)} %param.11) | copy-start | bytes 9437188
  32.8 1.0 copy-start.6
  33.8 9.1 %copy-start.1 = (bf16[1,2048,768]{2,1,0:T(8,128)(2,1)S(1)}, bf16[1,2048,768]{2,1,0:T(8,128)(2,1)}, u32[]{:S(2)}) copy-start(bf16[1,2048,768]{2,1,0:T(8,128)(2,1)} %param.9) | copy-start | bytes 9437188
  33.8 9.1 %copy-start.3 = (bf16[1,2048,768]{2,1,0:T(8,128)(2,1)S(1)}, bf16[1,2048,768]{2,1,0:T(8,128)(2,1)}, u32[]{:S(2)}) copy-start(bf16[1,2048,768]{2,1,0:T(8,128)(2,1)} %param.10) | copy-start | bytes 9437188
  33.8 9.1 %copy-start.5 = (bf16[1,768,2048]{2,1,0:T(8,128)(2,1)S(1)}, bf16[1,768,2048]{2,1,0:T(8,128)(2,1)}, u32[]{:S(2)}) copy-start(bf16[1,768,2048]{2,1,0:T(8,128)(2,1)} %param.11) | copy-start | bytes 9437188
  41.0 1.9 %collective-permute-start.11 = (bf16[128,2048]{1,0:T(8,128)(2,1)S(1)}, bf16[128,2048]{1,0:T(8,128)(2,1)S(1)}, u32[]{:S(2)}, u32[]{:S(2)}) collective-permute-start(bf16[128,2048]{1,0:T(8,128)(2,1)S(1)} %collective-permute-done.5.refs_1_), channel_id=1, source_target_pairs={{0,1},{1,0},{2,3},{3,2},{4,5},{5,4},{6,7},{7,6},{8,9},{9,8},{10,11... | collective-permute-start | bytes 1572872 | tf_op jit(solution)/shard_map/ppermute | solution.py:256
  41.1 14.4 %collective-permute-start.8 = (bf16[128,2048]{1,0:T(8,128)(2,1)S(1)}, bf16[128,2048]{1,0:T(8,128)(2,1)S(1)}, u32[]{:S(2)}, u32[]{:S(2)}) collective-permute-start(bf16[128,2048]{1,0:T(8,128)(2,1)S(1)} %constant_dynamic-update-slice_fusion.refs_0_), channel_id=1, source_target_pairs={{0,4},{1,5},{2,6},{3,7},{4,0},{5,1},{6,2},{7,3},{8,12},{9,13},{10,... | collective-permute-start | bytes 1572872 | tf_op jit(solution)/shard_map/ppermute | solution.py:256
  41.2 14.3 %collective-permute-start.9 = (bf16[128,2048]{1,0:T(8,128)(2,1)S(1)}, bf16[128,2048]{1,0:T(8,128)(2,1)S(1)}, u32[]{:S(2)}, u32[]{:S(2)}) collective-permute-start(bf16[128,2048]{1,0:T(8,128)(2,1)S(1)} %constant_dynamic-update-slice_fusion.refs_0_), channel_id=1, source_target_pairs={{0,2},{1,3},{2,0},{3,1},{4,6},{5,7},{6,4},{7,5},{8,10},{9,11},{10,... | collective-permute-start | bytes 1572872 | tf_op jit(solution)/shard_map/ppermute | solution.py:256
  42.7 12.8 %collective-permute-start.10 = (bf16[128,2048]{1,0:T(8,128)(2,1)S(1)}, bf16[128,2048]{1,0:T(8,128)(2,1)S(1)}, u32[]{:S(2)}, u32[]{:S(2)}) collective-permute-start(bf16[128,2048]{1,0:T(8,128)(2,1)S(1)} %constant_dynamic-update-slice_fusion.refs_0_), channel_id=1, source_target_pairs={{0,1},{1,0},{2,3},{3,2},{4,5},{5,4},{6,7},{7,6},{8,9},{9,8},{10,11... | collective-permute-start | bytes 1572872 | tf_op jit(solution)/shard_map/ppermute | solution.py:256
  48.4 7.1 %collective-permute-start.12 = (bf16[128,2048]{1,0:T(8,128)(2,1)S(1)}, bf16[128,2048]{1,0:T(8,128)(2,1)S(1)}, u32[]{:S(2)}, u32[]{:S(2)}) collective-permute-start(bf16[128,2048]{1,0:T(8,128)(2,1)S(1)} %get-tuple-element.97), channel_id=1, source_target_pairs={{0,1},{1,0},{2,3},{3,2},{4,5},{5,4},{6,7},{7,6},{8,9},{9,8},{10,11... | collective-permute-start | bytes 1572872 | tf_op jit(solution)/shard_map/ppermute | solution.py:256
  55.5 3.6 %collective-permute-start.16 = (bf16[128,2048]{1,0:T(8,128)(2,1)S(1)}, bf16[128,2048]{1,0:T(8,128)(2,1)S(1)}, u32[]{:S(2)}, u32[]{:S(2)}) collective-permute-start(bf16[128,2048]{1,0:T(8,128)(2,1)S(1)} %collective-permute-done.9.refs_1_), channel_id=1, source_target_pairs={{0,1},{1,0},{2,3},{3,2},{4,5},{5,4},{6,7},{7,6},{8,9},{9,8},{10,11... | collective-permute-start | bytes 1572872 | tf_op jit(solution)/shard_map/ppermute | solution.py:256
  55.6 14.3 %collective-permute-start.13 = (bf16[128,2048]{1,0:T(8,128)(2,1)S(1)}, bf16[128,2048]{1,0:T(8,128)(2,1)S(1)}, u32[]{:S(2)}, u32[]{:S(2)}) collective-permute-start(bf16[128,2048]{1,0:T(8,128)(2,1)S(1)} %collective-permute-done.9.refs_1_), channel_id=1, source_target_pairs={{0,4},{1,5},{2,6},{3,7},{4,0},{5,1},{6,2},{7,3},{8,12},{9,13},{10,... | collective-permute-start | bytes 1572872 | tf_op jit(solution)/shard_map/ppermute | solution.py:256
  57.3 8.0 %collective-permute-start.18 = (bf16[128,2048]{1,0:T(8,128)(2,1)S(1)}, bf16[128,2048]{1,0:T(8,128)(2,1)S(1)}, u32[]{:S(2)}, u32[]{:S(2)}) collective-permute-start(bf16[128,2048]{1,0:T(8,128)(2,1)S(1)} %collective-permute-done.8.refs_0_), channel_id=1, source_target_pairs={{0,1},{1,0},{2,3},{3,2},{4,5},{5,4},{6,7},{7,6},{8,9},{9,8},{10,11... | collective-permute-start | bytes 1572872 | tf_op jit(solution)/shard_map/ppermute | solution.py:256
  57.6 10.5 %collective-permute-start.14 = (bf16[64,2048]{1,0:T(8,128)(2,1)S(1)}, bf16[64,2048]{1,0:T(8,128)(2,1)S(1)}, u32[]{:S(2)}, u32[]{:S(2)}) collective-permute-start(bf16[64,2048]{1,0:T(8,128)(2,1)S(1)} %get-tuple-element.155), channel_id=1, source_target_pairs={{0,2},{1,3},{2,0},{3,1},{4,6},{5,7},{6,4},{7,5},{8,10},{9,11},{10,... | collective-permute-start | bytes 786440 | tf_op jit(solution)/shard_map/ppermute | solution.py:256
  59.1 10.8 %collective-permute-start.15 = (bf16[128,2048]{1,0:T(8,128)(2,1)S(1)}, bf16[128,2048]{1,0:T(8,128)(2,1)S(1)}, u32[]{:S(2)}, u32[]{:S(2)}) collective-permute-start(bf16[128,2048]{1,0:T(8,128)(2,1)S(1)} %get-tuple-element.101), channel_id=1, source_target_pairs={{0,1},{1,0},{2,3},{3,2},{4,5},{5,4},{6,7},{7,6},{8,9},{9,8},{10,11... | collective-permute-start | bytes 1572872 | tf_op jit(solution)/shard_map/ppermute | solution.py:256
  64.8 5.1 %collective-permute-start.17 = (bf16[64,2048]{1,0:T(8,128)(2,1)S(1)}, bf16[64,2048]{1,0:T(8,128)(2,1)S(1)}, u32[]{:S(2)}, u32[]{:S(2)}) collective-permute-start(bf16[64,2048]{1,0:T(8,128)(2,1)S(1)} %get-tuple-element.103), channel_id=1, source_target_pairs={{0,1},{1,0},{2,3},{3,2},{4,5},{5,4},{6,7},{7,6},{8,9},{9,8},{10,11... | collective-permute-start | bytes 786440 | tf_op jit(solution)/shard_map/ppermute | solution.py:256
  65.3 17.2 %collective-permute-start.27 = (bf16[256,2048]{1,0:T(8,128)(2,1)S(1)}, bf16[256,2048]{1,0:T(8,128)(2,1)S(1)}, u32[]{:S(2)}, u32[]{:S(2)}) collective-permute-start(bf16[256,2048]{1,0:T(8,128)(2,1)S(1)} %get-tuple-element.127), channel_id=1, source_target_pairs={{0,1},{1,0},{2,3},{3,2},{4,5},{5,4},{6,7},{7,6},{8,9},{9,8},{10,11... | collective-permute-start | bytes 3145736 | tf_op jit(solution)/shard_map/ppermute | solution.py:256
  69.9 2.2 %collective-permute-start.19 = (bf16[128,2048]{1,0:T(8,128)(2,1)S(1)}, bf16[128,2048]{1,0:T(8,128)(2,1)S(1)}, u32[]{:S(2)}, u32[]{:S(2)}) collective-permute-start(bf16[128,2048]{1,0:T(8,128)(2,1)S(1)} %collective-permute-done.13.refs_0_), channel_id=1, source_target_pairs={{0,1},{1,0},{2,3},{3,2},{4,5},{5,4},{6,7},{7,6},{8,9},{9,8},{10,11... | collective-permute-start | bytes 1572872 | tf_op jit(solution)/shard_map/ppermute | solution.py:256
  69.9 8.9 %collective-permute-start.20 = (bf16[128,2048]{1,0:T(8,128)(2,1)S(1)}, bf16[128,2048]{1,0:T(8,128)(2,1)S(1)}, u32[]{:S(2)}, u32[]{:S(2)}) collective-permute-start(bf16[128,2048]{1,0:T(8,128)(2,1)S(1)} %get-tuple-element.117), channel_id=1, source_target_pairs={{0,1},{1,0},{2,3},{3,2},{4,5},{5,4},{6,7},{7,6},{8,9},{9,8},{10,11... | collective-permute-start | bytes 1572872 | tf_op jit(solution)/shard_map/ppermute | solution.py:256
  70.5 8.3 %collective-permute-start.21 = (bf16[64,2048]{1,0:T(8,128)(2,1)S(1)}, bf16[64,2048]{1,0:T(8,128)(2,1)S(1)}, u32[]{:S(2)}, u32[]{:S(2)}) collective-permute-start(bf16[64,2048]{1,0:T(8,128)(2,1)S(1)} %add_convert_fusion.11), channel_id=1, source_target_pairs={{0,2},{1,3},{2,0},{3,1},{4,6},{5,7},{6,4},{7,5},{8,10},{9,11},{10,... | collective-permute-start | bytes 786440 | tf_op jit(solution)/shard_map/ppermute | solution.py:256
  78.9 2.4 %collective-permute-start.22 = (bf16[128,2048]{1,0:T(8,128)(2,1)S(1)}, bf16[128,2048]{1,0:T(8,128)(2,1)S(1)}, u32[]{:S(2)}, u32[]{:S(2)}) collective-permute-start(bf16[128,2048]{1,0:T(8,128)(2,1)S(1)} %get-tuple-element.123), channel_id=1, source_target_pairs={{0,1},{1,0},{2,3},{3,2},{4,5},{5,4},{6,7},{7,6},{8,9},{9,8},{10,11... | collective-permute-start | bytes 1572872 | tf_op jit(solution)/shard_map/ppermute | solution.py:256
  78.9 5.2 %collective-permute-start.28 = (bf16[64,2048]{1,0:T(8,128)(2,1)S(1)}, bf16[64,2048]{1,0:T(8,128)(2,1)S(1)}, u32[]{:S(2)}, u32[]{:S(2)}) collective-permute-start(bf16[64,2048]{1,0:T(8,128)(2,1)S(1)} %get-tuple-element.128), channel_id=1, source_target_pairs={{0,1},{1,0},{2,3},{3,2},{4,5},{5,4},{6,7},{7,6},{8,9},{9,8},{10,11... | collective-permute-start | bytes 786440 | tf_op jit(solution)/shard_map/ppermute | solution.py:256
  79.4 8.4 %collective-permute-start.29 = (bf16[128,2048]{1,0:T(8,128)(2,1)S(1)}, bf16[128,2048]{1,0:T(8,128)(2,1)S(1)}, u32[]{:S(2)}, u32[]{:S(2)}) collective-permute-start(bf16[128,2048]{1,0:T(8,128)(2,1)S(1)} %get-tuple-element.129), channel_id=1, source_target_pairs={{0,1},{1,0},{2,3},{3,2},{4,5},{5,4},{6,7},{7,6},{8,9},{9,8},{10,11... | collective-permute-start | bytes 1572872 | tf_op jit(solution)/shard_map/ppermute | solution.py:256
  79.5 15.3 %collective-permute-start.25 = (bf16[64,2048]{1,0:T(8,128)(2,1)S(1)}, bf16[64,2048]{1,0:T(8,128)(2,1)S(1)}, u32[]{:S(2)}, u32[]{:S(2)}) collective-permute-start(bf16[64,2048]{1,0:T(8,128)(2,1)S(1)} %add_convert_fusion.7), channel_id=1, source_target_pairs={{0,8},{1,9},{2,10},{3,11},{4,12},{5,13},{6,14},{7,15},{8,0},{9,1},... | collective-permute-start | bytes 786440 | tf_op jit(solution)/shard_map/ppermute | solution.py:256
  81.2 13.5 %collective-permute-start.26 = (bf16[64,2048]{1,0:T(8,128)(2,1)S(1)}, bf16[64,2048]{1,0:T(8,128)(2,1)S(1)}, u32[]{:S(2)}, u32[]{:S(2)}) collective-permute-start(bf16[64,2048]{1,0:T(8,128)(2,1)S(1)} %add_convert_fusion.10), channel_id=1, source_target_pairs={{0,4},{1,5},{2,6},{3,7},{4,0},{5,1},{6,2},{7,3},{8,12},{9,13},{10,... | collective-permute-start | bytes 786440 | tf_op jit(solution)/shard_map/ppermute | solution.py:256
  82.6 12.2 %collective-permute-start.23 = (bf16[64,2048]{1,0:T(8,128)(2,1)S(1)}, bf16[64,2048]{1,0:T(8,128)(2,1)S(1)}, u32[]{:S(2)}, u32[]{:S(2)}) collective-permute-start(bf16[64,2048]{1,0:T(8,128)(2,1)S(1)} %get-tuple-element.159), channel_id=1, source_target_pairs={{0,2},{1,3},{2,0},{3,1},{4,6},{5,7},{6,4},{7,5},{8,10},{9,11},{10,... | collective-permute-start | bytes 786440 | tf_op jit(solution)/shard_map/ppermute | solution.py:256
  84.1 12.2 %collective-permute-start.24 = (bf16[64,2048]{1,0:T(8,128)(2,1)S(1)}, bf16[64,2048]{1,0:T(8,128)(2,1)S(1)}, u32[]{:S(2)}, u32[]{:S(2)}) collective-permute-start(bf16[64,2048]{1,0:T(8,128)(2,1)S(1)} %get-tuple-element.158), channel_id=1, source_target_pairs={{0,2},{1,3},{2,0},{3,1},{4,6},{5,7},{6,4},{7,5},{8,10},{9,11},{10,... | collective-permute-start | bytes 786440 | tf_op jit(solution)/shard_map/ppermute | solution.py:256
  96.5 13.9 %collective-permute-start.30 = (bf16[64,2048]{1,0:T(8,128)(2,1)S(1)}, bf16[64,2048]{1,0:T(8,128)(2,1)S(1)}, u32[]{:S(2)}, u32[]{:S(2)}) collective-permute-start(bf16[64,2048]{1,0:T(8,128)(2,1)S(1)} %get-tuple-element.157), channel_id=1, source_target_pairs={{0,8},{1,9},{2,10},{3,11},{4,12},{5,13},{6,14},{7,15},{8,0},{9,1},... | collective-permute-start | bytes 786440 | tf_op jit(solution)/shard_map/ppermute | solution.py:256
  98.4 12.0 %collective-permute-start.31 = (bf16[64,2048]{1,0:T(8,128)(2,1)S(1)}, bf16[64,2048]{1,0:T(8,128)(2,1)S(1)}, u32[]{:S(2)}, u32[]{:S(2)}) collective-permute-start(bf16[64,2048]{1,0:T(8,128)(2,1)S(1)} %get-tuple-element.156), channel_id=1, source_target_pairs={{0,4},{1,5},{2,6},{3,7},{4,0},{5,1},{6,2},{7,3},{8,12},{9,13},{10,... | collective-permute-start | bytes 786440 | tf_op jit(solution)/shard_map/ppermute | solution.py:256
  98.9 11.6 %collective-permute-start.32 = (bf16[64,2048]{1,0:T(8,128)(2,1)S(1)}, bf16[64,2048]{1,0:T(8,128)(2,1)S(1)}, u32[]{:S(2)}, u32[]{:S(2)}) collective-permute-start(bf16[64,2048]{1,0:T(8,128)(2,1)S(1)} %add_convert_fusion.3), channel_id=1, source_target_pairs={{0,2},{1,3},{2,0},{3,1},{4,6},{5,7},{6,4},{7,5},{8,10},{9,11},{10,... | collective-permute-start | bytes 786440 | tf_op jit(solution)/shard_map/ppermute | solution.py:256
  100.4 10.9 %collective-permute-start.33 = (bf16[64,2048]{1,0:T(8,128)(2,1)S(1)}, bf16[64,2048]{1,0:T(8,128)(2,1)S(1)}, u32[]{:S(2)}, u32[]{:S(2)}) collective-permute-start(bf16[64,2048]{1,0:T(8,128)(2,1)S(1)} %get-tuple-element.134), channel_id=1, source_target_pairs={{0,2},{1,3},{2,0},{3,1},{4,6},{5,7},{6,4},{7,5},{8,10},{9,11},{10,... | collective-permute-start | bytes 786440 | tf_op jit(solution)/shard_map/ppermute | solution.py:256
  111.4 13.5 %collective-permute-start.34 = (bf16[64,2048]{1,0:T(8,128)(2,1)S(1)}, bf16[64,2048]{1,0:T(8,128)(2,1)S(1)}, u32[]{:S(2)}, u32[]{:S(2)}) collective-permute-start(bf16[64,2048]{1,0:T(8,128)(2,1)S(1)} %add_convert_fusion.2), channel_id=1, source_target_pairs={{0,8},{1,9},{2,10},{3,11},{4,12},{5,13},{6,14},{7,15},{8,0},{9,1},... | collective-permute-start | bytes 786440 | tf_op jit(solution)/shard_map/ppermute | solution.py:256
  113.2 12.3 %collective-permute-start.36 = (bf16[128,2048]{1,0:T(8,128)(2,1)S(1)}, bf16[128,2048]{1,0:T(8,128)(2,1)S(1)}, u32[]{:S(2)}, u32[]{:S(2)}) collective-permute-start(bf16[128,2048]{1,0:T(8,128)(2,1)S(1)} %add_convert_fusion), channel_id=1, source_target_pairs={{0,2},{1,3},{2,0},{3,1},{4,6},{5,7},{6,4},{7,5},{8,10},{9,11},{10,... | collective-permute-start | bytes 1572872 | tf_op jit(solution)/shard_map/ppermute | solution.py:256
  114.7 10.7 %collective-permute-start.35 = (bf16[64,2048]{1,0:T(8,128)(2,1)S(1)}, bf16[64,2048]{1,0:T(8,128)(2,1)S(1)}, u32[]{:S(2)}, u32[]{:S(2)}) collective-permute-start(bf16[64,2048]{1,0:T(8,128)(2,1)S(1)} %add_convert_fusion.1), channel_id=1, source_target_pairs={{0,4},{1,5},{2,6},{3,7},{4,0},{5,1},{6,2},{7,3},{8,12},{9,13},{10,... | collective-permute-start | bytes 786440 | tf_op jit(solution)/shard_map/ppermute | solution.py:256

commit v30 on v28

--- a/solution.py
+++ b/solution.py
@@ -326,8 +326,8 @@
     side_high = column(summed(keep2[tok + half :], got2_high))
     got2 = sibling(give2)
     keep3_side, give3_side, act4 = expert(3, b3, d3, picked=(1, 3))
-    keep3_side, give3_side, act4, got2, side_high, near1 = together(
-        keep3_side, give3_side, act4, got2, side_high, near1
+    side_high, keep3_side, give3_side, act4, got2, near1 = together(
+        side_high, keep3_side, give3_side, act4, got2, near1
     )
     got2_low, got3 = sibling(give2_low), sibling(give3)
     far2_high = far(summed(keep2[half:tok], got2[half:], side_high))

time: 126 us -> 126 us (level)
  no operation moved by 1% of the time
where the time goes in v30:
time: 126 us
  waiting for transfers between devices  42.3 us (34%)
  starting transfers between devices  30.8 us (24%)
  Pallas kernels  28.9 us (23%)
  blocking collectives  14.9 us (12%)
  local copies, waits for them, and re-layouts  6.84 us (5%)
    ppermute x37, waiting for transfers between devices, swapped(): return lax.ppermute(array, 'expert', [(i, i ^ bit) for i in range(size)])  42.3 us
    ppermute x37, starting transfers between devices, swapped(): return lax.ppermute(array, 'expert', [(i, i ^ bit) for i in range(size)])  30.8 us
    pallas_call x5, Pallas kernels, plane_pass(): pl.pallas_call(functools.partial(plane_kernel, k, picked, len(pieces)), o...  22 us
    all_to_all x1, blocking collectives, staged(): lax.all_to_all(mine, 'expert', split_axis=0, concat_axis=0, tiled=True)  14.9 us
    unnamed x15, local copies, waits for them, and re-layouts  6.73 us
    pallas_call x1, Pallas kernels, gram_pass(): pl.pallas_call(gram_kernel, out_shape=jax.ShapeDtypeStruct((hidden, hidde...  3.14 us
  transfers between devices with their start and end apart: 37, of which 11 were waited for; matrix products, arithmetic and copies ran while one was open for 1% of the time, Pallas kernels for 22%

profile of v30, /device:TPU:0, one launch (start us, length us, event | category | flops | bytes accessed | tf_op | source)
XLA Modules:
  0.0 125.9 jit_solution(3481392516660946397)
XLA Ops:
  0.6 3.1 %collective-permute-start = (bf16[128,2048]{1,0:T(8,128)(2,1)}, bf16[128,2048]{1,0:T(8,128)(2,1)S(1)}, u32[]{:S(2)}, u32[]{:S(2)}) collective-permute-start(bf16[128,2048]{1,0:T(8,128)(2,1)} %refs_0_.1), channel_id=1, source_target_pairs={{0,4},{1,5},{2,6},{3,7},{4,0},{5,1},{6,2},{7,3},{8,12},{9,13},{10,... | collective-permute-start | bytes 1572872 | tf_op jit(solution)/shard_map/ppermute | solution.py:256
  3.7 1.5 %collective-permute-start.2 = (bf16[128,2048]{1,0:T(8,128)(2,1)}, bf16[128,2048]{1,0:T(8,128)(2,1)S(1)}, u32[]{:S(2)}, u32[]{:S(2)}) collective-permute-start(bf16[128,2048]{1,0:T(8,128)(2,1)} %refs_0_.1), channel_id=1, source_target_pairs={{0,2},{1,3},{2,0},{3,1},{4,6},{5,7},{6,4},{7,5},{8,10},{9,11},{10,... | collective-permute-start | bytes 1572872 | tf_op jit(solution)/shard_map/ppermute | solution.py:256
  5.2 1.9 %shard_map.77 = (f32[16,128]{1,0:T(8,128)}, bf16[64,2048]{1,0:T(8,128)(2,1)}, bf16[64,2048]{1,0:T(8,128)(2,1)}) custom-call(s32[8,128]{1,0:T(8,128)} %bitcast.43, f32[8,128]{1,0:T(8,128)} %bitcast.44, bf16[128,2048]{1,0:T(8,128)(2,1)} %refs_0_.1), custom_call_target="tpu_custom_call" | custom-call | tf_op jit(solution)/shard_map/pallas_call | solution.py:57
  7.1 2.7 %collective-permute-start.1 = (bf16[64,2048]{1,0:T(8,128)(2,1)}, bf16[64,2048]{1,0:T(8,128)(2,1)S(1)}, u32[]{:S(2)}, u32[]{:S(2)}) collective-permute-start(bf16[64,2048]{1,0:T(8,128)(2,1)} %get-tuple-element.79), channel_id=1, source_target_pairs={{0,8},{1,9},{2,10},{3,11},{4,12},{5,13},{6,14},{7,15},{8,0},{9,1},... | collective-permute-start | bytes 786440 | tf_op jit(solution)/shard_map/ppermute | solution.py:256
  9.8 14.9 %all_to_all.12 = f32[16,1,128]{2,1,0:T(1,128)S(1)} all-to-all(f32[16,1,128]{2,1,0:T(1,128)} %bitcast.42), channel_id=1, replica_groups=mesh['parts'=2,'expert'=16] {'expert'}, dimensions={0} | all-to-all | bytes 16384 | tf_op jit(solution)/shard_map/all_to_all | solution.py:285
  24.7 0.1 collective-permute-start.7
  24.8 0.6 collective-permute-start.5
  25.4 0.2 collective-permute-start.6
  25.6 0.1 stack.67.spots
  25.6 0.7 collective-permute-start.4
  26.3 0.7 shard_map.78.tables
  27.1 1.9 %copy-done = bf16[1,2048,768]{2,1,0:T(8,128)(2,1)S(1)} copy-done((bf16[1,2048,768]{2,1,0:T(8,128)(2,1)S(1)}, bf16[1,2048,768]{2,1,0:T(8,128)(2,1)}, u32[]{:S(2)}) %copy-start) | copy-done | bytes 3145752
  29.0 1.9 %copy-done.2 = bf16[1,2048,768]{2,1,0:T(8,128)(2,1)S(1)} copy-done((bf16[1,2048,768]{2,1,0:T(8,128)(2,1)S(1)}, bf16[1,2048,768]{2,1,0:T(8,128)(2,1)}, u32[]{:S(2)}) %copy-start.2) | copy-done | bytes 3145752
  30.9 1.9 %copy-done.4 = bf16[1,768,2048]{2,1,0:T(8,128)(2,1)S(1)} copy-done((bf16[1,768,2048]{2,1,0:T(8,128)(2,1)S(1)}, bf16[1,768,2048]{2,1,0:T(8,128)(2,1)}, u32[]{:S(2)}) %copy-start.4) | copy-done | bytes 3145752
  32.8 1.0 copy-done.6
  33.8 5.5 %shard_map.79 = (bf16[256,2048]{1,0:T(8,128)(2,1)S(1)}, bf16[256,2048]{1,0:T(8,128)(2,1)S(1)}, bf16[320,768]{1,0:T(8,128)(2,1)S(1)}) custom-call(f32[16,512]{1,0:T(8,128)S(1)} %shard_map.78.tables, bf16[128,2048]{1,0:T(8,128)(2,1)S(1)} %copy-done.6, bf16[128,2048]{1,0:T(8,128)(2,1)S(1)} %collective-permute-done.2.refs_1_, ...), custom_call_target="tpu_custom_call" | custom-call | flops 4362076160 | bytes 13631488 | tf_op jit(solution)/shard_map/pallas_call | solution.py:178
  39.3 1.7 %collective-permute-done.4 = bf16[64,2048]{1,0:T(8,128)(2,1)S(1)} collective-permute-done((bf16[64,2048]{1,0:T(8,128)(2,1)}, bf16[64,2048]{1,0:T(8,128)(2,1)S(1)}, u32[]{:S(2)}, u32[]{:S(2)}) %collective-permute-start.4) | collective-permute-done | bytes 262176 | tf_op jit(solution)/shard_map/ppermute | solution.py:256
  41.1 0.2 collective-permute-start.8
  41.2 1.5 %collective-permute-start.9 = (bf16[128,2048]{1,0:T(8,128)(2,1)S(1)}, bf16[128,2048]{1,0:T(8,128)(2,1)S(1)}, u32[]{:S(2)}, u32[]{:S(2)}) collective-permute-start(bf16[128,2048]{1,0:T(8,128)(2,1)S(1)} %constant_dynamic-update-slice_fusion.refs_0_), channel_id=1, source_target_pairs={{0,2},{1,3},{2,0},{3,1},{4,6},{5,7},{6,4},{7,5},{8,10},{9,11},{10,... | collective-permute-start | bytes 1572872 | tf_op jit(solution)/shard_map/ppermute | solution.py:256
  42.7 0.2 collective-permute-start.10
  42.9 5.5 %shard_map.80 = (bf16[256,2048]{1,0:T(8,128)(2,1)S(1)}, bf16[128,2048]{1,0:T(8,128)(2,1)S(1)}, bf16[128,2048]{1,0:T(8,128)(2,1)S(1)}, bf16[320,768]{1,0:T(8,128)(2,1)S(1)}) custom-call(f32[16,512]{1,0:T(8,128)S(1)} %shard_map.78.tables, bf16[128,2048]{1,0:T(8,128)(2,1)S(1)} %collective-permute-done.refs_0_, ...), custom_call_target="tpu_custom_call" | custom-call | flops 4362076160 | bytes 13631488 | tf_op jit(solution)/shard_map/pallas_call | solution.py:178
  48.4 0.4 collective-permute-start.12
  48.8 6.7 %collective-permute-done.8.refs_0_ = bf16[128,2048]{1,0:T(8,128)(2,1)S(1)} collective-permute-done((bf16[128,2048]{1,0:T(8,128)(2,1)S(1)}, bf16[128,2048]{1,0:T(8,128)(2,1)S(1)}, u32[]{:S(2)}, u32[]{:S(2)}) %collective-permute-start.8) | collective-permute-done | bytes 524320 | tf_op jit(solution)/shard_map/ppermute | solution.py:256
  55.5 0.1 collective-permute-done.9.refs_1_
  55.6 0.5 collective-permute-start.15
  56.1 1.6 %collective-permute-start.13 = (bf16[128,2048]{1,0:T(8,128)(2,1)S(1)}, bf16[128,2048]{1,0:T(8,128)(2,1)S(1)}, u32[]{:S(2)}, u32[]{:S(2)}) collective-permute-start(bf16[128,2048]{1,0:T(8,128)(2,1)S(1)} %collective-permute-done.9.refs_1_), channel_id=1, source_target_pairs={{0,4},{1,5},{2,6},{3,7},{4,0},{5,1},{6,2},{7,3},{8,12},{9,13},{10,... | collective-permute-start | bytes 1572872 | tf_op jit(solution)/shard_map/ppermute | solution.py:256
  57.7 0.1 add_convert_fusion.6
  57.9 1.5 %collective-permute-start.14 = (bf16[64,2048]{1,0:T(8,128)(2,1)S(1)}, bf16[64,2048]{1,0:T(8,128)(2,1)S(1)}, u32[]{:S(2)}, u32[]{:S(2)}) collective-permute-start(bf16[64,2048]{1,0:T(8,128)(2,1)S(1)} %get-tuple-element.157), channel_id=1, source_target_pairs={{0,2},{1,3},{2,0},{3,1},{4,6},{5,7},{6,4},{7,5},{8,10},{9,11},{10,... | collective-permute-start | bytes 786440 | tf_op jit(solution)/shard_map/ppermute | solution.py:256
  59.4 0.2 collective-permute-start.16
  59.6 5.7 %shard_map.81 = (bf16[256,2048]{1,0:T(8,128)(2,1)S(1)}, bf16[128,2048]{1,0:T(8,128)(2,1)S(1)}, bf16[64,2048]{1,0:T(8,128)(2,1)S(1)}, bf16[64,2048]{1,0:T(8,128)(2,1)S(1)}, bf16[320,768]{1,0:T(8,128)(2,1)S(1)}) custom-call(f32[16,512]{1,0:T(8,128)S(1)} %shard_map.78.tables, bf16[128,2048]{1,0:T(8,128)(2,1)S(1)} %constant_dynamic-update-slice_fusion.refs_0_, ...), custom_call_target="tpu_custom_call" | custom-call | flops 4362076160 | bytes 13631488 | tf_op jit(solution)/shard_map/pallas_call | solution.py:178
  65.3 0.3 collective-permute-start.18
  65.6 2.7 %shard_map.82 = (bf16[128,2048]{1,0:T(8,128)(2,1)S(1)}, bf16[128,2048]{1,0:T(8,128)(2,1)S(1)}, bf16[160,768]{1,0:T(8,128)(2,1)S(1)}) custom-call(f32[16,512]{1,0:T(8,128)S(1)} %shard_map.78.tables, bf16[128,2048]{1,0:T(8,128)(2,1)S(1)} %collective-permute-done.8.refs_0_, bf16[128,2048]{1,0:T(8,128)(2,1)S(1)} %collective-permute-done.19.refs_1_, ...), custom_call_target="tpu_custom_call" | custom-call | flops 1845493760 | bytes 11534336 | tf_op jit(solution)/shard_map/pallas_call | solution.py:178
  68.4 1.6 %collective-permute-done.13.refs_0_ = bf16[128,2048]{1,0:T(8,128)(2,1)S(1)} collective-permute-done((bf16[128,2048]{1,0:T(8,128)(2,1)S(1)}, bf16[128,2048]{1,0:T(8,128)(2,1)S(1)}, u32[]{:S(2)}, u32[]{:S(2)}) %collective-permute-start.13) | collective-permute-done | bytes 524320 | tf_op jit(solution)/shard_map/ppermute | solution.py:256
  70.1 1.5 %collective-permute-start.20 = (bf16[64,2048]{1,0:T(8,128)(2,1)S(1)}, bf16[64,2048]{1,0:T(8,128)(2,1)S(1)}, u32[]{:S(2)}, u32[]{:S(2)}) collective-permute-start(bf16[64,2048]{1,0:T(8,128)(2,1)S(1)} %add_convert_fusion.11), channel_id=1, source_target_pairs={{0,2},{1,3},{2,0},{3,1},{4,6},{5,7},{6,4},{7,5},{8,10},{9,11},{10,... | collective-permute-start | bytes 786440 | tf_op jit(solution)/shard_map/ppermute | solution.py:256
  71.6 0.2 collective-permute-start.22
  71.8 0.1 add_convert_fusion.10
  71.9 2.7 %shard_map.83 = (bf16[128,2048]{1,0:T(8,128)(2,1)S(1)}, bf16[128,2048]{1,0:T(8,128)(2,1)S(1)}, bf16[160,768]{1,0:T(8,128)(2,1)S(1)}) custom-call(f32[16,512]{1,0:T(8,128)S(1)} %shard_map.78.tables, bf16[128,2048]{1,0:T(8,128)(2,1)S(1)} %collective-permute-done.13.refs_0_, bf16[128,2048]{1,0:T(8,128)(2,1)S(1)} %collective-permute-done.21.refs_1_, ...), custom_call_target="tpu_custom_call" | custom-call | flops 1845493760 | bytes 11534336 | tf_op jit(solution)/shard_map/pallas_call | solution.py:178
  74.7 4.2 %collective-permute-done.20 = bf16[64,2048]{1,0:T(8,128)(2,1)S(1)} collective-permute-done((bf16[64,2048]{1,0:T(8,128)(2,1)S(1)}, bf16[64,2048]{1,0:T(8,128)(2,1)S(1)}, u32[]{:S(2)}, u32[]{:S(2)}) %collective-permute-start.20) | collective-permute-done | bytes 262176 | tf_op jit(solution)/shard_map/ppermute | solution.py:256
  78.9 0.5 collective-permute-start.28
  79.4 0.1 add_convert_fusion.7
  79.5 1.8 %collective-permute-start.26 = (bf16[64,2048]{1,0:T(8,128)(2,1)S(1)}, bf16[64,2048]{1,0:T(8,128)(2,1)S(1)}, u32[]{:S(2)}, u32[]{:S(2)}) collective-permute-start(bf16[64,2048]{1,0:T(8,128)(2,1)S(1)} %add_convert_fusion.7), channel_id=1, source_target_pairs={{0,8},{1,9},{2,10},{3,11},{4,12},{5,13},{6,14},{7,15},{8,0},{9,1},... | collective-permute-start | bytes 786440 | tf_op jit(solution)/shard_map/ppermute | solution.py:256
  81.2 0.6 collective-permute-start.27
  81.9 0.1 add_convert_fusion.8
  82.0 1.6 %collective-permute-start.24 = (bf16[64,2048]{1,0:T(8,128)(2,1)S(1)}, bf16[64,2048]{1,0:T(8,128)(2,1)S(1)}, u32[]{:S(2)}, u32[]{:S(2)}) collective-permute-start(bf16[64,2048]{1,0:T(8,128)(2,1)S(1)} %get-tuple-element.161), channel_id=1, source_target_pairs={{0,2},{1,3},{2,0},{3,1},{4,6},{5,7},{6,4},{7,5},{8,10},{9,11},{10,... | collective-permute-start | bytes 786440 | tf_op jit(solution)/shard_map/ppermute | solution.py:256
  83.6 0.5 collective-permute-start.25
  84.1 0.1 add_convert_fusion
  84.2 10.5 %collective-permute-done.26.far_high = bf16[64,2048]{1,0:T(8,128)(2,1)S(1)} collective-permute-done((bf16[64,2048]{1,0:T(8,128)(2,1)S(1)}, bf16[64,2048]{1,0:T(8,128)(2,1)S(1)}, u32[]{:S(2)}, u32[]{:S(2)}) %collective-permute-start.26) | collective-permute-done | bytes 262176 | tf_op jit(solution)/shard_map/ppermute | solution.py:256
  94.8 1.1 collective-permute-done.25
  95.9 0.2 add_convert_fusion.4
  96.1 2.3 %collective-permute-start.30 = (bf16[64,2048]{1,0:T(8,128)(2,1)S(1)}, bf16[64,2048]{1,0:T(8,128)(2,1)S(1)}, u32[]{:S(2)}, u32[]{:S(2)}) collective-permute-start(bf16[64,2048]{1,0:T(8,128)(2,1)S(1)} %get-tuple-element.159), channel_id=1, source_target_pairs={{0,8},{1,9},{2,10},{3,11},{4,12},{5,13},{6,14},{7,15},{8,0},{9,1},... | collective-permute-start | bytes 786440 | tf_op jit(solution)/shard_map/ppermute | solution.py:256
  98.4 0.4 collective-permute-start.31
  98.8 1.5 %collective-permute-start.32 = (bf16[64,2048]{1,0:T(8,128)(2,1)S(1)}, bf16[64,2048]{1,0:T(8,128)(2,1)S(1)}, u32[]{:S(2)}, u32[]{:S(2)}) collective-permute-start(bf16[64,2048]{1,0:T(8,128)(2,1)S(1)} %add_convert_fusion.3), channel_id=1, source_target_pairs={{0,2},{1,3},{2,0},{3,1},{4,6},{5,7},{6,4},{7,5},{8,10},{9,11},{10,... | collective-permute-start | bytes 786440 | tf_op jit(solution)/shard_map/ppermute | solution.py:256
  100.4 0.6 collective-permute-start.33
  100.9 3.1 %shard_map.84 = f32[768,768]{1,0:T(8,128)} custom-call(f32[16,512]{1,0:T(8,128)S(1)} %shard_map.78.tables, bf16[320,768]{1,0:T(8,128)(2,1)S(1)} %get-tuple-element.139.refs_0_, bf16[320,768]{1,0:T(8,128)(2,1)S(1)} %get-tuple-element.140.refs_1_, bf16[320,768]{1,0:T(8,128)(2,1)S(1)} %get-tuple-element.141.refs_2_, ...), custom_call_target="tpu_custom_call" | custom-call | flops 1509949440 | bytes 4325376 | tf_op jit(solution)/shard_map/pallas_call | solution.py:209
  104.1 6.0 %collective-permute-done.30 = bf16[64,2048]{1,0:T(8,128)(2,1)S(1)} collective-permute-done((bf16[64,2048]{1,0:T(8,128)(2,1)S(1)}, bf16[64,2048]{1,0:T(8,128)(2,1)S(1)}, u32[]{:S(2)}, u32[]{:S(2)}) %collective-permute-start.30) | collective-permute-done | bytes 262176 | tf_op jit(solution)/shard_map/ppermute | solution.py:256
  110.1 1.2 collective-permute-done.33
  111.3 0.1 add_convert_fusion.2
  111.4 1.8 %collective-permute-start.34 = (bf16[64,2048]{1,0:T(8,128)(2,1)S(1)}, bf16[64,2048]{1,0:T(8,128)(2,1)S(1)}, u32[]{:S(2)}, u32[]{:S(2)}) collective-permute-start(bf16[64,2048]{1,0:T(8,128)(2,1)S(1)} %add_convert_fusion.2), channel_id=1, source_target_pairs={{0,8},{1,9},{2,10},{3,11},{4,12},{5,13},{6,14},{7,15},{8,0},{9,1},... | collective-permute-start | bytes 786440 | tf_op jit(solution)/shard_map/ppermute | solution.py:256
  113.2 1.4 %collective-permute-start.36 = (bf16[128,2048]{1,0:T(8,128)(2,1)S(1)}, bf16[128,2048]{1,0:T(8,128)(2,1)S(1)}, u32[]{:S(2)}, u32[]{:S(2)}) collective-permute-start(bf16[128,2048]{1,0:T(8,128)(2,1)S(1)} %add_convert_fusion), channel_id=1, source_target_pairs={{0,2},{1,3},{2,0},{3,1},{4,6},{5,7},{6,4},{7,5},{8,10},{9,11},{10,... | collective-permute-start | bytes 1572872 | tf_op jit(solution)/shard_map/ppermute | solution.py:256
  114.6 0.1 add_convert_fusion.1
  114.7 0.8 collective-permute-start.35
  115.5 8.7 %collective-permute-done.34.far_low = bf16[64,2048]{1,0:T(8,128)(2,1)S(1)} collective-permute-done((bf16[64,2048]{1,0:T(8,128)(2,1)S(1)}, bf16[64,2048]{1,0:T(8,128)(2,1)S(1)}, u32[]{:S(2)}, u32[]{:S(2)}) %collective-permute-start.34) | collective-permute-done | bytes 262176 | tf_op jit(solution)/shard_map/ppermute | solution.py:256
  124.2 0.6 collective-permute-done.35.near_high
  124.8 1.1 shard_map.85
  (47 shorter events, 0.3 us)
Async XLA Ops:
  0.6 24.1 %collective-permute-start = (bf16[128,2048]{1,0:T(8,128)(2,1)}, bf16[128,2048]{1,0:T(8,128)(2,1)S(1)}, u32[]{:S(2)}, u32[]{:S(2)}) collective-permute-start(bf16[128,2048]{1,0:T(8,128)(2,1)} %refs_0_.1), channel_id=1, source_target_pairs={{0,4},{1,5},{2,6},{3,7},{4,0},{5,1},{6,2},{7,3},{8,12},{9,13},{10,... | collective-permute-start | bytes 1572872 | tf_op jit(solution)/shard_map/ppermute | solution.py:256
  3.7 21.0 %collective-permute-start.2 = (bf16[128,2048]{1,0:T(8,128)(2,1)}, bf16[128,2048]{1,0:T(8,128)(2,1)S(1)}, u32[]{:S(2)}, u32[]{:S(2)}) collective-permute-start(bf16[128,2048]{1,0:T(8,128)(2,1)} %refs_0_.1), channel_id=1, source_target_pairs={{0,2},{1,3},{2,0},{3,1},{4,6},{5,7},{6,4},{7,5},{8,10},{9,11},{10,... | collective-permute-start | bytes 1572872 | tf_op jit(solution)/shard_map/ppermute | solution.py:256
  5.2 19.5 %collective-permute-start.3 = (bf16[128,2048]{1,0:T(8,128)(2,1)}, bf16[128,2048]{1,0:T(8,128)(2,1)S(1)}, u32[]{:S(2)}, u32[]{:S(2)}) collective-permute-start(bf16[128,2048]{1,0:T(8,128)(2,1)} %refs_0_.1), channel_id=1, source_target_pairs={{0,1},{1,0},{2,3},{3,2},{4,5},{5,4},{6,7},{7,6},{8,9},{9,8},{10,11... | collective-permute-start | bytes 1572872 | tf_op jit(solution)/shard_map/ppermute | solution.py:256
  7.1 17.6 %collective-permute-start.1 = (bf16[64,2048]{1,0:T(8,128)(2,1)}, bf16[64,2048]{1,0:T(8,128)(2,1)S(1)}, u32[]{:S(2)}, u32[]{:S(2)}) collective-permute-start(bf16[64,2048]{1,0:T(8,128)(2,1)} %get-tuple-element.79), channel_id=1, source_target_pairs={{0,8},{1,9},{2,10},{3,11},{4,12},{5,13},{6,14},{7,15},{8,0},{9,1},... | collective-permute-start | bytes 786440 | tf_op jit(solution)/shard_map/ppermute | solution.py:256
  24.7 2.4 %collective-permute-start.7 = (bf16[128,2048]{1,0:T(8,128)(2,1)S(1)}, bf16[128,2048]{1,0:T(8,128)(2,1)S(1)}, u32[]{:S(2)}, u32[]{:S(2)}) collective-permute-start(bf16[128,2048]{1,0:T(8,128)(2,1)S(1)} %collective-permute-done.2.refs_1_), channel_id=1, source_target_pairs={{0,1},{1,0},{2,3},{3,2},{4,5},{5,4},{6,7},{7,6},{8,9},{9,8},{10,11... | collective-permute-start | bytes 1572872 | tf_op jit(solution)/shard_map/ppermute | solution.py:256
  24.8 16.2 %collective-permute-start.5 = (bf16[128,2048]{1,0:T(8,128)(2,1)S(1)}, bf16[128,2048]{1,0:T(8,128)(2,1)S(1)}, u32[]{:S(2)}, u32[]{:S(2)}) collective-permute-start(bf16[128,2048]{1,0:T(8,128)(2,1)S(1)} %collective-permute-done.refs_0_), channel_id=1, source_target_pairs={{0,2},{1,3},{2,0},{3,1},{4,6},{5,7},{6,4},{7,5},{8,10},{9,11},{10,... | collective-permute-start | bytes 1572872 | tf_op jit(solution)/shard_map/ppermute | solution.py:256
  25.4 15.6 %collective-permute-start.6 = (bf16[128,2048]{1,0:T(8,128)(2,1)S(1)}, bf16[128,2048]{1,0:T(8,128)(2,1)S(1)}, u32[]{:S(2)}, u32[]{:S(2)}) collective-permute-start(bf16[128,2048]{1,0:T(8,128)(2,1)S(1)} %collective-permute-done.refs_0_), channel_id=1, source_target_pairs={{0,1},{1,0},{2,3},{3,2},{4,5},{5,4},{6,7},{7,6},{8,9},{9,8},{10,11... | collective-permute-start | bytes 1572872 | tf_op jit(solution)/shard_map/ppermute | solution.py:256
  25.6 15.3 %collective-permute-start.4 = (bf16[64,2048]{1,0:T(8,128)(2,1)}, bf16[64,2048]{1,0:T(8,128)(2,1)S(1)}, u32[]{:S(2)}, u32[]{:S(2)}) collective-permute-start(bf16[64,2048]{1,0:T(8,128)(2,1)} %get-tuple-element.83), channel_id=1, source_target_pairs={{0,8},{1,9},{2,10},{3,11},{4,12},{5,13},{6,14},{7,15},{8,0},{9,1},... | collective-permute-start | bytes 786440 | tf_op jit(solution)/shard_map/ppermute | solution.py:256
  27.1 1.9 %copy-start = (bf16[1,2048,768]{2,1,0:T(8,128)(2,1)S(1)}, bf16[1,2048,768]{2,1,0:T(8,128)(2,1)}, u32[]{:S(2)}) copy-start(bf16[1,2048,768]{2,1,0:T(8,128)(2,1)} %param.9) | copy-start | bytes 9437188
  29.0 1.9 %copy-start.2 = (bf16[1,2048,768]{2,1,0:T(8,128)(2,1)S(1)}, bf16[1,2048,768]{2,1,0:T(8,128)(2,1)}, u32[]{:S(2)}) copy-start(bf16[1,2048,768]{2,1,0:T(8,128)(2,1)} %param.10) | copy-start | bytes 9437188
  30.9 1.9 %copy-start.4 = (bf16[1,768,2048]{2,1,0:T(8,128)(2,1)S(1)}, bf16[1,768,2048]{2,1,0:T(8,128)(2,1)}, u32[]{:S(2)}) copy-start(bf16[1,768,2048]{2,1,0:T(8,128)(2,1)} %param.11) | copy-start | bytes 9437188
  32.8 1.0 copy-start.6
  33.8 9.1 %copy-start.1 = (bf16[1,2048,768]{2,1,0:T(8,128)(2,1)S(1)}, bf16[1,2048,768]{2,1,0:T(8,128)(2,1)}, u32[]{:S(2)}) copy-start(bf16[1,2048,768]{2,1,0:T(8,128)(2,1)} %param.9) | copy-start | bytes 9437188
  33.8 9.1 %copy-start.3 = (bf16[1,2048,768]{2,1,0:T(8,128)(2,1)S(1)}, bf16[1,2048,768]{2,1,0:T(8,128)(2,1)}, u32[]{:S(2)}) copy-start(bf16[1,2048,768]{2,1,0:T(8,128)(2,1)} %param.10) | copy-start | bytes 9437188
  33.8 9.1 %copy-start.5 = (bf16[1,768,2048]{2,1,0:T(8,128)(2,1)S(1)}, bf16[1,768,2048]{2,1,0:T(8,128)(2,1)}, u32[]{:S(2)}) copy-start(bf16[1,768,2048]{2,1,0:T(8,128)(2,1)} %param.11) | copy-start | bytes 9437188
  41.0 1.9 %collective-permute-start.11 = (bf16[128,2048]{1,0:T(8,128)(2,1)S(1)}, bf16[128,2048]{1,0:T(8,128)(2,1)S(1)}, u32[]{:S(2)}, u32[]{:S(2)}) collective-permute-start(bf16[128,2048]{1,0:T(8,128)(2,1)S(1)} %collective-permute-done.5.refs_1_), channel_id=1, source_target_pairs={{0,1},{1,0},{2,3},{3,2},{4,5},{5,4},{6,7},{7,6},{8,9},{9,8},{10,11... | collective-permute-start | bytes 1572872 | tf_op jit(solution)/shard_map/ppermute | solution.py:256
  41.1 14.4 %collective-permute-start.8 = (bf16[128,2048]{1,0:T(8,128)(2,1)S(1)}, bf16[128,2048]{1,0:T(8,128)(2,1)S(1)}, u32[]{:S(2)}, u32[]{:S(2)}) collective-permute-start(bf16[128,2048]{1,0:T(8,128)(2,1)S(1)} %constant_dynamic-update-slice_fusion.refs_0_), channel_id=1, source_target_pairs={{0,4},{1,5},{2,6},{3,7},{4,0},{5,1},{6,2},{7,3},{8,12},{9,13},{10,... | collective-permute-start | bytes 1572872 | tf_op jit(solution)/shard_map/ppermute | solution.py:256
  41.2 14.3 %collective-permute-start.9 = (bf16[128,2048]{1,0:T(8,128)(2,1)S(1)}, bf16[128,2048]{1,0:T(8,128)(2,1)S(1)}, u32[]{:S(2)}, u32[]{:S(2)}) collective-permute-start(bf16[128,2048]{1,0:T(8,128)(2,1)S(1)} %constant_dynamic-update-slice_fusion.refs_0_), channel_id=1, source_target_pairs={{0,2},{1,3},{2,0},{3,1},{4,6},{5,7},{6,4},{7,5},{8,10},{9,11},{10,... | collective-permute-start | bytes 1572872 | tf_op jit(solution)/shard_map/ppermute | solution.py:256
  42.7 12.8 %collective-permute-start.10 = (bf16[128,2048]{1,0:T(8,128)(2,1)S(1)}, bf16[128,2048]{1,0:T(8,128)(2,1)S(1)}, u32[]{:S(2)}, u32[]{:S(2)}) collective-permute-start(bf16[128,2048]{1,0:T(8,128)(2,1)S(1)} %constant_dynamic-update-slice_fusion.refs_0_), channel_id=1, source_target_pairs={{0,1},{1,0},{2,3},{3,2},{4,5},{5,4},{6,7},{7,6},{8,9},{9,8},{10,11... | collective-permute-start | bytes 1572872 | tf_op jit(solution)/shard_map/ppermute | solution.py:256
  48.4 7.1 %collective-permute-start.12 = (bf16[128,2048]{1,0:T(8,128)(2,1)S(1)}, bf16[128,2048]{1,0:T(8,128)(2,1)S(1)}, u32[]{:S(2)}, u32[]{:S(2)}) collective-permute-start(bf16[128,2048]{1,0:T(8,128)(2,1)S(1)} %get-tuple-element.98), channel_id=1, source_target_pairs={{0,1},{1,0},{2,3},{3,2},{4,5},{5,4},{6,7},{7,6},{8,9},{9,8},{10,11... | collective-permute-start | bytes 1572872 | tf_op jit(solution)/shard_map/ppermute | solution.py:256
  55.5 3.9 %collective-permute-start.17 = (bf16[128,2048]{1,0:T(8,128)(2,1)S(1)}, bf16[128,2048]{1,0:T(8,128)(2,1)S(1)}, u32[]{:S(2)}, u32[]{:S(2)}) collective-permute-start(bf16[128,2048]{1,0:T(8,128)(2,1)S(1)} %collective-permute-done.9.refs_1_), channel_id=1, source_target_pairs={{0,1},{1,0},{2,3},{3,2},{4,5},{5,4},{6,7},{7,6},{8,9},{9,8},{10,11... | collective-permute-start | bytes 1572872 | tf_op jit(solution)/shard_map/ppermute | solution.py:256
  55.6 12.8 %collective-permute-start.15 = (bf16[256,2048]{1,0:T(8,128)(2,1)S(1)}, bf16[256,2048]{1,0:T(8,128)(2,1)S(1)}, u32[]{:S(2)}, u32[]{:S(2)}) collective-permute-start(bf16[256,2048]{1,0:T(8,128)(2,1)S(1)} %get-tuple-element.102), channel_id=1, source_target_pairs={{0,1},{1,0},{2,3},{3,2},{4,5},{5,4},{6,7},{7,6},{8,9},{9,8},{10,11... | collective-permute-start | bytes 3145736 | tf_op jit(solution)/shard_map/ppermute | solution.py:256
  56.1 13.9 %collective-permute-start.13 = (bf16[128,2048]{1,0:T(8,128)(2,1)S(1)}, bf16[128,2048]{1,0:T(8,128)(2,1)S(1)}, u32[]{:S(2)}, u32[]{:S(2)}) collective-permute-start(bf16[128,2048]{1,0:T(8,128)(2,1)S(1)} %collective-permute-done.9.refs_1_), channel_id=1, source_target_pairs={{0,4},{1,5},{2,6},{3,7},{4,0},{5,1},{6,2},{7,3},{8,12},{9,13},{10,... | collective-permute-start | bytes 1572872 | tf_op jit(solution)/shard_map/ppermute | solution.py:256
  57.7 7.6 %collective-permute-start.19 = (bf16[128,2048]{1,0:T(8,128)(2,1)S(1)}, bf16[128,2048]{1,0:T(8,128)(2,1)S(1)}, u32[]{:S(2)}, u32[]{:S(2)}) collective-permute-start(bf16[128,2048]{1,0:T(8,128)(2,1)S(1)} %collective-permute-done.8.refs_0_), channel_id=1, source_target_pairs={{0,1},{1,0},{2,3},{3,2},{4,5},{5,4},{6,7},{7,6},{8,9},{9,8},{10,11... | collective-permute-start | bytes 1572872 | tf_op jit(solution)/shard_map/ppermute | solution.py:256
  57.9 10.5 %collective-permute-start.14 = (bf16[64,2048]{1,0:T(8,128)(2,1)S(1)}, bf16[64,2048]{1,0:T(8,128)(2,1)S(1)}, u32[]{:S(2)}, u32[]{:S(2)}) collective-permute-start(bf16[64,2048]{1,0:T(8,128)(2,1)S(1)} %get-tuple-element.157), channel_id=1, source_target_pairs={{0,2},{1,3},{2,0},{3,1},{4,6},{5,7},{6,4},{7,5},{8,10},{9,11},{10,... | collective-permute-start | bytes 786440 | tf_op jit(solution)/shard_map/ppermute | solution.py:256
  59.4 10.6 %collective-permute-start.16 = (bf16[128,2048]{1,0:T(8,128)(2,1)S(1)}, bf16[128,2048]{1,0:T(8,128)(2,1)S(1)}, u32[]{:S(2)}, u32[]{:S(2)}) collective-permute-start(bf16[128,2048]{1,0:T(8,128)(2,1)S(1)} %get-tuple-element.103), channel_id=1, source_target_pairs={{0,1},{1,0},{2,3},{3,2},{4,5},{5,4},{6,7},{7,6},{8,9},{9,8},{10,11... | collective-permute-start | bytes 1572872 | tf_op jit(solution)/shard_map/ppermute | solution.py:256
  65.3 4.7 %collective-permute-start.18 = (bf16[64,2048]{1,0:T(8,128)(2,1)S(1)}, bf16[64,2048]{1,0:T(8,128)(2,1)S(1)}, u32[]{:S(2)}, u32[]{:S(2)}) collective-permute-start(bf16[64,2048]{1,0:T(8,128)(2,1)S(1)} %get-tuple-element.105), channel_id=1, source_target_pairs={{0,1},{1,0},{2,3},{3,2},{4,5},{5,4},{6,7},{7,6},{8,9},{9,8},{10,11... | collective-permute-start | bytes 786440 | tf_op jit(solution)/shard_map/ppermute | solution.py:256
  70.0 1.9 %collective-permute-start.21 = (bf16[128,2048]{1,0:T(8,128)(2,1)S(1)}, bf16[128,2048]{1,0:T(8,128)(2,1)S(1)}, u32[]{:S(2)}, u32[]{:S(2)}) collective-permute-start(bf16[128,2048]{1,0:T(8,128)(2,1)S(1)} %collective-permute-done.13.refs_0_), channel_id=1, source_target_pairs={{0,1},{1,0},{2,3},{3,2},{4,5},{5,4},{6,7},{7,6},{8,9},{9,8},{10,11... | collective-permute-start | bytes 1572872 | tf_op jit(solution)/shard_map/ppermute | solution.py:256
  70.1 8.8 %collective-permute-start.20 = (bf16[64,2048]{1,0:T(8,128)(2,1)S(1)}, bf16[64,2048]{1,0:T(8,128)(2,1)S(1)}, u32[]{:S(2)}, u32[]{:S(2)}) collective-permute-start(bf16[64,2048]{1,0:T(8,128)(2,1)S(1)} %add_convert_fusion.11), channel_id=1, source_target_pairs={{0,2},{1,3},{2,0},{3,1},{4,6},{5,7},{6,4},{7,5},{8,10},{9,11},{10,... | collective-permute-start | bytes 786440 | tf_op jit(solution)/shard_map/ppermute | solution.py:256
  71.6 7.2 %collective-permute-start.22 = (bf16[128,2048]{1,0:T(8,128)(2,1)S(1)}, bf16[128,2048]{1,0:T(8,128)(2,1)S(1)}, u32[]{:S(2)}, u32[]{:S(2)}) collective-permute-start(bf16[128,2048]{1,0:T(8,128)(2,1)S(1)} %get-tuple-element.121), channel_id=1, source_target_pairs={{0,1},{1,0},{2,3},{3,2},{4,5},{5,4},{6,7},{7,6},{8,9},{9,8},{10,11... | collective-permute-start | bytes 1572872 | tf_op jit(solution)/shard_map/ppermute | solution.py:256
  78.9 3.0 %collective-permute-start.23 = (bf16[128,2048]{1,0:T(8,128)(2,1)S(1)}, bf16[128,2048]{1,0:T(8,128)(2,1)S(1)}, u32[]{:S(2)}, u32[]{:S(2)}) collective-permute-start(bf16[128,2048]{1,0:T(8,128)(2,1)S(1)} %get-tuple-element.125), channel_id=1, source_target_pairs={{0,1},{1,0},{2,3},{3,2},{4,5},{5,4},{6,7},{7,6},{8,9},{9,8},{10,11... | collective-permute-start | bytes 1572872 | tf_op jit(solution)/shard_map/ppermute | solution.py:256
  78.9 4.7 %collective-permute-start.28 = (bf16[64,2048]{1,0:T(8,128)(2,1)S(1)}, bf16[64,2048]{1,0:T(8,128)(2,1)S(1)}, u32[]{:S(2)}, u32[]{:S(2)}) collective-permute-start(bf16[64,2048]{1,0:T(8,128)(2,1)S(1)} %get-tuple-element.131), channel_id=1, source_target_pairs={{0,1},{1,0},{2,3},{3,2},{4,5},{5,4},{6,7},{7,6},{8,9},{9,8},{10,11... | collective-permute-start | bytes 786440 | tf_op jit(solution)/shard_map/ppermute | solution.py:256
  79.4 4.9 %collective-permute-start.29 = (bf16[128,2048]{1,0:T(8,128)(2,1)S(1)}, bf16[128,2048]{1,0:T(8,128)(2,1)S(1)}, u32[]{:S(2)}, u32[]{:S(2)}) collective-permute-start(bf16[128,2048]{1,0:T(8,128)(2,1)S(1)} %get-tuple-element.132), channel_id=1, source_target_pairs={{0,1},{1,0},{2,3},{3,2},{4,5},{5,4},{6,7},{7,6},{8,9},{9,8},{10,11... | collective-permute-start | bytes 1572872 | tf_op jit(solution)/shard_map/ppermute | solution.py:256
  79.5 15.3 %collective-permute-start.26 = (bf16[64,2048]{1,0:T(8,128)(2,1)S(1)}, bf16[64,2048]{1,0:T(8,128)(2,1)S(1)}, u32[]{:S(2)}, u32[]{:S(2)}) collective-permute-start(bf16[64,2048]{1,0:T(8,128)(2,1)S(1)} %add_convert_fusion.7), channel_id=1, source_target_pairs={{0,8},{1,9},{2,10},{3,11},{4,12},{5,13},{6,14},{7,15},{8,0},{9,1},... | collective-permute-start | bytes 786440 | tf_op jit(solution)/shard_map/ppermute | solution.py:256
  81.2 13.5 %collective-permute-start.27 = (bf16[64,2048]{1,0:T(8,128)(2,1)S(1)}, bf16[64,2048]{1,0:T(8,128)(2,1)S(1)}, u32[]{:S(2)}, u32[]{:S(2)}) collective-permute-start(bf16[64,2048]{1,0:T(8,128)(2,1)S(1)} %add_convert_fusion.10), channel_id=1, source_target_pairs={{0,4},{1,5},{2,6},{3,7},{4,0},{5,1},{6,2},{7,3},{8,12},{9,13},{10,... | collective-permute-start | bytes 786440 | tf_op jit(solution)/shard_map/ppermute | solution.py:256
  82.0 12.8 %collective-permute-start.24 = (bf16[64,2048]{1,0:T(8,128)(2,1)S(1)}, bf16[64,2048]{1,0:T(8,128)(2,1)S(1)}, u32[]{:S(2)}, u32[]{:S(2)}) collective-permute-start(bf16[64,2048]{1,0:T(8,128)(2,1)S(1)} %get-tuple-element.161), channel_id=1, source_target_pairs={{0,2},{1,3},{2,0},{3,1},{4,6},{5,7},{6,4},{7,5},{8,10},{9,11},{10,... | collective-permute-start | bytes 786440 | tf_op jit(solution)/shard_map/ppermute | solution.py:256
  83.6 12.3 %collective-permute-start.25 = (bf16[64,2048]{1,0:T(8,128)(2,1)S(1)}, bf16[64,2048]{1,0:T(8,128)(2,1)S(1)}, u32[]{:S(2)}, u32[]{:S(2)}) collective-permute-start(bf16[64,2048]{1,0:T(8,128)(2,1)S(1)} %get-tuple-element.160), channel_id=1, source_target_pairs={{0,2},{1,3},{2,0},{3,1},{4,6},{5,7},{6,4},{7,5},{8,10},{9,11},{10,... | collective-permute-start | bytes 786440 | tf_op jit(solution)/shard_map/ppermute | solution.py:256
  96.1 14.0 %collective-permute-start.30 = (bf16[64,2048]{1,0:T(8,128)(2,1)S(1)}, bf16[64,2048]{1,0:T(8,128)(2,1)S(1)}, u32[]{:S(2)}, u32[]{:S(2)}) collective-permute-start(bf16[64,2048]{1,0:T(8,128)(2,1)S(1)} %get-tuple-element.159), channel_id=1, source_target_pairs={{0,8},{1,9},{2,10},{3,11},{4,12},{5,13},{6,14},{7,15},{8,0},{9,1},... | collective-permute-start | bytes 786440 | tf_op jit(solution)/shard_map/ppermute | solution.py:256
  98.4 11.7 %collective-permute-start.31 = (bf16[64,2048]{1,0:T(8,128)(2,1)S(1)}, bf16[64,2048]{1,0:T(8,128)(2,1)S(1)}, u32[]{:S(2)}, u32[]{:S(2)}) collective-permute-start(bf16[64,2048]{1,0:T(8,128)(2,1)S(1)} %get-tuple-element.158), channel_id=1, source_target_pairs={{0,4},{1,5},{2,6},{3,7},{4,0},{5,1},{6,2},{7,3},{8,12},{9,13},{10,... | collective-permute-start | bytes 786440 | tf_op jit(solution)/shard_map/ppermute | solution.py:256
  98.8 11.3 %collective-permute-start.32 = (bf16[64,2048]{1,0:T(8,128)(2,1)S(1)}, bf16[64,2048]{1,0:T(8,128)(2,1)S(1)}, u32[]{:S(2)}, u32[]{:S(2)}) collective-permute-start(bf16[64,2048]{1,0:T(8,128)(2,1)S(1)} %add_convert_fusion.3), channel_id=1, source_target_pairs={{0,2},{1,3},{2,0},{3,1},{4,6},{5,7},{6,4},{7,5},{8,10},{9,11},{10,... | collective-permute-start | bytes 786440 | tf_op jit(solution)/shard_map/ppermute | solution.py:256
  100.4 10.9 %collective-permute-start.33 = (bf16[64,2048]{1,0:T(8,128)(2,1)S(1)}, bf16[64,2048]{1,0:T(8,128)(2,1)S(1)}, u32[]{:S(2)}, u32[]{:S(2)}) collective-permute-start(bf16[64,2048]{1,0:T(8,128)(2,1)S(1)} %get-tuple-element.137), channel_id=1, source_target_pairs={{0,2},{1,3},{2,0},{3,1},{4,6},{5,7},{6,4},{7,5},{8,10},{9,11},{10,... | collective-permute-start | bytes 786440 | tf_op jit(solution)/shard_map/ppermute | solution.py:256
  111.4 12.8 %collective-permute-start.34 = (bf16[64,2048]{1,0:T(8,128)(2,1)S(1)}, bf16[64,2048]{1,0:T(8,128)(2,1)S(1)}, u32[]{:S(2)}, u32[]{:S(2)}) collective-permute-start(bf16[64,2048]{1,0:T(8,128)(2,1)S(1)} %add_convert_fusion.2), channel_id=1, source_target_pairs={{0,8},{1,9},{2,10},{3,11},{4,12},{5,13},{6,14},{7,15},{8,0},{9,1},... | collective-permute-start | bytes 786440 | tf_op jit(solution)/shard_map/ppermute | solution.py:256
  113.2 11.6 %collective-permute-start.36 = (bf16[128,2048]{1,0:T(8,128)(2,1)S(1)}, bf16[128,2048]{1,0:T(8,128)(2,1)S(1)}, u32[]{:S(2)}, u32[]{:S(2)}) collective-permute-start(bf16[128,2048]{1,0:T(8,128)(2,1)S(1)} %add_convert_fusion), channel_id=1, source_target_pairs={{0,2},{1,3},{2,0},{3,1},{4,6},{5,7},{6,4},{7,5},{8,10},{9,11},{10,... | collective-permute-start | bytes 1572872 | tf_op jit(solution)/shard_map/ppermute | solution.py:256
  114.7 10.0 %collective-permute-start.35 = (bf16[64,2048]{1,0:T(8,128)(2,1)S(1)}, bf16[64,2048]{1,0:T(8,128)(2,1)S(1)}, u32[]{:S(2)}, u32[]{:S(2)}) collective-permute-start(bf16[64,2048]{1,0:T(8,128)(2,1)S(1)} %add_convert_fusion.1), channel_id=1, source_target_pairs={{0,4},{1,5},{2,6},{3,7},{4,0},{5,1},{6,2},{7,3},{8,12},{9,13},{10,... | collective-permute-start | bytes 786440 | tf_op jit(solution)/shard_map/ppermute | solution.py:256
